TPU v7x, 32 devices: a whole 2x2x4 slice. The times are simulated.
32 devices in a mesh: blk: 16 (over z, y, core), inner: 2 (over x).
Axes of the slice: x: 2, y: 2, z: 4, core: 2. Of those that a mesh axis runs over, the one named last changes fastest.
Arguments:
- queries: bfloat16 [3072, 5120], P('blk', 'inner'), may hold values from -48 to 48
- keys: bfloat16 [3072, 1024], P('blk', 'inner'), may hold values from -48 to 48
- values: bfloat16 [3072, 1024], P('blk', 'inner'), may hold values from -6 to 6
- positions: int32 [3072], P('blk'), may hold values from 0 to 3071, as said below
- out_weight: bfloat16 [5120, 5120], P('inner'), may hold values from -0.078125 to 0.078125
Outputs:
- projected: bfloat16 [3072, 5120], P(('blk', 'inner'))
Inputs may be any that keep to these rules, and one draw needn't show every extreme that they name: The rows of index b of blk (rows 192 b to 192 b + 191) hold the positions c * 96 to c * 96 + 95 followed by (31 - c) * 96 to (31 - c) * 96 + 95, in increasing order, with a different c from 0 to 15 for every b; every position appears once.
All inputs are finite; a program needn't handle non-finite values.
Results may differ from a plain program's by a relative error of at most 0.018.
Values may be sent and summed in bfloat16 or wider, within the bound.
No kernel may reach another device: no remote copies, remote signals or barrier semaphores. Data moves between devices by JAX's collectives and lax.ppermute only.
A program may use at most 128 MiB of HBM per device.

v0:
```python
import math

import jax
import jax.numpy as jnp
from jax import lax
from jax.sharding import PartitionSpec as P

HEAD_WIDTH = 128
QUERY_PER_KEY = 5


def initial_state(head_count, query_count):
    highest = jnp.full((head_count, QUERY_PER_KEY, query_count), -1e30, jnp.float32)
    totals = jnp.zeros((head_count, QUERY_PER_KEY, query_count), jnp.float32)
    summed = jnp.zeros((head_count, QUERY_PER_KEY, query_count, HEAD_WIDTH), jnp.float32)
    return (highest, totals, summed)


def attend(running, query_rows, query_pos, key_rows, value_rows, key_pos, block_size):
    highest, totals, summed = running
    inverse_root = 1.0 / math.sqrt(HEAD_WIDTH)
    head_count = key_rows.shape[1] // HEAD_WIDTH
    key_count = key_rows.shape[0]
    for offset in range(0, key_count, block_size):
        block_rows = min(block_size, key_count - offset)
        key_block = key_rows[offset : offset + block_rows].reshape(
            block_rows, head_count, HEAD_WIDTH
        )
        value_block = value_rows[offset : offset + block_rows].reshape(
            block_rows, head_count, HEAD_WIDTH
        )
        visible = key_pos[offset : offset + block_rows][None, :] <= query_pos[:, None]
        scores = (
            jnp.einsum("qhgd,khd->hgqk", query_rows, key_block, preferred_element_type=jnp.float32)
            * inverse_root
        )
        scores = jnp.where(visible[None, None], scores, -1e30)
        new_high = jnp.maximum(highest, jnp.max(scores, axis=-1))
        rescale = jnp.exp(highest - new_high)
        weights = jnp.where(visible[None, None], jnp.exp(scores - new_high[..., None]), 0.0)
        totals = totals * rescale + jnp.sum(weights, axis=-1)
        summed = summed * rescale[..., None] + jnp.einsum(
            "hgqk,khd->hgqd",
            weights.astype(jnp.bfloat16),
            value_block,
            preferred_element_type=jnp.float32,
        )
        highest = new_high
    return (highest, totals, summed)


def finish(totals, summed):
    mixed = (summed / totals[..., None]).astype(jnp.bfloat16)
    query_count = mixed.shape[2]
    return jnp.transpose(mixed, (2, 0, 1, 3)).reshape(
        query_count, mixed.shape[0] * QUERY_PER_KEY * HEAD_WIDTH
    )


def shards(queries, keys, values, positions, out_weight):
    own_rows = queries.shape[0]
    head_count = keys.shape[1] // HEAD_WIDTH
    query_rows = queries.reshape(own_rows, head_count, QUERY_PER_KEY, HEAD_WIDTH)
    start_states = initial_state(head_count, own_rows)
    folded = attend(
        start_states,
        query_rows,
        positions,
        lax.all_gather(keys, "blk", axis=0, tiled=True),
        lax.all_gather(values, "blk", axis=0, tiled=True),
        lax.all_gather(positions, "blk", axis=0, tiled=True),
        512,
    )
    attended_values = finish(folded[1], folded[2])
    return lax.psum_scatter(
        jnp.dot(attended_values, out_weight, preferred_element_type=jnp.float32).astype(
            jnp.bfloat16
        ),
        "inner",
        scatter_dimension=0,
        tiled=True,
    )


def solution(mesh):
    placed = (P("blk", "inner"), P("blk", "inner"), P("blk", "inner"), P("blk"), P("inner", None))
    return jax.shard_map(
        shards, mesh=mesh, in_specs=placed, out_specs=P(("blk", "inner"), None), check_vma=False
    )
```

profile of v0, /device:TPU:0, one launch (start us, length us, event | category | flops | bytes accessed | tf_op | source)
XLA Modules:
  0.0 246.3 jit_solution(13135417712974113145)
XLA Ops:
  6.5 0.7 all-gather.3.cloned.1.call-update
  7.3 0.0 all-gather.5.cloned.1.call-start
  7.3 0.7 all-gather.5.cloned.1.call-update
  8.0 0.0 reduce-scatter.2.cloned.1.call-start
  8.1 1.5 copy.35
  9.6 1.2 dynamic-slice
  11.5 0.9 dynamic-update-slice
  12.4 63.4 %all-reduce = s32[3072]{0:T(1024)S(1)} all-reduce(s32[3072]{0:T(1024)S(1)} %dynamic-update-slice), channel_id=1, replica_groups=mesh['blk'=16,'inner'=2] {'blk'}, use_global_device_ids=true, to_apply=%add | all-reduce | flops 3072 | bytes 24576
  75.8 1.8 broadcast_compare_fusion.5
  77.6 3.0 %fusion.77 = (bf16[512,512]{1,0:T(8,128)(2,1)}, bf16[512,512]{1,0:T(8,128)(2,1)}, bf16[512,512]{1,0:T(8,128)(2,1)}, bf16[512,512]{1,0:T(8,128)(2,1)S(1)}, bf16[5...) fusion(bf16[3072,512]{1,0:T(8,128)(2,1)} %all-gather.3.cloned.1.call-done), kind=kLoop, calls=%fused_computation.109 | loop fusion | bytes 6291456 | tf_op jit(solution)/shard_map/slice | solution.py:26
  80.6 1.3 copy.108
  81.9 22.5 %all-gather.5.cloned.1.call-done = bf16[3072,512]{1,0:T(8,128)(2,1)} async-done(((bf16[192,512]{1,0:T(8,128)(2,1)}), bf16[3072,512]{1,0:T(8,128)(2,1)}) %all-gather.5.cloned.1.call-update) | async-done | bytes 3145744 | tf_op jit(solution)/shard_map/all_gather | solution.py:70
  104.4 3.5 %fusion.76 = (bf16[512,512]{1,0:T(8,128)(2,1)}, bf16[512,512]{1,0:T(8,128)(2,1)}, bf16[512,512]{1,0:T(8,128)(2,1)}, bf16[512,512]{1,0:T(8,128)(2,1)}, bf16[512,512]{1,0:T(8,128)(2,1)}, /*index=5*/bf16[512,512]{1,0:T(8,128)(2,1)}) fusion(bf16[3072,512]{1,0:T(8,128)(2,1)} %all-gather.5.cloned.1.call-done), kind=kLoop, calls=%fused_computation.108 | loop fusion | bytes 6291456 | tf_op jit(solution)/shard_map/slice | solution.py:29
  107.9 2.1 copy.109
  110.0 2.1 copy.117
  112.1 2.1 copy.115
  114.2 2.0 copy.113
  116.3 2.1 copy.111
  118.3 2.0 copy.119
  120.4 2.1 copy.116
  122.5 2.1 copy.114
  124.5 1.0 copy.112
  125.5 0.2 copy.110
  125.8 0.2 copy.118
  126.0 1.8 fusion
  127.8 1.8 fusion.1
  129.7 0.0 copy-done.2
  129.7 0.0 copy-done.4
  129.7 0.0 copy-start
  129.7 0.0 copy-start.6
  129.7 1.8 fusion.2
  131.5 4.7 %fusion.3 = (f32[4,5,192]{2,1,0:T(8,128)S(1)}, f32[4,512,192,5]{1,2,3,0:T(8,128)}) fusion(pred[192,512]{1,0:T(8,128)(4,1)S(1)} %copy-done.5, bf16[512,4,128,1]{0,2,3,1:T(8,128)(2,1)S(1)} %bitcast.285, bf16[192,4,5,128]{0,3,2,1:T(8,128)(2,1)S(1)} %bitcast.278), kind=kOutput, calls=%fused_computation.15 | convolution fusion | flops 509210880 | bytes 9485312 | tf_op jit(solution)/shard_map/qhgd,khd->hgqk/dot_general | solution.py:34
  136.3 5.0 %fusion.4 = (f32[4,5,192]{2,1,0:T(8,128)S(1)}, f32[4,512,192,5]{1,2,3,0:T(8,128)}) fusion(pred[192,512]{1,0:T(8,128)(4,1)S(1)} %copy-done.6, bf16[512,4,128,1]{0,2,3,1:T(8,128)(2,1)S(1)} %bitcast.283, bf16[192,4,5,128]{0,3,2,1:T(8,128)(2,1)S(1)} %bitcast.279), kind=kOutput, calls=%fused_computation.16 | convolution fusion | flops 509210880 | bytes 9485312 | tf_op jit(solution)/shard_map/qhgd,khd->hgqk/dot_general | solution.py:34
  141.3 4.7 %fusion.5 = (f32[4,5,192]{2,1,0:T(8,128)S(1)}, f32[4,512,192,5]{1,2,3,0:T(8,128)}) fusion(pred[192,512]{1,0:T(8,128)(4,1)S(1)} %copy-done.7, bf16[512,4,128,1]{0,2,3,1:T(8,128)(2,1)S(1)} %bitcast.284, bf16[192,4,5,128]{0,3,2,1:T(8,128)(2,1)S(1)} %bitcast.280), kind=kOutput, calls=%fused_computation.17 | convolution fusion | flops 509210880 | bytes 9485312 | tf_op jit(solution)/shard_map/qhgd,khd->hgqk/dot_general | solution.py:34
  146.1 4.5 %fusion.18 = f32[4,5,192,128]{3,2,1,0:T(8,128)S(1)} fusion(bf16[512,4,128,1]{0,2,3,1:T(8,128)(2,1)S(1)} %bitcast.293, f32[4,512,192,5]{1,2,3,0:T(8,128)} %get-tuple-element.44, f32[4,5,192]{2,1,0:T(8,128)S(1)} %get-tuple-element.10, pred[192,512]{1,0:T(8,128)(4,1)S(1)} %copy-done.7), kind=kOutput, calls=%fused_computation.31 | convolution fusion | flops 513146880 | bytes 10468352 | tf_op jit(solution)/shard_map/hgqk,khd->hgqd/dot_general | solution.py:42
  150.6 8.4 %fusion.14 = (f32[4,5,192]{2,1,0:T(8,128)S(1)}, f32[4,5,192]{2,1,0:T(8,128)S(1)}) fusion(f32[4,512,192,5]{1,2,3,0:T(8,128)} %get-tuple-element.46, f32[4,5,192]{2,1,0:T(8,128)S(1)} %get-tuple-element.11, pred[192,512]{1,0:T(8,128)(4,1)S(1)} %copy-done.6, f32[4,5,192]{2,1,0:T(8,128)S(1)} %get-tuple-element.10, f32[4,512,192,5]{1,2,3,0:T(8,128)} %get-tuple-element.44, ...), kind=kLoop, calls=%fused_computation.27 | loop fusion | flops 19653120 | bytes 15986688 | tf_op jit(solution)/shard_map/reduce_sum | solution.py:41
  159.0 6.6 %fusion.20 = f32[4,5,192,128]{3,2,1,0:T(8,128)} fusion(bf16[512,4,128,1]{0,2,3,1:T(8,128)(2,1)S(1)} %bitcast.292, f32[4,512,192,5]{1,2,3,0:T(8,128)} %get-tuple-element.46, f32[4,5,192]{2,1,0:T(8,128)S(1)} %get-tuple-element.11, pred[192,512]{1,0:T(8,128)(4,1)S(1)} %copy-done.6), kind=kOutput, calls=%fused_computation.32 | convolution fusion | flops 513146880 | bytes 10468352 | tf_op jit(solution)/shard_map/hgqk,khd->hgqd/dot_general | solution.py:42
  165.5 6.6 %fusion.22 = f32[4,5,192,128]{3,2,1,0:T(8,128)} fusion(bf16[512,4,128,1]{0,2,3,1:T(8,128)(2,1)S(1)} %bitcast.291, f32[4,512,192,5]{1,2,3,0:T(8,128)} %get-tuple-element.48, f32[4,5,192]{2,1,0:T(8,128)S(1)} %get-tuple-element.12, pred[192,512]{1,0:T(8,128)(4,1)S(1)} %copy-done.5), kind=kOutput, calls=%fused_computation.33 | convolution fusion | flops 513146880 | bytes 10468352 | tf_op jit(solution)/shard_map/hgqk,khd->hgqd/dot_general | solution.py:42
  172.1 7.1 %fusion.10 = (f32[4,5,192]{2,1,0:T(8,128)S(1)}, f32[4,5,192]{2,1,0:T(8,128)S(1)}) fusion(f32[4,512,192,5]{1,2,3,0:T(8,128)S(1)} %get-tuple-element.50, f32[4,5,192]{2,1,0:T(8,128)S(1)} %get-tuple-element.13, pred[192,512]{1,0:T(8,128)(4,1)S(1)} %copy-done.4, f32[4,5,192]{2,1,0:T(8,128)S(1)} %get-tuple-element.12, f32[4,512,192,5]{1,2,3,0:T(8,128)} %get-tuple-element.48, ...), kind=kLoop, calls=%fused_computation.23 | loop fusion | flops 19653120 | bytes 15986688 | tf_op jit(solution)/shard_map/reduce_sum | solution.py:41
  179.3 3.6 %fusion.24 = f32[4,5,192,128]{3,2,1,0:T(8,128)} fusion(bf16[512,4,128,1]{0,2,3,1:T(8,128)(2,1)S(1)} %bitcast.290, f32[4,512,192,5]{1,2,3,0:T(8,128)S(1)} %get-tuple-element.50, f32[4,5,192]{2,1,0:T(8,128)S(1)} %get-tuple-element.13, pred[192,512]{1,0:T(8,128)(4,1)S(1)} %copy-done.4), kind=kOutput, calls=%fused_computation.34 | convolution fusion | flops 513146880 | bytes 10468352 | tf_op jit(solution)/shard_map/hgqk,khd->hgqd/dot_general | solution.py:42
  182.9 2.1 fusion.26
  185.1 5.5 %fusion.6 = (f32[4,5,192]{2,1,0:T(8,128)S(1)}, f32[4,5,192]{2,1,0:T(8,128)S(1)}) fusion(f32[4,512,192,5]{1,2,3,0:T(8,128)S(1)} %get-tuple-element.54, f32[4,5,192]{2,1,0:T(8,128)S(1)} %get-tuple-element.30, pred[192,512]{1,0:T(8,128)(4,1)S(1)} %get-tuple-element.37, f32[4,5,192]{2,1,0:T(8,128)S(1)} %get-tuple-element.14, ...), kind=kLoop, calls=%fused_computation.19 | loop fusion | flops 19653120 | bytes 15986688 | tf_op jit(solution)/shard_map/reduce_sum | solution.py:41
  190.6 0.1 bitcast_add_fusion.6
  190.7 6.3 %fusion.37 = bf16[192,4,5,128]{3,0,2,1:T(8,128)(2,1)S(1)} fusion(f32[4,5,192,128]{3,2,1,0:T(8,128)S(1)} %fusion.18, f32[4,5,192,128]{3,2,1,0:T(8,128)S(1)} %copy-done.14, f32[4,5,192,128]{3,2,1,0:T(8,128)S(1)} %copy-done.15, f32[4,5,192,128]{3,2,1,0:T(8,128)S(1)} %copy-done.16, f32[4,5,192,128]{3,2,1,0:T(8,128)S(1)} %fusion.26, ...), kind=kOutput, calls=%fused_computation.45 | convolution fusion | flops 519536640 | bytes 19423232 | tf_op jit(solution)/shard_map/hgqk,khd->hgqd/dot_general | solution.py:42
  197.0 0.6 copy.65
  197.6 12.7 %convolution_convert_fusion = bf16[192,5120]{1,0:T(8,128)(2,1)} fusion(bf16[192,2560]{0,1:T(8,128)(2,1)S(1)} %bitcast.281, bf16[2560,5120]{1,0:T(8,128)(2,1)} %param.9), kind=kOutput, calls=%fused_computation.18 | convolution fusion | flops 5034147840 | bytes 29163520 | tf_op jit(solution)/shard_map/dot_general | solution.py:76
  210.4 0.0 reduce-scatter.2.cloned.1.call-update
  210.4 29.3 %reduce-scatter.2.cloned.1.call-done = bf16[96,5120]{1,0:T(8,128)(2,1)} async-done(((bf16[192,5120]{1,0:T(8,128)(2,1)}), bf16[96,5120]{1,0:T(8,128)(2,1)}) %reduce-scatter.2.cloned.1.call-update) | async-done | bytes 983056 | tf_op jit(solution)/shard_map/reduce_scatter | solution.py:75
  (36 shorter events, 0.1 us)
Async XLA Ops:
  6.5 71.1 %all-gather.3.cloned.1.call-start = ((), (), s32[]{:S(2)}) async-start(), calls=%async_computation.1 | async-start | bytes 3342336 | tf_op jit(solution)/shard_map/all_gather | solution.py:69
  7.3 97.1 %all-gather.5.cloned.1.call-start = ((), (), s32[]{:S(2)}) async-start(), calls=%async_computation.2 | async-start | bytes 3342336 | tf_op jit(solution)/shard_map/all_gather | solution.py:70
  8.0 231.7 %reduce-scatter.2.cloned.1.call-start = ((), (), s32[]{:S(2)}) async-start(), calls=%async_computation.3 | async-start | bytes 2949120 | tf_op jit(solution)/shard_map/reduce_scatter | solution.py:75
  126.0 1.8 copy-start.3
  126.0 3.7 %copy-start.2 = (bf16[512,512]{0,1:T(8,128)(2,1)S(1)}, bf16[512,512]{0,1:T(8,128)(2,1)}, u32[]{:S(2)}) copy-start(bf16[512,512]{0,1:T(8,128)(2,1)} %copy.112) | copy-start | bytes 1572868
  126.0 3.7 %copy-start.4 = (pred[192,512]{1,0:T(8,128)(4,1)S(1)}, pred[192,512]{1,0:T(8,128)(4,1)}, u32[]{:S(2)}) copy-start(pred[192,512]{1,0:T(8,128)(4,1)} %get-tuple-element.39) | copy-start | bytes 294916
  127.8 3.7 %copy-start.1 = (bf16[512,512]{0,1:T(8,128)(2,1)S(1)}, bf16[512,512]{0,1:T(8,128)(2,1)}, u32[]{:S(2)}) copy-start(bf16[512,512]{0,1:T(8,128)(2,1)} %copy.114) | copy-start | bytes 1572868
  127.8 3.7 %copy-start.5 = (pred[192,512]{1,0:T(8,128)(4,1)S(1)}, pred[192,512]{1,0:T(8,128)(4,1)}, u32[]{:S(2)}) copy-start(pred[192,512]{1,0:T(8,128)(4,1)} %get-tuple-element.40) | copy-start | bytes 294916
  129.7 6.6 %copy-start = (bf16[512,512]{0,1:T(8,128)(2,1)S(1)}, bf16[512,512]{0,1:T(8,128)(2,1)}, u32[]{:S(2)}) copy-start(bf16[512,512]{0,1:T(8,128)(2,1)} %copy.116) | copy-start | bytes 1572868
  129.7 6.6 %copy-start.6 = (pred[192,512]{1,0:T(8,128)(4,1)S(1)}, pred[192,512]{1,0:T(8,128)(4,1)}, u32[]{:S(2)}) copy-start(pred[192,512]{1,0:T(8,128)(4,1)} %get-tuple-element.41) | copy-start | bytes 294916
  131.5 9.8 %copy-start.7 = (pred[192,512]{1,0:T(8,128)(4,1)S(1)}, pred[192,512]{1,0:T(8,128)(4,1)}, u32[]{:S(2)}) copy-start(pred[192,512]{1,0:T(8,128)(4,1)} %get-tuple-element.42) | copy-start | bytes 294916
  136.3 9.8 %copy-start.13 = (bf16[512,512]{0,1:T(8,128)(2,1)S(1)}, bf16[512,512]{0,1:T(8,128)(2,1)}, u32[]{:S(2)}) copy-start(bf16[512,512]{0,1:T(8,128)(2,1)} %copy.119) | copy-start | bytes 1572868
  150.6 8.4 %copy-start.12 = (bf16[512,512]{0,1:T(8,128)(2,1)S(1)}, bf16[512,512]{0,1:T(8,128)(2,1)}, u32[]{:S(2)}) copy-start(bf16[512,512]{0,1:T(8,128)(2,1)} %copy.117) | copy-start | bytes 1572868
  159.0 6.6 %copy-start.11 = (bf16[512,512]{0,1:T(8,128)(2,1)S(1)}, bf16[512,512]{0,1:T(8,128)(2,1)}, u32[]{:S(2)}) copy-start(bf16[512,512]{0,1:T(8,128)(2,1)} %copy.115) | copy-start | bytes 1572868
  172.1 7.1 %copy-start.10 = (bf16[512,512]{0,1:T(8,128)(2,1)S(1)}, bf16[512,512]{0,1:T(8,128)(2,1)}, u32[]{:S(2)}) copy-start(bf16[512,512]{0,1:T(8,128)(2,1)} %copy.113) | copy-start | bytes 1572868
  179.3 3.6 %copy-start.9 = (bf16[512,512]{0,1:T(8,128)(2,1)S(1)}, bf16[512,512]{0,1:T(8,128)(2,1)}, u32[]{:S(2)}) copy-start(bf16[512,512]{0,1:T(8,128)(2,1)} %copy.111) | copy-start | bytes 1572868
  185.1 5.6 %copy-start.8 = (bf16[512,512]{0,1:T(8,128)(2,1)S(1)}, bf16[512,512]{0,1:T(8,128)(2,1)}, u32[]{:S(2)}) copy-start(bf16[512,512]{0,1:T(8,128)(2,1)} %copy.109) | copy-start | bytes 1572868
  185.1 5.6 %copy-start.14 = (f32[4,5,192,128]{3,2,1,0:T(8,128)S(1)}, f32[4,5,192,128]{3,2,1,0:T(8,128)}, u32[]{:S(2)}) copy-start(f32[4,5,192,128]{3,2,1,0:T(8,128)} %fusion.20) | copy-start | bytes 5898244
  185.1 5.6 %copy-start.15 = (f32[4,5,192,128]{3,2,1,0:T(8,128)S(1)}, f32[4,5,192,128]{3,2,1,0:T(8,128)}, u32[]{:S(2)}) copy-start(f32[4,5,192,128]{3,2,1,0:T(8,128)} %fusion.22) | copy-start | bytes 5898244
  185.1 5.6 %copy-start.16 = (f32[4,5,192,128]{3,2,1,0:T(8,128)S(1)}, f32[4,5,192,128]{3,2,1,0:T(8,128)}, u32[]{:S(2)}) copy-start(f32[4,5,192,128]{3,2,1,0:T(8,128)} %fusion.24) | copy-start | bytes 5898244
Sparse Core Ops, SparseCore 0:
  9.6 48.5 all-gather.2
  60.5 43.8 all-gather.4
  210.5 29.1 reduce-scatter.1
where the time goes:
time: 247 us; the launch traced here: 246 us
  blocking collectives  63.4 us (26%)
  matrix products  62.3 us (25%)
  waiting for transfers between devices  53.3 us (22%)
  local copies, waits for them, and re-layouts  30.2 us (12%)
  other arithmetic  22.9 us (9%)
  between operations  14.1 us (6%)
    unnamed x1, blocking collectives  63.4 us
    dot_general x6, matrix products, attend(): jnp.einsum('hgqk,khd->hgqd', weights.astype(jnp.bfloat16), value_block, p...  29.7 us
    reduce_scatter x1, waiting for transfers between devices, shards(): lax.psum_scatter(jnp.dot(attended_values, out_weight, preferred_element_t...  29.3 us
    unnamed x50, local copies, waits for them, and re-layouts  23 us
    all_gather x1, waiting for transfers between devices, shards(): lax.all_gather(values, 'blk', axis=0, tiled=True)  22.5 us
    reduce_sum x3, other arithmetic, attend(): totals = totals * rescale + jnp.sum(weights, axis=-1)  21 us
    dot_general x6, matrix products, attend(): jnp.einsum('qhgd,khd->hgqk', query_rows, key_block, preferred_element_typ...  19.9 us
    dot_general x1, matrix products, shards(): jnp.dot(attended_values, out_weight, preferred_element_type=jnp.float32)  12.7 us
  transfers between devices with their start and end apart: 3, of which 2 were waited for; matrix products, arithmetic and copies ran while one was open for 4% of the time, Pallas kernels for 0%

commit v1 on v0

v1 whole, which is shorter than its diff:
```python
import functools
import math

import jax
import jax.numpy as jnp
from jax import lax
from jax.experimental import pallas as pl
from jax.experimental.pallas import tpu as pltpu
from jax.sharding import PartitionSpec as P

HEAD_WIDTH = 128
QUERY_PER_KEY = 5
GROUP = QUERY_PER_KEY * HEAD_WIDTH
EXP2_SCALE = math.log2(math.e) / math.sqrt(HEAD_WIDTH)
MASKED = -1e30
VMEM_LIMIT = 16 * 1024 * 1024
HEADER = 16
LAST_LAST = (((1,), (1,)), ((), ()))
FIRST_FIRST = (((0,), (0,)), ((), ()))


def ring_of_chips(chips):
    half = chips // 2
    if chips == 8:
        return [2 * z for z in range(half)] + [2 * z + 1 for z in reversed(range(half))]
    return list(range(half)) + list(reversed(range(half, chips)))


def ring_pairs(chips, step):
    ring = ring_of_chips(chips)
    return [
        (2 * ring[i] + core, 2 * ring[(i + step) % chips] + core)
        for i in range(chips)
        for core in range(2)
    ]


def fold(states, queries, keys, values, mask=None):
    out = []
    for state, q, k, v in zip(states, queries, keys, values):
        s = lax.dot_general(k, q, LAST_LAST, preferred_element_type=jnp.float32)
        if mask is not None:
            s = jnp.where(mask, s, MASKED)
        high = jnp.max(s, axis=0, keepdims=True)
        if state is not None:
            high = jnp.maximum(state[0], high)
        p = jnp.exp2((s - high) * EXP2_SCALE)
        totals = jnp.sum(p, axis=0, keepdims=True)
        sums = lax.dot_general(
            v, p.astype(jnp.bfloat16), FIRST_FIRST, preferred_element_type=jnp.float32
        )
        if state is not None:
            shrink = jnp.exp2((state[0] - high) * EXP2_SCALE)
            totals = state[1] * shrink + totals
            sums = state[2] * shrink + sums
        out.append((high, totals, sums))
    return out


def stacked_queries(q_ref, first_row, rows, first_column):
    return jnp.concatenate(
        [
            q_ref[
                pl.ds(first_row, rows),
                pl.ds(pl.multiple_of(first_column + g * HEAD_WIDTH, HEAD_WIDTH), HEAD_WIDTH),
            ]
            for g in range(QUERY_PER_KEY)
        ],
        axis=0,
    )


def attend_kernel(plan, *refs):
    heads, chunk = plan["heads"], plan["chunk"]
    owners, count = len(plan["owners"]), len(plan["members"])
    rows = QUERY_PER_KEY * chunk
    refs = list(refs)
    core_ref = refs.pop(0)
    q_refs = [refs.pop(0) for _ in range(owners)]
    mark_refs = [refs.pop(0) for _ in range(plan["marks"])]
    packets = [refs.pop(0) for _ in range(plan["packets"])]
    if plan["carried"]:
        in_ml, in_acc = refs.pop(0), refs.pop(0)
    if plan["last"]:
        out_refs = [refs.pop(0) for _ in range(owners)]
        ml_ref, acc_ref = refs.pop(0), refs.pop(0)
    else:
        ml_ref, acc_ref = refs.pop(0), refs.pop(0)
    early_ref, late_ref, head_ref, sems = refs

    places = plan["owner_headers"] + plan["headers"]
    sources = mark_refs + packets
    copies = []
    for i, (packet, row, column) in enumerate(places):
        copy = pltpu.make_async_copy(
            sources[packet].at[pl.ds(row, HEADER), pl.ds(column, HEAD_WIDTH)],
            head_ref.at[i],
            sems.at[2 * count + i],
        )
        copy.start()
        copies.append(copy)
    for copy in copies:
        copy.wait()
    numbers = [
        jnp.max(head_ref[i].astype(jnp.float32)).astype(jnp.int32) for i in range(len(places))
    ]
    owner_c, member_c = numbers[:owners], numbers[owners:]

    copies = []
    for j, (packet, row) in enumerate(plan["members"]):
        rank = sum((other < member_c[j]).astype(jnp.int32) for i, other in enumerate(member_c) if i != j)
        rank = jnp.clip(rank, 0, count - 1)
        for half, (ref, at) in enumerate(((early_ref, rank), (late_ref, count - 1 - rank))):
            copy = pltpu.make_async_copy(
                packets[packet].at[pl.ds(row + half * chunk, chunk)],
                ref.at[pl.ds(pl.multiple_of(at * chunk, chunk), chunk)],
                sems.at[2 * j + half],
            )
            copy.start()
            copies.append(copy)
    for copy in copies:
        copy.wait()

    def keys_of(ref, first, size):
        return (
            [ref[pl.ds(first, size), pl.ds(h * HEAD_WIDTH, HEAD_WIDTH)] for h in range(heads)],
            [ref[pl.ds(first, size), pl.ds((heads + h) * HEAD_WIDTH, HEAD_WIDTH)] for h in range(heads)],
        )

    def queries_of(i, half):
        base = core_ref[0] * (heads * GROUP) if plan["owners"][i] else 0
        return [stacked_queries(q_refs[i], half * chunk, chunk, base + h * GROUP) for h in range(heads)]

    def load(ml, acc, at):
        return [(ml[at + h][0:1], ml[at + h][1:2], acc[at + h]) for h in range(heads)]

    def store(states, at):
        for h, (high, totals, sums) in enumerate(states):
            ml_ref[at + h, 0:1] = high
            ml_ref[at + h, 1:2] = totals
            acc_ref[at + h] = sums

    tile = 2 * chunk

    def sweep(i, half, ref, at, full):
        def plain(t, carry):
            keys, values = keys_of(ref, pl.multiple_of(t * tile, tile), tile)
            store(fold(load(ml_ref, acc_ref, at), queries_of(i, half), keys, values), at)
            return carry

        lax.fori_loop(0, full // 2, plain, 0)
        if plan["own"]:
            first = (full // 2) * tile
            key_at = lax.broadcasted_iota(jnp.int32, (tile, rows), 0)
            query_at = lax.rem(lax.broadcasted_iota(jnp.int32, (tile, rows), 1), chunk)
            mask = key_at - query_at <= full * chunk - first
            keys, values = keys_of(ref, pl.multiple_of(first, tile), tile)
            store(fold(load(ml_ref, acc_ref, at), queries_of(i, half), keys, values, mask), at)
        else:

            @pl.when(full % 2 == 1)
            def _():
                keys, values = keys_of(ref, pl.multiple_of((full - 1) * chunk, chunk), chunk)
                store(fold(load(ml_ref, acc_ref, at), queries_of(i, half), keys, values), at)

    for i in range(owners):
        early_at, late_at = (2 * i) * heads, (2 * i + 1) * heads
        states = load(in_ml, in_acc, late_at) if plan["carried"] else [None] * heads
        keys_total = count * chunk
        cut = 480 if keys_total % 480 == 0 else 576 if keys_total % 576 == 0 else 512
        for first in range(0, keys_total, cut):
            keys, values = keys_of(early_ref, first, cut)
            states = fold(states, queries_of(i, 1), keys, values)
        store(states, late_at)
        if plan["carried"]:
            store(load(in_ml, in_acc, early_at), early_at)
        else:
            store(
                [
                    (
                        jnp.full((1, rows), MASKED, jnp.float32),
                        jnp.zeros((1, rows), jnp.float32),
                        jnp.zeros((HEAD_WIDTH, rows), jnp.float32),
                    )
                ]
                * heads,
                early_at,
            )
        below = sum((other < owner_c[i]).astype(jnp.int32) for other in member_c)
        above = sum((other > owner_c[i]).astype(jnp.int32) for other in member_c)
        most = count - 1 if plan["own"] else count
        sweep(i, 1, late_ref, late_at, jnp.clip(above, 0, most))
        sweep(i, 0, early_ref, early_at, jnp.clip(below, 0, most))
        if plan["last"]:
            for half, at in ((0, early_at), (1, late_at)):
                for h, (_, totals, sums) in enumerate(load(ml_ref, acc_ref, at)):
                    mixed = jnp.transpose(sums / totals).astype(out_refs[i].dtype)
                    for g in range(QUERY_PER_KEY):
                        out_refs[i][
                            half * chunk : (half + 1) * chunk,
                            h * GROUP + g * HEAD_WIDTH : h * GROUP + (g + 1) * HEAD_WIDTH,
                        ] = mixed[g * chunk : (g + 1) * chunk]


def attend(plan, core, queries, marks, packets, state):
    heads, chunk, count = plan["heads"], plan["chunk"], len(plan["members"])
    owners = len(plan["owners"])
    plan = dict(plan, marks=len(marks), packets=len(packets), carried=state is not None)
    rows = QUERY_PER_KEY * chunk
    slots = owners * 2 * heads
    vmem = pl.BlockSpec(memory_space=pltpu.VMEM)
    anywhere = pl.BlockSpec(memory_space=pl.ANY)
    ml_shape, acc_shape = (slots, 8, rows), (slots, HEAD_WIDTH, rows)
    scratch = [
        pltpu.VMEM((count * chunk, 2 * heads * HEAD_WIDTH), jnp.bfloat16),
        pltpu.VMEM((count * chunk, 2 * heads * HEAD_WIDTH), jnp.bfloat16),
        pltpu.VMEM((count + owners, HEADER, HEAD_WIDTH), jnp.bfloat16),
        pltpu.SemaphoreType.DMA((3 * count + owners,)),
    ]
    if plan["last"]:
        out_shape = [jax.ShapeDtypeStruct((2 * chunk, heads * GROUP), jnp.bfloat16)] * owners
        scratch = [pltpu.VMEM(ml_shape, jnp.float32), pltpu.VMEM(acc_shape, jnp.float32)] + scratch
    else:
        out_shape = [
            jax.ShapeDtypeStruct(ml_shape, jnp.float32),
            jax.ShapeDtypeStruct(acc_shape, jnp.float32),
        ]
    flops = 4 * owners * heads * rows * HEAD_WIDTH * count * chunk * 2
    return pl.pallas_call(
        functools.partial(attend_kernel, plan),
        out_shape=out_shape,
        in_specs=[pl.BlockSpec(memory_space=pltpu.SMEM)]
        + [vmem] * owners
        + [anywhere] * (len(marks) + len(packets))
        + [vmem] * (0 if state is None else 2),
        out_specs=[vmem] * len(out_shape),
        scratch_shapes=scratch,
        cost_estimate=pl.CostEstimate(
            flops=flops, bytes_accessed=4 << 20, transcendentals=flops // 512
        ),
        compiler_params=pltpu.CompilerParams(vmem_limit_bytes=VMEM_LIMIT),
        name="attend_last" if plan["last"] else "attend_first",
    )(core, *queries, *marks, *packets, *(state or ()))


def project_kernel(pick_ref, own_ref, other_ref, w_ref, out_ref, rows_ref):
    @pl.when(pl.program_id(0) == 0)
    def _():
        chunk, part = rows_ref.shape[0], own_ref.shape[1]
        at = pl.multiple_of(pick_ref[0] * chunk, chunk)
        own, other = own_ref[pl.ds(at, chunk)], other_ref[pl.ds(at, chunk)]
        first = pick_ref[1] == 0
        rows_ref[:, :part] = jnp.where(first, own, other)
        rows_ref[:, part:] = jnp.where(first, other, own)

    out_ref[...] = jnp.dot(
        rows_ref[...], w_ref[...], preferred_element_type=jnp.float32
    ).astype(out_ref.dtype)


def project(pick, own, other, out_weight, first, width, tile):
    chunk, depth = own.shape[0] // 2, out_weight.shape[0]
    whole = lambda j: (0, 0)
    return pl.pallas_call(
        project_kernel,
        out_shape=jax.ShapeDtypeStruct((chunk, width), jnp.bfloat16),
        grid=(width // tile,),
        in_specs=[
            pl.BlockSpec(memory_space=pltpu.SMEM),
            pl.BlockSpec(own.shape, whole),
            pl.BlockSpec(other.shape, whole),
            pl.BlockSpec((depth, tile), lambda j: (0, first // tile + j)),
        ],
        out_specs=pl.BlockSpec((chunk, tile), lambda j: (0, j)),
        scratch_shapes=[pltpu.VMEM((chunk, depth), jnp.bfloat16)],
        cost_estimate=pl.CostEstimate(
            flops=2 * chunk * depth * width, bytes_accessed=2 * depth * width, transcendentals=0
        ),
        compiler_params=pltpu.CompilerParams(vmem_limit_bytes=VMEM_LIMIT),
        name="project",
    )(pick, own, other, out_weight)


def after(value, *events):
    return lax.optimization_barrier((value, *events))[0]


def split_over_cores(count, queries, keys, values, c_rows):
    chips, half = count // 2, count // 4
    rows, chunk = queries.shape[0], queries.shape[0] // 2
    heads = keys.shape[1] // HEAD_WIDTH // 2
    core = lax.rem(lax.axis_index("blk"), 2).astype(jnp.int32)
    sibling = [(b, b ^ 1) for b in range(count)]
    clock, counter = ring_pairs(chips, 1), ring_pairs(chips, -1)
    width = heads * HEAD_WIDTH

    def of_core(k):
        return jnp.concatenate(
            [lax.dynamic_slice(x, (0, k * width), (rows, width)) for x in (keys, values)], axis=1
        )

    header = jnp.broadcast_to(c_rows, (HEADER, 2 * width))
    sent = jnp.concatenate([of_core(1 - core), header], axis=0)
    got = lax.ppermute(sent, "blk", sibling)
    packet = jnp.concatenate(
        [
            of_core(core),
            got[:rows],
            jnp.concatenate([header[:, :width], got[rows:, :width]], axis=1),
        ],
        axis=0,
    )
    q_sent = lax.dynamic_slice(queries, (0, (1 - core) * heads * GROUP), (rows, heads * GROUP))

    ups, downs = [packet], [packet]
    for r in range(half - 1):
        ups.append(lax.ppermute(ups[-1], "blk", clock))
        downs.append(lax.ppermute(downs[-1], "blk", counter))
        if r == 0:
            q_got = lax.ppermute(q_sent, "blk", sibling)
    far_up = lax.ppermute(ups[-1][:rows], "blk", clock)
    far_down = lax.ppermute(downs[-1][rows:], "blk", counter)

    def whole_packets(first, number):
        members = [(first + j, i * rows) for j in range(number) for i in range(2)]
        headers = [(1 + first + j, 2 * rows, i * width) for j in range(number) for i in range(2)]
        return members, headers

    shared = dict(heads=heads, chunk=chunk, owners=(True, False))
    owner_headers = [(0, 2 * rows, 0), (0, 2 * rows, width)]
    cores = core.reshape(1)
    near = [packet]
    for r in range(1, half - 1):
        near += [ups[r], downs[r]]
    members, headers = whole_packets(0, len(near))
    plan = dict(shared, own=True, last=False, members=members, headers=headers, owner_headers=owner_headers)
    state = attend(plan, cores, [queries, q_got], [packet], near, None)
    far = [ups[-1], downs[-1], far_up, far_down]
    members, headers = whole_packets(0, 2)
    members += [(2, 0), (3, 0)]
    headers += [(4, rows, 0), (4, rows, width)]
    plan = dict(shared, own=False, last=True, members=members, headers=headers, owner_headers=owner_headers)
    own, sibling_rows = attend(plan, cores, [queries, q_got], [packet], far, state)
    return own, lax.ppermute(sibling_rows, "blk", sibling), core


def one_head_a_device(count, queries, keys, values, c_rows):
    rows, chunk = queries.shape[0], queries.shape[0] // 2
    width = 2 * keys.shape[1]
    heads = keys.shape[1] // HEAD_WIDTH
    header = jnp.broadcast_to(c_rows, (HEADER, width))
    packet = jnp.concatenate([jnp.concatenate([keys, values], axis=1), header], axis=0)
    packets = lax.all_gather(packet, "blk", axis=0, tiled=True)
    size = rows + HEADER
    plan = dict(
        heads=heads,
        chunk=chunk,
        owners=(False,),
        own=True,
        last=True,
        members=[(0, j * size) for j in range(count)],
        headers=[(1, j * size + rows, 0) for j in range(count)],
        owner_headers=[(0, rows, 0)],
    )
    zero = jnp.zeros((1,), jnp.int32)
    return attend(plan, zero, [queries], [packet], [packets], None)[0]


def shards(count, inner, queries, keys, values, positions, out_weight):
    chunk = queries.shape[0] // 2
    heads = keys.shape[1] // HEAD_WIDTH
    c_rows = (positions[:1] // chunk).astype(jnp.bfloat16).reshape(1, 1)
    if heads % 2:
        attended = one_head_a_device(count, queries, keys, values, c_rows)
        partial = jnp.dot(attended, out_weight, preferred_element_type=jnp.float32)
        return lax.psum_scatter(
            partial.astype(jnp.bfloat16), "inner", scatter_dimension=0, tiled=True
        )
    own, other, core = split_over_cores(count, queries, keys, values, c_rows)
    mine = lax.axis_index("inner").astype(jnp.int32)
    sending, keeping = jnp.stack([1 - mine, core]), jnp.stack([mine, core])
    width = out_weight.shape[1]
    parts = 4
    step = width // parts
    received = []
    for j in range(parts):
        source = own if j < 2 else after(own, received[j - 2])
        sent = project(sending, source, other, out_weight, j * step, step, 256)
        received.append(lax.ppermute(sent, "inner", [(0, 1), (1, 0)]))
    kept = project(keeping, after(own, sent), other, out_weight, 0, width, 512)
    theirs = jnp.concatenate(received, axis=1)
    return (kept.astype(jnp.float32) + theirs.astype(jnp.float32)).astype(jnp.bfloat16)


def solution(mesh):
    placed = (P("blk", "inner"), P("blk", "inner"), P("blk", "inner"), P("blk"), P("inner", None))
    return jax.shard_map(
        functools.partial(shards, mesh.shape["blk"], mesh.shape["inner"]),
        mesh=mesh,
        in_specs=placed,
        out_specs=P(("blk", "inner"), None),
        check_vma=False,
    )
```

time: 247 us -> 118 us (0.48)
  blocking collectives: 63.4 us -> 0 us
  matrix products: 62.3 us -> 0 us
  Pallas kernels: 0 us -> 47.4 us
  other arithmetic: 22.9 us -> 1.39 us
  waiting for transfers between devices: 53.3 us -> 33.3 us
  starting transfers between devices: 0.08 us -> 14.2 us
  between operations: 14.1 us -> 2.14 us
  local copies, waits for them, and re-layouts: 30.2 us -> 19.3 us
    unnamed x1 -> x0, blocking collectives: 63.4 us -> none
    dot_general x13 -> x0, matrix products: 62.3 us -> none  [the longest x6 29.7 us: attend(): jnp.einsum('hgqk,khd->hgqd', weights.astype(jnp.bfloat16), value_block, p...]
    pallas_call x0 -> x7, Pallas kernels: none -> 47.4 us  [the longest x2 26.7 us: attend(): pl.pallas_call(functools.partial(attend_kernel, plan), out_shape=out_shap...]
    ppermute x0 -> x15, waiting for transfers between devices: none -> 33.3 us  [the longest x3 26.6 us: split_over_cores(): downs.append(lax.ppermute(downs[-1], 'blk', counter))]
    reduce_scatter x1 -> x0, waiting for transfers between devices: 29.3 us -> none  [shards(): lax.psum_scatter(jnp.dot(attended_values, out_weight, preferred_element_t...]
    all_gather x2 -> x0, waiting for transfers between devices: 22.5 us -> none  [the longest x1 22.5 us: shards(): lax.all_gather(values, 'blk', axis=0, tiled=True)]
    reduce_sum x3 -> x0, other arithmetic: 21 us -> none  [attend(): totals = totals * rescale + jnp.sum(weights, axis=-1)]
    ppermute x0 -> x15, starting transfers between devices: none -> 14.2 us  [the longest x3 5.99 us: split_over_cores(): downs.append(lax.ppermute(downs[-1], 'blk', counter))]
  transfers between devices with their start and end apart: 3 -> 15, of which waited for: 2 -> 7; matrix products, arithmetic and copies ran while one was open for 4% -> 0% of each run, Pallas kernels for 0% -> 29%
where the time goes in v1:
time: 118 us
  Pallas kernels  47.4 us (40%)
  waiting for transfers between devices  33.3 us (28%)
  local copies, waits for them, and re-layouts  19.3 us (16%)
  starting transfers between devices  14.2 us (12%)
  between operations  2.14 us (2%)
  other arithmetic  1.39 us (1%)
    pallas_call x2, Pallas kernels, attend(): pl.pallas_call(functools.partial(attend_kernel, plan), out_shape=out_shap...  26.7 us
    ppermute x3, waiting for transfers between devices, split_over_cores(): downs.append(lax.ppermute(downs[-1], 'blk', counter))  26.6 us
    pallas_call x5, Pallas kernels, project(): pl.pallas_call(project_kernel, out_shape=jax.ShapeDtypeStruct((chunk, wid...  20.6 us
    unnamed x6, local copies, waits for them, and re-layouts  16.9 us
    ppermute x3, starting transfers between devices, split_over_cores(): downs.append(lax.ppermute(downs[-1], 'blk', counter))  5.99 us
    ppermute x4, starting transfers between devices, shards(): received.append(lax.ppermute(sent, 'inner', [(0, 1), (1, 0)]))  4.29 us
    ppermute x4, waiting for transfers between devices, shards(): received.append(lax.ppermute(sent, 'inner', [(0, 1), (1, 0)]))  3.8 us
  transfers between devices with their start and end apart: 15, of which 7 were waited for; matrix products, arithmetic and copies ran while one was open for 0% of the time, Pallas kernels for 29%

profile of v1, /device:TPU:0, one launch (start us, length us, event | category | flops | bytes accessed | tf_op | source)
XLA Modules:
  0.0 117.7 jit_solution(16242258278919945036)
XLA Ops:
  0.0 0.0 copy-start.2
  0.0 1.3 %slice.16 = s32[1]{0:T(128)} slice(s32[192]{0:T(256)} %param.8), slice={[0:1]} | slice | bytes 8 | tf_op jit(solution)/shard_map/slice | solution.py:372
  3.2 1.1 constant_dynamic-slice_fusion.2
  4.3 0.5 collective-permute-start.1
  4.9 1.1 collective-permute-done.1
  6.0 2.9 %collective-permute-start.5 = (bf16[400,512]{1,0:T(8,128)(2,1)S(1)}, bf16[400,512]{1,0:T(8,128)(2,1)S(1)}, u32[]{:S(2)}, u32[]{:S(2)}) collective-permute-start(bf16[400,512]{1,0:T(8,128)(2,1)S(1)} %fusion.3.refs_3_.refs_4_), channel_id=1, source_target_pairs={{0,4},{2,6},{8,0},{10,2},{16,8},{18,10},{24,16},{26,18},{28,24},{3... | collective-permute-start | bytes 1228808 | tf_op jit(solution)/shard_map/ppermute | solution.py:318
  9.0 0.1 collective-permute-start.2
  9.1 9.7 %collective-permute-done.5.refs_6_ = bf16[400,512]{1,0:T(8,128)(2,1)S(1)} collective-permute-done((bf16[400,512]{1,0:T(8,128)(2,1)S(1)}, bf16[400,512]{1,0:T(8,128)(2,1)S(1)}, u32[]{:S(2)}, u32[]{:S(2)}) %collective-permute-start.5) | collective-permute-done | bytes 409632 | tf_op jit(solution)/shard_map/ppermute | solution.py:318
  18.8 1.7 %collective-permute-start.6 = (bf16[400,512]{1,0:T(8,128)(2,1)S(1)}, bf16[400,512]{1,0:T(8,128)(2,1)S(1)}, u32[]{:S(2)}, u32[]{:S(2)}) collective-permute-start(bf16[400,512]{1,0:T(8,128)(2,1)S(1)} %collective-permute-done.5.refs_6_), channel_id=1, source_target_pairs={{0,4},{2,6},{8,0},{10,2},{16,8},{18,10},{24,16},{26,18},{28,24},{3... | collective-permute-start | bytes 1228808 | tf_op jit(solution)/shard_map/ppermute | solution.py:318
  20.5 0.0 collective-permute-done.2.refs_5_
  20.5 0.3 collective-permute-start.3
  20.8 0.0 copy-done.2
  20.9 0.1 collective-permute-start
  20.9 8.8 %collective-permute-done.6.refs_8_ = bf16[400,512]{1,0:T(8,128)(2,1)S(1)} collective-permute-done((bf16[400,512]{1,0:T(8,128)(2,1)S(1)}, bf16[400,512]{1,0:T(8,128)(2,1)S(1)}, u32[]{:S(2)}, u32[]{:S(2)}) %collective-permute-start.6) | collective-permute-done | bytes 409632 | tf_op jit(solution)/shard_map/ppermute | solution.py:318
  29.8 1.4 %collective-permute-start.7 = (bf16[400,512]{1,0:T(8,128)(2,1)S(1)}, bf16[400,512]{1,0:T(8,128)(2,1)S(1)}, u32[]{:S(2)}, u32[]{:S(2)}) collective-permute-start(bf16[400,512]{1,0:T(8,128)(2,1)S(1)} %collective-permute-done.6.refs_8_), channel_id=1, source_target_pairs={{0,4},{2,6},{8,0},{10,2},{16,8},{18,10},{24,16},{26,18},{28,24},{3... | collective-permute-start | bytes 1228808 | tf_op jit(solution)/shard_map/ppermute | solution.py:318
  31.2 0.0 collective-permute-done.3.refs_7_
  31.2 0.7 collective-permute-start.4
  31.8 8.1 %collective-permute-done.7.refs_5_ = bf16[400,512]{1,0:T(8,128)(2,1)S(1)} collective-permute-done((bf16[400,512]{1,0:T(8,128)(2,1)S(1)}, bf16[400,512]{1,0:T(8,128)(2,1)S(1)}, u32[]{:S(2)}, u32[]{:S(2)}) %collective-permute-start.7) | collective-permute-done | bytes 409632 | tf_op jit(solution)/shard_map/ppermute | solution.py:318
  39.9 1.1 collective-permute-start.9
  41.0 0.0 collective-permute-done.4.refs_4_
  41.0 1.1 collective-permute-start.8
  42.1 0.0 collective-permute-done.refs_2_
  42.1 16.5 %attend_first.1 = (f32[8,8,480]{2,1,0:T(8,128)S(1)}, f32[8,128,480]{2,1,0:T(8,128)S(1)}) custom-call(s32[1]{0:T(128)} %bitcast.1.refs_0_, bf16[192,2560]{1,0:T(8,128)(2,1)S(1)} %copy-done.2, bf16[192,1280]{1,0:T(8,128)(2,1)S(1)} %collective-permute-done.refs_2_, bf16[400,512]{1,0:T(8,128)(2,1)S(1)} %fusion.3.refs_3_.refs_4_, ...), custom_call_target="tpu_custom_call" | custom-call | flops 1887436800 | bytes 4194304 | tf_op jit(solution)/shard_map/attend_first/pallas_call | solution.py:229
  58.6 0.0 collective-permute-done.8.refs_6_
  58.6 0.0 collective-permute-done.9.refs_7_
  58.6 10.2 %attend_last.1 = (bf16[192,1280]{1,0:T(8,128)(2,1)S(1)}, bf16[192,1280]{1,0:T(8,128)(2,1)S(1)}) custom-call(s32[1]{0:T(128)} %bitcast.1.refs_0_, bf16[192,2560]{1,0:T(8,128)(2,1)S(1)} %copy-done.2, bf16[192,1280]{1,0:T(8,128)(2,1)S(1)} %collective-permute-done.refs_2_, bf16[400,512]{1,0:T(8,128)(2,1)S(1)} %fusion.3.refs_3_.refs_4_, ...), custom_call_target="tpu_custom_call" | custom-call | flops 1132462080 | bytes 4194304 | tf_op jit(solution)/shard_map/attend_last/pallas_call | solution.py:229
  68.8 0.1 collective-permute-start.10
  68.9 0.1 pad_add_fusion.1.pick_ref
  69.0 1.8 %collective-permute-done.10.other_ref = bf16[192,1280]{1,0:T(8,128)(2,1)S(1)} collective-permute-done((bf16[192,1280]{1,0:T(8,128)(2,1)S(1)}, bf16[192,1280]{1,0:T(8,128)(2,1)S(1)}, u32[]{:S(2)}, u32[]{:S(2)}) %collective-permute-start.10) | collective-permute-done | bytes 491552 | tf_op jit(solution)/shard_map/ppermute | solution.py:344
  70.8 0.0 copy-start
  70.8 8.5 %copy-done = bf16[2560,5120]{1,0:T(8,128)(2,1)S(1)} copy-done((bf16[2560,5120]{1,0:T(8,128)(2,1)S(1)}, bf16[2560,5120]{1,0:T(8,128)(2,1)}, u32[]{:S(2)}) %copy-start) | copy-done | bytes 26214424
  79.2 3.2 %project.8 = bf16[96,1280]{1,0:T(8,128)(2,1)S(1)} custom-call(s32[2]{0:T(128)S(1)} %pad_add_fusion.1.pick_ref, bf16[192,1280]{1,0:T(8,128)(2,1)S(1)} %get-tuple-element.18.own_ref, bf16[192,1280]{1,0:T(8,128)(2,1)S(1)} %collective-permute-done.10.other_ref, bf16[2560,5120]{1,0:T(8,128)(2,1)S(1)} %copy-done), custom_call_target="tpu_custom_call" | custom-call | flops 629145600 | bytes 6553600 | tf_op jit(solution)/shard_map/project/pallas_call | solution.py:264
  82.4 1.1 collective-permute-start.12
  83.5 3.2 %project.5 = bf16[96,1280]{1,0:T(8,128)(2,1)S(1)} custom-call(s32[2]{0:T(128)S(1)} %pad_add_fusion.1.pick_ref, bf16[192,1280]{1,0:T(8,128)(2,1)S(1)} %get-tuple-element.18.own_ref, bf16[192,1280]{1,0:T(8,128)(2,1)S(1)} %collective-permute-done.10.other_ref, bf16[2560,5120]{1,0:T(8,128)(2,1)S(1)} %copy-done), custom_call_target="tpu_custom_call" | custom-call | flops 629145600 | bytes 6553600 | tf_op jit(solution)/shard_map/project/pallas_call | solution.py:264
  86.6 1.1 collective-permute-start.11
  87.7 3.5 %collective-permute-done.12 = bf16[96,1280]{1,0:T(8,128)(2,1)S(1)} collective-permute-done((bf16[96,1280]{1,0:T(8,128)(2,1)S(1)}, bf16[96,1280]{1,0:T(8,128)(2,1)S(1)}, u32[]{:S(2)}, u32[]{:S(2)}) %collective-permute-start.12) | collective-permute-done | bytes 245792 | tf_op jit(solution)/shard_map/ppermute | solution.py:389
  91.3 3.2 %project.9 = bf16[96,1280]{1,0:T(8,128)(2,1)S(1)} custom-call(s32[2]{0:T(128)S(1)} %pad_add_fusion.1.pick_ref, bf16[192,1280]{1,0:T(8,128)(2,1)S(1)} %get-tuple-element.18.own_ref, bf16[192,1280]{1,0:T(8,128)(2,1)S(1)} %collective-permute-done.10.other_ref, bf16[2560,5120]{1,0:T(8,128)(2,1)S(1)} %copy-done), custom_call_target="tpu_custom_call" | custom-call | flops 629145600 | bytes 6553600 | tf_op jit(solution)/shard_map/project/pallas_call | solution.py:264
  94.4 1.1 collective-permute-start.13
  95.5 0.3 collective-permute-done.11
  95.8 3.2 %project.6 = bf16[96,1280]{1,0:T(8,128)(2,1)S(1)} custom-call(s32[2]{0:T(128)S(1)} %pad_add_fusion.1.pick_ref, bf16[192,1280]{1,0:T(8,128)(2,1)S(1)} %get-tuple-element.18.own_ref, bf16[192,1280]{1,0:T(8,128)(2,1)S(1)} %collective-permute-done.10.other_ref, bf16[2560,5120]{1,0:T(8,128)(2,1)S(1)} %copy-done), custom_call_target="tpu_custom_call" | custom-call | flops 629145600 | bytes 6553600 | tf_op jit(solution)/shard_map/project/pallas_call | solution.py:264
  98.9 1.1 collective-permute-start.14
  100.0 0.1 pad_add_fusion.pick_ref
  100.1 0.0 copy-start.1
  100.1 8.5 %copy-done.1 = bf16[2560,5120]{1,0:T(8,128)(2,1)S(1)} copy-done((bf16[2560,5120]{1,0:T(8,128)(2,1)S(1)}, bf16[2560,5120]{1,0:T(8,128)(2,1)}, u32[]{:S(2)}) %copy-start.1) | copy-done | bytes 26214424
  108.5 7.9 %project.7 = bf16[96,5120]{1,0:T(8,128)(2,1)S(1)} custom-call(s32[2]{0:T(128)S(1)} %pad_add_fusion.pick_ref, bf16[192,1280]{1,0:T(8,128)(2,1)S(1)} %get-tuple-element.18.own_ref, bf16[192,1280]{1,0:T(8,128)(2,1)S(1)} %collective-permute-done.10.other_ref, bf16[2560,5120]{1,0:T(8,128)(2,1)S(1)} %copy-done.1), custom_call_target="tpu_custom_call" | custom-call | flops 2516582400 | bytes 26214400 | tf_op jit(solution)/shard_map/project/pallas_call | solution.py:264
  116.5 0.0 collective-permute-done.13
  116.5 0.0 collective-permute-done.14
  116.5 1.2 %add_convert_fusion = bf16[96,5120]{1,0:T(8,128)(2,1)} fusion(bf16[96,5120]{1,0:T(8,128)(2,1)S(1)} %project.7, bf16[96,1280]{1,0:T(8,128)(2,1)S(1)} %collective-permute-done.14, bf16[96,1280]{1,0:T(8,128)(2,1)S(1)} %collective-permute-done.13, bf16[96,1280]{1,0:T(8,128)(2,1)S(1)} %collective-permute-done.11, bf16[96,1280]{1,0:T(8,128)(2,1)S(1)} %collective-permute-done.12), kind=kLoop, calls=%fused_computation | loop fusion | flops 5406720 | bytes 2949120 | tf_op jit(solution)/shard_map/convert_element_type | solution.py:392
  (7 shorter events, 0.1 us)
Async XLA Ops:
  0.0 20.8 %copy-start.2 = (bf16[192,2560]{1,0:T(8,128)(2,1)S(1)}, bf16[192,2560]{1,0:T(8,128)(2,1)}, u32[]{:S(2)}) copy-start(bf16[192,2560]{1,0:T(8,128)(2,1)} %refs_1_.3) | copy-start | bytes 2949124
  4.3 1.6 %collective-permute-start.1 = (bf16[208,512]{1,0:T(8,128)(2,1)S(1)}, bf16[208,512]{1,0:T(8,128)(2,1)S(1)}, u32[]{:S(2)}, u32[]{:S(2)}) collective-permute-start(bf16[208,512]{1,0:T(8,128)(2,1)S(1)} %fusion.4), channel_id=1, source_target_pairs={{0,2},{2,0},{4,6},{6,4},{8,10},{10,8},{12,14},{14,12},{16,18},{18,... | collective-permute-start | bytes 638984 | tf_op jit(solution)/shard_map/ppermute | solution.py:304
  6.0 12.8 %collective-permute-start.5 = (bf16[400,512]{1,0:T(8,128)(2,1)S(1)}, bf16[400,512]{1,0:T(8,128)(2,1)S(1)}, u32[]{:S(2)}, u32[]{:S(2)}) collective-permute-start(bf16[400,512]{1,0:T(8,128)(2,1)S(1)} %fusion.3.refs_3_.refs_4_), channel_id=1, source_target_pairs={{0,4},{2,6},{8,0},{10,2},{16,8},{18,10},{24,16},{26,18},{28,24},{3... | collective-permute-start | bytes 1228808 | tf_op jit(solution)/shard_map/ppermute | solution.py:318
  9.0 11.5 %collective-permute-start.2 = (bf16[400,512]{1,0:T(8,128)(2,1)S(1)}, bf16[400,512]{1,0:T(8,128)(2,1)S(1)}, u32[]{:S(2)}, u32[]{:S(2)}) collective-permute-start(bf16[400,512]{1,0:T(8,128)(2,1)S(1)} %fusion.3.refs_3_.refs_4_), channel_id=1, source_target_pairs={{0,8},{2,10},{8,16},{10,18},{16,24},{18,26},{24,28},{26,30},{28,20... | collective-permute-start | bytes 1228808 | tf_op jit(solution)/shard_map/ppermute | solution.py:317
  18.8 11.0 %collective-permute-start.6 = (bf16[400,512]{1,0:T(8,128)(2,1)S(1)}, bf16[400,512]{1,0:T(8,128)(2,1)S(1)}, u32[]{:S(2)}, u32[]{:S(2)}) collective-permute-start(bf16[400,512]{1,0:T(8,128)(2,1)S(1)} %collective-permute-done.5.refs_6_), channel_id=1, source_target_pairs={{0,4},{2,6},{8,0},{10,2},{16,8},{18,10},{24,16},{26,18},{28,24},{3... | collective-permute-start | bytes 1228808 | tf_op jit(solution)/shard_map/ppermute | solution.py:318
  20.5 10.7 %collective-permute-start.3 = (bf16[400,512]{1,0:T(8,128)(2,1)S(1)}, bf16[400,512]{1,0:T(8,128)(2,1)S(1)}, u32[]{:S(2)}, u32[]{:S(2)}) collective-permute-start(bf16[400,512]{1,0:T(8,128)(2,1)S(1)} %collective-permute-done.2.refs_5_), channel_id=1, source_target_pairs={{0,8},{2,10},{8,16},{10,18},{16,24},{18,26},{24,28},{26,30},{28,20... | collective-permute-start | bytes 1228808 | tf_op jit(solution)/shard_map/ppermute | solution.py:317
  20.9 21.2 %collective-permute-start = (bf16[192,1280]{1,0:T(8,128)(2,1)S(1)}, bf16[192,1280]{1,0:T(8,128)(2,1)S(1)}, u32[]{:S(2)}, u32[]{:S(2)}) collective-permute-start(bf16[192,1280]{1,0:T(8,128)(2,1)S(1)} %constant_dynamic-slice_fusion.4), channel_id=1, source_target_pairs={{0,2},{2,0},{4,6},{6,4},{8,10},{10,8},{12,14},{14,12},{16,18},{18,... | collective-permute-start | bytes 1474568 | tf_op jit(solution)/shard_map/ppermute | solution.py:320
  29.8 10.1 %collective-permute-start.7 = (bf16[400,512]{1,0:T(8,128)(2,1)S(1)}, bf16[400,512]{1,0:T(8,128)(2,1)S(1)}, u32[]{:S(2)}, u32[]{:S(2)}) collective-permute-start(bf16[400,512]{1,0:T(8,128)(2,1)S(1)} %collective-permute-done.6.refs_8_), channel_id=1, source_target_pairs={{0,4},{2,6},{8,0},{10,2},{16,8},{18,10},{24,16},{26,18},{28,24},{3... | collective-permute-start | bytes 1228808 | tf_op jit(solution)/shard_map/ppermute | solution.py:318
  31.2 9.8 %collective-permute-start.4 = (bf16[400,512]{1,0:T(8,128)(2,1)S(1)}, bf16[400,512]{1,0:T(8,128)(2,1)S(1)}, u32[]{:S(2)}, u32[]{:S(2)}) collective-permute-start(bf16[400,512]{1,0:T(8,128)(2,1)S(1)} %collective-permute-done.3.refs_7_), channel_id=1, source_target_pairs={{0,8},{2,10},{8,16},{10,18},{16,24},{18,26},{24,28},{26,30},{28,20... | collective-permute-start | bytes 1228808 | tf_op jit(solution)/shard_map/ppermute | solution.py:317
  39.9 18.7 %collective-permute-start.9 = (bf16[208,512]{1,0:T(8,128)(2,1)S(1)}, bf16[208,512]{1,0:T(8,128)(2,1)S(1)}, u32[]{:S(2)}, u32[]{:S(2)}) collective-permute-start(bf16[208,512]{1,0:T(8,128)(2,1)S(1)} %slice.24), channel_id=1, source_target_pairs={{0,4},{2,6},{8,0},{10,2},{16,8},{18,10},{24,16},{26,18},{28,24},{3... | collective-permute-start | bytes 638984 | tf_op jit(solution)/shard_map/ppermute | solution.py:322
  41.0 17.6 %collective-permute-start.8 = (bf16[192,512]{1,0:T(8,128)(2,1)S(1)}, bf16[192,512]{1,0:T(8,128)(2,1)S(1)}, u32[]{:S(2)}, u32[]{:S(2)}) collective-permute-start(bf16[192,512]{1,0:T(8,128)(2,1)S(1)} %slice.23), channel_id=1, source_target_pairs={{0,8},{2,10},{8,16},{10,18},{16,24},{18,26},{24,28},{26,30},{28,20... | collective-permute-start | bytes 589832 | tf_op jit(solution)/shard_map/ppermute | solution.py:321
  68.8 1.9 %collective-permute-start.10 = (bf16[192,1280]{1,0:T(8,128)(2,1)S(1)}, bf16[192,1280]{1,0:T(8,128)(2,1)S(1)}, u32[]{:S(2)}, u32[]{:S(2)}) collective-permute-start(bf16[192,1280]{1,0:T(8,128)(2,1)S(1)} %get-tuple-element.15), channel_id=1, source_target_pairs={{0,2},{2,0},{4,6},{6,4},{8,10},{10,8},{12,14},{14,12},{16,18},{18,... | collective-permute-start | bytes 1474568 | tf_op jit(solution)/shard_map/ppermute | solution.py:344
  70.8 8.5 %copy-start = (bf16[2560,5120]{1,0:T(8,128)(2,1)S(1)}, bf16[2560,5120]{1,0:T(8,128)(2,1)}, u32[]{:S(2)}) copy-start(bf16[2560,5120]{1,0:T(8,128)(2,1)} %w_ref.9) | copy-start | bytes 78643200
  82.4 8.9 %collective-permute-start.12 = (bf16[96,1280]{1,0:T(8,128)(2,1)S(1)}, bf16[96,1280]{1,0:T(8,128)(2,1)S(1)}, u32[]{:S(2)}, u32[]{:S(2)}) collective-permute-start(bf16[96,1280]{1,0:T(8,128)(2,1)S(1)} %project.8), channel_id=1, source_target_pairs={{0,1},{1,0},{2,3},{3,2},{4,5},{5,4},{6,7},{7,6},{8,9},{9,8},{10,11... | collective-permute-start | bytes 737288 | tf_op jit(solution)/shard_map/ppermute | solution.py:389
  86.6 9.1 %collective-permute-start.11 = (bf16[96,1280]{1,0:T(8,128)(2,1)S(1)}, bf16[96,1280]{1,0:T(8,128)(2,1)S(1)}, u32[]{:S(2)}, u32[]{:S(2)}) collective-permute-start(bf16[96,1280]{1,0:T(8,128)(2,1)S(1)} %project.5), channel_id=1, source_target_pairs={{0,1},{1,0},{2,3},{3,2},{4,5},{5,4},{6,7},{7,6},{8,9},{9,8},{10,11... | collective-permute-start | bytes 737288 | tf_op jit(solution)/shard_map/ppermute | solution.py:389
  94.4 22.1 %collective-permute-start.13 = (bf16[96,1280]{1,0:T(8,128)(2,1)S(1)}, bf16[96,1280]{1,0:T(8,128)(2,1)S(1)}, u32[]{:S(2)}, u32[]{:S(2)}) collective-permute-start(bf16[96,1280]{1,0:T(8,128)(2,1)S(1)} %project.9), channel_id=1, source_target_pairs={{0,1},{1,0},{2,3},{3,2},{4,5},{5,4},{6,7},{7,6},{8,9},{9,8},{10,11... | collective-permute-start | bytes 737288 | tf_op jit(solution)/shard_map/ppermute | solution.py:389
  98.9 17.6 %collective-permute-start.14 = (bf16[96,1280]{1,0:T(8,128)(2,1)S(1)}, bf16[96,1280]{1,0:T(8,128)(2,1)S(1)}, u32[]{:S(2)}, u32[]{:S(2)}) collective-permute-start(bf16[96,1280]{1,0:T(8,128)(2,1)S(1)} %project.6), channel_id=1, source_target_pairs={{0,1},{1,0},{2,3},{3,2},{4,5},{5,4},{6,7},{7,6},{8,9},{9,8},{10,11... | collective-permute-start | bytes 737288 | tf_op jit(solution)/shard_map/ppermute | solution.py:389
  100.1 8.5 %copy-start.1 = (bf16[2560,5120]{1,0:T(8,128)(2,1)S(1)}, bf16[2560,5120]{1,0:T(8,128)(2,1)}, u32[]{:S(2)}) copy-start(bf16[2560,5120]{1,0:T(8,128)(2,1)} %w_ref.9) | copy-start | bytes 78643200

commit v2 on v1

v2 whole, which is shorter than its diff:
```python
import functools
import math

import jax
import jax.numpy as jnp
from jax import lax
from jax.experimental import pallas as pl
from jax.experimental.pallas import tpu as pltpu
from jax.sharding import PartitionSpec as P

HEAD_WIDTH = 128
QUERY_PER_KEY = 5
GROUP = QUERY_PER_KEY * HEAD_WIDTH
EXP2_SCALE = math.log2(math.e) / math.sqrt(HEAD_WIDTH)
MASKED = -1e30
VMEM_LIMIT = 16 * 1024 * 1024
HEADER = 16
LAST_LAST = (((1,), (1,)), ((), ()))


def ring_of_chips(chips):
    half = chips // 2
    if chips == 8:
        return [2 * z for z in range(half)] + [2 * z + 1 for z in reversed(range(half))]
    return list(range(half)) + list(reversed(range(half, chips)))


def ring_pairs(chips, step):
    ring = ring_of_chips(chips)
    return [
        (2 * ring[i] + core, 2 * ring[(i + step) % chips] + core)
        for i in range(chips)
        for core in range(2)
    ]


def fold(carried, q, keys, values, mask=None):
    scores = [lax.dot_general(k, q, LAST_LAST, preferred_element_type=jnp.float32) for k in keys]
    if mask is not None:
        scores = [jnp.where(mask, s, MASKED) for s in scores]
    high = functools.reduce(jnp.maximum, [jnp.max(s, axis=0, keepdims=True) for s in scores])
    if carried is not None:
        high = jnp.maximum(carried[0], high)
    sums = None
    for s, v in zip(scores, values):
        p = jnp.exp2((s - high) * EXP2_SCALE).astype(jnp.bfloat16)
        part = jnp.dot(v, p, preferred_element_type=jnp.float32)
        sums = part if sums is None else sums + part
    if carried is not None:
        sums = carried[1] * jnp.exp2((carried[0] - high) * EXP2_SCALE) + sums
    return high, sums


def stacked_queries(q_ref, first_row, rows, first_column):
    return jnp.concatenate(
        [
            q_ref[
                pl.ds(first_row, rows),
                pl.ds(pl.multiple_of(first_column + g * HEAD_WIDTH, HEAD_WIDTH), HEAD_WIDTH),
            ]
            for g in range(QUERY_PER_KEY)
        ],
        axis=0,
    )


def my_core():
    return lax.rem(lax.axis_index("blk"), 2).astype(jnp.int32)


def attend_kernel(plan, *refs):
    heads, chunk = plan["heads"], plan["chunk"]
    owners, count = len(plan["owners"]), len(plan["members"])
    rows, tile = QUERY_PER_KEY * chunk, 2 * chunk
    tiles = count // 2
    refs = list(refs)
    q_refs = [refs.pop(0) for _ in range(owners)]
    mark_refs = [refs.pop(0) for _ in range(plan["marks"])]
    packets = [refs.pop(0) for _ in range(plan["packets"])]
    if plan["carried"]:
        in_high, in_sums = refs.pop(0), refs.pop(0)
    high_ref, sums_ref = refs.pop(0), refs.pop(0)
    if plan["last"]:
        out_refs = [refs.pop(0) for _ in range(owners)]
    early_ref, late_ref, turned_ref, head_ref, sems = refs

    places = plan["owner_headers"] + plan["headers"]
    sources = mark_refs + packets
    copies = []
    for i, (packet, row, column) in enumerate(places):
        copy = pltpu.make_async_copy(
            sources[packet].at[pl.ds(row, HEADER), pl.ds(column, HEAD_WIDTH)],
            head_ref.at[i],
            sems.at[2 * count + i],
        )
        copy.start()
        copies.append(copy)
    for copy in copies:
        copy.wait()
    numbers = [
        jnp.max(head_ref[i].astype(jnp.float32)).astype(jnp.int32) for i in range(len(places))
    ]
    owner_c, member_c = numbers[:owners], numbers[owners:]

    copies = []
    for j, (packet, row) in enumerate(plan["members"]):
        rank = sum((other < member_c[j]).astype(jnp.int32) for i, other in enumerate(member_c) if i != j)
        rank = jnp.clip(rank, 0, count - 1)
        for half, (ref, at) in enumerate(((early_ref, rank), (late_ref, count - 1 - rank))):
            copy = pltpu.make_async_copy(
                packets[packet].at[pl.ds(row + half * chunk, chunk)],
                ref.at[pl.ds(pl.multiple_of(at * chunk, chunk), chunk)],
                sems.at[2 * j + half],
            )
            copy.start()
            copies.append(copy)
    for copy in copies:
        copy.wait()

    turned_ref[:, HEAD_WIDTH:] = jnp.ones((turned_ref.shape[0], HEADER, tile), jnp.bfloat16)
    key_refs = (early_ref, late_ref)

    def slot(half, h, t):
        return (half * heads + h) * tiles + t

    for half in range(2):
        for h in range(heads):
            for t in range(tiles):
                v = key_refs[half][
                    t * tile : (t + 1) * tile, (heads + h) * HEAD_WIDTH : (heads + h + 1) * HEAD_WIDTH
                ]
                turned_ref[slot(half, h, t), :HEAD_WIDTH] = jnp.transpose(v)

    def keys_of(half, h, t):
        first = t * tile if isinstance(t, int) else pl.multiple_of(t * tile, tile)
        k = key_refs[half][pl.ds(first, tile), h * HEAD_WIDTH : (h + 1) * HEAD_WIDTH]
        return k, turned_ref[slot(half, h, t)]

    def queries_of(i, half, h):
        base = my_core() * (heads * GROUP) if plan["owners"][i] else 0
        return stacked_queries(q_refs[i], half * chunk, chunk, base + h * GROUP)

    def state_at(i, half, h):
        return (2 * i + half) * heads + h

    def store(at, state):
        high_ref[at], sums_ref[at] = state

    for h in range(heads):
        for i in range(owners):
            at = state_at(i, 1, h)
            state = (in_high[at], in_sums[at]) if plan["carried"] else None
            for first in range(0, tiles, 5):
                blocks = [keys_of(0, h, t) for t in range(first, min(first + 5, tiles))]
                state = fold(state, queries_of(i, 1, h), [k for k, _ in blocks], [v for _, v in blocks])
            store(at, state)
            at = state_at(i, 0, h)
            if plan["carried"]:
                store(at, (in_high[at], in_sums[at]))
            else:
                high_ref[at] = jnp.full(high_ref.shape[1:], MASKED, jnp.float32)
                sums_ref[at] = jnp.zeros(sums_ref.shape[1:], jnp.float32)

    def sweep(i, half, full):
        def block(t, mask):
            for h in range(heads):
                at = state_at(i, half, h)
                k, v = keys_of(half, h, t)
                store(at, fold((high_ref[at], sums_ref[at]), queries_of(i, half, h), [k], [v], mask))

        def plain(t, carry):
            block(t, None)
            return carry

        lax.fori_loop(0, full // 2, plain, 0)
        key_at = lax.broadcasted_iota(jnp.int32, (tile, rows), 0)
        if plan["own"]:
            query_at = lax.rem(lax.broadcasted_iota(jnp.int32, (tile, rows), 1), chunk)
            block(full // 2, key_at - query_at <= lax.rem(full, 2) * chunk)
        else:

            @pl.when(lax.rem(full, 2) == 1)
            def _():
                block(full // 2, key_at < chunk)

    for i in range(owners):
        below = sum((other < owner_c[i]).astype(jnp.int32) for other in member_c)
        above = sum((other > owner_c[i]).astype(jnp.int32) for other in member_c)
        most = count - 1 if plan["own"] else count
        sweep(i, 1, jnp.clip(above, 0, most))
        sweep(i, 0, jnp.clip(below, 0, most))
        if plan["last"]:
            for half in range(2):
                for h in range(heads):
                    sums = sums_ref[state_at(i, half, h)]
                    mixed = sums[:HEAD_WIDTH] / sums[HEAD_WIDTH : HEAD_WIDTH + 1]
                    mixed = jnp.transpose(mixed).astype(out_refs[i].dtype)
                    for g in range(QUERY_PER_KEY):
                        out_refs[i][
                            half * chunk : (half + 1) * chunk,
                            h * GROUP + g * HEAD_WIDTH : h * GROUP + (g + 1) * HEAD_WIDTH,
                        ] = mixed[g * chunk : (g + 1) * chunk]


def attend(plan, queries, marks, packets, state):
    heads, chunk, count = plan["heads"], plan["chunk"], len(plan["members"])
    owners = len(plan["owners"])
    plan = dict(plan, marks=len(marks), packets=len(packets), carried=state is not None)
    rows = QUERY_PER_KEY * chunk
    slots = owners * 2 * heads
    vmem = pl.BlockSpec(memory_space=pltpu.VMEM)
    anywhere = pl.BlockSpec(memory_space=pl.ANY)
    out_shape = [
        jax.ShapeDtypeStruct((slots, 1, rows), jnp.float32),
        jax.ShapeDtypeStruct((slots, HEAD_WIDTH + HEADER, rows), jnp.float32),
    ]
    if plan["last"]:
        out_shape += [jax.ShapeDtypeStruct((2 * chunk, heads * GROUP), jnp.bfloat16)] * owners
    operands = owners + len(marks) + len(packets)
    flops = 4 * owners * heads * rows * HEAD_WIDTH * count * chunk * 2
    return pl.pallas_call(
        functools.partial(attend_kernel, plan),
        out_shape=out_shape,
        in_specs=[vmem] * owners
        + [anywhere] * (len(marks) + len(packets))
        + [vmem] * (0 if state is None else 2),
        out_specs=[vmem] * len(out_shape),
        input_output_aliases={} if state is None else {operands: 0, operands + 1: 1},
        scratch_shapes=[
            pltpu.VMEM((count * chunk, 2 * heads * HEAD_WIDTH), jnp.bfloat16),
            pltpu.VMEM((count * chunk, 2 * heads * HEAD_WIDTH), jnp.bfloat16),
            pltpu.VMEM((count * heads, HEAD_WIDTH + HEADER, 2 * chunk), jnp.bfloat16),
            pltpu.VMEM((count + owners, HEADER, HEAD_WIDTH), jnp.bfloat16),
            pltpu.SemaphoreType.DMA((3 * count + owners,)),
        ],
        cost_estimate=pl.CostEstimate(
            flops=flops, bytes_accessed=4 << 20, transcendentals=flops // 512
        ),
        compiler_params=pltpu.CompilerParams(vmem_limit_bytes=VMEM_LIMIT),
        name="attend",
    )(*queries, *marks, *packets, *(state or ()))


def project_kernel(own_ref, other_ref, w_ref, sent_ref, kept_ref, rows_ref):
    chunk, part = sent_ref.shape[0], own_ref.shape[1]

    @pl.when(pl.program_id(0) == 0)
    def _():
        mine = lax.axis_index("inner").astype(jnp.int32)
        first = my_core() == 0
        for place, half in enumerate((1 - mine, mine)):
            at = pl.multiple_of(half * chunk, chunk)
            own, other = own_ref[pl.ds(at, chunk)], other_ref[pl.ds(at, chunk)]
            to = pl.ds(place * chunk, chunk)
            rows_ref[to, :part] = jnp.where(first, own, other)
            rows_ref[to, part:] = jnp.where(first, other, own)

    product = jnp.dot(rows_ref[...], w_ref[...], preferred_element_type=jnp.float32)
    product = product.astype(sent_ref.dtype)
    sent_ref[...] = product[:chunk]
    kept_ref[...] = product[chunk:]


def project(own, other, out_weight, first, width, tile):
    rows, depth = own.shape[0], out_weight.shape[0]
    whole = lambda j: (0, 0)
    return pl.pallas_call(
        project_kernel,
        out_shape=[jax.ShapeDtypeStruct((rows // 2, width), jnp.bfloat16)] * 2,
        grid=(width // tile,),
        in_specs=[
            pl.BlockSpec(own.shape, whole),
            pl.BlockSpec(other.shape, whole),
            pl.BlockSpec((depth, tile), lambda j: (0, first // tile + j)),
        ],
        out_specs=[pl.BlockSpec((rows // 2, tile), lambda j: (0, j))] * 2,
        scratch_shapes=[pltpu.VMEM((rows, depth), jnp.bfloat16)],
        cost_estimate=pl.CostEstimate(
            flops=2 * rows * depth * width, bytes_accessed=2 * depth * width, transcendentals=0
        ),
        compiler_params=pltpu.CompilerParams(vmem_limit_bytes=VMEM_LIMIT),
        name="project",
    )(own, other, out_weight)


def prepare_kernel(chunk, k_ref, v_ref, position_ref, sent_ref, kept_ref):
    rows, width = k_ref.shape[0], k_ref.shape[1] // 2
    c = lax.div(position_ref[0], jnp.int32(chunk)).astype(jnp.float32)
    header = jnp.full((HEADER, 2 * width), c, jnp.float32).astype(jnp.bfloat16)
    for ref, core in ((kept_ref, my_core()), (sent_ref, 1 - my_core())):
        at = pl.ds(pl.multiple_of(core * width, width), width)
        ref[:rows, :width] = k_ref[:, at]
        ref[:rows, width:] = v_ref[:, at]
        ref[rows:] = header


def prepare(keys, values, positions):
    vmem = pl.BlockSpec(memory_space=pltpu.VMEM)
    rows = keys.shape[0]
    return pl.pallas_call(
        functools.partial(prepare_kernel, rows // 2),
        out_shape=[jax.ShapeDtypeStruct((rows + HEADER, keys.shape[1]), jnp.bfloat16)] * 2,
        in_specs=[vmem, vmem, pl.BlockSpec(memory_space=pltpu.SMEM)],
        out_specs=[vmem, vmem],
        compiler_params=pltpu.CompilerParams(vmem_limit_bytes=VMEM_LIMIT),
        name="prepare",
    )(keys, values, positions)


def after(value, *events):
    return lax.optimization_barrier((value, *events))[0]


def split_over_cores(count, queries, keys, values, positions):
    chips, half = count // 2, count // 4
    rows, chunk = queries.shape[0], queries.shape[0] // 2
    heads = keys.shape[1] // HEAD_WIDTH // 2
    sibling = [(b, b ^ 1) for b in range(count)]
    clock, counter = ring_pairs(chips, 1), ring_pairs(chips, -1)
    width = heads * HEAD_WIDTH

    sent, kept = prepare(keys, values, positions)
    got = lax.ppermute(sent, "blk", sibling)
    packet = jnp.concatenate(
        [kept[:rows], got[:rows], jnp.concatenate([kept[rows:, :width], got[rows:, :width]], axis=1)],
        axis=0,
    )
    q_sent = lax.dynamic_slice(
        queries, (0, (1 - my_core()) * heads * GROUP), (rows, heads * GROUP)
    )
    q_got = lax.ppermute(q_sent, "blk", sibling)

    shared = dict(heads=heads, chunk=chunk, owners=(True, False))
    shared["owner_headers"] = [(0, 2 * rows, 0), (0, 2 * rows, width)]

    def call(packets, state, own):
        each = range(len(packets))
        members = [(j, i * rows) for j in each for i in range(2)]
        headers = [(1 + j, 2 * rows, i * width) for j in each for i in range(2)]
        plan = dict(shared, own=own, last=False, members=members, headers=headers)
        return attend(plan, [queries, q_got], [packet], packets, state)

    ups, downs, state = [packet], [packet], None
    for r in range(1, half):
        up, down = ups[-1], downs[-1]
        if state is not None:
            up, down, *state = lax.optimization_barrier((up, down, *state))
        ups.append(lax.ppermute(up, "blk", clock))
        downs.append(lax.ppermute(down, "blk", counter))
        if r >= 2:
            here = [ups[r - 1], downs[r - 1]]
            state = call([packet] + here if r == 2 else here, state, r == 2)
    up, down, *state = lax.optimization_barrier((ups[-1], downs[-1], *state))
    far_up = lax.ppermute(up[:rows], "blk", clock)
    far_down = lax.ppermute(down[rows:], "blk", counter)
    state = call([up, down], state, False)
    plan = dict(
        shared,
        own=False,
        last=True,
        members=[(0, 0), (1, 0)],
        headers=[(2, rows, 0), (2, rows, width)],
    )
    _, _, own, theirs = attend(plan, [queries, q_got], [packet], [far_up, far_down], state)
    return own, lax.ppermute(theirs, "blk", sibling)


def one_head_a_device(count, queries, keys, values, positions):
    rows, chunk = queries.shape[0], queries.shape[0] // 2
    heads = keys.shape[1] // HEAD_WIDTH
    c = (positions[:1] // chunk).astype(jnp.bfloat16).reshape(1, 1)
    header = jnp.broadcast_to(c, (HEADER, 2 * keys.shape[1]))
    packet = jnp.concatenate([jnp.concatenate([keys, values], axis=1), header], axis=0)
    packets = lax.all_gather(packet, "blk", axis=0, tiled=True)
    size = rows + HEADER
    plan = dict(
        heads=heads,
        chunk=chunk,
        owners=(False,),
        own=True,
        last=True,
        members=[(0, j * size) for j in range(count)],
        headers=[(1, j * size + rows, 0) for j in range(count)],
        owner_headers=[(0, rows, 0)],
    )
    return attend(plan, [queries], [packet], [packets], None)[2]


def shards(count, inner, queries, keys, values, positions, out_weight):
    heads = keys.shape[1] // HEAD_WIDTH
    if heads % 2:
        attended = one_head_a_device(count, queries, keys, values, positions)
        partial = jnp.dot(attended, out_weight, preferred_element_type=jnp.float32)
        return lax.psum_scatter(
            partial.astype(jnp.bfloat16), "inner", scatter_dimension=0, tiled=True
        )
    own, other = split_over_cores(count, queries, keys, values, positions)
    out_weight = pltpu.with_memory_space_constraint(out_weight, pltpu.HBM)
    width, tile = out_weight.shape[1], 256
    shares = (3, 4, 6, 7)
    received, kept, first = [], [], 0
    for j, share in enumerate(shares):
        columns = width * share // sum(shares)
        source = own if j < 2 else after(own, received[j - 2])
        sent, keep = project(source, other, out_weight, first, columns, tile)
        received.append(lax.ppermute(sent, "inner", [(0, 1), (1, 0)]))
        kept.append(keep)
        first += columns
    mine, theirs = jnp.concatenate(kept, axis=1), jnp.concatenate(received, axis=1)
    return (mine.astype(jnp.float32) + theirs.astype(jnp.float32)).astype(jnp.bfloat16)


def solution(mesh):
    placed = (P("blk", "inner"), P("blk", "inner"), P("blk", "inner"), P("blk"), P("inner", None))
    return jax.shard_map(
        functools.partial(shards, mesh.shape["blk"], mesh.shape["inner"]),
        mesh=mesh,
        in_specs=placed,
        out_specs=P(("blk", "inner"), None),
        check_vma=False,
    )
```

time: 118 us -> 97.2 us (0.82)
  local copies, waits for them, and re-layouts: 19.3 us -> 2.71 us
  waiting for transfers between devices: 33.3 us -> 27.4 us
  Pallas kernels: 47.4 us -> 50.7 us
  between operations: 2.14 us -> 0.18 us
    ppermute x9, waiting for transfers between devices: 28.4 us -> 14.1 us  [the longest x3 11 us: split_over_cores(): ups.append(lax.ppermute(up, 'blk', clock))]
    unnamed x6 -> x8, local copies, waits for them, and re-layouts: 16.9 us -> 2.62 us
    ppermute x4, waiting for transfers between devices: 3.8 us -> 12.2 us  [shards(): received.append(lax.ppermute(sent, 'inner', [(0, 1), (1, 0)]))]
    pallas_call x2 -> x4, Pallas kernels: 26.7 us -> 29.1 us  [attend(): pl.pallas_call(functools.partial(attend_kernel, plan), out_shape=out_shap...]
    slice x3 -> x4, local copies, waits for them, and re-layouts: 1.3 us -> 0.04 us  [the longest x1 0.01 us: split_over_cores(): far_down = lax.ppermute(down[rows:], 'blk', counter)]
  transfers between devices with their start and end apart: 15 -> 15, of which waited for: 7 -> 7; matrix products, arithmetic and copies ran while one was open for 0% -> 0% of each run, Pallas kernels for 29% -> 35%
where the time goes in v2:
time: 97.2 us; the launch traced here: 96.4 us
  Pallas kernels  50.7 us (52%)
  waiting for transfers between devices  27.4 us (28%)
  starting transfers between devices  14.2 us (15%)
  local copies, waits for them, and re-layouts  2.71 us (3%)
  other arithmetic  1.22 us (1%)
    pallas_call x4, Pallas kernels, attend(): pl.pallas_call(functools.partial(attend_kernel, plan), out_shape=out_shap...  29.1 us
    pallas_call x4, Pallas kernels, project(): pl.pallas_call(project_kernel, out_shape=[jax.ShapeDtypeStruct((rows // 2...  21 us
    ppermute x4, waiting for transfers between devices, shards(): received.append(lax.ppermute(sent, 'inner', [(0, 1), (1, 0)]))  12.2 us
    ppermute x3, waiting for transfers between devices, split_over_cores(): ups.append(lax.ppermute(up, 'blk', clock))  11 us
    ppermute x3, starting transfers between devices, split_over_cores(): ups.append(lax.ppermute(up, 'blk', clock))  6.64 us
    ppermute x4, starting transfers between devices, shards(): received.append(lax.ppermute(sent, 'inner', [(0, 1), (1, 0)]))  4.31 us
    unnamed x8, local copies, waits for them, and re-layouts  2.62 us
  transfers between devices with their start and end apart: 15, of which 7 were waited for; matrix products, arithmetic and copies ran while one was open for 0% of the time, Pallas kernels for 35%

profile of v2, /device:TPU:0, one launch (start us, length us, event | category | flops | bytes accessed | tf_op | source)
XLA Modules:
  0.0 96.4 jit_solution(2238831162742718017)
XLA Ops:
  0.0 0.0 copy-start
  0.0 0.0 copy-start.1
  0.0 1.0 %copy-done.1 = bf16[192,512]{1,0:T(8,128)(2,1)S(1)} copy-done((bf16[192,512]{1,0:T(8,128)(2,1)S(1)}, bf16[192,512]{1,0:T(8,128)(2,1)}, u32[]{:S(2)}) %copy-start.1) | copy-done | bytes 196632
  1.0 0.0 copy-start.2
  1.0 0.9 copy-done.2
  1.9 0.0 copy-start.3
  1.9 0.7 copy-done.3
  2.6 0.6 prepare.1
  3.2 0.5 collective-permute-start.1
  3.8 1.1 %collective-permute-done.1 = bf16[208,512]{1,0:T(8,128)(2,1)S(1)} collective-permute-done((bf16[208,512]{1,0:T(8,128)(2,1)S(1)}, bf16[208,512]{1,0:T(8,128)(2,1)S(1)}, u32[]{:S(2)}, u32[]{:S(2)}) %collective-permute-start.1) | collective-permute-done | bytes 213024 | tf_op jit(solution)/shard_map/ppermute | solution.py:323
  4.9 3.0 %collective-permute-start.2 = (bf16[400,512]{1,0:T(8,128)(2,1)S(1)}, bf16[400,512]{1,0:T(8,128)(2,1)S(1)}, u32[]{:S(2)}, u32[]{:S(2)}) collective-permute-start(bf16[400,512]{1,0:T(8,128)(2,1)S(1)} %maximum_maximum_fusion.refs_2_.refs_3_), channel_id=1, source_target_pairs={{0,8},{2,10},{8,16},{10,18},{16,24},{18,26},{24,28},{26,30},{28,20... | collective-permute-start | bytes 1228808 | tf_op jit(solution)/shard_map/ppermute | solution.py:348
  7.9 0.0 collective-permute-start.4
  7.9 0.0 copy-done
  7.9 0.1 collective-permute-start
  8.0 9.6 %collective-permute-done.2.refs_4_ = bf16[400,512]{1,0:T(8,128)(2,1)S(1)} collective-permute-done((bf16[400,512]{1,0:T(8,128)(2,1)S(1)}, bf16[400,512]{1,0:T(8,128)(2,1)S(1)}, u32[]{:S(2)}, u32[]{:S(2)}) %collective-permute-start.2) | collective-permute-done | bytes 409632 | tf_op jit(solution)/shard_map/ppermute | solution.py:348
  17.6 1.8 %collective-permute-start.3 = (bf16[400,512]{1,0:T(8,128)(2,1)S(1)}, bf16[400,512]{1,0:T(8,128)(2,1)S(1)}, u32[]{:S(2)}, u32[]{:S(2)}) collective-permute-start(bf16[400,512]{1,0:T(8,128)(2,1)S(1)} %collective-permute-done.2.refs_4_), channel_id=1, source_target_pairs={{0,8},{2,10},{8,16},{10,18},{16,24},{18,26},{24,28},{26,30},{28,20... | collective-permute-start | bytes 1228808 | tf_op jit(solution)/shard_map/ppermute | solution.py:348
  19.4 0.0 collective-permute-done.4.refs_5_
  19.4 0.2 collective-permute-start.5
  19.6 0.0 collective-permute-done.refs_1_
  19.6 10.7 %attend.4 = (f32[8,1,480]{2,1,0:T(1,128)S(1)}, f32[8,144,480]{2,1,0:T(8,128)S(1)}) custom-call(bf16[192,2560]{1,0:T(8,128)(2,1)S(1)} %copy-done, bf16[192,1280]{1,0:T(8,128)(2,1)S(1)} %collective-permute-done.refs_1_, bf16[400,512]{1,0:T(8,128)(2,1)S(1)} %maximum_maximum_fusion.refs_2_.refs_3_, bf16[400,512]{1,0:T(8,128)(2,1)S(1)} %maximum_maximum_fusion.refs_2_.refs_3_, ...), custom_call_target="tpu_custom_call" | custom-call | flops 1132462080 | bytes 4194304 | tf_op jit(solution)/shard_map/attend/pallas_call | solution.py:221
  30.3 0.0 collective-permute-done.3.refs_3_
  30.4 0.0 collective-permute-done.5.refs_4_
  30.4 1.8 %collective-permute-start.6 = (bf16[400,512]{1,0:T(8,128)(2,1)S(1)}, bf16[400,512]{1,0:T(8,128)(2,1)S(1)}, u32[]{:S(2)}, u32[]{:S(2)}) collective-permute-start(bf16[400,512]{1,0:T(8,128)(2,1)S(1)} %collective-permute-done.3.refs_3_), channel_id=1, source_target_pairs={{0,8},{2,10},{8,16},{10,18},{16,24},{18,26},{24,28},{26,30},{28,20... | collective-permute-start | bytes 1228808 | tf_op jit(solution)/shard_map/ppermute | solution.py:348
  32.2 0.2 collective-permute-start.7
  32.4 7.0 %attend.5 = (f32[8,1,480]{2,1,0:T(1,128)S(1)}, f32[8,144,480]{2,1,0:T(8,128)S(1)}) custom-call(bf16[192,2560]{1,0:T(8,128)(2,1)S(1)} %copy-done, bf16[192,1280]{1,0:T(8,128)(2,1)S(1)} %collective-permute-done.refs_1_, bf16[400,512]{1,0:T(8,128)(2,1)S(1)} %maximum_maximum_fusion.refs_2_.refs_3_, ...), custom_call_target="tpu_custom_call", output_to_operand_aliasing={{0}: (5, {}), {1}: (6, {})} | custom-call | flops 754974720 | bytes 4194304 | tf_op jit(solution)/shard_map/attend/pallas_call | solution.py:221
  39.4 1.4 %collective-permute-done.6.refs_3_ = bf16[400,512]{1,0:T(8,128)(2,1)S(1)} collective-permute-done((bf16[400,512]{1,0:T(8,128)(2,1)S(1)}, bf16[400,512]{1,0:T(8,128)(2,1)S(1)}, u32[]{:S(2)}, u32[]{:S(2)}) %collective-permute-start.6) | collective-permute-done | bytes 409632 | tf_op jit(solution)/shard_map/ppermute | solution.py:348
  40.8 1.2 %collective-permute-done.7.refs_4_ = bf16[400,512]{1,0:T(8,128)(2,1)S(1)} collective-permute-done((bf16[400,512]{1,0:T(8,128)(2,1)S(1)}, bf16[400,512]{1,0:T(8,128)(2,1)S(1)}, u32[]{:S(2)}, u32[]{:S(2)}) %collective-permute-start.7) | collective-permute-done | bytes 409632 | tf_op jit(solution)/shard_map/ppermute | solution.py:349
  42.1 0.6 collective-permute-start.9
  42.7 1.5 %collective-permute-start.8 = (bf16[192,512]{1,0:T(8,128)(2,1)S(1)}, bf16[192,512]{1,0:T(8,128)(2,1)S(1)}, u32[]{:S(2)}, u32[]{:S(2)}) collective-permute-start(bf16[192,512]{1,0:T(8,128)(2,1)S(1)} %slice.22), channel_id=1, source_target_pairs={{0,8},{2,10},{8,16},{10,18},{16,24},{18,26},{24,28},{26,30},{28,20... | collective-permute-start | bytes 589832 | tf_op jit(solution)/shard_map/ppermute | solution.py:354
  44.2 6.8 %attend.6 = (f32[8,1,480]{2,1,0:T(1,128)S(1)}, f32[8,144,480]{2,1,0:T(8,128)S(1)}) custom-call(bf16[192,2560]{1,0:T(8,128)(2,1)S(1)} %copy-done, bf16[192,1280]{1,0:T(8,128)(2,1)S(1)} %collective-permute-done.refs_1_, bf16[400,512]{1,0:T(8,128)(2,1)S(1)} %maximum_maximum_fusion.refs_2_.refs_3_, ...), custom_call_target="tpu_custom_call", output_to_operand_aliasing={{0}: (5, {}), {1}: (6, {})} | custom-call | flops 754974720 | bytes 4194304 | tf_op jit(solution)/shard_map/attend/pallas_call | solution.py:221
  51.0 0.0 collective-permute-done.8.refs_3_
  51.0 0.0 collective-permute-done.9.refs_4_
  51.0 4.7 %attend.7 = (f32[8,1,480]{2,1,0:T(1,128)S(1)}, f32[8,144,480]{2,1,0:T(8,128)S(1)}, bf16[192,1280]{1,0:T(8,128)(2,1)S(1)}, bf16[192,1280]{1,0:T(8,128)(2,1)S(1)}) custom-call(bf16[192,2560]{1,0:T(8,128)(2,1)S(1)} %copy-done, bf16[192,1280]{1,0:T(8,128)(2,1)S(1)} %collective-permute-done.refs_1_, ...), custom_call_target="tpu_custom_call", output_to_operand_aliasing={{0}: (5, {}), {1}: (6, {})} | custom-call | flops 377487360 | bytes 4194304 | tf_op jit(solution)/shard_map/attend/pallas_call | solution.py:221
  55.7 0.1 collective-permute-start.10
  55.8 1.9 %collective-permute-done.10.other_ref = bf16[192,1280]{1,0:T(8,128)(2,1)S(1)} collective-permute-done((bf16[192,1280]{1,0:T(8,128)(2,1)S(1)}, bf16[192,1280]{1,0:T(8,128)(2,1)S(1)}, u32[]{:S(2)}, u32[]{:S(2)}) %collective-permute-start.10) | collective-permute-done | bytes 491552 | tf_op jit(solution)/shard_map/ppermute | solution.py:365
  57.6 4.2 %project.5 = (bf16[96,1024]{1,0:T(8,128)(2,1)S(1)}, bf16[96,1024]{1,0:T(8,128)(2,1)S(1)}) custom-call(bf16[192,1280]{1,0:T(8,128)(2,1)S(1)} %get-tuple-element.54.own_ref, bf16[192,1280]{1,0:T(8,128)(2,1)S(1)} %collective-permute-done.10.other_ref, bf16[2560,5120]{1,0:T(8,128)(2,1)} %w_ref.7), custom_call_target="tpu_custom_call" | custom-call | flops 1006632960 | bytes 5242880 | tf_op jit(solution)/shard_map/project/pallas_call | solution.py:267
  61.8 1.6 %collective-permute-start.12 = (bf16[96,1024]{1,0:T(8,128)(2,1)S(1)}, bf16[96,1024]{1,0:T(8,128)(2,1)S(1)}, u32[]{:S(2)}, u32[]{:S(2)}) collective-permute-start(bf16[96,1024]{1,0:T(8,128)(2,1)S(1)} %get-tuple-element.56), channel_id=1, source_target_pairs={{0,1},{1,0},{2,3},{3,2},{4,5},{5,4},{6,7},{7,6},{8,9},{9,8},{10,11... | collective-permute-start | bytes 589832 | tf_op jit(solution)/shard_map/ppermute | solution.py:406
  63.4 3.6 %project.4 = (bf16[96,768]{1,0:T(8,128)(2,1)S(1)}, bf16[96,768]{1,0:T(8,128)(2,1)S(1)}) custom-call(bf16[192,1280]{1,0:T(8,128)(2,1)S(1)} %get-tuple-element.54.own_ref, bf16[192,1280]{1,0:T(8,128)(2,1)S(1)} %collective-permute-done.10.other_ref, bf16[2560,5120]{1,0:T(8,128)(2,1)} %w_ref.7), custom_call_target="tpu_custom_call" | custom-call | flops 754974720 | bytes 3932160 | tf_op jit(solution)/shard_map/project/pallas_call | solution.py:267
  67.0 0.6 collective-permute-start.11
  67.6 5.1 %collective-permute-done.11 = bf16[96,768]{1,0:T(8,128)(2,1)S(1)} collective-permute-done((bf16[96,768]{1,0:T(8,128)(2,1)S(1)}, bf16[96,768]{1,0:T(8,128)(2,1)S(1)}, u32[]{:S(2)}, u32[]{:S(2)}) %collective-permute-start.11) | collective-permute-done | bytes 147488 | tf_op jit(solution)/shard_map/ppermute | solution.py:406
  72.6 0.0 collective-permute-done.12
  72.6 7.2 %project.7 = (bf16[96,1792]{1,0:T(8,128)(2,1)S(1)}, bf16[96,1792]{1,0:T(8,128)(2,1)S(1)}) custom-call(bf16[192,1280]{1,0:T(8,128)(2,1)S(1)} %get-tuple-element.54.own_ref, bf16[192,1280]{1,0:T(8,128)(2,1)S(1)} %collective-permute-done.10.other_ref, bf16[2560,5120]{1,0:T(8,128)(2,1)} %w_ref.7), custom_call_target="tpu_custom_call" | custom-call | flops 1761607680 | bytes 9175040 | tf_op jit(solution)/shard_map/project/pallas_call | solution.py:267
  79.9 0.9 collective-permute-start.14
  80.7 6.0 %project.6 = (bf16[96,1536]{1,0:T(8,128)(2,1)S(1)}, bf16[96,1536]{1,0:T(8,128)(2,1)S(1)}) custom-call(bf16[192,1280]{1,0:T(8,128)(2,1)S(1)} %get-tuple-element.54.own_ref, bf16[192,1280]{1,0:T(8,128)(2,1)S(1)} %collective-permute-done.10.other_ref, bf16[2560,5120]{1,0:T(8,128)(2,1)} %w_ref.7), custom_call_target="tpu_custom_call" | custom-call | flops 1509949440 | bytes 7864320 | tf_op jit(solution)/shard_map/project/pallas_call | solution.py:267
  86.8 1.3 %collective-permute-start.13 = (bf16[96,1536]{1,0:T(8,128)(2,1)S(1)}, bf16[96,1536]{1,0:T(8,128)(2,1)S(1)}, u32[]{:S(2)}, u32[]{:S(2)}) collective-permute-start(bf16[96,1536]{1,0:T(8,128)(2,1)S(1)} %get-tuple-element.59), channel_id=1, source_target_pairs={{0,1},{1,0},{2,3},{3,2},{4,5},{5,4},{6,7},{7,6},{8,9},{9,8},{10,11... | collective-permute-start | bytes 884744 | tf_op jit(solution)/shard_map/ppermute | solution.py:406
  88.0 7.2 %collective-permute-done.13 = bf16[96,1536]{1,0:T(8,128)(2,1)S(1)} collective-permute-done((bf16[96,1536]{1,0:T(8,128)(2,1)S(1)}, bf16[96,1536]{1,0:T(8,128)(2,1)S(1)}, u32[]{:S(2)}, u32[]{:S(2)}) %collective-permute-start.13) | collective-permute-done | bytes 294944 | tf_op jit(solution)/shard_map/ppermute | solution.py:406
  95.2 0.0 collective-permute-done.14
  95.2 1.2 %add_convert_fusion = bf16[96,5120]{1,0:T(8,128)(2,1)} fusion(bf16[96,1792]{1,0:T(8,128)(2,1)S(1)} %get-tuple-element.58, bf16[96,1536]{1,0:T(8,128)(2,1)S(1)} %get-tuple-element.55, bf16[96,1024]{1,0:T(8,128)(2,1)S(1)} %get-tuple-element.52, bf16[96,768]{1,0:T(8,128)(2,1)S(1)} %get-tuple-element.51, bf16[96,1792]{1,0:T(8,128)(2,1)S(1)} %collective-permute-done.14, ...), kind=kLoop, calls=%fused_computation | loop fusion | flops 8847360 | bytes 2949120 | tf_op jit(solution)/shard_map/convert_element_type | solution.py:410
  (8 shorter events, 0.1 us)
Async XLA Ops:
  0.0 7.9 %copy-start = (bf16[192,2560]{1,0:T(8,128)(2,1)S(1)}, bf16[192,2560]{1,0:T(8,128)(2,1)}, u32[]{:S(2)}) copy-start(bf16[192,2560]{1,0:T(8,128)(2,1)} %refs_0_.7) | copy-start | bytes 2949124
  0.0 1.0 %copy-start.1 = (bf16[192,512]{1,0:T(8,128)(2,1)S(1)}, bf16[192,512]{1,0:T(8,128)(2,1)}, u32[]{:S(2)}) copy-start(bf16[192,512]{1,0:T(8,128)(2,1)} %k_ref.1) | copy-start | bytes 589828
  1.0 0.9 copy-start.2
  1.9 0.7 copy-start.3
  3.2 1.6 %collective-permute-start.1 = (bf16[208,512]{1,0:T(8,128)(2,1)S(1)}, bf16[208,512]{1,0:T(8,128)(2,1)S(1)}, u32[]{:S(2)}, u32[]{:S(2)}) collective-permute-start(bf16[208,512]{1,0:T(8,128)(2,1)S(1)} %get-tuple-element.34), channel_id=1, source_target_pairs={{0,2},{2,0},{4,6},{6,4},{8,10},{10,8},{12,14},{14,12},{16,18},{18,... | collective-permute-start | bytes 638984 | tf_op jit(solution)/shard_map/ppermute | solution.py:323
  4.9 12.7 %collective-permute-start.2 = (bf16[400,512]{1,0:T(8,128)(2,1)S(1)}, bf16[400,512]{1,0:T(8,128)(2,1)S(1)}, u32[]{:S(2)}, u32[]{:S(2)}) collective-permute-start(bf16[400,512]{1,0:T(8,128)(2,1)S(1)} %maximum_maximum_fusion.refs_2_.refs_3_), channel_id=1, source_target_pairs={{0,8},{2,10},{8,16},{10,18},{16,24},{18,26},{24,28},{26,30},{28,20... | collective-permute-start | bytes 1228808 | tf_op jit(solution)/shard_map/ppermute | solution.py:348
  7.9 11.5 %collective-permute-start.4 = (bf16[400,512]{1,0:T(8,128)(2,1)S(1)}, bf16[400,512]{1,0:T(8,128)(2,1)S(1)}, u32[]{:S(2)}, u32[]{:S(2)}) collective-permute-start(bf16[400,512]{1,0:T(8,128)(2,1)S(1)} %maximum_maximum_fusion.refs_2_.refs_3_), channel_id=1, source_target_pairs={{0,4},{2,6},{8,0},{10,2},{16,8},{18,10},{24,16},{26,18},{28,24},{3... | collective-permute-start | bytes 1228808 | tf_op jit(solution)/shard_map/ppermute | solution.py:349
  7.9 11.7 %collective-permute-start = (bf16[192,1280]{1,0:T(8,128)(2,1)S(1)}, bf16[192,1280]{1,0:T(8,128)(2,1)S(1)}, u32[]{:S(2)}, u32[]{:S(2)}) collective-permute-start(bf16[192,1280]{1,0:T(8,128)(2,1)S(1)} %constant_dynamic-slice_fusion), channel_id=1, source_target_pairs={{0,2},{2,0},{4,6},{6,4},{8,10},{10,8},{12,14},{14,12},{16,18},{18,... | collective-permute-start | bytes 1474568 | tf_op jit(solution)/shard_map/ppermute | solution.py:331
  17.6 12.8 %collective-permute-start.3 = (bf16[400,512]{1,0:T(8,128)(2,1)S(1)}, bf16[400,512]{1,0:T(8,128)(2,1)S(1)}, u32[]{:S(2)}, u32[]{:S(2)}) collective-permute-start(bf16[400,512]{1,0:T(8,128)(2,1)S(1)} %collective-permute-done.2.refs_4_), channel_id=1, source_target_pairs={{0,8},{2,10},{8,16},{10,18},{16,24},{18,26},{24,28},{26,30},{28,20... | collective-permute-start | bytes 1228808 | tf_op jit(solution)/shard_map/ppermute | solution.py:348
  19.4 11.0 %collective-permute-start.5 = (bf16[400,512]{1,0:T(8,128)(2,1)S(1)}, bf16[400,512]{1,0:T(8,128)(2,1)S(1)}, u32[]{:S(2)}, u32[]{:S(2)}) collective-permute-start(bf16[400,512]{1,0:T(8,128)(2,1)S(1)} %collective-permute-done.4.refs_5_), channel_id=1, source_target_pairs={{0,4},{2,6},{8,0},{10,2},{16,8},{18,10},{24,16},{26,18},{28,24},{3... | collective-permute-start | bytes 1228808 | tf_op jit(solution)/shard_map/ppermute | solution.py:349
  30.4 10.5 %collective-permute-start.6 = (bf16[400,512]{1,0:T(8,128)(2,1)S(1)}, bf16[400,512]{1,0:T(8,128)(2,1)S(1)}, u32[]{:S(2)}, u32[]{:S(2)}) collective-permute-start(bf16[400,512]{1,0:T(8,128)(2,1)S(1)} %collective-permute-done.3.refs_3_), channel_id=1, source_target_pairs={{0,8},{2,10},{8,16},{10,18},{16,24},{18,26},{24,28},{26,30},{28,20... | collective-permute-start | bytes 1228808 | tf_op jit(solution)/shard_map/ppermute | solution.py:348
  32.2 9.8 %collective-permute-start.7 = (bf16[400,512]{1,0:T(8,128)(2,1)S(1)}, bf16[400,512]{1,0:T(8,128)(2,1)S(1)}, u32[]{:S(2)}, u32[]{:S(2)}) collective-permute-start(bf16[400,512]{1,0:T(8,128)(2,1)S(1)} %collective-permute-done.5.refs_4_), channel_id=1, source_target_pairs={{0,4},{2,6},{8,0},{10,2},{16,8},{18,10},{24,16},{26,18},{28,24},{3... | collective-permute-start | bytes 1228808 | tf_op jit(solution)/shard_map/ppermute | solution.py:349
  42.1 9.0 %collective-permute-start.9 = (bf16[208,512]{1,0:T(8,128)(2,1)S(1)}, bf16[208,512]{1,0:T(8,128)(2,1)S(1)}, u32[]{:S(2)}, u32[]{:S(2)}) collective-permute-start(bf16[208,512]{1,0:T(8,128)(2,1)S(1)} %slice.23), channel_id=1, source_target_pairs={{0,4},{2,6},{8,0},{10,2},{16,8},{18,10},{24,16},{26,18},{28,24},{3... | collective-permute-start | bytes 638984 | tf_op jit(solution)/shard_map/ppermute | solution.py:355
  42.7 8.3 %collective-permute-start.8 = (bf16[192,512]{1,0:T(8,128)(2,1)S(1)}, bf16[192,512]{1,0:T(8,128)(2,1)S(1)}, u32[]{:S(2)}, u32[]{:S(2)}) collective-permute-start(bf16[192,512]{1,0:T(8,128)(2,1)S(1)} %slice.22), channel_id=1, source_target_pairs={{0,8},{2,10},{8,16},{10,18},{16,24},{18,26},{24,28},{26,30},{28,20... | collective-permute-start | bytes 589832 | tf_op jit(solution)/shard_map/ppermute | solution.py:354
  55.7 1.9 %collective-permute-start.10 = (bf16[192,1280]{1,0:T(8,128)(2,1)S(1)}, bf16[192,1280]{1,0:T(8,128)(2,1)S(1)}, u32[]{:S(2)}, u32[]{:S(2)}) collective-permute-start(bf16[192,1280]{1,0:T(8,128)(2,1)S(1)} %get-tuple-element.50), channel_id=1, source_target_pairs={{0,2},{2,0},{4,6},{6,4},{8,10},{10,8},{12,14},{14,12},{16,18},{18,... | collective-permute-start | bytes 1474568 | tf_op jit(solution)/shard_map/ppermute | solution.py:365
  61.8 10.8 %collective-permute-start.12 = (bf16[96,1024]{1,0:T(8,128)(2,1)S(1)}, bf16[96,1024]{1,0:T(8,128)(2,1)S(1)}, u32[]{:S(2)}, u32[]{:S(2)}) collective-permute-start(bf16[96,1024]{1,0:T(8,128)(2,1)S(1)} %get-tuple-element.56), channel_id=1, source_target_pairs={{0,1},{1,0},{2,3},{3,2},{4,5},{5,4},{6,7},{7,6},{8,9},{9,8},{10,11... | collective-permute-start | bytes 589832 | tf_op jit(solution)/shard_map/ppermute | solution.py:406
  67.0 5.7 %collective-permute-start.11 = (bf16[96,768]{1,0:T(8,128)(2,1)S(1)}, bf16[96,768]{1,0:T(8,128)(2,1)S(1)}, u32[]{:S(2)}, u32[]{:S(2)}) collective-permute-start(bf16[96,768]{1,0:T(8,128)(2,1)S(1)} %get-tuple-element.53), channel_id=1, source_target_pairs={{0,1},{1,0},{2,3},{3,2},{4,5},{5,4},{6,7},{7,6},{8,9},{9,8},{10,11... | collective-permute-start | bytes 442376 | tf_op jit(solution)/shard_map/ppermute | solution.py:406
  79.9 15.3 %collective-permute-start.14 = (bf16[96,1792]{1,0:T(8,128)(2,1)S(1)}, bf16[96,1792]{1,0:T(8,128)(2,1)S(1)}, u32[]{:S(2)}, u32[]{:S(2)}) collective-permute-start(bf16[96,1792]{1,0:T(8,128)(2,1)S(1)} %get-tuple-element.60), channel_id=1, source_target_pairs={{0,1},{1,0},{2,3},{3,2},{4,5},{5,4},{6,7},{7,6},{8,9},{9,8},{10,11... | collective-permute-start | bytes 1032200 | tf_op jit(solution)/shard_map/ppermute | solution.py:406
  86.8 8.4 %collective-permute-start.13 = (bf16[96,1536]{1,0:T(8,128)(2,1)S(1)}, bf16[96,1536]{1,0:T(8,128)(2,1)S(1)}, u32[]{:S(2)}, u32[]{:S(2)}) collective-permute-start(bf16[96,1536]{1,0:T(8,128)(2,1)S(1)} %get-tuple-element.59), channel_id=1, source_target_pairs={{0,1},{1,0},{2,3},{3,2},{4,5},{5,4},{6,7},{7,6},{8,9},{9,8},{10,11... | collective-permute-start | bytes 884744 | tf_op jit(solution)/shard_map/ppermute | solution.py:406

commit v3 on v2

v3 whole, which is shorter than its diff:
```python
import functools
import math

import jax
import jax.numpy as jnp
from jax import lax
from jax.experimental import pallas as pl
from jax.experimental.pallas import tpu as pltpu
from jax.sharding import PartitionSpec as P

HEAD_WIDTH = 128
QUERY_PER_KEY = 5
GROUP = QUERY_PER_KEY * HEAD_WIDTH
EXP2_SCALE = math.log2(math.e) / math.sqrt(HEAD_WIDTH)
MASKED = -1e30
VMEM_LIMIT = 16 * 1024 * 1024
HEADER = 16


def ring_of_chips(chips):
    half = chips // 2
    if chips == 8:
        return [2 * z for z in range(half)] + [2 * z + 1 for z in reversed(range(half))]
    return list(range(half)) + list(reversed(range(half, chips)))


def ring_pairs(chips, step):
    ring = ring_of_chips(chips)
    return [
        (2 * ring[i] + core, 2 * ring[(i + step) % chips] + core)
        for i in range(chips)
        for core in range(2)
    ]


def my_core():
    return lax.rem(lax.axis_index("blk"), 2).astype(jnp.int32)


def product(a, b):
    return jnp.dot(a, b, preferred_element_type=jnp.float32)


def weigh(scores, high):
    return jnp.exp2((scores - high) * EXP2_SCALE).astype(jnp.bfloat16)


def turned_values(blocks):
    v = jnp.concatenate(blocks, axis=0)
    return jnp.concatenate([jnp.transpose(v), jnp.ones((HEADER, v.shape[0]), v.dtype)], axis=0)


def attend_kernel(plan, *refs):
    heads, chunk, owners = plan["heads"], plan["chunk"], plan["owners"]
    refs = list(refs)
    q_ref = refs.pop(0)
    mark_refs = [refs.pop(0) for _ in range(plan["marks"])]
    packets = [refs.pop(0) for _ in range(plan["packets"])]
    if plan["carried"]:
        in_high, in_sums = refs.pop(0), refs.pop(0)
    high_ref, sums_ref = refs.pop(0), refs.pop(0)
    out_refs = refs

    sources = mark_refs + packets
    numbers = [
        jnp.max(
            sources[packet][row : row + HEADER, column : column + HEAD_WIDTH].astype(jnp.float32)
        ).astype(jnp.int32)
        for packet, row, column in plan["owner_headers"] + plan["headers"]
    ]
    owner_c, member_c = numbers[:owners], numbers[owners:]

    def rows_of(j, half, column):
        packet, row = plan["members"][j]
        at = row + half * chunk
        at = at if isinstance(half, int) else pl.multiple_of(at, HEADER)
        return packets[packet][pl.ds(at, chunk), column : column + HEAD_WIDTH]

    def state_at(i, half, h):
        return (2 * i + half) * heads + h

    rows = QUERY_PER_KEY * chunk
    causal = lax.broadcasted_iota(jnp.int32, (chunk, rows), 0) <= lax.rem(
        lax.broadcasted_iota(jnp.int32, (chunk, rows), 1), chunk
    )
    count = len(plan["members"])
    for first in range(0, count, 6):
        group = range(first, min(first + 6, count))
        for h in range(heads):
            k_at, v_at = h * HEAD_WIDTH, (heads + h) * HEAD_WIDTH
            early_keys = jnp.concatenate([rows_of(j, 0, k_at) for j in group], axis=0)
            early_values = turned_values([rows_of(j, 0, v_at) for j in group])
            for i in range(owners):
                late_at, early_at = state_at(i, 1, h), state_at(i, 0, h)
                carried = None
                if first > 0:
                    carried = [(ref[early_at], ref[late_at]) for ref in (high_ref, sums_ref)]
                elif plan["carried"]:
                    carried = [(ref[early_at], ref[late_at]) for ref in (in_high, in_sums)]

                pairs = []
                for j in group:
                    if plan["own"] and j == plan["own_at"](i):
                        pairs += [(j, 0, causal), (j, 1, causal)]
                    else:
                        pairs.append((j, (member_c[j] > owner_c[i]).astype(jnp.int32), None))
                base = product(early_keys, q_ref[late_at])
                scores = []
                for j, half, mask in pairs:
                    s = product(rows_of(j, half, k_at), q_ref[state_at(i, half, h)])
                    scores.append(s if mask is None else jnp.where(mask, s, MASKED))
                tops = [jnp.max(s, axis=0, keepdims=True) for s in scores]
                highs = []
                for side in range(2):
                    some = [jnp.where(half == side, top, MASKED) for (_, half, _), top in zip(pairs, tops)]
                    if side == 1:
                        some.append(jnp.max(base, axis=0, keepdims=True))
                    if carried is not None:
                        some.append(carried[0][side])
                    highs.append(functools.reduce(jnp.maximum, some))
                weights = [
                    weigh(s, jnp.where(half == 1, highs[1], highs[0]))
                    for (_, half, _), s in zip(pairs, scores)
                ]
                values = turned_values([rows_of(j, half, v_at) for j, half, _ in pairs])
                zero = jnp.zeros_like(weights[0])
                for side, at in ((0, early_at), (1, late_at)):
                    chosen = [
                        jnp.where(half == side, w, zero) for (_, half, _), w in zip(pairs, weights)
                    ]
                    sums = product(values, jnp.concatenate(chosen, axis=0))
                    if side == 1:
                        sums = sums + product(early_values, weigh(base, highs[1]))
                    if carried is not None:
                        shrink = jnp.exp2((carried[0][side] - highs[side]) * EXP2_SCALE)
                        sums = sums + carried[1][side] * shrink
                    high_ref[at] = highs[side]
                    sums_ref[at] = sums
                    if plan["last"] and first + 6 >= count:
                        mixed = sums[:HEAD_WIDTH] / sums[HEAD_WIDTH : HEAD_WIDTH + 1]
                        mixed = jnp.transpose(mixed).astype(out_refs[i].dtype)
                        for g in range(QUERY_PER_KEY):
                            out_refs[i][
                                side * chunk : (side + 1) * chunk,
                                h * GROUP + g * HEAD_WIDTH : h * GROUP + (g + 1) * HEAD_WIDTH,
                            ] = mixed[g * chunk : (g + 1) * chunk]


def attend(plan, turned, marks, packets, state):
    heads, chunk, owners = plan["heads"], plan["chunk"], plan["owners"]
    count = len(plan["members"])
    plan = dict(plan, marks=len(marks), packets=len(packets), carried=state is not None)
    rows = QUERY_PER_KEY * chunk
    slots = owners * 2 * heads
    vmem = pl.BlockSpec(memory_space=pltpu.VMEM)
    out_shape = [
        jax.ShapeDtypeStruct((slots, 1, rows), jnp.float32),
        jax.ShapeDtypeStruct((slots, HEAD_WIDTH + HEADER, rows), jnp.float32),
    ]
    if plan["last"]:
        out_shape += [jax.ShapeDtypeStruct((2 * chunk, heads * GROUP), jnp.bfloat16)] * owners
    operands = 1 + len(marks) + len(packets)
    flops = 4 * owners * heads * rows * HEAD_WIDTH * count * chunk * 2
    return pl.pallas_call(
        functools.partial(attend_kernel, plan),
        out_shape=out_shape,
        in_specs=[vmem] * (operands + (0 if state is None else 2)),
        out_specs=[vmem] * len(out_shape),
        input_output_aliases={} if state is None else {operands: 0, operands + 1: 1},
        cost_estimate=pl.CostEstimate(
            flops=flops, bytes_accessed=4 << 20, transcendentals=flops // 512
        ),
        compiler_params=pltpu.CompilerParams(vmem_limit_bytes=VMEM_LIMIT),
        name="attend",
    )(turned, *marks, *packets, *(state or ()))


def turn_kernel(heads, chunk, whole_rows, *refs):
    q_refs, turned_ref = refs[:-1], refs[-1]
    for i, q_ref in enumerate(q_refs):
        base = my_core() * (heads * GROUP) if whole_rows[i] else 0
        for half in range(2):
            for h in range(heads):
                columns = [
                    pl.ds(pl.multiple_of(base + h * GROUP + g * HEAD_WIDTH, HEAD_WIDTH), HEAD_WIDTH)
                    for g in range(QUERY_PER_KEY)
                ]
                q = jnp.concatenate(
                    [q_ref[half * chunk : (half + 1) * chunk, at] for at in columns], axis=0
                )
                turned_ref[(2 * i + half) * heads + h] = jnp.transpose(q)


def turn(heads, chunk, whole_rows, queries):
    vmem = pl.BlockSpec(memory_space=pltpu.VMEM)
    owners = len(queries)
    shape = (2 * owners * heads, HEAD_WIDTH, QUERY_PER_KEY * chunk)
    return pl.pallas_call(
        functools.partial(turn_kernel, heads, chunk, whole_rows),
        out_shape=jax.ShapeDtypeStruct(shape, jnp.bfloat16),
        in_specs=[vmem] * owners,
        out_specs=vmem,
        cost_estimate=pl.CostEstimate(flops=1 << 20, bytes_accessed=4 << 20, transcendentals=0),
        compiler_params=pltpu.CompilerParams(vmem_limit_bytes=VMEM_LIMIT),
        name="turn",
    )(*queries)


def project_kernel(own_ref, other_ref, w_ref, sent_ref, kept_ref, rows_ref):
    chunk, part = sent_ref.shape[0], own_ref.shape[1]

    @pl.when(pl.program_id(0) == 0)
    def _():
        mine = lax.axis_index("inner").astype(jnp.int32)
        first = my_core() == 0
        for place, half in enumerate((1 - mine, mine)):
            at = pl.multiple_of(half * chunk, chunk)
            own, other = own_ref[pl.ds(at, chunk)], other_ref[pl.ds(at, chunk)]
            to = pl.ds(place * chunk, chunk)
            rows_ref[to, :part] = jnp.where(first, own, other)
            rows_ref[to, part:] = jnp.where(first, other, own)

    both = product(rows_ref[...], w_ref[...]).astype(sent_ref.dtype)
    sent_ref[...] = both[:chunk]
    kept_ref[...] = both[chunk:]


def project(own, other, out_weight, first, width, tile):
    rows, depth = own.shape[0], out_weight.shape[0]
    whole = lambda j: (0, 0)
    return pl.pallas_call(
        project_kernel,
        out_shape=[jax.ShapeDtypeStruct((rows // 2, width), jnp.bfloat16)] * 2,
        grid=(width // tile,),
        in_specs=[
            pl.BlockSpec(own.shape, whole),
            pl.BlockSpec(other.shape, whole),
            pl.BlockSpec((depth, tile), lambda j: (0, first // tile + j)),
        ],
        out_specs=[pl.BlockSpec((rows // 2, tile), lambda j: (0, j))] * 2,
        scratch_shapes=[pltpu.VMEM((rows, depth), jnp.bfloat16)],
        cost_estimate=pl.CostEstimate(
            flops=2 * rows * depth * width, bytes_accessed=2 * depth * width, transcendentals=0
        ),
        compiler_params=pltpu.CompilerParams(vmem_limit_bytes=VMEM_LIMIT),
        name="project",
    )(own, other, out_weight)


def prepare_kernel(chunk, k_ref, v_ref, position_ref, sent_ref, kept_ref, first_ref, sems):
    rows, width = k_ref.shape[0], k_ref.shape[1] // 2
    copies = [pltpu.make_async_copy(position_ref, first_ref, sems.at[4])]
    for n, (ref, core) in enumerate(((sent_ref, 1 - my_core()), (kept_ref, my_core()))):
        at = pl.ds(pl.multiple_of(core * width, width), width)
        for m, source in enumerate((k_ref, v_ref)):
            to = ref.at[pl.ds(0, rows), pl.ds(m * width, width)]
            copies.append(pltpu.make_async_copy(source.at[:, at], to, sems.at[2 * n + m]))
    for copy in copies:
        copy.start()
    copies[0].wait()
    c = lax.div(first_ref[0], jnp.int32(chunk)).astype(jnp.float32)
    header = jnp.full((HEADER, 2 * width), c, jnp.float32).astype(jnp.bfloat16)
    sent_ref[rows:] = header
    kept_ref[rows:] = header
    for copy in copies[1:]:
        copy.wait()


def prepare(keys, values, positions):
    vmem = pl.BlockSpec(memory_space=pltpu.VMEM)
    hbm = pl.BlockSpec(memory_space=pltpu.HBM)
    rows = keys.shape[0]
    return pl.pallas_call(
        functools.partial(prepare_kernel, rows // 2),
        out_shape=[jax.ShapeDtypeStruct((rows + HEADER, keys.shape[1]), jnp.bfloat16)] * 2,
        in_specs=[hbm, hbm, hbm],
        out_specs=[vmem, vmem],
        scratch_shapes=[
            pltpu.SMEM(positions.shape, jnp.int32),
            pltpu.SemaphoreType.DMA((5,)),
        ],
        compiler_params=pltpu.CompilerParams(vmem_limit_bytes=VMEM_LIMIT),
        name="prepare",
    )(keys, values, positions)


def after(value, *events):
    return lax.optimization_barrier((value, *events))[0]


def split_over_cores(count, queries, keys, values, positions):
    chips, half = count // 2, count // 4
    rows, chunk = queries.shape[0], queries.shape[0] // 2
    heads = keys.shape[1] // HEAD_WIDTH // 2
    sibling = [(b, b ^ 1) for b in range(count)]
    clock, counter = ring_pairs(chips, 1), ring_pairs(chips, -1)
    width = heads * HEAD_WIDTH

    sent, kept = prepare(keys, values, positions)
    got = lax.ppermute(sent, "blk", sibling)
    packet = jnp.concatenate(
        [kept[:rows], got[:rows], jnp.concatenate([kept[rows:, :width], got[rows:, :width]], axis=1)],
        axis=0,
    )
    q_sent = lax.dynamic_slice(
        queries, (0, (1 - my_core()) * heads * GROUP), (rows, heads * GROUP)
    )
    q_got = lax.ppermute(q_sent, "blk", sibling)

    shared = dict(heads=heads, chunk=chunk, owners=2, own_at=lambda i: i)
    shared["owner_headers"] = [(0, 2 * rows, 0), (0, 2 * rows, width)]

    def call(packets, state, own):
        each = range(len(packets))
        members = [(j, i * rows) for j in each for i in range(2)]
        headers = [(1 + j, 2 * rows, i * width) for j in each for i in range(2)]
        plan = dict(shared, own=own, last=False, members=members, headers=headers)
        return attend(plan, turned, [packet], packets, state)

    turned = turn(heads, chunk, (True, False), [queries, q_got])
    ups, downs, state = [packet], [packet], None
    for r in range(1, half):
        up, down = ups[-1], downs[-1]
        if r == 2:
            up, down, turned = lax.optimization_barrier((up, down, turned))
        elif r > 2:
            up, down, *state = lax.optimization_barrier((up, down, *state))
        ups.append(lax.ppermute(up, "blk", clock))
        downs.append(lax.ppermute(down, "blk", counter))
        if r >= 2:
            here = [ups[r - 1], downs[r - 1]]
            state = call([packet] + here if r == 2 else here, state, r == 2)
    up, down, *state = lax.optimization_barrier((ups[-1], downs[-1], *state))
    far_up = lax.ppermute(up[:rows], "blk", clock)
    far_down = lax.ppermute(down[rows:], "blk", counter)
    state = call([up, down], state, False)
    plan = dict(
        shared,
        own=False,
        last=True,
        members=[(0, 0), (1, 0)],
        headers=[(2, rows, 0), (2, rows, width)],
    )
    _, _, own, theirs = attend(plan, turned, [packet], [far_up, far_down], state)
    return own, lax.ppermute(theirs, "blk", sibling)


def one_head_a_device(count, queries, keys, values, positions):
    rows, chunk = queries.shape[0], queries.shape[0] // 2
    heads = keys.shape[1] // HEAD_WIDTH
    c = (positions[:1] // chunk).astype(jnp.bfloat16).reshape(1, 1)
    header = jnp.broadcast_to(c, (HEADER, 2 * keys.shape[1]))
    packet = jnp.concatenate([jnp.concatenate([keys, values], axis=1), header], axis=0)
    packets = lax.all_gather(packet, "blk", axis=0, tiled=True)
    size = rows + HEADER
    here = lax.axis_index("blk")
    order = lax.rem(here + jnp.arange(count), count)
    packets = packets.reshape(count, size, -1)[order].reshape(count * size, -1)
    plan = dict(
        heads=heads,
        chunk=chunk,
        owners=1,
        own=True,
        own_at=lambda i: 0,
        last=True,
        members=[(0, j * size) for j in range(count)],
        headers=[(0, j * size + rows, 0) for j in range(count)],
        owner_headers=[(0, rows, 0)],
    )
    turned = turn(heads, chunk, (False,), [queries])
    return attend(plan, turned, [], [packets], None)[2]


def shards(count, inner, queries, keys, values, positions, out_weight):
    heads = keys.shape[1] // HEAD_WIDTH
    if heads % 2:
        attended = one_head_a_device(count, queries, keys, values, positions)
        partial = jnp.dot(attended, out_weight, preferred_element_type=jnp.float32)
        return lax.psum_scatter(
            partial.astype(jnp.bfloat16), "inner", scatter_dimension=0, tiled=True
        )
    own, other = split_over_cores(count, queries, keys, values, positions)
    out_weight = pltpu.with_memory_space_constraint(out_weight, pltpu.HBM)
    width, tile = out_weight.shape[1], 512
    shares = (2, 2, 3, 3)
    received, kept, first, source = [], [], 0, own
    for j, share in enumerate(shares):
        columns = width * share // sum(shares)
        if j > 0:
            source = after(own, sent, *received[: j - 1][-1:])
        sent, keep = project(source, other, out_weight, first, columns, tile)
        received.append(lax.ppermute(sent, "inner", [(0, 1), (1, 0)]))
        kept.append(keep)
        first += columns
    mine, theirs = jnp.concatenate(kept, axis=1), jnp.concatenate(received, axis=1)
    return (mine.astype(jnp.float32) + theirs.astype(jnp.float32)).astype(jnp.bfloat16)


def solution(mesh):
    placed = (P("blk", "inner"), P("blk", "inner"), P("blk", "inner"), P("blk"), P("inner", None))
    return jax.shard_map(
        functools.partial(shards, mesh.shape["blk"], mesh.shape["inner"]),
        mesh=mesh,
        in_specs=placed,
        out_specs=P(("blk", "inner"), None),
        check_vma=False,
    )
```

time: 97.2 us -> 89.6 us (0.922)
  Pallas kernels: 50.7 us -> 32.9 us
  waiting for transfers between devices: 27.4 us -> 36.7 us
  local copies, waits for them, and re-layouts: 2.71 us -> 3.74 us
    pallas_call x4, Pallas kernels: 29.1 us -> 15.5 us  [attend(): pl.pallas_call(functools.partial(attend_kernel, plan), out_shape=out_shap...]
    ppermute x3, waiting for transfers between devices: 11 us -> 15.9 us  [split_over_cores(): ups.append(lax.ppermute(up, 'blk', clock))]
    pallas_call x4, Pallas kernels: 21 us -> 16.4 us  [project(): pl.pallas_call(project_kernel, out_shape=[jax.ShapeDtypeStruct((rows // 2...]
    ppermute x3, waiting for transfers between devices: 1.19 us -> 4.92 us  [split_over_cores(): downs.append(lax.ppermute(down, 'blk', counter))]
    ppermute x4, waiting for transfers between devices: 12.2 us -> 14 us  [shards(): received.append(lax.ppermute(sent, 'inner', [(0, 1), (1, 0)]))]
    ppermute x1, waiting for transfers between devices: 1.06 us -> 0.01 us  [split_over_cores(): got = lax.ppermute(sent, 'blk', sibling)]
    dynamic_slice x1, local copies, waits for them, and re-layouts: 0.03 us -> 1.06 us  [split_over_cores(): lax.dynamic_slice(queries, (0, (1 - my_core()) * heads * GROUP), (rows, h...]
  transfers between devices with their start and end apart: 15 -> 15, of which waited for: 7 -> 10; matrix products, arithmetic and copies ran while one was open for 0% -> 1% of each run, Pallas kernels for 35% -> 24%
where the time goes in v3:
time: 89.6 us; the launch traced here: 89.3 us
  waiting for transfers between devices  36.7 us (41%)
  Pallas kernels  32.9 us (37%)
  starting transfers between devices  14.5 us (16%)
  local copies, waits for them, and re-layouts  3.74 us (4%)
  other arithmetic  1.22 us (1%)
    pallas_call x4, Pallas kernels, project(): pl.pallas_call(project_kernel, out_shape=[jax.ShapeDtypeStruct((rows // 2...  16.4 us
    ppermute x3, waiting for transfers between devices, split_over_cores(): ups.append(lax.ppermute(up, 'blk', clock))  15.9 us
    pallas_call x4, Pallas kernels, attend(): pl.pallas_call(functools.partial(attend_kernel, plan), out_shape=out_shap...  15.5 us
    ppermute x4, waiting for transfers between devices, shards(): received.append(lax.ppermute(sent, 'inner', [(0, 1), (1, 0)]))  14 us
    ppermute x3, starting transfers between devices, split_over_cores(): ups.append(lax.ppermute(up, 'blk', clock))  6.23 us
    ppermute x3, waiting for transfers between devices, split_over_cores(): downs.append(lax.ppermute(down, 'blk', counter))  4.92 us
    ppermute x4, starting transfers between devices, shards(): received.append(lax.ppermute(sent, 'inner', [(0, 1), (1, 0)]))  4.36 us
    unnamed x8, local copies, waits for them, and re-layouts  2.62 us
  transfers between devices with their start and end apart: 15, of which 10 were waited for; matrix products, arithmetic and copies ran while one was open for 1% of the time, Pallas kernels for 24%

profile of v3, /device:TPU:0, one launch (start us, length us, event | category | flops | bytes accessed | tf_op | source)
XLA Modules:
  0.0 89.3 jit_solution(12554392187262612100)
XLA Ops:
  0.0 0.0 copy-start
  0.0 0.0 copy-start.1
  0.0 1.0 %copy-done.1 = bf16[192,512]{1,0:T(8,128)(2,1)S(1)} copy-done((bf16[192,512]{1,0:T(8,128)(2,1)S(1)}, bf16[192,512]{1,0:T(8,128)(2,1)}, u32[]{:S(2)}) %copy-start.1) | copy-done | bytes 196632
  1.0 0.9 %copy-done.2 = bf16[192,512]{1,0:T(8,128)(2,1)S(1)} copy-done((bf16[192,512]{1,0:T(8,128)(2,1)S(1)}, bf16[192,512]{1,0:T(8,128)(2,1)}, u32[]{:S(2)}) %copy-start.2) | copy-done | bytes 196632
  1.9 0.7 copy-done.3
  2.6 0.6 prepare.1
  3.2 0.5 collective-permute-start
  3.8 1.1 %constant_dynamic-slice_fusion = bf16[192,1280]{1,0:T(8,128)(2,1)S(1)} fusion(bf16[192,2560]{1,0:T(8,128)(2,1)} %refs_0_.1, s32[]{:T(128)S(6)} %select_n.3), kind=kLoop, calls=%fused_computation.2 | loop fusion | bytes 983044 | tf_op jit(solution)/shard_map/dynamic_slice | solution.py:305
  4.8 0.1 collective-permute-start.3
  5.0 0.0 collective-permute-done
  5.1 3.1 %collective-permute-start.1 = (bf16[400,512]{1,0:T(8,128)(2,1)S(1)}, bf16[400,512]{1,0:T(8,128)(2,1)S(1)}, u32[]{:S(2)}, u32[]{:S(2)}) collective-permute-start(bf16[400,512]{1,0:T(8,128)(2,1)S(1)} %maximum_maximum_fusion.refs_1_.refs_2_), channel_id=1, source_target_pairs={{0,8},{2,10},{8,16},{10,18},{16,24},{18,26},{24,28},{26,30},{28,20... | collective-permute-start | bytes 1228808 | tf_op jit(solution)/shard_map/ppermute | solution.py:328
  8.1 0.0 collective-permute-start.2
  8.1 0.0 collective-permute-done.3.refs_1_
  8.1 0.0 copy-done
  8.1 0.3 turn.1.refs_0_
  8.5 9.2 %collective-permute-done.1.refs_3_ = bf16[400,512]{1,0:T(8,128)(2,1)S(1)} collective-permute-done((bf16[400,512]{1,0:T(8,128)(2,1)S(1)}, bf16[400,512]{1,0:T(8,128)(2,1)S(1)}, u32[]{:S(2)}, u32[]{:S(2)}) %collective-permute-start.1) | collective-permute-done | bytes 409632 | tf_op jit(solution)/shard_map/ppermute | solution.py:328
  17.7 1.5 %collective-permute-done.2.refs_4_ = bf16[400,512]{1,0:T(8,128)(2,1)S(1)} collective-permute-done((bf16[400,512]{1,0:T(8,128)(2,1)S(1)}, bf16[400,512]{1,0:T(8,128)(2,1)S(1)}, u32[]{:S(2)}, u32[]{:S(2)}) %collective-permute-start.2) | collective-permute-done | bytes 409632 | tf_op jit(solution)/shard_map/ppermute | solution.py:329
  19.2 1.6 %collective-permute-start.4 = (bf16[400,512]{1,0:T(8,128)(2,1)S(1)}, bf16[400,512]{1,0:T(8,128)(2,1)S(1)}, u32[]{:S(2)}, u32[]{:S(2)}) collective-permute-start(bf16[400,512]{1,0:T(8,128)(2,1)S(1)} %collective-permute-done.1.refs_3_), channel_id=1, source_target_pairs={{0,8},{2,10},{8,16},{10,18},{16,24},{18,26},{24,28},{26,30},{28,20... | collective-permute-start | bytes 1228808 | tf_op jit(solution)/shard_map/ppermute | solution.py:328
  20.8 0.4 collective-permute-start.5
  21.3 4.4 %attend.4 = (f32[8,1,480]{2,1,0:T(1,128)S(1)}, f32[8,144,480]{2,1,0:T(8,128)S(1)}) custom-call(bf16[8,128,480]{2,1,0:T(8,128)(2,1)S(1)} %turn.1.refs_0_, bf16[400,512]{1,0:T(8,128)(2,1)S(1)} %maximum_maximum_fusion.refs_1_.refs_2_, bf16[400,512]{1,0:T(8,128)(2,1)S(1)} %maximum_maximum_fusion.refs_1_.refs_2_, ...), custom_call_target="tpu_custom_call" | custom-call | flops 1132462080 | bytes 4194304 | tf_op jit(solution)/shard_map/attend/pallas_call | solution.py:164
  25.7 3.8 %collective-permute-done.4.refs_2_ = bf16[400,512]{1,0:T(8,128)(2,1)S(1)} collective-permute-done((bf16[400,512]{1,0:T(8,128)(2,1)S(1)}, bf16[400,512]{1,0:T(8,128)(2,1)S(1)}, u32[]{:S(2)}, u32[]{:S(2)}) %collective-permute-start.4) | collective-permute-done | bytes 409632 | tf_op jit(solution)/shard_map/ppermute | solution.py:328
  29.5 1.3 %collective-permute-done.5.refs_3_ = bf16[400,512]{1,0:T(8,128)(2,1)S(1)} collective-permute-done((bf16[400,512]{1,0:T(8,128)(2,1)S(1)}, bf16[400,512]{1,0:T(8,128)(2,1)S(1)}, u32[]{:S(2)}, u32[]{:S(2)}) %collective-permute-start.5) | collective-permute-done | bytes 409632 | tf_op jit(solution)/shard_map/ppermute | solution.py:329
  30.8 1.6 %collective-permute-start.6 = (bf16[400,512]{1,0:T(8,128)(2,1)S(1)}, bf16[400,512]{1,0:T(8,128)(2,1)S(1)}, u32[]{:S(2)}, u32[]{:S(2)}) collective-permute-start(bf16[400,512]{1,0:T(8,128)(2,1)S(1)} %collective-permute-done.4.refs_2_), channel_id=1, source_target_pairs={{0,8},{2,10},{8,16},{10,18},{16,24},{18,26},{24,28},{26,30},{28,20... | collective-permute-start | bytes 1228808 | tf_op jit(solution)/shard_map/ppermute | solution.py:328
  32.4 0.4 collective-permute-start.7
  32.8 4.1 %attend.5 = (f32[8,1,480]{2,1,0:T(1,128)S(1)}, f32[8,144,480]{2,1,0:T(8,128)S(1)}) custom-call(bf16[8,128,480]{2,1,0:T(8,128)(2,1)S(1)} %turn.1.refs_0_, bf16[400,512]{1,0:T(8,128)(2,1)S(1)} %maximum_maximum_fusion.refs_1_.refs_2_, bf16[400,512]{1,0:T(8,128)(2,1)S(1)} %collective-permute-done.4.refs_2_, ...), custom_call_target="tpu_custom_call", output_to_operand_aliasing={{0}: (4, {}), {1}: (5, {})} | custom-call | flops 754974720 | bytes 4194304 | tf_op jit(solution)/shard_map/attend/pallas_call | solution.py:164
  36.9 2.9 %collective-permute-done.6.refs_2_ = bf16[400,512]{1,0:T(8,128)(2,1)S(1)} collective-permute-done((bf16[400,512]{1,0:T(8,128)(2,1)S(1)}, bf16[400,512]{1,0:T(8,128)(2,1)S(1)}, u32[]{:S(2)}, u32[]{:S(2)}) %collective-permute-start.6) | collective-permute-done | bytes 409632 | tf_op jit(solution)/shard_map/ppermute | solution.py:328
  39.8 2.1 %collective-permute-done.7.refs_3_ = bf16[400,512]{1,0:T(8,128)(2,1)S(1)} collective-permute-done((bf16[400,512]{1,0:T(8,128)(2,1)S(1)}, bf16[400,512]{1,0:T(8,128)(2,1)S(1)}, u32[]{:S(2)}, u32[]{:S(2)}) %collective-permute-start.7) | collective-permute-done | bytes 409632 | tf_op jit(solution)/shard_map/ppermute | solution.py:329
  41.9 0.5 collective-permute-start.9
  42.4 1.8 %collective-permute-start.8 = (bf16[192,512]{1,0:T(8,128)(2,1)S(1)}, bf16[192,512]{1,0:T(8,128)(2,1)S(1)}, u32[]{:S(2)}, u32[]{:S(2)}) collective-permute-start(bf16[192,512]{1,0:T(8,128)(2,1)S(1)} %slice.22), channel_id=1, source_target_pairs={{0,8},{2,10},{8,16},{10,18},{16,24},{18,26},{24,28},{26,30},{28,20... | collective-permute-start | bytes 589832 | tf_op jit(solution)/shard_map/ppermute | solution.py:334
  44.3 4.1 %attend.6 = (f32[8,1,480]{2,1,0:T(1,128)S(1)}, f32[8,144,480]{2,1,0:T(8,128)S(1)}) custom-call(bf16[8,128,480]{2,1,0:T(8,128)(2,1)S(1)} %turn.1.refs_0_, bf16[400,512]{1,0:T(8,128)(2,1)S(1)} %maximum_maximum_fusion.refs_1_.refs_2_, bf16[400,512]{1,0:T(8,128)(2,1)S(1)} %collective-permute-done.6.refs_2_, ...), custom_call_target="tpu_custom_call", output_to_operand_aliasing={{0}: (4, {}), {1}: (5, {})} | custom-call | flops 754974720 | bytes 4194304 | tf_op jit(solution)/shard_map/attend/pallas_call | solution.py:164
  48.3 0.0 collective-permute-done.8.refs_2_
  48.4 0.0 collective-permute-done.9.refs_3_
  48.4 3.0 %attend.7 = (f32[8,1,480]{2,1,0:T(1,128)S(1)}, f32[8,144,480]{2,1,0:T(8,128)S(1)}, bf16[192,1280]{1,0:T(8,128)(2,1)S(1)}, bf16[192,1280]{1,0:T(8,128)(2,1)S(1)}) custom-call(bf16[8,128,480]{2,1,0:T(8,128)(2,1)S(1)} %turn.1.refs_0_, bf16[400,512]{1,0:T(8,128)(2,1)S(1)} %maximum_maximum_fusion.refs_1_.refs_2_, ...), custom_call_target="tpu_custom_call", output_to_operand_aliasing={{0}: (4, {}), {1}: (5, {})} | custom-call | flops 377487360 | bytes 4194304 | tf_op jit(solution)/shard_map/attend/pallas_call | solution.py:164
  51.3 0.1 collective-permute-start.10
  51.4 1.9 %collective-permute-done.10.other_ref = bf16[192,1280]{1,0:T(8,128)(2,1)S(1)} collective-permute-done((bf16[192,1280]{1,0:T(8,128)(2,1)S(1)}, bf16[192,1280]{1,0:T(8,128)(2,1)S(1)}, u32[]{:S(2)}, u32[]{:S(2)}) %collective-permute-start.10) | collective-permute-done | bytes 491552 | tf_op jit(solution)/shard_map/ppermute | solution.py:345
  53.3 3.2 %project.4 = (bf16[96,1024]{1,0:T(8,128)(2,1)S(1)}, bf16[96,1024]{1,0:T(8,128)(2,1)S(1)}) custom-call(bf16[192,1280]{1,0:T(8,128)(2,1)S(1)} %get-tuple-element.66.own_ref, bf16[192,1280]{1,0:T(8,128)(2,1)S(1)} %collective-permute-done.10.other_ref, bf16[2560,5120]{1,0:T(8,128)(2,1)} %w_ref.7), custom_call_target="tpu_custom_call" | custom-call | flops 1006632960 | bytes 5242880 | tf_op jit(solution)/shard_map/project/pallas_call | solution.py:231
  56.5 1.6 %collective-permute-start.11 = (bf16[96,1024]{1,0:T(8,128)(2,1)S(1)}, bf16[96,1024]{1,0:T(8,128)(2,1)S(1)}, u32[]{:S(2)}, u32[]{:S(2)}) collective-permute-start(bf16[96,1024]{1,0:T(8,128)(2,1)S(1)} %get-tuple-element.59), channel_id=1, source_target_pairs={{0,1},{1,0},{2,3},{3,2},{4,5},{5,4},{6,7},{7,6},{8,9},{9,8},{10,11... | collective-permute-start | bytes 589832 | tf_op jit(solution)/shard_map/ppermute | solution.py:392
  58.1 3.3 %project.5 = (bf16[96,1024]{1,0:T(8,128)(2,1)S(1)}, bf16[96,1024]{1,0:T(8,128)(2,1)S(1)}) custom-call(bf16[192,1280]{1,0:T(8,128)(2,1)S(1)} %get-tuple-element.66.own_ref, bf16[192,1280]{1,0:T(8,128)(2,1)S(1)} %collective-permute-done.10.other_ref, bf16[2560,5120]{1,0:T(8,128)(2,1)} %w_ref.7), custom_call_target="tpu_custom_call" | custom-call | flops 1006632960 | bytes 5242880 | tf_op jit(solution)/shard_map/project/pallas_call | solution.py:231
  61.3 0.6 collective-permute-start.12
  61.9 1.6 %collective-permute-done.11 = bf16[96,1024]{1,0:T(8,128)(2,1)S(1)} collective-permute-done((bf16[96,1024]{1,0:T(8,128)(2,1)S(1)}, bf16[96,1024]{1,0:T(8,128)(2,1)S(1)}, u32[]{:S(2)}, u32[]{:S(2)}) %collective-permute-start.11) | collective-permute-done | bytes 196640 | tf_op jit(solution)/shard_map/ppermute | solution.py:392
  63.5 5.0 %project.6 = (bf16[96,1536]{1,0:T(8,128)(2,1)S(1)}, bf16[96,1536]{1,0:T(8,128)(2,1)S(1)}) custom-call(bf16[192,1280]{1,0:T(8,128)(2,1)S(1)} %get-tuple-element.66.own_ref, bf16[192,1280]{1,0:T(8,128)(2,1)S(1)} %collective-permute-done.10.other_ref, bf16[2560,5120]{1,0:T(8,128)(2,1)} %w_ref.7), custom_call_target="tpu_custom_call" | custom-call | flops 1509949440 | bytes 7864320 | tf_op jit(solution)/shard_map/project/pallas_call | solution.py:231
  68.5 0.0 collective-permute-done.12
  68.5 5.0 %project.7 = (bf16[96,1536]{1,0:T(8,128)(2,1)S(1)}, bf16[96,1536]{1,0:T(8,128)(2,1)S(1)}) custom-call(bf16[192,1280]{1,0:T(8,128)(2,1)S(1)} %get-tuple-element.66.own_ref, bf16[192,1280]{1,0:T(8,128)(2,1)S(1)} %collective-permute-done.10.other_ref, bf16[2560,5120]{1,0:T(8,128)(2,1)} %w_ref.7), custom_call_target="tpu_custom_call" | custom-call | flops 1509949440 | bytes 7864320 | tf_op jit(solution)/shard_map/project/pallas_call | solution.py:231
  73.5 2.1 %collective-permute-start.14 = (bf16[96,1536]{1,0:T(8,128)(2,1)S(1)}, bf16[96,1536]{1,0:T(8,128)(2,1)S(1)}, u32[]{:S(2)}, u32[]{:S(2)}) collective-permute-start(bf16[96,1536]{1,0:T(8,128)(2,1)S(1)} %get-tuple-element.68), channel_id=1, source_target_pairs={{0,1},{1,0},{2,3},{3,2},{4,5},{5,4},{6,7},{7,6},{8,9},{9,8},{10,11... | collective-permute-start | bytes 884744 | tf_op jit(solution)/shard_map/ppermute | solution.py:392
  75.6 0.1 collective-permute-start.13
  75.7 7.8 %collective-permute-done.14 = bf16[96,1536]{1,0:T(8,128)(2,1)S(1)} collective-permute-done((bf16[96,1536]{1,0:T(8,128)(2,1)S(1)}, bf16[96,1536]{1,0:T(8,128)(2,1)S(1)}, u32[]{:S(2)}, u32[]{:S(2)}) %collective-permute-start.14) | collective-permute-done | bytes 294944 | tf_op jit(solution)/shard_map/ppermute | solution.py:392
  83.6 4.6 %collective-permute-done.13 = bf16[96,1536]{1,0:T(8,128)(2,1)S(1)} collective-permute-done((bf16[96,1536]{1,0:T(8,128)(2,1)S(1)}, bf16[96,1536]{1,0:T(8,128)(2,1)S(1)}, u32[]{:S(2)}, u32[]{:S(2)}) %collective-permute-start.13) | collective-permute-done | bytes 294944 | tf_op jit(solution)/shard_map/ppermute | solution.py:392
  88.1 1.2 %add_convert_fusion = bf16[96,5120]{1,0:T(8,128)(2,1)} fusion(bf16[96,1536]{1,0:T(8,128)(2,1)S(1)} %get-tuple-element.67, bf16[96,1536]{1,0:T(8,128)(2,1)S(1)} %get-tuple-element.64, bf16[96,1024]{1,0:T(8,128)(2,1)S(1)} %get-tuple-element.61, bf16[96,1024]{1,0:T(8,128)(2,1)S(1)} %get-tuple-element.58, bf16[96,1536]{1,0:T(8,128)(2,1)S(1)} %collective-permute-done.14, ...), kind=kLoop, calls=%fused_computation | loop fusion | flops 8847360 | bytes 2949120 | tf_op jit(solution)/shard_map/convert_element_type | solution.py:396
  (9 shorter events, 0.1 us)
Async XLA Ops:
  0.0 8.1 %copy-start = (bf16[192,2560]{1,0:T(8,128)(2,1)S(1)}, bf16[192,2560]{1,0:T(8,128)(2,1)}, u32[]{:S(2)}) copy-start(bf16[192,2560]{1,0:T(8,128)(2,1)} %refs_0_.1) | copy-start | bytes 2949124
  0.0 1.0 %copy-start.1 = (bf16[192,512]{1,0:T(8,128)(2,1)S(1)}, bf16[192,512]{1,0:T(8,128)(2,1)}, u32[]{:S(2)}) copy-start(bf16[192,512]{1,0:T(8,128)(2,1)} %k_ref.1) | copy-start | bytes 589828
  1.0 0.9 %copy-start.2 = (bf16[192,512]{1,0:T(8,128)(2,1)S(1)}, bf16[192,512]{1,0:T(8,128)(2,1)}, u32[]{:S(2)}) copy-start(bf16[192,512]{1,0:T(8,128)(2,1)} %v_ref.1) | copy-start | bytes 589828
  1.9 0.7 copy-start.3
  3.2 1.7 %collective-permute-start = (bf16[208,512]{1,0:T(8,128)(2,1)S(1)}, bf16[208,512]{1,0:T(8,128)(2,1)S(1)}, u32[]{:S(2)}, u32[]{:S(2)}) collective-permute-start(bf16[208,512]{1,0:T(8,128)(2,1)S(1)} %get-tuple-element.38), channel_id=1, source_target_pairs={{0,2},{2,0},{4,6},{6,4},{8,10},{10,8},{12,14},{14,12},{16,18},{18,... | collective-permute-start | bytes 638984 | tf_op jit(solution)/shard_map/ppermute | solution.py:300
  4.8 3.3 %collective-permute-start.3 = (bf16[192,1280]{1,0:T(8,128)(2,1)S(1)}, bf16[192,1280]{1,0:T(8,128)(2,1)S(1)}, u32[]{:S(2)}, u32[]{:S(2)}) collective-permute-start(bf16[192,1280]{1,0:T(8,128)(2,1)S(1)} %constant_dynamic-slice_fusion), channel_id=1, source_target_pairs={{0,2},{2,0},{4,6},{6,4},{8,10},{10,8},{12,14},{14,12},{16,18},{18,... | collective-permute-start | bytes 1474568 | tf_op jit(solution)/shard_map/ppermute | solution.py:308
  5.1 12.7 %collective-permute-start.1 = (bf16[400,512]{1,0:T(8,128)(2,1)S(1)}, bf16[400,512]{1,0:T(8,128)(2,1)S(1)}, u32[]{:S(2)}, u32[]{:S(2)}) collective-permute-start(bf16[400,512]{1,0:T(8,128)(2,1)S(1)} %maximum_maximum_fusion.refs_1_.refs_2_), channel_id=1, source_target_pairs={{0,8},{2,10},{8,16},{10,18},{16,24},{18,26},{24,28},{26,30},{28,20... | collective-permute-start | bytes 1228808 | tf_op jit(solution)/shard_map/ppermute | solution.py:328
  8.1 11.1 %collective-permute-start.2 = (bf16[400,512]{1,0:T(8,128)(2,1)S(1)}, bf16[400,512]{1,0:T(8,128)(2,1)S(1)}, u32[]{:S(2)}, u32[]{:S(2)}) collective-permute-start(bf16[400,512]{1,0:T(8,128)(2,1)S(1)} %maximum_maximum_fusion.refs_1_.refs_2_), channel_id=1, source_target_pairs={{0,4},{2,6},{8,0},{10,2},{16,8},{18,10},{24,16},{26,18},{28,24},{3... | collective-permute-start | bytes 1228808 | tf_op jit(solution)/shard_map/ppermute | solution.py:329
  19.2 10.2 %collective-permute-start.4 = (bf16[400,512]{1,0:T(8,128)(2,1)S(1)}, bf16[400,512]{1,0:T(8,128)(2,1)S(1)}, u32[]{:S(2)}, u32[]{:S(2)}) collective-permute-start(bf16[400,512]{1,0:T(8,128)(2,1)S(1)} %collective-permute-done.1.refs_3_), channel_id=1, source_target_pairs={{0,8},{2,10},{8,16},{10,18},{16,24},{18,26},{24,28},{26,30},{28,20... | collective-permute-start | bytes 1228808 | tf_op jit(solution)/shard_map/ppermute | solution.py:328
  20.8 9.9 %collective-permute-start.5 = (bf16[400,512]{1,0:T(8,128)(2,1)S(1)}, bf16[400,512]{1,0:T(8,128)(2,1)S(1)}, u32[]{:S(2)}, u32[]{:S(2)}) collective-permute-start(bf16[400,512]{1,0:T(8,128)(2,1)S(1)} %collective-permute-done.2.refs_4_), channel_id=1, source_target_pairs={{0,4},{2,6},{8,0},{10,2},{16,8},{18,10},{24,16},{26,18},{28,24},{3... | collective-permute-start | bytes 1228808 | tf_op jit(solution)/shard_map/ppermute | solution.py:329
  30.8 9.0 %collective-permute-start.6 = (bf16[400,512]{1,0:T(8,128)(2,1)S(1)}, bf16[400,512]{1,0:T(8,128)(2,1)S(1)}, u32[]{:S(2)}, u32[]{:S(2)}) collective-permute-start(bf16[400,512]{1,0:T(8,128)(2,1)S(1)} %collective-permute-done.4.refs_2_), channel_id=1, source_target_pairs={{0,8},{2,10},{8,16},{10,18},{16,24},{18,26},{24,28},{26,30},{28,20... | collective-permute-start | bytes 1228808 | tf_op jit(solution)/shard_map/ppermute | solution.py:328
  32.4 9.6 %collective-permute-start.7 = (bf16[400,512]{1,0:T(8,128)(2,1)S(1)}, bf16[400,512]{1,0:T(8,128)(2,1)S(1)}, u32[]{:S(2)}, u32[]{:S(2)}) collective-permute-start(bf16[400,512]{1,0:T(8,128)(2,1)S(1)} %collective-permute-done.5.refs_3_), channel_id=1, source_target_pairs={{0,4},{2,6},{8,0},{10,2},{16,8},{18,10},{24,16},{26,18},{28,24},{3... | collective-permute-start | bytes 1228808 | tf_op jit(solution)/shard_map/ppermute | solution.py:329
  41.9 6.4 %collective-permute-start.9 = (bf16[208,512]{1,0:T(8,128)(2,1)S(1)}, bf16[208,512]{1,0:T(8,128)(2,1)S(1)}, u32[]{:S(2)}, u32[]{:S(2)}) collective-permute-start(bf16[208,512]{1,0:T(8,128)(2,1)S(1)} %slice.23), channel_id=1, source_target_pairs={{0,4},{2,6},{8,0},{10,2},{16,8},{18,10},{24,16},{26,18},{28,24},{3... | collective-permute-start | bytes 638984 | tf_op jit(solution)/shard_map/ppermute | solution.py:335
  42.4 5.9 %collective-permute-start.8 = (bf16[192,512]{1,0:T(8,128)(2,1)S(1)}, bf16[192,512]{1,0:T(8,128)(2,1)S(1)}, u32[]{:S(2)}, u32[]{:S(2)}) collective-permute-start(bf16[192,512]{1,0:T(8,128)(2,1)S(1)} %slice.22), channel_id=1, source_target_pairs={{0,8},{2,10},{8,16},{10,18},{16,24},{18,26},{24,28},{26,30},{28,20... | collective-permute-start | bytes 589832 | tf_op jit(solution)/shard_map/ppermute | solution.py:334
  51.3 1.9 %collective-permute-start.10 = (bf16[192,1280]{1,0:T(8,128)(2,1)S(1)}, bf16[192,1280]{1,0:T(8,128)(2,1)S(1)}, u32[]{:S(2)}, u32[]{:S(2)}) collective-permute-start(bf16[192,1280]{1,0:T(8,128)(2,1)S(1)} %get-tuple-element.57), channel_id=1, source_target_pairs={{0,2},{2,0},{4,6},{6,4},{8,10},{10,8},{12,14},{14,12},{16,18},{18,... | collective-permute-start | bytes 1474568 | tf_op jit(solution)/shard_map/ppermute | solution.py:345
  56.5 7.0 %collective-permute-start.11 = (bf16[96,1024]{1,0:T(8,128)(2,1)S(1)}, bf16[96,1024]{1,0:T(8,128)(2,1)S(1)}, u32[]{:S(2)}, u32[]{:S(2)}) collective-permute-start(bf16[96,1024]{1,0:T(8,128)(2,1)S(1)} %get-tuple-element.59), channel_id=1, source_target_pairs={{0,1},{1,0},{2,3},{3,2},{4,5},{5,4},{6,7},{7,6},{8,9},{9,8},{10,11... | collective-permute-start | bytes 589832 | tf_op jit(solution)/shard_map/ppermute | solution.py:392
  61.3 7.2 %collective-permute-start.12 = (bf16[96,1024]{1,0:T(8,128)(2,1)S(1)}, bf16[96,1024]{1,0:T(8,128)(2,1)S(1)}, u32[]{:S(2)}, u32[]{:S(2)}) collective-permute-start(bf16[96,1024]{1,0:T(8,128)(2,1)S(1)} %get-tuple-element.62), channel_id=1, source_target_pairs={{0,1},{1,0},{2,3},{3,2},{4,5},{5,4},{6,7},{7,6},{8,9},{9,8},{10,11... | collective-permute-start | bytes 589832 | tf_op jit(solution)/shard_map/ppermute | solution.py:392
  73.5 10.1 %collective-permute-start.14 = (bf16[96,1536]{1,0:T(8,128)(2,1)S(1)}, bf16[96,1536]{1,0:T(8,128)(2,1)S(1)}, u32[]{:S(2)}, u32[]{:S(2)}) collective-permute-start(bf16[96,1536]{1,0:T(8,128)(2,1)S(1)} %get-tuple-element.68), channel_id=1, source_target_pairs={{0,1},{1,0},{2,3},{3,2},{4,5},{5,4},{6,7},{7,6},{8,9},{9,8},{10,11... | collective-permute-start | bytes 884744 | tf_op jit(solution)/shard_map/ppermute | solution.py:392
  75.6 12.5 %collective-permute-start.13 = (bf16[96,1536]{1,0:T(8,128)(2,1)S(1)}, bf16[96,1536]{1,0:T(8,128)(2,1)S(1)}, u32[]{:S(2)}, u32[]{:S(2)}) collective-permute-start(bf16[96,1536]{1,0:T(8,128)(2,1)S(1)} %get-tuple-element.65), channel_id=1, source_target_pairs={{0,1},{1,0},{2,3},{3,2},{4,5},{5,4},{6,7},{7,6},{8,9},{9,8},{10,11... | collective-permute-start | bytes 884744 | tf_op jit(solution)/shard_map/ppermute | solution.py:392

commit v4 on v3

--- a/solution.py
+++ b/solution.py
@@ -206,48 +206,58 @@
     )(*queries)
 
 
-def project_kernel(own_ref, other_ref, w_ref, sent_ref, kept_ref, rows_ref):
-    chunk, part = sent_ref.shape[0], own_ref.shape[1]
-
-    @pl.when(pl.program_id(0) == 0)
+def project_kernel(keep, own_ref, other_ref, w_ref, out_ref, rows_ref, total_ref):
+    step = pl.program_id(0)
+    chunk, part = rows_ref.shape[0], own_ref.shape[1]
+    depth = w_ref.shape[0]
+
+    @pl.when(step == 0)
     def _():
         mine = lax.axis_index("inner").astype(jnp.int32)
-        first = my_core() == 0
-        for place, half in enumerate((1 - mine, mine)):
-            at = pl.multiple_of(half * chunk, chunk)
-            own, other = own_ref[pl.ds(at, chunk)], other_ref[pl.ds(at, chunk)]
-            to = pl.ds(place * chunk, chunk)
-            rows_ref[to, :part] = jnp.where(first, own, other)
-            rows_ref[to, part:] = jnp.where(first, other, own)
-
-    both = product(rows_ref[...], w_ref[...]).astype(sent_ref.dtype)
-    sent_ref[...] = both[:chunk]
-    kept_ref[...] = both[chunk:]
-
-
-def project(own, other, out_weight, first, width, tile):
-    rows, depth = own.shape[0], out_weight.shape[0]
+        half = mine if keep else 1 - mine
+        at = pl.ds(pl.multiple_of(half * chunk, chunk), chunk)
+        own, other = own_ref[at], other_ref[at]
+        left = my_core() == 0
+        rows_ref[:, :part] = jnp.where(left, own, other)
+        rows_ref[:, part:] = jnp.where(left, other, own)
+        total_ref[...] = jnp.zeros_like(total_ref)
+
+    at = pl.multiple_of(step * depth, depth)
+    total_ref[...] += product(rows_ref[:, pl.ds(at, depth)], w_ref[...])
+
+    @pl.when(step == pl.num_programs(0) - 1)
+    def _():
+        out_ref[...] = total_ref[...].astype(out_ref.dtype)
+
+
+def project(own, other, out_weight, first, width, depth, keep):
+    chunk = own.shape[0] // 2
     whole = lambda j: (0, 0)
     return pl.pallas_call(
-        project_kernel,
-        out_shape=[jax.ShapeDtypeStruct((rows // 2, width), jnp.bfloat16)] * 2,
-        grid=(width // tile,),
+        functools.partial(project_kernel, keep),
+        out_shape=jax.ShapeDtypeStruct((chunk, width), jnp.bfloat16),
+        grid=(out_weight.shape[0] // depth,),
         in_specs=[
             pl.BlockSpec(own.shape, whole),
             pl.BlockSpec(other.shape, whole),
-            pl.BlockSpec((depth, tile), lambda j: (0, first // tile + j)),
+            pl.BlockSpec((pl.Element(depth), pl.Element(width)), lambda j: (j * depth, first)),
         ],
-        out_specs=[pl.BlockSpec((rows // 2, tile), lambda j: (0, j))] * 2,
-        scratch_shapes=[pltpu.VMEM((rows, depth), jnp.bfloat16)],
+        out_specs=pl.BlockSpec((chunk, width), whole),
+        scratch_shapes=[
+            pltpu.VMEM((chunk, out_weight.shape[0]), jnp.bfloat16),
+            pltpu.VMEM((chunk, width), jnp.float32),
+        ],
         cost_estimate=pl.CostEstimate(
-            flops=2 * rows * depth * width, bytes_accessed=2 * depth * width, transcendentals=0
+            flops=2 * chunk * out_weight.shape[0] * width,
+            bytes_accessed=2 * out_weight.shape[0] * width,
+            transcendentals=0,
         ),
         compiler_params=pltpu.CompilerParams(vmem_limit_bytes=VMEM_LIMIT),
         name="project",
     )(own, other, out_weight)
 
 
-def prepare_kernel(chunk, k_ref, v_ref, position_ref, sent_ref, kept_ref, first_ref, sems):
+def prepare_kernel(chunk, k_ref, v_ref, position_ref, sent_ref, kept_ref, mark_ref, first_ref, sems):
     rows, width = k_ref.shape[0], k_ref.shape[1] // 2
     copies = [pltpu.make_async_copy(position_ref, first_ref, sems.at[4])]
     for n, (ref, core) in enumerate(((sent_ref, 1 - my_core()), (kept_ref, my_core()))):
@@ -259,9 +269,8 @@
         copy.start()
     copies[0].wait()
     c = lax.div(first_ref[0], jnp.int32(chunk)).astype(jnp.float32)
-    header = jnp.full((HEADER, 2 * width), c, jnp.float32).astype(jnp.bfloat16)
-    sent_ref[rows:] = header
-    kept_ref[rows:] = header
+    mark_ref[...] = jnp.full(mark_ref.shape, c, jnp.float32).astype(jnp.bfloat16)
+    sent_ref[rows:] = jnp.full((HEADER, 2 * width), c, jnp.float32).astype(jnp.bfloat16)
     for copy in copies[1:]:
         copy.wait()
 
@@ -269,19 +278,24 @@
 def prepare(keys, values, positions):
     vmem = pl.BlockSpec(memory_space=pltpu.VMEM)
     hbm = pl.BlockSpec(memory_space=pltpu.HBM)
-    rows = keys.shape[0]
+    rows, width = keys.shape
+    operands = [pltpu.with_memory_space_constraint(x, pltpu.HBM) for x in (keys, values, positions)]
     return pl.pallas_call(
         functools.partial(prepare_kernel, rows // 2),
-        out_shape=[jax.ShapeDtypeStruct((rows + HEADER, keys.shape[1]), jnp.bfloat16)] * 2,
+        out_shape=[
+            jax.ShapeDtypeStruct((rows + HEADER, width), jnp.bfloat16),
+            jax.ShapeDtypeStruct((rows, width), jnp.bfloat16),
+            jax.ShapeDtypeStruct((HEADER, width // 2), jnp.bfloat16),
+        ],
         in_specs=[hbm, hbm, hbm],
-        out_specs=[vmem, vmem],
+        out_specs=[vmem, vmem, vmem],
         scratch_shapes=[
             pltpu.SMEM(positions.shape, jnp.int32),
             pltpu.SemaphoreType.DMA((5,)),
         ],
         compiler_params=pltpu.CompilerParams(vmem_limit_bytes=VMEM_LIMIT),
         name="prepare",
-    )(keys, values, positions)
+    )(*operands)
 
 
 def after(value, *events):
@@ -295,53 +309,53 @@
     sibling = [(b, b ^ 1) for b in range(count)]
     clock, counter = ring_pairs(chips, 1), ring_pairs(chips, -1)
     width = heads * HEAD_WIDTH
-
-    sent, kept = prepare(keys, values, positions)
+    up = lambda x: lax.ppermute(x, "blk", clock)
+    down = lambda x: lax.ppermute(x, "blk", counter)
+
+    sent, x, mark = prepare(keys, values, positions)
     got = lax.ppermute(sent, "blk", sibling)
-    packet = jnp.concatenate(
-        [kept[:rows], got[:rows], jnp.concatenate([kept[rows:, :width], got[rows:, :width]], axis=1)],
-        axis=0,
+    y = jnp.concatenate(
+        [got[:rows], jnp.concatenate([mark, got[rows:, :width]], axis=1)], axis=0
     )
     q_sent = lax.dynamic_slice(
         queries, (0, (1 - my_core()) * heads * GROUP), (rows, heads * GROUP)
     )
     q_got = lax.ppermute(q_sent, "blk", sibling)
-
-    shared = dict(heads=heads, chunk=chunk, owners=2, own_at=lambda i: i)
-    shared["owner_headers"] = [(0, 2 * rows, 0), (0, 2 * rows, width)]
-
-    def call(packets, state, own):
-        each = range(len(packets))
-        members = [(j, i * rows) for j in each for i in range(2)]
-        headers = [(1 + j, 2 * rows, i * width) for j in each for i in range(2)]
-        plan = dict(shared, own=own, last=False, members=members, headers=headers)
-        return attend(plan, turned, [packet], packets, state)
-
     turned = turn(heads, chunk, (True, False), [queries, q_got])
-    ups, downs, state = [packet], [packet], None
+
+    def call(pairs, state, own, last=False):
+        each = range(len(pairs))
+        plan = dict(
+            heads=heads,
+            chunk=chunk,
+            owners=2,
+            own=own,
+            own_at=lambda i: i,
+            last=last,
+            members=[(2 * j + i, 0) for j in each for i in range(2)],
+            headers=[(2 + 2 * j, rows, i * width) for j in each for i in range(2)],
+            owner_headers=[(0, rows, 0), (0, rows, width)],
+        )
+        return attend(plan, turned, [y], [packet for pair in pairs for packet in pair], state)
+
+    state = None
+    ups = downs = (x, y)
+    arrived = [(x, y)]
     for r in range(1, half):
-        up, down = ups[-1], downs[-1]
+        (x_up, y_up), (x_down, y_down) = ups, downs
         if r == 2:
-            up, down, turned = lax.optimization_barrier((up, down, turned))
+            x_up, x_down, turned = lax.optimization_barrier((x_up, x_down, turned))
         elif r > 2:
-            up, down, *state = lax.optimization_barrier((up, down, *state))
-        ups.append(lax.ppermute(up, "blk", clock))
-        downs.append(lax.ppermute(down, "blk", counter))
+            x_up, x_down, *state = lax.optimization_barrier((x_up, x_down, *state))
+        ups, downs = (up(x_up), up(y_up)), (down(x_down), down(y_down))
         if r >= 2:
-            here = [ups[r - 1], downs[r - 1]]
-            state = call([packet] + here if r == 2 else here, state, r == 2)
-    up, down, *state = lax.optimization_barrier((ups[-1], downs[-1], *state))
-    far_up = lax.ppermute(up[:rows], "blk", clock)
-    far_down = lax.ppermute(down[rows:], "blk", counter)
-    state = call([up, down], state, False)
-    plan = dict(
-        shared,
-        own=False,
-        last=True,
-        members=[(0, 0), (1, 0)],
-        headers=[(2, rows, 0), (2, rows, width)],
-    )
-    _, _, own, theirs = attend(plan, turned, [packet], [far_up, far_down], state)
+            state = call(arrived, state, r == 2)
+            arrived = []
+        arrived += [ups, downs]
+    x_up, y_down, *state = lax.optimization_barrier((ups[0], downs[1], *state))
+    far = (up(x_up), down(y_down))
+    state = call(arrived, state, False)
+    _, _, own, theirs = call([far], state, False, True)
     return own, lax.ppermute(theirs, "blk", sibling)
 
 
@@ -381,19 +395,19 @@
         )
     own, other = split_over_cores(count, queries, keys, values, positions)
     out_weight = pltpu.with_memory_space_constraint(out_weight, pltpu.HBM)
-    width, tile = out_weight.shape[1], 512
-    shares = (2, 2, 3, 3)
-    received, kept, first, source = [], [], 0, own
+    width = out_weight.shape[1]
+    shares = (5, 5, 6, 4)
+    received, first, source = [], 0, own
     for j, share in enumerate(shares):
         columns = width * share // sum(shares)
         if j > 0:
             source = after(own, sent, *received[: j - 1][-1:])
-        sent, keep = project(source, other, out_weight, first, columns, tile)
+        sent = project(source, other, out_weight, first, columns, 512, False)
         received.append(lax.ppermute(sent, "inner", [(0, 1), (1, 0)]))
-        kept.append(keep)
         first += columns
-    mine, theirs = jnp.concatenate(kept, axis=1), jnp.concatenate(received, axis=1)
-    return (mine.astype(jnp.float32) + theirs.astype(jnp.float32)).astype(jnp.bfloat16)
+    kept = project(after(own, sent), other, out_weight, 0, width, 256, True)
+    theirs = jnp.concatenate(received, axis=1)
+    return (kept.astype(jnp.float32) + theirs.astype(jnp.float32)).astype(jnp.bfloat16)
 
 
 def solution(mesh):

time: 89.6 us -> 88.2 us (0.984)
  waiting for transfers between devices: 36.7 us -> 11.4 us
  Pallas kernels: 32.9 us -> 50.9 us
  starting transfers between devices: 14.5 us -> 22.8 us
  local copies, waits for them, and re-layouts: 3.74 us -> 1.08 us
    pallas_call x4 -> x5, Pallas kernels: 16.4 us -> 33.9 us  [project(): pl.pallas_call(functools.partial(project_kernel, keep), out_shape=jax.Sha...]
    ppermute x4, waiting for transfers between devices: 14 us -> 0.76 us  [shards(): received.append(lax.ppermute(sent, 'inner', [(0, 1), (1, 0)]))]
    ppermute x8 -> x14, waiting for transfers between devices: 20.9 us -> 8.76 us  [the longest x7 6.31 us: split_over_cores(): down = lambda x: lax.ppermute(x, 'blk', counter)]
    ppermute x8 -> x14, starting transfers between devices: 9.45 us -> 17.8 us  [the longest x7 10.9 us: split_over_cores(): down = lambda x: lax.ppermute(x, 'blk', counter)]
    unnamed x8 -> x2, local copies, waits for them, and re-layouts: 2.62 us -> 0.01 us
  transfers between devices with their start and end apart: 15 -> 21, of which waited for: 10 -> 7; matrix products, arithmetic and copies ran while one was open for 1% -> 1% of each run, Pallas kernels for 24% -> 48%
where the time goes in v4:
time: 88.2 us; the launch traced here: 87.6 us
  Pallas kernels  50.9 us (58%)
  starting transfers between devices  22.8 us (26%)
  waiting for transfers between devices  11.4 us (13%)
  other arithmetic  1.21 us (1%)
  local copies, waits for them, and re-layouts  1.08 us (1%)
    pallas_call x5, Pallas kernels, project(): pl.pallas_call(functools.partial(project_kernel, keep), out_shape=jax.Sha...  33.9 us
    pallas_call x4, Pallas kernels, attend(): pl.pallas_call(functools.partial(attend_kernel, plan), out_shape=out_shap...  15.5 us
    ppermute x7, starting transfers between devices, split_over_cores(): down = lambda x: lax.ppermute(x, 'blk', counter)  10.9 us
    ppermute x7, starting transfers between devices, split_over_cores(): up = lambda x: lax.ppermute(x, 'blk', clock)  6.91 us
    ppermute x7, waiting for transfers between devices, split_over_cores(): down = lambda x: lax.ppermute(x, 'blk', counter)  6.31 us
    ppermute x4, starting transfers between devices, shards(): received.append(lax.ppermute(sent, 'inner', [(0, 1), (1, 0)]))  4.31 us
    ppermute x7, waiting for transfers between devices, split_over_cores(): up = lambda x: lax.ppermute(x, 'blk', clock)  2.46 us
    ppermute x1, waiting for transfers between devices, split_over_cores(): return (own, lax.ppermute(theirs, 'blk', sibling))  1.85 us
  transfers between devices with their start and end apart: 21, of which 7 were waited for; matrix products, arithmetic and copies ran while one was open for 1% of the time, Pallas kernels for 48%

profile of v4, /device:TPU:0, one launch (start us, length us, event | category | flops | bytes accessed | tf_op | source)
XLA Modules:
  0.0 87.6 jit_solution(6717329572274818511)
XLA Ops:
  0.0 1.2 %prepare.1 = (bf16[208,512]{1,0:T(8,128)(2,1)S(1)}, bf16[192,512]{1,0:T(8,128)(2,1)S(1)}, bf16[16,256]{1,0:T(8,128)(2,1)S(1)}) custom-call(bf16[192,512]{1,0:T(8,128)(2,1)} %k_ref.1, bf16[192,512]{1,0:T(8,128)(2,1)} %v_ref.1, s32[192]{0:T(256)} %position_ref.1), custom_call_target="tpu_custom_call" | custom-call | tf_op jit(solution)/shard_map/prepare/pallas_call | solution.py:283
  1.2 0.5 collective-permute-start.3
  1.7 1.1 %constant_dynamic-slice_fusion = bf16[192,1280]{1,0:T(8,128)(2,1)S(1)} fusion(bf16[192,2560]{1,0:T(8,128)(2,1)} %refs_0_.1, s32[]{:T(128)S(6)} %select_n.3), kind=kLoop, calls=%fused_computation.2 | loop fusion | bytes 983044 | tf_op jit(solution)/shard_map/dynamic_slice | solution.py:320
  2.8 0.1 collective-permute-start.2
  2.9 0.0 collective-permute-done.3
  2.9 3.0 %collective-permute-start.7 = (bf16[208,512]{1,0:T(8,128)(2,1)S(1)}, bf16[208,512]{1,0:T(8,128)(2,1)S(1)}, u32[]{:S(2)}, u32[]{:S(2)}) collective-permute-start(bf16[208,512]{1,0:T(8,128)(2,1)S(1)} %maximum_maximum_fusion.refs_1_.refs_3_), channel_id=1, source_target_pairs={{0,4},{2,6},{8,0},{10,2},{16,8},{18,10},{24,16},{26,18},{28,24},{3... | collective-permute-start | bytes 638984 | tf_op jit(solution)/shard_map/ppermute | solution.py:313
  6.0 0.1 collective-permute-start
  6.1 1.9 %collective-permute-start.1 = (bf16[192,512]{1,0:T(8,128)(2,1)S(1)}, bf16[192,512]{1,0:T(8,128)(2,1)S(1)}, u32[]{:S(2)}, u32[]{:S(2)}) collective-permute-start(bf16[192,512]{1,0:T(8,128)(2,1)S(1)} %get-tuple-element.31.refs_2_), channel_id=1, source_target_pairs={{0,4},{2,6},{8,0},{10,2},{16,8},{18,10},{24,16},{26,18},{28,24},{3... | collective-permute-start | bytes 589832 | tf_op jit(solution)/shard_map/ppermute | solution.py:313
  8.0 0.1 collective-permute-start.6
  8.1 4.0 %collective-permute-done.7.refs_7_ = bf16[208,512]{1,0:T(8,128)(2,1)S(1)} collective-permute-done((bf16[208,512]{1,0:T(8,128)(2,1)S(1)}, bf16[208,512]{1,0:T(8,128)(2,1)S(1)}, u32[]{:S(2)}, u32[]{:S(2)}) %collective-permute-start.7) | collective-permute-done | bytes 213024 | tf_op jit(solution)/shard_map/ppermute | solution.py:313
  12.1 2.0 %collective-permute-start.9 = (bf16[208,512]{1,0:T(8,128)(2,1)S(1)}, bf16[208,512]{1,0:T(8,128)(2,1)S(1)}, u32[]{:S(2)}, u32[]{:S(2)}) collective-permute-start(bf16[208,512]{1,0:T(8,128)(2,1)S(1)} %collective-permute-done.7.refs_7_), channel_id=1, source_target_pairs={{0,4},{2,6},{8,0},{10,2},{16,8},{18,10},{24,16},{26,18},{28,24},{3... | collective-permute-start | bytes 638984 | tf_op jit(solution)/shard_map/ppermute | solution.py:313
  14.1 0.0 collective-permute-done.2.refs_1_
  14.1 0.3 turn.1.refs_0_
  14.4 1.9 %collective-permute-done.1.refs_6_ = bf16[192,512]{1,0:T(8,128)(2,1)S(1)} collective-permute-done((bf16[192,512]{1,0:T(8,128)(2,1)S(1)}, bf16[192,512]{1,0:T(8,128)(2,1)S(1)}, u32[]{:S(2)}, u32[]{:S(2)}) %collective-permute-start.1) | collective-permute-done | bytes 196640 | tf_op jit(solution)/shard_map/ppermute | solution.py:313
  16.3 2.1 %collective-permute-start.4 = (bf16[192,512]{1,0:T(8,128)(2,1)S(1)}, bf16[192,512]{1,0:T(8,128)(2,1)S(1)}, u32[]{:S(2)}, u32[]{:S(2)}) collective-permute-start(bf16[192,512]{1,0:T(8,128)(2,1)S(1)} %collective-permute-done.refs_4_), channel_id=1, source_target_pairs={{0,8},{2,10},{8,16},{10,18},{16,24},{18,26},{24,28},{26,30},{28,20... | collective-permute-start | bytes 589832 | tf_op jit(solution)/shard_map/ppermute | solution.py:312
  18.3 0.0 collective-permute-start.5
  18.3 0.0 collective-permute-done.6.refs_5_
  18.3 2.0 %collective-permute-start.11 = (bf16[208,512]{1,0:T(8,128)(2,1)S(1)}, bf16[208,512]{1,0:T(8,128)(2,1)S(1)}, u32[]{:S(2)}, u32[]{:S(2)}) collective-permute-start(bf16[208,512]{1,0:T(8,128)(2,1)S(1)} %collective-permute-done.6.refs_5_), channel_id=1, source_target_pairs={{0,8},{2,10},{8,16},{10,18},{16,24},{18,26},{24,28},{26,30},{28,20... | collective-permute-start | bytes 638984 | tf_op jit(solution)/shard_map/ppermute | solution.py:312
  20.4 0.5 collective-permute-done.9.refs_5_
  20.8 2.0 %collective-permute-start.10 = (bf16[208,512]{1,0:T(8,128)(2,1)S(1)}, bf16[208,512]{1,0:T(8,128)(2,1)S(1)}, u32[]{:S(2)}, u32[]{:S(2)}) collective-permute-start(bf16[208,512]{1,0:T(8,128)(2,1)S(1)} %collective-permute-done.9.refs_5_), channel_id=1, source_target_pairs={{0,4},{2,6},{8,0},{10,2},{16,8},{18,10},{24,16},{26,18},{28,24},{3... | collective-permute-start | bytes 638984 | tf_op jit(solution)/shard_map/ppermute | solution.py:313
  22.8 4.4 %attend.4 = (f32[8,1,480]{2,1,0:T(1,128)S(1)}, f32[8,144,480]{2,1,0:T(8,128)S(1)}) custom-call(bf16[8,128,480]{2,1,0:T(8,128)(2,1)S(1)} %turn.1.refs_0_, bf16[208,512]{1,0:T(8,128)(2,1)S(1)} %maximum_maximum_fusion.refs_1_.refs_3_, bf16[192,512]{1,0:T(8,128)(2,1)S(1)} %get-tuple-element.31.refs_2_, bf16[208,512]{1,0:T(8,128)(2,1)S(1)} %maximum_maximum_fusion.refs_1_.refs_3_, ...), custom_call_target="tpu_custom_call" | custom-call | flops 1132462080 | bytes 4194304 | tf_op jit(solution)/shard_map/attend/pallas_call | solution.py:164
  27.3 0.0 collective-permute-done.4.refs_2_
  27.3 0.5 collective-permute-start.8
  27.8 0.0 collective-permute-done.11.refs_3_
  27.8 1.7 %collective-permute-start.14 = (bf16[208,512]{1,0:T(8,128)(2,1)S(1)}, bf16[208,512]{1,0:T(8,128)(2,1)S(1)}, u32[]{:S(2)}, u32[]{:S(2)}) collective-permute-start(bf16[208,512]{1,0:T(8,128)(2,1)S(1)} %collective-permute-done.11.refs_3_), channel_id=1, source_target_pairs={{0,8},{2,10},{8,16},{10,18},{16,24},{18,26},{24,28},{26,30},{28,20... | collective-permute-start | bytes 638984 | tf_op jit(solution)/shard_map/ppermute | solution.py:312
  29.4 0.3 collective-permute-start.15
  29.8 4.1 %attend.5 = (f32[8,1,480]{2,1,0:T(1,128)S(1)}, f32[8,144,480]{2,1,0:T(8,128)S(1)}) custom-call(bf16[8,128,480]{2,1,0:T(8,128)(2,1)S(1)} %turn.1.refs_0_, bf16[208,512]{1,0:T(8,128)(2,1)S(1)} %maximum_maximum_fusion.refs_1_.refs_3_, bf16[192,512]{1,0:T(8,128)(2,1)S(1)} %collective-permute-done.4.refs_2_, ...), custom_call_target="tpu_custom_call", output_to_operand_aliasing={{0}: (6, {}), {1}: (7, {})} | custom-call | flops 754974720 | bytes 4194304 | tf_op jit(solution)/shard_map/attend/pallas_call | solution.py:164
  33.8 0.0 collective-permute-done.10.refs_5_
  33.9 0.5 collective-permute-done.8.refs_2_
  34.4 1.6 %collective-permute-start.13 = (bf16[208,512]{1,0:T(8,128)(2,1)S(1)}, bf16[208,512]{1,0:T(8,128)(2,1)S(1)}, u32[]{:S(2)}, u32[]{:S(2)}) collective-permute-start(bf16[208,512]{1,0:T(8,128)(2,1)S(1)} %collective-permute-done.10.refs_5_), channel_id=1, source_target_pairs={{0,4},{2,6},{8,0},{10,2},{16,8},{18,10},{24,16},{26,18},{28,24},{3... | collective-permute-start | bytes 638984 | tf_op jit(solution)/shard_map/ppermute | solution.py:313
  36.0 0.4 collective-permute-start.12
  36.4 1.9 %collective-permute-done.14.refs_3_ = bf16[208,512]{1,0:T(8,128)(2,1)S(1)} collective-permute-done((bf16[208,512]{1,0:T(8,128)(2,1)S(1)}, bf16[208,512]{1,0:T(8,128)(2,1)S(1)}, u32[]{:S(2)}, u32[]{:S(2)}) %collective-permute-start.14) | collective-permute-done | bytes 213024 | tf_op jit(solution)/shard_map/ppermute | solution.py:312
  38.3 4.0 %attend.6 = (f32[8,1,480]{2,1,0:T(1,128)S(1)}, f32[8,144,480]{2,1,0:T(8,128)S(1)}) custom-call(bf16[8,128,480]{2,1,0:T(8,128)(2,1)S(1)} %turn.1.refs_0_, bf16[208,512]{1,0:T(8,128)(2,1)S(1)} %maximum_maximum_fusion.refs_1_.refs_3_, bf16[192,512]{1,0:T(8,128)(2,1)S(1)} %collective-permute-done.8.refs_2_, ...), custom_call_target="tpu_custom_call", output_to_operand_aliasing={{0}: (6, {}), {1}: (7, {})} | custom-call | flops 754974720 | bytes 4194304 | tf_op jit(solution)/shard_map/attend/pallas_call | solution.py:164
  42.4 0.0 collective-permute-done.12.refs_2_
  42.4 3.0 %attend.7 = (f32[8,1,480]{2,1,0:T(1,128)S(1)}, f32[8,144,480]{2,1,0:T(8,128)S(1)}, bf16[192,1280]{1,0:T(8,128)(2,1)S(1)}, bf16[192,1280]{1,0:T(8,128)(2,1)S(1)}) custom-call(bf16[8,128,480]{2,1,0:T(8,128)(2,1)S(1)} %turn.1.refs_0_, bf16[208,512]{1,0:T(8,128)(2,1)S(1)} %maximum_maximum_fusion.refs_1_.refs_3_, ...), custom_call_target="tpu_custom_call", output_to_operand_aliasing={{0}: (4, {}), {1}: (5, {})} | custom-call | flops 377487360 | bytes 4194304 | tf_op jit(solution)/shard_map/attend/pallas_call | solution.py:164
  45.4 0.1 collective-permute-start.16
  45.5 1.9 %collective-permute-done.16.other_ref = bf16[192,1280]{1,0:T(8,128)(2,1)S(1)} collective-permute-done((bf16[192,1280]{1,0:T(8,128)(2,1)S(1)}, bf16[192,1280]{1,0:T(8,128)(2,1)S(1)}, u32[]{:S(2)}, u32[]{:S(2)}) %collective-permute-start.16) | collective-permute-done | bytes 491552 | tf_op jit(solution)/shard_map/ppermute | solution.py:359
  47.3 5.1 %project.5 = bf16[96,1280]{1,0:T(8,128)(2,1)S(1)} custom-call(bf16[192,1280]{1,0:T(8,128)(2,1)S(1)} %get-tuple-element.56.own_ref, bf16[192,1280]{1,0:T(8,128)(2,1)S(1)} %collective-permute-done.16.other_ref, bf16[2560,5120]{1,0:T(8,128)(2,1)} %w_ref.9), custom_call_target="tpu_custom_call" | custom-call | flops 629145600 | bytes 6553600 | tf_op jit(solution)/shard_map/project/pallas_call | solution.py:236
  52.5 1.6 %collective-permute-start.17 = (bf16[96,1280]{1,0:T(8,128)(2,1)S(1)}, bf16[96,1280]{1,0:T(8,128)(2,1)S(1)}, u32[]{:S(2)}, u32[]{:S(2)}) collective-permute-start(bf16[96,1280]{1,0:T(8,128)(2,1)S(1)} %project.5), channel_id=1, source_target_pairs={{0,1},{1,0},{2,3},{3,2},{4,5},{5,4},{6,7},{7,6},{8,9},{9,8},{10,11... | collective-permute-start | bytes 737288 | tf_op jit(solution)/shard_map/ppermute | solution.py:406
  54.0 5.1 %project.6 = bf16[96,1280]{1,0:T(8,128)(2,1)S(1)} custom-call(bf16[192,1280]{1,0:T(8,128)(2,1)S(1)} %get-tuple-element.56.own_ref, bf16[192,1280]{1,0:T(8,128)(2,1)S(1)} %collective-permute-done.16.other_ref, bf16[2560,5120]{1,0:T(8,128)(2,1)} %w_ref.9), custom_call_target="tpu_custom_call" | custom-call | flops 629145600 | bytes 6553600 | tf_op jit(solution)/shard_map/project/pallas_call | solution.py:236
  59.2 0.6 collective-permute-start.18
  59.8 0.7 collective-permute-done.17
  60.5 5.6 %project.7 = bf16[96,1536]{1,0:T(8,128)(2,1)S(1)} custom-call(bf16[192,1280]{1,0:T(8,128)(2,1)S(1)} %get-tuple-element.56.own_ref, bf16[192,1280]{1,0:T(8,128)(2,1)S(1)} %collective-permute-done.16.other_ref, bf16[2560,5120]{1,0:T(8,128)(2,1)} %w_ref.9), custom_call_target="tpu_custom_call" | custom-call | flops 754974720 | bytes 7864320 | tf_op jit(solution)/shard_map/project/pallas_call | solution.py:236
  66.1 1.6 %collective-permute-start.19 = (bf16[96,1536]{1,0:T(8,128)(2,1)S(1)}, bf16[96,1536]{1,0:T(8,128)(2,1)S(1)}, u32[]{:S(2)}, u32[]{:S(2)}) collective-permute-start(bf16[96,1536]{1,0:T(8,128)(2,1)S(1)} %project.7), channel_id=1, source_target_pairs={{0,1},{1,0},{2,3},{3,2},{4,5},{5,4},{6,7},{7,6},{8,9},{9,8},{10,11... | collective-permute-start | bytes 884744 | tf_op jit(solution)/shard_map/ppermute | solution.py:406
  67.7 4.7 %project.8 = bf16[96,1024]{1,0:T(8,128)(2,1)S(1)} custom-call(bf16[192,1280]{1,0:T(8,128)(2,1)S(1)} %get-tuple-element.56.own_ref, bf16[192,1280]{1,0:T(8,128)(2,1)S(1)} %collective-permute-done.16.other_ref, bf16[2560,5120]{1,0:T(8,128)(2,1)} %w_ref.9), custom_call_target="tpu_custom_call" | custom-call | flops 503316480 | bytes 5242880 | tf_op jit(solution)/shard_map/project/pallas_call | solution.py:236
  72.4 0.6 collective-permute-start.20
  73.0 13.4 %project.9 = bf16[96,5120]{1,0:T(8,128)(2,1)S(1)} custom-call(bf16[192,1280]{1,0:T(8,128)(2,1)S(1)} %get-tuple-element.56.own_ref, bf16[192,1280]{1,0:T(8,128)(2,1)S(1)} %collective-permute-done.16.other_ref, bf16[2560,5120]{1,0:T(8,128)(2,1)} %w_ref.9), custom_call_target="tpu_custom_call" | custom-call | flops 2516582400 | bytes 26214400 | tf_op jit(solution)/shard_map/project/pallas_call | solution.py:236
  86.4 1.2 %add_convert_fusion = bf16[96,5120]{1,0:T(8,128)(2,1)} fusion(bf16[96,5120]{1,0:T(8,128)(2,1)S(1)} %project.9, bf16[96,1024]{1,0:T(8,128)(2,1)S(1)} %collective-permute-done.20, bf16[96,1536]{1,0:T(8,128)(2,1)S(1)} %collective-permute-done.19, bf16[96,1280]{1,0:T(8,128)(2,1)S(1)} %collective-permute-done.18, bf16[96,1280]{1,0:T(8,128)(2,1)S(1)} %collective-permute-done.17), kind=kLoop, calls=%fused_computation | loop fusion | flops 5406720 | bytes 2949120 | tf_op jit(solution)/shard_map/convert_element_type | solution.py:410
  (12 shorter events, 0.1 us)
Async XLA Ops:
  0.0 14.1 %copy-start = (bf16[192,2560]{1,0:T(8,128)(2,1)S(1)}, bf16[192,2560]{1,0:T(8,128)(2,1)}, u32[]{:S(2)}) copy-start(bf16[192,2560]{1,0:T(8,128)(2,1)} %refs_0_.1) | copy-start | bytes 2949124
  1.2 1.7 %collective-permute-start.3 = (bf16[208,512]{1,0:T(8,128)(2,1)S(1)}, bf16[208,512]{1,0:T(8,128)(2,1)S(1)}, u32[]{:S(2)}, u32[]{:S(2)}) collective-permute-start(bf16[208,512]{1,0:T(8,128)(2,1)S(1)} %get-tuple-element.33), channel_id=1, source_target_pairs={{0,2},{2,0},{4,6},{6,4},{8,10},{10,8},{12,14},{14,12},{16,18},{18,... | collective-permute-start | bytes 638984 | tf_op jit(solution)/shard_map/ppermute | solution.py:316
  2.8 11.3 %collective-permute-start.2 = (bf16[192,1280]{1,0:T(8,128)(2,1)S(1)}, bf16[192,1280]{1,0:T(8,128)(2,1)S(1)}, u32[]{:S(2)}, u32[]{:S(2)}) collective-permute-start(bf16[192,1280]{1,0:T(8,128)(2,1)S(1)} %constant_dynamic-slice_fusion), channel_id=1, source_target_pairs={{0,2},{2,0},{4,6},{6,4},{8,10},{10,8},{12,14},{14,12},{16,18},{18,... | collective-permute-start | bytes 1474568 | tf_op jit(solution)/shard_map/ppermute | solution.py:323
  2.9 9.1 %collective-permute-start.7 = (bf16[208,512]{1,0:T(8,128)(2,1)S(1)}, bf16[208,512]{1,0:T(8,128)(2,1)S(1)}, u32[]{:S(2)}, u32[]{:S(2)}) collective-permute-start(bf16[208,512]{1,0:T(8,128)(2,1)S(1)} %maximum_maximum_fusion.refs_1_.refs_3_), channel_id=1, source_target_pairs={{0,4},{2,6},{8,0},{10,2},{16,8},{18,10},{24,16},{26,18},{28,24},{3... | collective-permute-start | bytes 638984 | tf_op jit(solution)/shard_map/ppermute | solution.py:313
  6.0 8.5 %collective-permute-start = (bf16[192,512]{1,0:T(8,128)(2,1)S(1)}, bf16[192,512]{1,0:T(8,128)(2,1)S(1)}, u32[]{:S(2)}, u32[]{:S(2)}) collective-permute-start(bf16[192,512]{1,0:T(8,128)(2,1)S(1)} %get-tuple-element.31.refs_2_), channel_id=1, source_target_pairs={{0,8},{2,10},{8,16},{10,18},{16,24},{18,26},{24,28},{26,30},{28,20... | collective-permute-start | bytes 589832 | tf_op jit(solution)/shard_map/ppermute | solution.py:312
  6.1 10.2 %collective-permute-start.1 = (bf16[192,512]{1,0:T(8,128)(2,1)S(1)}, bf16[192,512]{1,0:T(8,128)(2,1)S(1)}, u32[]{:S(2)}, u32[]{:S(2)}) collective-permute-start(bf16[192,512]{1,0:T(8,128)(2,1)S(1)} %get-tuple-element.31.refs_2_), channel_id=1, source_target_pairs={{0,4},{2,6},{8,0},{10,2},{16,8},{18,10},{24,16},{26,18},{28,24},{3... | collective-permute-start | bytes 589832 | tf_op jit(solution)/shard_map/ppermute | solution.py:313
  8.0 10.4 %collective-permute-start.6 = (bf16[208,512]{1,0:T(8,128)(2,1)S(1)}, bf16[208,512]{1,0:T(8,128)(2,1)S(1)}, u32[]{:S(2)}, u32[]{:S(2)}) collective-permute-start(bf16[208,512]{1,0:T(8,128)(2,1)S(1)} %maximum_maximum_fusion.refs_1_.refs_3_), channel_id=1, source_target_pairs={{0,8},{2,10},{8,16},{10,18},{16,24},{18,26},{24,28},{26,30},{28,20... | collective-permute-start | bytes 638984 | tf_op jit(solution)/shard_map/ppermute | solution.py:312
  12.1 8.8 %collective-permute-start.9 = (bf16[208,512]{1,0:T(8,128)(2,1)S(1)}, bf16[208,512]{1,0:T(8,128)(2,1)S(1)}, u32[]{:S(2)}, u32[]{:S(2)}) collective-permute-start(bf16[208,512]{1,0:T(8,128)(2,1)S(1)} %collective-permute-done.7.refs_7_), channel_id=1, source_target_pairs={{0,4},{2,6},{8,0},{10,2},{16,8},{18,10},{24,16},{26,18},{28,24},{3... | collective-permute-start | bytes 638984 | tf_op jit(solution)/shard_map/ppermute | solution.py:313
  16.3 11.0 %collective-permute-start.4 = (bf16[192,512]{1,0:T(8,128)(2,1)S(1)}, bf16[192,512]{1,0:T(8,128)(2,1)S(1)}, u32[]{:S(2)}, u32[]{:S(2)}) collective-permute-start(bf16[192,512]{1,0:T(8,128)(2,1)S(1)} %collective-permute-done.refs_4_), channel_id=1, source_target_pairs={{0,8},{2,10},{8,16},{10,18},{16,24},{18,26},{24,28},{26,30},{28,20... | collective-permute-start | bytes 589832 | tf_op jit(solution)/shard_map/ppermute | solution.py:312
  18.3 8.9 %collective-permute-start.5 = (bf16[192,512]{1,0:T(8,128)(2,1)S(1)}, bf16[192,512]{1,0:T(8,128)(2,1)S(1)}, u32[]{:S(2)}, u32[]{:S(2)}) collective-permute-start(bf16[192,512]{1,0:T(8,128)(2,1)S(1)} %collective-permute-done.1.refs_6_), channel_id=1, source_target_pairs={{0,4},{2,6},{8,0},{10,2},{16,8},{18,10},{24,16},{26,18},{28,24},{3... | collective-permute-start | bytes 589832 | tf_op jit(solution)/shard_map/ppermute | solution.py:313
  18.3 9.4 %collective-permute-start.11 = (bf16[208,512]{1,0:T(8,128)(2,1)S(1)}, bf16[208,512]{1,0:T(8,128)(2,1)S(1)}, u32[]{:S(2)}, u32[]{:S(2)}) collective-permute-start(bf16[208,512]{1,0:T(8,128)(2,1)S(1)} %collective-permute-done.6.refs_5_), channel_id=1, source_target_pairs={{0,8},{2,10},{8,16},{10,18},{16,24},{18,26},{24,28},{26,30},{28,20... | collective-permute-start | bytes 638984 | tf_op jit(solution)/shard_map/ppermute | solution.py:312
  20.8 13.0 %collective-permute-start.10 = (bf16[208,512]{1,0:T(8,128)(2,1)S(1)}, bf16[208,512]{1,0:T(8,128)(2,1)S(1)}, u32[]{:S(2)}, u32[]{:S(2)}) collective-permute-start(bf16[208,512]{1,0:T(8,128)(2,1)S(1)} %collective-permute-done.9.refs_5_), channel_id=1, source_target_pairs={{0,4},{2,6},{8,0},{10,2},{16,8},{18,10},{24,16},{26,18},{28,24},{3... | collective-permute-start | bytes 638984 | tf_op jit(solution)/shard_map/ppermute | solution.py:313
  27.3 7.1 %collective-permute-start.8 = (bf16[192,512]{1,0:T(8,128)(2,1)S(1)}, bf16[192,512]{1,0:T(8,128)(2,1)S(1)}, u32[]{:S(2)}, u32[]{:S(2)}) collective-permute-start(bf16[192,512]{1,0:T(8,128)(2,1)S(1)} %collective-permute-done.4.refs_2_), channel_id=1, source_target_pairs={{0,8},{2,10},{8,16},{10,18},{16,24},{18,26},{24,28},{26,30},{28,20... | collective-permute-start | bytes 589832 | tf_op jit(solution)/shard_map/ppermute | solution.py:312
  27.8 10.6 %collective-permute-start.14 = (bf16[208,512]{1,0:T(8,128)(2,1)S(1)}, bf16[208,512]{1,0:T(8,128)(2,1)S(1)}, u32[]{:S(2)}, u32[]{:S(2)}) collective-permute-start(bf16[208,512]{1,0:T(8,128)(2,1)S(1)} %collective-permute-done.11.refs_3_), channel_id=1, source_target_pairs={{0,8},{2,10},{8,16},{10,18},{16,24},{18,26},{24,28},{26,30},{28,20... | collective-permute-start | bytes 638984 | tf_op jit(solution)/shard_map/ppermute | solution.py:312
  29.4 8.9 %collective-permute-start.15 = (bf16[192,512]{1,0:T(8,128)(2,1)S(1)}, bf16[192,512]{1,0:T(8,128)(2,1)S(1)}, u32[]{:S(2)}, u32[]{:S(2)}) collective-permute-start(bf16[192,512]{1,0:T(8,128)(2,1)S(1)} %collective-permute-done.5.refs_4_), channel_id=1, source_target_pairs={{0,4},{2,6},{8,0},{10,2},{16,8},{18,10},{24,16},{26,18},{28,24},{3... | collective-permute-start | bytes 589832 | tf_op jit(solution)/shard_map/ppermute | solution.py:313
  34.4 8.0 %collective-permute-start.13 = (bf16[208,512]{1,0:T(8,128)(2,1)S(1)}, bf16[208,512]{1,0:T(8,128)(2,1)S(1)}, u32[]{:S(2)}, u32[]{:S(2)}) collective-permute-start(bf16[208,512]{1,0:T(8,128)(2,1)S(1)} %collective-permute-done.10.refs_5_), channel_id=1, source_target_pairs={{0,4},{2,6},{8,0},{10,2},{16,8},{18,10},{24,16},{26,18},{28,24},{3... | collective-permute-start | bytes 638984 | tf_op jit(solution)/shard_map/ppermute | solution.py:313
  36.0 6.4 %collective-permute-start.12 = (bf16[192,512]{1,0:T(8,128)(2,1)S(1)}, bf16[192,512]{1,0:T(8,128)(2,1)S(1)}, u32[]{:S(2)}, u32[]{:S(2)}) collective-permute-start(bf16[192,512]{1,0:T(8,128)(2,1)S(1)} %collective-permute-done.8.refs_2_), channel_id=1, source_target_pairs={{0,8},{2,10},{8,16},{10,18},{16,24},{18,26},{24,28},{26,30},{28,20... | collective-permute-start | bytes 589832 | tf_op jit(solution)/shard_map/ppermute | solution.py:312
  45.4 1.9 %collective-permute-start.16 = (bf16[192,1280]{1,0:T(8,128)(2,1)S(1)}, bf16[192,1280]{1,0:T(8,128)(2,1)S(1)}, u32[]{:S(2)}, u32[]{:S(2)}) collective-permute-start(bf16[192,1280]{1,0:T(8,128)(2,1)S(1)} %get-tuple-element.52), channel_id=1, source_target_pairs={{0,2},{2,0},{4,6},{6,4},{8,10},{10,8},{12,14},{14,12},{16,18},{18,... | collective-permute-start | bytes 1474568 | tf_op jit(solution)/shard_map/ppermute | solution.py:359
  52.5 8.1 %collective-permute-start.17 = (bf16[96,1280]{1,0:T(8,128)(2,1)S(1)}, bf16[96,1280]{1,0:T(8,128)(2,1)S(1)}, u32[]{:S(2)}, u32[]{:S(2)}) collective-permute-start(bf16[96,1280]{1,0:T(8,128)(2,1)S(1)} %project.5), channel_id=1, source_target_pairs={{0,1},{1,0},{2,3},{3,2},{4,5},{5,4},{6,7},{7,6},{8,9},{9,8},{10,11... | collective-permute-start | bytes 737288 | tf_op jit(solution)/shard_map/ppermute | solution.py:406
  59.2 8.5 %collective-permute-start.18 = (bf16[96,1280]{1,0:T(8,128)(2,1)S(1)}, bf16[96,1280]{1,0:T(8,128)(2,1)S(1)}, u32[]{:S(2)}, u32[]{:S(2)}) collective-permute-start(bf16[96,1280]{1,0:T(8,128)(2,1)S(1)} %project.6), channel_id=1, source_target_pairs={{0,1},{1,0},{2,3},{3,2},{4,5},{5,4},{6,7},{7,6},{8,9},{9,8},{10,11... | collective-permute-start | bytes 737288 | tf_op jit(solution)/shard_map/ppermute | solution.py:406
  66.1 20.3 %collective-permute-start.19 = (bf16[96,1536]{1,0:T(8,128)(2,1)S(1)}, bf16[96,1536]{1,0:T(8,128)(2,1)S(1)}, u32[]{:S(2)}, u32[]{:S(2)}) collective-permute-start(bf16[96,1536]{1,0:T(8,128)(2,1)S(1)} %project.7), channel_id=1, source_target_pairs={{0,1},{1,0},{2,3},{3,2},{4,5},{5,4},{6,7},{7,6},{8,9},{9,8},{10,11... | collective-permute-start | bytes 884744 | tf_op jit(solution)/shard_map/ppermute | solution.py:406
  72.4 14.0 %collective-permute-start.20 = (bf16[96,1024]{1,0:T(8,128)(2,1)S(1)}, bf16[96,1024]{1,0:T(8,128)(2,1)S(1)}, u32[]{:S(2)}, u32[]{:S(2)}) collective-permute-start(bf16[96,1024]{1,0:T(8,128)(2,1)S(1)} %project.8), channel_id=1, source_target_pairs={{0,1},{1,0},{2,3},{3,2},{4,5},{5,4},{6,7},{7,6},{8,9},{9,8},{10,11... | collective-permute-start | bytes 589832 | tf_op jit(solution)/shard_map/ppermute | solution.py:406

commit v5 on v4

--- a/solution.py
+++ b/solution.py
@@ -137,8 +137,8 @@
                     high_ref[at] = highs[side]
                     sums_ref[at] = sums
                     if plan["last"] and first + 6 >= count:
-                        mixed = sums[:HEAD_WIDTH] / sums[HEAD_WIDTH : HEAD_WIDTH + 1]
-                        mixed = jnp.transpose(mixed).astype(out_refs[i].dtype)
+                        mixed = sums[:HEAD_WIDTH] * (1.0 / sums[HEAD_WIDTH : HEAD_WIDTH + 1])
+                        mixed = jnp.transpose(mixed.astype(out_refs[i].dtype))
                         for g in range(QUERY_PER_KEY):
                             out_refs[i][
                                 side * chunk : (side + 1) * chunk,
@@ -206,51 +206,52 @@
     )(*queries)
 
 
-def project_kernel(keep, own_ref, other_ref, w_ref, out_ref, rows_ref, total_ref):
-    step = pl.program_id(0)
-    chunk, part = rows_ref.shape[0], own_ref.shape[1]
-    depth = w_ref.shape[0]
-
-    @pl.when(step == 0)
-    def _():
-        mine = lax.axis_index("inner").astype(jnp.int32)
-        half = mine if keep else 1 - mine
+def project_kernel(first, own_ref, other_ref, w_ref, sent_ref, kept_ref, rows_ref, held_ref, sems):
+    chunk, width = sent_ref.shape
+    pieces = sems.shape[0]
+    depth = held_ref.shape[0] // pieces
+    copies = []
+    for p in range(pieces):
+        at = pl.ds(p * depth, depth)
+        copies.append(
+            pltpu.make_async_copy(w_ref.at[at, pl.ds(first, width)], held_ref.at[at], sems.at[p])
+        )
+        copies[-1].start()
+    part = own_ref.shape[1]
+    mine = lax.axis_index("inner").astype(jnp.int32)
+    left = my_core() == 0
+    for place, half in enumerate((1 - mine, mine)):
         at = pl.ds(pl.multiple_of(half * chunk, chunk), chunk)
         own, other = own_ref[at], other_ref[at]
-        left = my_core() == 0
-        rows_ref[:, :part] = jnp.where(left, own, other)
-        rows_ref[:, part:] = jnp.where(left, other, own)
-        total_ref[...] = jnp.zeros_like(total_ref)
-
-    at = pl.multiple_of(step * depth, depth)
-    total_ref[...] += product(rows_ref[:, pl.ds(at, depth)], w_ref[...])
-
-    @pl.when(step == pl.num_programs(0) - 1)
-    def _():
-        out_ref[...] = total_ref[...].astype(out_ref.dtype)
-
-
-def project(own, other, out_weight, first, width, depth, keep):
-    chunk = own.shape[0] // 2
-    whole = lambda j: (0, 0)
+        to = slice(place * chunk, (place + 1) * chunk)
+        rows_ref[to, :part] = jnp.where(left, own, other)
+        rows_ref[to, part:] = jnp.where(left, other, own)
+    total = None
+    for p in range(pieces):
+        copies[p].wait()
+        at = slice(p * depth, (p + 1) * depth)
+        term = product(rows_ref[:, at], held_ref[at])
+        total = term if total is None else total + term
+    total = total.astype(sent_ref.dtype)
+    sent_ref[...] = total[:chunk]
+    kept_ref[...] = total[chunk:]
+
+
+def project(own, other, out_weight, first, width, pieces):
+    rows, depth = own.shape[0], out_weight.shape[0]
+    vmem = pl.BlockSpec(memory_space=pltpu.VMEM)
     return pl.pallas_call(
-        functools.partial(project_kernel, keep),
-        out_shape=jax.ShapeDtypeStruct((chunk, width), jnp.bfloat16),
-        grid=(out_weight.shape[0] // depth,),
-        in_specs=[
-            pl.BlockSpec(own.shape, whole),
-            pl.BlockSpec(other.shape, whole),
-            pl.BlockSpec((pl.Element(depth), pl.Element(width)), lambda j: (j * depth, first)),
-        ],
-        out_specs=pl.BlockSpec((chunk, width), whole),
+        functools.partial(project_kernel, first),
+        out_shape=[jax.ShapeDtypeStruct((rows // 2, width), jnp.bfloat16)] * 2,
+        in_specs=[vmem, vmem, pl.BlockSpec(memory_space=pltpu.HBM)],
+        out_specs=[vmem, vmem],
         scratch_shapes=[
-            pltpu.VMEM((chunk, out_weight.shape[0]), jnp.bfloat16),
-            pltpu.VMEM((chunk, width), jnp.float32),
+            pltpu.VMEM((rows, depth), jnp.bfloat16),
+            pltpu.VMEM((depth, width), jnp.bfloat16),
+            pltpu.SemaphoreType.DMA((pieces,)),
         ],
         cost_estimate=pl.CostEstimate(
-            flops=2 * chunk * out_weight.shape[0] * width,
-            bytes_accessed=2 * out_weight.shape[0] * width,
-            transcendentals=0,
+            flops=2 * rows * depth * width, bytes_accessed=2 * depth * width, transcendentals=0
         ),
         compiler_params=pltpu.CompilerParams(vmem_limit_bytes=VMEM_LIMIT),
         name="project",
@@ -396,18 +397,18 @@
     own, other = split_over_cores(count, queries, keys, values, positions)
     out_weight = pltpu.with_memory_space_constraint(out_weight, pltpu.HBM)
     width = out_weight.shape[1]
-    shares = (5, 5, 6, 4)
-    received, first, source = [], 0, own
+    shares = (4, 4, 7, 5)
+    received, kept, first, source = [], [], 0, own
     for j, share in enumerate(shares):
         columns = width * share // sum(shares)
         if j > 0:
             source = after(own, sent, *received[: j - 1][-1:])
-        sent = project(source, other, out_weight, first, columns, 512, False)
+        sent, keep = project(source, other, out_weight, first, columns, 5)
         received.append(lax.ppermute(sent, "inner", [(0, 1), (1, 0)]))
+        kept.append(keep)
         first += columns
-    kept = project(after(own, sent), other, out_weight, 0, width, 256, True)
-    theirs = jnp.concatenate(received, axis=1)
-    return (kept.astype(jnp.float32) + theirs.astype(jnp.float32)).astype(jnp.bfloat16)
+    mine, theirs = jnp.concatenate(kept, axis=1), jnp.concatenate(received, axis=1)
+    return (mine.astype(jnp.float32) + theirs.astype(jnp.float32)).astype(jnp.bfloat16)
 
 
 def solution(mesh):

time: 88.2 us -> 77.7 us (0.88)
  Pallas kernels: 50.9 us -> 31 us
  waiting for transfers between devices: 11.4 us -> 21 us
    pallas_call x5 -> x4, Pallas kernels: 33.9 us -> 14.1 us  [project(): pl.pallas_call(functools.partial(project_kernel, first), out_shape=[jax.S...]
    ppermute x4, waiting for transfers between devices: 0.76 us -> 10.4 us  [shards(): received.append(lax.ppermute(sent, 'inner', [(0, 1), (1, 0)]))]
  transfers between devices with their start and end apart: 21 -> 21, of which waited for: 7 -> 8; matrix products, arithmetic and copies ran while one was open for 1% -> 1% of each run, Pallas kernels for 48% -> 31%
where the time goes in v5:
time: 77.7 us; the launch traced here: 77.5 us
  Pallas kernels  31 us (40%)
  starting transfers between devices  23.1 us (30%)
  waiting for transfers between devices  21 us (27%)
  other arithmetic  1.21 us (2%)
  local copies, waits for them, and re-layouts  1.08 us (1%)
    pallas_call x4, Pallas kernels, attend(): pl.pallas_call(functools.partial(attend_kernel, plan), out_shape=out_shap...  15.4 us
    pallas_call x4, Pallas kernels, project(): pl.pallas_call(functools.partial(project_kernel, first), out_shape=[jax.S...  14.1 us
    ppermute x7, starting transfers between devices, split_over_cores(): down = lambda x: lax.ppermute(x, 'blk', counter)  10.9 us
    ppermute x4, waiting for transfers between devices, shards(): received.append(lax.ppermute(sent, 'inner', [(0, 1), (1, 0)]))  10.4 us
    ppermute x7, starting transfers between devices, split_over_cores(): up = lambda x: lax.ppermute(x, 'blk', clock)  6.91 us
    ppermute x7, waiting for transfers between devices, split_over_cores(): down = lambda x: lax.ppermute(x, 'blk', counter)  6.31 us
    ppermute x4, starting transfers between devices, shards(): received.append(lax.ppermute(sent, 'inner', [(0, 1), (1, 0)]))  4.6 us
    ppermute x7, waiting for transfers between devices, split_over_cores(): up = lambda x: lax.ppermute(x, 'blk', clock)  2.46 us
  transfers between devices with their start and end apart: 21, of which 8 were waited for; matrix products, arithmetic and copies ran while one was open for 1% of the time, Pallas kernels for 31%

profile of v5, /device:TPU:0, one launch (start us, length us, event | category | flops | bytes accessed | tf_op | source)
XLA Modules:
  0.0 77.5 jit_solution(12374027679391628486)
XLA Ops:
  0.0 1.2 %prepare.1 = (bf16[208,512]{1,0:T(8,128)(2,1)S(1)}, bf16[192,512]{1,0:T(8,128)(2,1)S(1)}, bf16[16,256]{1,0:T(8,128)(2,1)S(1)}) custom-call(bf16[192,512]{1,0:T(8,128)(2,1)} %k_ref.1, bf16[192,512]{1,0:T(8,128)(2,1)} %v_ref.1, s32[192]{0:T(256)} %position_ref.1), custom_call_target="tpu_custom_call" | custom-call | tf_op jit(solution)/shard_map/prepare/pallas_call | solution.py:284
  1.2 0.5 collective-permute-start.3
  1.7 1.1 %constant_dynamic-slice_fusion = bf16[192,1280]{1,0:T(8,128)(2,1)S(1)} fusion(bf16[192,2560]{1,0:T(8,128)(2,1)} %refs_0_.1, s32[]{:T(128)S(6)} %select_n.3), kind=kLoop, calls=%fused_computation.2 | loop fusion | bytes 983044 | tf_op jit(solution)/shard_map/dynamic_slice | solution.py:321
  2.8 0.1 collective-permute-start.2
  2.9 0.0 collective-permute-done.3
  2.9 3.0 %collective-permute-start.7 = (bf16[208,512]{1,0:T(8,128)(2,1)S(1)}, bf16[208,512]{1,0:T(8,128)(2,1)S(1)}, u32[]{:S(2)}, u32[]{:S(2)}) collective-permute-start(bf16[208,512]{1,0:T(8,128)(2,1)S(1)} %maximum_maximum_fusion.refs_1_.refs_3_), channel_id=1, source_target_pairs={{0,4},{2,6},{8,0},{10,2},{16,8},{18,10},{24,16},{26,18},{28,24},{3... | collective-permute-start | bytes 638984 | tf_op jit(solution)/shard_map/ppermute | solution.py:314
  6.0 0.1 collective-permute-start
  6.1 1.9 %collective-permute-start.1 = (bf16[192,512]{1,0:T(8,128)(2,1)S(1)}, bf16[192,512]{1,0:T(8,128)(2,1)S(1)}, u32[]{:S(2)}, u32[]{:S(2)}) collective-permute-start(bf16[192,512]{1,0:T(8,128)(2,1)S(1)} %get-tuple-element.38.refs_2_), channel_id=1, source_target_pairs={{0,4},{2,6},{8,0},{10,2},{16,8},{18,10},{24,16},{26,18},{28,24},{3... | collective-permute-start | bytes 589832 | tf_op jit(solution)/shard_map/ppermute | solution.py:314
  8.0 0.1 collective-permute-start.6
  8.1 4.0 %collective-permute-done.7.refs_7_ = bf16[208,512]{1,0:T(8,128)(2,1)S(1)} collective-permute-done((bf16[208,512]{1,0:T(8,128)(2,1)S(1)}, bf16[208,512]{1,0:T(8,128)(2,1)S(1)}, u32[]{:S(2)}, u32[]{:S(2)}) %collective-permute-start.7) | collective-permute-done | bytes 213024 | tf_op jit(solution)/shard_map/ppermute | solution.py:314
  12.1 2.0 %collective-permute-start.9 = (bf16[208,512]{1,0:T(8,128)(2,1)S(1)}, bf16[208,512]{1,0:T(8,128)(2,1)S(1)}, u32[]{:S(2)}, u32[]{:S(2)}) collective-permute-start(bf16[208,512]{1,0:T(8,128)(2,1)S(1)} %collective-permute-done.7.refs_7_), channel_id=1, source_target_pairs={{0,4},{2,6},{8,0},{10,2},{16,8},{18,10},{24,16},{26,18},{28,24},{3... | collective-permute-start | bytes 638984 | tf_op jit(solution)/shard_map/ppermute | solution.py:314
  14.1 0.3 turn.1.refs_0_
  14.4 0.0 collective-permute-done.refs_4_
  14.4 1.9 %collective-permute-done.1.refs_6_ = bf16[192,512]{1,0:T(8,128)(2,1)S(1)} collective-permute-done((bf16[192,512]{1,0:T(8,128)(2,1)S(1)}, bf16[192,512]{1,0:T(8,128)(2,1)S(1)}, u32[]{:S(2)}, u32[]{:S(2)}) %collective-permute-start.1) | collective-permute-done | bytes 196640 | tf_op jit(solution)/shard_map/ppermute | solution.py:314
  16.3 2.1 %collective-permute-start.4 = (bf16[192,512]{1,0:T(8,128)(2,1)S(1)}, bf16[192,512]{1,0:T(8,128)(2,1)S(1)}, u32[]{:S(2)}, u32[]{:S(2)}) collective-permute-start(bf16[192,512]{1,0:T(8,128)(2,1)S(1)} %collective-permute-done.refs_4_), channel_id=1, source_target_pairs={{0,8},{2,10},{8,16},{10,18},{16,24},{18,26},{24,28},{26,30},{28,20... | collective-permute-start | bytes 589832 | tf_op jit(solution)/shard_map/ppermute | solution.py:313
  18.3 0.0 collective-permute-done.6.refs_5_
  18.3 2.0 %collective-permute-start.11 = (bf16[208,512]{1,0:T(8,128)(2,1)S(1)}, bf16[208,512]{1,0:T(8,128)(2,1)S(1)}, u32[]{:S(2)}, u32[]{:S(2)}) collective-permute-start(bf16[208,512]{1,0:T(8,128)(2,1)S(1)} %collective-permute-done.6.refs_5_), channel_id=1, source_target_pairs={{0,8},{2,10},{8,16},{10,18},{16,24},{18,26},{24,28},{26,30},{28,20... | collective-permute-start | bytes 638984 | tf_op jit(solution)/shard_map/ppermute | solution.py:313
  20.4 0.5 collective-permute-done.9.refs_5_
  20.8 2.0 %collective-permute-start.10 = (bf16[208,512]{1,0:T(8,128)(2,1)S(1)}, bf16[208,512]{1,0:T(8,128)(2,1)S(1)}, u32[]{:S(2)}, u32[]{:S(2)}) collective-permute-start(bf16[208,512]{1,0:T(8,128)(2,1)S(1)} %collective-permute-done.9.refs_5_), channel_id=1, source_target_pairs={{0,4},{2,6},{8,0},{10,2},{16,8},{18,10},{24,16},{26,18},{28,24},{3... | collective-permute-start | bytes 638984 | tf_op jit(solution)/shard_map/ppermute | solution.py:314
  22.8 4.4 %attend.4 = (f32[8,1,480]{2,1,0:T(1,128)S(1)}, f32[8,144,480]{2,1,0:T(8,128)S(1)}) custom-call(bf16[8,128,480]{2,1,0:T(8,128)(2,1)S(1)} %turn.1.refs_0_, bf16[208,512]{1,0:T(8,128)(2,1)S(1)} %maximum_maximum_fusion.refs_1_.refs_3_, bf16[192,512]{1,0:T(8,128)(2,1)S(1)} %get-tuple-element.38.refs_2_, bf16[208,512]{1,0:T(8,128)(2,1)S(1)} %maximum_maximum_fusion.refs_1_.refs_3_, ...), custom_call_target="tpu_custom_call" | custom-call | flops 1132462080 | bytes 4194304 | tf_op jit(solution)/shard_map/attend/pallas_call | solution.py:164
  27.3 0.0 collective-permute-done.5.refs_4_
  27.3 0.5 collective-permute-start.8
  27.8 0.0 collective-permute-done.11.refs_3_
  27.8 1.7 %collective-permute-start.14 = (bf16[208,512]{1,0:T(8,128)(2,1)S(1)}, bf16[208,512]{1,0:T(8,128)(2,1)S(1)}, u32[]{:S(2)}, u32[]{:S(2)}) collective-permute-start(bf16[208,512]{1,0:T(8,128)(2,1)S(1)} %collective-permute-done.11.refs_3_), channel_id=1, source_target_pairs={{0,8},{2,10},{8,16},{10,18},{16,24},{18,26},{24,28},{26,30},{28,20... | collective-permute-start | bytes 638984 | tf_op jit(solution)/shard_map/ppermute | solution.py:313
  29.4 0.3 collective-permute-start.15
  29.8 4.1 %attend.5 = (f32[8,1,480]{2,1,0:T(1,128)S(1)}, f32[8,144,480]{2,1,0:T(8,128)S(1)}) custom-call(bf16[8,128,480]{2,1,0:T(8,128)(2,1)S(1)} %turn.1.refs_0_, bf16[208,512]{1,0:T(8,128)(2,1)S(1)} %maximum_maximum_fusion.refs_1_.refs_3_, bf16[192,512]{1,0:T(8,128)(2,1)S(1)} %collective-permute-done.4.refs_2_, ...), custom_call_target="tpu_custom_call", output_to_operand_aliasing={{0}: (6, {}), {1}: (7, {})} | custom-call | flops 754974720 | bytes 4194304 | tf_op jit(solution)/shard_map/attend/pallas_call | solution.py:164
  33.8 0.0 collective-permute-done.10.refs_5_
  33.9 0.5 collective-permute-done.8.refs_2_
  34.4 1.6 %collective-permute-start.13 = (bf16[208,512]{1,0:T(8,128)(2,1)S(1)}, bf16[208,512]{1,0:T(8,128)(2,1)S(1)}, u32[]{:S(2)}, u32[]{:S(2)}) collective-permute-start(bf16[208,512]{1,0:T(8,128)(2,1)S(1)} %collective-permute-done.10.refs_5_), channel_id=1, source_target_pairs={{0,4},{2,6},{8,0},{10,2},{16,8},{18,10},{24,16},{26,18},{28,24},{3... | collective-permute-start | bytes 638984 | tf_op jit(solution)/shard_map/ppermute | solution.py:314
  36.0 0.4 collective-permute-start.12
  36.4 1.9 %collective-permute-done.14.refs_3_ = bf16[208,512]{1,0:T(8,128)(2,1)S(1)} collective-permute-done((bf16[208,512]{1,0:T(8,128)(2,1)S(1)}, bf16[208,512]{1,0:T(8,128)(2,1)S(1)}, u32[]{:S(2)}, u32[]{:S(2)}) %collective-permute-start.14) | collective-permute-done | bytes 213024 | tf_op jit(solution)/shard_map/ppermute | solution.py:313
  38.3 0.0 collective-permute-done.15.refs_4_
  38.3 4.0 %attend.6 = (f32[8,1,480]{2,1,0:T(1,128)S(1)}, f32[8,144,480]{2,1,0:T(8,128)S(1)}) custom-call(bf16[8,128,480]{2,1,0:T(8,128)(2,1)S(1)} %turn.1.refs_0_, bf16[208,512]{1,0:T(8,128)(2,1)S(1)} %maximum_maximum_fusion.refs_1_.refs_3_, bf16[192,512]{1,0:T(8,128)(2,1)S(1)} %collective-permute-done.8.refs_2_, ...), custom_call_target="tpu_custom_call", output_to_operand_aliasing={{0}: (6, {}), {1}: (7, {})} | custom-call | flops 754974720 | bytes 4194304 | tf_op jit(solution)/shard_map/attend/pallas_call | solution.py:164
  42.4 0.0 collective-permute-done.13.refs_3_
  42.4 2.9 %attend.7 = (f32[8,1,480]{2,1,0:T(1,128)S(1)}, f32[8,144,480]{2,1,0:T(8,128)S(1)}, bf16[192,1280]{1,0:T(8,128)(2,1)S(1)}, bf16[192,1280]{1,0:T(8,128)(2,1)S(1)}) custom-call(bf16[8,128,480]{2,1,0:T(8,128)(2,1)S(1)} %turn.1.refs_0_, bf16[208,512]{1,0:T(8,128)(2,1)S(1)} %maximum_maximum_fusion.refs_1_.refs_3_, ...), custom_call_target="tpu_custom_call", output_to_operand_aliasing={{0}: (4, {}), {1}: (5, {})} | custom-call | flops 377487360 | bytes 4194304 | tf_op jit(solution)/shard_map/attend/pallas_call | solution.py:164
  45.3 0.1 collective-permute-start.16
  45.4 1.9 %collective-permute-done.16.other_ref = bf16[192,1280]{1,0:T(8,128)(2,1)S(1)} collective-permute-done((bf16[192,1280]{1,0:T(8,128)(2,1)S(1)}, bf16[192,1280]{1,0:T(8,128)(2,1)S(1)}, u32[]{:S(2)}, u32[]{:S(2)}) %collective-permute-start.16) | collective-permute-done | bytes 491552 | tf_op jit(solution)/shard_map/ppermute | solution.py:360
  47.2 3.0 %project.4 = (bf16[96,1024]{1,0:T(8,128)(2,1)S(1)}, bf16[96,1024]{1,0:T(8,128)(2,1)S(1)}) custom-call(bf16[192,1280]{1,0:T(8,128)(2,1)S(1)} %get-tuple-element.68.own_ref, bf16[192,1280]{1,0:T(8,128)(2,1)S(1)} %collective-permute-done.16.other_ref, bf16[2560,5120]{1,0:T(8,128)(2,1)} %w_ref.7), custom_call_target="tpu_custom_call" | custom-call | flops 1006632960 | bytes 5242880 | tf_op jit(solution)/shard_map/project/pallas_call | solution.py:243
  50.2 1.6 %collective-permute-start.17 = (bf16[96,1024]{1,0:T(8,128)(2,1)S(1)}, bf16[96,1024]{1,0:T(8,128)(2,1)S(1)}, u32[]{:S(2)}, u32[]{:S(2)}) collective-permute-start(bf16[96,1024]{1,0:T(8,128)(2,1)S(1)} %get-tuple-element.61), channel_id=1, source_target_pairs={{0,1},{1,0},{2,3},{3,2},{4,5},{5,4},{6,7},{7,6},{8,9},{9,8},{10,11... | collective-permute-start | bytes 589832 | tf_op jit(solution)/shard_map/ppermute | solution.py:407
  51.8 3.0 %project.5 = (bf16[96,1024]{1,0:T(8,128)(2,1)S(1)}, bf16[96,1024]{1,0:T(8,128)(2,1)S(1)}) custom-call(bf16[192,1280]{1,0:T(8,128)(2,1)S(1)} %get-tuple-element.68.own_ref, bf16[192,1280]{1,0:T(8,128)(2,1)S(1)} %collective-permute-done.16.other_ref, bf16[2560,5120]{1,0:T(8,128)(2,1)} %w_ref.7), custom_call_target="tpu_custom_call" | custom-call | flops 1006632960 | bytes 5242880 | tf_op jit(solution)/shard_map/project/pallas_call | solution.py:243
  54.8 0.6 collective-permute-start.18
  55.4 1.9 %collective-permute-done.17 = bf16[96,1024]{1,0:T(8,128)(2,1)S(1)} collective-permute-done((bf16[96,1024]{1,0:T(8,128)(2,1)S(1)}, bf16[96,1024]{1,0:T(8,128)(2,1)S(1)}, u32[]{:S(2)}, u32[]{:S(2)}) %collective-permute-start.17) | collective-permute-done | bytes 196640 | tf_op jit(solution)/shard_map/ppermute | solution.py:407
  57.2 4.5 %project.6 = (bf16[96,1792]{1,0:T(8,128)(2,1)S(1)}, bf16[96,1792]{1,0:T(8,128)(2,1)S(1)}) custom-call(bf16[192,1280]{1,0:T(8,128)(2,1)S(1)} %get-tuple-element.68.own_ref, bf16[192,1280]{1,0:T(8,128)(2,1)S(1)} %collective-permute-done.16.other_ref, bf16[2560,5120]{1,0:T(8,128)(2,1)} %w_ref.7), custom_call_target="tpu_custom_call" | custom-call | flops 1761607680 | bytes 9175040 | tf_op jit(solution)/shard_map/project/pallas_call | solution.py:243
  61.7 2.4 %collective-permute-start.19 = (bf16[96,1792]{1,0:T(8,128)(2,1)S(1)}, bf16[96,1792]{1,0:T(8,128)(2,1)S(1)}, u32[]{:S(2)}, u32[]{:S(2)}) collective-permute-start(bf16[96,1792]{1,0:T(8,128)(2,1)S(1)} %get-tuple-element.67), channel_id=1, source_target_pairs={{0,1},{1,0},{2,3},{3,2},{4,5},{5,4},{6,7},{7,6},{8,9},{9,8},{10,11... | collective-permute-start | bytes 1032200 | tf_op jit(solution)/shard_map/ppermute | solution.py:407
  64.1 3.6 %project.7 = (bf16[96,1280]{1,0:T(8,128)(2,1)S(1)}, bf16[96,1280]{1,0:T(8,128)(2,1)S(1)}) custom-call(bf16[192,1280]{1,0:T(8,128)(2,1)S(1)} %get-tuple-element.68.own_ref, bf16[192,1280]{1,0:T(8,128)(2,1)S(1)} %collective-permute-done.16.other_ref, bf16[2560,5120]{1,0:T(8,128)(2,1)} %w_ref.7), custom_call_target="tpu_custom_call" | custom-call | flops 1258291200 | bytes 6553600 | tf_op jit(solution)/shard_map/project/pallas_call | solution.py:243
  67.7 0.1 collective-permute-start.20
  67.8 8.5 %collective-permute-done.20 = bf16[96,1280]{1,0:T(8,128)(2,1)S(1)} collective-permute-done((bf16[96,1280]{1,0:T(8,128)(2,1)S(1)}, bf16[96,1280]{1,0:T(8,128)(2,1)S(1)}, u32[]{:S(2)}, u32[]{:S(2)}) %collective-permute-start.20) | collective-permute-done | bytes 245792 | tf_op jit(solution)/shard_map/ppermute | solution.py:407
  76.3 1.2 %add_convert_fusion = bf16[96,5120]{1,0:T(8,128)(2,1)} fusion(bf16[96,1280]{1,0:T(8,128)(2,1)S(1)} %get-tuple-element.69, bf16[96,1792]{1,0:T(8,128)(2,1)S(1)} %get-tuple-element.66, bf16[96,1024]{1,0:T(8,128)(2,1)S(1)} %get-tuple-element.63, bf16[96,1024]{1,0:T(8,128)(2,1)S(1)} %get-tuple-element.60, bf16[96,1280]{1,0:T(8,128)(2,1)S(1)} %collective-permute-done.20, ...), kind=kLoop, calls=%fused_computation | loop fusion | flops 8847360 | bytes 2949120 | tf_op jit(solution)/shard_map/convert_element_type | solution.py:411
  (11 shorter events, 0.1 us)
Async XLA Ops:
  0.0 14.1 %copy-start = (bf16[192,2560]{1,0:T(8,128)(2,1)S(1)}, bf16[192,2560]{1,0:T(8,128)(2,1)}, u32[]{:S(2)}) copy-start(bf16[192,2560]{1,0:T(8,128)(2,1)} %refs_0_.1) | copy-start | bytes 2949124
  1.2 1.7 %collective-permute-start.3 = (bf16[208,512]{1,0:T(8,128)(2,1)S(1)}, bf16[208,512]{1,0:T(8,128)(2,1)S(1)}, u32[]{:S(2)}, u32[]{:S(2)}) collective-permute-start(bf16[208,512]{1,0:T(8,128)(2,1)S(1)} %get-tuple-element.40), channel_id=1, source_target_pairs={{0,2},{2,0},{4,6},{6,4},{8,10},{10,8},{12,14},{14,12},{16,18},{18,... | collective-permute-start | bytes 638984 | tf_op jit(solution)/shard_map/ppermute | solution.py:317
  2.8 11.3 %collective-permute-start.2 = (bf16[192,1280]{1,0:T(8,128)(2,1)S(1)}, bf16[192,1280]{1,0:T(8,128)(2,1)S(1)}, u32[]{:S(2)}, u32[]{:S(2)}) collective-permute-start(bf16[192,1280]{1,0:T(8,128)(2,1)S(1)} %constant_dynamic-slice_fusion), channel_id=1, source_target_pairs={{0,2},{2,0},{4,6},{6,4},{8,10},{10,8},{12,14},{14,12},{16,18},{18,... | collective-permute-start | bytes 1474568 | tf_op jit(solution)/shard_map/ppermute | solution.py:324
  2.9 9.1 %collective-permute-start.7 = (bf16[208,512]{1,0:T(8,128)(2,1)S(1)}, bf16[208,512]{1,0:T(8,128)(2,1)S(1)}, u32[]{:S(2)}, u32[]{:S(2)}) collective-permute-start(bf16[208,512]{1,0:T(8,128)(2,1)S(1)} %maximum_maximum_fusion.refs_1_.refs_3_), channel_id=1, source_target_pairs={{0,4},{2,6},{8,0},{10,2},{16,8},{18,10},{24,16},{26,18},{28,24},{3... | collective-permute-start | bytes 638984 | tf_op jit(solution)/shard_map/ppermute | solution.py:314
  6.0 8.5 %collective-permute-start = (bf16[192,512]{1,0:T(8,128)(2,1)S(1)}, bf16[192,512]{1,0:T(8,128)(2,1)S(1)}, u32[]{:S(2)}, u32[]{:S(2)}) collective-permute-start(bf16[192,512]{1,0:T(8,128)(2,1)S(1)} %get-tuple-element.38.refs_2_), channel_id=1, source_target_pairs={{0,8},{2,10},{8,16},{10,18},{16,24},{18,26},{24,28},{26,30},{28,20... | collective-permute-start | bytes 589832 | tf_op jit(solution)/shard_map/ppermute | solution.py:313
  6.1 10.2 %collective-permute-start.1 = (bf16[192,512]{1,0:T(8,128)(2,1)S(1)}, bf16[192,512]{1,0:T(8,128)(2,1)S(1)}, u32[]{:S(2)}, u32[]{:S(2)}) collective-permute-start(bf16[192,512]{1,0:T(8,128)(2,1)S(1)} %get-tuple-element.38.refs_2_), channel_id=1, source_target_pairs={{0,4},{2,6},{8,0},{10,2},{16,8},{18,10},{24,16},{26,18},{28,24},{3... | collective-permute-start | bytes 589832 | tf_op jit(solution)/shard_map/ppermute | solution.py:314
  8.0 10.4 %collective-permute-start.6 = (bf16[208,512]{1,0:T(8,128)(2,1)S(1)}, bf16[208,512]{1,0:T(8,128)(2,1)S(1)}, u32[]{:S(2)}, u32[]{:S(2)}) collective-permute-start(bf16[208,512]{1,0:T(8,128)(2,1)S(1)} %maximum_maximum_fusion.refs_1_.refs_3_), channel_id=1, source_target_pairs={{0,8},{2,10},{8,16},{10,18},{16,24},{18,26},{24,28},{26,30},{28,20... | collective-permute-start | bytes 638984 | tf_op jit(solution)/shard_map/ppermute | solution.py:313
  12.1 8.8 %collective-permute-start.9 = (bf16[208,512]{1,0:T(8,128)(2,1)S(1)}, bf16[208,512]{1,0:T(8,128)(2,1)S(1)}, u32[]{:S(2)}, u32[]{:S(2)}) collective-permute-start(bf16[208,512]{1,0:T(8,128)(2,1)S(1)} %collective-permute-done.7.refs_7_), channel_id=1, source_target_pairs={{0,4},{2,6},{8,0},{10,2},{16,8},{18,10},{24,16},{26,18},{28,24},{3... | collective-permute-start | bytes 638984 | tf_op jit(solution)/shard_map/ppermute | solution.py:314
  16.3 11.0 %collective-permute-start.4 = (bf16[192,512]{1,0:T(8,128)(2,1)S(1)}, bf16[192,512]{1,0:T(8,128)(2,1)S(1)}, u32[]{:S(2)}, u32[]{:S(2)}) collective-permute-start(bf16[192,512]{1,0:T(8,128)(2,1)S(1)} %collective-permute-done.refs_4_), channel_id=1, source_target_pairs={{0,8},{2,10},{8,16},{10,18},{16,24},{18,26},{24,28},{26,30},{28,20... | collective-permute-start | bytes 589832 | tf_op jit(solution)/shard_map/ppermute | solution.py:313
  18.3 8.9 %collective-permute-start.5 = (bf16[192,512]{1,0:T(8,128)(2,1)S(1)}, bf16[192,512]{1,0:T(8,128)(2,1)S(1)}, u32[]{:S(2)}, u32[]{:S(2)}) collective-permute-start(bf16[192,512]{1,0:T(8,128)(2,1)S(1)} %collective-permute-done.1.refs_6_), channel_id=1, source_target_pairs={{0,4},{2,6},{8,0},{10,2},{16,8},{18,10},{24,16},{26,18},{28,24},{3... | collective-permute-start | bytes 589832 | tf_op jit(solution)/shard_map/ppermute | solution.py:314
  18.3 9.4 %collective-permute-start.11 = (bf16[208,512]{1,0:T(8,128)(2,1)S(1)}, bf16[208,512]{1,0:T(8,128)(2,1)S(1)}, u32[]{:S(2)}, u32[]{:S(2)}) collective-permute-start(bf16[208,512]{1,0:T(8,128)(2,1)S(1)} %collective-permute-done.6.refs_5_), channel_id=1, source_target_pairs={{0,8},{2,10},{8,16},{10,18},{16,24},{18,26},{24,28},{26,30},{28,20... | collective-permute-start | bytes 638984 | tf_op jit(solution)/shard_map/ppermute | solution.py:313
  20.8 13.0 %collective-permute-start.10 = (bf16[208,512]{1,0:T(8,128)(2,1)S(1)}, bf16[208,512]{1,0:T(8,128)(2,1)S(1)}, u32[]{:S(2)}, u32[]{:S(2)}) collective-permute-start(bf16[208,512]{1,0:T(8,128)(2,1)S(1)} %collective-permute-done.9.refs_5_), channel_id=1, source_target_pairs={{0,4},{2,6},{8,0},{10,2},{16,8},{18,10},{24,16},{26,18},{28,24},{3... | collective-permute-start | bytes 638984 | tf_op jit(solution)/shard_map/ppermute | solution.py:314
  27.3 7.1 %collective-permute-start.8 = (bf16[192,512]{1,0:T(8,128)(2,1)S(1)}, bf16[192,512]{1,0:T(8,128)(2,1)S(1)}, u32[]{:S(2)}, u32[]{:S(2)}) collective-permute-start(bf16[192,512]{1,0:T(8,128)(2,1)S(1)} %collective-permute-done.4.refs_2_), channel_id=1, source_target_pairs={{0,8},{2,10},{8,16},{10,18},{16,24},{18,26},{24,28},{26,30},{28,20... | collective-permute-start | bytes 589832 | tf_op jit(solution)/shard_map/ppermute | solution.py:313
  27.8 10.6 %collective-permute-start.14 = (bf16[208,512]{1,0:T(8,128)(2,1)S(1)}, bf16[208,512]{1,0:T(8,128)(2,1)S(1)}, u32[]{:S(2)}, u32[]{:S(2)}) collective-permute-start(bf16[208,512]{1,0:T(8,128)(2,1)S(1)} %collective-permute-done.11.refs_3_), channel_id=1, source_target_pairs={{0,8},{2,10},{8,16},{10,18},{16,24},{18,26},{24,28},{26,30},{28,20... | collective-permute-start | bytes 638984 | tf_op jit(solution)/shard_map/ppermute | solution.py:313
  29.4 8.9 %collective-permute-start.15 = (bf16[192,512]{1,0:T(8,128)(2,1)S(1)}, bf16[192,512]{1,0:T(8,128)(2,1)S(1)}, u32[]{:S(2)}, u32[]{:S(2)}) collective-permute-start(bf16[192,512]{1,0:T(8,128)(2,1)S(1)} %collective-permute-done.5.refs_4_), channel_id=1, source_target_pairs={{0,4},{2,6},{8,0},{10,2},{16,8},{18,10},{24,16},{26,18},{28,24},{3... | collective-permute-start | bytes 589832 | tf_op jit(solution)/shard_map/ppermute | solution.py:314
  34.4 8.0 %collective-permute-start.13 = (bf16[208,512]{1,0:T(8,128)(2,1)S(1)}, bf16[208,512]{1,0:T(8,128)(2,1)S(1)}, u32[]{:S(2)}, u32[]{:S(2)}) collective-permute-start(bf16[208,512]{1,0:T(8,128)(2,1)S(1)} %collective-permute-done.10.refs_5_), channel_id=1, source_target_pairs={{0,4},{2,6},{8,0},{10,2},{16,8},{18,10},{24,16},{26,18},{28,24},{3... | collective-permute-start | bytes 638984 | tf_op jit(solution)/shard_map/ppermute | solution.py:314
  36.0 6.4 %collective-permute-start.12 = (bf16[192,512]{1,0:T(8,128)(2,1)S(1)}, bf16[192,512]{1,0:T(8,128)(2,1)S(1)}, u32[]{:S(2)}, u32[]{:S(2)}) collective-permute-start(bf16[192,512]{1,0:T(8,128)(2,1)S(1)} %collective-permute-done.8.refs_2_), channel_id=1, source_target_pairs={{0,8},{2,10},{8,16},{10,18},{16,24},{18,26},{24,28},{26,30},{28,20... | collective-permute-start | bytes 589832 | tf_op jit(solution)/shard_map/ppermute | solution.py:313
  45.3 1.9 %collective-permute-start.16 = (bf16[192,1280]{1,0:T(8,128)(2,1)S(1)}, bf16[192,1280]{1,0:T(8,128)(2,1)S(1)}, u32[]{:S(2)}, u32[]{:S(2)}) collective-permute-start(bf16[192,1280]{1,0:T(8,128)(2,1)S(1)} %get-tuple-element.59), channel_id=1, source_target_pairs={{0,2},{2,0},{4,6},{6,4},{8,10},{10,8},{12,14},{14,12},{16,18},{18,... | collective-permute-start | bytes 1474568 | tf_op jit(solution)/shard_map/ppermute | solution.py:360
  50.2 7.0 %collective-permute-start.17 = (bf16[96,1024]{1,0:T(8,128)(2,1)S(1)}, bf16[96,1024]{1,0:T(8,128)(2,1)S(1)}, u32[]{:S(2)}, u32[]{:S(2)}) collective-permute-start(bf16[96,1024]{1,0:T(8,128)(2,1)S(1)} %get-tuple-element.61), channel_id=1, source_target_pairs={{0,1},{1,0},{2,3},{3,2},{4,5},{5,4},{6,7},{7,6},{8,9},{9,8},{10,11... | collective-permute-start | bytes 589832 | tf_op jit(solution)/shard_map/ppermute | solution.py:407
  54.8 9.3 %collective-permute-start.18 = (bf16[96,1024]{1,0:T(8,128)(2,1)S(1)}, bf16[96,1024]{1,0:T(8,128)(2,1)S(1)}, u32[]{:S(2)}, u32[]{:S(2)}) collective-permute-start(bf16[96,1024]{1,0:T(8,128)(2,1)S(1)} %get-tuple-element.64), channel_id=1, source_target_pairs={{0,1},{1,0},{2,3},{3,2},{4,5},{5,4},{6,7},{7,6},{8,9},{9,8},{10,11... | collective-permute-start | bytes 589832 | tf_op jit(solution)/shard_map/ppermute | solution.py:407
  61.7 14.6 %collective-permute-start.19 = (bf16[96,1792]{1,0:T(8,128)(2,1)S(1)}, bf16[96,1792]{1,0:T(8,128)(2,1)S(1)}, u32[]{:S(2)}, u32[]{:S(2)}) collective-permute-start(bf16[96,1792]{1,0:T(8,128)(2,1)S(1)} %get-tuple-element.67), channel_id=1, source_target_pairs={{0,1},{1,0},{2,3},{3,2},{4,5},{5,4},{6,7},{7,6},{8,9},{9,8},{10,11... | collective-permute-start | bytes 1032200 | tf_op jit(solution)/shard_map/ppermute | solution.py:407
  67.7 8.6 %collective-permute-start.20 = (bf16[96,1280]{1,0:T(8,128)(2,1)S(1)}, bf16[96,1280]{1,0:T(8,128)(2,1)S(1)}, u32[]{:S(2)}, u32[]{:S(2)}) collective-permute-start(bf16[96,1280]{1,0:T(8,128)(2,1)S(1)} %get-tuple-element.70), channel_id=1, source_target_pairs={{0,1},{1,0},{2,3},{3,2},{4,5},{5,4},{6,7},{7,6},{8,9},{9,8},{10,11... | collective-permute-start | bytes 737288 | tf_op jit(solution)/shard_map/ppermute | solution.py:407

commit v6 on v5

--- a/solution.py
+++ b/solution.py
@@ -15,6 +15,7 @@
 MASKED = -1e30
 VMEM_LIMIT = 16 * 1024 * 1024
 HEADER = 16
+PIECES = 5
 
 
 def ring_of_chips(chips):
@@ -48,6 +49,19 @@
 def turned_values(blocks):
     v = jnp.concatenate(blocks, axis=0)
     return jnp.concatenate([jnp.transpose(v), jnp.ones((HEADER, v.shape[0]), v.dtype)], axis=0)
+
+
+def fetch_columns(w_ref, first, held_ref, sems):
+    pieces = sems.shape[0]
+    depth, width = held_ref.shape[0] // pieces, held_ref.shape[1]
+    copies = []
+    for p in range(pieces):
+        at = pl.ds(p * depth, depth)
+        copies.append(
+            pltpu.make_async_copy(w_ref.at[at, pl.ds(first, width)], held_ref.at[at], sems.at[p])
+        )
+        copies[-1].start()
+    return copies
 
 
 def attend_kernel(plan, *refs):
@@ -58,8 +72,15 @@
     packets = [refs.pop(0) for _ in range(plan["packets"])]
     if plan["carried"]:
         in_high, in_sums = refs.pop(0), refs.pop(0)
-    high_ref, sums_ref = refs.pop(0), refs.pop(0)
-    out_refs = refs
+    fetch = plan["fetch"]
+    if fetch:
+        w_ref = refs.pop(0)
+    if plan["last"]:
+        out_refs = [refs.pop(0) for _ in range(owners)]
+    if fetch:
+        held_ref, sems = (refs.pop(0) if plan["last"] else refs.pop(2)), refs.pop()
+        copies = fetch_columns(w_ref, fetch[0], held_ref, sems)
+    high_ref, sums_ref = refs
 
     sources = mark_refs + packets
     numbers = [
@@ -144,35 +165,44 @@
                                 side * chunk : (side + 1) * chunk,
                                 h * GROUP + g * HEAD_WIDTH : h * GROUP + (g + 1) * HEAD_WIDTH,
                             ] = mixed[g * chunk : (g + 1) * chunk]
-
-
-def attend(plan, turned, marks, packets, state):
+    if fetch:
+        for copy in copies:
+            copy.wait()
+
+
+def attend(plan, turned, marks, packets, state, out_weight=None):
     heads, chunk, owners = plan["heads"], plan["chunk"], plan["owners"]
     count = len(plan["members"])
     plan = dict(plan, marks=len(marks), packets=len(packets), carried=state is not None)
+    fetch = plan.setdefault("fetch", None)
     rows = QUERY_PER_KEY * chunk
     slots = owners * 2 * heads
     vmem = pl.BlockSpec(memory_space=pltpu.VMEM)
-    out_shape = [
-        jax.ShapeDtypeStruct((slots, 1, rows), jnp.float32),
-        jax.ShapeDtypeStruct((slots, HEAD_WIDTH + HEADER, rows), jnp.float32),
-    ]
+    kept = [(slots, 1, rows), (slots, HEAD_WIDTH + HEADER, rows)]
     if plan["last"]:
-        out_shape += [jax.ShapeDtypeStruct((2 * chunk, heads * GROUP), jnp.bfloat16)] * owners
-    operands = 1 + len(marks) + len(packets)
+        out_shape = [jax.ShapeDtypeStruct((2 * chunk, heads * GROUP), jnp.bfloat16)] * owners
+    else:
+        out_shape = [jax.ShapeDtypeStruct(shape, jnp.float32) for shape in kept]
+    operands = 1 + len(marks) + len(packets) + (0 if state is None else 2)
+    in_specs = [vmem] * operands
+    scratch = [pltpu.VMEM(shape, jnp.float32) for shape in kept] if plan["last"] else []
+    if fetch:
+        in_specs.append(pl.BlockSpec(memory_space=pltpu.HBM))
+        out_shape.append(jax.ShapeDtypeStruct((out_weight.shape[0], fetch[1]), out_weight.dtype))
+        scratch.append(pltpu.SemaphoreType.DMA((PIECES,)))
     flops = 4 * owners * heads * rows * HEAD_WIDTH * count * chunk * 2
     return pl.pallas_call(
         functools.partial(attend_kernel, plan),
         out_shape=out_shape,
-        in_specs=[vmem] * (operands + (0 if state is None else 2)),
+        in_specs=in_specs,
         out_specs=[vmem] * len(out_shape),
-        input_output_aliases={} if state is None else {operands: 0, operands + 1: 1},
+        scratch_shapes=scratch,
         cost_estimate=pl.CostEstimate(
             flops=flops, bytes_accessed=4 << 20, transcendentals=flops // 512
         ),
         compiler_params=pltpu.CompilerParams(vmem_limit_bytes=VMEM_LIMIT),
         name="attend",
-    )(turned, *marks, *packets, *(state or ()))
+    )(turned, *marks, *packets, *(state or ()), *([out_weight] if fetch else []))
 
 
 def turn_kernel(heads, chunk, whole_rows, *refs):
@@ -206,18 +236,13 @@
     )(*queries)
 
 
-def project_kernel(first, own_ref, other_ref, w_ref, sent_ref, kept_ref, rows_ref, held_ref, sems):
-    chunk, width = sent_ref.shape
-    pieces = sems.shape[0]
-    depth = held_ref.shape[0] // pieces
-    copies = []
-    for p in range(pieces):
-        at = pl.ds(p * depth, depth)
-        copies.append(
-            pltpu.make_async_copy(w_ref.at[at, pl.ds(first, width)], held_ref.at[at], sems.at[p])
-        )
-        copies[-1].start()
-    part = own_ref.shape[1]
+def project_kernel(following, own_ref, other_ref, held_ref, *refs):
+    if following:
+        w_ref, sent_ref, kept_ref, next_ref, rows_ref, sems = refs
+        copies = fetch_columns(w_ref, following[0], next_ref, sems)
+    else:
+        sent_ref, kept_ref, rows_ref = refs
+    chunk, part = sent_ref.shape[0], own_ref.shape[1]
     mine = lax.axis_index("inner").astype(jnp.int32)
     left = my_core() == 0
     for place, half in enumerate((1 - mine, mine)):
@@ -226,36 +251,37 @@
         to = slice(place * chunk, (place + 1) * chunk)
         rows_ref[to, :part] = jnp.where(left, own, other)
         rows_ref[to, part:] = jnp.where(left, other, own)
-    total = None
-    for p in range(pieces):
-        copies[p].wait()
-        at = slice(p * depth, (p + 1) * depth)
-        term = product(rows_ref[:, at], held_ref[at])
-        total = term if total is None else total + term
-    total = total.astype(sent_ref.dtype)
-    sent_ref[...] = total[:chunk]
-    kept_ref[...] = total[chunk:]
-
-
-def project(own, other, out_weight, first, width, pieces):
-    rows, depth = own.shape[0], out_weight.shape[0]
+    both = product(rows_ref[...], held_ref[...]).astype(sent_ref.dtype)
+    sent_ref[...] = both[:chunk]
+    kept_ref[...] = both[chunk:]
+    if following:
+        for copy in copies:
+            copy.wait()
+
+
+def project(own, other, held, out_weight, following):
+    rows, (depth, width) = own.shape[0], held.shape
     vmem = pl.BlockSpec(memory_space=pltpu.VMEM)
+    out_shape = [jax.ShapeDtypeStruct((rows // 2, width), jnp.bfloat16)] * 2
+    in_specs, operands = [vmem] * 3, [own, other, held]
+    scratch = [pltpu.VMEM((rows, depth), jnp.bfloat16)]
+    if following:
+        out_shape.append(jax.ShapeDtypeStruct((depth, following[1]), held.dtype))
+        in_specs.append(pl.BlockSpec(memory_space=pltpu.HBM))
+        operands.append(out_weight)
+        scratch.append(pltpu.SemaphoreType.DMA((PIECES,)))
     return pl.pallas_call(
-        functools.partial(project_kernel, first),
-        out_shape=[jax.ShapeDtypeStruct((rows // 2, width), jnp.bfloat16)] * 2,
-        in_specs=[vmem, vmem, pl.BlockSpec(memory_space=pltpu.HBM)],
-        out_specs=[vmem, vmem],
-        scratch_shapes=[
-            pltpu.VMEM((rows, depth), jnp.bfloat16),
-            pltpu.VMEM((depth, width), jnp.bfloat16),
-            pltpu.SemaphoreType.DMA((pieces,)),
-        ],
+        functools.partial(project_kernel, following),
+        out_shape=out_shape,
+        in_specs=in_specs,
+        out_specs=[vmem] * len(out_shape),
+        scratch_shapes=scratch,
         cost_estimate=pl.CostEstimate(
             flops=2 * rows * depth * width, bytes_accessed=2 * depth * width, transcendentals=0
         ),
         compiler_params=pltpu.CompilerParams(vmem_limit_bytes=VMEM_LIMIT),
         name="project",
-    )(own, other, out_weight)
+    )(*operands)
 
 
 def prepare_kernel(chunk, k_ref, v_ref, position_ref, sent_ref, kept_ref, mark_ref, first_ref, sems):
@@ -303,7 +329,7 @@
     return lax.optimization_barrier((value, *events))[0]
 
 
-def split_over_cores(count, queries, keys, values, positions):
+def split_over_cores(count, queries, keys, values, positions, out_weight, fetch):
     chips, half = count // 2, count // 4
     rows, chunk = queries.shape[0], queries.shape[0] // 2
     heads = keys.shape[1] // HEAD_WIDTH // 2
@@ -336,8 +362,10 @@
             members=[(2 * j + i, 0) for j in each for i in range(2)],
             headers=[(2 + 2 * j, rows, i * width) for j in each for i in range(2)],
             owner_headers=[(0, rows, 0), (0, rows, width)],
+            fetch=fetch if last else None,
         )
-        return attend(plan, turned, [y], [packet for pair in pairs for packet in pair], state)
+        packets = [packet for pair in pairs for packet in pair]
+        return attend(plan, turned, [y], packets, state, out_weight)
 
     state = None
     ups = downs = (x, y)
@@ -356,8 +384,8 @@
     x_up, y_down, *state = lax.optimization_barrier((ups[0], downs[1], *state))
     far = (up(x_up), down(y_down))
     state = call(arrived, state, False)
-    _, _, own, theirs = call([far], state, False, True)
-    return own, lax.ppermute(theirs, "blk", sibling)
+    own, theirs, held = call([far], state, False, True)
+    return own, lax.ppermute(theirs, "blk", sibling), held
 
 
 def one_head_a_device(count, queries, keys, values, positions):
@@ -383,7 +411,7 @@
         owner_headers=[(0, rows, 0)],
     )
     turned = turn(heads, chunk, (False,), [queries])
-    return attend(plan, turned, [], [packets], None)[2]
+    return attend(plan, turned, [], [packets], None)[0]
 
 
 def shards(count, inner, queries, keys, values, positions, out_weight):
@@ -394,19 +422,23 @@
         return lax.psum_scatter(
             partial.astype(jnp.bfloat16), "inner", scatter_dimension=0, tiled=True
         )
-    own, other = split_over_cores(count, queries, keys, values, positions)
     out_weight = pltpu.with_memory_space_constraint(out_weight, pltpu.HBM)
-    width = out_weight.shape[1]
-    shares = (4, 4, 7, 5)
-    received, kept, first, source = [], [], 0, own
-    for j, share in enumerate(shares):
-        columns = width * share // sum(shares)
+    shares = (5, 5, 6, 4)
+    widths = [out_weight.shape[1] * share // sum(shares) for share in shares]
+    cuts = [(sum(widths[:j]), columns) for j, columns in enumerate(widths)]
+    own, other, held = split_over_cores(
+        count, queries, keys, values, positions, out_weight, cuts[0]
+    )
+    received, kept, source = [], [], own
+    for j in range(len(cuts)):
         if j > 0:
             source = after(own, sent, *received[: j - 1][-1:])
-        sent, keep = project(source, other, out_weight, first, columns, 5)
+        following = cuts[j + 1] if j + 1 < len(cuts) else None
+        sent, keep, *rest = project(source, other, held, out_weight, following)
+        if rest:
+            held = rest[0]
         received.append(lax.ppermute(sent, "inner", [(0, 1), (1, 0)]))
         kept.append(keep)
-        first += columns
     mine, theirs = jnp.concatenate(kept, axis=1), jnp.concatenate(received, axis=1)
     return (mine.astype(jnp.float32) + theirs.astype(jnp.float32)).astype(jnp.bfloat16)
 

time: 77.7 us -> 77 us (level)
  Pallas kernels: 31 us -> 27.9 us
  waiting for transfers between devices: 21 us -> 23 us
    pallas_call x4, Pallas kernels: 14.1 us -> 10.8 us  [project(): pl.pallas_call(functools.partial(project_kernel, following), out_shape=ou...]
    ppermute x7, waiting for transfers between devices: 2.46 us -> 4.24 us  [split_over_cores(): up = lambda x: lax.ppermute(x, 'blk', clock)]
    ppermute x4, starting transfers between devices: 4.6 us -> 5.52 us  [shards(): received.append(lax.ppermute(sent, 'inner', [(0, 1), (1, 0)]))]
  transfers between devices with their start and end apart: 21 -> 21, of which waited for: 8 -> 9; matrix products, arithmetic and copies ran while one was open for 1% -> 1% of each run, Pallas kernels for 31% -> 25%
where the time goes in v6:
time: 77 us; the launch traced here: 76.8 us
  Pallas kernels  27.9 us (36%)
  starting transfers between devices  23.4 us (30%)
  waiting for transfers between devices  23 us (30%)
  other arithmetic  1.21 us (2%)
  local copies, waits for them, and re-layouts  1.08 us (1%)
    pallas_call x4, Pallas kernels, attend(): pl.pallas_call(functools.partial(attend_kernel, plan), out_shape=out_shap...  15.6 us
    pallas_call x4, Pallas kernels, project(): pl.pallas_call(functools.partial(project_kernel, following), out_shape=ou...  10.8 us
    ppermute x4, waiting for transfers between devices, shards(): received.append(lax.ppermute(sent, 'inner', [(0, 1), (1, 0)]))  10.6 us
    ppermute x7, starting transfers between devices, split_over_cores(): down = lambda x: lax.ppermute(x, 'blk', counter)  10.5 us
    ppermute x7, starting transfers between devices, split_over_cores(): up = lambda x: lax.ppermute(x, 'blk', clock)  6.68 us
    ppermute x7, waiting for transfers between devices, split_over_cores(): down = lambda x: lax.ppermute(x, 'blk', counter)  6.31 us
    ppermute x4, starting transfers between devices, shards(): received.append(lax.ppermute(sent, 'inner', [(0, 1), (1, 0)]))  5.52 us
    ppermute x7, waiting for transfers between devices, split_over_cores(): up = lambda x: lax.ppermute(x, 'blk', clock)  4.24 us
  transfers between devices with their start and end apart: 21, of which 9 were waited for; matrix products, arithmetic and copies ran while one was open for 1% of the time, Pallas kernels for 25%

profile of v6, /device:TPU:0, one launch (start us, length us, event | category | flops | bytes accessed | tf_op | source)
XLA Modules:
  0.0 76.8 jit_solution(17938466298497143810)
XLA Ops:
  0.0 1.2 %prepare.1 = (bf16[208,512]{1,0:T(8,128)(2,1)S(1)}, bf16[192,512]{1,0:T(8,128)(2,1)S(1)}, bf16[16,256]{1,0:T(8,128)(2,1)S(1)}) custom-call(bf16[192,512]{1,0:T(8,128)(2,1)} %k_ref.1, bf16[192,512]{1,0:T(8,128)(2,1)} %v_ref.1, s32[192]{0:T(256)} %position_ref.1), custom_call_target="tpu_custom_call" | custom-call | tf_op jit(solution)/shard_map/prepare/pallas_call | solution.py:310
  1.2 0.5 collective-permute-start.3
  1.7 1.1 %constant_dynamic-slice_fusion = bf16[192,1280]{1,0:T(8,128)(2,1)S(1)} fusion(bf16[192,2560]{1,0:T(8,128)(2,1)} %refs_0_.4, s32[]{:T(128)S(6)} %select_n.3), kind=kLoop, calls=%fused_computation.2 | loop fusion | bytes 983044 | tf_op jit(solution)/shard_map/dynamic_slice | solution.py:347
  2.8 0.1 collective-permute-start.2
  2.9 0.0 collective-permute-done.3
  2.9 3.0 %collective-permute-start.7 = (bf16[208,512]{1,0:T(8,128)(2,1)S(1)}, bf16[208,512]{1,0:T(8,128)(2,1)S(1)}, u32[]{:S(2)}, u32[]{:S(2)}) collective-permute-start(bf16[208,512]{1,0:T(8,128)(2,1)S(1)} %maximum_maximum_fusion.refs_1_.refs_3_), channel_id=1, source_target_pairs={{0,4},{2,6},{8,0},{10,2},{16,8},{18,10},{24,16},{26,18},{28,24},{3... | collective-permute-start | bytes 638984 | tf_op jit(solution)/shard_map/ppermute | solution.py:340
  5.9 1.6 %collective-permute-start.1 = (bf16[192,512]{1,0:T(8,128)(2,1)S(1)}, bf16[192,512]{1,0:T(8,128)(2,1)S(1)}, u32[]{:S(2)}, u32[]{:S(2)}) collective-permute-start(bf16[192,512]{1,0:T(8,128)(2,1)S(1)} %get-tuple-element.42.refs_2_), channel_id=1, source_target_pairs={{0,4},{2,6},{8,0},{10,2},{16,8},{18,10},{24,16},{26,18},{28,24},{3... | collective-permute-start | bytes 589832 | tf_op jit(solution)/shard_map/ppermute | solution.py:340
  7.5 0.4 collective-permute-start
  8.0 0.1 collective-permute-start.6
  8.1 4.0 %collective-permute-done.7.refs_7_ = bf16[208,512]{1,0:T(8,128)(2,1)S(1)} collective-permute-done((bf16[208,512]{1,0:T(8,128)(2,1)S(1)}, bf16[208,512]{1,0:T(8,128)(2,1)S(1)}, u32[]{:S(2)}, u32[]{:S(2)}) %collective-permute-start.7) | collective-permute-done | bytes 213024 | tf_op jit(solution)/shard_map/ppermute | solution.py:340
  12.1 2.0 %collective-permute-start.9 = (bf16[208,512]{1,0:T(8,128)(2,1)S(1)}, bf16[208,512]{1,0:T(8,128)(2,1)S(1)}, u32[]{:S(2)}, u32[]{:S(2)}) collective-permute-start(bf16[208,512]{1,0:T(8,128)(2,1)S(1)} %collective-permute-done.7.refs_7_), channel_id=1, source_target_pairs={{0,4},{2,6},{8,0},{10,2},{16,8},{18,10},{24,16},{26,18},{28,24},{3... | collective-permute-start | bytes 638984 | tf_op jit(solution)/shard_map/ppermute | solution.py:340
  14.1 0.0 collective-permute-done.2.refs_1_
  14.1 0.3 turn.1.refs_0_
  14.4 1.9 %collective-permute-done.1.refs_6_ = bf16[192,512]{1,0:T(8,128)(2,1)S(1)} collective-permute-done((bf16[192,512]{1,0:T(8,128)(2,1)S(1)}, bf16[192,512]{1,0:T(8,128)(2,1)S(1)}, u32[]{:S(2)}, u32[]{:S(2)}) %collective-permute-start.1) | collective-permute-done | bytes 196640 | tf_op jit(solution)/shard_map/ppermute | solution.py:340
  16.3 0.0 collective-permute-done.refs_4_
  16.3 2.1 %collective-permute-start.4 = (bf16[192,512]{1,0:T(8,128)(2,1)S(1)}, bf16[192,512]{1,0:T(8,128)(2,1)S(1)}, u32[]{:S(2)}, u32[]{:S(2)}) collective-permute-start(bf16[192,512]{1,0:T(8,128)(2,1)S(1)} %collective-permute-done.refs_4_), channel_id=1, source_target_pairs={{0,8},{2,10},{8,16},{10,18},{16,24},{18,26},{24,28},{26,30},{28,20... | collective-permute-start | bytes 589832 | tf_op jit(solution)/shard_map/ppermute | solution.py:339
  18.3 0.0 collective-permute-start.5
  18.3 0.6 collective-permute-done.6.refs_5_
  18.9 1.5 %collective-permute-start.11 = (bf16[208,512]{1,0:T(8,128)(2,1)S(1)}, bf16[208,512]{1,0:T(8,128)(2,1)S(1)}, u32[]{:S(2)}, u32[]{:S(2)}) collective-permute-start(bf16[208,512]{1,0:T(8,128)(2,1)S(1)} %collective-permute-done.6.refs_5_), channel_id=1, source_target_pairs={{0,8},{2,10},{8,16},{10,18},{16,24},{18,26},{24,28},{26,30},{28,20... | collective-permute-start | bytes 638984 | tf_op jit(solution)/shard_map/ppermute | solution.py:339
  20.4 0.5 collective-permute-done.9.refs_5_
  20.8 2.0 %collective-permute-start.10 = (bf16[208,512]{1,0:T(8,128)(2,1)S(1)}, bf16[208,512]{1,0:T(8,128)(2,1)S(1)}, u32[]{:S(2)}, u32[]{:S(2)}) collective-permute-start(bf16[208,512]{1,0:T(8,128)(2,1)S(1)} %collective-permute-done.9.refs_5_), channel_id=1, source_target_pairs={{0,4},{2,6},{8,0},{10,2},{16,8},{18,10},{24,16},{26,18},{28,24},{3... | collective-permute-start | bytes 638984 | tf_op jit(solution)/shard_map/ppermute | solution.py:340
  22.8 4.4 %attend.4 = (f32[8,1,480]{2,1,0:T(1,128)S(1)}, f32[8,144,480]{2,1,0:T(8,128)S(1)}) custom-call(bf16[8,128,480]{2,1,0:T(8,128)(2,1)S(1)} %turn.1.refs_0_, bf16[208,512]{1,0:T(8,128)(2,1)S(1)} %maximum_maximum_fusion.refs_1_.refs_3_, bf16[192,512]{1,0:T(8,128)(2,1)S(1)} %get-tuple-element.42.refs_2_, bf16[208,512]{1,0:T(8,128)(2,1)S(1)} %maximum_maximum_fusion.refs_1_.refs_3_, ...), custom_call_target="tpu_custom_call" | custom-call | flops 1132462080 | bytes 4194304 | tf_op jit(solution)/shard_map/attend/pallas_call | solution.py:194
  27.3 0.5 collective-permute-start.8
  27.8 1.7 %collective-permute-start.14 = (bf16[208,512]{1,0:T(8,128)(2,1)S(1)}, bf16[208,512]{1,0:T(8,128)(2,1)S(1)}, u32[]{:S(2)}, u32[]{:S(2)}) collective-permute-start(bf16[208,512]{1,0:T(8,128)(2,1)S(1)} %collective-permute-done.11.refs_3_), channel_id=1, source_target_pairs={{0,8},{2,10},{8,16},{10,18},{16,24},{18,26},{24,28},{26,30},{28,20... | collective-permute-start | bytes 638984 | tf_op jit(solution)/shard_map/ppermute | solution.py:339
  29.4 0.4 collective-permute-start.15
  29.8 3.3 %attend.5 = (f32[8,1,480]{2,1,0:T(1,128)S(1)}, f32[8,144,480]{2,1,0:T(8,128)S(1)}) custom-call(bf16[8,128,480]{2,1,0:T(8,128)(2,1)S(1)} %turn.1.refs_0_, bf16[208,512]{1,0:T(8,128)(2,1)S(1)} %maximum_maximum_fusion.refs_1_.refs_3_, bf16[192,512]{1,0:T(8,128)(2,1)S(1)} %collective-permute-done.4.refs_2_, ...), custom_call_target="tpu_custom_call" | custom-call | flops 754974720 | bytes 4194304 | tf_op jit(solution)/shard_map/attend/pallas_call | solution.py:194
  33.1 1.4 %collective-permute-done.8.refs_2_ = bf16[192,512]{1,0:T(8,128)(2,1)S(1)} collective-permute-done((bf16[192,512]{1,0:T(8,128)(2,1)S(1)}, bf16[192,512]{1,0:T(8,128)(2,1)S(1)}, u32[]{:S(2)}, u32[]{:S(2)}) %collective-permute-start.8) | collective-permute-done | bytes 196640 | tf_op jit(solution)/shard_map/ppermute | solution.py:339
  34.5 1.6 %collective-permute-start.13 = (bf16[208,512]{1,0:T(8,128)(2,1)S(1)}, bf16[208,512]{1,0:T(8,128)(2,1)S(1)}, u32[]{:S(2)}, u32[]{:S(2)}) collective-permute-start(bf16[208,512]{1,0:T(8,128)(2,1)S(1)} %collective-permute-done.10.refs_5_), channel_id=1, source_target_pairs={{0,4},{2,6},{8,0},{10,2},{16,8},{18,10},{24,16},{26,18},{28,24},{3... | collective-permute-start | bytes 638984 | tf_op jit(solution)/shard_map/ppermute | solution.py:340
  36.1 0.4 collective-permute-start.12
  36.5 2.3 %collective-permute-done.14.refs_3_ = bf16[208,512]{1,0:T(8,128)(2,1)S(1)} collective-permute-done((bf16[208,512]{1,0:T(8,128)(2,1)S(1)}, bf16[208,512]{1,0:T(8,128)(2,1)S(1)}, u32[]{:S(2)}, u32[]{:S(2)}) %collective-permute-start.14) | collective-permute-done | bytes 213024 | tf_op jit(solution)/shard_map/ppermute | solution.py:339
  38.8 3.3 %attend.6 = (f32[8,1,480]{2,1,0:T(1,128)S(1)}, f32[8,144,480]{2,1,0:T(8,128)S(1)}) custom-call(bf16[8,128,480]{2,1,0:T(8,128)(2,1)S(1)} %turn.1.refs_0_, bf16[208,512]{1,0:T(8,128)(2,1)S(1)} %maximum_maximum_fusion.refs_1_.refs_3_, bf16[192,512]{1,0:T(8,128)(2,1)S(1)} %collective-permute-done.8.refs_2_, ...), custom_call_target="tpu_custom_call" | custom-call | flops 754974720 | bytes 4194304 | tf_op jit(solution)/shard_map/attend/pallas_call | solution.py:194
  42.1 0.0 collective-permute-done.12.refs_2_
  42.1 0.0 collective-permute-done.13.refs_3_
  42.1 4.6 %attend.7 = (bf16[192,1280]{1,0:T(8,128)(2,1)S(1)}, bf16[192,1280]{1,0:T(8,128)(2,1)S(1)}, bf16[2560,1280]{1,0:T(8,128)(2,1)S(1)}) custom-call(bf16[8,128,480]{2,1,0:T(8,128)(2,1)S(1)} %turn.1.refs_0_, bf16[208,512]{1,0:T(8,128)(2,1)S(1)} %maximum_maximum_fusion.refs_1_.refs_3_, bf16[192,512]{1,0:T(8,128)(2,1)S(1)} %collective-permute-done.12.refs_2_, ...), custom_call_target="tpu_custom_call" | custom-call | flops 377487360 | bytes 4194304 | tf_op jit(solution)/shard_map/attend/pallas_call | solution.py:194
  46.8 0.1 collective-permute-start.16
  46.8 1.9 %collective-permute-done.16.other_ref = bf16[192,1280]{1,0:T(8,128)(2,1)S(1)} collective-permute-done((bf16[192,1280]{1,0:T(8,128)(2,1)S(1)}, bf16[192,1280]{1,0:T(8,128)(2,1)S(1)}, u32[]{:S(2)}, u32[]{:S(2)}) %collective-permute-start.16) | collective-permute-done | bytes 491552 | tf_op jit(solution)/shard_map/ppermute | solution.py:388
  48.7 3.0 %project.4 = (bf16[96,1280]{1,0:T(8,128)(2,1)S(1)}, bf16[96,1280]{1,0:T(8,128)(2,1)S(1)}, bf16[2560,1280]{1,0:T(8,128)(2,1)S(1)}) custom-call(bf16[192,1280]{1,0:T(8,128)(2,1)S(1)} %get-tuple-element.75.own_ref, bf16[192,1280]{1,0:T(8,128)(2,1)S(1)} %collective-permute-done.16.other_ref, bf16[2560,1280]{1,0:T(8,128)(2,1)S(1)} %get-tuple-element.64.held_ref, ...), custom_call_target="tpu_custom_call" | custom-call | flops 1258291200 | bytes 6553600 | tf_op jit(solution)/shard_map/project/pallas_call | solution.py:273
  51.7 1.6 %collective-permute-start.17 = (bf16[96,1280]{1,0:T(8,128)(2,1)S(1)}, bf16[96,1280]{1,0:T(8,128)(2,1)S(1)}, u32[]{:S(2)}, u32[]{:S(2)}) collective-permute-start(bf16[96,1280]{1,0:T(8,128)(2,1)S(1)} %get-tuple-element.66), channel_id=1, source_target_pairs={{0,1},{1,0},{2,3},{3,2},{4,5},{5,4},{6,7},{7,6},{8,9},{9,8},{10,11... | collective-permute-start | bytes 737288 | tf_op jit(solution)/shard_map/ppermute | solution.py:440
  53.3 3.4 %project.5 = (bf16[96,1280]{1,0:T(8,128)(2,1)S(1)}, bf16[96,1280]{1,0:T(8,128)(2,1)S(1)}, bf16[2560,1536]{1,0:T(8,128)(2,1)S(1)}) custom-call(bf16[192,1280]{1,0:T(8,128)(2,1)S(1)} %get-tuple-element.75.own_ref, bf16[192,1280]{1,0:T(8,128)(2,1)S(1)} %collective-permute-done.16.other_ref, bf16[2560,1280]{1,0:T(8,128)(2,1)S(1)} %get-tuple-element.68.held_ref, ...), custom_call_target="tpu_custom_call" | custom-call | flops 1258291200 | bytes 6553600 | tf_op jit(solution)/shard_map/project/pallas_call | solution.py:273
  56.7 0.6 collective-permute-start.18
  57.3 2.9 %collective-permute-done.17 = bf16[96,1280]{1,0:T(8,128)(2,1)S(1)} collective-permute-done((bf16[96,1280]{1,0:T(8,128)(2,1)S(1)}, bf16[96,1280]{1,0:T(8,128)(2,1)S(1)}, u32[]{:S(2)}, u32[]{:S(2)}) %collective-permute-start.17) | collective-permute-done | bytes 245792 | tf_op jit(solution)/shard_map/ppermute | solution.py:440
  60.3 3.1 %project.6 = (bf16[96,1536]{1,0:T(8,128)(2,1)S(1)}, bf16[96,1536]{1,0:T(8,128)(2,1)S(1)}, bf16[2560,1024]{1,0:T(8,128)(2,1)S(1)}) custom-call(bf16[192,1280]{1,0:T(8,128)(2,1)S(1)} %get-tuple-element.75.own_ref, bf16[192,1280]{1,0:T(8,128)(2,1)S(1)} %collective-permute-done.16.other_ref, bf16[2560,1536]{1,0:T(8,128)(2,1)S(1)} %get-tuple-element.72.held_ref, ...), custom_call_target="tpu_custom_call" | custom-call | flops 1509949440 | bytes 7864320 | tf_op jit(solution)/shard_map/project/pallas_call | solution.py:273
  63.4 1.9 %collective-permute-start.19 = (bf16[96,1536]{1,0:T(8,128)(2,1)S(1)}, bf16[96,1536]{1,0:T(8,128)(2,1)S(1)}, u32[]{:S(2)}, u32[]{:S(2)}) collective-permute-start(bf16[96,1536]{1,0:T(8,128)(2,1)S(1)} %get-tuple-element.74), channel_id=1, source_target_pairs={{0,1},{1,0},{2,3},{3,2},{4,5},{5,4},{6,7},{7,6},{8,9},{9,8},{10,11... | collective-permute-start | bytes 884744 | tf_op jit(solution)/shard_map/ppermute | solution.py:440
  65.3 1.2 %project.7 = (bf16[96,1024]{1,0:T(8,128)(2,1)S(1)}, bf16[96,1024]{1,0:T(8,128)(2,1)S(1)}) custom-call(bf16[192,1280]{1,0:T(8,128)(2,1)S(1)} %get-tuple-element.75.own_ref, bf16[192,1280]{1,0:T(8,128)(2,1)S(1)} %collective-permute-done.16.other_ref, bf16[2560,1024]{1,0:T(8,128)(2,1)S(1)} %get-tuple-element.76.held_ref), custom_call_target="tpu_custom_call" | custom-call | flops 1006632960 | bytes 5242880 | tf_op jit(solution)/shard_map/project/pallas_call | solution.py:273
  66.5 1.5 %collective-permute-start.20 = (bf16[96,1024]{1,0:T(8,128)(2,1)S(1)}, bf16[96,1024]{1,0:T(8,128)(2,1)S(1)}, u32[]{:S(2)}, u32[]{:S(2)}) collective-permute-start(bf16[96,1024]{1,0:T(8,128)(2,1)S(1)} %get-tuple-element.78), channel_id=1, source_target_pairs={{0,1},{1,0},{2,3},{3,2},{4,5},{5,4},{6,7},{7,6},{8,9},{9,8},{10,11... | collective-permute-start | bytes 589832 | tf_op jit(solution)/shard_map/ppermute | solution.py:440
  68.0 7.6 %collective-permute-done.20 = bf16[96,1024]{1,0:T(8,128)(2,1)S(1)} collective-permute-done((bf16[96,1024]{1,0:T(8,128)(2,1)S(1)}, bf16[96,1024]{1,0:T(8,128)(2,1)S(1)}, u32[]{:S(2)}, u32[]{:S(2)}) %collective-permute-start.20) | collective-permute-done | bytes 196640 | tf_op jit(solution)/shard_map/ppermute | solution.py:440
  75.6 0.0 collective-permute-done.19
  75.6 1.2 %add_convert_fusion = bf16[96,5120]{1,0:T(8,128)(2,1)} fusion(bf16[96,1024]{1,0:T(8,128)(2,1)S(1)} %get-tuple-element.77, bf16[96,1536]{1,0:T(8,128)(2,1)S(1)} %get-tuple-element.73, bf16[96,1280]{1,0:T(8,128)(2,1)S(1)} %get-tuple-element.69, bf16[96,1280]{1,0:T(8,128)(2,1)S(1)} %get-tuple-element.65, bf16[96,1024]{1,0:T(8,128)(2,1)S(1)} %collective-permute-done.20, ...), kind=kLoop, calls=%fused_computation | loop fusion | flops 8847360 | bytes 2949120 | tf_op jit(solution)/shard_map/convert_element_type | solution.py:443
  (11 shorter events, 0.1 us)
Async XLA Ops:
  0.0 14.1 %copy-start = (bf16[192,2560]{1,0:T(8,128)(2,1)S(1)}, bf16[192,2560]{1,0:T(8,128)(2,1)}, u32[]{:S(2)}) copy-start(bf16[192,2560]{1,0:T(8,128)(2,1)} %refs_0_.4) | copy-start | bytes 2949124
  1.2 1.7 %collective-permute-start.3 = (bf16[208,512]{1,0:T(8,128)(2,1)S(1)}, bf16[208,512]{1,0:T(8,128)(2,1)S(1)}, u32[]{:S(2)}, u32[]{:S(2)}) collective-permute-start(bf16[208,512]{1,0:T(8,128)(2,1)S(1)} %get-tuple-element.44), channel_id=1, source_target_pairs={{0,2},{2,0},{4,6},{6,4},{8,10},{10,8},{12,14},{14,12},{16,18},{18,... | collective-permute-start | bytes 638984 | tf_op jit(solution)/shard_map/ppermute | solution.py:343
  2.8 11.3 %collective-permute-start.2 = (bf16[192,1280]{1,0:T(8,128)(2,1)S(1)}, bf16[192,1280]{1,0:T(8,128)(2,1)S(1)}, u32[]{:S(2)}, u32[]{:S(2)}) collective-permute-start(bf16[192,1280]{1,0:T(8,128)(2,1)S(1)} %constant_dynamic-slice_fusion), channel_id=1, source_target_pairs={{0,2},{2,0},{4,6},{6,4},{8,10},{10,8},{12,14},{14,12},{16,18},{18,... | collective-permute-start | bytes 1474568 | tf_op jit(solution)/shard_map/ppermute | solution.py:350
  2.9 9.1 %collective-permute-start.7 = (bf16[208,512]{1,0:T(8,128)(2,1)S(1)}, bf16[208,512]{1,0:T(8,128)(2,1)S(1)}, u32[]{:S(2)}, u32[]{:S(2)}) collective-permute-start(bf16[208,512]{1,0:T(8,128)(2,1)S(1)} %maximum_maximum_fusion.refs_1_.refs_3_), channel_id=1, source_target_pairs={{0,4},{2,6},{8,0},{10,2},{16,8},{18,10},{24,16},{26,18},{28,24},{3... | collective-permute-start | bytes 638984 | tf_op jit(solution)/shard_map/ppermute | solution.py:340
  5.9 10.3 %collective-permute-start.1 = (bf16[192,512]{1,0:T(8,128)(2,1)S(1)}, bf16[192,512]{1,0:T(8,128)(2,1)S(1)}, u32[]{:S(2)}, u32[]{:S(2)}) collective-permute-start(bf16[192,512]{1,0:T(8,128)(2,1)S(1)} %get-tuple-element.42.refs_2_), channel_id=1, source_target_pairs={{0,4},{2,6},{8,0},{10,2},{16,8},{18,10},{24,16},{26,18},{28,24},{3... | collective-permute-start | bytes 589832 | tf_op jit(solution)/shard_map/ppermute | solution.py:340
  7.5 8.8 %collective-permute-start = (bf16[192,512]{1,0:T(8,128)(2,1)S(1)}, bf16[192,512]{1,0:T(8,128)(2,1)S(1)}, u32[]{:S(2)}, u32[]{:S(2)}) collective-permute-start(bf16[192,512]{1,0:T(8,128)(2,1)S(1)} %get-tuple-element.42.refs_2_), channel_id=1, source_target_pairs={{0,8},{2,10},{8,16},{10,18},{16,24},{18,26},{24,28},{26,30},{28,20... | collective-permute-start | bytes 589832 | tf_op jit(solution)/shard_map/ppermute | solution.py:339
  8.0 10.9 %collective-permute-start.6 = (bf16[208,512]{1,0:T(8,128)(2,1)S(1)}, bf16[208,512]{1,0:T(8,128)(2,1)S(1)}, u32[]{:S(2)}, u32[]{:S(2)}) collective-permute-start(bf16[208,512]{1,0:T(8,128)(2,1)S(1)} %maximum_maximum_fusion.refs_1_.refs_3_), channel_id=1, source_target_pairs={{0,8},{2,10},{8,16},{10,18},{16,24},{18,26},{24,28},{26,30},{28,20... | collective-permute-start | bytes 638984 | tf_op jit(solution)/shard_map/ppermute | solution.py:339
  12.1 8.8 %collective-permute-start.9 = (bf16[208,512]{1,0:T(8,128)(2,1)S(1)}, bf16[208,512]{1,0:T(8,128)(2,1)S(1)}, u32[]{:S(2)}, u32[]{:S(2)}) collective-permute-start(bf16[208,512]{1,0:T(8,128)(2,1)S(1)} %collective-permute-done.7.refs_7_), channel_id=1, source_target_pairs={{0,4},{2,6},{8,0},{10,2},{16,8},{18,10},{24,16},{26,18},{28,24},{3... | collective-permute-start | bytes 638984 | tf_op jit(solution)/shard_map/ppermute | solution.py:340
  16.3 11.0 %collective-permute-start.4 = (bf16[192,512]{1,0:T(8,128)(2,1)S(1)}, bf16[192,512]{1,0:T(8,128)(2,1)S(1)}, u32[]{:S(2)}, u32[]{:S(2)}) collective-permute-start(bf16[192,512]{1,0:T(8,128)(2,1)S(1)} %collective-permute-done.refs_4_), channel_id=1, source_target_pairs={{0,8},{2,10},{8,16},{10,18},{16,24},{18,26},{24,28},{26,30},{28,20... | collective-permute-start | bytes 589832 | tf_op jit(solution)/shard_map/ppermute | solution.py:339
  18.3 8.9 %collective-permute-start.5 = (bf16[192,512]{1,0:T(8,128)(2,1)S(1)}, bf16[192,512]{1,0:T(8,128)(2,1)S(1)}, u32[]{:S(2)}, u32[]{:S(2)}) collective-permute-start(bf16[192,512]{1,0:T(8,128)(2,1)S(1)} %collective-permute-done.1.refs_6_), channel_id=1, source_target_pairs={{0,4},{2,6},{8,0},{10,2},{16,8},{18,10},{24,16},{26,18},{28,24},{3... | collective-permute-start | bytes 589832 | tf_op jit(solution)/shard_map/ppermute | solution.py:340
  18.9 8.9 %collective-permute-start.11 = (bf16[208,512]{1,0:T(8,128)(2,1)S(1)}, bf16[208,512]{1,0:T(8,128)(2,1)S(1)}, u32[]{:S(2)}, u32[]{:S(2)}) collective-permute-start(bf16[208,512]{1,0:T(8,128)(2,1)S(1)} %collective-permute-done.6.refs_5_), channel_id=1, source_target_pairs={{0,8},{2,10},{8,16},{10,18},{16,24},{18,26},{24,28},{26,30},{28,20... | collective-permute-start | bytes 638984 | tf_op jit(solution)/shard_map/ppermute | solution.py:339
  20.8 12.3 %collective-permute-start.10 = (bf16[208,512]{1,0:T(8,128)(2,1)S(1)}, bf16[208,512]{1,0:T(8,128)(2,1)S(1)}, u32[]{:S(2)}, u32[]{:S(2)}) collective-permute-start(bf16[208,512]{1,0:T(8,128)(2,1)S(1)} %collective-permute-done.9.refs_5_), channel_id=1, source_target_pairs={{0,4},{2,6},{8,0},{10,2},{16,8},{18,10},{24,16},{26,18},{28,24},{3... | collective-permute-start | bytes 638984 | tf_op jit(solution)/shard_map/ppermute | solution.py:340
  27.3 7.2 %collective-permute-start.8 = (bf16[192,512]{1,0:T(8,128)(2,1)S(1)}, bf16[192,512]{1,0:T(8,128)(2,1)S(1)}, u32[]{:S(2)}, u32[]{:S(2)}) collective-permute-start(bf16[192,512]{1,0:T(8,128)(2,1)S(1)} %collective-permute-done.4.refs_2_), channel_id=1, source_target_pairs={{0,8},{2,10},{8,16},{10,18},{16,24},{18,26},{24,28},{26,30},{28,20... | collective-permute-start | bytes 589832 | tf_op jit(solution)/shard_map/ppermute | solution.py:339
  27.8 11.1 %collective-permute-start.14 = (bf16[208,512]{1,0:T(8,128)(2,1)S(1)}, bf16[208,512]{1,0:T(8,128)(2,1)S(1)}, u32[]{:S(2)}, u32[]{:S(2)}) collective-permute-start(bf16[208,512]{1,0:T(8,128)(2,1)S(1)} %collective-permute-done.11.refs_3_), channel_id=1, source_target_pairs={{0,8},{2,10},{8,16},{10,18},{16,24},{18,26},{24,28},{26,30},{28,20... | collective-permute-start | bytes 638984 | tf_op jit(solution)/shard_map/ppermute | solution.py:339
  29.4 9.4 %collective-permute-start.15 = (bf16[192,512]{1,0:T(8,128)(2,1)S(1)}, bf16[192,512]{1,0:T(8,128)(2,1)S(1)}, u32[]{:S(2)}, u32[]{:S(2)}) collective-permute-start(bf16[192,512]{1,0:T(8,128)(2,1)S(1)} %collective-permute-done.5.refs_4_), channel_id=1, source_target_pairs={{0,4},{2,6},{8,0},{10,2},{16,8},{18,10},{24,16},{26,18},{28,24},{3... | collective-permute-start | bytes 589832 | tf_op jit(solution)/shard_map/ppermute | solution.py:340
  34.5 7.6 %collective-permute-start.13 = (bf16[208,512]{1,0:T(8,128)(2,1)S(1)}, bf16[208,512]{1,0:T(8,128)(2,1)S(1)}, u32[]{:S(2)}, u32[]{:S(2)}) collective-permute-start(bf16[208,512]{1,0:T(8,128)(2,1)S(1)} %collective-permute-done.10.refs_5_), channel_id=1, source_target_pairs={{0,4},{2,6},{8,0},{10,2},{16,8},{18,10},{24,16},{26,18},{28,24},{3... | collective-permute-start | bytes 638984 | tf_op jit(solution)/shard_map/ppermute | solution.py:340
  36.1 6.0 %collective-permute-start.12 = (bf16[192,512]{1,0:T(8,128)(2,1)S(1)}, bf16[192,512]{1,0:T(8,128)(2,1)S(1)}, u32[]{:S(2)}, u32[]{:S(2)}) collective-permute-start(bf16[192,512]{1,0:T(8,128)(2,1)S(1)} %collective-permute-done.8.refs_2_), channel_id=1, source_target_pairs={{0,8},{2,10},{8,16},{10,18},{16,24},{18,26},{24,28},{26,30},{28,20... | collective-permute-start | bytes 589832 | tf_op jit(solution)/shard_map/ppermute | solution.py:339
  46.8 1.9 %collective-permute-start.16 = (bf16[192,1280]{1,0:T(8,128)(2,1)S(1)}, bf16[192,1280]{1,0:T(8,128)(2,1)S(1)}, u32[]{:S(2)}, u32[]{:S(2)}) collective-permute-start(bf16[192,1280]{1,0:T(8,128)(2,1)S(1)} %get-tuple-element.63), channel_id=1, source_target_pairs={{0,2},{2,0},{4,6},{6,4},{8,10},{10,8},{12,14},{14,12},{16,18},{18,... | collective-permute-start | bytes 1474568 | tf_op jit(solution)/shard_map/ppermute | solution.py:388
  51.7 8.5 %collective-permute-start.17 = (bf16[96,1280]{1,0:T(8,128)(2,1)S(1)}, bf16[96,1280]{1,0:T(8,128)(2,1)S(1)}, u32[]{:S(2)}, u32[]{:S(2)}) collective-permute-start(bf16[96,1280]{1,0:T(8,128)(2,1)S(1)} %get-tuple-element.66), channel_id=1, source_target_pairs={{0,1},{1,0},{2,3},{3,2},{4,5},{5,4},{6,7},{7,6},{8,9},{9,8},{10,11... | collective-permute-start | bytes 737288 | tf_op jit(solution)/shard_map/ppermute | solution.py:440
  56.7 8.5 %collective-permute-start.18 = (bf16[96,1280]{1,0:T(8,128)(2,1)S(1)}, bf16[96,1280]{1,0:T(8,128)(2,1)S(1)}, u32[]{:S(2)}, u32[]{:S(2)}) collective-permute-start(bf16[96,1280]{1,0:T(8,128)(2,1)S(1)} %get-tuple-element.70), channel_id=1, source_target_pairs={{0,1},{1,0},{2,3},{3,2},{4,5},{5,4},{6,7},{7,6},{8,9},{9,8},{10,11... | collective-permute-start | bytes 737288 | tf_op jit(solution)/shard_map/ppermute | solution.py:440
  63.4 12.2 %collective-permute-start.19 = (bf16[96,1536]{1,0:T(8,128)(2,1)S(1)}, bf16[96,1536]{1,0:T(8,128)(2,1)S(1)}, u32[]{:S(2)}, u32[]{:S(2)}) collective-permute-start(bf16[96,1536]{1,0:T(8,128)(2,1)S(1)} %get-tuple-element.74), channel_id=1, source_target_pairs={{0,1},{1,0},{2,3},{3,2},{4,5},{5,4},{6,7},{7,6},{8,9},{9,8},{10,11... | collective-permute-start | bytes 884744 | tf_op jit(solution)/shard_map/ppermute | solution.py:440
  66.5 9.1 %collective-permute-start.20 = (bf16[96,1024]{1,0:T(8,128)(2,1)S(1)}, bf16[96,1024]{1,0:T(8,128)(2,1)S(1)}, u32[]{:S(2)}, u32[]{:S(2)}) collective-permute-start(bf16[96,1024]{1,0:T(8,128)(2,1)S(1)} %get-tuple-element.78), channel_id=1, source_target_pairs={{0,1},{1,0},{2,3},{3,2},{4,5},{5,4},{6,7},{7,6},{8,9},{9,8},{10,11... | collective-permute-start | bytes 589832 | tf_op jit(solution)/shard_map/ppermute | solution.py:440

commit v7 on v6

--- a/solution.py
+++ b/solution.py
@@ -51,14 +51,15 @@
     return jnp.concatenate([jnp.transpose(v), jnp.ones((HEADER, v.shape[0]), v.dtype)], axis=0)
 
 
-def fetch_columns(w_ref, first, held_ref, sems):
-    pieces = sems.shape[0]
-    depth, width = held_ref.shape[0] // pieces, held_ref.shape[1]
+def fetch_columns(w_ref, first, held_ref, sems, sem):
+    depth, width = held_ref.shape[0] // PIECES, held_ref.shape[1]
     copies = []
-    for p in range(pieces):
+    for p in range(PIECES):
         at = pl.ds(p * depth, depth)
         copies.append(
-            pltpu.make_async_copy(w_ref.at[at, pl.ds(first, width)], held_ref.at[at], sems.at[p])
+            pltpu.make_async_copy(
+                w_ref.at[at, pl.ds(first, width)], held_ref.at[at], sems.at[sem + p]
+            )
         )
         copies[-1].start()
     return copies
@@ -77,9 +78,12 @@
         w_ref = refs.pop(0)
     if plan["last"]:
         out_refs = [refs.pop(0) for _ in range(owners)]
+    copies = []
     if fetch:
-        held_ref, sems = (refs.pop(0) if plan["last"] else refs.pop(2)), refs.pop()
-        copies = fetch_columns(w_ref, fetch[0], held_ref, sems)
+        sems = refs.pop()
+        for n, (first, _) in enumerate(fetch):
+            held_ref = refs.pop(0 if plan["last"] else 2)
+            copies += fetch_columns(w_ref, first, held_ref, sems, n * PIECES)
     high_ref, sums_ref = refs
 
     sources = mark_refs + packets
@@ -165,9 +169,8 @@
                                 side * chunk : (side + 1) * chunk,
                                 h * GROUP + g * HEAD_WIDTH : h * GROUP + (g + 1) * HEAD_WIDTH,
                             ] = mixed[g * chunk : (g + 1) * chunk]
-    if fetch:
-        for copy in copies:
-            copy.wait()
+    for copy in copies:
+        copy.wait()
 
 
 def attend(plan, turned, marks, packets, state, out_weight=None):
@@ -188,8 +191,9 @@
     scratch = [pltpu.VMEM(shape, jnp.float32) for shape in kept] if plan["last"] else []
     if fetch:
         in_specs.append(pl.BlockSpec(memory_space=pltpu.HBM))
-        out_shape.append(jax.ShapeDtypeStruct((out_weight.shape[0], fetch[1]), out_weight.dtype))
-        scratch.append(pltpu.SemaphoreType.DMA((PIECES,)))
+        for _, columns in fetch:
+            out_shape.append(jax.ShapeDtypeStruct((out_weight.shape[0], columns), out_weight.dtype))
+        scratch.append(pltpu.SemaphoreType.DMA((PIECES * len(fetch),)))
     flops = 4 * owners * heads * rows * HEAD_WIDTH * count * chunk * 2
     return pl.pallas_call(
         functools.partial(attend_kernel, plan),
@@ -239,7 +243,7 @@
 def project_kernel(following, own_ref, other_ref, held_ref, *refs):
     if following:
         w_ref, sent_ref, kept_ref, next_ref, rows_ref, sems = refs
-        copies = fetch_columns(w_ref, following[0], next_ref, sems)
+        copies = fetch_columns(w_ref, following[0], next_ref, sems, 0)
     else:
         sent_ref, kept_ref, rows_ref = refs
     chunk, part = sent_ref.shape[0], own_ref.shape[1]
@@ -350,7 +354,7 @@
     q_got = lax.ppermute(q_sent, "blk", sibling)
     turned = turn(heads, chunk, (True, False), [queries, q_got])
 
-    def call(pairs, state, own, last=False):
+    def call(pairs, state, own=False, last=False, fetch=None):
         each = range(len(pairs))
         plan = dict(
             heads=heads,
@@ -362,30 +366,27 @@
             members=[(2 * j + i, 0) for j in each for i in range(2)],
             headers=[(2 + 2 * j, rows, i * width) for j in each for i in range(2)],
             owner_headers=[(0, rows, 0), (0, rows, width)],
-            fetch=fetch if last else None,
+            fetch=fetch,
         )
         packets = [packet for pair in pairs for packet in pair]
         return attend(plan, turned, [y], packets, state, out_weight)
 
-    state = None
     ups = downs = (x, y)
-    arrived = [(x, y)]
     for r in range(1, half):
         (x_up, y_up), (x_down, y_down) = ups, downs
-        if r == 2:
-            x_up, x_down, turned = lax.optimization_barrier((x_up, x_down, turned))
-        elif r > 2:
-            x_up, x_down, *state = lax.optimization_barrier((x_up, x_down, *state))
+        if r > 1:
+            y_up, y_down, *state = lax.optimization_barrier((y_up, y_down, *state))
         ups, downs = (up(x_up), up(y_up)), (down(x_down), down(y_down))
-        if r >= 2:
-            state = call(arrived, state, r == 2)
-            arrived = []
-        arrived += [ups, downs]
+        if r == 1:
+            *state, first, second = call([(x, y)], None, own=True, fetch=fetch)
+        else:
+            state = call(arrived, state)
+        arrived = [ups, downs]
     x_up, y_down, *state = lax.optimization_barrier((ups[0], downs[1], *state))
     far = (up(x_up), down(y_down))
-    state = call(arrived, state, False)
-    own, theirs, held = call([far], state, False, True)
-    return own, lax.ppermute(theirs, "blk", sibling), held
+    state = call(arrived, state)
+    own, theirs = call([far], state, last=True)
+    return own, lax.ppermute(theirs, "blk", sibling), [first, second]
 
 
 def one_head_a_device(count, queries, keys, values, positions):
@@ -427,16 +428,15 @@
     widths = [out_weight.shape[1] * share // sum(shares) for share in shares]
     cuts = [(sum(widths[:j]), columns) for j, columns in enumerate(widths)]
     own, other, held = split_over_cores(
-        count, queries, keys, values, positions, out_weight, cuts[0]
+        count, queries, keys, values, positions, out_weight, cuts[:2]
     )
     received, kept, source = [], [], own
     for j in range(len(cuts)):
         if j > 0:
             source = after(own, sent, *received[: j - 1][-1:])
-        following = cuts[j + 1] if j + 1 < len(cuts) else None
-        sent, keep, *rest = project(source, other, held, out_weight, following)
-        if rest:
-            held = rest[0]
+        following = cuts[j + 1] if 0 < j < len(cuts) - 1 else None
+        sent, keep, *rest = project(source, other, held[j], out_weight, following)
+        held += rest
         received.append(lax.ppermute(sent, "inner", [(0, 1), (1, 0)]))
         kept.append(keep)
     mine, theirs = jnp.concatenate(kept, axis=1), jnp.concatenate(received, axis=1)

time: 77 us -> 72.3 us (0.939)
  waiting for transfers between devices: 23 us -> 18.9 us
  starting transfers between devices: 23.4 us -> 21.3 us
  Pallas kernels: 27.9 us -> 29.4 us
    ppermute x7, starting transfers between devices: 10.5 us -> 0.18 us  [split_over_cores(): down = lambda x: lax.ppermute(x, 'blk', counter)]
    ppermute x7, starting transfers between devices: 6.68 us -> 14.9 us  [split_over_cores(): up = lambda x: lax.ppermute(x, 'blk', clock)]
    ppermute x7, waiting for transfers between devices: 4.24 us -> 1.14 us  [split_over_cores(): up = lambda x: lax.ppermute(x, 'blk', clock)]
    pallas_call x4 -> x5, Pallas kernels: 15.6 us -> 18.7 us  [attend(): pl.pallas_call(functools.partial(attend_kernel, plan), out_shape=out_shap...]
    pallas_call x4, Pallas kernels: 10.8 us -> 9.17 us  [project(): pl.pallas_call(functools.partial(project_kernel, following), out_shape=ou...]
    ppermute x7, waiting for transfers between devices: 6.31 us -> 5.35 us  [split_over_cores(): down = lambda x: lax.ppermute(x, 'blk', counter)]
  transfers between devices with their start and end apart: 21 -> 21, of which waited for: 9 -> 8; matrix products, arithmetic and copies ran while one was open for 1% -> 2% of each run, Pallas kernels for 25% -> 34%
where the time goes in v7:
time: 72.3 us; the launch traced here: 72.2 us
  Pallas kernels  29.4 us (41%)
  starting transfers between devices  21.3 us (29%)
  waiting for transfers between devices  18.9 us (26%)
  other arithmetic  1.21 us (2%)
  local copies, waits for them, and re-layouts  1.08 us (1%)
    pallas_call x5, Pallas kernels, attend(): pl.pallas_call(functools.partial(attend_kernel, plan), out_shape=out_shap...  18.7 us
    ppermute x7, starting transfers between devices, split_over_cores(): up = lambda x: lax.ppermute(x, 'blk', clock)  14.9 us
    ppermute x4, waiting for transfers between devices, shards(): received.append(lax.ppermute(sent, 'inner', [(0, 1), (1, 0)]))  10.6 us
    pallas_call x4, Pallas kernels, project(): pl.pallas_call(functools.partial(project_kernel, following), out_shape=ou...  9.17 us
    ppermute x4, starting transfers between devices, shards(): received.append(lax.ppermute(sent, 'inner', [(0, 1), (1, 0)]))  5.51 us
    ppermute x7, waiting for transfers between devices, split_over_cores(): down = lambda x: lax.ppermute(x, 'blk', counter)  5.35 us
    ppermute x1, waiting for transfers between devices, split_over_cores(): return (own, lax.ppermute(theirs, 'blk', sibling), [first, second])  1.85 us
  transfers between devices with their start and end apart: 21, of which 8 were waited for; matrix products, arithmetic and copies ran while one was open for 2% of the time, Pallas kernels for 34%

profile of v7, /device:TPU:0, one launch (start us, length us, event | category | flops | bytes accessed | tf_op | source)
XLA Modules:
  0.0 72.2 jit_solution(9670209886864638204)
XLA Ops:
  0.0 1.2 %prepare.1 = (bf16[208,512]{1,0:T(8,128)(2,1)S(1)}, bf16[192,512]{1,0:T(8,128)(2,1)S(1)}, bf16[16,256]{1,0:T(8,128)(2,1)S(1)}) custom-call(bf16[192,512]{1,0:T(8,128)(2,1)} %k_ref.1, bf16[192,512]{1,0:T(8,128)(2,1)} %v_ref.1, s32[192]{0:T(256)} %position_ref.1), custom_call_target="tpu_custom_call" | custom-call | tf_op jit(solution)/shard_map/prepare/pallas_call | solution.py:314
  1.2 0.5 collective-permute-start.1
  1.7 1.1 %constant_dynamic-slice_fusion = bf16[192,1280]{1,0:T(8,128)(2,1)S(1)} fusion(bf16[192,2560]{1,0:T(8,128)(2,1)} %refs_0_.3, s32[]{:T(128)S(6)} %select_n.3), kind=kLoop, calls=%fused_computation.2 | loop fusion | bytes 983044 | tf_op jit(solution)/shard_map/dynamic_slice | solution.py:351
  2.8 0.1 collective-permute-start
  2.9 0.0 collective-permute-done.1
  2.9 3.1 %collective-permute-start.5 = (bf16[208,512]{1,0:T(8,128)(2,1)S(1)}, bf16[208,512]{1,0:T(8,128)(2,1)S(1)}, u32[]{:S(2)}, u32[]{:S(2)}) collective-permute-start(bf16[208,512]{1,0:T(8,128)(2,1)S(1)} %maximum_maximum_fusion.refs_1_.refs_3_), channel_id=1, source_target_pairs={{0,8},{2,10},{8,16},{10,18},{16,24},{18,26},{24,28},{26,30},{28,20... | collective-permute-start | bytes 638984 | tf_op jit(solution)/shard_map/ppermute | solution.py:343
  6.0 0.0 collective-permute-start.6
  6.0 2.0 %collective-permute-start.2 = (bf16[192,512]{1,0:T(8,128)(2,1)S(1)}, bf16[192,512]{1,0:T(8,128)(2,1)S(1)}, u32[]{:S(2)}, u32[]{:S(2)}) collective-permute-start(bf16[192,512]{1,0:T(8,128)(2,1)S(1)} %get-tuple-element.47.refs_2_), channel_id=1, source_target_pairs={{0,8},{2,10},{8,16},{10,18},{16,24},{18,26},{24,28},{26,30},{28,20... | collective-permute-start | bytes 589832 | tf_op jit(solution)/shard_map/ppermute | solution.py:343
  8.0 0.0 collective-permute-start.9
  8.1 0.3 turn.1.refs_0_
  8.4 6.7 %attend.5 = (f32[8,1,480]{2,1,0:T(1,128)S(1)}, f32[8,144,480]{2,1,0:T(8,128)S(1)}, bf16[2560,1280]{1,0:T(8,128)(2,1)S(1)}, bf16[2560,1280]{1,0:T(8,128)(2,1)S(1)}) custom-call(bf16[8,128,480]{2,1,0:T(8,128)(2,1)S(1)} %turn.1.refs_0_, bf16[208,512]{1,0:T(8,128)(2,1)S(1)} %maximum_maximum_fusion.refs_1_.refs_3_, ...), custom_call_target="tpu_custom_call" | custom-call | flops 377487360 | bytes 4194304 | tf_op jit(solution)/shard_map/attend/pallas_call | solution.py:198
  15.1 0.0 collective-permute-done.5.refs_3_
  15.1 2.1 %collective-permute-start.7 = (bf16[208,512]{1,0:T(8,128)(2,1)S(1)}, bf16[208,512]{1,0:T(8,128)(2,1)S(1)}, u32[]{:S(2)}, u32[]{:S(2)}) collective-permute-start(bf16[208,512]{1,0:T(8,128)(2,1)S(1)} %collective-permute-done.5.refs_3_), channel_id=1, source_target_pairs={{0,8},{2,10},{8,16},{10,18},{16,24},{18,26},{24,28},{26,30},{28,20... | collective-permute-start | bytes 638984 | tf_op jit(solution)/shard_map/ppermute | solution.py:343
  17.2 0.0 collective-permute-start.8
  17.2 0.0 collective-permute-done.2.refs_2_
  17.2 2.0 %collective-permute-start.3 = (bf16[192,512]{1,0:T(8,128)(2,1)S(1)}, bf16[192,512]{1,0:T(8,128)(2,1)S(1)}, u32[]{:S(2)}, u32[]{:S(2)}) collective-permute-start(bf16[192,512]{1,0:T(8,128)(2,1)S(1)} %collective-permute-done.2.refs_2_), channel_id=1, source_target_pairs={{0,8},{2,10},{8,16},{10,18},{16,24},{18,26},{24,28},{26,30},{28,20... | collective-permute-start | bytes 589832 | tf_op jit(solution)/shard_map/ppermute | solution.py:343
  19.2 0.0 collective-permute-done.9.refs_4_
  19.2 0.0 collective-permute-start.11
  19.3 3.3 %attend.6 = (f32[8,1,480]{2,1,0:T(1,128)S(1)}, f32[8,144,480]{2,1,0:T(8,128)S(1)}) custom-call(bf16[8,128,480]{2,1,0:T(8,128)(2,1)S(1)} %turn.1.refs_0_, bf16[208,512]{1,0:T(8,128)(2,1)S(1)} %maximum_maximum_fusion.refs_1_.refs_3_, bf16[192,512]{1,0:T(8,128)(2,1)S(1)} %collective-permute-done.2.refs_2_, bf16[208,512]{1,0:T(8,128)(2,1)S(1)} %collective-permute-done.5.refs_3_, ...), custom_call_target="tpu_custom_call" | custom-call | flops 754974720 | bytes 4194304 | tf_op jit(solution)/shard_map/attend/pallas_call | solution.py:198
  22.6 0.8 %collective-permute-done.7.refs_3_ = bf16[208,512]{1,0:T(8,128)(2,1)S(1)} collective-permute-done((bf16[208,512]{1,0:T(8,128)(2,1)S(1)}, bf16[208,512]{1,0:T(8,128)(2,1)S(1)}, u32[]{:S(2)}, u32[]{:S(2)}) %collective-permute-start.7) | collective-permute-done | bytes 213024 | tf_op jit(solution)/shard_map/ppermute | solution.py:343
  23.4 2.0 %collective-permute-done.8.refs_5_ = bf16[208,512]{1,0:T(8,128)(2,1)S(1)} collective-permute-done((bf16[208,512]{1,0:T(8,128)(2,1)S(1)}, bf16[208,512]{1,0:T(8,128)(2,1)S(1)}, u32[]{:S(2)}, u32[]{:S(2)}) %collective-permute-start.8) | collective-permute-done | bytes 213024 | tf_op jit(solution)/shard_map/ppermute | solution.py:344
  25.4 0.0 collective-permute-start.10
  25.4 0.3 collective-permute-done.3.refs_2_
  25.7 1.7 %collective-permute-start.4 = (bf16[192,512]{1,0:T(8,128)(2,1)S(1)}, bf16[192,512]{1,0:T(8,128)(2,1)S(1)}, u32[]{:S(2)}, u32[]{:S(2)}) collective-permute-start(bf16[192,512]{1,0:T(8,128)(2,1)S(1)} %collective-permute-done.3.refs_2_), channel_id=1, source_target_pairs={{0,8},{2,10},{8,16},{10,18},{16,24},{18,26},{24,28},{26,30},{28,20... | collective-permute-start | bytes 589832 | tf_op jit(solution)/shard_map/ppermute | solution.py:343
  27.5 2.1 %collective-permute-done.11.refs_4_ = bf16[192,512]{1,0:T(8,128)(2,1)S(1)} collective-permute-done((bf16[192,512]{1,0:T(8,128)(2,1)S(1)}, bf16[192,512]{1,0:T(8,128)(2,1)S(1)}, u32[]{:S(2)}, u32[]{:S(2)}) %collective-permute-start.11) | collective-permute-done | bytes 196640 | tf_op jit(solution)/shard_map/ppermute | solution.py:344
  29.6 0.0 collective-permute-start.15
  29.6 2.0 %collective-permute-start.14 = (bf16[208,512]{1,0:T(8,128)(2,1)S(1)}, bf16[208,512]{1,0:T(8,128)(2,1)S(1)}, u32[]{:S(2)}, u32[]{:S(2)}) collective-permute-start(bf16[208,512]{1,0:T(8,128)(2,1)S(1)} %collective-permute-done.7.refs_3_), channel_id=1, source_target_pairs={{0,8},{2,10},{8,16},{10,18},{16,24},{18,26},{24,28},{26,30},{28,20... | collective-permute-start | bytes 638984 | tf_op jit(solution)/shard_map/ppermute | solution.py:343
  31.7 3.3 %attend.7 = (f32[8,1,480]{2,1,0:T(1,128)S(1)}, f32[8,144,480]{2,1,0:T(8,128)S(1)}) custom-call(bf16[8,128,480]{2,1,0:T(8,128)(2,1)S(1)} %turn.1.refs_0_, bf16[208,512]{1,0:T(8,128)(2,1)S(1)} %maximum_maximum_fusion.refs_1_.refs_3_, bf16[192,512]{1,0:T(8,128)(2,1)S(1)} %collective-permute-done.3.refs_2_, bf16[208,512]{1,0:T(8,128)(2,1)S(1)} %collective-permute-done.7.refs_3_, ...), custom_call_target="tpu_custom_call" | custom-call | flops 754974720 | bytes 4194304 | tf_op jit(solution)/shard_map/attend/pallas_call | solution.py:198
  35.0 0.1 collective-permute-start.13
  35.1 2.0 %collective-permute-start.12 = (bf16[192,512]{1,0:T(8,128)(2,1)S(1)}, bf16[192,512]{1,0:T(8,128)(2,1)S(1)}, u32[]{:S(2)}, u32[]{:S(2)}) collective-permute-start(bf16[192,512]{1,0:T(8,128)(2,1)S(1)} %collective-permute-done.4.refs_2_), channel_id=1, source_target_pairs={{0,8},{2,10},{8,16},{10,18},{16,24},{18,26},{24,28},{26,30},{28,20... | collective-permute-start | bytes 589832 | tf_op jit(solution)/shard_map/ppermute | solution.py:343
  37.1 1.2 %collective-permute-done.15.refs_4_ = bf16[192,512]{1,0:T(8,128)(2,1)S(1)} collective-permute-done((bf16[192,512]{1,0:T(8,128)(2,1)S(1)}, bf16[192,512]{1,0:T(8,128)(2,1)S(1)}, u32[]{:S(2)}, u32[]{:S(2)}) %collective-permute-start.15) | collective-permute-done | bytes 196640 | tf_op jit(solution)/shard_map/ppermute | solution.py:344
  38.2 0.0 collective-permute-done.14.refs_3_
  38.2 3.3 %attend.8 = (f32[8,1,480]{2,1,0:T(1,128)S(1)}, f32[8,144,480]{2,1,0:T(8,128)S(1)}) custom-call(bf16[8,128,480]{2,1,0:T(8,128)(2,1)S(1)} %turn.1.refs_0_, bf16[208,512]{1,0:T(8,128)(2,1)S(1)} %maximum_maximum_fusion.refs_1_.refs_3_, bf16[192,512]{1,0:T(8,128)(2,1)S(1)} %collective-permute-done.4.refs_2_, ...), custom_call_target="tpu_custom_call" | custom-call | flops 754974720 | bytes 4194304 | tf_op jit(solution)/shard_map/attend/pallas_call | solution.py:198
  41.6 0.0 collective-permute-done.13.refs_3_
  41.6 2.1 %attend.9 = (bf16[192,1280]{1,0:T(8,128)(2,1)S(1)}, bf16[192,1280]{1,0:T(8,128)(2,1)S(1)}) custom-call(bf16[8,128,480]{2,1,0:T(8,128)(2,1)S(1)} %turn.1.refs_0_, bf16[208,512]{1,0:T(8,128)(2,1)S(1)} %maximum_maximum_fusion.refs_1_.refs_3_, bf16[192,512]{1,0:T(8,128)(2,1)S(1)} %collective-permute-done.12.refs_2_, ...), custom_call_target="tpu_custom_call" | custom-call | flops 377487360 | bytes 4194304 | tf_op jit(solution)/shard_map/attend/pallas_call | solution.py:198
  43.7 0.1 collective-permute-start.16
  43.8 1.9 %collective-permute-done.16.other_ref = bf16[192,1280]{1,0:T(8,128)(2,1)S(1)} collective-permute-done((bf16[192,1280]{1,0:T(8,128)(2,1)S(1)}, bf16[192,1280]{1,0:T(8,128)(2,1)S(1)}, u32[]{:S(2)}, u32[]{:S(2)}) %collective-permute-start.16) | collective-permute-done | bytes 491552 | tf_op jit(solution)/shard_map/ppermute | solution.py:389
  45.6 1.4 %project.4 = (bf16[96,1280]{1,0:T(8,128)(2,1)S(1)}, bf16[96,1280]{1,0:T(8,128)(2,1)S(1)}) custom-call(bf16[192,1280]{1,0:T(8,128)(2,1)S(1)} %get-tuple-element.81.own_ref, bf16[192,1280]{1,0:T(8,128)(2,1)S(1)} %collective-permute-done.16.other_ref, bf16[2560,1280]{1,0:T(8,128)(2,1)S(1)} %get-tuple-element.70.held_ref), custom_call_target="tpu_custom_call" | custom-call | flops 1258291200 | bytes 6553600 | tf_op jit(solution)/shard_map/project/pallas_call | solution.py:277
  47.1 1.6 %collective-permute-start.17 = (bf16[96,1280]{1,0:T(8,128)(2,1)S(1)}, bf16[96,1280]{1,0:T(8,128)(2,1)S(1)}, u32[]{:S(2)}, u32[]{:S(2)}) collective-permute-start(bf16[96,1280]{1,0:T(8,128)(2,1)S(1)} %get-tuple-element.72), channel_id=1, source_target_pairs={{0,1},{1,0},{2,3},{3,2},{4,5},{5,4},{6,7},{7,6},{8,9},{9,8},{10,11... | collective-permute-start | bytes 737288 | tf_op jit(solution)/shard_map/ppermute | solution.py:440
  48.7 3.4 %project.5 = (bf16[96,1280]{1,0:T(8,128)(2,1)S(1)}, bf16[96,1280]{1,0:T(8,128)(2,1)S(1)}, bf16[2560,1536]{1,0:T(8,128)(2,1)S(1)}) custom-call(bf16[192,1280]{1,0:T(8,128)(2,1)S(1)} %get-tuple-element.81.own_ref, bf16[192,1280]{1,0:T(8,128)(2,1)S(1)} %collective-permute-done.16.other_ref, bf16[2560,1280]{1,0:T(8,128)(2,1)S(1)} %get-tuple-element.74.held_ref, ...), custom_call_target="tpu_custom_call" | custom-call | flops 1258291200 | bytes 6553600 | tf_op jit(solution)/shard_map/project/pallas_call | solution.py:277
  52.1 0.6 collective-permute-start.18
  52.7 2.9 %collective-permute-done.17 = bf16[96,1280]{1,0:T(8,128)(2,1)S(1)} collective-permute-done((bf16[96,1280]{1,0:T(8,128)(2,1)S(1)}, bf16[96,1280]{1,0:T(8,128)(2,1)S(1)}, u32[]{:S(2)}, u32[]{:S(2)}) %collective-permute-start.17) | collective-permute-done | bytes 245792 | tf_op jit(solution)/shard_map/ppermute | solution.py:440
  55.6 3.1 %project.6 = (bf16[96,1536]{1,0:T(8,128)(2,1)S(1)}, bf16[96,1536]{1,0:T(8,128)(2,1)S(1)}, bf16[2560,1024]{1,0:T(8,128)(2,1)S(1)}) custom-call(bf16[192,1280]{1,0:T(8,128)(2,1)S(1)} %get-tuple-element.81.own_ref, bf16[192,1280]{1,0:T(8,128)(2,1)S(1)} %collective-permute-done.16.other_ref, bf16[2560,1536]{1,0:T(8,128)(2,1)S(1)} %get-tuple-element.78.held_ref, ...), custom_call_target="tpu_custom_call" | custom-call | flops 1509949440 | bytes 7864320 | tf_op jit(solution)/shard_map/project/pallas_call | solution.py:277
  58.7 1.9 %collective-permute-start.19 = (bf16[96,1536]{1,0:T(8,128)(2,1)S(1)}, bf16[96,1536]{1,0:T(8,128)(2,1)S(1)}, u32[]{:S(2)}, u32[]{:S(2)}) collective-permute-start(bf16[96,1536]{1,0:T(8,128)(2,1)S(1)} %get-tuple-element.80), channel_id=1, source_target_pairs={{0,1},{1,0},{2,3},{3,2},{4,5},{5,4},{6,7},{7,6},{8,9},{9,8},{10,11... | collective-permute-start | bytes 884744 | tf_op jit(solution)/shard_map/ppermute | solution.py:440
  60.6 1.2 %project.7 = (bf16[96,1024]{1,0:T(8,128)(2,1)S(1)}, bf16[96,1024]{1,0:T(8,128)(2,1)S(1)}) custom-call(bf16[192,1280]{1,0:T(8,128)(2,1)S(1)} %get-tuple-element.81.own_ref, bf16[192,1280]{1,0:T(8,128)(2,1)S(1)} %collective-permute-done.16.other_ref, bf16[2560,1024]{1,0:T(8,128)(2,1)S(1)} %get-tuple-element.82.held_ref), custom_call_target="tpu_custom_call" | custom-call | flops 1006632960 | bytes 5242880 | tf_op jit(solution)/shard_map/project/pallas_call | solution.py:277
  61.8 1.5 %collective-permute-start.20 = (bf16[96,1024]{1,0:T(8,128)(2,1)S(1)}, bf16[96,1024]{1,0:T(8,128)(2,1)S(1)}, u32[]{:S(2)}, u32[]{:S(2)}) collective-permute-start(bf16[96,1024]{1,0:T(8,128)(2,1)S(1)} %get-tuple-element.84), channel_id=1, source_target_pairs={{0,1},{1,0},{2,3},{3,2},{4,5},{5,4},{6,7},{7,6},{8,9},{9,8},{10,11... | collective-permute-start | bytes 589832 | tf_op jit(solution)/shard_map/ppermute | solution.py:440
  63.3 7.7 %collective-permute-done.20 = bf16[96,1024]{1,0:T(8,128)(2,1)S(1)} collective-permute-done((bf16[96,1024]{1,0:T(8,128)(2,1)S(1)}, bf16[96,1024]{1,0:T(8,128)(2,1)S(1)}, u32[]{:S(2)}, u32[]{:S(2)}) %collective-permute-start.20) | collective-permute-done | bytes 196640 | tf_op jit(solution)/shard_map/ppermute | solution.py:440
  71.0 1.2 %add_convert_fusion = bf16[96,5120]{1,0:T(8,128)(2,1)} fusion(bf16[96,1024]{1,0:T(8,128)(2,1)S(1)} %get-tuple-element.83, bf16[96,1536]{1,0:T(8,128)(2,1)S(1)} %get-tuple-element.79, bf16[96,1280]{1,0:T(8,128)(2,1)S(1)} %get-tuple-element.75, bf16[96,1280]{1,0:T(8,128)(2,1)S(1)} %get-tuple-element.71, bf16[96,1024]{1,0:T(8,128)(2,1)S(1)} %collective-permute-done.20, ...), kind=kLoop, calls=%fused_computation | loop fusion | flops 8847360 | bytes 2949120 | tf_op jit(solution)/shard_map/convert_element_type | solution.py:443
  (12 shorter events, 0.1 us)
Async XLA Ops:
  0.0 8.1 %copy-start = (bf16[192,2560]{1,0:T(8,128)(2,1)S(1)}, bf16[192,2560]{1,0:T(8,128)(2,1)}, u32[]{:S(2)}) copy-start(bf16[192,2560]{1,0:T(8,128)(2,1)} %refs_0_.3) | copy-start | bytes 2949124
  1.2 1.7 %collective-permute-start.1 = (bf16[208,512]{1,0:T(8,128)(2,1)S(1)}, bf16[208,512]{1,0:T(8,128)(2,1)S(1)}, u32[]{:S(2)}, u32[]{:S(2)}) collective-permute-start(bf16[208,512]{1,0:T(8,128)(2,1)S(1)} %get-tuple-element.45), channel_id=1, source_target_pairs={{0,2},{2,0},{4,6},{6,4},{8,10},{10,8},{12,14},{14,12},{16,18},{18,... | collective-permute-start | bytes 638984 | tf_op jit(solution)/shard_map/ppermute | solution.py:347
  2.8 5.3 %collective-permute-start = (bf16[192,1280]{1,0:T(8,128)(2,1)S(1)}, bf16[192,1280]{1,0:T(8,128)(2,1)S(1)}, u32[]{:S(2)}, u32[]{:S(2)}) collective-permute-start(bf16[192,1280]{1,0:T(8,128)(2,1)S(1)} %constant_dynamic-slice_fusion), channel_id=1, source_target_pairs={{0,2},{2,0},{4,6},{6,4},{8,10},{10,8},{12,14},{14,12},{16,18},{18,... | collective-permute-start | bytes 1474568 | tf_op jit(solution)/shard_map/ppermute | solution.py:354
  2.9 12.2 %collective-permute-start.5 = (bf16[208,512]{1,0:T(8,128)(2,1)S(1)}, bf16[208,512]{1,0:T(8,128)(2,1)S(1)}, u32[]{:S(2)}, u32[]{:S(2)}) collective-permute-start(bf16[208,512]{1,0:T(8,128)(2,1)S(1)} %maximum_maximum_fusion.refs_1_.refs_3_), channel_id=1, source_target_pairs={{0,8},{2,10},{8,16},{10,18},{16,24},{18,26},{24,28},{26,30},{28,20... | collective-permute-start | bytes 638984 | tf_op jit(solution)/shard_map/ppermute | solution.py:343
  6.0 9.1 %collective-permute-start.6 = (bf16[208,512]{1,0:T(8,128)(2,1)S(1)}, bf16[208,512]{1,0:T(8,128)(2,1)S(1)}, u32[]{:S(2)}, u32[]{:S(2)}) collective-permute-start(bf16[208,512]{1,0:T(8,128)(2,1)S(1)} %maximum_maximum_fusion.refs_1_.refs_3_), channel_id=1, source_target_pairs={{0,4},{2,6},{8,0},{10,2},{16,8},{18,10},{24,16},{26,18},{28,24},{3... | collective-permute-start | bytes 638984 | tf_op jit(solution)/shard_map/ppermute | solution.py:344
  6.0 11.2 %collective-permute-start.2 = (bf16[192,512]{1,0:T(8,128)(2,1)S(1)}, bf16[192,512]{1,0:T(8,128)(2,1)S(1)}, u32[]{:S(2)}, u32[]{:S(2)}) collective-permute-start(bf16[192,512]{1,0:T(8,128)(2,1)S(1)} %get-tuple-element.47.refs_2_), channel_id=1, source_target_pairs={{0,8},{2,10},{8,16},{10,18},{16,24},{18,26},{24,28},{26,30},{28,20... | collective-permute-start | bytes 589832 | tf_op jit(solution)/shard_map/ppermute | solution.py:343
  8.0 11.2 %collective-permute-start.9 = (bf16[192,512]{1,0:T(8,128)(2,1)S(1)}, bf16[192,512]{1,0:T(8,128)(2,1)S(1)}, u32[]{:S(2)}, u32[]{:S(2)}) collective-permute-start(bf16[192,512]{1,0:T(8,128)(2,1)S(1)} %get-tuple-element.47.refs_2_), channel_id=1, source_target_pairs={{0,4},{2,6},{8,0},{10,2},{16,8},{18,10},{24,16},{26,18},{28,24},{3... | collective-permute-start | bytes 589832 | tf_op jit(solution)/shard_map/ppermute | solution.py:344
  15.1 8.2 %collective-permute-start.7 = (bf16[208,512]{1,0:T(8,128)(2,1)S(1)}, bf16[208,512]{1,0:T(8,128)(2,1)S(1)}, u32[]{:S(2)}, u32[]{:S(2)}) collective-permute-start(bf16[208,512]{1,0:T(8,128)(2,1)S(1)} %collective-permute-done.5.refs_3_), channel_id=1, source_target_pairs={{0,8},{2,10},{8,16},{10,18},{16,24},{18,26},{24,28},{26,30},{28,20... | collective-permute-start | bytes 638984 | tf_op jit(solution)/shard_map/ppermute | solution.py:343
  17.2 8.2 %collective-permute-start.8 = (bf16[208,512]{1,0:T(8,128)(2,1)S(1)}, bf16[208,512]{1,0:T(8,128)(2,1)S(1)}, u32[]{:S(2)}, u32[]{:S(2)}) collective-permute-start(bf16[208,512]{1,0:T(8,128)(2,1)S(1)} %collective-permute-done.6.refs_5_), channel_id=1, source_target_pairs={{0,4},{2,6},{8,0},{10,2},{16,8},{18,10},{24,16},{26,18},{28,24},{3... | collective-permute-start | bytes 638984 | tf_op jit(solution)/shard_map/ppermute | solution.py:344
  17.2 8.5 %collective-permute-start.3 = (bf16[192,512]{1,0:T(8,128)(2,1)S(1)}, bf16[192,512]{1,0:T(8,128)(2,1)S(1)}, u32[]{:S(2)}, u32[]{:S(2)}) collective-permute-start(bf16[192,512]{1,0:T(8,128)(2,1)S(1)} %collective-permute-done.2.refs_2_), channel_id=1, source_target_pairs={{0,8},{2,10},{8,16},{10,18},{16,24},{18,26},{24,28},{26,30},{28,20... | collective-permute-start | bytes 589832 | tf_op jit(solution)/shard_map/ppermute | solution.py:343
  19.2 10.4 %collective-permute-start.11 = (bf16[192,512]{1,0:T(8,128)(2,1)S(1)}, bf16[192,512]{1,0:T(8,128)(2,1)S(1)}, u32[]{:S(2)}, u32[]{:S(2)}) collective-permute-start(bf16[192,512]{1,0:T(8,128)(2,1)S(1)} %collective-permute-done.9.refs_4_), channel_id=1, source_target_pairs={{0,4},{2,6},{8,0},{10,2},{16,8},{18,10},{24,16},{26,18},{28,24},{3... | collective-permute-start | bytes 589832 | tf_op jit(solution)/shard_map/ppermute | solution.py:344
  25.4 9.6 %collective-permute-start.10 = (bf16[208,512]{1,0:T(8,128)(2,1)S(1)}, bf16[208,512]{1,0:T(8,128)(2,1)S(1)}, u32[]{:S(2)}, u32[]{:S(2)}) collective-permute-start(bf16[208,512]{1,0:T(8,128)(2,1)S(1)} %collective-permute-done.8.refs_5_), channel_id=1, source_target_pairs={{0,4},{2,6},{8,0},{10,2},{16,8},{18,10},{24,16},{26,18},{28,24},{3... | collective-permute-start | bytes 638984 | tf_op jit(solution)/shard_map/ppermute | solution.py:344
  25.7 9.2 %collective-permute-start.4 = (bf16[192,512]{1,0:T(8,128)(2,1)S(1)}, bf16[192,512]{1,0:T(8,128)(2,1)S(1)}, u32[]{:S(2)}, u32[]{:S(2)}) collective-permute-start(bf16[192,512]{1,0:T(8,128)(2,1)S(1)} %collective-permute-done.3.refs_2_), channel_id=1, source_target_pairs={{0,8},{2,10},{8,16},{10,18},{16,24},{18,26},{24,28},{26,30},{28,20... | collective-permute-start | bytes 589832 | tf_op jit(solution)/shard_map/ppermute | solution.py:343
  29.6 8.6 %collective-permute-start.15 = (bf16[192,512]{1,0:T(8,128)(2,1)S(1)}, bf16[192,512]{1,0:T(8,128)(2,1)S(1)}, u32[]{:S(2)}, u32[]{:S(2)}) collective-permute-start(bf16[192,512]{1,0:T(8,128)(2,1)S(1)} %collective-permute-done.11.refs_4_), channel_id=1, source_target_pairs={{0,4},{2,6},{8,0},{10,2},{16,8},{18,10},{24,16},{26,18},{28,24},{3... | collective-permute-start | bytes 589832 | tf_op jit(solution)/shard_map/ppermute | solution.py:344
  29.6 8.6 %collective-permute-start.14 = (bf16[208,512]{1,0:T(8,128)(2,1)S(1)}, bf16[208,512]{1,0:T(8,128)(2,1)S(1)}, u32[]{:S(2)}, u32[]{:S(2)}) collective-permute-start(bf16[208,512]{1,0:T(8,128)(2,1)S(1)} %collective-permute-done.7.refs_3_), channel_id=1, source_target_pairs={{0,8},{2,10},{8,16},{10,18},{16,24},{18,26},{24,28},{26,30},{28,20... | collective-permute-start | bytes 638984 | tf_op jit(solution)/shard_map/ppermute | solution.py:343
  35.0 6.6 %collective-permute-start.13 = (bf16[208,512]{1,0:T(8,128)(2,1)S(1)}, bf16[208,512]{1,0:T(8,128)(2,1)S(1)}, u32[]{:S(2)}, u32[]{:S(2)}) collective-permute-start(bf16[208,512]{1,0:T(8,128)(2,1)S(1)} %collective-permute-done.10.refs_5_), channel_id=1, source_target_pairs={{0,4},{2,6},{8,0},{10,2},{16,8},{18,10},{24,16},{26,18},{28,24},{3... | collective-permute-start | bytes 638984 | tf_op jit(solution)/shard_map/ppermute | solution.py:344
  35.1 6.5 %collective-permute-start.12 = (bf16[192,512]{1,0:T(8,128)(2,1)S(1)}, bf16[192,512]{1,0:T(8,128)(2,1)S(1)}, u32[]{:S(2)}, u32[]{:S(2)}) collective-permute-start(bf16[192,512]{1,0:T(8,128)(2,1)S(1)} %collective-permute-done.4.refs_2_), channel_id=1, source_target_pairs={{0,8},{2,10},{8,16},{10,18},{16,24},{18,26},{24,28},{26,30},{28,20... | collective-permute-start | bytes 589832 | tf_op jit(solution)/shard_map/ppermute | solution.py:343
  43.7 1.9 %collective-permute-start.16 = (bf16[192,1280]{1,0:T(8,128)(2,1)S(1)}, bf16[192,1280]{1,0:T(8,128)(2,1)S(1)}, u32[]{:S(2)}, u32[]{:S(2)}) collective-permute-start(bf16[192,1280]{1,0:T(8,128)(2,1)S(1)} %get-tuple-element.69), channel_id=1, source_target_pairs={{0,2},{2,0},{4,6},{6,4},{8,10},{10,8},{12,14},{14,12},{16,18},{18,... | collective-permute-start | bytes 1474568 | tf_op jit(solution)/shard_map/ppermute | solution.py:389
  47.1 8.5 %collective-permute-start.17 = (bf16[96,1280]{1,0:T(8,128)(2,1)S(1)}, bf16[96,1280]{1,0:T(8,128)(2,1)S(1)}, u32[]{:S(2)}, u32[]{:S(2)}) collective-permute-start(bf16[96,1280]{1,0:T(8,128)(2,1)S(1)} %get-tuple-element.72), channel_id=1, source_target_pairs={{0,1},{1,0},{2,3},{3,2},{4,5},{5,4},{6,7},{7,6},{8,9},{9,8},{10,11... | collective-permute-start | bytes 737288 | tf_op jit(solution)/shard_map/ppermute | solution.py:440
  52.1 8.5 %collective-permute-start.18 = (bf16[96,1280]{1,0:T(8,128)(2,1)S(1)}, bf16[96,1280]{1,0:T(8,128)(2,1)S(1)}, u32[]{:S(2)}, u32[]{:S(2)}) collective-permute-start(bf16[96,1280]{1,0:T(8,128)(2,1)S(1)} %get-tuple-element.76), channel_id=1, source_target_pairs={{0,1},{1,0},{2,3},{3,2},{4,5},{5,4},{6,7},{7,6},{8,9},{9,8},{10,11... | collective-permute-start | bytes 737288 | tf_op jit(solution)/shard_map/ppermute | solution.py:440
  58.7 12.2 %collective-permute-start.19 = (bf16[96,1536]{1,0:T(8,128)(2,1)S(1)}, bf16[96,1536]{1,0:T(8,128)(2,1)S(1)}, u32[]{:S(2)}, u32[]{:S(2)}) collective-permute-start(bf16[96,1536]{1,0:T(8,128)(2,1)S(1)} %get-tuple-element.80), channel_id=1, source_target_pairs={{0,1},{1,0},{2,3},{3,2},{4,5},{5,4},{6,7},{7,6},{8,9},{9,8},{10,11... | collective-permute-start | bytes 884744 | tf_op jit(solution)/shard_map/ppermute | solution.py:440
  61.8 9.1 %collective-permute-start.20 = (bf16[96,1024]{1,0:T(8,128)(2,1)S(1)}, bf16[96,1024]{1,0:T(8,128)(2,1)S(1)}, u32[]{:S(2)}, u32[]{:S(2)}) collective-permute-start(bf16[96,1024]{1,0:T(8,128)(2,1)S(1)} %get-tuple-element.84), channel_id=1, source_target_pairs={{0,1},{1,0},{2,3},{3,2},{4,5},{5,4},{6,7},{7,6},{8,9},{9,8},{10,11... | collective-permute-start | bytes 589832 | tf_op jit(solution)/shard_map/ppermute | solution.py:440

commit v8 on v7

--- a/solution.py
+++ b/solution.py
@@ -99,7 +99,7 @@
         packet, row = plan["members"][j]
         at = row + half * chunk
         at = at if isinstance(half, int) else pl.multiple_of(at, HEADER)
-        return packets[packet][pl.ds(at, chunk), column : column + HEAD_WIDTH]
+        return packets[packet][pl.ds(at, chunk), pl.ds(column, HEAD_WIDTH)]
 
     def state_at(i, half, h):
         return (2 * i + half) * heads + h
@@ -111,8 +111,10 @@
     count = len(plan["members"])
     for first in range(0, count, 6):
         group = range(first, min(first + 6, count))
-        for h in range(heads):
-            k_at, v_at = h * HEAD_WIDTH, (heads + h) * HEAD_WIDTH
+
+        def one_head(h, carry, first=first, group=group):
+            k_at = pl.multiple_of(h * HEAD_WIDTH, HEAD_WIDTH)
+            v_at = pl.multiple_of((heads + h) * HEAD_WIDTH, HEAD_WIDTH)
             early_keys = jnp.concatenate([rows_of(j, 0, k_at) for j in group], axis=0)
             early_values = turned_values([rows_of(j, 0, v_at) for j in group])
             for i in range(owners):
@@ -165,10 +167,13 @@
                         mixed = sums[:HEAD_WIDTH] * (1.0 / sums[HEAD_WIDTH : HEAD_WIDTH + 1])
                         mixed = jnp.transpose(mixed.astype(out_refs[i].dtype))
                         for g in range(QUERY_PER_KEY):
+                            to = pl.multiple_of(h * GROUP + g * HEAD_WIDTH, HEAD_WIDTH)
                             out_refs[i][
-                                side * chunk : (side + 1) * chunk,
-                                h * GROUP + g * HEAD_WIDTH : h * GROUP + (g + 1) * HEAD_WIDTH,
+                                side * chunk : (side + 1) * chunk, pl.ds(to, HEAD_WIDTH)
                             ] = mixed[g * chunk : (g + 1) * chunk]
+            return carry
+
+        lax.fori_loop(0, heads, one_head, 0)
     for copy in copies:
         copy.wait()
 
@@ -240,12 +245,26 @@
     )(*queries)
 
 
-def project_kernel(following, own_ref, other_ref, held_ref, *refs):
-    if following:
-        w_ref, sent_ref, kept_ref, next_ref, rows_ref, sems = refs
-        copies = fetch_columns(w_ref, following[0], next_ref, sems, 0)
+def project_kernel(columns, bring, own_ref, other_ref, *refs):
+    refs = list(refs)
+    held_ref = None if bring and bring[0] == columns else refs.pop(0)
+    if bring:
+        w_ref = refs.pop(0)
+    sent_ref, kept_ref = refs.pop(0), refs.pop(0)
+    copies = []
+    if bring:
+        sems = refs.pop()
+        rows_ref = refs.pop()
+        for n, (first, _) in enumerate(bring):
+            if n == 0 and held_ref is None:
+                here_ref = refs.pop()
+            else:
+                here_ref = refs.pop(0)
+            copies.append(fetch_columns(w_ref, first, here_ref, sems, n * PIECES))
+            if n == 0 and held_ref is None:
+                held_ref = here_ref
     else:
-        sent_ref, kept_ref, rows_ref = refs
+        rows_ref = refs.pop()
     chunk, part = sent_ref.shape[0], own_ref.shape[1]
     mine = lax.axis_index("inner").astype(jnp.int32)
     left = my_core() == 0
@@ -255,34 +274,51 @@
         to = slice(place * chunk, (place + 1) * chunk)
         rows_ref[to, :part] = jnp.where(left, own, other)
         rows_ref[to, part:] = jnp.where(left, other, own)
-    both = product(rows_ref[...], held_ref[...]).astype(sent_ref.dtype)
+    if bring and bring[0] == columns:
+        depth = held_ref.shape[0] // PIECES
+        total = None
+        for p, copy in enumerate(copies.pop(0)):
+            copy.wait()
+            at = slice(p * depth, (p + 1) * depth)
+            term = product(rows_ref[:, at], held_ref[at])
+            total = term if total is None else total + term
+    else:
+        total = product(rows_ref[...], held_ref[...])
+    both = total.astype(sent_ref.dtype)
     sent_ref[...] = both[:chunk]
     kept_ref[...] = both[chunk:]
-    if following:
-        for copy in copies:
+    for group in copies:
+        for copy in group:
             copy.wait()
 
 
-def project(own, other, held, out_weight, following):
-    rows, (depth, width) = own.shape[0], held.shape
+def project(own, other, held, out_weight, columns, bring):
+    rows, depth = own.shape[0], out_weight.shape[0]
+    width = columns[1]
     vmem = pl.BlockSpec(memory_space=pltpu.VMEM)
     out_shape = [jax.ShapeDtypeStruct((rows // 2, width), jnp.bfloat16)] * 2
-    in_specs, operands = [vmem] * 3, [own, other, held]
-    scratch = [pltpu.VMEM((rows, depth), jnp.bfloat16)]
-    if following:
-        out_shape.append(jax.ShapeDtypeStruct((depth, following[1]), held.dtype))
+    operands, in_specs, scratch = [own, other], [vmem] * 2, []
+    for there in bring:
+        shape = (depth, there[1])
+        if there == columns:
+            scratch.append(pltpu.VMEM(shape, out_weight.dtype))
+        else:
+            out_shape.append(jax.ShapeDtypeStruct(shape, out_weight.dtype))
+    if not scratch:
+        operands.append(held)
+        in_specs.append(vmem)
+    scratch.append(pltpu.VMEM((rows, depth), jnp.bfloat16))
+    if bring:
+        operands.append(out_weight)
         in_specs.append(pl.BlockSpec(memory_space=pltpu.HBM))
-        operands.append(out_weight)
-        scratch.append(pltpu.SemaphoreType.DMA((PIECES,)))
+        scratch.append(pltpu.SemaphoreType.DMA((PIECES * len(bring),)))
     return pl.pallas_call(
-        functools.partial(project_kernel, following),
+        functools.partial(project_kernel, columns, bring),
         out_shape=out_shape,
         in_specs=in_specs,
         out_specs=[vmem] * len(out_shape),
         scratch_shapes=scratch,
-        cost_estimate=pl.CostEstimate(
-            flops=2 * rows * depth * width, bytes_accessed=2 * depth * width, transcendentals=0
-        ),
+        cost_estimate=pl.CostEstimate(flops=1 << 10, bytes_accessed=1 << 10, transcendentals=0),
         compiler_params=pltpu.CompilerParams(vmem_limit_bytes=VMEM_LIMIT),
         name="project",
     )(*operands)
@@ -378,7 +414,7 @@
             y_up, y_down, *state = lax.optimization_barrier((y_up, y_down, *state))
         ups, downs = (up(x_up), up(y_up)), (down(x_down), down(y_down))
         if r == 1:
-            *state, first, second = call([(x, y)], None, own=True, fetch=fetch)
+            *state, held = call([(x, y)], None, own=True, fetch=fetch)
         else:
             state = call(arrived, state)
         arrived = [ups, downs]
@@ -386,7 +422,7 @@
     far = (up(x_up), down(y_down))
     state = call(arrived, state)
     own, theirs = call([far], state, last=True)
-    return own, lax.ppermute(theirs, "blk", sibling), [first, second]
+    return own, lax.ppermute(theirs, "blk", sibling), held
 
 
 def one_head_a_device(count, queries, keys, values, positions):
@@ -424,19 +460,19 @@
             partial.astype(jnp.bfloat16), "inner", scatter_dimension=0, tiled=True
         )
     out_weight = pltpu.with_memory_space_constraint(out_weight, pltpu.HBM)
-    shares = (5, 5, 6, 4)
+    shares = (12, 11, 9, 8)
     widths = [out_weight.shape[1] * share // sum(shares) for share in shares]
     cuts = [(sum(widths[:j]), columns) for j, columns in enumerate(widths)]
     own, other, held = split_over_cores(
-        count, queries, keys, values, positions, out_weight, cuts[:2]
-    )
-    received, kept, source = [], [], own
+        count, queries, keys, values, positions, out_weight, cuts[:1]
+    )
+    bring = ((), (cuts[1], cuts[2]), (cuts[3],), ())
+    received, kept = [], []
     for j in range(len(cuts)):
-        if j > 0:
-            source = after(own, sent, *received[: j - 1][-1:])
-        following = cuts[j + 1] if 0 < j < len(cuts) - 1 else None
-        sent, keep, *rest = project(source, other, held[j], out_weight, following)
-        held += rest
+        source = own if j == 0 else after(own, sent)
+        sent, keep, *rest = project(source, other, held, out_weight, cuts[j], bring[j])
+        if rest:
+            held = rest[0]
         received.append(lax.ppermute(sent, "inner", [(0, 1), (1, 0)]))
         kept.append(keep)
     mine, theirs = jnp.concatenate(kept, axis=1), jnp.concatenate(received, axis=1)

time: 72.3 us -> 71.8 us (level)
  waiting for transfers between devices: 18.9 us -> 20 us
  starting transfers between devices: 21.3 us -> 20.3 us
    pallas_call x5, Pallas kernels: 18.7 us -> 16.5 us  [attend(): pl.pallas_call(functools.partial(attend_kernel, plan), out_shape=out_shap...]
    pallas_call x4, Pallas kernels: 9.17 us -> 10.8 us  [project(): pl.pallas_call(functools.partial(project_kernel, columns, bring), out_sha...]
    ppermute x7, waiting for transfers between devices: 5.35 us -> 6.89 us  [split_over_cores(): down = lambda x: lax.ppermute(x, 'blk', counter)]
    ppermute x4, starting transfers between devices: 5.51 us -> 4.31 us  [shards(): received.append(lax.ppermute(sent, 'inner', [(0, 1), (1, 0)]))]
  transfers between devices with their start and end apart: 21 -> 21, of which waited for: 8 -> 9; matrix products, arithmetic and copies ran while one was open for 2% -> 2% of each run, Pallas kernels for 34% -> 33%
where the time goes in v8:
time: 71.8 us; the launch traced here: 71.7 us
  Pallas kernels  28.9 us (40%)
  starting transfers between devices  20.3 us (28%)
  waiting for transfers between devices  20 us (28%)
  other arithmetic  1.2 us (2%)
  local copies, waits for them, and re-layouts  1.08 us (2%)
    pallas_call x5, Pallas kernels, attend(): pl.pallas_call(functools.partial(attend_kernel, plan), out_shape=out_shap...  16.5 us
    ppermute x7, starting transfers between devices, split_over_cores(): up = lambda x: lax.ppermute(x, 'blk', clock)  14.5 us
    pallas_call x4, Pallas kernels, project(): pl.pallas_call(functools.partial(project_kernel, columns, bring), out_sha...  10.8 us
    ppermute x4, waiting for transfers between devices, shards(): received.append(lax.ppermute(sent, 'inner', [(0, 1), (1, 0)]))  10.4 us
    ppermute x7, waiting for transfers between devices, split_over_cores(): down = lambda x: lax.ppermute(x, 'blk', counter)  6.89 us
    ppermute x4, starting transfers between devices, shards(): received.append(lax.ppermute(sent, 'inner', [(0, 1), (1, 0)]))  4.31 us
    ppermute x1, waiting for transfers between devices, split_over_cores(): return (own, lax.ppermute(theirs, 'blk', sibling), held)  1.85 us
  transfers between devices with their start and end apart: 21, of which 9 were waited for; matrix products, arithmetic and copies ran while one was open for 2% of the time, Pallas kernels for 33%

profile of v8, /device:TPU:0, one launch (start us, length us, event | category | flops | bytes accessed | tf_op | source)
XLA Modules:
  0.0 71.7 jit_solution(15115979805784310732)
XLA Ops:
  0.0 1.2 %prepare.1 = (bf16[208,512]{1,0:T(8,128)(2,1)S(1)}, bf16[192,512]{1,0:T(8,128)(2,1)S(1)}, bf16[16,256]{1,0:T(8,128)(2,1)S(1)}) custom-call(bf16[192,512]{1,0:T(8,128)(2,1)} %k_ref.1, bf16[192,512]{1,0:T(8,128)(2,1)} %v_ref.1, s32[192]{0:T(256)} %position_ref.1), custom_call_target="tpu_custom_call" | custom-call | tf_op jit(solution)/shard_map/prepare/pallas_call | solution.py:350
  1.2 0.5 collective-permute-start.1
  1.7 1.1 %constant_dynamic-slice_fusion = bf16[192,1280]{1,0:T(8,128)(2,1)S(1)} fusion(bf16[192,2560]{1,0:T(8,128)(2,1)} %refs_0_.2, s32[]{:T(128)S(6)} %select_n.3), kind=kLoop, calls=%fused_computation.2 | loop fusion | bytes 983044 | tf_op jit(solution)/shard_map/dynamic_slice | solution.py:387
  2.8 0.1 collective-permute-start
  2.9 0.0 collective-permute-done.1
  2.9 3.1 %collective-permute-start.5 = (bf16[208,512]{1,0:T(8,128)(2,1)S(1)}, bf16[208,512]{1,0:T(8,128)(2,1)S(1)}, u32[]{:S(2)}, u32[]{:S(2)}) collective-permute-start(bf16[208,512]{1,0:T(8,128)(2,1)S(1)} %maximum_maximum_fusion.refs_1_.refs_3_), channel_id=1, source_target_pairs={{0,8},{2,10},{8,16},{10,18},{16,24},{18,26},{24,28},{26,30},{28,20... | collective-permute-start | bytes 638984 | tf_op jit(solution)/shard_map/ppermute | solution.py:379
  6.0 0.0 collective-permute-start.6
  6.0 2.0 %collective-permute-start.2 = (bf16[192,512]{1,0:T(8,128)(2,1)S(1)}, bf16[192,512]{1,0:T(8,128)(2,1)S(1)}, u32[]{:S(2)}, u32[]{:S(2)}) collective-permute-start(bf16[192,512]{1,0:T(8,128)(2,1)S(1)} %get-tuple-element.46.refs_2_), channel_id=1, source_target_pairs={{0,8},{2,10},{8,16},{10,18},{16,24},{18,26},{24,28},{26,30},{28,20... | collective-permute-start | bytes 589832 | tf_op jit(solution)/shard_map/ppermute | solution.py:379
  8.0 0.0 collective-permute-start.9
  8.0 0.0 collective-permute-done.refs_1_
  8.1 0.3 turn.1.refs_0_
  8.4 3.4 %attend.5 = (f32[8,1,480]{2,1,0:T(1,128)S(1)}, f32[8,144,480]{2,1,0:T(8,128)S(1)}, bf16[2560,1536]{1,0:T(8,128)(2,1)S(1)}) custom-call(bf16[8,128,480]{2,1,0:T(8,128)(2,1)S(1)} %turn.1.refs_0_, bf16[208,512]{1,0:T(8,128)(2,1)S(1)} %maximum_maximum_fusion.refs_1_.refs_3_, bf16[192,512]{1,0:T(8,128)(2,1)S(1)} %get-tuple-element.46.refs_2_, ...), custom_call_target="tpu_custom_call" | custom-call | flops 377487360 | bytes 4194304 | tf_op jit(solution)/shard_map/attend/pallas_call | solution.py:203
  11.8 0.3 collective-permute-done.5.refs_3_
  12.0 2.2 %collective-permute-done.6.refs_5_ = bf16[208,512]{1,0:T(8,128)(2,1)S(1)} collective-permute-done((bf16[208,512]{1,0:T(8,128)(2,1)S(1)}, bf16[208,512]{1,0:T(8,128)(2,1)S(1)}, u32[]{:S(2)}, u32[]{:S(2)}) %collective-permute-start.6) | collective-permute-done | bytes 213024 | tf_op jit(solution)/shard_map/ppermute | solution.py:380
  14.2 1.6 %collective-permute-start.7 = (bf16[208,512]{1,0:T(8,128)(2,1)S(1)}, bf16[208,512]{1,0:T(8,128)(2,1)S(1)}, u32[]{:S(2)}, u32[]{:S(2)}) collective-permute-start(bf16[208,512]{1,0:T(8,128)(2,1)S(1)} %collective-permute-done.5.refs_3_), channel_id=1, source_target_pairs={{0,8},{2,10},{8,16},{10,18},{16,24},{18,26},{24,28},{26,30},{28,20... | collective-permute-start | bytes 638984 | tf_op jit(solution)/shard_map/ppermute | solution.py:379
  15.7 0.4 collective-permute-start.8
  16.2 0.0 collective-permute-done.2.refs_2_
  16.2 2.1 %collective-permute-start.3 = (bf16[192,512]{1,0:T(8,128)(2,1)S(1)}, bf16[192,512]{1,0:T(8,128)(2,1)S(1)}, u32[]{:S(2)}, u32[]{:S(2)}) collective-permute-start(bf16[192,512]{1,0:T(8,128)(2,1)S(1)} %collective-permute-done.2.refs_2_), channel_id=1, source_target_pairs={{0,8},{2,10},{8,16},{10,18},{16,24},{18,26},{24,28},{26,30},{28,20... | collective-permute-start | bytes 589832 | tf_op jit(solution)/shard_map/ppermute | solution.py:379
  18.3 0.0 collective-permute-done.9.refs_4_
  18.4 0.0 collective-permute-start.11
  18.4 3.6 %attend.6 = (f32[8,1,480]{2,1,0:T(1,128)S(1)}, f32[8,144,480]{2,1,0:T(8,128)S(1)}) custom-call(bf16[8,128,480]{2,1,0:T(8,128)(2,1)S(1)} %turn.1.refs_0_, bf16[208,512]{1,0:T(8,128)(2,1)S(1)} %maximum_maximum_fusion.refs_1_.refs_3_, bf16[192,512]{1,0:T(8,128)(2,1)S(1)} %collective-permute-done.2.refs_2_, bf16[208,512]{1,0:T(8,128)(2,1)S(1)} %collective-permute-done.5.refs_3_, ...), custom_call_target="tpu_custom_call" | custom-call | flops 754974720 | bytes 4194304 | tf_op jit(solution)/shard_map/attend/pallas_call | solution.py:203
  22.0 0.3 collective-permute-done.7.refs_3_
  22.3 1.7 %collective-permute-done.8.refs_5_ = bf16[208,512]{1,0:T(8,128)(2,1)S(1)} collective-permute-done((bf16[208,512]{1,0:T(8,128)(2,1)S(1)}, bf16[208,512]{1,0:T(8,128)(2,1)S(1)}, u32[]{:S(2)}, u32[]{:S(2)}) %collective-permute-start.8) | collective-permute-done | bytes 213024 | tf_op jit(solution)/shard_map/ppermute | solution.py:380
  23.9 0.2 collective-permute-start.10
  24.1 0.3 collective-permute-done.3.refs_2_
  24.4 1.8 %collective-permute-start.4 = (bf16[192,512]{1,0:T(8,128)(2,1)S(1)}, bf16[192,512]{1,0:T(8,128)(2,1)S(1)}, u32[]{:S(2)}, u32[]{:S(2)}) collective-permute-start(bf16[192,512]{1,0:T(8,128)(2,1)S(1)} %collective-permute-done.3.refs_2_), channel_id=1, source_target_pairs={{0,8},{2,10},{8,16},{10,18},{16,24},{18,26},{24,28},{26,30},{28,20... | collective-permute-start | bytes 589832 | tf_op jit(solution)/shard_map/ppermute | solution.py:379
  26.2 2.0 %collective-permute-done.11.refs_4_ = bf16[192,512]{1,0:T(8,128)(2,1)S(1)} collective-permute-done((bf16[192,512]{1,0:T(8,128)(2,1)S(1)}, bf16[192,512]{1,0:T(8,128)(2,1)S(1)}, u32[]{:S(2)}, u32[]{:S(2)}) %collective-permute-start.11) | collective-permute-done | bytes 196640 | tf_op jit(solution)/shard_map/ppermute | solution.py:380
  28.2 2.0 %collective-permute-start.14 = (bf16[208,512]{1,0:T(8,128)(2,1)S(1)}, bf16[208,512]{1,0:T(8,128)(2,1)S(1)}, u32[]{:S(2)}, u32[]{:S(2)}) collective-permute-start(bf16[208,512]{1,0:T(8,128)(2,1)S(1)} %collective-permute-done.7.refs_3_), channel_id=1, source_target_pairs={{0,8},{2,10},{8,16},{10,18},{16,24},{18,26},{24,28},{26,30},{28,20... | collective-permute-start | bytes 638984 | tf_op jit(solution)/shard_map/ppermute | solution.py:379
  30.2 3.6 %attend.7 = (f32[8,1,480]{2,1,0:T(1,128)S(1)}, f32[8,144,480]{2,1,0:T(8,128)S(1)}) custom-call(bf16[8,128,480]{2,1,0:T(8,128)(2,1)S(1)} %turn.1.refs_0_, bf16[208,512]{1,0:T(8,128)(2,1)S(1)} %maximum_maximum_fusion.refs_1_.refs_3_, bf16[192,512]{1,0:T(8,128)(2,1)S(1)} %collective-permute-done.3.refs_2_, bf16[208,512]{1,0:T(8,128)(2,1)S(1)} %collective-permute-done.7.refs_3_, ...), custom_call_target="tpu_custom_call" | custom-call | flops 754974720 | bytes 4194304 | tf_op jit(solution)/shard_map/attend/pallas_call | solution.py:203
  33.8 0.0 collective-permute-done.4.refs_2_
  33.8 0.0 collective-permute-done.10.refs_5_
  33.8 0.2 collective-permute-start.13
  34.0 1.9 %collective-permute-start.12 = (bf16[192,512]{1,0:T(8,128)(2,1)S(1)}, bf16[192,512]{1,0:T(8,128)(2,1)S(1)}, u32[]{:S(2)}, u32[]{:S(2)}) collective-permute-start(bf16[192,512]{1,0:T(8,128)(2,1)S(1)} %collective-permute-done.4.refs_2_), channel_id=1, source_target_pairs={{0,8},{2,10},{8,16},{10,18},{16,24},{18,26},{24,28},{26,30},{28,20... | collective-permute-start | bytes 589832 | tf_op jit(solution)/shard_map/ppermute | solution.py:379
  35.9 1.1 %collective-permute-done.15.refs_4_ = bf16[192,512]{1,0:T(8,128)(2,1)S(1)} collective-permute-done((bf16[192,512]{1,0:T(8,128)(2,1)S(1)}, bf16[192,512]{1,0:T(8,128)(2,1)S(1)}, u32[]{:S(2)}, u32[]{:S(2)}) %collective-permute-start.15) | collective-permute-done | bytes 196640 | tf_op jit(solution)/shard_map/ppermute | solution.py:380
  36.9 3.6 %attend.8 = (f32[8,1,480]{2,1,0:T(1,128)S(1)}, f32[8,144,480]{2,1,0:T(8,128)S(1)}) custom-call(bf16[8,128,480]{2,1,0:T(8,128)(2,1)S(1)} %turn.1.refs_0_, bf16[208,512]{1,0:T(8,128)(2,1)S(1)} %maximum_maximum_fusion.refs_1_.refs_3_, bf16[192,512]{1,0:T(8,128)(2,1)S(1)} %collective-permute-done.4.refs_2_, ...), custom_call_target="tpu_custom_call" | custom-call | flops 754974720 | bytes 4194304 | tf_op jit(solution)/shard_map/attend/pallas_call | solution.py:203
  40.5 2.4 %attend.9 = (bf16[192,1280]{1,0:T(8,128)(2,1)S(1)}, bf16[192,1280]{1,0:T(8,128)(2,1)S(1)}) custom-call(bf16[8,128,480]{2,1,0:T(8,128)(2,1)S(1)} %turn.1.refs_0_, bf16[208,512]{1,0:T(8,128)(2,1)S(1)} %maximum_maximum_fusion.refs_1_.refs_3_, bf16[192,512]{1,0:T(8,128)(2,1)S(1)} %collective-permute-done.12.refs_2_, ...), custom_call_target="tpu_custom_call" | custom-call | flops 377487360 | bytes 4194304 | tf_op jit(solution)/shard_map/attend/pallas_call | solution.py:203
  43.0 0.1 collective-permute-start.16
  43.1 1.9 %collective-permute-done.16.other_ref = bf16[192,1280]{1,0:T(8,128)(2,1)S(1)} collective-permute-done((bf16[192,1280]{1,0:T(8,128)(2,1)S(1)}, bf16[192,1280]{1,0:T(8,128)(2,1)S(1)}, u32[]{:S(2)}, u32[]{:S(2)}) %collective-permute-start.16) | collective-permute-done | bytes 491552 | tf_op jit(solution)/shard_map/ppermute | solution.py:425
  44.9 1.7 %project.4 = (bf16[96,1536]{1,0:T(8,128)(2,1)S(1)}, bf16[96,1536]{1,0:T(8,128)(2,1)S(1)}) custom-call(bf16[192,1280]{1,0:T(8,128)(2,1)S(1)} %get-tuple-element.79.own_ref, bf16[192,1280]{1,0:T(8,128)(2,1)S(1)} %collective-permute-done.16.other_ref, bf16[2560,1536]{1,0:T(8,128)(2,1)S(1)} %get-tuple-element.69.refs_0_), custom_call_target="tpu_custom_call" | custom-call | flops 1024 | bytes 1024 | tf_op jit(solution)/shard_map/project/pallas_call | solution.py:315
  46.6 1.6 %collective-permute-start.17 = (bf16[96,1536]{1,0:T(8,128)(2,1)S(1)}, bf16[96,1536]{1,0:T(8,128)(2,1)S(1)}, u32[]{:S(2)}, u32[]{:S(2)}) collective-permute-start(bf16[96,1536]{1,0:T(8,128)(2,1)S(1)} %get-tuple-element.71), channel_id=1, source_target_pairs={{0,1},{1,0},{2,3},{3,2},{4,5},{5,4},{6,7},{7,6},{8,9},{9,8},{10,11... | collective-permute-start | bytes 884744 | tf_op jit(solution)/shard_map/ppermute | solution.py:476
  48.2 4.9 %project.5 = (bf16[96,1408]{1,0:T(8,128)(2,1)S(1)}, bf16[96,1408]{1,0:T(8,128)(2,1)S(1)}, bf16[2560,1152]{1,0:T(8,128)(2,1)S(1)}) custom-call(bf16[192,1280]{1,0:T(8,128)(2,1)S(1)} %get-tuple-element.79.own_ref, bf16[192,1280]{1,0:T(8,128)(2,1)S(1)} %collective-permute-done.16.other_ref, bf16[2560,5120]{1,0:T(8,128)(2,1)} %refs_1_.1), custom_call_target="tpu_custom_call" | custom-call | flops 1024 | bytes 1024 | tf_op jit(solution)/shard_map/project/pallas_call | solution.py:315
  53.1 0.5 collective-permute-start.18
  53.6 3.1 %project.6 = (bf16[96,1152]{1,0:T(8,128)(2,1)S(1)}, bf16[96,1152]{1,0:T(8,128)(2,1)S(1)}, bf16[2560,1024]{1,0:T(8,128)(2,1)S(1)}) custom-call(bf16[192,1280]{1,0:T(8,128)(2,1)S(1)} %get-tuple-element.79.own_ref, bf16[192,1280]{1,0:T(8,128)(2,1)S(1)} %collective-permute-done.16.other_ref, bf16[2560,1152]{1,0:T(8,128)(2,1)S(1)} %get-tuple-element.76.refs_0_, ...), custom_call_target="tpu_custom_call" | custom-call | flops 1024 | bytes 1024 | tf_op jit(solution)/shard_map/project/pallas_call | solution.py:315
  56.7 1.6 %collective-permute-start.19 = (bf16[96,1152]{1,0:T(8,128)(2,1)S(1)}, bf16[96,1152]{1,0:T(8,128)(2,1)S(1)}, u32[]{:S(2)}, u32[]{:S(2)}) collective-permute-start(bf16[96,1152]{1,0:T(8,128)(2,1)S(1)} %get-tuple-element.78), channel_id=1, source_target_pairs={{0,1},{1,0},{2,3},{3,2},{4,5},{5,4},{6,7},{7,6},{8,9},{9,8},{10,11... | collective-permute-start | bytes 663560 | tf_op jit(solution)/shard_map/ppermute | solution.py:476
  58.4 1.2 %project.7 = (bf16[96,1024]{1,0:T(8,128)(2,1)S(1)}, bf16[96,1024]{1,0:T(8,128)(2,1)S(1)}) custom-call(bf16[192,1280]{1,0:T(8,128)(2,1)S(1)} %get-tuple-element.79.own_ref, bf16[192,1280]{1,0:T(8,128)(2,1)S(1)} %collective-permute-done.16.other_ref, bf16[2560,1024]{1,0:T(8,128)(2,1)S(1)} %get-tuple-element.80.refs_0_), custom_call_target="tpu_custom_call" | custom-call | flops 1024 | bytes 1024 | tf_op jit(solution)/shard_map/project/pallas_call | solution.py:315
  59.6 0.5 collective-permute-start.20
  60.1 10.4 %collective-permute-done.20 = bf16[96,1024]{1,0:T(8,128)(2,1)S(1)} collective-permute-done((bf16[96,1024]{1,0:T(8,128)(2,1)S(1)}, bf16[96,1024]{1,0:T(8,128)(2,1)S(1)}, u32[]{:S(2)}, u32[]{:S(2)}) %collective-permute-start.20) | collective-permute-done | bytes 196640 | tf_op jit(solution)/shard_map/ppermute | solution.py:476
  70.5 1.2 %add_convert_fusion = bf16[96,5120]{1,0:T(8,128)(2,1)} fusion(bf16[96,1024]{1,0:T(8,128)(2,1)S(1)} %get-tuple-element.81, bf16[96,1152]{1,0:T(8,128)(2,1)S(1)} %get-tuple-element.77, bf16[96,1408]{1,0:T(8,128)(2,1)S(1)} %get-tuple-element.73, bf16[96,1536]{1,0:T(8,128)(2,1)S(1)} %get-tuple-element.70, bf16[96,1024]{1,0:T(8,128)(2,1)S(1)} %collective-permute-done.20, ...), kind=kLoop, calls=%fused_computation | loop fusion | flops 8847360 | bytes 2949120 | tf_op jit(solution)/shard_map/convert_element_type | solution.py:479
  (12 shorter events, 0.1 us)
Async XLA Ops:
  0.0 8.1 %copy-start = (bf16[192,2560]{1,0:T(8,128)(2,1)S(1)}, bf16[192,2560]{1,0:T(8,128)(2,1)}, u32[]{:S(2)}) copy-start(bf16[192,2560]{1,0:T(8,128)(2,1)} %refs_0_.2) | copy-start | bytes 2949124
  1.2 1.7 %collective-permute-start.1 = (bf16[208,512]{1,0:T(8,128)(2,1)S(1)}, bf16[208,512]{1,0:T(8,128)(2,1)S(1)}, u32[]{:S(2)}, u32[]{:S(2)}) collective-permute-start(bf16[208,512]{1,0:T(8,128)(2,1)S(1)} %get-tuple-element.44), channel_id=1, source_target_pairs={{0,2},{2,0},{4,6},{6,4},{8,10},{10,8},{12,14},{14,12},{16,18},{18,... | collective-permute-start | bytes 638984 | tf_op jit(solution)/shard_map/ppermute | solution.py:383
  2.8 5.3 %collective-permute-start = (bf16[192,1280]{1,0:T(8,128)(2,1)S(1)}, bf16[192,1280]{1,0:T(8,128)(2,1)S(1)}, u32[]{:S(2)}, u32[]{:S(2)}) collective-permute-start(bf16[192,1280]{1,0:T(8,128)(2,1)S(1)} %constant_dynamic-slice_fusion), channel_id=1, source_target_pairs={{0,2},{2,0},{4,6},{6,4},{8,10},{10,8},{12,14},{14,12},{16,18},{18,... | collective-permute-start | bytes 1474568 | tf_op jit(solution)/shard_map/ppermute | solution.py:390
  2.9 9.1 %collective-permute-start.5 = (bf16[208,512]{1,0:T(8,128)(2,1)S(1)}, bf16[208,512]{1,0:T(8,128)(2,1)S(1)}, u32[]{:S(2)}, u32[]{:S(2)}) collective-permute-start(bf16[208,512]{1,0:T(8,128)(2,1)S(1)} %maximum_maximum_fusion.refs_1_.refs_3_), channel_id=1, source_target_pairs={{0,8},{2,10},{8,16},{10,18},{16,24},{18,26},{24,28},{26,30},{28,20... | collective-permute-start | bytes 638984 | tf_op jit(solution)/shard_map/ppermute | solution.py:379
  6.0 8.2 %collective-permute-start.6 = (bf16[208,512]{1,0:T(8,128)(2,1)S(1)}, bf16[208,512]{1,0:T(8,128)(2,1)S(1)}, u32[]{:S(2)}, u32[]{:S(2)}) collective-permute-start(bf16[208,512]{1,0:T(8,128)(2,1)S(1)} %maximum_maximum_fusion.refs_1_.refs_3_), channel_id=1, source_target_pairs={{0,4},{2,6},{8,0},{10,2},{16,8},{18,10},{24,16},{26,18},{28,24},{3... | collective-permute-start | bytes 638984 | tf_op jit(solution)/shard_map/ppermute | solution.py:380
  6.0 10.2 %collective-permute-start.2 = (bf16[192,512]{1,0:T(8,128)(2,1)S(1)}, bf16[192,512]{1,0:T(8,128)(2,1)S(1)}, u32[]{:S(2)}, u32[]{:S(2)}) collective-permute-start(bf16[192,512]{1,0:T(8,128)(2,1)S(1)} %get-tuple-element.46.refs_2_), channel_id=1, source_target_pairs={{0,8},{2,10},{8,16},{10,18},{16,24},{18,26},{24,28},{26,30},{28,20... | collective-permute-start | bytes 589832 | tf_op jit(solution)/shard_map/ppermute | solution.py:379
  8.0 10.3 %collective-permute-start.9 = (bf16[192,512]{1,0:T(8,128)(2,1)S(1)}, bf16[192,512]{1,0:T(8,128)(2,1)S(1)}, u32[]{:S(2)}, u32[]{:S(2)}) collective-permute-start(bf16[192,512]{1,0:T(8,128)(2,1)S(1)} %get-tuple-element.46.refs_2_), channel_id=1, source_target_pairs={{0,4},{2,6},{8,0},{10,2},{16,8},{18,10},{24,16},{26,18},{28,24},{3... | collective-permute-start | bytes 589832 | tf_op jit(solution)/shard_map/ppermute | solution.py:380
  14.2 8.1 %collective-permute-start.7 = (bf16[208,512]{1,0:T(8,128)(2,1)S(1)}, bf16[208,512]{1,0:T(8,128)(2,1)S(1)}, u32[]{:S(2)}, u32[]{:S(2)}) collective-permute-start(bf16[208,512]{1,0:T(8,128)(2,1)S(1)} %collective-permute-done.5.refs_3_), channel_id=1, source_target_pairs={{0,8},{2,10},{8,16},{10,18},{16,24},{18,26},{24,28},{26,30},{28,20... | collective-permute-start | bytes 638984 | tf_op jit(solution)/shard_map/ppermute | solution.py:379
  15.7 8.2 %collective-permute-start.8 = (bf16[208,512]{1,0:T(8,128)(2,1)S(1)}, bf16[208,512]{1,0:T(8,128)(2,1)S(1)}, u32[]{:S(2)}, u32[]{:S(2)}) collective-permute-start(bf16[208,512]{1,0:T(8,128)(2,1)S(1)} %collective-permute-done.6.refs_5_), channel_id=1, source_target_pairs={{0,4},{2,6},{8,0},{10,2},{16,8},{18,10},{24,16},{26,18},{28,24},{3... | collective-permute-start | bytes 638984 | tf_op jit(solution)/shard_map/ppermute | solution.py:380
  16.2 8.2 %collective-permute-start.3 = (bf16[192,512]{1,0:T(8,128)(2,1)S(1)}, bf16[192,512]{1,0:T(8,128)(2,1)S(1)}, u32[]{:S(2)}, u32[]{:S(2)}) collective-permute-start(bf16[192,512]{1,0:T(8,128)(2,1)S(1)} %collective-permute-done.2.refs_2_), channel_id=1, source_target_pairs={{0,8},{2,10},{8,16},{10,18},{16,24},{18,26},{24,28},{26,30},{28,20... | collective-permute-start | bytes 589832 | tf_op jit(solution)/shard_map/ppermute | solution.py:379
  18.4 9.8 %collective-permute-start.11 = (bf16[192,512]{1,0:T(8,128)(2,1)S(1)}, bf16[192,512]{1,0:T(8,128)(2,1)S(1)}, u32[]{:S(2)}, u32[]{:S(2)}) collective-permute-start(bf16[192,512]{1,0:T(8,128)(2,1)S(1)} %collective-permute-done.9.refs_4_), channel_id=1, source_target_pairs={{0,4},{2,6},{8,0},{10,2},{16,8},{18,10},{24,16},{26,18},{28,24},{3... | collective-permute-start | bytes 589832 | tf_op jit(solution)/shard_map/ppermute | solution.py:380
  23.9 9.8 %collective-permute-start.10 = (bf16[208,512]{1,0:T(8,128)(2,1)S(1)}, bf16[208,512]{1,0:T(8,128)(2,1)S(1)}, u32[]{:S(2)}, u32[]{:S(2)}) collective-permute-start(bf16[208,512]{1,0:T(8,128)(2,1)S(1)} %collective-permute-done.8.refs_5_), channel_id=1, source_target_pairs={{0,4},{2,6},{8,0},{10,2},{16,8},{18,10},{24,16},{26,18},{28,24},{3... | collective-permute-start | bytes 638984 | tf_op jit(solution)/shard_map/ppermute | solution.py:380
  24.4 9.4 %collective-permute-start.4 = (bf16[192,512]{1,0:T(8,128)(2,1)S(1)}, bf16[192,512]{1,0:T(8,128)(2,1)S(1)}, u32[]{:S(2)}, u32[]{:S(2)}) collective-permute-start(bf16[192,512]{1,0:T(8,128)(2,1)S(1)} %collective-permute-done.3.refs_2_), channel_id=1, source_target_pairs={{0,8},{2,10},{8,16},{10,18},{16,24},{18,26},{24,28},{26,30},{28,20... | collective-permute-start | bytes 589832 | tf_op jit(solution)/shard_map/ppermute | solution.py:379
  28.1 8.8 %collective-permute-start.15 = (bf16[192,512]{1,0:T(8,128)(2,1)S(1)}, bf16[192,512]{1,0:T(8,128)(2,1)S(1)}, u32[]{:S(2)}, u32[]{:S(2)}) collective-permute-start(bf16[192,512]{1,0:T(8,128)(2,1)S(1)} %collective-permute-done.11.refs_4_), channel_id=1, source_target_pairs={{0,4},{2,6},{8,0},{10,2},{16,8},{18,10},{24,16},{26,18},{28,24},{3... | collective-permute-start | bytes 589832 | tf_op jit(solution)/shard_map/ppermute | solution.py:380
  28.2 8.8 %collective-permute-start.14 = (bf16[208,512]{1,0:T(8,128)(2,1)S(1)}, bf16[208,512]{1,0:T(8,128)(2,1)S(1)}, u32[]{:S(2)}, u32[]{:S(2)}) collective-permute-start(bf16[208,512]{1,0:T(8,128)(2,1)S(1)} %collective-permute-done.7.refs_3_), channel_id=1, source_target_pairs={{0,8},{2,10},{8,16},{10,18},{16,24},{18,26},{24,28},{26,30},{28,20... | collective-permute-start | bytes 638984 | tf_op jit(solution)/shard_map/ppermute | solution.py:379
  33.8 6.7 %collective-permute-start.13 = (bf16[208,512]{1,0:T(8,128)(2,1)S(1)}, bf16[208,512]{1,0:T(8,128)(2,1)S(1)}, u32[]{:S(2)}, u32[]{:S(2)}) collective-permute-start(bf16[208,512]{1,0:T(8,128)(2,1)S(1)} %collective-permute-done.10.refs_5_), channel_id=1, source_target_pairs={{0,4},{2,6},{8,0},{10,2},{16,8},{18,10},{24,16},{26,18},{28,24},{3... | collective-permute-start | bytes 638984 | tf_op jit(solution)/shard_map/ppermute | solution.py:380
  34.0 6.5 %collective-permute-start.12 = (bf16[192,512]{1,0:T(8,128)(2,1)S(1)}, bf16[192,512]{1,0:T(8,128)(2,1)S(1)}, u32[]{:S(2)}, u32[]{:S(2)}) collective-permute-start(bf16[192,512]{1,0:T(8,128)(2,1)S(1)} %collective-permute-done.4.refs_2_), channel_id=1, source_target_pairs={{0,8},{2,10},{8,16},{10,18},{16,24},{18,26},{24,28},{26,30},{28,20... | collective-permute-start | bytes 589832 | tf_op jit(solution)/shard_map/ppermute | solution.py:379
  43.0 1.9 %collective-permute-start.16 = (bf16[192,1280]{1,0:T(8,128)(2,1)S(1)}, bf16[192,1280]{1,0:T(8,128)(2,1)S(1)}, u32[]{:S(2)}, u32[]{:S(2)}) collective-permute-start(bf16[192,1280]{1,0:T(8,128)(2,1)S(1)} %get-tuple-element.68), channel_id=1, source_target_pairs={{0,2},{2,0},{4,6},{6,4},{8,10},{10,8},{12,14},{14,12},{16,18},{18,... | collective-permute-start | bytes 1474568 | tf_op jit(solution)/shard_map/ppermute | solution.py:425
  46.6 23.9 %collective-permute-start.17 = (bf16[96,1536]{1,0:T(8,128)(2,1)S(1)}, bf16[96,1536]{1,0:T(8,128)(2,1)S(1)}, u32[]{:S(2)}, u32[]{:S(2)}) collective-permute-start(bf16[96,1536]{1,0:T(8,128)(2,1)S(1)} %get-tuple-element.71), channel_id=1, source_target_pairs={{0,1},{1,0},{2,3},{3,2},{4,5},{5,4},{6,7},{7,6},{8,9},{9,8},{10,11... | collective-permute-start | bytes 884744 | tf_op jit(solution)/shard_map/ppermute | solution.py:476
  53.1 17.4 %collective-permute-start.18 = (bf16[96,1408]{1,0:T(8,128)(2,1)S(1)}, bf16[96,1408]{1,0:T(8,128)(2,1)S(1)}, u32[]{:S(2)}, u32[]{:S(2)}) collective-permute-start(bf16[96,1408]{1,0:T(8,128)(2,1)S(1)} %get-tuple-element.74), channel_id=1, source_target_pairs={{0,1},{1,0},{2,3},{3,2},{4,5},{5,4},{6,7},{7,6},{8,9},{9,8},{10,11... | collective-permute-start | bytes 811016 | tf_op jit(solution)/shard_map/ppermute | solution.py:476
  56.7 13.7 %collective-permute-start.19 = (bf16[96,1152]{1,0:T(8,128)(2,1)S(1)}, bf16[96,1152]{1,0:T(8,128)(2,1)S(1)}, u32[]{:S(2)}, u32[]{:S(2)}) collective-permute-start(bf16[96,1152]{1,0:T(8,128)(2,1)S(1)} %get-tuple-element.78), channel_id=1, source_target_pairs={{0,1},{1,0},{2,3},{3,2},{4,5},{5,4},{6,7},{7,6},{8,9},{9,8},{10,11... | collective-permute-start | bytes 663560 | tf_op jit(solution)/shard_map/ppermute | solution.py:476
  59.6 10.9 %collective-permute-start.20 = (bf16[96,1024]{1,0:T(8,128)(2,1)S(1)}, bf16[96,1024]{1,0:T(8,128)(2,1)S(1)}, u32[]{:S(2)}, u32[]{:S(2)}) collective-permute-start(bf16[96,1024]{1,0:T(8,128)(2,1)S(1)} %get-tuple-element.82), channel_id=1, source_target_pairs={{0,1},{1,0},{2,3},{3,2},{4,5},{5,4},{6,7},{7,6},{8,9},{9,8},{10,11... | collective-permute-start | bytes 589832 | tf_op jit(solution)/shard_map/ppermute | solution.py:476

commit v9 on v7

--- a/solution.py
+++ b/solution.py
@@ -99,7 +99,7 @@
         packet, row = plan["members"][j]
         at = row + half * chunk
         at = at if isinstance(half, int) else pl.multiple_of(at, HEADER)
-        return packets[packet][pl.ds(at, chunk), column : column + HEAD_WIDTH]
+        return packets[packet][pl.ds(at, chunk), pl.ds(column, HEAD_WIDTH)]
 
     def state_at(i, half, h):
         return (2 * i + half) * heads + h
@@ -109,66 +109,99 @@
         lax.broadcasted_iota(jnp.int32, (chunk, rows), 1), chunk
     )
     count = len(plan["members"])
+
+    def one_chain(group, h, i, shared):
+        first, done = group[0], group[-1] == count - 1
+        k_at = pl.multiple_of(h * HEAD_WIDTH, HEAD_WIDTH)
+        v_at = pl.multiple_of((heads + h) * HEAD_WIDTH, HEAD_WIDTH)
+        late_at, early_at = state_at(i, 1, h), state_at(i, 0, h)
+        if i == 0:
+            shared["keys"] = jnp.concatenate([rows_of(j, 0, k_at) for j in group], axis=0)
+            shared["values"] = turned_values([rows_of(j, 0, v_at) for j in group])
+        carried = None
+        if first > 0:
+            carried = [(ref[early_at], ref[late_at]) for ref in (high_ref, sums_ref)]
+        elif plan["carried"]:
+            carried = [(ref[early_at], ref[late_at]) for ref in (in_high, in_sums)]
+        pairs = []
+        for j in group:
+            if plan["own"] and j == plan["own_at"](i):
+                pairs += [(j, 0, causal), (j, 1, causal)]
+            else:
+                pairs.append((j, (member_c[j] > owner_c[i]).astype(jnp.int32), None))
+        base = product(shared["keys"], q_ref[late_at])
+        scores = []
+        for j, half, mask in pairs:
+            s = product(rows_of(j, half, k_at), q_ref[state_at(i, half, h)])
+            scores.append(s if mask is None else jnp.where(mask, s, MASKED))
+        values = turned_values([rows_of(j, half, v_at) for j, half, _ in pairs])
+        tops = [jnp.max(s, axis=0, keepdims=True) for s in scores]
+        highs = []
+        for side in range(2):
+            some = [jnp.where(half == side, top, MASKED) for (_, half, _), top in zip(pairs, tops)]
+            if side == 1:
+                some.append(jnp.max(base, axis=0, keepdims=True))
+            if carried is not None:
+                some.append(carried[0][side])
+            highs.append(functools.reduce(jnp.maximum, some))
+        yield
+        base_weights = weigh(base, highs[1])
+        weights = [
+            weigh(s, jnp.where(half == 1, highs[1], highs[0])) for (_, half, _), s in zip(pairs, scores)
+        ]
+        zero = jnp.zeros_like(weights[0])
+        chosen = [
+            jnp.concatenate(
+                [jnp.where(half == side, w, zero) for (_, half, _), w in zip(pairs, weights)], axis=0
+            )
+            for side in range(2)
+        ]
+        yield
+        for side, at in ((0, early_at), (1, late_at)):
+            sums = product(values, chosen[side])
+            if side == 1:
+                sums = sums + product(shared["values"], base_weights)
+            if carried is not None:
+                shrink = jnp.exp2((carried[0][side] - highs[side]) * EXP2_SCALE)
+                sums = sums + carried[1][side] * shrink
+            if plan["last"] and done:
+                mixed = sums[:HEAD_WIDTH] * (1.0 / sums[HEAD_WIDTH : HEAD_WIDTH + 1])
+                mixed = jnp.transpose(mixed.astype(out_refs[i].dtype))
+                for g in range(QUERY_PER_KEY):
+                    to = pl.multiple_of(h * GROUP + g * HEAD_WIDTH, HEAD_WIDTH)
+                    out_refs[i][side * chunk : (side + 1) * chunk, pl.ds(to, HEAD_WIDTH)] = mixed[
+                        g * chunk : (g + 1) * chunk
+                    ]
+            else:
+                high_ref[at] = highs[side]
+                sums_ref[at] = sums
+        yield
+
+    def staggered(chains):
+        for t in range(len(chains) + 2):
+            for stage in (2, 1, 0):
+                if 0 <= t - stage < len(chains):
+                    next(chains[t - stage])
+
     for first in range(0, count, 6):
         group = range(first, min(first + 6, count))
-        for h in range(heads):
-            k_at, v_at = h * HEAD_WIDTH, (heads + h) * HEAD_WIDTH
-            early_keys = jnp.concatenate([rows_of(j, 0, k_at) for j in group], axis=0)
-            early_values = turned_values([rows_of(j, 0, v_at) for j in group])
-            for i in range(owners):
-                late_at, early_at = state_at(i, 1, h), state_at(i, 0, h)
-                carried = None
-                if first > 0:
-                    carried = [(ref[early_at], ref[late_at]) for ref in (high_ref, sums_ref)]
-                elif plan["carried"]:
-                    carried = [(ref[early_at], ref[late_at]) for ref in (in_high, in_sums)]
-
-                pairs = []
-                for j in group:
-                    if plan["own"] and j == plan["own_at"](i):
-                        pairs += [(j, 0, causal), (j, 1, causal)]
-                    else:
-                        pairs.append((j, (member_c[j] > owner_c[i]).astype(jnp.int32), None))
-                base = product(early_keys, q_ref[late_at])
-                scores = []
-                for j, half, mask in pairs:
-                    s = product(rows_of(j, half, k_at), q_ref[state_at(i, half, h)])
-                    scores.append(s if mask is None else jnp.where(mask, s, MASKED))
-                tops = [jnp.max(s, axis=0, keepdims=True) for s in scores]
-                highs = []
-                for side in range(2):
-                    some = [jnp.where(half == side, top, MASKED) for (_, half, _), top in zip(pairs, tops)]
-                    if side == 1:
-                        some.append(jnp.max(base, axis=0, keepdims=True))
-                    if carried is not None:
-                        some.append(carried[0][side])
-                    highs.append(functools.reduce(jnp.maximum, some))
-                weights = [
-                    weigh(s, jnp.where(half == 1, highs[1], highs[0]))
-                    for (_, half, _), s in zip(pairs, scores)
-                ]
-                values = turned_values([rows_of(j, half, v_at) for j, half, _ in pairs])
-                zero = jnp.zeros_like(weights[0])
-                for side, at in ((0, early_at), (1, late_at)):
-                    chosen = [
-                        jnp.where(half == side, w, zero) for (_, half, _), w in zip(pairs, weights)
-                    ]
-                    sums = product(values, jnp.concatenate(chosen, axis=0))
-                    if side == 1:
-                        sums = sums + product(early_values, weigh(base, highs[1]))
-                    if carried is not None:
-                        shrink = jnp.exp2((carried[0][side] - highs[side]) * EXP2_SCALE)
-                        sums = sums + carried[1][side] * shrink
-                    high_ref[at] = highs[side]
-                    sums_ref[at] = sums
-                    if plan["last"] and first + 6 >= count:
-                        mixed = sums[:HEAD_WIDTH] * (1.0 / sums[HEAD_WIDTH : HEAD_WIDTH + 1])
-                        mixed = jnp.transpose(mixed.astype(out_refs[i].dtype))
-                        for g in range(QUERY_PER_KEY):
-                            out_refs[i][
-                                side * chunk : (side + 1) * chunk,
-                                h * GROUP + g * HEAD_WIDTH : h * GROUP + (g + 1) * HEAD_WIDTH,
-                            ] = mixed[g * chunk : (g + 1) * chunk]
+
+        def run(heads_at_once, group=group):
+            chains = []
+            for h in heads_at_once:
+                shared = {}
+                chains += [one_chain(group, h, i, shared) for i in range(owners)]
+            staggered(chains)
+
+        if fetch:
+
+            def one_head(h, carry):
+                run([h])
+                return carry
+
+            lax.fori_loop(0, heads, one_head, 0)
+        else:
+            run(range(heads))
     for copy in copies:
         copy.wait()
 
@@ -240,10 +273,12 @@
     )(*queries)
 
 
-def project_kernel(following, own_ref, other_ref, held_ref, *refs):
-    if following:
-        w_ref, sent_ref, kept_ref, next_ref, rows_ref, sems = refs
-        copies = fetch_columns(w_ref, following[0], next_ref, sems, 0)
+def project_kernel(bring, own_ref, other_ref, held_ref, *refs):
+    copies = []
+    if bring:
+        w_ref, sent_ref, kept_ref, *next_refs, rows_ref, sems = refs
+        for n, ((first, _), next_ref) in enumerate(zip(bring, next_refs)):
+            copies += fetch_columns(w_ref, first, next_ref, sems, n * PIECES)
     else:
         sent_ref, kept_ref, rows_ref = refs
     chunk, part = sent_ref.shape[0], own_ref.shape[1]
@@ -258,44 +293,46 @@
     both = product(rows_ref[...], held_ref[...]).astype(sent_ref.dtype)
     sent_ref[...] = both[:chunk]
     kept_ref[...] = both[chunk:]
-    if following:
-        for copy in copies:
-            copy.wait()
-
-
-def project(own, other, held, out_weight, following):
+    for copy in copies:
+        copy.wait()
+
+
+def project(own, other, held, out_weight, bring):
     rows, (depth, width) = own.shape[0], held.shape
     vmem = pl.BlockSpec(memory_space=pltpu.VMEM)
     out_shape = [jax.ShapeDtypeStruct((rows // 2, width), jnp.bfloat16)] * 2
+    out_shape += [jax.ShapeDtypeStruct((depth, columns), held.dtype) for _, columns in bring]
     in_specs, operands = [vmem] * 3, [own, other, held]
     scratch = [pltpu.VMEM((rows, depth), jnp.bfloat16)]
-    if following:
-        out_shape.append(jax.ShapeDtypeStruct((depth, following[1]), held.dtype))
+    if bring:
         in_specs.append(pl.BlockSpec(memory_space=pltpu.HBM))
         operands.append(out_weight)
-        scratch.append(pltpu.SemaphoreType.DMA((PIECES,)))
+        scratch.append(pltpu.SemaphoreType.DMA((PIECES * len(bring),)))
     return pl.pallas_call(
-        functools.partial(project_kernel, following),
+        functools.partial(project_kernel, bring),
         out_shape=out_shape,
         in_specs=in_specs,
         out_specs=[vmem] * len(out_shape),
         scratch_shapes=scratch,
-        cost_estimate=pl.CostEstimate(
-            flops=2 * rows * depth * width, bytes_accessed=2 * depth * width, transcendentals=0
-        ),
+        cost_estimate=pl.CostEstimate(flops=1 << 10, bytes_accessed=1 << 10, transcendentals=0),
         compiler_params=pltpu.CompilerParams(vmem_limit_bytes=VMEM_LIMIT),
         name="project",
     )(*operands)
 
 
-def prepare_kernel(chunk, k_ref, v_ref, position_ref, sent_ref, kept_ref, mark_ref, first_ref, sems):
+def prepare_kernel(
+    chunk, q_ref, k_ref, v_ref, position_ref, sent_ref, kept_ref, mark_ref, query_ref, first_ref, sems
+):
     rows, width = k_ref.shape[0], k_ref.shape[1] // 2
+    columns = query_ref.shape[1]
     copies = [pltpu.make_async_copy(position_ref, first_ref, sems.at[4])]
     for n, (ref, core) in enumerate(((sent_ref, 1 - my_core()), (kept_ref, my_core()))):
         at = pl.ds(pl.multiple_of(core * width, width), width)
         for m, source in enumerate((k_ref, v_ref)):
             to = ref.at[pl.ds(0, rows), pl.ds(m * width, width)]
             copies.append(pltpu.make_async_copy(source.at[:, at], to, sems.at[2 * n + m]))
+    at = pl.ds(pl.multiple_of((1 - my_core()) * columns, columns), columns)
+    copies.append(pltpu.make_async_copy(q_ref.at[:, at], query_ref, sems.at[5]))
     for copy in copies:
         copy.start()
     copies[0].wait()
@@ -306,27 +343,58 @@
         copy.wait()
 
 
-def prepare(keys, values, positions):
+def prepare(queries, keys, values, positions):
     vmem = pl.BlockSpec(memory_space=pltpu.VMEM)
     hbm = pl.BlockSpec(memory_space=pltpu.HBM)
     rows, width = keys.shape
-    operands = [pltpu.with_memory_space_constraint(x, pltpu.HBM) for x in (keys, values, positions)]
+    operands = [pltpu.with_memory_space_constraint(x, pltpu.HBM) for x in (queries, keys, values, positions)]
     return pl.pallas_call(
         functools.partial(prepare_kernel, rows // 2),
         out_shape=[
             jax.ShapeDtypeStruct((rows + HEADER, width), jnp.bfloat16),
             jax.ShapeDtypeStruct((rows, width), jnp.bfloat16),
             jax.ShapeDtypeStruct((HEADER, width // 2), jnp.bfloat16),
+            jax.ShapeDtypeStruct((rows, queries.shape[1] // 2), jnp.bfloat16),
         ],
-        in_specs=[hbm, hbm, hbm],
-        out_specs=[vmem, vmem, vmem],
+        in_specs=[hbm] * 4,
+        out_specs=[vmem] * 4,
         scratch_shapes=[
             pltpu.SMEM(positions.shape, jnp.int32),
-            pltpu.SemaphoreType.DMA((5,)),
+            pltpu.SemaphoreType.DMA((6,)),
         ],
         compiler_params=pltpu.CompilerParams(vmem_limit_bytes=VMEM_LIMIT),
         name="prepare",
     )(*operands)
+
+
+def finish_kernel(first, pairs, *refs):
+    out_ref, total_ref, sem = refs[-3:]
+    at = 0
+    for mine, theirs in zip(refs[:pairs], refs[pairs : 2 * pairs]):
+        width = mine.shape[1]
+        total = mine[...].astype(jnp.float32) + theirs[...].astype(jnp.float32)
+        total_ref[:, at : at + width] = total.astype(total_ref.dtype)
+        at += width
+    copy = pltpu.make_async_copy(total_ref, out_ref.at[:, pl.ds(first, at)], sem)
+    copy.start()
+    copy.wait()
+
+
+def finish(kept, received, first, columns, written=None):
+    vmem, hbm = pl.BlockSpec(memory_space=pltpu.VMEM), pl.BlockSpec(memory_space=pltpu.HBM)
+    rows, width = kept[0].shape[0], sum(part.shape[1] for part in kept)
+    pairs = len(kept)
+    return pl.pallas_call(
+        functools.partial(finish_kernel, first, pairs),
+        out_shape=jax.ShapeDtypeStruct((rows, columns), kept[0].dtype),
+        in_specs=[vmem] * (2 * pairs) + ([] if written is None else [hbm]),
+        out_specs=hbm,
+        input_output_aliases={} if written is None else {2 * pairs: 0},
+        scratch_shapes=[pltpu.VMEM((rows, width), kept[0].dtype), pltpu.SemaphoreType.DMA],
+        cost_estimate=pl.CostEstimate(flops=1 << 10, bytes_accessed=1 << 10, transcendentals=0),
+        compiler_params=pltpu.CompilerParams(vmem_limit_bytes=VMEM_LIMIT),
+        name="finish",
+    )(*kept, *received, *([] if written is None else [written]))
 
 
 def after(value, *events):
@@ -343,13 +411,10 @@
     up = lambda x: lax.ppermute(x, "blk", clock)
     down = lambda x: lax.ppermute(x, "blk", counter)
 
-    sent, x, mark = prepare(keys, values, positions)
+    sent, x, mark, q_sent = prepare(queries, keys, values, positions)
     got = lax.ppermute(sent, "blk", sibling)
     y = jnp.concatenate(
         [got[:rows], jnp.concatenate([mark, got[rows:, :width]], axis=1)], axis=0
-    )
-    q_sent = lax.dynamic_slice(
-        queries, (0, (1 - my_core()) * heads * GROUP), (rows, heads * GROUP)
     )
     q_got = lax.ppermute(q_sent, "blk", sibling)
     turned = turn(heads, chunk, (True, False), [queries, q_got])
@@ -378,7 +443,9 @@
             y_up, y_down, *state = lax.optimization_barrier((y_up, y_down, *state))
         ups, downs = (up(x_up), up(y_up)), (down(x_down), down(y_down))
         if r == 1:
-            *state, first, second = call([(x, y)], None, own=True, fetch=fetch)
+            *state, held = call([(x, y)], None, own=True, fetch=fetch[:1])
+        elif r == 2:
+            *state, more = call(arrived, state, fetch=fetch[1:])
         else:
             state = call(arrived, state)
         arrived = [ups, downs]
@@ -386,7 +453,7 @@
     far = (up(x_up), down(y_down))
     state = call(arrived, state)
     own, theirs = call([far], state, last=True)
-    return own, lax.ppermute(theirs, "blk", sibling), [first, second]
+    return own, lax.ppermute(theirs, "blk", sibling), [held, more]
 
 
 def one_head_a_device(count, queries, keys, values, positions):
@@ -424,23 +491,23 @@
             partial.astype(jnp.bfloat16), "inner", scatter_dimension=0, tiled=True
         )
     out_weight = pltpu.with_memory_space_constraint(out_weight, pltpu.HBM)
-    shares = (5, 5, 6, 4)
+    shares = (10, 9, 8, 7, 6)
     widths = [out_weight.shape[1] * share // sum(shares) for share in shares]
     cuts = [(sum(widths[:j]), columns) for j, columns in enumerate(widths)]
     own, other, held = split_over_cores(
         count, queries, keys, values, positions, out_weight, cuts[:2]
     )
-    received, kept, source = [], [], own
+    bring = [cuts[j + 1 : j + 2] if j > 0 else [] for j in range(len(cuts))]
+    received, kept = [], []
     for j in range(len(cuts)):
-        if j > 0:
-            source = after(own, sent, *received[: j - 1][-1:])
-        following = cuts[j + 1] if 0 < j < len(cuts) - 1 else None
-        sent, keep, *rest = project(source, other, held[j], out_weight, following)
+        source = own if j == 0 else after(own, sent)
+        sent, keep, *rest = project(source, other, held[j], out_weight, bring[j])
         held += rest
         received.append(lax.ppermute(sent, "inner", [(0, 1), (1, 0)]))
         kept.append(keep)
-    mine, theirs = jnp.concatenate(kept, axis=1), jnp.concatenate(received, axis=1)
-    return (mine.astype(jnp.float32) + theirs.astype(jnp.float32)).astype(jnp.bfloat16)
+    columns = out_weight.shape[1]
+    result = finish(kept[:-1], received[:-1], 0, columns)
+    return finish(kept[-1:], received[-1:], cuts[-1][0], columns, result)
 
 
 def solution(mesh):

time: 72.3 us -> 69.6 us (0.963)
  Pallas kernels: 29.4 us -> 26.8 us
  other arithmetic: 1.21 us -> 0.02 us
  starting transfers between devices: 21.3 us -> 22.1 us
    pallas_call x5, Pallas kernels: 18.7 us -> 12.7 us  [attend(): pl.pallas_call(functools.partial(attend_kernel, plan), out_shape=out_shap...]
    pallas_call x4 -> x7, Pallas kernels: 9.17 us -> 12.5 us  [the longest x5 10.7 us: project(): pl.pallas_call(functools.partial(project_kernel, bring), out_shape=out_sh...]
    ppermute x4 -> x5, waiting for transfers between devices: 10.6 us -> 7.61 us  [shards(): received.append(lax.ppermute(sent, 'inner', [(0, 1), (1, 0)]))]
    ppermute x7, starting transfers between devices: 0.18 us -> 2.73 us  [split_over_cores(): down = lambda x: lax.ppermute(x, 'blk', counter)]
    ppermute x7, starting transfers between devices: 14.9 us -> 12.8 us  [split_over_cores(): up = lambda x: lax.ppermute(x, 'blk', clock)]
    ppermute x7, waiting for transfers between devices: 5.35 us -> 7.17 us  [split_over_cores(): down = lambda x: lax.ppermute(x, 'blk', counter)]
    unnamed x2, local copies, waits for them, and re-layouts: 0.01 us -> 1.2 us
    convert_element_type x1 -> x0, other arithmetic: 1.2 us -> none  [shards(): (mine.astype(jnp.float32) + theirs.astype(jnp.float32)).astype(jnp.bfloat16)]
  transfers between devices with their start and end apart: 21 -> 22, of which waited for: 8 -> 11; matrix products, arithmetic and copies ran while one was open for 2% -> 0% of each run, Pallas kernels for 34% -> 31%
where the time goes in v9:
time: 69.6 us; the launch traced here: 69.4 us
  Pallas kernels  26.8 us (39%)
  starting transfers between devices  22.1 us (32%)
  waiting for transfers between devices  19 us (27%)
  local copies, waits for them, and re-layouts  1.22 us (2%)
    ppermute x7, starting transfers between devices, split_over_cores(): up = lambda x: lax.ppermute(x, 'blk', clock)  12.8 us
    pallas_call x5, Pallas kernels, attend(): pl.pallas_call(functools.partial(attend_kernel, plan), out_shape=out_shap...  12.7 us
    pallas_call x5, Pallas kernels, project(): pl.pallas_call(functools.partial(project_kernel, bring), out_shape=out_sh...  10.7 us
    ppermute x5, waiting for transfers between devices, shards(): received.append(lax.ppermute(sent, 'inner', [(0, 1), (1, 0)]))  7.61 us
    ppermute x7, waiting for transfers between devices, split_over_cores(): down = lambda x: lax.ppermute(x, 'blk', counter)  7.17 us
    ppermute x5, starting transfers between devices, shards(): received.append(lax.ppermute(sent, 'inner', [(0, 1), (1, 0)]))  5.87 us
    ppermute x7, starting transfers between devices, split_over_cores(): down = lambda x: lax.ppermute(x, 'blk', counter)  2.73 us
    ppermute x1, waiting for transfers between devices, split_over_cores(): return (own, lax.ppermute(theirs, 'blk', sibling), [held, more])  1.85 us
  transfers between devices with their start and end apart: 22, of which 11 were waited for; matrix products, arithmetic and copies ran while one was open for 0% of the time, Pallas kernels for 31%

profile of v9, /device:TPU:0, one launch (start us, length us, event | category | flops | bytes accessed | tf_op | source)
XLA Modules:
  0.0 69.4 jit_solution(3557596082145427369)
XLA Ops:
  0.0 1.3 %prepare.1 = (bf16[208,512]{1,0:T(8,128)(2,1)S(1)}, bf16[192,512]{1,0:T(8,128)(2,1)S(1)}, bf16[16,256]{1,0:T(8,128)(2,1)S(1)}, bf16[192,1280]{1,0:T(8,128)(2,1)S(1)}) custom-call(bf16[192,2560]{1,0:T(8,128)(2,1)} %refs_0_.4, bf16[192,512]{1,0:T(8,128)(2,1)} %k_ref.1, bf16[192,512]{1,0:T(8,128)(2,1)} %v_ref.1, s32[192]{0:T(256)} %position_ref.1), custom_call_target="tpu_custom_call" | custom-call | tf_op jit(solution)/shard_map/prepare/pallas_call | solution.py:351
  1.3 0.5 collective-permute-start.1
  1.8 0.1 collective-permute-start
  1.9 1.0 %collective-permute-done.1 = bf16[208,512]{1,0:T(8,128)(2,1)S(1)} collective-permute-done((bf16[208,512]{1,0:T(8,128)(2,1)S(1)}, bf16[208,512]{1,0:T(8,128)(2,1)S(1)}, u32[]{:S(2)}, u32[]{:S(2)}) %collective-permute-start.1) | collective-permute-done | bytes 213024 | tf_op jit(solution)/shard_map/ppermute | solution.py:415
  3.0 3.0 %collective-permute-start.5 = (bf16[208,512]{1,0:T(8,128)(2,1)S(1)}, bf16[208,512]{1,0:T(8,128)(2,1)S(1)}, u32[]{:S(2)}, u32[]{:S(2)}) collective-permute-start(bf16[208,512]{1,0:T(8,128)(2,1)S(1)} %maximum_maximum_fusion.refs_1_.refs_3_), channel_id=1, source_target_pairs={{0,8},{2,10},{8,16},{10,18},{16,24},{18,26},{24,28},{26,30},{28,20... | collective-permute-start | bytes 638984 | tf_op jit(solution)/shard_map/ppermute | solution.py:411
  5.9 0.0 collective-permute-start.6
  6.0 2.0 %collective-permute-start.2 = (bf16[192,512]{1,0:T(8,128)(2,1)S(1)}, bf16[192,512]{1,0:T(8,128)(2,1)S(1)}, u32[]{:S(2)}, u32[]{:S(2)}) collective-permute-start(bf16[192,512]{1,0:T(8,128)(2,1)S(1)} %get-tuple-element.53.refs_2_), channel_id=1, source_target_pairs={{0,8},{2,10},{8,16},{10,18},{16,24},{18,26},{24,28},{26,30},{28,20... | collective-permute-start | bytes 589832 | tf_op jit(solution)/shard_map/ppermute | solution.py:411
  8.0 1.2 %copy-done = bf16[192,2560]{1,0:T(8,128)(2,1)S(1)} copy-done((bf16[192,2560]{1,0:T(8,128)(2,1)S(1)}, bf16[192,2560]{1,0:T(8,128)(2,1)}, u32[]{:S(2)}) %copy-start) | copy-done | bytes 983064
  9.2 0.3 turn.1.refs_0_
  9.5 3.0 %attend.5 = (f32[8,1,480]{2,1,0:T(1,128)S(1)}, f32[8,144,480]{2,1,0:T(8,128)S(1)}, bf16[2560,1280]{1,0:T(8,128)(2,1)S(1)}) custom-call(bf16[8,128,480]{2,1,0:T(8,128)(2,1)S(1)} %turn.1.refs_0_, bf16[208,512]{1,0:T(8,128)(2,1)S(1)} %maximum_maximum_fusion.refs_1_.refs_3_, bf16[192,512]{1,0:T(8,128)(2,1)S(1)} %get-tuple-element.53.refs_2_, ...), custom_call_target="tpu_custom_call" | custom-call | flops 377487360 | bytes 4194304 | tf_op jit(solution)/shard_map/attend/pallas_call | solution.py:231
  12.5 1.6 %collective-permute-done.6.refs_5_ = bf16[208,512]{1,0:T(8,128)(2,1)S(1)} collective-permute-done((bf16[208,512]{1,0:T(8,128)(2,1)S(1)}, bf16[208,512]{1,0:T(8,128)(2,1)S(1)}, u32[]{:S(2)}, u32[]{:S(2)}) %collective-permute-start.6) | collective-permute-done | bytes 213024 | tf_op jit(solution)/shard_map/ppermute | solution.py:412
  14.1 1.6 %collective-permute-start.7 = (bf16[208,512]{1,0:T(8,128)(2,1)S(1)}, bf16[208,512]{1,0:T(8,128)(2,1)S(1)}, u32[]{:S(2)}, u32[]{:S(2)}) collective-permute-start(bf16[208,512]{1,0:T(8,128)(2,1)S(1)} %collective-permute-done.5.refs_3_), channel_id=1, source_target_pairs={{0,8},{2,10},{8,16},{10,18},{16,24},{18,26},{24,28},{26,30},{28,20... | collective-permute-start | bytes 638984 | tf_op jit(solution)/shard_map/ppermute | solution.py:411
  15.7 0.4 collective-permute-start.8
  16.1 0.0 collective-permute-done.2.refs_2_
  16.1 2.1 %collective-permute-start.3 = (bf16[192,512]{1,0:T(8,128)(2,1)S(1)}, bf16[192,512]{1,0:T(8,128)(2,1)S(1)}, u32[]{:S(2)}, u32[]{:S(2)}) collective-permute-start(bf16[192,512]{1,0:T(8,128)(2,1)S(1)} %collective-permute-done.2.refs_2_), channel_id=1, source_target_pairs={{0,8},{2,10},{8,16},{10,18},{16,24},{18,26},{24,28},{26,30},{28,20... | collective-permute-start | bytes 589832 | tf_op jit(solution)/shard_map/ppermute | solution.py:411
  18.3 0.0 collective-permute-done.9.refs_4_
  18.3 3.1 %attend.6 = (f32[8,1,480]{2,1,0:T(1,128)S(1)}, f32[8,144,480]{2,1,0:T(8,128)S(1)}, bf16[2560,1152]{1,0:T(8,128)(2,1)S(1)}) custom-call(bf16[8,128,480]{2,1,0:T(8,128)(2,1)S(1)} %turn.1.refs_0_, bf16[208,512]{1,0:T(8,128)(2,1)S(1)} %maximum_maximum_fusion.refs_1_.refs_3_, bf16[192,512]{1,0:T(8,128)(2,1)S(1)} %collective-permute-done.2.refs_2_, ...), custom_call_target="tpu_custom_call" | custom-call | flops 754974720 | bytes 4194304 | tf_op jit(solution)/shard_map/attend/pallas_call | solution.py:231
  21.4 0.9 %collective-permute-done.7.refs_3_ = bf16[208,512]{1,0:T(8,128)(2,1)S(1)} collective-permute-done((bf16[208,512]{1,0:T(8,128)(2,1)S(1)}, bf16[208,512]{1,0:T(8,128)(2,1)S(1)}, u32[]{:S(2)}, u32[]{:S(2)}) %collective-permute-start.7) | collective-permute-done | bytes 213024 | tf_op jit(solution)/shard_map/ppermute | solution.py:411
  22.3 1.6 %collective-permute-done.8.refs_5_ = bf16[208,512]{1,0:T(8,128)(2,1)S(1)} collective-permute-done((bf16[208,512]{1,0:T(8,128)(2,1)S(1)}, bf16[208,512]{1,0:T(8,128)(2,1)S(1)}, u32[]{:S(2)}, u32[]{:S(2)}) %collective-permute-start.8) | collective-permute-done | bytes 213024 | tf_op jit(solution)/shard_map/ppermute | solution.py:412
  23.9 0.4 collective-permute-start.10
  24.3 0.1 collective-permute-done.3.refs_2_
  24.4 1.8 %collective-permute-start.4 = (bf16[192,512]{1,0:T(8,128)(2,1)S(1)}, bf16[192,512]{1,0:T(8,128)(2,1)S(1)}, u32[]{:S(2)}, u32[]{:S(2)}) collective-permute-start(bf16[192,512]{1,0:T(8,128)(2,1)S(1)} %collective-permute-done.3.refs_2_), channel_id=1, source_target_pairs={{0,8},{2,10},{8,16},{10,18},{16,24},{18,26},{24,28},{26,30},{28,20... | collective-permute-start | bytes 589832 | tf_op jit(solution)/shard_map/ppermute | solution.py:411
  26.2 1.8 %collective-permute-done.11.refs_4_ = bf16[192,512]{1,0:T(8,128)(2,1)S(1)} collective-permute-done((bf16[192,512]{1,0:T(8,128)(2,1)S(1)}, bf16[192,512]{1,0:T(8,128)(2,1)S(1)}, u32[]{:S(2)}, u32[]{:S(2)}) %collective-permute-start.11) | collective-permute-done | bytes 196640 | tf_op jit(solution)/shard_map/ppermute | solution.py:412
  28.1 0.4 collective-permute-start.15
  28.5 1.6 %collective-permute-start.14 = (bf16[208,512]{1,0:T(8,128)(2,1)S(1)}, bf16[208,512]{1,0:T(8,128)(2,1)S(1)}, u32[]{:S(2)}, u32[]{:S(2)}) collective-permute-start(bf16[208,512]{1,0:T(8,128)(2,1)S(1)} %collective-permute-done.7.refs_3_), channel_id=1, source_target_pairs={{0,8},{2,10},{8,16},{10,18},{16,24},{18,26},{24,28},{26,30},{28,20... | collective-permute-start | bytes 638984 | tf_op jit(solution)/shard_map/ppermute | solution.py:411
  30.1 2.5 %attend.7 = (f32[8,1,480]{2,1,0:T(1,128)S(1)}, f32[8,144,480]{2,1,0:T(8,128)S(1)}) custom-call(bf16[8,128,480]{2,1,0:T(8,128)(2,1)S(1)} %turn.1.refs_0_, bf16[208,512]{1,0:T(8,128)(2,1)S(1)} %maximum_maximum_fusion.refs_1_.refs_3_, bf16[192,512]{1,0:T(8,128)(2,1)S(1)} %collective-permute-done.3.refs_2_, bf16[208,512]{1,0:T(8,128)(2,1)S(1)} %collective-permute-done.7.refs_3_, ...), custom_call_target="tpu_custom_call" | custom-call | flops 754974720 | bytes 4194304 | tf_op jit(solution)/shard_map/attend/pallas_call | solution.py:231
  32.6 1.4 %collective-permute-start.13 = (bf16[208,512]{1,0:T(8,128)(2,1)S(1)}, bf16[208,512]{1,0:T(8,128)(2,1)S(1)}, u32[]{:S(2)}, u32[]{:S(2)}) collective-permute-start(bf16[208,512]{1,0:T(8,128)(2,1)S(1)} %collective-permute-done.10.refs_5_), channel_id=1, source_target_pairs={{0,4},{2,6},{8,0},{10,2},{16,8},{18,10},{24,16},{26,18},{28,24},{3... | collective-permute-start | bytes 638984 | tf_op jit(solution)/shard_map/ppermute | solution.py:412
  34.0 0.7 %collective-permute-start.12 = (bf16[192,512]{1,0:T(8,128)(2,1)S(1)}, bf16[192,512]{1,0:T(8,128)(2,1)S(1)}, u32[]{:S(2)}, u32[]{:S(2)}) collective-permute-start(bf16[192,512]{1,0:T(8,128)(2,1)S(1)} %collective-permute-done.4.refs_2_), channel_id=1, source_target_pairs={{0,8},{2,10},{8,16},{10,18},{16,24},{18,26},{24,28},{26,30},{28,20... | collective-permute-start | bytes 589832 | tf_op jit(solution)/shard_map/ppermute | solution.py:411
  34.7 2.1 %collective-permute-done.15.refs_4_ = bf16[192,512]{1,0:T(8,128)(2,1)S(1)} collective-permute-done((bf16[192,512]{1,0:T(8,128)(2,1)S(1)}, bf16[192,512]{1,0:T(8,128)(2,1)S(1)}, u32[]{:S(2)}, u32[]{:S(2)}) %collective-permute-start.15) | collective-permute-done | bytes 196640 | tf_op jit(solution)/shard_map/ppermute | solution.py:412
  36.9 2.5 %attend.8 = (f32[8,1,480]{2,1,0:T(1,128)S(1)}, f32[8,144,480]{2,1,0:T(8,128)S(1)}) custom-call(bf16[8,128,480]{2,1,0:T(8,128)(2,1)S(1)} %turn.1.refs_0_, bf16[208,512]{1,0:T(8,128)(2,1)S(1)} %maximum_maximum_fusion.refs_1_.refs_3_, bf16[192,512]{1,0:T(8,128)(2,1)S(1)} %collective-permute-done.4.refs_2_, ...), custom_call_target="tpu_custom_call" | custom-call | flops 754974720 | bytes 4194304 | tf_op jit(solution)/shard_map/attend/pallas_call | solution.py:231
  39.4 0.3 collective-permute-done.12.refs_2_
  39.7 1.6 %attend.9 = (bf16[192,1280]{1,0:T(8,128)(2,1)S(1)}, bf16[192,1280]{1,0:T(8,128)(2,1)S(1)}) custom-call(bf16[8,128,480]{2,1,0:T(8,128)(2,1)S(1)} %turn.1.refs_0_, bf16[208,512]{1,0:T(8,128)(2,1)S(1)} %maximum_maximum_fusion.refs_1_.refs_3_, bf16[192,512]{1,0:T(8,128)(2,1)S(1)} %collective-permute-done.12.refs_2_, ...), custom_call_target="tpu_custom_call" | custom-call | flops 377487360 | bytes 4194304 | tf_op jit(solution)/shard_map/attend/pallas_call | solution.py:231
  41.3 0.1 collective-permute-start.16
  41.4 1.9 %collective-permute-done.16.other_ref = bf16[192,1280]{1,0:T(8,128)(2,1)S(1)} collective-permute-done((bf16[192,1280]{1,0:T(8,128)(2,1)S(1)}, bf16[192,1280]{1,0:T(8,128)(2,1)S(1)}, u32[]{:S(2)}, u32[]{:S(2)}) %collective-permute-start.16) | collective-permute-done | bytes 491552 | tf_op jit(solution)/shard_map/ppermute | solution.py:456
  43.3 1.4 %project.5 = (bf16[96,1280]{1,0:T(8,128)(2,1)S(1)}, bf16[96,1280]{1,0:T(8,128)(2,1)S(1)}) custom-call(bf16[192,1280]{1,0:T(8,128)(2,1)S(1)} %get-tuple-element.87.own_ref, bf16[192,1280]{1,0:T(8,128)(2,1)S(1)} %collective-permute-done.16.other_ref, bf16[2560,1280]{1,0:T(8,128)(2,1)S(1)} %get-tuple-element.76.held_ref), custom_call_target="tpu_custom_call" | custom-call | flops 1024 | bytes 1024 | tf_op jit(solution)/shard_map/project/pallas_call | solution.py:311
  44.7 1.6 %collective-permute-start.18 = (bf16[96,1280]{1,0:T(8,128)(2,1)S(1)}, bf16[96,1280]{1,0:T(8,128)(2,1)S(1)}, u32[]{:S(2)}, u32[]{:S(2)}) collective-permute-start(bf16[96,1280]{1,0:T(8,128)(2,1)S(1)} %get-tuple-element.77), channel_id=1, source_target_pairs={{0,1},{1,0},{2,3},{3,2},{4,5},{5,4},{6,7},{7,6},{8,9},{9,8},{10,11... | collective-permute-start | bytes 737288 | tf_op jit(solution)/shard_map/ppermute | solution.py:506
  46.3 3.1 %project.6 = (bf16[96,1152]{1,0:T(8,128)(2,1)S(1)}, bf16[96,1152]{1,0:T(8,128)(2,1)S(1)}, bf16[2560,1024]{1,0:T(8,128)(2,1)S(1)}) custom-call(bf16[192,1280]{1,0:T(8,128)(2,1)S(1)} %get-tuple-element.87.own_ref, bf16[192,1280]{1,0:T(8,128)(2,1)S(1)} %collective-permute-done.16.other_ref, bf16[2560,1152]{1,0:T(8,128)(2,1)S(1)} %get-tuple-element.79.held_ref, ...), custom_call_target="tpu_custom_call" | custom-call | flops 1024 | bytes 1024 | tf_op jit(solution)/shard_map/project/pallas_call | solution.py:311
  49.4 0.6 collective-permute-start.19
  50.0 2.5 %project.7 = (bf16[96,1024]{1,0:T(8,128)(2,1)S(1)}, bf16[96,1024]{1,0:T(8,128)(2,1)S(1)}, bf16[2560,896]{1,0:T(8,128)(2,1)S(1)}) custom-call(bf16[192,1280]{1,0:T(8,128)(2,1)S(1)} %get-tuple-element.87.own_ref, bf16[192,1280]{1,0:T(8,128)(2,1)S(1)} %collective-permute-done.16.other_ref, bf16[2560,1024]{1,0:T(8,128)(2,1)S(1)} %get-tuple-element.82.held_ref, ...), custom_call_target="tpu_custom_call" | custom-call | flops 1024 | bytes 1024 | tf_op jit(solution)/shard_map/project/pallas_call | solution.py:311
  52.5 1.6 %collective-permute-start.20 = (bf16[96,1024]{1,0:T(8,128)(2,1)S(1)}, bf16[96,1024]{1,0:T(8,128)(2,1)S(1)}, u32[]{:S(2)}, u32[]{:S(2)}) collective-permute-start(bf16[96,1024]{1,0:T(8,128)(2,1)S(1)} %get-tuple-element.83), channel_id=1, source_target_pairs={{0,1},{1,0},{2,3},{3,2},{4,5},{5,4},{6,7},{7,6},{8,9},{9,8},{10,11... | collective-permute-start | bytes 589832 | tf_op jit(solution)/shard_map/ppermute | solution.py:506
  54.0 2.7 %project.8 = (bf16[96,896]{1,0:T(8,128)(2,1)S(1)}, bf16[96,896]{1,0:T(8,128)(2,1)S(1)}, bf16[2560,768]{1,0:T(8,128)(2,1)S(1)}) custom-call(bf16[192,1280]{1,0:T(8,128)(2,1)S(1)} %get-tuple-element.87.own_ref, bf16[192,1280]{1,0:T(8,128)(2,1)S(1)} %collective-permute-done.16.other_ref, bf16[2560,896]{1,0:T(8,128)(2,1)S(1)} %get-tuple-element.85.held_ref, ...), custom_call_target="tpu_custom_call" | custom-call | flops 1024 | bytes 1024 | tf_op jit(solution)/shard_map/project/pallas_call | solution.py:311
  56.7 0.6 collective-permute-start.21
  57.4 0.9 %project.9 = (bf16[96,768]{1,0:T(8,128)(2,1)S(1)}, bf16[96,768]{1,0:T(8,128)(2,1)S(1)}) custom-call(bf16[192,1280]{1,0:T(8,128)(2,1)S(1)} %get-tuple-element.87.own_ref, bf16[192,1280]{1,0:T(8,128)(2,1)S(1)} %collective-permute-done.16.other_ref, bf16[2560,768]{1,0:T(8,128)(2,1)S(1)} %get-tuple-element.88.held_ref), custom_call_target="tpu_custom_call" | custom-call | flops 1024 | bytes 1024 | tf_op jit(solution)/shard_map/project/pallas_call | solution.py:311
  58.3 1.6 %collective-permute-start.17 = (bf16[96,768]{1,0:T(8,128)(2,1)S(1)}, bf16[96,768]{1,0:T(8,128)(2,1)S(1)}, u32[]{:S(2)}, u32[]{:S(2)}) collective-permute-start(bf16[96,768]{1,0:T(8,128)(2,1)S(1)} %get-tuple-element.90), channel_id=1, source_target_pairs={{0,1},{1,0},{2,3},{3,2},{4,5},{5,4},{6,7},{7,6},{8,9},{9,8},{10,11... | collective-permute-start | bytes 442376 | tf_op jit(solution)/shard_map/ppermute | solution.py:506
  59.8 6.4 %collective-permute-done.21.refs_7_ = bf16[96,896]{1,0:T(8,128)(2,1)S(1)} collective-permute-done((bf16[96,896]{1,0:T(8,128)(2,1)S(1)}, bf16[96,896]{1,0:T(8,128)(2,1)S(1)}, u32[]{:S(2)}, u32[]{:S(2)}) %collective-permute-start.21) | collective-permute-done | bytes 172064 | tf_op jit(solution)/shard_map/ppermute | solution.py:506
  66.2 1.1 %finish.2.refs_2_ = bf16[96,5120]{1,0:T(8,128)(2,1)} custom-call(bf16[96,1280]{1,0:T(8,128)(2,1)S(1)} %get-tuple-element.91.refs_0_, bf16[96,1152]{1,0:T(8,128)(2,1)S(1)} %get-tuple-element.92.refs_1_, bf16[96,1024]{1,0:T(8,128)(2,1)S(1)} %get-tuple-element.93.refs_2_, bf16[96,896]{1,0:T(8,128)(2,1)S(1)} %get-tuple-element.94.refs_3_, ...), custom_call_target="tpu_custom_call" | custom-call | flops 1024 | bytes 1024 | tf_op jit(solution)/shard_map/finish/pallas_call | solution.py:387
  67.3 1.2 %collective-permute-done.17.refs_1_ = bf16[96,768]{1,0:T(8,128)(2,1)S(1)} collective-permute-done((bf16[96,768]{1,0:T(8,128)(2,1)S(1)}, bf16[96,768]{1,0:T(8,128)(2,1)S(1)}, u32[]{:S(2)}, u32[]{:S(2)}) %collective-permute-start.17) | collective-permute-done | bytes 147488 | tf_op jit(solution)/shard_map/ppermute | solution.py:506
  68.6 0.7 %finish.3 = bf16[96,5120]{1,0:T(8,128)(2,1)} custom-call(bf16[96,768]{1,0:T(8,128)(2,1)S(1)} %get-tuple-element.89.refs_0_, bf16[96,768]{1,0:T(8,128)(2,1)S(1)} %collective-permute-done.17.refs_1_, bf16[96,5120]{1,0:T(8,128)(2,1)} %finish.2.refs_2_), custom_call_target="tpu_custom_call", output_to_operand_aliasing={{}: (2, {})} | custom-call | flops 1024 | bytes 1024 | tf_op jit(solution)/shard_map/finish/pallas_call | solution.py:387
  (15 shorter events, 0.1 us)
Async XLA Ops:
  1.3 1.6 %collective-permute-start.1 = (bf16[208,512]{1,0:T(8,128)(2,1)S(1)}, bf16[208,512]{1,0:T(8,128)(2,1)S(1)}, u32[]{:S(2)}, u32[]{:S(2)}) collective-permute-start(bf16[208,512]{1,0:T(8,128)(2,1)S(1)} %get-tuple-element.51), channel_id=1, source_target_pairs={{0,2},{2,0},{4,6},{6,4},{8,10},{10,8},{12,14},{14,12},{16,18},{18,... | collective-permute-start | bytes 638984 | tf_op jit(solution)/shard_map/ppermute | solution.py:415
  1.8 6.2 %collective-permute-start = (bf16[192,1280]{1,0:T(8,128)(2,1)S(1)}, bf16[192,1280]{1,0:T(8,128)(2,1)S(1)}, u32[]{:S(2)}, u32[]{:S(2)}) collective-permute-start(bf16[192,1280]{1,0:T(8,128)(2,1)S(1)} %get-tuple-element.50), channel_id=1, source_target_pairs={{0,2},{2,0},{4,6},{6,4},{8,10},{10,8},{12,14},{14,12},{16,18},{18,... | collective-permute-start | bytes 1474568 | tf_op jit(solution)/shard_map/ppermute | solution.py:419
  3.0 9.5 %collective-permute-start.5 = (bf16[208,512]{1,0:T(8,128)(2,1)S(1)}, bf16[208,512]{1,0:T(8,128)(2,1)S(1)}, u32[]{:S(2)}, u32[]{:S(2)}) collective-permute-start(bf16[208,512]{1,0:T(8,128)(2,1)S(1)} %maximum_maximum_fusion.refs_1_.refs_3_), channel_id=1, source_target_pairs={{0,8},{2,10},{8,16},{10,18},{16,24},{18,26},{24,28},{26,30},{28,20... | collective-permute-start | bytes 638984 | tf_op jit(solution)/shard_map/ppermute | solution.py:411
  5.9 8.1 %collective-permute-start.6 = (bf16[208,512]{1,0:T(8,128)(2,1)S(1)}, bf16[208,512]{1,0:T(8,128)(2,1)S(1)}, u32[]{:S(2)}, u32[]{:S(2)}) collective-permute-start(bf16[208,512]{1,0:T(8,128)(2,1)S(1)} %maximum_maximum_fusion.refs_1_.refs_3_), channel_id=1, source_target_pairs={{0,4},{2,6},{8,0},{10,2},{16,8},{18,10},{24,16},{26,18},{28,24},{3... | collective-permute-start | bytes 638984 | tf_op jit(solution)/shard_map/ppermute | solution.py:412
  6.0 10.2 %collective-permute-start.2 = (bf16[192,512]{1,0:T(8,128)(2,1)S(1)}, bf16[192,512]{1,0:T(8,128)(2,1)S(1)}, u32[]{:S(2)}, u32[]{:S(2)}) collective-permute-start(bf16[192,512]{1,0:T(8,128)(2,1)S(1)} %get-tuple-element.53.refs_2_), channel_id=1, source_target_pairs={{0,8},{2,10},{8,16},{10,18},{16,24},{18,26},{24,28},{26,30},{28,20... | collective-permute-start | bytes 589832 | tf_op jit(solution)/shard_map/ppermute | solution.py:411
  8.0 10.3 %collective-permute-start.9 = (bf16[192,512]{1,0:T(8,128)(2,1)S(1)}, bf16[192,512]{1,0:T(8,128)(2,1)S(1)}, u32[]{:S(2)}, u32[]{:S(2)}) collective-permute-start(bf16[192,512]{1,0:T(8,128)(2,1)S(1)} %get-tuple-element.53.refs_2_), channel_id=1, source_target_pairs={{0,4},{2,6},{8,0},{10,2},{16,8},{18,10},{24,16},{26,18},{28,24},{3... | collective-permute-start | bytes 589832 | tf_op jit(solution)/shard_map/ppermute | solution.py:412
  8.0 1.2 %copy-start = (bf16[192,2560]{1,0:T(8,128)(2,1)S(1)}, bf16[192,2560]{1,0:T(8,128)(2,1)}, u32[]{:S(2)}) copy-start(bf16[192,2560]{1,0:T(8,128)(2,1)} %refs_0_.4) | copy-start | bytes 2949124
  14.1 8.2 %collective-permute-start.7 = (bf16[208,512]{1,0:T(8,128)(2,1)S(1)}, bf16[208,512]{1,0:T(8,128)(2,1)S(1)}, u32[]{:S(2)}, u32[]{:S(2)}) collective-permute-start(bf16[208,512]{1,0:T(8,128)(2,1)S(1)} %collective-permute-done.5.refs_3_), channel_id=1, source_target_pairs={{0,8},{2,10},{8,16},{10,18},{16,24},{18,26},{24,28},{26,30},{28,20... | collective-permute-start | bytes 638984 | tf_op jit(solution)/shard_map/ppermute | solution.py:411
  15.7 8.2 %collective-permute-start.8 = (bf16[208,512]{1,0:T(8,128)(2,1)S(1)}, bf16[208,512]{1,0:T(8,128)(2,1)S(1)}, u32[]{:S(2)}, u32[]{:S(2)}) collective-permute-start(bf16[208,512]{1,0:T(8,128)(2,1)S(1)} %collective-permute-done.6.refs_5_), channel_id=1, source_target_pairs={{0,4},{2,6},{8,0},{10,2},{16,8},{18,10},{24,16},{26,18},{28,24},{3... | collective-permute-start | bytes 638984 | tf_op jit(solution)/shard_map/ppermute | solution.py:412
  16.1 8.3 %collective-permute-start.3 = (bf16[192,512]{1,0:T(8,128)(2,1)S(1)}, bf16[192,512]{1,0:T(8,128)(2,1)S(1)}, u32[]{:S(2)}, u32[]{:S(2)}) collective-permute-start(bf16[192,512]{1,0:T(8,128)(2,1)S(1)} %collective-permute-done.2.refs_2_), channel_id=1, source_target_pairs={{0,8},{2,10},{8,16},{10,18},{16,24},{18,26},{24,28},{26,30},{28,20... | collective-permute-start | bytes 589832 | tf_op jit(solution)/shard_map/ppermute | solution.py:411
  18.3 9.8 %collective-permute-start.11 = (bf16[192,512]{1,0:T(8,128)(2,1)S(1)}, bf16[192,512]{1,0:T(8,128)(2,1)S(1)}, u32[]{:S(2)}, u32[]{:S(2)}) collective-permute-start(bf16[192,512]{1,0:T(8,128)(2,1)S(1)} %collective-permute-done.9.refs_4_), channel_id=1, source_target_pairs={{0,4},{2,6},{8,0},{10,2},{16,8},{18,10},{24,16},{26,18},{28,24},{3... | collective-permute-start | bytes 589832 | tf_op jit(solution)/shard_map/ppermute | solution.py:412
  23.9 8.8 %collective-permute-start.10 = (bf16[208,512]{1,0:T(8,128)(2,1)S(1)}, bf16[208,512]{1,0:T(8,128)(2,1)S(1)}, u32[]{:S(2)}, u32[]{:S(2)}) collective-permute-start(bf16[208,512]{1,0:T(8,128)(2,1)S(1)} %collective-permute-done.8.refs_5_), channel_id=1, source_target_pairs={{0,4},{2,6},{8,0},{10,2},{16,8},{18,10},{24,16},{26,18},{28,24},{3... | collective-permute-start | bytes 638984 | tf_op jit(solution)/shard_map/ppermute | solution.py:412
  24.4 8.2 %collective-permute-start.4 = (bf16[192,512]{1,0:T(8,128)(2,1)S(1)}, bf16[192,512]{1,0:T(8,128)(2,1)S(1)}, u32[]{:S(2)}, u32[]{:S(2)}) collective-permute-start(bf16[192,512]{1,0:T(8,128)(2,1)S(1)} %collective-permute-done.3.refs_2_), channel_id=1, source_target_pairs={{0,8},{2,10},{8,16},{10,18},{16,24},{18,26},{24,28},{26,30},{28,20... | collective-permute-start | bytes 589832 | tf_op jit(solution)/shard_map/ppermute | solution.py:411
  28.1 8.8 %collective-permute-start.15 = (bf16[192,512]{1,0:T(8,128)(2,1)S(1)}, bf16[192,512]{1,0:T(8,128)(2,1)S(1)}, u32[]{:S(2)}, u32[]{:S(2)}) collective-permute-start(bf16[192,512]{1,0:T(8,128)(2,1)S(1)} %collective-permute-done.11.refs_4_), channel_id=1, source_target_pairs={{0,4},{2,6},{8,0},{10,2},{16,8},{18,10},{24,16},{26,18},{28,24},{3... | collective-permute-start | bytes 589832 | tf_op jit(solution)/shard_map/ppermute | solution.py:412
  28.5 8.3 %collective-permute-start.14 = (bf16[208,512]{1,0:T(8,128)(2,1)S(1)}, bf16[208,512]{1,0:T(8,128)(2,1)S(1)}, u32[]{:S(2)}, u32[]{:S(2)}) collective-permute-start(bf16[208,512]{1,0:T(8,128)(2,1)S(1)} %collective-permute-done.7.refs_3_), channel_id=1, source_target_pairs={{0,8},{2,10},{8,16},{10,18},{16,24},{18,26},{24,28},{26,30},{28,20... | collective-permute-start | bytes 638984 | tf_op jit(solution)/shard_map/ppermute | solution.py:411
  32.6 7.0 %collective-permute-start.13 = (bf16[208,512]{1,0:T(8,128)(2,1)S(1)}, bf16[208,512]{1,0:T(8,128)(2,1)S(1)}, u32[]{:S(2)}, u32[]{:S(2)}) collective-permute-start(bf16[208,512]{1,0:T(8,128)(2,1)S(1)} %collective-permute-done.10.refs_5_), channel_id=1, source_target_pairs={{0,4},{2,6},{8,0},{10,2},{16,8},{18,10},{24,16},{26,18},{28,24},{3... | collective-permute-start | bytes 638984 | tf_op jit(solution)/shard_map/ppermute | solution.py:412
  34.0 5.7 %collective-permute-start.12 = (bf16[192,512]{1,0:T(8,128)(2,1)S(1)}, bf16[192,512]{1,0:T(8,128)(2,1)S(1)}, u32[]{:S(2)}, u32[]{:S(2)}) collective-permute-start(bf16[192,512]{1,0:T(8,128)(2,1)S(1)} %collective-permute-done.4.refs_2_), channel_id=1, source_target_pairs={{0,8},{2,10},{8,16},{10,18},{16,24},{18,26},{24,28},{26,30},{28,20... | collective-permute-start | bytes 589832 | tf_op jit(solution)/shard_map/ppermute | solution.py:411
  41.3 1.9 %collective-permute-start.16 = (bf16[192,1280]{1,0:T(8,128)(2,1)S(1)}, bf16[192,1280]{1,0:T(8,128)(2,1)S(1)}, u32[]{:S(2)}, u32[]{:S(2)}) collective-permute-start(bf16[192,1280]{1,0:T(8,128)(2,1)S(1)} %get-tuple-element.75), channel_id=1, source_target_pairs={{0,2},{2,0},{4,6},{6,4},{8,10},{10,8},{12,14},{14,12},{16,18},{18,... | collective-permute-start | bytes 1474568 | tf_op jit(solution)/shard_map/ppermute | solution.py:456
  44.7 21.5 %collective-permute-start.18 = (bf16[96,1280]{1,0:T(8,128)(2,1)S(1)}, bf16[96,1280]{1,0:T(8,128)(2,1)S(1)}, u32[]{:S(2)}, u32[]{:S(2)}) collective-permute-start(bf16[96,1280]{1,0:T(8,128)(2,1)S(1)} %get-tuple-element.77), channel_id=1, source_target_pairs={{0,1},{1,0},{2,3},{3,2},{4,5},{5,4},{6,7},{7,6},{8,9},{9,8},{10,11... | collective-permute-start | bytes 737288 | tf_op jit(solution)/shard_map/ppermute | solution.py:506
  49.4 16.8 %collective-permute-start.19 = (bf16[96,1152]{1,0:T(8,128)(2,1)S(1)}, bf16[96,1152]{1,0:T(8,128)(2,1)S(1)}, u32[]{:S(2)}, u32[]{:S(2)}) collective-permute-start(bf16[96,1152]{1,0:T(8,128)(2,1)S(1)} %get-tuple-element.80), channel_id=1, source_target_pairs={{0,1},{1,0},{2,3},{3,2},{4,5},{5,4},{6,7},{7,6},{8,9},{9,8},{10,11... | collective-permute-start | bytes 663560 | tf_op jit(solution)/shard_map/ppermute | solution.py:506
  52.5 13.7 %collective-permute-start.20 = (bf16[96,1024]{1,0:T(8,128)(2,1)S(1)}, bf16[96,1024]{1,0:T(8,128)(2,1)S(1)}, u32[]{:S(2)}, u32[]{:S(2)}) collective-permute-start(bf16[96,1024]{1,0:T(8,128)(2,1)S(1)} %get-tuple-element.83), channel_id=1, source_target_pairs={{0,1},{1,0},{2,3},{3,2},{4,5},{5,4},{6,7},{7,6},{8,9},{9,8},{10,11... | collective-permute-start | bytes 589832 | tf_op jit(solution)/shard_map/ppermute | solution.py:506
  56.7 9.5 %collective-permute-start.21 = (bf16[96,896]{1,0:T(8,128)(2,1)S(1)}, bf16[96,896]{1,0:T(8,128)(2,1)S(1)}, u32[]{:S(2)}, u32[]{:S(2)}) collective-permute-start(bf16[96,896]{1,0:T(8,128)(2,1)S(1)} %get-tuple-element.86), channel_id=1, source_target_pairs={{0,1},{1,0},{2,3},{3,2},{4,5},{5,4},{6,7},{7,6},{8,9},{9,8},{10,11... | collective-permute-start | bytes 516104 | tf_op jit(solution)/shard_map/ppermute | solution.py:506
  58.3 10.3 %collective-permute-start.17 = (bf16[96,768]{1,0:T(8,128)(2,1)S(1)}, bf16[96,768]{1,0:T(8,128)(2,1)S(1)}, u32[]{:S(2)}, u32[]{:S(2)}) collective-permute-start(bf16[96,768]{1,0:T(8,128)(2,1)S(1)} %get-tuple-element.90), channel_id=1, source_target_pairs={{0,1},{1,0},{2,3},{3,2},{4,5},{5,4},{6,7},{7,6},{8,9},{9,8},{10,11... | collective-permute-start | bytes 442376 | tf_op jit(solution)/shard_map/ppermute | solution.py:506

commit v10 on v9

--- a/solution.py
+++ b/solution.py
@@ -14,7 +14,8 @@
 EXP2_SCALE = math.log2(math.e) / math.sqrt(HEAD_WIDTH)
 MASKED = -1e30
 VMEM_LIMIT = 16 * 1024 * 1024
-HEADER = 16
+TILE = 16
+HEADER = 8
 PIECES = 5
 
 
@@ -48,7 +49,7 @@
 
 def turned_values(blocks):
     v = jnp.concatenate(blocks, axis=0)
-    return jnp.concatenate([jnp.transpose(v), jnp.ones((HEADER, v.shape[0]), v.dtype)], axis=0)
+    return jnp.concatenate([jnp.transpose(v), jnp.ones((TILE, v.shape[0]), v.dtype)], axis=0)
 
 
 def fetch_columns(w_ref, first, held_ref, sems, sem):
@@ -77,7 +78,7 @@
     if fetch:
         w_ref = refs.pop(0)
     if plan["last"]:
-        out_refs = [refs.pop(0) for _ in range(owners)]
+        out_refs = {i: refs.pop(0) for i in plan["which"]}
     copies = []
     if fetch:
         sems = refs.pop()
@@ -98,7 +99,7 @@
     def rows_of(j, half, column):
         packet, row = plan["members"][j]
         at = row + half * chunk
-        at = at if isinstance(half, int) else pl.multiple_of(at, HEADER)
+        at = at if isinstance(half, int) else pl.multiple_of(at, TILE)
         return packets[packet][pl.ds(at, chunk), pl.ds(column, HEAD_WIDTH)]
 
     def state_at(i, half, h):
@@ -115,7 +116,7 @@
         k_at = pl.multiple_of(h * HEAD_WIDTH, HEAD_WIDTH)
         v_at = pl.multiple_of((heads + h) * HEAD_WIDTH, HEAD_WIDTH)
         late_at, early_at = state_at(i, 1, h), state_at(i, 0, h)
-        if i == 0:
+        if "keys" not in shared:
             shared["keys"] = jnp.concatenate([rows_of(j, 0, k_at) for j in group], axis=0)
             shared["values"] = turned_values([rows_of(j, 0, v_at) for j in group])
         carried = None
@@ -190,7 +191,7 @@
             chains = []
             for h in heads_at_once:
                 shared = {}
-                chains += [one_chain(group, h, i, shared) for i in range(owners)]
+                chains += [one_chain(group, h, i, shared) for i in plan["which"]]
             staggered(chains)
 
         if fetch:
@@ -211,12 +212,13 @@
     count = len(plan["members"])
     plan = dict(plan, marks=len(marks), packets=len(packets), carried=state is not None)
     fetch = plan.setdefault("fetch", None)
+    which = plan.setdefault("which", range(owners))
     rows = QUERY_PER_KEY * chunk
     slots = owners * 2 * heads
     vmem = pl.BlockSpec(memory_space=pltpu.VMEM)
-    kept = [(slots, 1, rows), (slots, HEAD_WIDTH + HEADER, rows)]
+    kept = [(slots, 1, rows), (slots, HEAD_WIDTH + TILE, rows)]
     if plan["last"]:
-        out_shape = [jax.ShapeDtypeStruct((2 * chunk, heads * GROUP), jnp.bfloat16)] * owners
+        out_shape = [jax.ShapeDtypeStruct((2 * chunk, heads * GROUP), jnp.bfloat16)] * len(which)
     else:
         out_shape = [jax.ShapeDtypeStruct(shape, jnp.float32) for shape in kept]
     operands = 1 + len(marks) + len(packets) + (0 if state is None else 2)
@@ -273,43 +275,72 @@
     )(*queries)
 
 
-def project_kernel(bring, own_ref, other_ref, held_ref, *refs):
-    copies = []
+def leaving_first(ref):
+    chunk = ref.shape[0] // 2
+    mine = lax.axis_index("inner").astype(jnp.int32)
+    halves = [ref[pl.ds(pl.multiple_of(half * chunk, chunk), chunk)] for half in (1 - mine, mine)]
+    return jnp.concatenate(halves, axis=0)
+
+
+def rows_of_core(held_ref, core):
+    depth = held_ref.shape[0] // 2
+    return held_ref[pl.ds(pl.multiple_of(core * depth, depth), depth)]
+
+
+def begin_kernel(own_ref, held_ref, begun_ref):
+    begun_ref[...] = product(leaving_first(own_ref), rows_of_core(held_ref, my_core()))
+
+
+def begin(own, held):
+    vmem = pl.BlockSpec(memory_space=pltpu.VMEM)
+    return pl.pallas_call(
+        begin_kernel,
+        out_shape=jax.ShapeDtypeStruct((own.shape[0], held.shape[1]), jnp.float32),
+        in_specs=[vmem, vmem],
+        out_specs=vmem,
+        cost_estimate=pl.CostEstimate(flops=1 << 10, bytes_accessed=1 << 10, transcendentals=0),
+        compiler_params=pltpu.CompilerParams(vmem_limit_bytes=VMEM_LIMIT),
+        name="begin",
+    )(own, held)
+
+
+def project_kernel(bring, begun, own_ref, other_ref, held_ref, *refs):
+    refs, copies = list(refs), []
     if bring:
-        w_ref, sent_ref, kept_ref, *next_refs, rows_ref, sems = refs
-        for n, ((first, _), next_ref) in enumerate(zip(bring, next_refs)):
-            copies += fetch_columns(w_ref, first, next_ref, sems, n * PIECES)
+        w_ref, sems = refs.pop(0), refs.pop()
+    if begun:
+        begun_ref = refs.pop(0)
+    sent_ref, kept_ref = refs.pop(0), refs.pop(0)
+    for n, (first, _) in enumerate(bring):
+        copies += fetch_columns(w_ref, first, refs.pop(0), sems, n * PIECES)
+    chunk, core = sent_ref.shape[0], my_core()
+    total = product(leaving_first(other_ref), rows_of_core(held_ref, 1 - core))
+    if begun:
+        total = total + begun_ref[...]
     else:
-        sent_ref, kept_ref, rows_ref = refs
-    chunk, part = sent_ref.shape[0], own_ref.shape[1]
-    mine = lax.axis_index("inner").astype(jnp.int32)
-    left = my_core() == 0
-    for place, half in enumerate((1 - mine, mine)):
-        at = pl.ds(pl.multiple_of(half * chunk, chunk), chunk)
-        own, other = own_ref[at], other_ref[at]
-        to = slice(place * chunk, (place + 1) * chunk)
-        rows_ref[to, :part] = jnp.where(left, own, other)
-        rows_ref[to, part:] = jnp.where(left, other, own)
-    both = product(rows_ref[...], held_ref[...]).astype(sent_ref.dtype)
+        total = total + product(leaving_first(own_ref), rows_of_core(held_ref, core))
+    both = total.astype(sent_ref.dtype)
     sent_ref[...] = both[:chunk]
     kept_ref[...] = both[chunk:]
     for copy in copies:
         copy.wait()
 
 
-def project(own, other, held, out_weight, bring):
+def project(own, other, held, out_weight, bring, begun=None):
     rows, (depth, width) = own.shape[0], held.shape
     vmem = pl.BlockSpec(memory_space=pltpu.VMEM)
     out_shape = [jax.ShapeDtypeStruct((rows // 2, width), jnp.bfloat16)] * 2
     out_shape += [jax.ShapeDtypeStruct((depth, columns), held.dtype) for _, columns in bring]
-    in_specs, operands = [vmem] * 3, [own, other, held]
-    scratch = [pltpu.VMEM((rows, depth), jnp.bfloat16)]
+    in_specs, operands, scratch = [vmem] * 3, [own, other, held], []
     if bring:
         in_specs.append(pl.BlockSpec(memory_space=pltpu.HBM))
         operands.append(out_weight)
         scratch.append(pltpu.SemaphoreType.DMA((PIECES * len(bring),)))
+    if begun is not None:
+        in_specs.append(vmem)
+        operands.append(begun)
     return pl.pallas_call(
-        functools.partial(project_kernel, bring),
+        functools.partial(project_kernel, bring, begun is not None),
         out_shape=out_shape,
         in_specs=in_specs,
         out_specs=[vmem] * len(out_shape),
@@ -338,7 +369,7 @@
     copies[0].wait()
     c = lax.div(first_ref[0], jnp.int32(chunk)).astype(jnp.float32)
     mark_ref[...] = jnp.full(mark_ref.shape, c, jnp.float32).astype(jnp.bfloat16)
-    sent_ref[rows:] = jnp.full((HEADER, 2 * width), c, jnp.float32).astype(jnp.bfloat16)
+    sent_ref[rows:] = jnp.full((TILE, 2 * width), c, jnp.float32).astype(jnp.bfloat16)
     for copy in copies[1:]:
         copy.wait()
 
@@ -351,7 +382,7 @@
     return pl.pallas_call(
         functools.partial(prepare_kernel, rows // 2),
         out_shape=[
-            jax.ShapeDtypeStruct((rows + HEADER, width), jnp.bfloat16),
+            jax.ShapeDtypeStruct((rows + TILE, width), jnp.bfloat16),
             jax.ShapeDtypeStruct((rows, width), jnp.bfloat16),
             jax.ShapeDtypeStruct((HEADER, width // 2), jnp.bfloat16),
             jax.ShapeDtypeStruct((rows, queries.shape[1] // 2), jnp.bfloat16),
@@ -414,12 +445,12 @@
     sent, x, mark, q_sent = prepare(queries, keys, values, positions)
     got = lax.ppermute(sent, "blk", sibling)
     y = jnp.concatenate(
-        [got[:rows], jnp.concatenate([mark, got[rows:, :width]], axis=1)], axis=0
+        [got[:rows], jnp.concatenate([mark, got[rows : rows + HEADER, :width]], axis=1)], axis=0
     )
     q_got = lax.ppermute(q_sent, "blk", sibling)
     turned = turn(heads, chunk, (True, False), [queries, q_got])
 
-    def call(pairs, state, own=False, last=False, fetch=None):
+    def call(pairs, state, own=False, last=False, fetch=None, which=(0, 1)):
         each = range(len(pairs))
         plan = dict(
             heads=heads,
@@ -432,6 +463,7 @@
             headers=[(2 + 2 * j, rows, i * width) for j in each for i in range(2)],
             owner_headers=[(0, rows, 0), (0, rows, width)],
             fetch=fetch,
+            which=which,
         )
         packets = [packet for pair in pairs for packet in pair]
         return attend(plan, turned, [y], packets, state, out_weight)
@@ -449,21 +481,24 @@
         else:
             state = call(arrived, state)
         arrived = [ups, downs]
-    x_up, y_down, *state = lax.optimization_barrier((ups[0], downs[1], *state))
+    x_up, y_down, y_up, *state = lax.optimization_barrier((ups[0], downs[1], ups[1], *state))
+    arrived = [(x_up, y_up), downs]
     far = (up(x_up), down(y_down))
     state = call(arrived, state)
-    own, theirs = call([far], state, last=True)
-    return own, lax.ppermute(theirs, "blk", sibling), [held, more]
+    (theirs,) = call([far], state, last=True, which=(1,))
+    other = lax.ppermute(theirs, "blk", sibling)
+    (own,) = call([far], state, last=True, which=(0,))
+    return own, other, [held, more]
 
 
 def one_head_a_device(count, queries, keys, values, positions):
     rows, chunk = queries.shape[0], queries.shape[0] // 2
     heads = keys.shape[1] // HEAD_WIDTH
     c = (positions[:1] // chunk).astype(jnp.bfloat16).reshape(1, 1)
-    header = jnp.broadcast_to(c, (HEADER, 2 * keys.shape[1]))
+    header = jnp.broadcast_to(c, (TILE, 2 * keys.shape[1]))
     packet = jnp.concatenate([jnp.concatenate([keys, values], axis=1), header], axis=0)
     packets = lax.all_gather(packet, "blk", axis=0, tiled=True)
-    size = rows + HEADER
+    size = rows + TILE
     here = lax.axis_index("blk")
     order = lax.rem(here + jnp.arange(count), count)
     packets = packets.reshape(count, size, -1)[order].reshape(count * size, -1)
@@ -501,7 +536,8 @@
     received, kept = [], []
     for j in range(len(cuts)):
         source = own if j == 0 else after(own, sent)
-        sent, keep, *rest = project(source, other, held[j], out_weight, bring[j])
+        begun = begin(own, held[0]) if j == 0 else None
+        sent, keep, *rest = project(source, other, held[j], out_weight, bring[j], begun)
         held += rest
         received.append(lax.ppermute(sent, "inner", [(0, 1), (1, 0)]))
         kept.append(keep)

time: 69.6 us -> 69.1 us (level)
  waiting for transfers between devices: 19 us -> 15.8 us
  Pallas kernels: 26.8 us -> 29.5 us
    ppermute x7, waiting for transfers between devices: 1.37 us -> 4.35 us  [split_over_cores(): up = lambda x: lax.ppermute(x, 'blk', clock)]
    ppermute x7, waiting for transfers between devices: 7.17 us -> 4.59 us  [split_over_cores(): down = lambda x: lax.ppermute(x, 'blk', counter)]
    pallas_call x5 -> x6, Pallas kernels: 10.7 us -> 13 us  [the longest x5 12.2 us: project(): pl.pallas_call(functools.partial(project_kernel, bring, begun is not None...]
    ppermute x1, waiting for transfers between devices: 1.85 us -> 0.05 us  [split_over_cores(): other = lax.ppermute(theirs, 'blk', sibling)]
    ppermute x5, waiting for transfers between devices: 7.61 us -> 5.82 us  [shards(): received.append(lax.ppermute(sent, 'inner', [(0, 1), (1, 0)]))]
    pallas_call x5 -> x6, Pallas kernels: 12.7 us -> 13.1 us  [attend(): pl.pallas_call(functools.partial(attend_kernel, plan), out_shape=out_shap...]
  transfers between devices with their start and end apart: 22 -> 22, of which waited for: 11 -> 10; matrix products, arithmetic and copies ran while one was open for 0% -> 0% of each run, Pallas kernels for 31% -> 37%
where the time goes in v10:
time: 69.1 us; the launch traced here: 68.9 us
  Pallas kernels  29.5 us (43%)
  starting transfers between devices  22 us (32%)
  waiting for transfers between devices  15.8 us (23%)
  local copies, waits for them, and re-layouts  1.22 us (2%)
    pallas_call x6, Pallas kernels, attend(): pl.pallas_call(functools.partial(attend_kernel, plan), out_shape=out_shap...  13.1 us
    ppermute x7, starting transfers between devices, split_over_cores(): up = lambda x: lax.ppermute(x, 'blk', clock)  12.8 us
    pallas_call x5, Pallas kernels, project(): pl.pallas_call(functools.partial(project_kernel, bring, begun is not None...  12.2 us
    ppermute x5, starting transfers between devices, shards(): received.append(lax.ppermute(sent, 'inner', [(0, 1), (1, 0)]))  5.87 us
    ppermute x5, waiting for transfers between devices, shards(): received.append(lax.ppermute(sent, 'inner', [(0, 1), (1, 0)]))  5.82 us
    ppermute x7, waiting for transfers between devices, split_over_cores(): down = lambda x: lax.ppermute(x, 'blk', counter)  4.59 us
    ppermute x7, waiting for transfers between devices, split_over_cores(): up = lambda x: lax.ppermute(x, 'blk', clock)  4.35 us
    ppermute x7, starting transfers between devices, split_over_cores(): down = lambda x: lax.ppermute(x, 'blk', counter)  2.68 us
  transfers between devices with their start and end apart: 22, of which 10 were waited for; matrix products, arithmetic and copies ran while one was open for 0% of the time, Pallas kernels for 37%

profile of v10, /device:TPU:0, one launch (start us, length us, event | category | flops | bytes accessed | tf_op | source)
XLA Modules:
  0.0 68.9 jit_solution(560844343230992101)
XLA Ops:
  0.0 1.3 %prepare.1 = (bf16[208,512]{1,0:T(8,128)(2,1)S(1)}, bf16[192,512]{1,0:T(8,128)(2,1)S(1)}, bf16[8,256]{1,0:T(8,128)(2,1)S(1)}, bf16[192,1280]{1,0:T(8,128)(2,1)S(1)}) custom-call(bf16[192,2560]{1,0:T(8,128)(2,1)} %refs_0_.4, bf16[192,512]{1,0:T(8,128)(2,1)} %k_ref.1, bf16[192,512]{1,0:T(8,128)(2,1)} %v_ref.1, s32[192]{0:T(256)} %position_ref.1), custom_call_target="tpu_custom_call" | custom-call | tf_op jit(solution)/shard_map/prepare/pallas_call | solution.py:382
  1.3 0.5 collective-permute-start.1
  1.8 0.1 collective-permute-start
  1.9 1.0 %collective-permute-done.1 = bf16[208,512]{1,0:T(8,128)(2,1)S(1)} collective-permute-done((bf16[208,512]{1,0:T(8,128)(2,1)S(1)}, bf16[208,512]{1,0:T(8,128)(2,1)S(1)}, u32[]{:S(2)}, u32[]{:S(2)}) %collective-permute-start.1) | collective-permute-done | bytes 213024 | tf_op jit(solution)/shard_map/ppermute | solution.py:446
  2.9 3.0 %collective-permute-start.5 = (bf16[200,512]{1,0:T(8,128)(2,1)S(1)}, bf16[200,512]{1,0:T(8,128)(2,1)S(1)}, u32[]{:S(2)}, u32[]{:S(2)}) collective-permute-start(bf16[200,512]{1,0:T(8,128)(2,1)S(1)} %maximum_maximum_fusion.refs_1_.refs_3_), channel_id=1, source_target_pairs={{0,8},{2,10},{8,16},{10,18},{16,24},{18,26},{24,28},{26,30},{28,20... | collective-permute-start | bytes 614408 | tf_op jit(solution)/shard_map/ppermute | solution.py:442
  6.0 2.0 %collective-permute-start.2 = (bf16[192,512]{1,0:T(8,128)(2,1)S(1)}, bf16[192,512]{1,0:T(8,128)(2,1)S(1)}, u32[]{:S(2)}, u32[]{:S(2)}) collective-permute-start(bf16[192,512]{1,0:T(8,128)(2,1)S(1)} %get-tuple-element.52.refs_2_), channel_id=1, source_target_pairs={{0,8},{2,10},{8,16},{10,18},{16,24},{18,26},{24,28},{26,30},{28,20... | collective-permute-start | bytes 589832 | tf_op jit(solution)/shard_map/ppermute | solution.py:442
  8.0 1.2 %copy-done = bf16[192,2560]{1,0:T(8,128)(2,1)S(1)} copy-done((bf16[192,2560]{1,0:T(8,128)(2,1)S(1)}, bf16[192,2560]{1,0:T(8,128)(2,1)}, u32[]{:S(2)}) %copy-start) | copy-done | bytes 983064
  9.2 0.3 turn.1.refs_0_
  9.5 3.0 %attend.6 = (f32[8,1,480]{2,1,0:T(1,128)S(1)}, f32[8,144,480]{2,1,0:T(8,128)S(1)}, bf16[2560,1280]{1,0:T(8,128)(2,1)S(1)}) custom-call(bf16[8,128,480]{2,1,0:T(8,128)(2,1)S(1)} %turn.1.refs_0_, bf16[200,512]{1,0:T(8,128)(2,1)S(1)} %maximum_maximum_fusion.refs_1_.refs_3_, bf16[192,512]{1,0:T(8,128)(2,1)S(1)} %get-tuple-element.52.refs_2_, ...), custom_call_target="tpu_custom_call" | custom-call | flops 377487360 | bytes 4194304 | tf_op jit(solution)/shard_map/attend/pallas_call | solution.py:233
  12.5 1.4 %collective-permute-done.6.refs_5_ = bf16[200,512]{1,0:T(8,128)(2,1)S(1)} collective-permute-done((bf16[200,512]{1,0:T(8,128)(2,1)S(1)}, bf16[200,512]{1,0:T(8,128)(2,1)S(1)}, u32[]{:S(2)}, u32[]{:S(2)}) %collective-permute-start.6) | collective-permute-done | bytes 204832 | tf_op jit(solution)/shard_map/ppermute | solution.py:443
  13.9 1.6 %collective-permute-start.7 = (bf16[200,512]{1,0:T(8,128)(2,1)S(1)}, bf16[200,512]{1,0:T(8,128)(2,1)S(1)}, u32[]{:S(2)}, u32[]{:S(2)}) collective-permute-start(bf16[200,512]{1,0:T(8,128)(2,1)S(1)} %collective-permute-done.5.refs_3_), channel_id=1, source_target_pairs={{0,8},{2,10},{8,16},{10,18},{16,24},{18,26},{24,28},{26,30},{28,20... | collective-permute-start | bytes 614408 | tf_op jit(solution)/shard_map/ppermute | solution.py:442
  15.5 0.4 collective-permute-start.8
  15.9 0.0 collective-permute-done.2.refs_2_
  16.0 2.1 %collective-permute-start.3 = (bf16[192,512]{1,0:T(8,128)(2,1)S(1)}, bf16[192,512]{1,0:T(8,128)(2,1)S(1)}, u32[]{:S(2)}, u32[]{:S(2)}) collective-permute-start(bf16[192,512]{1,0:T(8,128)(2,1)S(1)} %collective-permute-done.2.refs_2_), channel_id=1, source_target_pairs={{0,8},{2,10},{8,16},{10,18},{16,24},{18,26},{24,28},{26,30},{28,20... | collective-permute-start | bytes 589832 | tf_op jit(solution)/shard_map/ppermute | solution.py:442
  18.1 3.1 %attend.7 = (f32[8,1,480]{2,1,0:T(1,128)S(1)}, f32[8,144,480]{2,1,0:T(8,128)S(1)}, bf16[2560,1152]{1,0:T(8,128)(2,1)S(1)}) custom-call(bf16[8,128,480]{2,1,0:T(8,128)(2,1)S(1)} %turn.1.refs_0_, bf16[200,512]{1,0:T(8,128)(2,1)S(1)} %maximum_maximum_fusion.refs_1_.refs_3_, bf16[192,512]{1,0:T(8,128)(2,1)S(1)} %collective-permute-done.2.refs_2_, ...), custom_call_target="tpu_custom_call" | custom-call | flops 754974720 | bytes 4194304 | tf_op jit(solution)/shard_map/attend/pallas_call | solution.py:233
  21.2 0.7 %collective-permute-done.7.refs_3_ = bf16[200,512]{1,0:T(8,128)(2,1)S(1)} collective-permute-done((bf16[200,512]{1,0:T(8,128)(2,1)S(1)}, bf16[200,512]{1,0:T(8,128)(2,1)S(1)}, u32[]{:S(2)}, u32[]{:S(2)}) %collective-permute-start.7) | collective-permute-done | bytes 204832 | tf_op jit(solution)/shard_map/ppermute | solution.py:442
  21.9 1.6 %collective-permute-done.8.refs_5_ = bf16[200,512]{1,0:T(8,128)(2,1)S(1)} collective-permute-done((bf16[200,512]{1,0:T(8,128)(2,1)S(1)}, bf16[200,512]{1,0:T(8,128)(2,1)S(1)}, u32[]{:S(2)}, u32[]{:S(2)}) %collective-permute-start.8) | collective-permute-done | bytes 204832 | tf_op jit(solution)/shard_map/ppermute | solution.py:443
  23.5 0.3 collective-permute-start.10
  23.8 1.8 %collective-permute-start.11 = (bf16[200,512]{1,0:T(8,128)(2,1)S(1)}, bf16[200,512]{1,0:T(8,128)(2,1)S(1)}, u32[]{:S(2)}, u32[]{:S(2)}) collective-permute-start(bf16[200,512]{1,0:T(8,128)(2,1)S(1)} %collective-permute-done.7.refs_3_), channel_id=1, source_target_pairs={{0,8},{2,10},{8,16},{10,18},{16,24},{18,26},{24,28},{26,30},{28,20... | collective-permute-start | bytes 614408 | tf_op jit(solution)/shard_map/ppermute | solution.py:442
  25.6 2.0 %collective-permute-start.4 = (bf16[192,512]{1,0:T(8,128)(2,1)S(1)}, bf16[192,512]{1,0:T(8,128)(2,1)S(1)}, u32[]{:S(2)}, u32[]{:S(2)}) collective-permute-start(bf16[192,512]{1,0:T(8,128)(2,1)S(1)} %collective-permute-done.3.refs_2_), channel_id=1, source_target_pairs={{0,8},{2,10},{8,16},{10,18},{16,24},{18,26},{24,28},{26,30},{28,20... | collective-permute-start | bytes 589832 | tf_op jit(solution)/shard_map/ppermute | solution.py:442
  27.6 0.1 collective-permute-done.12.refs_4_
  27.7 0.2 collective-permute-start.15
  27.9 2.5 %attend.8 = (f32[8,1,480]{2,1,0:T(1,128)S(1)}, f32[8,144,480]{2,1,0:T(8,128)S(1)}) custom-call(bf16[8,128,480]{2,1,0:T(8,128)(2,1)S(1)} %turn.1.refs_0_, bf16[200,512]{1,0:T(8,128)(2,1)S(1)} %maximum_maximum_fusion.refs_1_.refs_3_, bf16[192,512]{1,0:T(8,128)(2,1)S(1)} %collective-permute-done.3.refs_2_, bf16[200,512]{1,0:T(8,128)(2,1)S(1)} %collective-permute-done.7.refs_3_, ...), custom_call_target="tpu_custom_call" | custom-call | flops 754974720 | bytes 4194304 | tf_op jit(solution)/shard_map/attend/pallas_call | solution.py:233
  30.5 2.2 %collective-permute-done.4.refs_2_ = bf16[192,512]{1,0:T(8,128)(2,1)S(1)} collective-permute-done((bf16[192,512]{1,0:T(8,128)(2,1)S(1)}, bf16[192,512]{1,0:T(8,128)(2,1)S(1)}, u32[]{:S(2)}, u32[]{:S(2)}) %collective-permute-start.4) | collective-permute-done | bytes 196640 | tf_op jit(solution)/shard_map/ppermute | solution.py:442
  32.7 1.7 %collective-permute-start.14 = (bf16[200,512]{1,0:T(8,128)(2,1)S(1)}, bf16[200,512]{1,0:T(8,128)(2,1)S(1)}, u32[]{:S(2)}, u32[]{:S(2)}) collective-permute-start(bf16[200,512]{1,0:T(8,128)(2,1)S(1)} %collective-permute-done.10.refs_5_), channel_id=1, source_target_pairs={{0,4},{2,6},{8,0},{10,2},{16,8},{18,10},{24,16},{26,18},{28,24},{3... | collective-permute-start | bytes 614408 | tf_op jit(solution)/shard_map/ppermute | solution.py:443
  34.4 0.3 collective-permute-start.13
  34.7 1.4 %collective-permute-done.15.refs_4_ = bf16[192,512]{1,0:T(8,128)(2,1)S(1)} collective-permute-done((bf16[192,512]{1,0:T(8,128)(2,1)S(1)}, bf16[192,512]{1,0:T(8,128)(2,1)S(1)}, u32[]{:S(2)}, u32[]{:S(2)}) %collective-permute-start.15) | collective-permute-done | bytes 196640 | tf_op jit(solution)/shard_map/ppermute | solution.py:443
  36.2 2.5 %attend.9 = (f32[8,1,480]{2,1,0:T(1,128)S(1)}, f32[8,144,480]{2,1,0:T(8,128)S(1)}) custom-call(bf16[8,128,480]{2,1,0:T(8,128)(2,1)S(1)} %turn.1.refs_0_, bf16[200,512]{1,0:T(8,128)(2,1)S(1)} %maximum_maximum_fusion.refs_1_.refs_3_, bf16[192,512]{1,0:T(8,128)(2,1)S(1)} %collective-permute-done.4.refs_2_, ...), custom_call_target="tpu_custom_call" | custom-call | flops 754974720 | bytes 4194304 | tf_op jit(solution)/shard_map/attend/pallas_call | solution.py:233
  38.7 1.4 %collective-permute-done.13.refs_2_ = bf16[192,512]{1,0:T(8,128)(2,1)S(1)} collective-permute-done((bf16[192,512]{1,0:T(8,128)(2,1)S(1)}, bf16[192,512]{1,0:T(8,128)(2,1)S(1)}, u32[]{:S(2)}, u32[]{:S(2)}) %collective-permute-start.13) | collective-permute-done | bytes 196640 | tf_op jit(solution)/shard_map/ppermute | solution.py:442
  40.1 1.0 %attend.11 = bf16[192,1280]{1,0:T(8,128)(2,1)S(1)} custom-call(bf16[8,128,480]{2,1,0:T(8,128)(2,1)S(1)} %turn.1.refs_0_, bf16[200,512]{1,0:T(8,128)(2,1)S(1)} %maximum_maximum_fusion.refs_1_.refs_3_, bf16[192,512]{1,0:T(8,128)(2,1)S(1)} %collective-permute-done.13.refs_2_, bf16[200,512]{1,0:T(8,128)(2,1)S(1)} %collective-permute-done.14.refs_3_, ...), custom_call_target="tpu_custom_call" | custom-call | flops 377487360 | bytes 4194304 | tf_op jit(solution)/shard_map/attend/pallas_call | solution.py:233
  41.1 0.1 collective-permute-start.16
  41.2 1.0 %attend.10.own_ref = bf16[192,1280]{1,0:T(8,128)(2,1)S(1)} custom-call(bf16[8,128,480]{2,1,0:T(8,128)(2,1)S(1)} %turn.1.refs_0_, bf16[200,512]{1,0:T(8,128)(2,1)S(1)} %maximum_maximum_fusion.refs_1_.refs_3_, bf16[192,512]{1,0:T(8,128)(2,1)S(1)} %collective-permute-done.13.refs_2_, bf16[200,512]{1,0:T(8,128)(2,1)S(1)} %collective-permute-done.14.refs_3_, ...), custom_call_target="tpu_custom_call" | custom-call | flops 377487360 | bytes 4194304 | tf_op jit(solution)/shard_map/attend/pallas_call | solution.py:233
  42.1 0.8 %begin.1.refs_0_ = f32[192,1280]{1,0:T(8,128)S(1)} custom-call(bf16[192,1280]{1,0:T(8,128)(2,1)S(1)} %attend.10.own_ref, bf16[2560,1280]{1,0:T(8,128)(2,1)S(1)} %get-tuple-element.74.held_ref), custom_call_target="tpu_custom_call" | custom-call | flops 1024 | bytes 1024 | tf_op jit(solution)/shard_map/begin/pallas_call | solution.py:296
  43.0 0.0 collective-permute-done.16.other_ref
  43.0 0.8 %project.5 = (bf16[96,1280]{1,0:T(8,128)(2,1)S(1)}, bf16[96,1280]{1,0:T(8,128)(2,1)S(1)}) custom-call(bf16[192,1280]{1,0:T(8,128)(2,1)S(1)} %attend.10.own_ref, bf16[192,1280]{1,0:T(8,128)(2,1)S(1)} %collective-permute-done.16.other_ref, bf16[2560,1280]{1,0:T(8,128)(2,1)S(1)} %get-tuple-element.74.held_ref, f32[192,1280]{1,0:T(8,128)S(1)} %begin.1.refs_0_), custom_call_target="tpu_custom_call" | custom-call | flops 1024 | bytes 1024 | tf_op jit(solution)/shard_map/project/pallas_call | solution.py:342
  43.9 1.6 %collective-permute-start.18 = (bf16[96,1280]{1,0:T(8,128)(2,1)S(1)}, bf16[96,1280]{1,0:T(8,128)(2,1)S(1)}, u32[]{:S(2)}, u32[]{:S(2)}) collective-permute-start(bf16[96,1280]{1,0:T(8,128)(2,1)S(1)} %get-tuple-element.75), channel_id=1, source_target_pairs={{0,1},{1,0},{2,3},{3,2},{4,5},{5,4},{6,7},{7,6},{8,9},{9,8},{10,11... | collective-permute-start | bytes 737288 | tf_op jit(solution)/shard_map/ppermute | solution.py:542
  45.4 3.8 %project.6 = (bf16[96,1152]{1,0:T(8,128)(2,1)S(1)}, bf16[96,1152]{1,0:T(8,128)(2,1)S(1)}, bf16[2560,1024]{1,0:T(8,128)(2,1)S(1)}) custom-call(bf16[192,1280]{1,0:T(8,128)(2,1)S(1)} %attend.10.own_ref, bf16[192,1280]{1,0:T(8,128)(2,1)S(1)} %collective-permute-done.16.other_ref, bf16[2560,1152]{1,0:T(8,128)(2,1)S(1)} %get-tuple-element.77.held_ref, ...), custom_call_target="tpu_custom_call" | custom-call | flops 1024 | bytes 1024 | tf_op jit(solution)/shard_map/project/pallas_call | solution.py:342
  49.3 0.6 collective-permute-start.19
  49.9 3.4 %project.7 = (bf16[96,1024]{1,0:T(8,128)(2,1)S(1)}, bf16[96,1024]{1,0:T(8,128)(2,1)S(1)}, bf16[2560,896]{1,0:T(8,128)(2,1)S(1)}) custom-call(bf16[192,1280]{1,0:T(8,128)(2,1)S(1)} %attend.10.own_ref, bf16[192,1280]{1,0:T(8,128)(2,1)S(1)} %collective-permute-done.16.other_ref, bf16[2560,1024]{1,0:T(8,128)(2,1)S(1)} %get-tuple-element.80.held_ref, ...), custom_call_target="tpu_custom_call" | custom-call | flops 1024 | bytes 1024 | tf_op jit(solution)/shard_map/project/pallas_call | solution.py:342
  53.2 1.6 %collective-permute-start.20 = (bf16[96,1024]{1,0:T(8,128)(2,1)S(1)}, bf16[96,1024]{1,0:T(8,128)(2,1)S(1)}, u32[]{:S(2)}, u32[]{:S(2)}) collective-permute-start(bf16[96,1024]{1,0:T(8,128)(2,1)S(1)} %get-tuple-element.81), channel_id=1, source_target_pairs={{0,1},{1,0},{2,3},{3,2},{4,5},{5,4},{6,7},{7,6},{8,9},{9,8},{10,11... | collective-permute-start | bytes 589832 | tf_op jit(solution)/shard_map/ppermute | solution.py:542
  54.8 3.2 %project.8 = (bf16[96,896]{1,0:T(8,128)(2,1)S(1)}, bf16[96,896]{1,0:T(8,128)(2,1)S(1)}, bf16[2560,768]{1,0:T(8,128)(2,1)S(1)}) custom-call(bf16[192,1280]{1,0:T(8,128)(2,1)S(1)} %attend.10.own_ref, bf16[192,1280]{1,0:T(8,128)(2,1)S(1)} %collective-permute-done.16.other_ref, bf16[2560,896]{1,0:T(8,128)(2,1)S(1)} %get-tuple-element.83.held_ref, ...), custom_call_target="tpu_custom_call" | custom-call | flops 1024 | bytes 1024 | tf_op jit(solution)/shard_map/project/pallas_call | solution.py:342
  58.0 0.6 collective-permute-start.21
  58.6 0.9 %project.9 = (bf16[96,768]{1,0:T(8,128)(2,1)S(1)}, bf16[96,768]{1,0:T(8,128)(2,1)S(1)}) custom-call(bf16[192,1280]{1,0:T(8,128)(2,1)S(1)} %attend.10.own_ref, bf16[192,1280]{1,0:T(8,128)(2,1)S(1)} %collective-permute-done.16.other_ref, bf16[2560,768]{1,0:T(8,128)(2,1)S(1)} %get-tuple-element.86.held_ref), custom_call_target="tpu_custom_call" | custom-call | flops 1024 | bytes 1024 | tf_op jit(solution)/shard_map/project/pallas_call | solution.py:342
  59.6 1.6 %collective-permute-start.17 = (bf16[96,768]{1,0:T(8,128)(2,1)S(1)}, bf16[96,768]{1,0:T(8,128)(2,1)S(1)}, u32[]{:S(2)}, u32[]{:S(2)}) collective-permute-start(bf16[96,768]{1,0:T(8,128)(2,1)S(1)} %get-tuple-element.88), channel_id=1, source_target_pairs={{0,1},{1,0},{2,3},{3,2},{4,5},{5,4},{6,7},{7,6},{8,9},{9,8},{10,11... | collective-permute-start | bytes 442376 | tf_op jit(solution)/shard_map/ppermute | solution.py:542
  61.1 4.4 %collective-permute-done.21.refs_7_ = bf16[96,896]{1,0:T(8,128)(2,1)S(1)} collective-permute-done((bf16[96,896]{1,0:T(8,128)(2,1)S(1)}, bf16[96,896]{1,0:T(8,128)(2,1)S(1)}, u32[]{:S(2)}, u32[]{:S(2)}) %collective-permute-start.21) | collective-permute-done | bytes 172064 | tf_op jit(solution)/shard_map/ppermute | solution.py:542
  65.5 1.1 %finish.2.refs_2_ = bf16[96,5120]{1,0:T(8,128)(2,1)} custom-call(bf16[96,1280]{1,0:T(8,128)(2,1)S(1)} %get-tuple-element.89.refs_0_, bf16[96,1152]{1,0:T(8,128)(2,1)S(1)} %get-tuple-element.90.refs_1_, bf16[96,1024]{1,0:T(8,128)(2,1)S(1)} %get-tuple-element.91.refs_2_, bf16[96,896]{1,0:T(8,128)(2,1)S(1)} %get-tuple-element.92.refs_3_, ...), custom_call_target="tpu_custom_call" | custom-call | flops 1024 | bytes 1024 | tf_op jit(solution)/shard_map/finish/pallas_call | solution.py:418
  66.6 1.4 %collective-permute-done.17.refs_1_ = bf16[96,768]{1,0:T(8,128)(2,1)S(1)} collective-permute-done((bf16[96,768]{1,0:T(8,128)(2,1)S(1)}, bf16[96,768]{1,0:T(8,128)(2,1)S(1)}, u32[]{:S(2)}, u32[]{:S(2)}) %collective-permute-start.17) | collective-permute-done | bytes 147488 | tf_op jit(solution)/shard_map/ppermute | solution.py:542
  68.1 0.7 %finish.3 = bf16[96,5120]{1,0:T(8,128)(2,1)} custom-call(bf16[96,768]{1,0:T(8,128)(2,1)S(1)} %get-tuple-element.87.refs_0_, bf16[96,768]{1,0:T(8,128)(2,1)S(1)} %collective-permute-done.17.refs_1_, bf16[96,5120]{1,0:T(8,128)(2,1)} %finish.2.refs_2_), custom_call_target="tpu_custom_call", output_to_operand_aliasing={{}: (2, {})} | custom-call | flops 1024 | bytes 1024 | tf_op jit(solution)/shard_map/finish/pallas_call | solution.py:418
  (17 shorter events, 0.1 us)
Async XLA Ops:
  1.3 1.6 %collective-permute-start.1 = (bf16[208,512]{1,0:T(8,128)(2,1)S(1)}, bf16[208,512]{1,0:T(8,128)(2,1)S(1)}, u32[]{:S(2)}, u32[]{:S(2)}) collective-permute-start(bf16[208,512]{1,0:T(8,128)(2,1)S(1)} %get-tuple-element.50), channel_id=1, source_target_pairs={{0,2},{2,0},{4,6},{6,4},{8,10},{10,8},{12,14},{14,12},{16,18},{18,... | collective-permute-start | bytes 638984 | tf_op jit(solution)/shard_map/ppermute | solution.py:446
  1.8 6.2 %collective-permute-start = (bf16[192,1280]{1,0:T(8,128)(2,1)S(1)}, bf16[192,1280]{1,0:T(8,128)(2,1)S(1)}, u32[]{:S(2)}, u32[]{:S(2)}) collective-permute-start(bf16[192,1280]{1,0:T(8,128)(2,1)S(1)} %get-tuple-element.49), channel_id=1, source_target_pairs={{0,2},{2,0},{4,6},{6,4},{8,10},{10,8},{12,14},{14,12},{16,18},{18,... | collective-permute-start | bytes 1474568 | tf_op jit(solution)/shard_map/ppermute | solution.py:450
  2.9 9.5 %collective-permute-start.5 = (bf16[200,512]{1,0:T(8,128)(2,1)S(1)}, bf16[200,512]{1,0:T(8,128)(2,1)S(1)}, u32[]{:S(2)}, u32[]{:S(2)}) collective-permute-start(bf16[200,512]{1,0:T(8,128)(2,1)S(1)} %maximum_maximum_fusion.refs_1_.refs_3_), channel_id=1, source_target_pairs={{0,8},{2,10},{8,16},{10,18},{16,24},{18,26},{24,28},{26,30},{28,20... | collective-permute-start | bytes 614408 | tf_op jit(solution)/shard_map/ppermute | solution.py:442
  5.9 8.0 %collective-permute-start.6 = (bf16[200,512]{1,0:T(8,128)(2,1)S(1)}, bf16[200,512]{1,0:T(8,128)(2,1)S(1)}, u32[]{:S(2)}, u32[]{:S(2)}) collective-permute-start(bf16[200,512]{1,0:T(8,128)(2,1)S(1)} %maximum_maximum_fusion.refs_1_.refs_3_), channel_id=1, source_target_pairs={{0,4},{2,6},{8,0},{10,2},{16,8},{18,10},{24,16},{26,18},{28,24},{3... | collective-permute-start | bytes 614408 | tf_op jit(solution)/shard_map/ppermute | solution.py:443
  6.0 10.0 %collective-permute-start.2 = (bf16[192,512]{1,0:T(8,128)(2,1)S(1)}, bf16[192,512]{1,0:T(8,128)(2,1)S(1)}, u32[]{:S(2)}, u32[]{:S(2)}) collective-permute-start(bf16[192,512]{1,0:T(8,128)(2,1)S(1)} %get-tuple-element.52.refs_2_), channel_id=1, source_target_pairs={{0,8},{2,10},{8,16},{10,18},{16,24},{18,26},{24,28},{26,30},{28,20... | collective-permute-start | bytes 589832 | tf_op jit(solution)/shard_map/ppermute | solution.py:442
  8.0 10.1 %collective-permute-start.9 = (bf16[192,512]{1,0:T(8,128)(2,1)S(1)}, bf16[192,512]{1,0:T(8,128)(2,1)S(1)}, u32[]{:S(2)}, u32[]{:S(2)}) collective-permute-start(bf16[192,512]{1,0:T(8,128)(2,1)S(1)} %get-tuple-element.52.refs_2_), channel_id=1, source_target_pairs={{0,4},{2,6},{8,0},{10,2},{16,8},{18,10},{24,16},{26,18},{28,24},{3... | collective-permute-start | bytes 589832 | tf_op jit(solution)/shard_map/ppermute | solution.py:443
  8.0 1.2 %copy-start = (bf16[192,2560]{1,0:T(8,128)(2,1)S(1)}, bf16[192,2560]{1,0:T(8,128)(2,1)}, u32[]{:S(2)}) copy-start(bf16[192,2560]{1,0:T(8,128)(2,1)} %refs_0_.4) | copy-start | bytes 2949124
  13.9 8.0 %collective-permute-start.7 = (bf16[200,512]{1,0:T(8,128)(2,1)S(1)}, bf16[200,512]{1,0:T(8,128)(2,1)S(1)}, u32[]{:S(2)}, u32[]{:S(2)}) collective-permute-start(bf16[200,512]{1,0:T(8,128)(2,1)S(1)} %collective-permute-done.5.refs_3_), channel_id=1, source_target_pairs={{0,8},{2,10},{8,16},{10,18},{16,24},{18,26},{24,28},{26,30},{28,20... | collective-permute-start | bytes 614408 | tf_op jit(solution)/shard_map/ppermute | solution.py:442
  15.5 8.0 %collective-permute-start.8 = (bf16[200,512]{1,0:T(8,128)(2,1)S(1)}, bf16[200,512]{1,0:T(8,128)(2,1)S(1)}, u32[]{:S(2)}, u32[]{:S(2)}) collective-permute-start(bf16[200,512]{1,0:T(8,128)(2,1)S(1)} %collective-permute-done.6.refs_5_), channel_id=1, source_target_pairs={{0,4},{2,6},{8,0},{10,2},{16,8},{18,10},{24,16},{26,18},{28,24},{3... | collective-permute-start | bytes 614408 | tf_op jit(solution)/shard_map/ppermute | solution.py:443
  16.0 9.6 %collective-permute-start.3 = (bf16[192,512]{1,0:T(8,128)(2,1)S(1)}, bf16[192,512]{1,0:T(8,128)(2,1)S(1)}, u32[]{:S(2)}, u32[]{:S(2)}) collective-permute-start(bf16[192,512]{1,0:T(8,128)(2,1)S(1)} %collective-permute-done.2.refs_2_), channel_id=1, source_target_pairs={{0,8},{2,10},{8,16},{10,18},{16,24},{18,26},{24,28},{26,30},{28,20... | collective-permute-start | bytes 589832 | tf_op jit(solution)/shard_map/ppermute | solution.py:442
  18.1 9.6 %collective-permute-start.12 = (bf16[192,512]{1,0:T(8,128)(2,1)S(1)}, bf16[192,512]{1,0:T(8,128)(2,1)S(1)}, u32[]{:S(2)}, u32[]{:S(2)}) collective-permute-start(bf16[192,512]{1,0:T(8,128)(2,1)S(1)} %collective-permute-done.9.refs_4_), channel_id=1, source_target_pairs={{0,4},{2,6},{8,0},{10,2},{16,8},{18,10},{24,16},{26,18},{28,24},{3... | collective-permute-start | bytes 589832 | tf_op jit(solution)/shard_map/ppermute | solution.py:443
  23.5 9.2 %collective-permute-start.10 = (bf16[200,512]{1,0:T(8,128)(2,1)S(1)}, bf16[200,512]{1,0:T(8,128)(2,1)S(1)}, u32[]{:S(2)}, u32[]{:S(2)}) collective-permute-start(bf16[200,512]{1,0:T(8,128)(2,1)S(1)} %collective-permute-done.8.refs_5_), channel_id=1, source_target_pairs={{0,4},{2,6},{8,0},{10,2},{16,8},{18,10},{24,16},{26,18},{28,24},{3... | collective-permute-start | bytes 614408 | tf_op jit(solution)/shard_map/ppermute | solution.py:443
  23.8 8.9 %collective-permute-start.11 = (bf16[200,512]{1,0:T(8,128)(2,1)S(1)}, bf16[200,512]{1,0:T(8,128)(2,1)S(1)}, u32[]{:S(2)}, u32[]{:S(2)}) collective-permute-start(bf16[200,512]{1,0:T(8,128)(2,1)S(1)} %collective-permute-done.7.refs_3_), channel_id=1, source_target_pairs={{0,8},{2,10},{8,16},{10,18},{16,24},{18,26},{24,28},{26,30},{28,20... | collective-permute-start | bytes 614408 | tf_op jit(solution)/shard_map/ppermute | solution.py:442
  25.6 7.1 %collective-permute-start.4 = (bf16[192,512]{1,0:T(8,128)(2,1)S(1)}, bf16[192,512]{1,0:T(8,128)(2,1)S(1)}, u32[]{:S(2)}, u32[]{:S(2)}) collective-permute-start(bf16[192,512]{1,0:T(8,128)(2,1)S(1)} %collective-permute-done.3.refs_2_), channel_id=1, source_target_pairs={{0,8},{2,10},{8,16},{10,18},{16,24},{18,26},{24,28},{26,30},{28,20... | collective-permute-start | bytes 589832 | tf_op jit(solution)/shard_map/ppermute | solution.py:442
  27.7 8.5 %collective-permute-start.15 = (bf16[192,512]{1,0:T(8,128)(2,1)S(1)}, bf16[192,512]{1,0:T(8,128)(2,1)S(1)}, u32[]{:S(2)}, u32[]{:S(2)}) collective-permute-start(bf16[192,512]{1,0:T(8,128)(2,1)S(1)} %collective-permute-done.12.refs_4_), channel_id=1, source_target_pairs={{0,4},{2,6},{8,0},{10,2},{16,8},{18,10},{24,16},{26,18},{28,24},{3... | collective-permute-start | bytes 589832 | tf_op jit(solution)/shard_map/ppermute | solution.py:443
  32.7 7.4 %collective-permute-start.14 = (bf16[200,512]{1,0:T(8,128)(2,1)S(1)}, bf16[200,512]{1,0:T(8,128)(2,1)S(1)}, u32[]{:S(2)}, u32[]{:S(2)}) collective-permute-start(bf16[200,512]{1,0:T(8,128)(2,1)S(1)} %collective-permute-done.10.refs_5_), channel_id=1, source_target_pairs={{0,4},{2,6},{8,0},{10,2},{16,8},{18,10},{24,16},{26,18},{28,24},{3... | collective-permute-start | bytes 614408 | tf_op jit(solution)/shard_map/ppermute | solution.py:443
  34.4 5.7 %collective-permute-start.13 = (bf16[192,512]{1,0:T(8,128)(2,1)S(1)}, bf16[192,512]{1,0:T(8,128)(2,1)S(1)}, u32[]{:S(2)}, u32[]{:S(2)}) collective-permute-start(bf16[192,512]{1,0:T(8,128)(2,1)S(1)} %collective-permute-done.4.refs_2_), channel_id=1, source_target_pairs={{0,8},{2,10},{8,16},{10,18},{16,24},{18,26},{24,28},{26,30},{28,20... | collective-permute-start | bytes 589832 | tf_op jit(solution)/shard_map/ppermute | solution.py:442
  41.1 1.9 %collective-permute-start.16 = (bf16[192,1280]{1,0:T(8,128)(2,1)S(1)}, bf16[192,1280]{1,0:T(8,128)(2,1)S(1)}, u32[]{:S(2)}, u32[]{:S(2)}) collective-permute-start(bf16[192,1280]{1,0:T(8,128)(2,1)S(1)} %attend.11), channel_id=1, source_target_pairs={{0,2},{2,0},{4,6},{6,4},{8,10},{10,8},{12,14},{14,12},{16,18},{18,... | collective-permute-start | bytes 1474568 | tf_op jit(solution)/shard_map/ppermute | solution.py:489
  43.9 21.6 %collective-permute-start.18 = (bf16[96,1280]{1,0:T(8,128)(2,1)S(1)}, bf16[96,1280]{1,0:T(8,128)(2,1)S(1)}, u32[]{:S(2)}, u32[]{:S(2)}) collective-permute-start(bf16[96,1280]{1,0:T(8,128)(2,1)S(1)} %get-tuple-element.75), channel_id=1, source_target_pairs={{0,1},{1,0},{2,3},{3,2},{4,5},{5,4},{6,7},{7,6},{8,9},{9,8},{10,11... | collective-permute-start | bytes 737288 | tf_op jit(solution)/shard_map/ppermute | solution.py:542
  49.3 16.2 %collective-permute-start.19 = (bf16[96,1152]{1,0:T(8,128)(2,1)S(1)}, bf16[96,1152]{1,0:T(8,128)(2,1)S(1)}, u32[]{:S(2)}, u32[]{:S(2)}) collective-permute-start(bf16[96,1152]{1,0:T(8,128)(2,1)S(1)} %get-tuple-element.78), channel_id=1, source_target_pairs={{0,1},{1,0},{2,3},{3,2},{4,5},{5,4},{6,7},{7,6},{8,9},{9,8},{10,11... | collective-permute-start | bytes 663560 | tf_op jit(solution)/shard_map/ppermute | solution.py:542
  53.2 12.3 %collective-permute-start.20 = (bf16[96,1024]{1,0:T(8,128)(2,1)S(1)}, bf16[96,1024]{1,0:T(8,128)(2,1)S(1)}, u32[]{:S(2)}, u32[]{:S(2)}) collective-permute-start(bf16[96,1024]{1,0:T(8,128)(2,1)S(1)} %get-tuple-element.81), channel_id=1, source_target_pairs={{0,1},{1,0},{2,3},{3,2},{4,5},{5,4},{6,7},{7,6},{8,9},{9,8},{10,11... | collective-permute-start | bytes 589832 | tf_op jit(solution)/shard_map/ppermute | solution.py:542
  58.0 7.5 %collective-permute-start.21 = (bf16[96,896]{1,0:T(8,128)(2,1)S(1)}, bf16[96,896]{1,0:T(8,128)(2,1)S(1)}, u32[]{:S(2)}, u32[]{:S(2)}) collective-permute-start(bf16[96,896]{1,0:T(8,128)(2,1)S(1)} %get-tuple-element.84), channel_id=1, source_target_pairs={{0,1},{1,0},{2,3},{3,2},{4,5},{5,4},{6,7},{7,6},{8,9},{9,8},{10,11... | collective-permute-start | bytes 516104 | tf_op jit(solution)/shard_map/ppermute | solution.py:542
  59.6 8.5 %collective-permute-start.17 = (bf16[96,768]{1,0:T(8,128)(2,1)S(1)}, bf16[96,768]{1,0:T(8,128)(2,1)S(1)}, u32[]{:S(2)}, u32[]{:S(2)}) collective-permute-start(bf16[96,768]{1,0:T(8,128)(2,1)S(1)} %get-tuple-element.88), channel_id=1, source_target_pairs={{0,1},{1,0},{2,3},{3,2},{4,5},{5,4},{6,7},{7,6},{8,9},{9,8},{10,11... | collective-permute-start | bytes 442376 | tf_op jit(solution)/shard_map/ppermute | solution.py:542

commit v11 on v10

--- a/solution.py
+++ b/solution.py
@@ -244,32 +244,28 @@
     )(turned, *marks, *packets, *(state or ()), *([out_weight] if fetch else []))
 
 
-def turn_kernel(heads, chunk, whole_rows, *refs):
+def turn_kernel(heads, chunk, *refs):
     q_refs, turned_ref = refs[:-1], refs[-1]
     for i, q_ref in enumerate(q_refs):
-        base = my_core() * (heads * GROUP) if whole_rows[i] else 0
         for half in range(2):
             for h in range(heads):
-                columns = [
-                    pl.ds(pl.multiple_of(base + h * GROUP + g * HEAD_WIDTH, HEAD_WIDTH), HEAD_WIDTH)
-                    for g in range(QUERY_PER_KEY)
-                ]
+                columns = [slice(at, at + HEAD_WIDTH) for at in range(h * GROUP, (h + 1) * GROUP, HEAD_WIDTH)]
                 q = jnp.concatenate(
                     [q_ref[half * chunk : (half + 1) * chunk, at] for at in columns], axis=0
                 )
                 turned_ref[(2 * i + half) * heads + h] = jnp.transpose(q)
 
 
-def turn(heads, chunk, whole_rows, queries):
+def turn(heads, chunk, queries):
     vmem = pl.BlockSpec(memory_space=pltpu.VMEM)
     owners = len(queries)
     shape = (2 * owners * heads, HEAD_WIDTH, QUERY_PER_KEY * chunk)
     return pl.pallas_call(
-        functools.partial(turn_kernel, heads, chunk, whole_rows),
+        functools.partial(turn_kernel, heads, chunk),
         out_shape=jax.ShapeDtypeStruct(shape, jnp.bfloat16),
         in_specs=[vmem] * owners,
         out_specs=vmem,
-        cost_estimate=pl.CostEstimate(flops=1 << 20, bytes_accessed=4 << 20, transcendentals=0),
+        cost_estimate=pl.CostEstimate(flops=1 << 10, bytes_accessed=1 << 10, transcendentals=0),
         compiler_params=pltpu.CompilerParams(vmem_limit_bytes=VMEM_LIMIT),
         name="turn",
     )(*queries)
@@ -314,11 +310,15 @@
     for n, (first, _) in enumerate(bring):
         copies += fetch_columns(w_ref, first, refs.pop(0), sems, n * PIECES)
     chunk, core = sent_ref.shape[0], my_core()
-    total = product(leaving_first(other_ref), rows_of_core(held_ref, 1 - core))
+    other = leaving_first(other_ref)
     if begun:
-        total = total + begun_ref[...]
+        total = begun_ref[...] + product(other, rows_of_core(held_ref, 1 - core))
     else:
-        total = total + product(leaving_first(own_ref), rows_of_core(held_ref, core))
+        (rows_ref,) = refs
+        own, part = leaving_first(own_ref), own_ref.shape[1]
+        rows_ref[:, :part] = jnp.where(core == 0, own, other)
+        rows_ref[:, part:] = jnp.where(core == 0, other, own)
+        total = product(rows_ref[...], held_ref[...])
     both = total.astype(sent_ref.dtype)
     sent_ref[...] = both[:chunk]
     kept_ref[...] = both[chunk:]
@@ -332,6 +332,8 @@
     out_shape = [jax.ShapeDtypeStruct((rows // 2, width), jnp.bfloat16)] * 2
     out_shape += [jax.ShapeDtypeStruct((depth, columns), held.dtype) for _, columns in bring]
     in_specs, operands, scratch = [vmem] * 3, [own, other, held], []
+    if begun is None:
+        scratch.append(pltpu.VMEM((rows, depth), jnp.bfloat16))
     if bring:
         in_specs.append(pl.BlockSpec(memory_space=pltpu.HBM))
         operands.append(out_weight)
@@ -352,18 +354,20 @@
 
 
 def prepare_kernel(
-    chunk, q_ref, k_ref, v_ref, position_ref, sent_ref, kept_ref, mark_ref, query_ref, first_ref, sems
+    chunk, q_ref, k_ref, v_ref, position_ref, sent_ref, kept_ref, mark_ref, *query_refs_and_scratch
 ):
+    *query_refs, first_ref, sems = query_refs_and_scratch
     rows, width = k_ref.shape[0], k_ref.shape[1] // 2
-    columns = query_ref.shape[1]
+    columns = query_refs[0].shape[1]
     copies = [pltpu.make_async_copy(position_ref, first_ref, sems.at[4])]
     for n, (ref, core) in enumerate(((sent_ref, 1 - my_core()), (kept_ref, my_core()))):
         at = pl.ds(pl.multiple_of(core * width, width), width)
         for m, source in enumerate((k_ref, v_ref)):
             to = ref.at[pl.ds(0, rows), pl.ds(m * width, width)]
             copies.append(pltpu.make_async_copy(source.at[:, at], to, sems.at[2 * n + m]))
-    at = pl.ds(pl.multiple_of((1 - my_core()) * columns, columns), columns)
-    copies.append(pltpu.make_async_copy(q_ref.at[:, at], query_ref, sems.at[5]))
+    for n, (ref, core) in enumerate(zip(query_refs, (1 - my_core(), my_core()))):
+        at = pl.ds(pl.multiple_of(core * columns, columns), columns)
+        copies.append(pltpu.make_async_copy(q_ref.at[:, at], ref, sems.at[5 + n]))
     for copy in copies:
         copy.start()
     copies[0].wait()
@@ -385,13 +389,13 @@
             jax.ShapeDtypeStruct((rows + TILE, width), jnp.bfloat16),
             jax.ShapeDtypeStruct((rows, width), jnp.bfloat16),
             jax.ShapeDtypeStruct((HEADER, width // 2), jnp.bfloat16),
-            jax.ShapeDtypeStruct((rows, queries.shape[1] // 2), jnp.bfloat16),
-        ],
+        ]
+        + [jax.ShapeDtypeStruct((rows, queries.shape[1] // 2), jnp.bfloat16)] * 2,
         in_specs=[hbm] * 4,
-        out_specs=[vmem] * 4,
+        out_specs=[vmem] * 5,
         scratch_shapes=[
             pltpu.SMEM(positions.shape, jnp.int32),
-            pltpu.SemaphoreType.DMA((6,)),
+            pltpu.SemaphoreType.DMA((7,)),
         ],
         compiler_params=pltpu.CompilerParams(vmem_limit_bytes=VMEM_LIMIT),
         name="prepare",
@@ -442,13 +446,13 @@
     up = lambda x: lax.ppermute(x, "blk", clock)
     down = lambda x: lax.ppermute(x, "blk", counter)
 
-    sent, x, mark, q_sent = prepare(queries, keys, values, positions)
+    sent, x, mark, q_sent, q_own = prepare(queries, keys, values, positions)
     got = lax.ppermute(sent, "blk", sibling)
-    y = jnp.concatenate(
-        [got[:rows], jnp.concatenate([mark, got[rows : rows + HEADER, :width]], axis=1)], axis=0
-    )
+    header = jnp.concatenate([mark, got[rows : rows + HEADER, :width]], axis=1)
+    y = got[:rows]
+    x_first, y_first = (jnp.concatenate([part, header], axis=0) for part in (x, y))
     q_got = lax.ppermute(q_sent, "blk", sibling)
-    turned = turn(heads, chunk, (True, False), [queries, q_got])
+    turned = turn(heads, chunk, [q_own, q_got])
 
     def call(pairs, state, own=False, last=False, fetch=None, which=(0, 1)):
         each = range(len(pairs))
@@ -460,35 +464,34 @@
             own_at=lambda i: i,
             last=last,
             members=[(2 * j + i, 0) for j in each for i in range(2)],
-            headers=[(2 + 2 * j, rows, i * width) for j in each for i in range(2)],
+            headers=[(1 + 2 * j + pairs[j][2], rows, i * width) for j in each for i in range(2)],
             owner_headers=[(0, rows, 0), (0, rows, width)],
             fetch=fetch,
             which=which,
         )
-        packets = [packet for pair in pairs for packet in pair]
-        return attend(plan, turned, [y], packets, state, out_weight)
-
-    ups = downs = (x, y)
+        packets = [packet for pair in pairs for packet in pair[:2]]
+        return attend(plan, turned, [y_first], packets, state, out_weight)
+
+    up_first, up_second, down_first, down_second = x_first, y, y_first, x
+    state = call([(x, y_first, 1)], None, own=True)
+    held = []
     for r in range(1, half):
-        (x_up, y_up), (x_down, y_down) = ups, downs
         if r > 1:
-            y_up, y_down, *state = lax.optimization_barrier((y_up, y_down, *state))
-        ups, downs = (up(x_up), up(y_up)), (down(x_down), down(y_down))
-        if r == 1:
-            *state, held = call([(x, y)], None, own=True, fetch=fetch[:1])
-        elif r == 2:
-            *state, more = call(arrived, state, fetch=fetch[1:])
-        else:
-            state = call(arrived, state)
-        arrived = [ups, downs]
-    x_up, y_down, y_up, *state = lax.optimization_barrier((ups[0], downs[1], ups[1], *state))
-    arrived = [(x_up, y_up), downs]
-    far = (up(x_up), down(y_down))
-    state = call(arrived, state)
+            up_first, down_first, *state = lax.optimization_barrier((up_first, down_first, *state))
+        up_first, up_second = up(up_first), up(up_second)
+        down_first, down_second = down(down_first), down(down_second)
+        if r > 1:
+            *state, more = call(arrived, state, fetch=fetch[len(held) : len(held) + 1])
+            held.append(more)
+        arrived = [(up_first, up_second, 0), (down_second, down_first, 1)]
+    up_first, down_first, *state = lax.optimization_barrier((up_first, down_first, *state))
+    far = (up(up_first), down(down_first), 1)
+    *state, more = call(arrived, state, fetch=fetch[len(held) :])
+    held.append(more)
     (theirs,) = call([far], state, last=True, which=(1,))
     other = lax.ppermute(theirs, "blk", sibling)
     (own,) = call([far], state, last=True, which=(0,))
-    return own, other, [held, more]
+    return own, other, held
 
 
 def one_head_a_device(count, queries, keys, values, positions):
@@ -513,7 +516,7 @@
         headers=[(0, j * size + rows, 0) for j in range(count)],
         owner_headers=[(0, rows, 0)],
     )
-    turned = turn(heads, chunk, (False,), [queries])
+    turned = turn(heads, chunk, [queries])
     return attend(plan, turned, [], [packets], None)[0]
 
 
@@ -530,9 +533,9 @@
     widths = [out_weight.shape[1] * share // sum(shares) for share in shares]
     cuts = [(sum(widths[:j]), columns) for j, columns in enumerate(widths)]
     own, other, held = split_over_cores(
-        count, queries, keys, values, positions, out_weight, cuts[:2]
+        count, queries, keys, values, positions, out_weight, cuts[:3]
     )
-    bring = [cuts[j + 1 : j + 2] if j > 0 else [] for j in range(len(cuts))]
+    bring = [cuts[j + 2 : j + 3] if j > 0 else [] for j in range(len(cuts))]
     received, kept = [], []
     for j in range(len(cuts)):
         source = own if j == 0 else after(own, sent)

time: 69.1 us -> 67.7 us (0.980)
  Pallas kernels: 29.5 us -> 26.2 us
  waiting for transfers between devices: 15.8 us -> 18.9 us
  local copies, waits for them, and re-layouts: 1.22 us -> 0.02 us
    ppermute x7, starting transfers between devices: 2.68 us -> 12.5 us  [split_over_cores(): down = lambda x: lax.ppermute(x, 'blk', counter)]
    ppermute x7, starting transfers between devices: 12.8 us -> 3.03 us  [split_over_cores(): up = lambda x: lax.ppermute(x, 'blk', clock)]
    ppermute x5, waiting for transfers between devices: 5.82 us -> 9.42 us  [shards(): received.append(lax.ppermute(sent, 'inner', [(0, 1), (1, 0)]))]
    pallas_call x5, Pallas kernels: 12.2 us -> 8.62 us  [project(): pl.pallas_call(functools.partial(project_kernel, bring, begun is not None...]
    ppermute x7, waiting for transfers between devices: 4.59 us -> 2.3 us  [split_over_cores(): down = lambda x: lax.ppermute(x, 'blk', counter)]
    ppermute x7, waiting for transfers between devices: 4.35 us -> 6.12 us  [split_over_cores(): up = lambda x: lax.ppermute(x, 'blk', clock)]
    unnamed x2 -> x0, local copies, waits for them, and re-layouts: 1.2 us -> none
  transfers between devices with their start and end apart: 22 -> 22, of which waited for: 10 -> 12; matrix products, arithmetic and copies ran while one was open for 0% -> 0% of each run, Pallas kernels for 37% -> 33%
where the time goes in v11:
time: 67.7 us; the launch traced here: 67.5 us
  Pallas kernels  26.2 us (39%)
  starting transfers between devices  22.1 us (33%)
  waiting for transfers between devices  18.9 us (28%)
    pallas_call x6, Pallas kernels, attend(): pl.pallas_call(functools.partial(attend_kernel, plan), out_shape=out_shap...  13.2 us
    ppermute x7, starting transfers between devices, split_over_cores(): down = lambda x: lax.ppermute(x, 'blk', counter)  12.5 us
    ppermute x5, waiting for transfers between devices, shards(): received.append(lax.ppermute(sent, 'inner', [(0, 1), (1, 0)]))  9.42 us
    pallas_call x5, Pallas kernels, project(): pl.pallas_call(functools.partial(project_kernel, bring, begun is not None...  8.62 us
    ppermute x7, waiting for transfers between devices, split_over_cores(): up = lambda x: lax.ppermute(x, 'blk', clock)  6.12 us
    ppermute x5, starting transfers between devices, shards(): received.append(lax.ppermute(sent, 'inner', [(0, 1), (1, 0)]))  5.87 us
    ppermute x7, starting transfers between devices, split_over_cores(): up = lambda x: lax.ppermute(x, 'blk', clock)  3.03 us
    ppermute x7, waiting for transfers between devices, split_over_cores(): down = lambda x: lax.ppermute(x, 'blk', counter)  2.3 us
  transfers between devices with their start and end apart: 22, of which 12 were waited for; matrix products, arithmetic and copies ran while one was open for 0% of the time, Pallas kernels for 33%

profile of v11, /device:TPU:0, one launch (start us, length us, event | category | flops | bytes accessed | tf_op | source)
XLA Modules:
  0.0 67.5 jit_solution(13963003218221687640)
XLA Ops:
  0.0 1.4 %prepare.1 = (bf16[208,512]{1,0:T(8,128)(2,1)S(1)}, bf16[192,512]{1,0:T(8,128)(2,1)S(1)}, bf16[8,256]{1,0:T(8,128)(2,1)S(1)}, bf16[192,1280]{1,0:T(8,128)(2,1)S(1)}, bf16[192,1280]{1,0:T(8,128)(2,1)S(1)}) custom-call(bf16[192,2560]{1,0:T(8,128)(2,1)} %q_ref.1, bf16[192,512]{1,0:T(8,128)(2,1)} %k_ref.1, bf16[192,512]{1,0:T(8,128)(2,1)} %v_ref.1, s32[192]{0:T(256)} %position_ref.1), custom_call_target="tpu_custom_call" | custom-call | tf_op jit(solution)/shard_map/prepare/pallas_call | solution.py:386
  1.4 0.5 collective-permute-start.1
  2.0 0.1 collective-permute-start
  2.0 1.0 %collective-permute-done.1 = bf16[208,512]{1,0:T(8,128)(2,1)S(1)} collective-permute-done((bf16[208,512]{1,0:T(8,128)(2,1)S(1)}, bf16[208,512]{1,0:T(8,128)(2,1)S(1)}, u32[]{:S(2)}, u32[]{:S(2)}) %collective-permute-start.1) | collective-permute-done | bytes 213024 | tf_op jit(solution)/shard_map/ppermute | solution.py:450
  3.1 2.9 %collective-permute-start.3 = (bf16[200,512]{1,0:T(8,128)(2,1)S(1)}, bf16[200,512]{1,0:T(8,128)(2,1)S(1)}, u32[]{:S(2)}, u32[]{:S(2)}) collective-permute-start(bf16[200,512]{1,0:T(8,128)(2,1)S(1)} %get-tuple-element.94.refs_1_.refs_3_), channel_id=1, source_target_pairs={{0,4},{2,6},{8,0},{10,2},{16,8},{18,10},{24,16},{26,18},{28,24},{3... | collective-permute-start | bytes 614408 | tf_op jit(solution)/shard_map/ppermute | solution.py:447
  6.1 0.1 collective-permute-start.2
  6.2 1.9 %collective-permute-start.7 = (bf16[192,512]{1,0:T(8,128)(2,1)S(1)}, bf16[192,512]{1,0:T(8,128)(2,1)S(1)}, u32[]{:S(2)}, u32[]{:S(2)}) collective-permute-start(bf16[192,512]{1,0:T(8,128)(2,1)S(1)} %get-tuple-element.53.refs_2_), channel_id=1, source_target_pairs={{0,4},{2,6},{8,0},{10,2},{16,8},{18,10},{24,16},{26,18},{28,24},{3... | collective-permute-start | bytes 589832 | tf_op jit(solution)/shard_map/ppermute | solution.py:447
  8.1 0.1 collective-permute-start.6
  8.2 0.3 turn.1.refs_0_
  8.5 1.9 %attend.6 = (f32[8,1,480]{2,1,0:T(1,128)S(1)}, f32[8,144,480]{2,1,0:T(8,128)S(1)}) custom-call(bf16[8,128,480]{2,1,0:T(8,128)(2,1)S(1)} %turn.1.refs_0_, bf16[200,512]{1,0:T(8,128)(2,1)S(1)} %get-tuple-element.94.refs_1_.refs_3_, bf16[192,512]{1,0:T(8,128)(2,1)S(1)} %get-tuple-element.53.refs_2_, bf16[200,512]{1,0:T(8,128)(2,1)S(1)} %get-tuple-element.94.refs_1_.refs_3_), custom_call_target="tpu_custom_call" | custom-call | flops 377487360 | bytes 4194304 | tf_op jit(solution)/shard_map/attend/pallas_call | solution.py:233
  10.4 1.5 %collective-permute-done.3.refs_5_ = bf16[200,512]{1,0:T(8,128)(2,1)S(1)} collective-permute-done((bf16[200,512]{1,0:T(8,128)(2,1)S(1)}, bf16[200,512]{1,0:T(8,128)(2,1)S(1)}, u32[]{:S(2)}, u32[]{:S(2)}) %collective-permute-start.3) | collective-permute-done | bytes 204832 | tf_op jit(solution)/shard_map/ppermute | solution.py:447
  12.0 2.0 %collective-permute-done.2.refs_2_ = bf16[200,512]{1,0:T(8,128)(2,1)S(1)} collective-permute-done((bf16[200,512]{1,0:T(8,128)(2,1)S(1)}, bf16[200,512]{1,0:T(8,128)(2,1)S(1)}, u32[]{:S(2)}, u32[]{:S(2)}) %collective-permute-start.2) | collective-permute-done | bytes 204832 | tf_op jit(solution)/shard_map/ppermute | solution.py:446
  14.0 0.1 collective-permute-start.4
  14.1 1.9 %collective-permute-start.5 = (bf16[200,512]{1,0:T(8,128)(2,1)S(1)}, bf16[200,512]{1,0:T(8,128)(2,1)S(1)}, u32[]{:S(2)}, u32[]{:S(2)}) collective-permute-start(bf16[200,512]{1,0:T(8,128)(2,1)S(1)} %collective-permute-done.3.refs_5_), channel_id=1, source_target_pairs={{0,4},{2,6},{8,0},{10,2},{16,8},{18,10},{24,16},{26,18},{28,24},{3... | collective-permute-start | bytes 614408 | tf_op jit(solution)/shard_map/ppermute | solution.py:447
  16.1 0.1 collective-permute-done.7.refs_4_
  16.2 2.0 %collective-permute-start.11 = (bf16[192,512]{1,0:T(8,128)(2,1)S(1)}, bf16[192,512]{1,0:T(8,128)(2,1)S(1)}, u32[]{:S(2)}, u32[]{:S(2)}) collective-permute-start(bf16[192,512]{1,0:T(8,128)(2,1)S(1)} %collective-permute-done.7.refs_4_), channel_id=1, source_target_pairs={{0,4},{2,6},{8,0},{10,2},{16,8},{18,10},{24,16},{26,18},{28,24},{3... | collective-permute-start | bytes 589832 | tf_op jit(solution)/shard_map/ppermute | solution.py:447
  18.2 0.1 collective-permute-start.10
  18.3 3.1 %attend.7 = (f32[8,1,480]{2,1,0:T(1,128)S(1)}, f32[8,144,480]{2,1,0:T(8,128)S(1)}, bf16[2560,1280]{1,0:T(8,128)(2,1)S(1)}) custom-call(bf16[8,128,480]{2,1,0:T(8,128)(2,1)S(1)} %turn.1.refs_0_, bf16[200,512]{1,0:T(8,128)(2,1)S(1)} %get-tuple-element.94.refs_1_.refs_3_, bf16[200,512]{1,0:T(8,128)(2,1)S(1)} %collective-permute-done.2.refs_2_, ...), custom_call_target="tpu_custom_call" | custom-call | flops 754974720 | bytes 4194304 | tf_op jit(solution)/shard_map/attend/pallas_call | solution.py:233
  21.4 1.2 %collective-permute-done.4.refs_2_ = bf16[200,512]{1,0:T(8,128)(2,1)S(1)} collective-permute-done((bf16[200,512]{1,0:T(8,128)(2,1)S(1)}, bf16[200,512]{1,0:T(8,128)(2,1)S(1)}, u32[]{:S(2)}, u32[]{:S(2)}) %collective-permute-start.4) | collective-permute-done | bytes 204832 | tf_op jit(solution)/shard_map/ppermute | solution.py:446
  22.6 1.3 %collective-permute-start.8 = (bf16[200,512]{1,0:T(8,128)(2,1)S(1)}, bf16[200,512]{1,0:T(8,128)(2,1)S(1)}, u32[]{:S(2)}, u32[]{:S(2)}) collective-permute-start(bf16[200,512]{1,0:T(8,128)(2,1)S(1)} %collective-permute-done.4.refs_2_), channel_id=1, source_target_pairs={{0,8},{2,10},{8,16},{10,18},{16,24},{18,26},{24,28},{26,30},{28,20... | collective-permute-start | bytes 614408 | tf_op jit(solution)/shard_map/ppermute | solution.py:446
  23.9 0.7 %collective-permute-start.9 = (bf16[200,512]{1,0:T(8,128)(2,1)S(1)}, bf16[200,512]{1,0:T(8,128)(2,1)S(1)}, u32[]{:S(2)}, u32[]{:S(2)}) collective-permute-start(bf16[200,512]{1,0:T(8,128)(2,1)S(1)} %collective-permute-done.5.refs_5_), channel_id=1, source_target_pairs={{0,4},{2,6},{8,0},{10,2},{16,8},{18,10},{24,16},{26,18},{28,24},{3... | collective-permute-start | bytes 614408 | tf_op jit(solution)/shard_map/ppermute | solution.py:447
  24.7 0.1 collective-permute-done.11.refs_4_
  24.8 2.3 %collective-permute-start.15 = (bf16[192,512]{1,0:T(8,128)(2,1)S(1)}, bf16[192,512]{1,0:T(8,128)(2,1)S(1)}, u32[]{:S(2)}, u32[]{:S(2)}) collective-permute-start(bf16[192,512]{1,0:T(8,128)(2,1)S(1)} %collective-permute-done.11.refs_4_), channel_id=1, source_target_pairs={{0,4},{2,6},{8,0},{10,2},{16,8},{18,10},{24,16},{26,18},{28,24},{3... | collective-permute-start | bytes 589832 | tf_op jit(solution)/shard_map/ppermute | solution.py:447
  27.1 3.1 %attend.8 = (f32[8,1,480]{2,1,0:T(1,128)S(1)}, f32[8,144,480]{2,1,0:T(8,128)S(1)}, bf16[2560,1152]{1,0:T(8,128)(2,1)S(1)}) custom-call(bf16[8,128,480]{2,1,0:T(8,128)(2,1)S(1)} %turn.1.refs_0_, bf16[200,512]{1,0:T(8,128)(2,1)S(1)} %get-tuple-element.94.refs_1_.refs_3_, bf16[200,512]{1,0:T(8,128)(2,1)S(1)} %collective-permute-done.4.refs_2_, ...), custom_call_target="tpu_custom_call" | custom-call | flops 754974720 | bytes 4194304 | tf_op jit(solution)/shard_map/attend/pallas_call | solution.py:233
  30.2 1.0 %collective-permute-done.8.refs_2_ = bf16[200,512]{1,0:T(8,128)(2,1)S(1)} collective-permute-done((bf16[200,512]{1,0:T(8,128)(2,1)S(1)}, bf16[200,512]{1,0:T(8,128)(2,1)S(1)}, u32[]{:S(2)}, u32[]{:S(2)}) %collective-permute-start.8) | collective-permute-done | bytes 204832 | tf_op jit(solution)/shard_map/ppermute | solution.py:446
  31.2 1.3 %collective-permute-start.12 = (bf16[200,512]{1,0:T(8,128)(2,1)S(1)}, bf16[200,512]{1,0:T(8,128)(2,1)S(1)}, u32[]{:S(2)}, u32[]{:S(2)}) collective-permute-start(bf16[200,512]{1,0:T(8,128)(2,1)S(1)} %collective-permute-done.8.refs_2_), channel_id=1, source_target_pairs={{0,8},{2,10},{8,16},{10,18},{16,24},{18,26},{24,28},{26,30},{28,20... | collective-permute-start | bytes 614408 | tf_op jit(solution)/shard_map/ppermute | solution.py:446
  32.5 0.7 %collective-permute-start.13 = (bf16[200,512]{1,0:T(8,128)(2,1)S(1)}, bf16[200,512]{1,0:T(8,128)(2,1)S(1)}, u32[]{:S(2)}, u32[]{:S(2)}) collective-permute-start(bf16[200,512]{1,0:T(8,128)(2,1)S(1)} %collective-permute-done.9.refs_5_), channel_id=1, source_target_pairs={{0,4},{2,6},{8,0},{10,2},{16,8},{18,10},{24,16},{26,18},{28,24},{3... | collective-permute-start | bytes 614408 | tf_op jit(solution)/shard_map/ppermute | solution.py:447
  33.3 0.5 collective-permute-done.15.refs_4_
  33.7 1.7 %collective-permute-done.14.refs_3_ = bf16[192,512]{1,0:T(8,128)(2,1)S(1)} collective-permute-done((bf16[192,512]{1,0:T(8,128)(2,1)S(1)}, bf16[192,512]{1,0:T(8,128)(2,1)S(1)}, u32[]{:S(2)}, u32[]{:S(2)}) %collective-permute-start.14) | collective-permute-done | bytes 196640 | tf_op jit(solution)/shard_map/ppermute | solution.py:446
  35.4 3.1 %attend.9 = (f32[8,1,480]{2,1,0:T(1,128)S(1)}, f32[8,144,480]{2,1,0:T(8,128)S(1)}, bf16[2560,1024]{1,0:T(8,128)(2,1)S(1)}) custom-call(bf16[8,128,480]{2,1,0:T(8,128)(2,1)S(1)} %turn.1.refs_0_, bf16[200,512]{1,0:T(8,128)(2,1)S(1)} %get-tuple-element.94.refs_1_.refs_3_, bf16[200,512]{1,0:T(8,128)(2,1)S(1)} %collective-permute-done.8.refs_2_, ...), custom_call_target="tpu_custom_call" | custom-call | flops 754974720 | bytes 4194304 | tf_op jit(solution)/shard_map/attend/pallas_call | solution.py:233
  38.6 0.1 collective-permute-done.12.refs_2_
  38.7 1.0 %attend.11 = bf16[192,1280]{1,0:T(8,128)(2,1)S(1)} custom-call(bf16[8,128,480]{2,1,0:T(8,128)(2,1)S(1)} %turn.1.refs_0_, bf16[200,512]{1,0:T(8,128)(2,1)S(1)} %get-tuple-element.94.refs_1_.refs_3_, bf16[200,512]{1,0:T(8,128)(2,1)S(1)} %collective-permute-done.12.refs_2_, bf16[200,512]{1,0:T(8,128)(2,1)S(1)} %collective-permute-done.13.refs_3_, ...), custom_call_target="tpu_custom_call" | custom-call | flops 377487360 | bytes 4194304 | tf_op jit(solution)/shard_map/attend/pallas_call | solution.py:233
  39.8 1.0 %attend.10.own_ref = bf16[192,1280]{1,0:T(8,128)(2,1)S(1)} custom-call(bf16[8,128,480]{2,1,0:T(8,128)(2,1)S(1)} %turn.1.refs_0_, bf16[200,512]{1,0:T(8,128)(2,1)S(1)} %get-tuple-element.94.refs_1_.refs_3_, bf16[200,512]{1,0:T(8,128)(2,1)S(1)} %collective-permute-done.12.refs_2_, bf16[200,512]{1,0:T(8,128)(2,1)S(1)} %collective-permute-done.13.refs_3_, ...), custom_call_target="tpu_custom_call" | custom-call | flops 377487360 | bytes 4194304 | tf_op jit(solution)/shard_map/attend/pallas_call | solution.py:233
  40.8 0.8 %begin.1.refs_0_ = f32[192,1280]{1,0:T(8,128)S(1)} custom-call(bf16[192,1280]{1,0:T(8,128)(2,1)S(1)} %attend.10.own_ref, bf16[2560,1280]{1,0:T(8,128)(2,1)S(1)} %get-tuple-element.74.held_ref), custom_call_target="tpu_custom_call" | custom-call | flops 1024 | bytes 1024 | tf_op jit(solution)/shard_map/begin/pallas_call | solution.py:292
  41.6 0.8 %project.5 = (bf16[96,1280]{1,0:T(8,128)(2,1)S(1)}, bf16[96,1280]{1,0:T(8,128)(2,1)S(1)}) custom-call(bf16[192,1280]{1,0:T(8,128)(2,1)S(1)} %attend.10.own_ref, bf16[192,1280]{1,0:T(8,128)(2,1)S(1)} %collective-permute-done.16.other_ref, bf16[2560,1280]{1,0:T(8,128)(2,1)S(1)} %get-tuple-element.74.held_ref, f32[192,1280]{1,0:T(8,128)S(1)} %begin.1.refs_0_), custom_call_target="tpu_custom_call" | custom-call | flops 1024 | bytes 1024 | tf_op jit(solution)/shard_map/project/pallas_call | solution.py:344
  42.5 1.6 %collective-permute-start.18 = (bf16[96,1280]{1,0:T(8,128)(2,1)S(1)}, bf16[96,1280]{1,0:T(8,128)(2,1)S(1)}, u32[]{:S(2)}, u32[]{:S(2)}) collective-permute-start(bf16[96,1280]{1,0:T(8,128)(2,1)S(1)} %get-tuple-element.75), channel_id=1, source_target_pairs={{0,1},{1,0},{2,3},{3,2},{4,5},{5,4},{6,7},{7,6},{8,9},{9,8},{10,11... | collective-permute-start | bytes 737288 | tf_op jit(solution)/shard_map/ppermute | solution.py:545
  44.0 2.9 %project.6 = (bf16[96,1152]{1,0:T(8,128)(2,1)S(1)}, bf16[96,1152]{1,0:T(8,128)(2,1)S(1)}, bf16[2560,896]{1,0:T(8,128)(2,1)S(1)}) custom-call(bf16[192,1280]{1,0:T(8,128)(2,1)S(1)} %attend.10.own_ref, bf16[192,1280]{1,0:T(8,128)(2,1)S(1)} %collective-permute-done.16.other_ref, bf16[2560,1152]{1,0:T(8,128)(2,1)S(1)} %get-tuple-element.77.held_ref, ...), custom_call_target="tpu_custom_call" | custom-call | flops 1024 | bytes 1024 | tf_op jit(solution)/shard_map/project/pallas_call | solution.py:344
  46.9 0.6 collective-permute-start.19
  47.5 2.7 %project.7 = (bf16[96,1024]{1,0:T(8,128)(2,1)S(1)}, bf16[96,1024]{1,0:T(8,128)(2,1)S(1)}, bf16[2560,768]{1,0:T(8,128)(2,1)S(1)}) custom-call(bf16[192,1280]{1,0:T(8,128)(2,1)S(1)} %attend.10.own_ref, bf16[192,1280]{1,0:T(8,128)(2,1)S(1)} %collective-permute-done.16.other_ref, bf16[2560,1024]{1,0:T(8,128)(2,1)S(1)} %get-tuple-element.80.held_ref, ...), custom_call_target="tpu_custom_call" | custom-call | flops 1024 | bytes 1024 | tf_op jit(solution)/shard_map/project/pallas_call | solution.py:344
  50.3 1.6 %collective-permute-start.20 = (bf16[96,1024]{1,0:T(8,128)(2,1)S(1)}, bf16[96,1024]{1,0:T(8,128)(2,1)S(1)}, u32[]{:S(2)}, u32[]{:S(2)}) collective-permute-start(bf16[96,1024]{1,0:T(8,128)(2,1)S(1)} %get-tuple-element.81), channel_id=1, source_target_pairs={{0,1},{1,0},{2,3},{3,2},{4,5},{5,4},{6,7},{7,6},{8,9},{9,8},{10,11... | collective-permute-start | bytes 589832 | tf_op jit(solution)/shard_map/ppermute | solution.py:545
  51.8 1.2 %project.8 = (bf16[96,896]{1,0:T(8,128)(2,1)S(1)}, bf16[96,896]{1,0:T(8,128)(2,1)S(1)}) custom-call(bf16[192,1280]{1,0:T(8,128)(2,1)S(1)} %attend.10.own_ref, bf16[192,1280]{1,0:T(8,128)(2,1)S(1)} %collective-permute-done.16.other_ref, bf16[2560,896]{1,0:T(8,128)(2,1)S(1)} %get-tuple-element.83.held_ref), custom_call_target="tpu_custom_call" | custom-call | flops 1024 | bytes 1024 | tf_op jit(solution)/shard_map/project/pallas_call | solution.py:344
  53.0 0.6 collective-permute-start.21
  53.7 0.9 %project.9 = (bf16[96,768]{1,0:T(8,128)(2,1)S(1)}, bf16[96,768]{1,0:T(8,128)(2,1)S(1)}) custom-call(bf16[192,1280]{1,0:T(8,128)(2,1)S(1)} %attend.10.own_ref, bf16[192,1280]{1,0:T(8,128)(2,1)S(1)} %collective-permute-done.16.other_ref, bf16[2560,768]{1,0:T(8,128)(2,1)S(1)} %get-tuple-element.86.held_ref), custom_call_target="tpu_custom_call" | custom-call | flops 1024 | bytes 1024 | tf_op jit(solution)/shard_map/project/pallas_call | solution.py:344
  54.6 1.5 %collective-permute-start.17 = (bf16[96,768]{1,0:T(8,128)(2,1)S(1)}, bf16[96,768]{1,0:T(8,128)(2,1)S(1)}, u32[]{:S(2)}, u32[]{:S(2)}) collective-permute-start(bf16[96,768]{1,0:T(8,128)(2,1)S(1)} %get-tuple-element.88), channel_id=1, source_target_pairs={{0,1},{1,0},{2,3},{3,2},{4,5},{5,4},{6,7},{7,6},{8,9},{9,8},{10,11... | collective-permute-start | bytes 442376 | tf_op jit(solution)/shard_map/ppermute | solution.py:545
  56.1 7.8 %collective-permute-done.21.refs_7_ = bf16[96,896]{1,0:T(8,128)(2,1)S(1)} collective-permute-done((bf16[96,896]{1,0:T(8,128)(2,1)S(1)}, bf16[96,896]{1,0:T(8,128)(2,1)S(1)}, u32[]{:S(2)}, u32[]{:S(2)}) %collective-permute-start.21) | collective-permute-done | bytes 172064 | tf_op jit(solution)/shard_map/ppermute | solution.py:545
  63.9 1.1 %finish.2.refs_2_ = bf16[96,5120]{1,0:T(8,128)(2,1)} custom-call(bf16[96,1280]{1,0:T(8,128)(2,1)S(1)} %get-tuple-element.89.refs_0_, bf16[96,1152]{1,0:T(8,128)(2,1)S(1)} %get-tuple-element.90.refs_1_, bf16[96,1024]{1,0:T(8,128)(2,1)S(1)} %get-tuple-element.91.refs_2_, bf16[96,896]{1,0:T(8,128)(2,1)S(1)} %get-tuple-element.92.refs_3_, ...), custom_call_target="tpu_custom_call" | custom-call | flops 1024 | bytes 1024 | tf_op jit(solution)/shard_map/finish/pallas_call | solution.py:422
  65.0 1.6 %collective-permute-done.17.refs_1_ = bf16[96,768]{1,0:T(8,128)(2,1)S(1)} collective-permute-done((bf16[96,768]{1,0:T(8,128)(2,1)S(1)}, bf16[96,768]{1,0:T(8,128)(2,1)S(1)}, u32[]{:S(2)}, u32[]{:S(2)}) %collective-permute-start.17) | collective-permute-done | bytes 147488 | tf_op jit(solution)/shard_map/ppermute | solution.py:545
  66.7 0.7 %finish.3 = bf16[96,5120]{1,0:T(8,128)(2,1)} custom-call(bf16[96,768]{1,0:T(8,128)(2,1)S(1)} %get-tuple-element.87.refs_0_, bf16[96,768]{1,0:T(8,128)(2,1)S(1)} %collective-permute-done.17.refs_1_, bf16[96,5120]{1,0:T(8,128)(2,1)} %finish.2.refs_2_), custom_call_target="tpu_custom_call", output_to_operand_aliasing={{}: (2, {})} | custom-call | flops 1024 | bytes 1024 | tf_op jit(solution)/shard_map/finish/pallas_call | solution.py:422
  (15 shorter events, 0.2 us)
Async XLA Ops:
  1.4 1.6 %collective-permute-start.1 = (bf16[208,512]{1,0:T(8,128)(2,1)S(1)}, bf16[208,512]{1,0:T(8,128)(2,1)S(1)}, u32[]{:S(2)}, u32[]{:S(2)}) collective-permute-start(bf16[208,512]{1,0:T(8,128)(2,1)S(1)} %get-tuple-element.51), channel_id=1, source_target_pairs={{0,2},{2,0},{4,6},{6,4},{8,10},{10,8},{12,14},{14,12},{16,18},{18,... | collective-permute-start | bytes 638984 | tf_op jit(solution)/shard_map/ppermute | solution.py:450
  2.0 6.2 %collective-permute-start = (bf16[192,1280]{1,0:T(8,128)(2,1)S(1)}, bf16[192,1280]{1,0:T(8,128)(2,1)S(1)}, u32[]{:S(2)}, u32[]{:S(2)}) collective-permute-start(bf16[192,1280]{1,0:T(8,128)(2,1)S(1)} %get-tuple-element.50), channel_id=1, source_target_pairs={{0,2},{2,0},{4,6},{6,4},{8,10},{10,8},{12,14},{14,12},{16,18},{18,... | collective-permute-start | bytes 1474568 | tf_op jit(solution)/shard_map/ppermute | solution.py:454
  3.1 8.9 %collective-permute-start.3 = (bf16[200,512]{1,0:T(8,128)(2,1)S(1)}, bf16[200,512]{1,0:T(8,128)(2,1)S(1)}, u32[]{:S(2)}, u32[]{:S(2)}) collective-permute-start(bf16[200,512]{1,0:T(8,128)(2,1)S(1)} %get-tuple-element.94.refs_1_.refs_3_), channel_id=1, source_target_pairs={{0,4},{2,6},{8,0},{10,2},{16,8},{18,10},{24,16},{26,18},{28,24},{3... | collective-permute-start | bytes 614408 | tf_op jit(solution)/shard_map/ppermute | solution.py:447
  6.1 8.0 %collective-permute-start.2 = (bf16[200,512]{1,0:T(8,128)(2,1)S(1)}, bf16[200,512]{1,0:T(8,128)(2,1)S(1)}, u32[]{:S(2)}, u32[]{:S(2)}) collective-permute-start(bf16[200,512]{1,0:T(8,128)(2,1)S(1)} %get-tuple-element.93), channel_id=1, source_target_pairs={{0,8},{2,10},{8,16},{10,18},{16,24},{18,26},{24,28},{26,30},{28,20... | collective-permute-start | bytes 614408 | tf_op jit(solution)/shard_map/ppermute | solution.py:446
  6.2 10.0 %collective-permute-start.7 = (bf16[192,512]{1,0:T(8,128)(2,1)S(1)}, bf16[192,512]{1,0:T(8,128)(2,1)S(1)}, u32[]{:S(2)}, u32[]{:S(2)}) collective-permute-start(bf16[192,512]{1,0:T(8,128)(2,1)S(1)} %get-tuple-element.53.refs_2_), channel_id=1, source_target_pairs={{0,4},{2,6},{8,0},{10,2},{16,8},{18,10},{24,16},{26,18},{28,24},{3... | collective-permute-start | bytes 589832 | tf_op jit(solution)/shard_map/ppermute | solution.py:447
  8.1 10.1 %collective-permute-start.6 = (bf16[192,512]{1,0:T(8,128)(2,1)S(1)}, bf16[192,512]{1,0:T(8,128)(2,1)S(1)}, u32[]{:S(2)}, u32[]{:S(2)}) collective-permute-start(bf16[192,512]{1,0:T(8,128)(2,1)S(1)} %slice.8), channel_id=1, source_target_pairs={{0,8},{2,10},{8,16},{10,18},{16,24},{18,26},{24,28},{26,30},{28,20... | collective-permute-start | bytes 589832 | tf_op jit(solution)/shard_map/ppermute | solution.py:446
  14.0 8.6 %collective-permute-start.4 = (bf16[200,512]{1,0:T(8,128)(2,1)S(1)}, bf16[200,512]{1,0:T(8,128)(2,1)S(1)}, u32[]{:S(2)}, u32[]{:S(2)}) collective-permute-start(bf16[200,512]{1,0:T(8,128)(2,1)S(1)} %collective-permute-done.2.refs_2_), channel_id=1, source_target_pairs={{0,8},{2,10},{8,16},{10,18},{16,24},{18,26},{24,28},{26,30},{28,20... | collective-permute-start | bytes 614408 | tf_op jit(solution)/shard_map/ppermute | solution.py:446
  14.1 8.5 %collective-permute-start.5 = (bf16[200,512]{1,0:T(8,128)(2,1)S(1)}, bf16[200,512]{1,0:T(8,128)(2,1)S(1)}, u32[]{:S(2)}, u32[]{:S(2)}) collective-permute-start(bf16[200,512]{1,0:T(8,128)(2,1)S(1)} %collective-permute-done.3.refs_5_), channel_id=1, source_target_pairs={{0,4},{2,6},{8,0},{10,2},{16,8},{18,10},{24,16},{26,18},{28,24},{3... | collective-permute-start | bytes 614408 | tf_op jit(solution)/shard_map/ppermute | solution.py:447
  16.2 8.6 %collective-permute-start.11 = (bf16[192,512]{1,0:T(8,128)(2,1)S(1)}, bf16[192,512]{1,0:T(8,128)(2,1)S(1)}, u32[]{:S(2)}, u32[]{:S(2)}) collective-permute-start(bf16[192,512]{1,0:T(8,128)(2,1)S(1)} %collective-permute-done.7.refs_4_), channel_id=1, source_target_pairs={{0,4},{2,6},{8,0},{10,2},{16,8},{18,10},{24,16},{26,18},{28,24},{3... | collective-permute-start | bytes 589832 | tf_op jit(solution)/shard_map/ppermute | solution.py:447
  18.2 8.9 %collective-permute-start.10 = (bf16[192,512]{1,0:T(8,128)(2,1)S(1)}, bf16[192,512]{1,0:T(8,128)(2,1)S(1)}, u32[]{:S(2)}, u32[]{:S(2)}) collective-permute-start(bf16[192,512]{1,0:T(8,128)(2,1)S(1)} %collective-permute-done.6.refs_3_), channel_id=1, source_target_pairs={{0,8},{2,10},{8,16},{10,18},{16,24},{18,26},{24,28},{26,30},{28,20... | collective-permute-start | bytes 589832 | tf_op jit(solution)/shard_map/ppermute | solution.py:446
  22.6 8.6 %collective-permute-start.8 = (bf16[200,512]{1,0:T(8,128)(2,1)S(1)}, bf16[200,512]{1,0:T(8,128)(2,1)S(1)}, u32[]{:S(2)}, u32[]{:S(2)}) collective-permute-start(bf16[200,512]{1,0:T(8,128)(2,1)S(1)} %collective-permute-done.4.refs_2_), channel_id=1, source_target_pairs={{0,8},{2,10},{8,16},{10,18},{16,24},{18,26},{24,28},{26,30},{28,20... | collective-permute-start | bytes 614408 | tf_op jit(solution)/shard_map/ppermute | solution.py:446
  23.9 7.3 %collective-permute-start.9 = (bf16[200,512]{1,0:T(8,128)(2,1)S(1)}, bf16[200,512]{1,0:T(8,128)(2,1)S(1)}, u32[]{:S(2)}, u32[]{:S(2)}) collective-permute-start(bf16[200,512]{1,0:T(8,128)(2,1)S(1)} %collective-permute-done.5.refs_5_), channel_id=1, source_target_pairs={{0,4},{2,6},{8,0},{10,2},{16,8},{18,10},{24,16},{26,18},{28,24},{3... | collective-permute-start | bytes 614408 | tf_op jit(solution)/shard_map/ppermute | solution.py:447
  24.8 8.9 %collective-permute-start.15 = (bf16[192,512]{1,0:T(8,128)(2,1)S(1)}, bf16[192,512]{1,0:T(8,128)(2,1)S(1)}, u32[]{:S(2)}, u32[]{:S(2)}) collective-permute-start(bf16[192,512]{1,0:T(8,128)(2,1)S(1)} %collective-permute-done.11.refs_4_), channel_id=1, source_target_pairs={{0,4},{2,6},{8,0},{10,2},{16,8},{18,10},{24,16},{26,18},{28,24},{3... | collective-permute-start | bytes 589832 | tf_op jit(solution)/shard_map/ppermute | solution.py:447
  27.1 8.3 %collective-permute-start.14 = (bf16[192,512]{1,0:T(8,128)(2,1)S(1)}, bf16[192,512]{1,0:T(8,128)(2,1)S(1)}, u32[]{:S(2)}, u32[]{:S(2)}) collective-permute-start(bf16[192,512]{1,0:T(8,128)(2,1)S(1)} %collective-permute-done.10.refs_3_), channel_id=1, source_target_pairs={{0,8},{2,10},{8,16},{10,18},{16,24},{18,26},{24,28},{26,30},{28,20... | collective-permute-start | bytes 589832 | tf_op jit(solution)/shard_map/ppermute | solution.py:446
  31.2 7.5 %collective-permute-start.12 = (bf16[200,512]{1,0:T(8,128)(2,1)S(1)}, bf16[200,512]{1,0:T(8,128)(2,1)S(1)}, u32[]{:S(2)}, u32[]{:S(2)}) collective-permute-start(bf16[200,512]{1,0:T(8,128)(2,1)S(1)} %collective-permute-done.8.refs_2_), channel_id=1, source_target_pairs={{0,8},{2,10},{8,16},{10,18},{16,24},{18,26},{24,28},{26,30},{28,20... | collective-permute-start | bytes 614408 | tf_op jit(solution)/shard_map/ppermute | solution.py:446
  32.5 6.2 %collective-permute-start.13 = (bf16[200,512]{1,0:T(8,128)(2,1)S(1)}, bf16[200,512]{1,0:T(8,128)(2,1)S(1)}, u32[]{:S(2)}, u32[]{:S(2)}) collective-permute-start(bf16[200,512]{1,0:T(8,128)(2,1)S(1)} %collective-permute-done.9.refs_5_), channel_id=1, source_target_pairs={{0,4},{2,6},{8,0},{10,2},{16,8},{18,10},{24,16},{26,18},{28,24},{3... | collective-permute-start | bytes 614408 | tf_op jit(solution)/shard_map/ppermute | solution.py:447
  39.7 1.9 %collective-permute-start.16 = (bf16[192,1280]{1,0:T(8,128)(2,1)S(1)}, bf16[192,1280]{1,0:T(8,128)(2,1)S(1)}, u32[]{:S(2)}, u32[]{:S(2)}) collective-permute-start(bf16[192,1280]{1,0:T(8,128)(2,1)S(1)} %attend.11), channel_id=1, source_target_pairs={{0,2},{2,0},{4,6},{6,4},{8,10},{10,8},{12,14},{14,12},{16,18},{18,... | collective-permute-start | bytes 1474568 | tf_op jit(solution)/shard_map/ppermute | solution.py:492
  42.5 21.5 %collective-permute-start.18 = (bf16[96,1280]{1,0:T(8,128)(2,1)S(1)}, bf16[96,1280]{1,0:T(8,128)(2,1)S(1)}, u32[]{:S(2)}, u32[]{:S(2)}) collective-permute-start(bf16[96,1280]{1,0:T(8,128)(2,1)S(1)} %get-tuple-element.75), channel_id=1, source_target_pairs={{0,1},{1,0},{2,3},{3,2},{4,5},{5,4},{6,7},{7,6},{8,9},{9,8},{10,11... | collective-permute-start | bytes 737288 | tf_op jit(solution)/shard_map/ppermute | solution.py:545
  46.9 17.0 %collective-permute-start.19 = (bf16[96,1152]{1,0:T(8,128)(2,1)S(1)}, bf16[96,1152]{1,0:T(8,128)(2,1)S(1)}, u32[]{:S(2)}, u32[]{:S(2)}) collective-permute-start(bf16[96,1152]{1,0:T(8,128)(2,1)S(1)} %get-tuple-element.78), channel_id=1, source_target_pairs={{0,1},{1,0},{2,3},{3,2},{4,5},{5,4},{6,7},{7,6},{8,9},{9,8},{10,11... | collective-permute-start | bytes 663560 | tf_op jit(solution)/shard_map/ppermute | solution.py:545
  50.3 13.7 %collective-permute-start.20 = (bf16[96,1024]{1,0:T(8,128)(2,1)S(1)}, bf16[96,1024]{1,0:T(8,128)(2,1)S(1)}, u32[]{:S(2)}, u32[]{:S(2)}) collective-permute-start(bf16[96,1024]{1,0:T(8,128)(2,1)S(1)} %get-tuple-element.81), channel_id=1, source_target_pairs={{0,1},{1,0},{2,3},{3,2},{4,5},{5,4},{6,7},{7,6},{8,9},{9,8},{10,11... | collective-permute-start | bytes 589832 | tf_op jit(solution)/shard_map/ppermute | solution.py:545
  53.0 10.9 %collective-permute-start.21 = (bf16[96,896]{1,0:T(8,128)(2,1)S(1)}, bf16[96,896]{1,0:T(8,128)(2,1)S(1)}, u32[]{:S(2)}, u32[]{:S(2)}) collective-permute-start(bf16[96,896]{1,0:T(8,128)(2,1)S(1)} %get-tuple-element.84), channel_id=1, source_target_pairs={{0,1},{1,0},{2,3},{3,2},{4,5},{5,4},{6,7},{7,6},{8,9},{9,8},{10,11... | collective-permute-start | bytes 516104 | tf_op jit(solution)/shard_map/ppermute | solution.py:545
  54.6 12.1 %collective-permute-start.17 = (bf16[96,768]{1,0:T(8,128)(2,1)S(1)}, bf16[96,768]{1,0:T(8,128)(2,1)S(1)}, u32[]{:S(2)}, u32[]{:S(2)}) collective-permute-start(bf16[96,768]{1,0:T(8,128)(2,1)S(1)} %get-tuple-element.88), channel_id=1, source_target_pairs={{0,1},{1,0},{2,3},{3,2},{4,5},{5,4},{6,7},{7,6},{8,9},{9,8},{10,11... | collective-permute-start | bytes 442376 | tf_op jit(solution)/shard_map/ppermute | solution.py:545

commit v12 on v11

--- a/solution.py
+++ b/solution.py
@@ -473,21 +473,26 @@
         return attend(plan, turned, [y_first], packets, state, out_weight)
 
     up_first, up_second, down_first, down_second = x_first, y, y_first, x
-    state = call([(x, y_first, 1)], None, own=True)
-    held = []
+    held = {}
+
+    def bring_with(groups, *arguments, **settings):
+        cuts = [fetch[j] for j in groups]
+        results = call(*arguments, fetch=cuts, **settings)
+        held.update(zip(groups, results[2:]))
+        return results[:2]
+
+    state = bring_with((2, 3), [(x, y_first, 1)], None, own=True)
     for r in range(1, half):
         if r > 1:
             up_first, down_first, *state = lax.optimization_barrier((up_first, down_first, *state))
         up_first, up_second = up(up_first), up(up_second)
         down_first, down_second = down(down_first), down(down_second)
         if r > 1:
-            *state, more = call(arrived, state, fetch=fetch[len(held) : len(held) + 1])
-            held.append(more)
+            state = bring_with((r - 2,), arrived, state)
         arrived = [(up_first, up_second, 0), (down_second, down_first, 1)]
     up_first, down_first, *state = lax.optimization_barrier((up_first, down_first, *state))
     far = (up(up_first), down(down_first), 1)
-    *state, more = call(arrived, state, fetch=fetch[len(held) :])
-    held.append(more)
+    state = call(arrived, state)
     (theirs,) = call([far], state, last=True, which=(1,))
     other = lax.ppermute(theirs, "blk", sibling)
     (own,) = call([far], state, last=True, which=(0,))
@@ -533,15 +538,16 @@
     widths = [out_weight.shape[1] * share // sum(shares) for share in shares]
     cuts = [(sum(widths[:j]), columns) for j, columns in enumerate(widths)]
     own, other, held = split_over_cores(
-        count, queries, keys, values, positions, out_weight, cuts[:3]
+        count, queries, keys, values, positions, out_weight, cuts[:4]
     )
-    bring = [cuts[j + 2 : j + 3] if j > 0 else [] for j in range(len(cuts))]
+    bring = [cuts[4:] if j == 2 else [] for j in range(len(cuts))]
     received, kept = [], []
     for j in range(len(cuts)):
         source = own if j == 0 else after(own, sent)
         begun = begin(own, held[0]) if j == 0 else None
         sent, keep, *rest = project(source, other, held[j], out_weight, bring[j], begun)
-        held += rest
+        if rest:
+            held[len(held)] = rest[0]
         received.append(lax.ppermute(sent, "inner", [(0, 1), (1, 0)]))
         kept.append(keep)
     columns = out_weight.shape[1]

time: 67.7 us -> 67.7 us (level)
    ppermute x5, waiting for transfers between devices: 9.42 us -> 10.9 us  [shards(): received.append(lax.ppermute(sent, 'inner', [(0, 1), (1, 0)]))]
    pallas_call x5, Pallas kernels: 8.62 us -> 7.12 us  [project(): pl.pallas_call(functools.partial(project_kernel, bring, begun is not None...]
    pallas_call x6, Pallas kernels: 13.2 us -> 14.7 us  [attend(): pl.pallas_call(functools.partial(attend_kernel, plan), out_shape=out_shap...]
    ppermute x7, waiting for transfers between devices: 2.3 us -> 1.22 us  [split_over_cores(): down = lambda x: lax.ppermute(x, 'blk', counter)]
  transfers between devices with their start and end apart: 22 -> 22, of which waited for: 12 -> 10; matrix products, arithmetic and copies ran while one was open for 0% -> 0% of each run, Pallas kernels for 33% -> 33%
where the time goes in v12:
time: 67.7 us; the launch traced here: 67.6 us
  Pallas kernels  26.2 us (39%)
  starting transfers between devices  21.9 us (32%)
  waiting for transfers between devices  19 us (28%)
    pallas_call x6, Pallas kernels, attend(): pl.pallas_call(functools.partial(attend_kernel, plan), out_shape=out_shap...  14.7 us
    ppermute x7, starting transfers between devices, split_over_cores(): down = lambda x: lax.ppermute(x, 'blk', counter)  11.9 us
    ppermute x5, waiting for transfers between devices, shards(): received.append(lax.ppermute(sent, 'inner', [(0, 1), (1, 0)]))  10.9 us
    pallas_call x5, Pallas kernels, project(): pl.pallas_call(functools.partial(project_kernel, bring, begun is not None...  7.12 us
    ppermute x5, starting transfers between devices, shards(): received.append(lax.ppermute(sent, 'inner', [(0, 1), (1, 0)]))  5.86 us
    ppermute x7, waiting for transfers between devices, split_over_cores(): up = lambda x: lax.ppermute(x, 'blk', clock)  5.83 us
    ppermute x7, starting transfers between devices, split_over_cores(): up = lambda x: lax.ppermute(x, 'blk', clock)  3.48 us
    pallas_call x2, Pallas kernels, finish(): pl.pallas_call(functools.partial(finish_kernel, first, pairs), out_shape=...  1.8 us
  transfers between devices with their start and end apart: 22, of which 10 were waited for; matrix products, arithmetic and copies ran while one was open for 0% of the time, Pallas kernels for 33%

profile of v12, /device:TPU:0, one launch (start us, length us, event | category | flops | bytes accessed | tf_op | source)
XLA Modules:
  0.0 67.6 jit_solution(10684725684258312918)
XLA Ops:
  0.0 1.4 %prepare.1 = (bf16[208,512]{1,0:T(8,128)(2,1)S(1)}, bf16[192,512]{1,0:T(8,128)(2,1)S(1)}, bf16[8,256]{1,0:T(8,128)(2,1)S(1)}, bf16[192,1280]{1,0:T(8,128)(2,1)S(1)}, bf16[192,1280]{1,0:T(8,128)(2,1)S(1)}) custom-call(bf16[192,2560]{1,0:T(8,128)(2,1)} %q_ref.1, bf16[192,512]{1,0:T(8,128)(2,1)} %k_ref.1, bf16[192,512]{1,0:T(8,128)(2,1)} %v_ref.1, s32[192]{0:T(256)} %position_ref.1), custom_call_target="tpu_custom_call" | custom-call | tf_op jit(solution)/shard_map/prepare/pallas_call | solution.py:386
  1.4 0.5 collective-permute-start.1
  2.0 0.1 collective-permute-start
  2.0 1.0 %collective-permute-done.1 = bf16[208,512]{1,0:T(8,128)(2,1)S(1)} collective-permute-done((bf16[208,512]{1,0:T(8,128)(2,1)S(1)}, bf16[208,512]{1,0:T(8,128)(2,1)S(1)}, u32[]{:S(2)}, u32[]{:S(2)}) %collective-permute-start.1) | collective-permute-done | bytes 213024 | tf_op jit(solution)/shard_map/ppermute | solution.py:450
  3.1 2.9 %collective-permute-start.3 = (bf16[200,512]{1,0:T(8,128)(2,1)S(1)}, bf16[200,512]{1,0:T(8,128)(2,1)S(1)}, u32[]{:S(2)}, u32[]{:S(2)}) collective-permute-start(bf16[200,512]{1,0:T(8,128)(2,1)S(1)} %get-tuple-element.94.refs_1_.refs_3_), channel_id=1, source_target_pairs={{0,4},{2,6},{8,0},{10,2},{16,8},{18,10},{24,16},{26,18},{28,24},{3... | collective-permute-start | bytes 614408 | tf_op jit(solution)/shard_map/ppermute | solution.py:447
  6.1 0.1 collective-permute-start.2
  6.2 1.9 %collective-permute-start.7 = (bf16[192,512]{1,0:T(8,128)(2,1)S(1)}, bf16[192,512]{1,0:T(8,128)(2,1)S(1)}, u32[]{:S(2)}, u32[]{:S(2)}) collective-permute-start(bf16[192,512]{1,0:T(8,128)(2,1)S(1)} %get-tuple-element.53.refs_2_), channel_id=1, source_target_pairs={{0,4},{2,6},{8,0},{10,2},{16,8},{18,10},{24,16},{26,18},{28,24},{3... | collective-permute-start | bytes 589832 | tf_op jit(solution)/shard_map/ppermute | solution.py:447
  8.1 0.1 collective-permute-start.6
  8.2 0.3 turn.1.refs_0_
  8.5 3.9 %attend.6 = (f32[8,1,480]{2,1,0:T(1,128)S(1)}, f32[8,144,480]{2,1,0:T(8,128)S(1)}, bf16[2560,1024]{1,0:T(8,128)(2,1)S(1)}, bf16[2560,896]{1,0:T(8,128)(2,1)S(1)}) custom-call(bf16[8,128,480]{2,1,0:T(8,128)(2,1)S(1)} %turn.1.refs_0_, bf16[200,512]{1,0:T(8,128)(2,1)S(1)} %get-tuple-element.94.refs_1_.refs_3_, bf16[192,512]{1,0:T(8,128)(2,1)S(1)} %get-tuple-element.53.refs_2_, ...), custom_call_target="tpu_custom_call" | custom-call | flops 377487360 | bytes 4194304 | tf_op jit(solution)/shard_map/attend/pallas_call | solution.py:233
  12.5 1.5 %collective-permute-done.2.refs_2_ = bf16[200,512]{1,0:T(8,128)(2,1)S(1)} collective-permute-done((bf16[200,512]{1,0:T(8,128)(2,1)S(1)}, bf16[200,512]{1,0:T(8,128)(2,1)S(1)}, u32[]{:S(2)}, u32[]{:S(2)}) %collective-permute-start.2) | collective-permute-done | bytes 204832 | tf_op jit(solution)/shard_map/ppermute | solution.py:446
  14.0 0.5 collective-permute-start.4
  14.5 1.5 %collective-permute-start.5 = (bf16[200,512]{1,0:T(8,128)(2,1)S(1)}, bf16[200,512]{1,0:T(8,128)(2,1)S(1)}, u32[]{:S(2)}, u32[]{:S(2)}) collective-permute-start(bf16[200,512]{1,0:T(8,128)(2,1)S(1)} %collective-permute-done.3.refs_5_), channel_id=1, source_target_pairs={{0,4},{2,6},{8,0},{10,2},{16,8},{18,10},{24,16},{26,18},{28,24},{3... | collective-permute-start | bytes 614408 | tf_op jit(solution)/shard_map/ppermute | solution.py:447
  16.1 2.1 %collective-permute-start.11 = (bf16[192,512]{1,0:T(8,128)(2,1)S(1)}, bf16[192,512]{1,0:T(8,128)(2,1)S(1)}, u32[]{:S(2)}, u32[]{:S(2)}) collective-permute-start(bf16[192,512]{1,0:T(8,128)(2,1)S(1)} %collective-permute-done.7.refs_4_), channel_id=1, source_target_pairs={{0,4},{2,6},{8,0},{10,2},{16,8},{18,10},{24,16},{26,18},{28,24},{3... | collective-permute-start | bytes 589832 | tf_op jit(solution)/shard_map/ppermute | solution.py:447
  18.2 0.0 collective-permute-done.6.refs_3_
  18.2 0.1 collective-permute-start.10
  18.3 3.1 %attend.7 = (f32[8,1,480]{2,1,0:T(1,128)S(1)}, f32[8,144,480]{2,1,0:T(8,128)S(1)}, bf16[2560,1280]{1,0:T(8,128)(2,1)S(1)}) custom-call(bf16[8,128,480]{2,1,0:T(8,128)(2,1)S(1)} %turn.1.refs_0_, bf16[200,512]{1,0:T(8,128)(2,1)S(1)} %get-tuple-element.94.refs_1_.refs_3_, bf16[200,512]{1,0:T(8,128)(2,1)S(1)} %collective-permute-done.2.refs_2_, ...), custom_call_target="tpu_custom_call" | custom-call | flops 754974720 | bytes 4194304 | tf_op jit(solution)/shard_map/attend/pallas_call | solution.py:233
  21.4 1.2 %collective-permute-done.4.refs_2_ = bf16[200,512]{1,0:T(8,128)(2,1)S(1)} collective-permute-done((bf16[200,512]{1,0:T(8,128)(2,1)S(1)}, bf16[200,512]{1,0:T(8,128)(2,1)S(1)}, u32[]{:S(2)}, u32[]{:S(2)}) %collective-permute-start.4) | collective-permute-done | bytes 204832 | tf_op jit(solution)/shard_map/ppermute | solution.py:446
  22.6 1.3 %collective-permute-start.8 = (bf16[200,512]{1,0:T(8,128)(2,1)S(1)}, bf16[200,512]{1,0:T(8,128)(2,1)S(1)}, u32[]{:S(2)}, u32[]{:S(2)}) collective-permute-start(bf16[200,512]{1,0:T(8,128)(2,1)S(1)} %collective-permute-done.4.refs_2_), channel_id=1, source_target_pairs={{0,8},{2,10},{8,16},{10,18},{16,24},{18,26},{24,28},{26,30},{28,20... | collective-permute-start | bytes 614408 | tf_op jit(solution)/shard_map/ppermute | solution.py:446
  23.9 0.7 %collective-permute-start.9 = (bf16[200,512]{1,0:T(8,128)(2,1)S(1)}, bf16[200,512]{1,0:T(8,128)(2,1)S(1)}, u32[]{:S(2)}, u32[]{:S(2)}) collective-permute-start(bf16[200,512]{1,0:T(8,128)(2,1)S(1)} %collective-permute-done.5.refs_5_), channel_id=1, source_target_pairs={{0,4},{2,6},{8,0},{10,2},{16,8},{18,10},{24,16},{26,18},{28,24},{3... | collective-permute-start | bytes 614408 | tf_op jit(solution)/shard_map/ppermute | solution.py:447
  24.7 0.4 collective-permute-done.11.refs_4_
  25.1 2.0 %collective-permute-start.15 = (bf16[192,512]{1,0:T(8,128)(2,1)S(1)}, bf16[192,512]{1,0:T(8,128)(2,1)S(1)}, u32[]{:S(2)}, u32[]{:S(2)}) collective-permute-start(bf16[192,512]{1,0:T(8,128)(2,1)S(1)} %collective-permute-done.11.refs_4_), channel_id=1, source_target_pairs={{0,4},{2,6},{8,0},{10,2},{16,8},{18,10},{24,16},{26,18},{28,24},{3... | collective-permute-start | bytes 589832 | tf_op jit(solution)/shard_map/ppermute | solution.py:447
  27.1 3.1 %attend.8 = (f32[8,1,480]{2,1,0:T(1,128)S(1)}, f32[8,144,480]{2,1,0:T(8,128)S(1)}, bf16[2560,1152]{1,0:T(8,128)(2,1)S(1)}) custom-call(bf16[8,128,480]{2,1,0:T(8,128)(2,1)S(1)} %turn.1.refs_0_, bf16[200,512]{1,0:T(8,128)(2,1)S(1)} %get-tuple-element.94.refs_1_.refs_3_, bf16[200,512]{1,0:T(8,128)(2,1)S(1)} %collective-permute-done.4.refs_2_, ...), custom_call_target="tpu_custom_call" | custom-call | flops 754974720 | bytes 4194304 | tf_op jit(solution)/shard_map/attend/pallas_call | solution.py:233
  30.3 1.0 %collective-permute-done.8.refs_2_ = bf16[200,512]{1,0:T(8,128)(2,1)S(1)} collective-permute-done((bf16[200,512]{1,0:T(8,128)(2,1)S(1)}, bf16[200,512]{1,0:T(8,128)(2,1)S(1)}, u32[]{:S(2)}, u32[]{:S(2)}) %collective-permute-start.8) | collective-permute-done | bytes 204832 | tf_op jit(solution)/shard_map/ppermute | solution.py:446
  31.2 1.3 %collective-permute-start.12 = (bf16[200,512]{1,0:T(8,128)(2,1)S(1)}, bf16[200,512]{1,0:T(8,128)(2,1)S(1)}, u32[]{:S(2)}, u32[]{:S(2)}) collective-permute-start(bf16[200,512]{1,0:T(8,128)(2,1)S(1)} %collective-permute-done.8.refs_2_), channel_id=1, source_target_pairs={{0,8},{2,10},{8,16},{10,18},{16,24},{18,26},{24,28},{26,30},{28,20... | collective-permute-start | bytes 614408 | tf_op jit(solution)/shard_map/ppermute | solution.py:446
  32.5 0.7 %collective-permute-start.13 = (bf16[200,512]{1,0:T(8,128)(2,1)S(1)}, bf16[200,512]{1,0:T(8,128)(2,1)S(1)}, u32[]{:S(2)}, u32[]{:S(2)}) collective-permute-start(bf16[200,512]{1,0:T(8,128)(2,1)S(1)} %collective-permute-done.9.refs_5_), channel_id=1, source_target_pairs={{0,4},{2,6},{8,0},{10,2},{16,8},{18,10},{24,16},{26,18},{28,24},{3... | collective-permute-start | bytes 614408 | tf_op jit(solution)/shard_map/ppermute | solution.py:447
  33.3 0.8 %collective-permute-done.15.refs_4_ = bf16[192,512]{1,0:T(8,128)(2,1)S(1)} collective-permute-done((bf16[192,512]{1,0:T(8,128)(2,1)S(1)}, bf16[192,512]{1,0:T(8,128)(2,1)S(1)}, u32[]{:S(2)}, u32[]{:S(2)}) %collective-permute-start.15) | collective-permute-done | bytes 196640 | tf_op jit(solution)/shard_map/ppermute | solution.py:447
  34.0 1.4 %collective-permute-done.14.refs_3_ = bf16[192,512]{1,0:T(8,128)(2,1)S(1)} collective-permute-done((bf16[192,512]{1,0:T(8,128)(2,1)S(1)}, bf16[192,512]{1,0:T(8,128)(2,1)S(1)}, u32[]{:S(2)}, u32[]{:S(2)}) %collective-permute-start.14) | collective-permute-done | bytes 196640 | tf_op jit(solution)/shard_map/ppermute | solution.py:446
  35.4 2.5 %attend.9 = (f32[8,1,480]{2,1,0:T(1,128)S(1)}, f32[8,144,480]{2,1,0:T(8,128)S(1)}) custom-call(bf16[8,128,480]{2,1,0:T(8,128)(2,1)S(1)} %turn.1.refs_0_, bf16[200,512]{1,0:T(8,128)(2,1)S(1)} %get-tuple-element.94.refs_1_.refs_3_, bf16[200,512]{1,0:T(8,128)(2,1)S(1)} %collective-permute-done.8.refs_2_, bf16[192,512]{1,0:T(8,128)(2,1)S(1)} %collective-permute-done.14.refs_3_, ...), custom_call_target="tpu_custom_call" | custom-call | flops 754974720 | bytes 4194304 | tf_op jit(solution)/shard_map/attend/pallas_call | solution.py:233
  38.0 0.7 %collective-permute-done.12.refs_2_ = bf16[200,512]{1,0:T(8,128)(2,1)S(1)} collective-permute-done((bf16[200,512]{1,0:T(8,128)(2,1)S(1)}, bf16[200,512]{1,0:T(8,128)(2,1)S(1)}, u32[]{:S(2)}, u32[]{:S(2)}) %collective-permute-start.12) | collective-permute-done | bytes 204832 | tf_op jit(solution)/shard_map/ppermute | solution.py:446
  38.7 1.0 %attend.11 = bf16[192,1280]{1,0:T(8,128)(2,1)S(1)} custom-call(bf16[8,128,480]{2,1,0:T(8,128)(2,1)S(1)} %turn.1.refs_0_, bf16[200,512]{1,0:T(8,128)(2,1)S(1)} %get-tuple-element.94.refs_1_.refs_3_, bf16[200,512]{1,0:T(8,128)(2,1)S(1)} %collective-permute-done.12.refs_2_, bf16[200,512]{1,0:T(8,128)(2,1)S(1)} %collective-permute-done.13.refs_3_, ...), custom_call_target="tpu_custom_call" | custom-call | flops 377487360 | bytes 4194304 | tf_op jit(solution)/shard_map/attend/pallas_call | solution.py:233
  39.7 0.1 collective-permute-start.16
  39.8 1.0 %attend.10.own_ref = bf16[192,1280]{1,0:T(8,128)(2,1)S(1)} custom-call(bf16[8,128,480]{2,1,0:T(8,128)(2,1)S(1)} %turn.1.refs_0_, bf16[200,512]{1,0:T(8,128)(2,1)S(1)} %get-tuple-element.94.refs_1_.refs_3_, bf16[200,512]{1,0:T(8,128)(2,1)S(1)} %collective-permute-done.12.refs_2_, bf16[200,512]{1,0:T(8,128)(2,1)S(1)} %collective-permute-done.13.refs_3_, ...), custom_call_target="tpu_custom_call" | custom-call | flops 377487360 | bytes 4194304 | tf_op jit(solution)/shard_map/attend/pallas_call | solution.py:233
  40.8 0.8 %begin.1.refs_0_ = f32[192,1280]{1,0:T(8,128)S(1)} custom-call(bf16[192,1280]{1,0:T(8,128)(2,1)S(1)} %attend.10.own_ref, bf16[2560,1280]{1,0:T(8,128)(2,1)S(1)} %get-tuple-element.74.held_ref), custom_call_target="tpu_custom_call" | custom-call | flops 1024 | bytes 1024 | tf_op jit(solution)/shard_map/begin/pallas_call | solution.py:292
  41.6 0.9 %project.5 = (bf16[96,1280]{1,0:T(8,128)(2,1)S(1)}, bf16[96,1280]{1,0:T(8,128)(2,1)S(1)}) custom-call(bf16[192,1280]{1,0:T(8,128)(2,1)S(1)} %attend.10.own_ref, bf16[192,1280]{1,0:T(8,128)(2,1)S(1)} %collective-permute-done.16.other_ref, bf16[2560,1280]{1,0:T(8,128)(2,1)S(1)} %get-tuple-element.74.held_ref, f32[192,1280]{1,0:T(8,128)S(1)} %begin.1.refs_0_), custom_call_target="tpu_custom_call" | custom-call | flops 1024 | bytes 1024 | tf_op jit(solution)/shard_map/project/pallas_call | solution.py:344
  42.5 1.5 %collective-permute-start.18 = (bf16[96,1280]{1,0:T(8,128)(2,1)S(1)}, bf16[96,1280]{1,0:T(8,128)(2,1)S(1)}, u32[]{:S(2)}, u32[]{:S(2)}) collective-permute-start(bf16[96,1280]{1,0:T(8,128)(2,1)S(1)} %get-tuple-element.75), channel_id=1, source_target_pairs={{0,1},{1,0},{2,3},{3,2},{4,5},{5,4},{6,7},{7,6},{8,9},{9,8},{10,11... | collective-permute-start | bytes 737288 | tf_op jit(solution)/shard_map/ppermute | solution.py:551
  44.0 1.4 %project.6 = (bf16[96,1152]{1,0:T(8,128)(2,1)S(1)}, bf16[96,1152]{1,0:T(8,128)(2,1)S(1)}) custom-call(bf16[192,1280]{1,0:T(8,128)(2,1)S(1)} %attend.10.own_ref, bf16[192,1280]{1,0:T(8,128)(2,1)S(1)} %collective-permute-done.16.other_ref, bf16[2560,1152]{1,0:T(8,128)(2,1)S(1)} %get-tuple-element.77.held_ref), custom_call_target="tpu_custom_call" | custom-call | flops 1024 | bytes 1024 | tf_op jit(solution)/shard_map/project/pallas_call | solution.py:344
  45.5 0.6 collective-permute-start.19
  46.1 2.7 %project.7 = (bf16[96,1024]{1,0:T(8,128)(2,1)S(1)}, bf16[96,1024]{1,0:T(8,128)(2,1)S(1)}, bf16[2560,768]{1,0:T(8,128)(2,1)S(1)}) custom-call(bf16[192,1280]{1,0:T(8,128)(2,1)S(1)} %attend.10.own_ref, bf16[192,1280]{1,0:T(8,128)(2,1)S(1)} %collective-permute-done.16.other_ref, bf16[2560,1024]{1,0:T(8,128)(2,1)S(1)} %get-tuple-element.80.held_ref, ...), custom_call_target="tpu_custom_call" | custom-call | flops 1024 | bytes 1024 | tf_op jit(solution)/shard_map/project/pallas_call | solution.py:344
  48.8 1.5 %collective-permute-start.20 = (bf16[96,1024]{1,0:T(8,128)(2,1)S(1)}, bf16[96,1024]{1,0:T(8,128)(2,1)S(1)}, u32[]{:S(2)}, u32[]{:S(2)}) collective-permute-start(bf16[96,1024]{1,0:T(8,128)(2,1)S(1)} %get-tuple-element.81), channel_id=1, source_target_pairs={{0,1},{1,0},{2,3},{3,2},{4,5},{5,4},{6,7},{7,6},{8,9},{9,8},{10,11... | collective-permute-start | bytes 589832 | tf_op jit(solution)/shard_map/ppermute | solution.py:551
  50.3 1.2 %project.8 = (bf16[96,896]{1,0:T(8,128)(2,1)S(1)}, bf16[96,896]{1,0:T(8,128)(2,1)S(1)}) custom-call(bf16[192,1280]{1,0:T(8,128)(2,1)S(1)} %attend.10.own_ref, bf16[192,1280]{1,0:T(8,128)(2,1)S(1)} %collective-permute-done.16.other_ref, bf16[2560,896]{1,0:T(8,128)(2,1)S(1)} %get-tuple-element.83.held_ref), custom_call_target="tpu_custom_call" | custom-call | flops 1024 | bytes 1024 | tf_op jit(solution)/shard_map/project/pallas_call | solution.py:344
  51.5 0.6 collective-permute-start.21
  52.2 0.9 %project.9 = (bf16[96,768]{1,0:T(8,128)(2,1)S(1)}, bf16[96,768]{1,0:T(8,128)(2,1)S(1)}) custom-call(bf16[192,1280]{1,0:T(8,128)(2,1)S(1)} %attend.10.own_ref, bf16[192,1280]{1,0:T(8,128)(2,1)S(1)} %collective-permute-done.16.other_ref, bf16[2560,768]{1,0:T(8,128)(2,1)S(1)} %get-tuple-element.86.held_ref), custom_call_target="tpu_custom_call" | custom-call | flops 1024 | bytes 1024 | tf_op jit(solution)/shard_map/project/pallas_call | solution.py:344
  53.1 1.5 %collective-permute-start.17 = (bf16[96,768]{1,0:T(8,128)(2,1)S(1)}, bf16[96,768]{1,0:T(8,128)(2,1)S(1)}, u32[]{:S(2)}, u32[]{:S(2)}) collective-permute-start(bf16[96,768]{1,0:T(8,128)(2,1)S(1)} %get-tuple-element.88), channel_id=1, source_target_pairs={{0,1},{1,0},{2,3},{3,2},{4,5},{5,4},{6,7},{7,6},{8,9},{9,8},{10,11... | collective-permute-start | bytes 442376 | tf_op jit(solution)/shard_map/ppermute | solution.py:551
  54.6 9.3 %collective-permute-done.21.refs_7_ = bf16[96,896]{1,0:T(8,128)(2,1)S(1)} collective-permute-done((bf16[96,896]{1,0:T(8,128)(2,1)S(1)}, bf16[96,896]{1,0:T(8,128)(2,1)S(1)}, u32[]{:S(2)}, u32[]{:S(2)}) %collective-permute-start.21) | collective-permute-done | bytes 172064 | tf_op jit(solution)/shard_map/ppermute | solution.py:551
  63.9 1.1 %finish.2.refs_2_ = bf16[96,5120]{1,0:T(8,128)(2,1)} custom-call(bf16[96,1280]{1,0:T(8,128)(2,1)S(1)} %get-tuple-element.89.refs_0_, bf16[96,1152]{1,0:T(8,128)(2,1)S(1)} %get-tuple-element.90.refs_1_, bf16[96,1024]{1,0:T(8,128)(2,1)S(1)} %get-tuple-element.91.refs_2_, bf16[96,896]{1,0:T(8,128)(2,1)S(1)} %get-tuple-element.92.refs_3_, ...), custom_call_target="tpu_custom_call" | custom-call | flops 1024 | bytes 1024 | tf_op jit(solution)/shard_map/finish/pallas_call | solution.py:422
  65.1 1.6 %collective-permute-done.17.refs_1_ = bf16[96,768]{1,0:T(8,128)(2,1)S(1)} collective-permute-done((bf16[96,768]{1,0:T(8,128)(2,1)S(1)}, bf16[96,768]{1,0:T(8,128)(2,1)S(1)}, u32[]{:S(2)}, u32[]{:S(2)}) %collective-permute-start.17) | collective-permute-done | bytes 147488 | tf_op jit(solution)/shard_map/ppermute | solution.py:551
  66.7 0.7 %finish.3 = bf16[96,5120]{1,0:T(8,128)(2,1)} custom-call(bf16[96,768]{1,0:T(8,128)(2,1)S(1)} %get-tuple-element.87.refs_0_, bf16[96,768]{1,0:T(8,128)(2,1)S(1)} %collective-permute-done.17.refs_1_, bf16[96,5120]{1,0:T(8,128)(2,1)} %finish.2.refs_2_), custom_call_target="tpu_custom_call", output_to_operand_aliasing={{}: (2, {})} | custom-call | flops 1024 | bytes 1024 | tf_op jit(solution)/shard_map/finish/pallas_call | solution.py:422
  (15 shorter events, 0.1 us)
Async XLA Ops:
  1.4 1.6 %collective-permute-start.1 = (bf16[208,512]{1,0:T(8,128)(2,1)S(1)}, bf16[208,512]{1,0:T(8,128)(2,1)S(1)}, u32[]{:S(2)}, u32[]{:S(2)}) collective-permute-start(bf16[208,512]{1,0:T(8,128)(2,1)S(1)} %get-tuple-element.51), channel_id=1, source_target_pairs={{0,2},{2,0},{4,6},{6,4},{8,10},{10,8},{12,14},{14,12},{16,18},{18,... | collective-permute-start | bytes 638984 | tf_op jit(solution)/shard_map/ppermute | solution.py:450
  2.0 6.2 %collective-permute-start = (bf16[192,1280]{1,0:T(8,128)(2,1)S(1)}, bf16[192,1280]{1,0:T(8,128)(2,1)S(1)}, u32[]{:S(2)}, u32[]{:S(2)}) collective-permute-start(bf16[192,1280]{1,0:T(8,128)(2,1)S(1)} %get-tuple-element.50), channel_id=1, source_target_pairs={{0,2},{2,0},{4,6},{6,4},{8,10},{10,8},{12,14},{14,12},{16,18},{18,... | collective-permute-start | bytes 1474568 | tf_op jit(solution)/shard_map/ppermute | solution.py:454
  3.1 9.4 %collective-permute-start.3 = (bf16[200,512]{1,0:T(8,128)(2,1)S(1)}, bf16[200,512]{1,0:T(8,128)(2,1)S(1)}, u32[]{:S(2)}, u32[]{:S(2)}) collective-permute-start(bf16[200,512]{1,0:T(8,128)(2,1)S(1)} %get-tuple-element.94.refs_1_.refs_3_), channel_id=1, source_target_pairs={{0,4},{2,6},{8,0},{10,2},{16,8},{18,10},{24,16},{26,18},{28,24},{3... | collective-permute-start | bytes 614408 | tf_op jit(solution)/shard_map/ppermute | solution.py:447
  6.1 8.0 %collective-permute-start.2 = (bf16[200,512]{1,0:T(8,128)(2,1)S(1)}, bf16[200,512]{1,0:T(8,128)(2,1)S(1)}, u32[]{:S(2)}, u32[]{:S(2)}) collective-permute-start(bf16[200,512]{1,0:T(8,128)(2,1)S(1)} %get-tuple-element.93), channel_id=1, source_target_pairs={{0,8},{2,10},{8,16},{10,18},{16,24},{18,26},{24,28},{26,30},{28,20... | collective-permute-start | bytes 614408 | tf_op jit(solution)/shard_map/ppermute | solution.py:446
  6.2 9.9 %collective-permute-start.7 = (bf16[192,512]{1,0:T(8,128)(2,1)S(1)}, bf16[192,512]{1,0:T(8,128)(2,1)S(1)}, u32[]{:S(2)}, u32[]{:S(2)}) collective-permute-start(bf16[192,512]{1,0:T(8,128)(2,1)S(1)} %get-tuple-element.53.refs_2_), channel_id=1, source_target_pairs={{0,4},{2,6},{8,0},{10,2},{16,8},{18,10},{24,16},{26,18},{28,24},{3... | collective-permute-start | bytes 589832 | tf_op jit(solution)/shard_map/ppermute | solution.py:447
  8.1 10.1 %collective-permute-start.6 = (bf16[192,512]{1,0:T(8,128)(2,1)S(1)}, bf16[192,512]{1,0:T(8,128)(2,1)S(1)}, u32[]{:S(2)}, u32[]{:S(2)}) collective-permute-start(bf16[192,512]{1,0:T(8,128)(2,1)S(1)} %slice.8), channel_id=1, source_target_pairs={{0,8},{2,10},{8,16},{10,18},{16,24},{18,26},{24,28},{26,30},{28,20... | collective-permute-start | bytes 589832 | tf_op jit(solution)/shard_map/ppermute | solution.py:446
  14.0 8.6 %collective-permute-start.4 = (bf16[200,512]{1,0:T(8,128)(2,1)S(1)}, bf16[200,512]{1,0:T(8,128)(2,1)S(1)}, u32[]{:S(2)}, u32[]{:S(2)}) collective-permute-start(bf16[200,512]{1,0:T(8,128)(2,1)S(1)} %collective-permute-done.2.refs_2_), channel_id=1, source_target_pairs={{0,8},{2,10},{8,16},{10,18},{16,24},{18,26},{24,28},{26,30},{28,20... | collective-permute-start | bytes 614408 | tf_op jit(solution)/shard_map/ppermute | solution.py:446
  14.5 8.1 %collective-permute-start.5 = (bf16[200,512]{1,0:T(8,128)(2,1)S(1)}, bf16[200,512]{1,0:T(8,128)(2,1)S(1)}, u32[]{:S(2)}, u32[]{:S(2)}) collective-permute-start(bf16[200,512]{1,0:T(8,128)(2,1)S(1)} %collective-permute-done.3.refs_5_), channel_id=1, source_target_pairs={{0,4},{2,6},{8,0},{10,2},{16,8},{18,10},{24,16},{26,18},{28,24},{3... | collective-permute-start | bytes 614408 | tf_op jit(solution)/shard_map/ppermute | solution.py:447
  16.1 9.0 %collective-permute-start.11 = (bf16[192,512]{1,0:T(8,128)(2,1)S(1)}, bf16[192,512]{1,0:T(8,128)(2,1)S(1)}, u32[]{:S(2)}, u32[]{:S(2)}) collective-permute-start(bf16[192,512]{1,0:T(8,128)(2,1)S(1)} %collective-permute-done.7.refs_4_), channel_id=1, source_target_pairs={{0,4},{2,6},{8,0},{10,2},{16,8},{18,10},{24,16},{26,18},{28,24},{3... | collective-permute-start | bytes 589832 | tf_op jit(solution)/shard_map/ppermute | solution.py:447
  18.2 8.9 %collective-permute-start.10 = (bf16[192,512]{1,0:T(8,128)(2,1)S(1)}, bf16[192,512]{1,0:T(8,128)(2,1)S(1)}, u32[]{:S(2)}, u32[]{:S(2)}) collective-permute-start(bf16[192,512]{1,0:T(8,128)(2,1)S(1)} %collective-permute-done.6.refs_3_), channel_id=1, source_target_pairs={{0,8},{2,10},{8,16},{10,18},{16,24},{18,26},{24,28},{26,30},{28,20... | collective-permute-start | bytes 589832 | tf_op jit(solution)/shard_map/ppermute | solution.py:446
  22.6 8.6 %collective-permute-start.8 = (bf16[200,512]{1,0:T(8,128)(2,1)S(1)}, bf16[200,512]{1,0:T(8,128)(2,1)S(1)}, u32[]{:S(2)}, u32[]{:S(2)}) collective-permute-start(bf16[200,512]{1,0:T(8,128)(2,1)S(1)} %collective-permute-done.4.refs_2_), channel_id=1, source_target_pairs={{0,8},{2,10},{8,16},{10,18},{16,24},{18,26},{24,28},{26,30},{28,20... | collective-permute-start | bytes 614408 | tf_op jit(solution)/shard_map/ppermute | solution.py:446
  23.9 7.3 %collective-permute-start.9 = (bf16[200,512]{1,0:T(8,128)(2,1)S(1)}, bf16[200,512]{1,0:T(8,128)(2,1)S(1)}, u32[]{:S(2)}, u32[]{:S(2)}) collective-permute-start(bf16[200,512]{1,0:T(8,128)(2,1)S(1)} %collective-permute-done.5.refs_5_), channel_id=1, source_target_pairs={{0,4},{2,6},{8,0},{10,2},{16,8},{18,10},{24,16},{26,18},{28,24},{3... | collective-permute-start | bytes 614408 | tf_op jit(solution)/shard_map/ppermute | solution.py:447
  25.1 8.9 %collective-permute-start.15 = (bf16[192,512]{1,0:T(8,128)(2,1)S(1)}, bf16[192,512]{1,0:T(8,128)(2,1)S(1)}, u32[]{:S(2)}, u32[]{:S(2)}) collective-permute-start(bf16[192,512]{1,0:T(8,128)(2,1)S(1)} %collective-permute-done.11.refs_4_), channel_id=1, source_target_pairs={{0,4},{2,6},{8,0},{10,2},{16,8},{18,10},{24,16},{26,18},{28,24},{3... | collective-permute-start | bytes 589832 | tf_op jit(solution)/shard_map/ppermute | solution.py:447
  27.1 8.3 %collective-permute-start.14 = (bf16[192,512]{1,0:T(8,128)(2,1)S(1)}, bf16[192,512]{1,0:T(8,128)(2,1)S(1)}, u32[]{:S(2)}, u32[]{:S(2)}) collective-permute-start(bf16[192,512]{1,0:T(8,128)(2,1)S(1)} %collective-permute-done.10.refs_3_), channel_id=1, source_target_pairs={{0,8},{2,10},{8,16},{10,18},{16,24},{18,26},{24,28},{26,30},{28,20... | collective-permute-start | bytes 589832 | tf_op jit(solution)/shard_map/ppermute | solution.py:446
  31.2 7.5 %collective-permute-start.12 = (bf16[200,512]{1,0:T(8,128)(2,1)S(1)}, bf16[200,512]{1,0:T(8,128)(2,1)S(1)}, u32[]{:S(2)}, u32[]{:S(2)}) collective-permute-start(bf16[200,512]{1,0:T(8,128)(2,1)S(1)} %collective-permute-done.8.refs_2_), channel_id=1, source_target_pairs={{0,8},{2,10},{8,16},{10,18},{16,24},{18,26},{24,28},{26,30},{28,20... | collective-permute-start | bytes 614408 | tf_op jit(solution)/shard_map/ppermute | solution.py:446
  32.5 6.2 %collective-permute-start.13 = (bf16[200,512]{1,0:T(8,128)(2,1)S(1)}, bf16[200,512]{1,0:T(8,128)(2,1)S(1)}, u32[]{:S(2)}, u32[]{:S(2)}) collective-permute-start(bf16[200,512]{1,0:T(8,128)(2,1)S(1)} %collective-permute-done.9.refs_5_), channel_id=1, source_target_pairs={{0,4},{2,6},{8,0},{10,2},{16,8},{18,10},{24,16},{26,18},{28,24},{3... | collective-permute-start | bytes 614408 | tf_op jit(solution)/shard_map/ppermute | solution.py:447
  39.7 1.9 %collective-permute-start.16 = (bf16[192,1280]{1,0:T(8,128)(2,1)S(1)}, bf16[192,1280]{1,0:T(8,128)(2,1)S(1)}, u32[]{:S(2)}, u32[]{:S(2)}) collective-permute-start(bf16[192,1280]{1,0:T(8,128)(2,1)S(1)} %attend.11), channel_id=1, source_target_pairs={{0,2},{2,0},{4,6},{6,4},{8,10},{10,8},{12,14},{14,12},{16,18},{18,... | collective-permute-start | bytes 1474568 | tf_op jit(solution)/shard_map/ppermute | solution.py:497
  42.5 21.5 %collective-permute-start.18 = (bf16[96,1280]{1,0:T(8,128)(2,1)S(1)}, bf16[96,1280]{1,0:T(8,128)(2,1)S(1)}, u32[]{:S(2)}, u32[]{:S(2)}) collective-permute-start(bf16[96,1280]{1,0:T(8,128)(2,1)S(1)} %get-tuple-element.75), channel_id=1, source_target_pairs={{0,1},{1,0},{2,3},{3,2},{4,5},{5,4},{6,7},{7,6},{8,9},{9,8},{10,11... | collective-permute-start | bytes 737288 | tf_op jit(solution)/shard_map/ppermute | solution.py:551
  45.5 18.5 %collective-permute-start.19 = (bf16[96,1152]{1,0:T(8,128)(2,1)S(1)}, bf16[96,1152]{1,0:T(8,128)(2,1)S(1)}, u32[]{:S(2)}, u32[]{:S(2)}) collective-permute-start(bf16[96,1152]{1,0:T(8,128)(2,1)S(1)} %get-tuple-element.78), channel_id=1, source_target_pairs={{0,1},{1,0},{2,3},{3,2},{4,5},{5,4},{6,7},{7,6},{8,9},{9,8},{10,11... | collective-permute-start | bytes 663560 | tf_op jit(solution)/shard_map/ppermute | solution.py:551
  48.8 15.1 %collective-permute-start.20 = (bf16[96,1024]{1,0:T(8,128)(2,1)S(1)}, bf16[96,1024]{1,0:T(8,128)(2,1)S(1)}, u32[]{:S(2)}, u32[]{:S(2)}) collective-permute-start(bf16[96,1024]{1,0:T(8,128)(2,1)S(1)} %get-tuple-element.81), channel_id=1, source_target_pairs={{0,1},{1,0},{2,3},{3,2},{4,5},{5,4},{6,7},{7,6},{8,9},{9,8},{10,11... | collective-permute-start | bytes 589832 | tf_op jit(solution)/shard_map/ppermute | solution.py:551
  51.5 12.4 %collective-permute-start.21 = (bf16[96,896]{1,0:T(8,128)(2,1)S(1)}, bf16[96,896]{1,0:T(8,128)(2,1)S(1)}, u32[]{:S(2)}, u32[]{:S(2)}) collective-permute-start(bf16[96,896]{1,0:T(8,128)(2,1)S(1)} %get-tuple-element.84), channel_id=1, source_target_pairs={{0,1},{1,0},{2,3},{3,2},{4,5},{5,4},{6,7},{7,6},{8,9},{9,8},{10,11... | collective-permute-start | bytes 516104 | tf_op jit(solution)/shard_map/ppermute | solution.py:551
  53.1 13.6 %collective-permute-start.17 = (bf16[96,768]{1,0:T(8,128)(2,1)S(1)}, bf16[96,768]{1,0:T(8,128)(2,1)S(1)}, u32[]{:S(2)}, u32[]{:S(2)}) collective-permute-start(bf16[96,768]{1,0:T(8,128)(2,1)S(1)} %get-tuple-element.88), channel_id=1, source_target_pairs={{0,1},{1,0},{2,3},{3,2},{4,5},{5,4},{6,7},{7,6},{8,9},{9,8},{10,11... | collective-permute-start | bytes 442376 | tf_op jit(solution)/shard_map/ppermute | solution.py:551

commit v13 on v12

--- a/solution.py
+++ b/solution.py
@@ -26,10 +26,10 @@
     return list(range(half)) + list(reversed(range(half, chips)))
 
 
-def ring_pairs(chips, step):
+def ring_pairs(chips, step, cross=False):
     ring = ring_of_chips(chips)
     return [
-        (2 * ring[i] + core, 2 * ring[(i + step) % chips] + core)
+        (2 * ring[i] + core, 2 * ring[(i + step) % chips] + (1 - core if cross else core))
         for i in range(chips)
         for core in range(2)
     ]
@@ -354,7 +354,7 @@
 
 
 def prepare_kernel(
-    chunk, q_ref, k_ref, v_ref, position_ref, sent_ref, kept_ref, mark_ref, *query_refs_and_scratch
+    chunk, q_ref, k_ref, v_ref, position_ref, sent_ref, kept_ref, *query_refs_and_scratch
 ):
     *query_refs, first_ref, sems = query_refs_and_scratch
     rows, width = k_ref.shape[0], k_ref.shape[1] // 2
@@ -372,8 +372,9 @@
         copy.start()
     copies[0].wait()
     c = lax.div(first_ref[0], jnp.int32(chunk)).astype(jnp.float32)
-    mark_ref[...] = jnp.full(mark_ref.shape, c, jnp.float32).astype(jnp.bfloat16)
-    sent_ref[rows:] = jnp.full((TILE, 2 * width), c, jnp.float32).astype(jnp.bfloat16)
+    header = jnp.full((HEADER, 2 * width), c, jnp.float32).astype(jnp.bfloat16)
+    sent_ref[rows:] = header
+    kept_ref[rows:] = header
     for copy in copies[1:]:
         copy.wait()
 
@@ -385,14 +386,10 @@
     operands = [pltpu.with_memory_space_constraint(x, pltpu.HBM) for x in (queries, keys, values, positions)]
     return pl.pallas_call(
         functools.partial(prepare_kernel, rows // 2),
-        out_shape=[
-            jax.ShapeDtypeStruct((rows + TILE, width), jnp.bfloat16),
-            jax.ShapeDtypeStruct((rows, width), jnp.bfloat16),
-            jax.ShapeDtypeStruct((HEADER, width // 2), jnp.bfloat16),
-        ]
+        out_shape=[jax.ShapeDtypeStruct((rows + HEADER, width), jnp.bfloat16)] * 2
         + [jax.ShapeDtypeStruct((rows, queries.shape[1] // 2), jnp.bfloat16)] * 2,
         in_specs=[hbm] * 4,
-        out_specs=[vmem] * 5,
+        out_specs=[vmem] * 4,
         scratch_shapes=[
             pltpu.SMEM(positions.shape, jnp.int32),
             pltpu.SemaphoreType.DMA((7,)),
@@ -442,15 +439,12 @@
     heads = keys.shape[1] // HEAD_WIDTH // 2
     sibling = [(b, b ^ 1) for b in range(count)]
     clock, counter = ring_pairs(chips, 1), ring_pairs(chips, -1)
-    width = heads * HEAD_WIDTH
     up = lambda x: lax.ppermute(x, "blk", clock)
     down = lambda x: lax.ppermute(x, "blk", counter)
-
-    sent, x, mark, q_sent, q_own = prepare(queries, keys, values, positions)
-    got = lax.ppermute(sent, "blk", sibling)
-    header = jnp.concatenate([mark, got[rows : rows + HEADER, :width]], axis=1)
-    y = got[:rows]
-    x_first, y_first = (jnp.concatenate([part, header], axis=0) for part in (x, y))
+    cross_up, cross_down = ring_pairs(chips, 1, True), ring_pairs(chips, -1, True)
+
+    sent, x, q_sent, q_own = prepare(queries, keys, values, positions)
+    y = lax.ppermute(sent, "blk", sibling)
     q_got = lax.ppermute(q_sent, "blk", sibling)
     turned = turn(heads, chunk, [q_own, q_got])
 
@@ -464,15 +458,14 @@
             own_at=lambda i: i,
             last=last,
             members=[(2 * j + i, 0) for j in each for i in range(2)],
-            headers=[(1 + 2 * j + pairs[j][2], rows, i * width) for j in each for i in range(2)],
-            owner_headers=[(0, rows, 0), (0, rows, width)],
+            headers=[(2 + 2 * j + i, rows, 0) for j in each for i in range(2)],
+            owner_headers=[(0, rows, 0), (1, rows, 0)],
             fetch=fetch,
             which=which,
         )
-        packets = [packet for pair in pairs for packet in pair[:2]]
-        return attend(plan, turned, [y_first], packets, state, out_weight)
-
-    up_first, up_second, down_first, down_second = x_first, y, y_first, x
+        packets = [packet for pair in pairs for packet in pair]
+        return attend(plan, turned, [x, y], packets, state, out_weight)
+
     held = {}
 
     def bring_with(groups, *arguments, **settings):
@@ -481,17 +474,19 @@
         held.update(zip(groups, results[2:]))
         return results[:2]
 
-    state = bring_with((2, 3), [(x, y_first, 1)], None, own=True)
+    state = bring_with((2, 3), [(x, y)], None, own=True)
     for r in range(1, half):
-        if r > 1:
+        if r == 1:
+            up_first, up_second = up(x), lax.ppermute(sent, "blk", cross_up)
+            down_first, down_second = lax.ppermute(sent, "blk", cross_down), down(x)
+        else:
             up_first, down_first, *state = lax.optimization_barrier((up_first, down_first, *state))
-        up_first, up_second = up(up_first), up(up_second)
-        down_first, down_second = down(down_first), down(down_second)
-        if r > 1:
+            up_first, up_second = up(up_first), up(up_second)
+            down_first, down_second = down(down_first), down(down_second)
             state = bring_with((r - 2,), arrived, state)
-        arrived = [(up_first, up_second, 0), (down_second, down_first, 1)]
+        arrived = [(up_first, up_second), (down_second, down_first)]
     up_first, down_first, *state = lax.optimization_barrier((up_first, down_first, *state))
-    far = (up(up_first), down(down_first), 1)
+    far = (up(up_first), down(down_first))
     state = call(arrived, state)
     (theirs,) = call([far], state, last=True, which=(1,))
     other = lax.ppermute(theirs, "blk", sibling)

time: 67.7 us -> 67.9 us (level)
  waiting for transfers between devices: 19 us -> 19.8 us
    ppermute x7 -> x6, starting transfers between devices: 11.9 us -> 2.8 us  [split_over_cores(): down = lambda x: lax.ppermute(x, 'blk', counter)]
    ppermute x7 -> x6, starting transfers between devices: 3.48 us -> 11.8 us  [split_over_cores(): up = lambda x: lax.ppermute(x, 'blk', clock)]
    ppermute x7 -> x6, waiting for transfers between devices: 1.22 us -> 7.71 us  [split_over_cores(): down = lambda x: lax.ppermute(x, 'blk', counter)]
    ppermute x7 -> x6, waiting for transfers between devices: 5.83 us -> 0.08 us  [split_over_cores(): up = lambda x: lax.ppermute(x, 'blk', clock)]
where the time goes in v13:
time: 67.9 us; the launch traced here: 67.7 us
  Pallas kernels  26.1 us (38%)
  starting transfers between devices  21.5 us (32%)
  waiting for transfers between devices  19.8 us (29%)
    pallas_call x6, Pallas kernels, attend(): pl.pallas_call(functools.partial(attend_kernel, plan), out_shape=out_shap...  14.5 us
    ppermute x6, starting transfers between devices, split_over_cores(): up = lambda x: lax.ppermute(x, 'blk', clock)  11.8 us
    ppermute x5, waiting for transfers between devices, shards(): received.append(lax.ppermute(sent, 'inner', [(0, 1), (1, 0)]))  10.7 us
    ppermute x6, waiting for transfers between devices, split_over_cores(): down = lambda x: lax.ppermute(x, 'blk', counter)  7.71 us
    pallas_call x5, Pallas kernels, project(): pl.pallas_call(functools.partial(project_kernel, bring, begun is not None...  7.25 us
    ppermute x5, starting transfers between devices, shards(): received.append(lax.ppermute(sent, 'inner', [(0, 1), (1, 0)]))  5.89 us
    ppermute x6, starting transfers between devices, split_over_cores(): down = lambda x: lax.ppermute(x, 'blk', counter)  2.8 us
    pallas_call x2, Pallas kernels, finish(): pl.pallas_call(functools.partial(finish_kernel, first, pairs), out_shape=...  1.8 us
  transfers between devices with their start and end apart: 22, of which 10 were waited for; matrix products, arithmetic and copies ran while one was open for 0% of the time, Pallas kernels for 33%

profile of v13, /device:TPU:0, one launch (start us, length us, event | category | flops | bytes accessed | tf_op | source)
XLA Modules:
  0.0 67.7 jit_solution(5402457648022301304)
XLA Ops:
  0.0 1.4 %prepare.1 = (bf16[200,512]{1,0:T(8,128)(2,1)S(1)}, bf16[200,512]{1,0:T(8,128)(2,1)S(1)}, bf16[192,1280]{1,0:T(8,128)(2,1)S(1)}, bf16[192,1280]{1,0:T(8,128)(2,1)S(1)}) custom-call(bf16[192,2560]{1,0:T(8,128)(2,1)} %q_ref.1, bf16[192,512]{1,0:T(8,128)(2,1)} %k_ref.1, bf16[192,512]{1,0:T(8,128)(2,1)} %v_ref.1, s32[192]{0:T(256)} %position_ref.1), custom_call_target="tpu_custom_call" | custom-call | tf_op jit(solution)/shard_map/prepare/pallas_call | solution.py:387
  1.4 0.5 collective-permute-start
  2.0 0.1 collective-permute-start.1
  2.0 3.0 %collective-permute-start.2 = (bf16[200,512]{1,0:T(8,128)(2,1)S(1)}, bf16[200,512]{1,0:T(8,128)(2,1)S(1)}, u32[]{:S(2)}, u32[]{:S(2)}) collective-permute-start(bf16[200,512]{1,0:T(8,128)(2,1)S(1)} %get-tuple-element.50.refs_1_.refs_3_), channel_id=1, source_target_pairs={{0,8},{2,10},{8,16},{10,18},{16,24},{18,26},{24,28},{26,30},{28,20... | collective-permute-start | bytes 614408 | tf_op jit(solution)/shard_map/ppermute | solution.py:442
  5.0 1.4 %collective-permute-start.7 = (bf16[200,512]{1,0:T(8,128)(2,1)S(1)}, bf16[200,512]{1,0:T(8,128)(2,1)S(1)}, u32[]{:S(2)}, u32[]{:S(2)}) collective-permute-start(bf16[200,512]{1,0:T(8,128)(2,1)S(1)} %get-tuple-element.50.refs_1_.refs_3_), channel_id=1, source_target_pairs={{0,4},{2,6},{8,0},{10,2},{16,8},{18,10},{24,16},{26,18},{28,24},{3... | collective-permute-start | bytes 614408 | tf_op jit(solution)/shard_map/ppermute | solution.py:443
  6.4 0.4 collective-permute-start.6
  6.8 0.3 turn.1.refs_0_
  7.1 3.9 %attend.6 = (f32[8,1,480]{2,1,0:T(1,128)S(1)}, f32[8,144,480]{2,1,0:T(8,128)S(1)}, bf16[2560,1024]{1,0:T(8,128)(2,1)S(1)}, bf16[2560,896]{1,0:T(8,128)(2,1)S(1)}) custom-call(bf16[8,128,480]{2,1,0:T(8,128)(2,1)S(1)} %turn.1.refs_0_, bf16[200,512]{1,0:T(8,128)(2,1)S(1)} %get-tuple-element.50.refs_1_.refs_3_, ...), custom_call_target="tpu_custom_call" | custom-call | flops 377487360 | bytes 4194304 | tf_op jit(solution)/shard_map/attend/pallas_call | solution.py:233
  11.1 0.0 collective-permute-done.2.refs_3_
  11.1 1.2 %collective-permute-done.3.refs_6_ = bf16[200,512]{1,0:T(8,128)(2,1)S(1)} collective-permute-done((bf16[200,512]{1,0:T(8,128)(2,1)S(1)}, bf16[200,512]{1,0:T(8,128)(2,1)S(1)}, u32[]{:S(2)}, u32[]{:S(2)}) %collective-permute-start.3) | collective-permute-done | bytes 204832 | tf_op jit(solution)/shard_map/ppermute | solution.py:481
  12.3 1.6 %collective-permute-start.4 = (bf16[200,512]{1,0:T(8,128)(2,1)S(1)}, bf16[200,512]{1,0:T(8,128)(2,1)S(1)}, u32[]{:S(2)}, u32[]{:S(2)}) collective-permute-start(bf16[200,512]{1,0:T(8,128)(2,1)S(1)} %collective-permute-done.2.refs_3_), channel_id=1, source_target_pairs={{0,8},{2,10},{8,16},{10,18},{16,24},{18,26},{24,28},{26,30},{28,20... | collective-permute-start | bytes 614408 | tf_op jit(solution)/shard_map/ppermute | solution.py:442
  13.9 0.4 collective-permute-start.5
  14.3 2.6 %collective-permute-done.7.refs_5_ = bf16[200,512]{1,0:T(8,128)(2,1)S(1)} collective-permute-done((bf16[200,512]{1,0:T(8,128)(2,1)S(1)}, bf16[200,512]{1,0:T(8,128)(2,1)S(1)}, u32[]{:S(2)}, u32[]{:S(2)}) %collective-permute-start.7) | collective-permute-done | bytes 204832 | tf_op jit(solution)/shard_map/ppermute | solution.py:443
  16.9 2.0 %collective-permute-start.10 = (bf16[200,512]{1,0:T(8,128)(2,1)S(1)}, bf16[200,512]{1,0:T(8,128)(2,1)S(1)}, u32[]{:S(2)}, u32[]{:S(2)}) collective-permute-start(bf16[200,512]{1,0:T(8,128)(2,1)S(1)} %collective-permute-done.6.refs_4_), channel_id=1, source_target_pairs={{0,8},{2,10},{8,16},{10,18},{16,24},{18,26},{24,28},{26,30},{28,20... | collective-permute-start | bytes 614408 | tf_op jit(solution)/shard_map/ppermute | solution.py:442
  19.0 3.1 %attend.7 = (f32[8,1,480]{2,1,0:T(1,128)S(1)}, f32[8,144,480]{2,1,0:T(8,128)S(1)}, bf16[2560,1280]{1,0:T(8,128)(2,1)S(1)}) custom-call(bf16[8,128,480]{2,1,0:T(8,128)(2,1)S(1)} %turn.1.refs_0_, bf16[200,512]{1,0:T(8,128)(2,1)S(1)} %get-tuple-element.50.refs_1_.refs_3_, bf16[200,512]{1,0:T(8,128)(2,1)S(1)} %collective-permute-done.1.refs_2_.refs_4_, ...), custom_call_target="tpu_custom_call" | custom-call | flops 754974720 | bytes 4194304 | tf_op jit(solution)/shard_map/attend/pallas_call | solution.py:233
  22.1 1.6 %collective-permute-start.8 = (bf16[200,512]{1,0:T(8,128)(2,1)S(1)}, bf16[200,512]{1,0:T(8,128)(2,1)S(1)}, u32[]{:S(2)}, u32[]{:S(2)}) collective-permute-start(bf16[200,512]{1,0:T(8,128)(2,1)S(1)} %collective-permute-done.4.refs_3_), channel_id=1, source_target_pairs={{0,8},{2,10},{8,16},{10,18},{16,24},{18,26},{24,28},{26,30},{28,20... | collective-permute-start | bytes 614408 | tf_op jit(solution)/shard_map/ppermute | solution.py:442
  23.7 0.5 collective-permute-start.9
  24.1 1.7 %collective-permute-done.11.refs_5_ = bf16[200,512]{1,0:T(8,128)(2,1)S(1)} collective-permute-done((bf16[200,512]{1,0:T(8,128)(2,1)S(1)}, bf16[200,512]{1,0:T(8,128)(2,1)S(1)}, u32[]{:S(2)}, u32[]{:S(2)}) %collective-permute-start.11) | collective-permute-done | bytes 204832 | tf_op jit(solution)/shard_map/ppermute | solution.py:443
  25.8 0.0 collective-permute-start.15
  25.8 2.0 %collective-permute-start.14 = (bf16[200,512]{1,0:T(8,128)(2,1)S(1)}, bf16[200,512]{1,0:T(8,128)(2,1)S(1)}, u32[]{:S(2)}, u32[]{:S(2)}) collective-permute-start(bf16[200,512]{1,0:T(8,128)(2,1)S(1)} %collective-permute-done.10.refs_4_), channel_id=1, source_target_pairs={{0,8},{2,10},{8,16},{10,18},{16,24},{18,26},{24,28},{26,30},{28,20... | collective-permute-start | bytes 614408 | tf_op jit(solution)/shard_map/ppermute | solution.py:442
  27.8 3.1 %attend.8 = (f32[8,1,480]{2,1,0:T(1,128)S(1)}, f32[8,144,480]{2,1,0:T(8,128)S(1)}, bf16[2560,1152]{1,0:T(8,128)(2,1)S(1)}) custom-call(bf16[8,128,480]{2,1,0:T(8,128)(2,1)S(1)} %turn.1.refs_0_, bf16[200,512]{1,0:T(8,128)(2,1)S(1)} %get-tuple-element.50.refs_1_.refs_3_, bf16[200,512]{1,0:T(8,128)(2,1)S(1)} %collective-permute-done.1.refs_2_.refs_4_, ...), custom_call_target="tpu_custom_call" | custom-call | flops 754974720 | bytes 4194304 | tf_op jit(solution)/shard_map/attend/pallas_call | solution.py:233
  30.9 0.0 collective-permute-done.8.refs_3_
  30.9 0.8 %collective-permute-done.9.refs_6_ = bf16[200,512]{1,0:T(8,128)(2,1)S(1)} collective-permute-done((bf16[200,512]{1,0:T(8,128)(2,1)S(1)}, bf16[200,512]{1,0:T(8,128)(2,1)S(1)}, u32[]{:S(2)}, u32[]{:S(2)}) %collective-permute-start.9) | collective-permute-done | bytes 204832 | tf_op jit(solution)/shard_map/ppermute | solution.py:443
  31.7 1.5 %collective-permute-start.12 = (bf16[200,512]{1,0:T(8,128)(2,1)S(1)}, bf16[200,512]{1,0:T(8,128)(2,1)S(1)}, u32[]{:S(2)}, u32[]{:S(2)}) collective-permute-start(bf16[200,512]{1,0:T(8,128)(2,1)S(1)} %collective-permute-done.8.refs_3_), channel_id=1, source_target_pairs={{0,8},{2,10},{8,16},{10,18},{16,24},{18,26},{24,28},{26,30},{28,20... | collective-permute-start | bytes 614408 | tf_op jit(solution)/shard_map/ppermute | solution.py:442
  33.2 0.5 collective-permute-start.13
  33.7 1.1 %collective-permute-done.15.refs_5_ = bf16[200,512]{1,0:T(8,128)(2,1)S(1)} collective-permute-done((bf16[200,512]{1,0:T(8,128)(2,1)S(1)}, bf16[200,512]{1,0:T(8,128)(2,1)S(1)}, u32[]{:S(2)}, u32[]{:S(2)}) %collective-permute-start.15) | collective-permute-done | bytes 204832 | tf_op jit(solution)/shard_map/ppermute | solution.py:443
  34.9 2.5 %attend.9 = (f32[8,1,480]{2,1,0:T(1,128)S(1)}, f32[8,144,480]{2,1,0:T(8,128)S(1)}) custom-call(bf16[8,128,480]{2,1,0:T(8,128)(2,1)S(1)} %turn.1.refs_0_, bf16[200,512]{1,0:T(8,128)(2,1)S(1)} %get-tuple-element.50.refs_1_.refs_3_, bf16[200,512]{1,0:T(8,128)(2,1)S(1)} %collective-permute-done.1.refs_2_.refs_4_, ...), custom_call_target="tpu_custom_call" | custom-call | flops 754974720 | bytes 4194304 | tf_op jit(solution)/shard_map/attend/pallas_call | solution.py:233
  37.4 0.1 collective-permute-done.12.refs_3_
  37.5 1.5 %collective-permute-done.13.refs_4_ = bf16[200,512]{1,0:T(8,128)(2,1)S(1)} collective-permute-done((bf16[200,512]{1,0:T(8,128)(2,1)S(1)}, bf16[200,512]{1,0:T(8,128)(2,1)S(1)}, u32[]{:S(2)}, u32[]{:S(2)}) %collective-permute-start.13) | collective-permute-done | bytes 204832 | tf_op jit(solution)/shard_map/ppermute | solution.py:443
  39.0 1.0 %attend.11 = bf16[192,1280]{1,0:T(8,128)(2,1)S(1)} custom-call(bf16[8,128,480]{2,1,0:T(8,128)(2,1)S(1)} %turn.1.refs_0_, bf16[200,512]{1,0:T(8,128)(2,1)S(1)} %get-tuple-element.50.refs_1_.refs_3_, bf16[200,512]{1,0:T(8,128)(2,1)S(1)} %collective-permute-done.1.refs_2_.refs_4_, bf16[200,512]{1,0:T(8,128)(2,1)S(1)} %collective-permute-done.12.refs_3_, ...), custom_call_target="tpu_custom_call" | custom-call | flops 377487360 | bytes 4194304 | tf_op jit(solution)/shard_map/attend/pallas_call | solution.py:233
  39.9 0.1 collective-permute-start.16
  40.0 1.0 %attend.10.own_ref = bf16[192,1280]{1,0:T(8,128)(2,1)S(1)} custom-call(bf16[8,128,480]{2,1,0:T(8,128)(2,1)S(1)} %turn.1.refs_0_, bf16[200,512]{1,0:T(8,128)(2,1)S(1)} %get-tuple-element.50.refs_1_.refs_3_, bf16[200,512]{1,0:T(8,128)(2,1)S(1)} %collective-permute-done.1.refs_2_.refs_4_, bf16[200,512]{1,0:T(8,128)(2,1)S(1)} %collective-permute-done.12.refs_3_, ...), custom_call_target="tpu_custom_call" | custom-call | flops 377487360 | bytes 4194304 | tf_op jit(solution)/shard_map/attend/pallas_call | solution.py:233
  41.0 0.8 %begin.1.refs_0_ = f32[192,1280]{1,0:T(8,128)S(1)} custom-call(bf16[192,1280]{1,0:T(8,128)(2,1)S(1)} %attend.10.own_ref, bf16[2560,1280]{1,0:T(8,128)(2,1)S(1)} %get-tuple-element.72.held_ref), custom_call_target="tpu_custom_call" | custom-call | flops 1024 | bytes 1024 | tf_op jit(solution)/shard_map/begin/pallas_call | solution.py:292
  41.8 0.1 collective-permute-done.16.other_ref
  41.9 0.8 %project.5 = (bf16[96,1280]{1,0:T(8,128)(2,1)S(1)}, bf16[96,1280]{1,0:T(8,128)(2,1)S(1)}) custom-call(bf16[192,1280]{1,0:T(8,128)(2,1)S(1)} %attend.10.own_ref, bf16[192,1280]{1,0:T(8,128)(2,1)S(1)} %collective-permute-done.16.other_ref, bf16[2560,1280]{1,0:T(8,128)(2,1)S(1)} %get-tuple-element.72.held_ref, f32[192,1280]{1,0:T(8,128)S(1)} %begin.1.refs_0_), custom_call_target="tpu_custom_call" | custom-call | flops 1024 | bytes 1024 | tf_op jit(solution)/shard_map/project/pallas_call | solution.py:344
  42.7 1.6 %collective-permute-start.18 = (bf16[96,1280]{1,0:T(8,128)(2,1)S(1)}, bf16[96,1280]{1,0:T(8,128)(2,1)S(1)}, u32[]{:S(2)}, u32[]{:S(2)}) collective-permute-start(bf16[96,1280]{1,0:T(8,128)(2,1)S(1)} %get-tuple-element.73), channel_id=1, source_target_pairs={{0,1},{1,0},{2,3},{3,2},{4,5},{5,4},{6,7},{7,6},{8,9},{9,8},{10,11... | collective-permute-start | bytes 737288 | tf_op jit(solution)/shard_map/ppermute | solution.py:546
  44.3 1.5 %project.6 = (bf16[96,1152]{1,0:T(8,128)(2,1)S(1)}, bf16[96,1152]{1,0:T(8,128)(2,1)S(1)}) custom-call(bf16[192,1280]{1,0:T(8,128)(2,1)S(1)} %attend.10.own_ref, bf16[192,1280]{1,0:T(8,128)(2,1)S(1)} %collective-permute-done.16.other_ref, bf16[2560,1152]{1,0:T(8,128)(2,1)S(1)} %get-tuple-element.75.held_ref), custom_call_target="tpu_custom_call" | custom-call | flops 1024 | bytes 1024 | tf_op jit(solution)/shard_map/project/pallas_call | solution.py:344
  45.8 0.6 collective-permute-start.19
  46.3 2.8 %project.7 = (bf16[96,1024]{1,0:T(8,128)(2,1)S(1)}, bf16[96,1024]{1,0:T(8,128)(2,1)S(1)}, bf16[2560,768]{1,0:T(8,128)(2,1)S(1)}) custom-call(bf16[192,1280]{1,0:T(8,128)(2,1)S(1)} %attend.10.own_ref, bf16[192,1280]{1,0:T(8,128)(2,1)S(1)} %collective-permute-done.16.other_ref, bf16[2560,1024]{1,0:T(8,128)(2,1)S(1)} %get-tuple-element.78.held_ref, ...), custom_call_target="tpu_custom_call" | custom-call | flops 1024 | bytes 1024 | tf_op jit(solution)/shard_map/project/pallas_call | solution.py:344
  49.1 1.6 %collective-permute-start.20 = (bf16[96,1024]{1,0:T(8,128)(2,1)S(1)}, bf16[96,1024]{1,0:T(8,128)(2,1)S(1)}, u32[]{:S(2)}, u32[]{:S(2)}) collective-permute-start(bf16[96,1024]{1,0:T(8,128)(2,1)S(1)} %get-tuple-element.79), channel_id=1, source_target_pairs={{0,1},{1,0},{2,3},{3,2},{4,5},{5,4},{6,7},{7,6},{8,9},{9,8},{10,11... | collective-permute-start | bytes 589832 | tf_op jit(solution)/shard_map/ppermute | solution.py:546
  50.7 1.2 %project.8 = (bf16[96,896]{1,0:T(8,128)(2,1)S(1)}, bf16[96,896]{1,0:T(8,128)(2,1)S(1)}) custom-call(bf16[192,1280]{1,0:T(8,128)(2,1)S(1)} %attend.10.own_ref, bf16[192,1280]{1,0:T(8,128)(2,1)S(1)} %collective-permute-done.16.other_ref, bf16[2560,896]{1,0:T(8,128)(2,1)S(1)} %get-tuple-element.81.held_ref), custom_call_target="tpu_custom_call" | custom-call | flops 1024 | bytes 1024 | tf_op jit(solution)/shard_map/project/pallas_call | solution.py:344
  52.0 0.6 collective-permute-start.21
  52.5 0.9 %project.9 = (bf16[96,768]{1,0:T(8,128)(2,1)S(1)}, bf16[96,768]{1,0:T(8,128)(2,1)S(1)}) custom-call(bf16[192,1280]{1,0:T(8,128)(2,1)S(1)} %attend.10.own_ref, bf16[192,1280]{1,0:T(8,128)(2,1)S(1)} %collective-permute-done.16.other_ref, bf16[2560,768]{1,0:T(8,128)(2,1)S(1)} %get-tuple-element.84.held_ref), custom_call_target="tpu_custom_call" | custom-call | flops 1024 | bytes 1024 | tf_op jit(solution)/shard_map/project/pallas_call | solution.py:344
  53.5 1.6 %collective-permute-start.17 = (bf16[96,768]{1,0:T(8,128)(2,1)S(1)}, bf16[96,768]{1,0:T(8,128)(2,1)S(1)}, u32[]{:S(2)}, u32[]{:S(2)}) collective-permute-start(bf16[96,768]{1,0:T(8,128)(2,1)S(1)} %get-tuple-element.86), channel_id=1, source_target_pairs={{0,1},{1,0},{2,3},{3,2},{4,5},{5,4},{6,7},{7,6},{8,9},{9,8},{10,11... | collective-permute-start | bytes 442376 | tf_op jit(solution)/shard_map/ppermute | solution.py:546
  55.0 9.1 %collective-permute-done.21.refs_7_ = bf16[96,896]{1,0:T(8,128)(2,1)S(1)} collective-permute-done((bf16[96,896]{1,0:T(8,128)(2,1)S(1)}, bf16[96,896]{1,0:T(8,128)(2,1)S(1)}, u32[]{:S(2)}, u32[]{:S(2)}) %collective-permute-start.21) | collective-permute-done | bytes 172064 | tf_op jit(solution)/shard_map/ppermute | solution.py:546
  64.2 1.1 %finish.2.refs_2_ = bf16[96,5120]{1,0:T(8,128)(2,1)} custom-call(bf16[96,1280]{1,0:T(8,128)(2,1)S(1)} %get-tuple-element.87.refs_0_, bf16[96,1152]{1,0:T(8,128)(2,1)S(1)} %get-tuple-element.88.refs_1_, bf16[96,1024]{1,0:T(8,128)(2,1)S(1)} %get-tuple-element.89.refs_2_, bf16[96,896]{1,0:T(8,128)(2,1)S(1)} %get-tuple-element.90.refs_3_, ...), custom_call_target="tpu_custom_call" | custom-call | flops 1024 | bytes 1024 | tf_op jit(solution)/shard_map/finish/pallas_call | solution.py:419
  65.3 1.6 %collective-permute-done.17.refs_1_ = bf16[96,768]{1,0:T(8,128)(2,1)S(1)} collective-permute-done((bf16[96,768]{1,0:T(8,128)(2,1)S(1)}, bf16[96,768]{1,0:T(8,128)(2,1)S(1)}, u32[]{:S(2)}, u32[]{:S(2)}) %collective-permute-start.17) | collective-permute-done | bytes 147488 | tf_op jit(solution)/shard_map/ppermute | solution.py:546
  66.9 0.7 %finish.3 = bf16[96,5120]{1,0:T(8,128)(2,1)} custom-call(bf16[96,768]{1,0:T(8,128)(2,1)S(1)} %get-tuple-element.85.refs_0_, bf16[96,768]{1,0:T(8,128)(2,1)S(1)} %collective-permute-done.17.refs_1_, bf16[96,5120]{1,0:T(8,128)(2,1)} %finish.2.refs_2_), custom_call_target="tpu_custom_call", output_to_operand_aliasing={{}: (2, {})} | custom-call | flops 1024 | bytes 1024 | tf_op jit(solution)/shard_map/finish/pallas_call | solution.py:419
  (12 shorter events, 0.0 us)
Async XLA Ops:
  1.4 5.0 %collective-permute-start = (bf16[192,1280]{1,0:T(8,128)(2,1)S(1)}, bf16[192,1280]{1,0:T(8,128)(2,1)S(1)}, u32[]{:S(2)}, u32[]{:S(2)}) collective-permute-start(bf16[192,1280]{1,0:T(8,128)(2,1)S(1)} %get-tuple-element.49), channel_id=1, source_target_pairs={{0,2},{2,0},{4,6},{6,4},{8,10},{10,8},{12,14},{14,12},{16,18},{18,... | collective-permute-start | bytes 1474568 | tf_op jit(solution)/shard_map/ppermute | solution.py:448
  2.0 5.2 %collective-permute-start.1 = (bf16[200,512]{1,0:T(8,128)(2,1)S(1)}, bf16[200,512]{1,0:T(8,128)(2,1)S(1)}, u32[]{:S(2)}, u32[]{:S(2)}) collective-permute-start(bf16[200,512]{1,0:T(8,128)(2,1)S(1)} %get-tuple-element.51), channel_id=1, source_target_pairs={{0,2},{2,0},{4,6},{6,4},{8,10},{10,8},{12,14},{14,12},{16,18},{18,... | collective-permute-start | bytes 614408 | tf_op jit(solution)/shard_map/ppermute | solution.py:447
  2.0 9.0 %collective-permute-start.2 = (bf16[200,512]{1,0:T(8,128)(2,1)S(1)}, bf16[200,512]{1,0:T(8,128)(2,1)S(1)}, u32[]{:S(2)}, u32[]{:S(2)}) collective-permute-start(bf16[200,512]{1,0:T(8,128)(2,1)S(1)} %get-tuple-element.50.refs_1_.refs_3_), channel_id=1, source_target_pairs={{0,8},{2,10},{8,16},{10,18},{16,24},{18,26},{24,28},{26,30},{28,20... | collective-permute-start | bytes 614408 | tf_op jit(solution)/shard_map/ppermute | solution.py:442
  5.0 7.2 %collective-permute-start.3 = (bf16[200,512]{1,0:T(8,128)(2,1)S(1)}, bf16[200,512]{1,0:T(8,128)(2,1)S(1)}, u32[]{:S(2)}, u32[]{:S(2)}) collective-permute-start(bf16[200,512]{1,0:T(8,128)(2,1)S(1)} %get-tuple-element.51), channel_id=1, source_target_pairs={{0,6},{2,4},{8,2},{10,0},{16,10},{18,8},{24,18},{26,16},{28,26},{3... | collective-permute-start | bytes 614408 | tf_op jit(solution)/shard_map/ppermute | solution.py:481
  5.0 11.9 %collective-permute-start.7 = (bf16[200,512]{1,0:T(8,128)(2,1)S(1)}, bf16[200,512]{1,0:T(8,128)(2,1)S(1)}, u32[]{:S(2)}, u32[]{:S(2)}) collective-permute-start(bf16[200,512]{1,0:T(8,128)(2,1)S(1)} %get-tuple-element.50.refs_1_.refs_3_), channel_id=1, source_target_pairs={{0,4},{2,6},{8,0},{10,2},{16,8},{18,10},{24,16},{26,18},{28,24},{3... | collective-permute-start | bytes 614408 | tf_op jit(solution)/shard_map/ppermute | solution.py:443
  6.4 10.5 %collective-permute-start.6 = (bf16[200,512]{1,0:T(8,128)(2,1)S(1)}, bf16[200,512]{1,0:T(8,128)(2,1)S(1)}, u32[]{:S(2)}, u32[]{:S(2)}) collective-permute-start(bf16[200,512]{1,0:T(8,128)(2,1)S(1)} %get-tuple-element.51), channel_id=1, source_target_pairs={{0,10},{2,8},{8,18},{10,16},{16,26},{18,24},{24,30},{26,28},{28,22... | collective-permute-start | bytes 614408 | tf_op jit(solution)/shard_map/ppermute | solution.py:480
  12.3 9.8 %collective-permute-start.4 = (bf16[200,512]{1,0:T(8,128)(2,1)S(1)}, bf16[200,512]{1,0:T(8,128)(2,1)S(1)}, u32[]{:S(2)}, u32[]{:S(2)}) collective-permute-start(bf16[200,512]{1,0:T(8,128)(2,1)S(1)} %collective-permute-done.2.refs_3_), channel_id=1, source_target_pairs={{0,8},{2,10},{8,16},{10,18},{16,24},{18,26},{24,28},{26,30},{28,20... | collective-permute-start | bytes 614408 | tf_op jit(solution)/shard_map/ppermute | solution.py:442
  13.9 8.2 %collective-permute-start.5 = (bf16[200,512]{1,0:T(8,128)(2,1)S(1)}, bf16[200,512]{1,0:T(8,128)(2,1)S(1)}, u32[]{:S(2)}, u32[]{:S(2)}) collective-permute-start(bf16[200,512]{1,0:T(8,128)(2,1)S(1)} %collective-permute-done.3.refs_6_), channel_id=1, source_target_pairs={{0,4},{2,6},{8,0},{10,2},{16,8},{18,10},{24,16},{26,18},{28,24},{3... | collective-permute-start | bytes 614408 | tf_op jit(solution)/shard_map/ppermute | solution.py:443
  16.9 8.9 %collective-permute-start.11 = (bf16[200,512]{1,0:T(8,128)(2,1)S(1)}, bf16[200,512]{1,0:T(8,128)(2,1)S(1)}, u32[]{:S(2)}, u32[]{:S(2)}) collective-permute-start(bf16[200,512]{1,0:T(8,128)(2,1)S(1)} %collective-permute-done.7.refs_5_), channel_id=1, source_target_pairs={{0,4},{2,6},{8,0},{10,2},{16,8},{18,10},{24,16},{26,18},{28,24},{3... | collective-permute-start | bytes 614408 | tf_op jit(solution)/shard_map/ppermute | solution.py:443
  16.9 8.9 %collective-permute-start.10 = (bf16[200,512]{1,0:T(8,128)(2,1)S(1)}, bf16[200,512]{1,0:T(8,128)(2,1)S(1)}, u32[]{:S(2)}, u32[]{:S(2)}) collective-permute-start(bf16[200,512]{1,0:T(8,128)(2,1)S(1)} %collective-permute-done.6.refs_4_), channel_id=1, source_target_pairs={{0,8},{2,10},{8,16},{10,18},{16,24},{18,26},{24,28},{26,30},{28,20... | collective-permute-start | bytes 614408 | tf_op jit(solution)/shard_map/ppermute | solution.py:442
  22.1 8.8 %collective-permute-start.8 = (bf16[200,512]{1,0:T(8,128)(2,1)S(1)}, bf16[200,512]{1,0:T(8,128)(2,1)S(1)}, u32[]{:S(2)}, u32[]{:S(2)}) collective-permute-start(bf16[200,512]{1,0:T(8,128)(2,1)S(1)} %collective-permute-done.4.refs_3_), channel_id=1, source_target_pairs={{0,8},{2,10},{8,16},{10,18},{16,24},{18,26},{24,28},{26,30},{28,20... | collective-permute-start | bytes 614408 | tf_op jit(solution)/shard_map/ppermute | solution.py:442
  23.7 8.0 %collective-permute-start.9 = (bf16[200,512]{1,0:T(8,128)(2,1)S(1)}, bf16[200,512]{1,0:T(8,128)(2,1)S(1)}, u32[]{:S(2)}, u32[]{:S(2)}) collective-permute-start(bf16[200,512]{1,0:T(8,128)(2,1)S(1)} %collective-permute-done.5.refs_6_), channel_id=1, source_target_pairs={{0,4},{2,6},{8,0},{10,2},{16,8},{18,10},{24,16},{26,18},{28,24},{3... | collective-permute-start | bytes 614408 | tf_op jit(solution)/shard_map/ppermute | solution.py:443
  25.8 9.1 %collective-permute-start.15 = (bf16[200,512]{1,0:T(8,128)(2,1)S(1)}, bf16[200,512]{1,0:T(8,128)(2,1)S(1)}, u32[]{:S(2)}, u32[]{:S(2)}) collective-permute-start(bf16[200,512]{1,0:T(8,128)(2,1)S(1)} %collective-permute-done.11.refs_5_), channel_id=1, source_target_pairs={{0,4},{2,6},{8,0},{10,2},{16,8},{18,10},{24,16},{26,18},{28,24},{3... | collective-permute-start | bytes 614408 | tf_op jit(solution)/shard_map/ppermute | solution.py:443
  25.8 9.1 %collective-permute-start.14 = (bf16[200,512]{1,0:T(8,128)(2,1)S(1)}, bf16[200,512]{1,0:T(8,128)(2,1)S(1)}, u32[]{:S(2)}, u32[]{:S(2)}) collective-permute-start(bf16[200,512]{1,0:T(8,128)(2,1)S(1)} %collective-permute-done.10.refs_4_), channel_id=1, source_target_pairs={{0,8},{2,10},{8,16},{10,18},{16,24},{18,26},{24,28},{26,30},{28,20... | collective-permute-start | bytes 614408 | tf_op jit(solution)/shard_map/ppermute | solution.py:442
  31.7 5.8 %collective-permute-start.12 = (bf16[200,512]{1,0:T(8,128)(2,1)S(1)}, bf16[200,512]{1,0:T(8,128)(2,1)S(1)}, u32[]{:S(2)}, u32[]{:S(2)}) collective-permute-start(bf16[200,512]{1,0:T(8,128)(2,1)S(1)} %collective-permute-done.8.refs_3_), channel_id=1, source_target_pairs={{0,8},{2,10},{8,16},{10,18},{16,24},{18,26},{24,28},{26,30},{28,20... | collective-permute-start | bytes 614408 | tf_op jit(solution)/shard_map/ppermute | solution.py:442
  33.2 5.8 %collective-permute-start.13 = (bf16[200,512]{1,0:T(8,128)(2,1)S(1)}, bf16[200,512]{1,0:T(8,128)(2,1)S(1)}, u32[]{:S(2)}, u32[]{:S(2)}) collective-permute-start(bf16[200,512]{1,0:T(8,128)(2,1)S(1)} %collective-permute-done.9.refs_6_), channel_id=1, source_target_pairs={{0,4},{2,6},{8,0},{10,2},{16,8},{18,10},{24,16},{26,18},{28,24},{3... | collective-permute-start | bytes 614408 | tf_op jit(solution)/shard_map/ppermute | solution.py:443
  39.9 1.9 %collective-permute-start.16 = (bf16[192,1280]{1,0:T(8,128)(2,1)S(1)}, bf16[192,1280]{1,0:T(8,128)(2,1)S(1)}, u32[]{:S(2)}, u32[]{:S(2)}) collective-permute-start(bf16[192,1280]{1,0:T(8,128)(2,1)S(1)} %attend.11), channel_id=1, source_target_pairs={{0,2},{2,0},{4,6},{6,4},{8,10},{10,8},{12,14},{14,12},{16,18},{18,... | collective-permute-start | bytes 1474568 | tf_op jit(solution)/shard_map/ppermute | solution.py:492
  42.7 21.5 %collective-permute-start.18 = (bf16[96,1280]{1,0:T(8,128)(2,1)S(1)}, bf16[96,1280]{1,0:T(8,128)(2,1)S(1)}, u32[]{:S(2)}, u32[]{:S(2)}) collective-permute-start(bf16[96,1280]{1,0:T(8,128)(2,1)S(1)} %get-tuple-element.73), channel_id=1, source_target_pairs={{0,1},{1,0},{2,3},{3,2},{4,5},{5,4},{6,7},{7,6},{8,9},{9,8},{10,11... | collective-permute-start | bytes 737288 | tf_op jit(solution)/shard_map/ppermute | solution.py:546
  45.8 18.4 %collective-permute-start.19 = (bf16[96,1152]{1,0:T(8,128)(2,1)S(1)}, bf16[96,1152]{1,0:T(8,128)(2,1)S(1)}, u32[]{:S(2)}, u32[]{:S(2)}) collective-permute-start(bf16[96,1152]{1,0:T(8,128)(2,1)S(1)} %get-tuple-element.76), channel_id=1, source_target_pairs={{0,1},{1,0},{2,3},{3,2},{4,5},{5,4},{6,7},{7,6},{8,9},{9,8},{10,11... | collective-permute-start | bytes 663560 | tf_op jit(solution)/shard_map/ppermute | solution.py:546
  49.1 15.0 %collective-permute-start.20 = (bf16[96,1024]{1,0:T(8,128)(2,1)S(1)}, bf16[96,1024]{1,0:T(8,128)(2,1)S(1)}, u32[]{:S(2)}, u32[]{:S(2)}) collective-permute-start(bf16[96,1024]{1,0:T(8,128)(2,1)S(1)} %get-tuple-element.79), channel_id=1, source_target_pairs={{0,1},{1,0},{2,3},{3,2},{4,5},{5,4},{6,7},{7,6},{8,9},{9,8},{10,11... | collective-permute-start | bytes 589832 | tf_op jit(solution)/shard_map/ppermute | solution.py:546
  52.0 12.2 %collective-permute-start.21 = (bf16[96,896]{1,0:T(8,128)(2,1)S(1)}, bf16[96,896]{1,0:T(8,128)(2,1)S(1)}, u32[]{:S(2)}, u32[]{:S(2)}) collective-permute-start(bf16[96,896]{1,0:T(8,128)(2,1)S(1)} %get-tuple-element.82), channel_id=1, source_target_pairs={{0,1},{1,0},{2,3},{3,2},{4,5},{5,4},{6,7},{7,6},{8,9},{9,8},{10,11... | collective-permute-start | bytes 516104 | tf_op jit(solution)/shard_map/ppermute | solution.py:546
  53.5 13.4 %collective-permute-start.17 = (bf16[96,768]{1,0:T(8,128)(2,1)S(1)}, bf16[96,768]{1,0:T(8,128)(2,1)S(1)}, u32[]{:S(2)}, u32[]{:S(2)}) collective-permute-start(bf16[96,768]{1,0:T(8,128)(2,1)S(1)} %get-tuple-element.86), channel_id=1, source_target_pairs={{0,1},{1,0},{2,3},{3,2},{4,5},{5,4},{6,7},{7,6},{8,9},{9,8},{10,11... | collective-permute-start | bytes 442376 | tf_op jit(solution)/shard_map/ppermute | solution.py:546

commit v14 on v13

--- a/solution.py
+++ b/solution.py
@@ -474,7 +474,7 @@
         held.update(zip(groups, results[2:]))
         return results[:2]
 
-    state = bring_with((2, 3), [(x, y)], None, own=True)
+    state = bring_with((2,), [(x, y)], None, own=True)
     for r in range(1, half):
         if r == 1:
             up_first, up_second = up(x), lax.ppermute(sent, "blk", cross_up)
@@ -483,11 +483,11 @@
             up_first, down_first, *state = lax.optimization_barrier((up_first, down_first, *state))
             up_first, up_second = up(up_first), up(up_second)
             down_first, down_second = down(down_first), down(down_second)
-            state = bring_with((r - 2,), arrived, state)
+            state = bring_with((0,) if r == half - 1 else (), arrived, state)
         arrived = [(up_first, up_second), (down_second, down_first)]
     up_first, down_first, *state = lax.optimization_barrier((up_first, down_first, *state))
     far = (up(up_first), down(down_first))
-    state = call(arrived, state)
+    state = bring_with((1,), arrived, state)
     (theirs,) = call([far], state, last=True, which=(1,))
     other = lax.ppermute(theirs, "blk", sibling)
     (own,) = call([far], state, last=True, which=(0,))
@@ -533,9 +533,9 @@
     widths = [out_weight.shape[1] * share // sum(shares) for share in shares]
     cuts = [(sum(widths[:j]), columns) for j, columns in enumerate(widths)]
     own, other, held = split_over_cores(
-        count, queries, keys, values, positions, out_weight, cuts[:4]
+        count, queries, keys, values, positions, out_weight, cuts[:3]
     )
-    bring = [cuts[4:] if j == 2 else [] for j in range(len(cuts))]
+    bring = [cuts[j + 2 : j + 3] if j > 0 else [] for j in range(len(cuts))]
     received, kept = [], []
     for j in range(len(cuts)):
         source = own if j == 0 else after(own, sent)

time: 67.9 us -> 67.8 us (level)
    pallas_call x6, Pallas kernels: 14.5 us -> 13.1 us  [attend(): pl.pallas_call(functools.partial(attend_kernel, plan), out_shape=out_shap...]
    pallas_call x5, Pallas kernels: 7.25 us -> 8.53 us  [project(): pl.pallas_call(functools.partial(project_kernel, bring, begun is not None...]
    ppermute x5, waiting for transfers between devices: 10.7 us -> 9.45 us  [shards(): received.append(lax.ppermute(sent, 'inner', [(0, 1), (1, 0)]))]
    ppermute x6, waiting for transfers between devices: 0.08 us -> 1.17 us  [split_over_cores(): up = lambda x: lax.ppermute(x, 'blk', clock)]
where the time goes in v14:
time: 67.8 us; the launch traced here: 67.7 us
  Pallas kernels  26 us (38%)
  starting transfers between devices  21.4 us (32%)
  waiting for transfers between devices  19.8 us (29%)
    pallas_call x6, Pallas kernels, attend(): pl.pallas_call(functools.partial(attend_kernel, plan), out_shape=out_shap...  13.1 us
    ppermute x6, starting transfers between devices, split_over_cores(): up = lambda x: lax.ppermute(x, 'blk', clock)  11.8 us
    ppermute x5, waiting for transfers between devices, shards(): received.append(lax.ppermute(sent, 'inner', [(0, 1), (1, 0)]))  9.45 us
    pallas_call x5, Pallas kernels, project(): pl.pallas_call(functools.partial(project_kernel, bring, begun is not None...  8.53 us
    ppermute x6, waiting for transfers between devices, split_over_cores(): down = lambda x: lax.ppermute(x, 'blk', counter)  7.74 us
    ppermute x5, starting transfers between devices, shards(): received.append(lax.ppermute(sent, 'inner', [(0, 1), (1, 0)]))  5.87 us
    ppermute x6, starting transfers between devices, split_over_cores(): down = lambda x: lax.ppermute(x, 'blk', counter)  2.68 us
    pallas_call x2, Pallas kernels, finish(): pl.pallas_call(functools.partial(finish_kernel, first, pairs), out_shape=...  1.8 us
  transfers between devices with their start and end apart: 22, of which 10 were waited for; matrix products, arithmetic and copies ran while one was open for 0% of the time, Pallas kernels for 33%

profile of v14, /device:TPU:0, one launch (start us, length us, event | category | flops | bytes accessed | tf_op | source)
XLA Modules:
  0.0 67.7 jit_solution(16839235315604946563)
XLA Ops:
  0.0 1.4 %prepare.1 = (bf16[200,512]{1,0:T(8,128)(2,1)S(1)}, bf16[200,512]{1,0:T(8,128)(2,1)S(1)}, bf16[192,1280]{1,0:T(8,128)(2,1)S(1)}, bf16[192,1280]{1,0:T(8,128)(2,1)S(1)}) custom-call(bf16[192,2560]{1,0:T(8,128)(2,1)} %q_ref.1, bf16[192,512]{1,0:T(8,128)(2,1)} %k_ref.1, bf16[192,512]{1,0:T(8,128)(2,1)} %v_ref.1, s32[192]{0:T(256)} %position_ref.1), custom_call_target="tpu_custom_call" | custom-call | tf_op jit(solution)/shard_map/prepare/pallas_call | solution.py:387
  1.4 0.5 collective-permute-start
  2.0 0.1 collective-permute-start.1
  2.0 3.0 %collective-permute-start.2 = (bf16[200,512]{1,0:T(8,128)(2,1)S(1)}, bf16[200,512]{1,0:T(8,128)(2,1)S(1)}, u32[]{:S(2)}, u32[]{:S(2)}) collective-permute-start(bf16[200,512]{1,0:T(8,128)(2,1)S(1)} %get-tuple-element.50.refs_1_.refs_3_), channel_id=1, source_target_pairs={{0,8},{2,10},{8,16},{10,18},{16,24},{18,26},{24,28},{26,30},{28,20... | collective-permute-start | bytes 614408 | tf_op jit(solution)/shard_map/ppermute | solution.py:442
  5.0 1.4 %collective-permute-start.7 = (bf16[200,512]{1,0:T(8,128)(2,1)S(1)}, bf16[200,512]{1,0:T(8,128)(2,1)S(1)}, u32[]{:S(2)}, u32[]{:S(2)}) collective-permute-start(bf16[200,512]{1,0:T(8,128)(2,1)S(1)} %get-tuple-element.50.refs_1_.refs_3_), channel_id=1, source_target_pairs={{0,4},{2,6},{8,0},{10,2},{16,8},{18,10},{24,16},{26,18},{28,24},{3... | collective-permute-start | bytes 614408 | tf_op jit(solution)/shard_map/ppermute | solution.py:443
  6.4 0.4 collective-permute-start.6
  6.8 0.3 turn.1.refs_0_
  7.1 2.6 %attend.6 = (f32[8,1,480]{2,1,0:T(1,128)S(1)}, f32[8,144,480]{2,1,0:T(8,128)S(1)}, bf16[2560,1024]{1,0:T(8,128)(2,1)S(1)}) custom-call(bf16[8,128,480]{2,1,0:T(8,128)(2,1)S(1)} %turn.1.refs_0_, bf16[200,512]{1,0:T(8,128)(2,1)S(1)} %get-tuple-element.50.refs_1_.refs_3_, bf16[200,512]{1,0:T(8,128)(2,1)S(1)} %collective-permute-done.1.refs_2_.refs_4_, ...), custom_call_target="tpu_custom_call" | custom-call | flops 377487360 | bytes 4194304 | tf_op jit(solution)/shard_map/attend/pallas_call | solution.py:233
  9.7 1.2 %collective-permute-done.2.refs_3_ = bf16[200,512]{1,0:T(8,128)(2,1)S(1)} collective-permute-done((bf16[200,512]{1,0:T(8,128)(2,1)S(1)}, bf16[200,512]{1,0:T(8,128)(2,1)S(1)}, u32[]{:S(2)}, u32[]{:S(2)}) %collective-permute-start.2) | collective-permute-done | bytes 204832 | tf_op jit(solution)/shard_map/ppermute | solution.py:442
  10.9 1.4 %collective-permute-done.3.refs_6_ = bf16[200,512]{1,0:T(8,128)(2,1)S(1)} collective-permute-done((bf16[200,512]{1,0:T(8,128)(2,1)S(1)}, bf16[200,512]{1,0:T(8,128)(2,1)S(1)}, u32[]{:S(2)}, u32[]{:S(2)}) %collective-permute-start.3) | collective-permute-done | bytes 204832 | tf_op jit(solution)/shard_map/ppermute | solution.py:481
  12.3 1.6 %collective-permute-start.4 = (bf16[200,512]{1,0:T(8,128)(2,1)S(1)}, bf16[200,512]{1,0:T(8,128)(2,1)S(1)}, u32[]{:S(2)}, u32[]{:S(2)}) collective-permute-start(bf16[200,512]{1,0:T(8,128)(2,1)S(1)} %collective-permute-done.2.refs_3_), channel_id=1, source_target_pairs={{0,8},{2,10},{8,16},{10,18},{16,24},{18,26},{24,28},{26,30},{28,20... | collective-permute-start | bytes 614408 | tf_op jit(solution)/shard_map/ppermute | solution.py:442
  13.9 0.4 collective-permute-start.5
  14.3 2.6 %collective-permute-done.7.refs_5_ = bf16[200,512]{1,0:T(8,128)(2,1)S(1)} collective-permute-done((bf16[200,512]{1,0:T(8,128)(2,1)S(1)}, bf16[200,512]{1,0:T(8,128)(2,1)S(1)}, u32[]{:S(2)}, u32[]{:S(2)}) %collective-permute-start.7) | collective-permute-done | bytes 204832 | tf_op jit(solution)/shard_map/ppermute | solution.py:443
  16.9 0.0 collective-permute-done.6.refs_4_
  16.9 2.0 %collective-permute-start.10 = (bf16[200,512]{1,0:T(8,128)(2,1)S(1)}, bf16[200,512]{1,0:T(8,128)(2,1)S(1)}, u32[]{:S(2)}, u32[]{:S(2)}) collective-permute-start(bf16[200,512]{1,0:T(8,128)(2,1)S(1)} %collective-permute-done.6.refs_4_), channel_id=1, source_target_pairs={{0,8},{2,10},{8,16},{10,18},{16,24},{18,26},{24,28},{26,30},{28,20... | collective-permute-start | bytes 614408 | tf_op jit(solution)/shard_map/ppermute | solution.py:442
  19.0 2.5 %attend.7 = (f32[8,1,480]{2,1,0:T(1,128)S(1)}, f32[8,144,480]{2,1,0:T(8,128)S(1)}) custom-call(bf16[8,128,480]{2,1,0:T(8,128)(2,1)S(1)} %turn.1.refs_0_, bf16[200,512]{1,0:T(8,128)(2,1)S(1)} %get-tuple-element.50.refs_1_.refs_3_, bf16[200,512]{1,0:T(8,128)(2,1)S(1)} %collective-permute-done.1.refs_2_.refs_4_, ...), custom_call_target="tpu_custom_call" | custom-call | flops 754974720 | bytes 4194304 | tf_op jit(solution)/shard_map/attend/pallas_call | solution.py:233
  21.5 0.4 collective-permute-done.5.refs_6_
  21.9 1.6 %collective-permute-start.8 = (bf16[200,512]{1,0:T(8,128)(2,1)S(1)}, bf16[200,512]{1,0:T(8,128)(2,1)S(1)}, u32[]{:S(2)}, u32[]{:S(2)}) collective-permute-start(bf16[200,512]{1,0:T(8,128)(2,1)S(1)} %collective-permute-done.4.refs_3_), channel_id=1, source_target_pairs={{0,8},{2,10},{8,16},{10,18},{16,24},{18,26},{24,28},{26,30},{28,20... | collective-permute-start | bytes 614408 | tf_op jit(solution)/shard_map/ppermute | solution.py:442
  23.5 0.4 collective-permute-start.9
  23.9 2.4 %collective-permute-done.11.refs_5_ = bf16[200,512]{1,0:T(8,128)(2,1)S(1)} collective-permute-done((bf16[200,512]{1,0:T(8,128)(2,1)S(1)}, bf16[200,512]{1,0:T(8,128)(2,1)S(1)}, u32[]{:S(2)}, u32[]{:S(2)}) %collective-permute-start.11) | collective-permute-done | bytes 204832 | tf_op jit(solution)/shard_map/ppermute | solution.py:443
  26.3 0.0 collective-permute-start.15
  26.3 2.0 %collective-permute-start.14 = (bf16[200,512]{1,0:T(8,128)(2,1)S(1)}, bf16[200,512]{1,0:T(8,128)(2,1)S(1)}, u32[]{:S(2)}, u32[]{:S(2)}) collective-permute-start(bf16[200,512]{1,0:T(8,128)(2,1)S(1)} %collective-permute-done.10.refs_4_), channel_id=1, source_target_pairs={{0,8},{2,10},{8,16},{10,18},{16,24},{18,26},{24,28},{26,30},{28,20... | collective-permute-start | bytes 614408 | tf_op jit(solution)/shard_map/ppermute | solution.py:442
  28.3 3.1 %attend.8 = (f32[8,1,480]{2,1,0:T(1,128)S(1)}, f32[8,144,480]{2,1,0:T(8,128)S(1)}, bf16[2560,1280]{1,0:T(8,128)(2,1)S(1)}) custom-call(bf16[8,128,480]{2,1,0:T(8,128)(2,1)S(1)} %turn.1.refs_0_, bf16[200,512]{1,0:T(8,128)(2,1)S(1)} %get-tuple-element.50.refs_1_.refs_3_, bf16[200,512]{1,0:T(8,128)(2,1)S(1)} %collective-permute-done.1.refs_2_.refs_4_, ...), custom_call_target="tpu_custom_call" | custom-call | flops 754974720 | bytes 4194304 | tf_op jit(solution)/shard_map/attend/pallas_call | solution.py:233
  31.4 0.1 collective-permute-done.9.refs_6_
  31.5 1.6 %collective-permute-start.12 = (bf16[200,512]{1,0:T(8,128)(2,1)S(1)}, bf16[200,512]{1,0:T(8,128)(2,1)S(1)}, u32[]{:S(2)}, u32[]{:S(2)}) collective-permute-start(bf16[200,512]{1,0:T(8,128)(2,1)S(1)} %collective-permute-done.8.refs_3_), channel_id=1, source_target_pairs={{0,8},{2,10},{8,16},{10,18},{16,24},{18,26},{24,28},{26,30},{28,20... | collective-permute-start | bytes 614408 | tf_op jit(solution)/shard_map/ppermute | solution.py:442
  33.1 0.4 collective-permute-start.13
  33.6 1.3 %collective-permute-done.15.refs_5_ = bf16[200,512]{1,0:T(8,128)(2,1)S(1)} collective-permute-done((bf16[200,512]{1,0:T(8,128)(2,1)S(1)}, bf16[200,512]{1,0:T(8,128)(2,1)S(1)}, u32[]{:S(2)}, u32[]{:S(2)}) %collective-permute-start.15) | collective-permute-done | bytes 204832 | tf_op jit(solution)/shard_map/ppermute | solution.py:443
  34.8 3.1 %attend.9 = (f32[8,1,480]{2,1,0:T(1,128)S(1)}, f32[8,144,480]{2,1,0:T(8,128)S(1)}, bf16[2560,1152]{1,0:T(8,128)(2,1)S(1)}) custom-call(bf16[8,128,480]{2,1,0:T(8,128)(2,1)S(1)} %turn.1.refs_0_, bf16[200,512]{1,0:T(8,128)(2,1)S(1)} %get-tuple-element.50.refs_1_.refs_3_, bf16[200,512]{1,0:T(8,128)(2,1)S(1)} %collective-permute-done.1.refs_2_.refs_4_, ...), custom_call_target="tpu_custom_call" | custom-call | flops 754974720 | bytes 4194304 | tf_op jit(solution)/shard_map/attend/pallas_call | solution.py:233
  37.9 1.0 %collective-permute-done.13.refs_4_ = bf16[200,512]{1,0:T(8,128)(2,1)S(1)} collective-permute-done((bf16[200,512]{1,0:T(8,128)(2,1)S(1)}, bf16[200,512]{1,0:T(8,128)(2,1)S(1)}, u32[]{:S(2)}, u32[]{:S(2)}) %collective-permute-start.13) | collective-permute-done | bytes 204832 | tf_op jit(solution)/shard_map/ppermute | solution.py:443
  38.9 1.0 %attend.11 = bf16[192,1280]{1,0:T(8,128)(2,1)S(1)} custom-call(bf16[8,128,480]{2,1,0:T(8,128)(2,1)S(1)} %turn.1.refs_0_, bf16[200,512]{1,0:T(8,128)(2,1)S(1)} %get-tuple-element.50.refs_1_.refs_3_, bf16[200,512]{1,0:T(8,128)(2,1)S(1)} %collective-permute-done.1.refs_2_.refs_4_, bf16[200,512]{1,0:T(8,128)(2,1)S(1)} %collective-permute-done.12.refs_3_, ...), custom_call_target="tpu_custom_call" | custom-call | flops 377487360 | bytes 4194304 | tf_op jit(solution)/shard_map/attend/pallas_call | solution.py:233
  39.9 0.1 collective-permute-start.16
  39.9 1.0 %attend.10.own_ref = bf16[192,1280]{1,0:T(8,128)(2,1)S(1)} custom-call(bf16[8,128,480]{2,1,0:T(8,128)(2,1)S(1)} %turn.1.refs_0_, bf16[200,512]{1,0:T(8,128)(2,1)S(1)} %get-tuple-element.50.refs_1_.refs_3_, bf16[200,512]{1,0:T(8,128)(2,1)S(1)} %collective-permute-done.1.refs_2_.refs_4_, bf16[200,512]{1,0:T(8,128)(2,1)S(1)} %collective-permute-done.12.refs_3_, ...), custom_call_target="tpu_custom_call" | custom-call | flops 377487360 | bytes 4194304 | tf_op jit(solution)/shard_map/attend/pallas_call | solution.py:233
  40.9 0.8 %begin.1.refs_0_ = f32[192,1280]{1,0:T(8,128)S(1)} custom-call(bf16[192,1280]{1,0:T(8,128)(2,1)S(1)} %attend.10.own_ref, bf16[2560,1280]{1,0:T(8,128)(2,1)S(1)} %get-tuple-element.72.held_ref), custom_call_target="tpu_custom_call" | custom-call | flops 1024 | bytes 1024 | tf_op jit(solution)/shard_map/begin/pallas_call | solution.py:292
  41.7 0.0 collective-permute-done.16.other_ref
  41.8 0.8 %project.5 = (bf16[96,1280]{1,0:T(8,128)(2,1)S(1)}, bf16[96,1280]{1,0:T(8,128)(2,1)S(1)}) custom-call(bf16[192,1280]{1,0:T(8,128)(2,1)S(1)} %attend.10.own_ref, bf16[192,1280]{1,0:T(8,128)(2,1)S(1)} %collective-permute-done.16.other_ref, bf16[2560,1280]{1,0:T(8,128)(2,1)S(1)} %get-tuple-element.72.held_ref, f32[192,1280]{1,0:T(8,128)S(1)} %begin.1.refs_0_), custom_call_target="tpu_custom_call" | custom-call | flops 1024 | bytes 1024 | tf_op jit(solution)/shard_map/project/pallas_call | solution.py:344
  42.6 1.6 %collective-permute-start.18 = (bf16[96,1280]{1,0:T(8,128)(2,1)S(1)}, bf16[96,1280]{1,0:T(8,128)(2,1)S(1)}, u32[]{:S(2)}, u32[]{:S(2)}) collective-permute-start(bf16[96,1280]{1,0:T(8,128)(2,1)S(1)} %get-tuple-element.73), channel_id=1, source_target_pairs={{0,1},{1,0},{2,3},{3,2},{4,5},{5,4},{6,7},{7,6},{8,9},{9,8},{10,11... | collective-permute-start | bytes 737288 | tf_op jit(solution)/shard_map/ppermute | solution.py:546
  44.2 2.9 %project.6 = (bf16[96,1152]{1,0:T(8,128)(2,1)S(1)}, bf16[96,1152]{1,0:T(8,128)(2,1)S(1)}, bf16[2560,896]{1,0:T(8,128)(2,1)S(1)}) custom-call(bf16[192,1280]{1,0:T(8,128)(2,1)S(1)} %attend.10.own_ref, bf16[192,1280]{1,0:T(8,128)(2,1)S(1)} %collective-permute-done.16.other_ref, bf16[2560,1152]{1,0:T(8,128)(2,1)S(1)} %get-tuple-element.75.held_ref, ...), custom_call_target="tpu_custom_call" | custom-call | flops 1024 | bytes 1024 | tf_op jit(solution)/shard_map/project/pallas_call | solution.py:344
  47.1 0.6 collective-permute-start.19
  47.7 2.7 %project.7 = (bf16[96,1024]{1,0:T(8,128)(2,1)S(1)}, bf16[96,1024]{1,0:T(8,128)(2,1)S(1)}, bf16[2560,768]{1,0:T(8,128)(2,1)S(1)}) custom-call(bf16[192,1280]{1,0:T(8,128)(2,1)S(1)} %attend.10.own_ref, bf16[192,1280]{1,0:T(8,128)(2,1)S(1)} %collective-permute-done.16.other_ref, bf16[2560,1024]{1,0:T(8,128)(2,1)S(1)} %get-tuple-element.78.held_ref, ...), custom_call_target="tpu_custom_call" | custom-call | flops 1024 | bytes 1024 | tf_op jit(solution)/shard_map/project/pallas_call | solution.py:344
  50.4 1.6 %collective-permute-start.20 = (bf16[96,1024]{1,0:T(8,128)(2,1)S(1)}, bf16[96,1024]{1,0:T(8,128)(2,1)S(1)}, u32[]{:S(2)}, u32[]{:S(2)}) collective-permute-start(bf16[96,1024]{1,0:T(8,128)(2,1)S(1)} %get-tuple-element.79), channel_id=1, source_target_pairs={{0,1},{1,0},{2,3},{3,2},{4,5},{5,4},{6,7},{7,6},{8,9},{9,8},{10,11... | collective-permute-start | bytes 589832 | tf_op jit(solution)/shard_map/ppermute | solution.py:546
  51.9 1.2 %project.8 = (bf16[96,896]{1,0:T(8,128)(2,1)S(1)}, bf16[96,896]{1,0:T(8,128)(2,1)S(1)}) custom-call(bf16[192,1280]{1,0:T(8,128)(2,1)S(1)} %attend.10.own_ref, bf16[192,1280]{1,0:T(8,128)(2,1)S(1)} %collective-permute-done.16.other_ref, bf16[2560,896]{1,0:T(8,128)(2,1)S(1)} %get-tuple-element.81.held_ref), custom_call_target="tpu_custom_call" | custom-call | flops 1024 | bytes 1024 | tf_op jit(solution)/shard_map/project/pallas_call | solution.py:344
  53.1 0.6 collective-permute-start.21
  53.7 0.9 %project.9 = (bf16[96,768]{1,0:T(8,128)(2,1)S(1)}, bf16[96,768]{1,0:T(8,128)(2,1)S(1)}) custom-call(bf16[192,1280]{1,0:T(8,128)(2,1)S(1)} %attend.10.own_ref, bf16[192,1280]{1,0:T(8,128)(2,1)S(1)} %collective-permute-done.16.other_ref, bf16[2560,768]{1,0:T(8,128)(2,1)S(1)} %get-tuple-element.84.held_ref), custom_call_target="tpu_custom_call" | custom-call | flops 1024 | bytes 1024 | tf_op jit(solution)/shard_map/project/pallas_call | solution.py:344
  54.7 1.6 %collective-permute-start.17 = (bf16[96,768]{1,0:T(8,128)(2,1)S(1)}, bf16[96,768]{1,0:T(8,128)(2,1)S(1)}, u32[]{:S(2)}, u32[]{:S(2)}) collective-permute-start(bf16[96,768]{1,0:T(8,128)(2,1)S(1)} %get-tuple-element.86), channel_id=1, source_target_pairs={{0,1},{1,0},{2,3},{3,2},{4,5},{5,4},{6,7},{7,6},{8,9},{9,8},{10,11... | collective-permute-start | bytes 442376 | tf_op jit(solution)/shard_map/ppermute | solution.py:546
  56.2 7.8 %collective-permute-done.21.refs_7_ = bf16[96,896]{1,0:T(8,128)(2,1)S(1)} collective-permute-done((bf16[96,896]{1,0:T(8,128)(2,1)S(1)}, bf16[96,896]{1,0:T(8,128)(2,1)S(1)}, u32[]{:S(2)}, u32[]{:S(2)}) %collective-permute-start.21) | collective-permute-done | bytes 172064 | tf_op jit(solution)/shard_map/ppermute | solution.py:546
  64.1 1.1 %finish.2.refs_2_ = bf16[96,5120]{1,0:T(8,128)(2,1)} custom-call(bf16[96,1280]{1,0:T(8,128)(2,1)S(1)} %get-tuple-element.87.refs_0_, bf16[96,1152]{1,0:T(8,128)(2,1)S(1)} %get-tuple-element.88.refs_1_, bf16[96,1024]{1,0:T(8,128)(2,1)S(1)} %get-tuple-element.89.refs_2_, bf16[96,896]{1,0:T(8,128)(2,1)S(1)} %get-tuple-element.90.refs_3_, ...), custom_call_target="tpu_custom_call" | custom-call | flops 1024 | bytes 1024 | tf_op jit(solution)/shard_map/finish/pallas_call | solution.py:419
  65.2 1.6 %collective-permute-done.17.refs_1_ = bf16[96,768]{1,0:T(8,128)(2,1)S(1)} collective-permute-done((bf16[96,768]{1,0:T(8,128)(2,1)S(1)}, bf16[96,768]{1,0:T(8,128)(2,1)S(1)}, u32[]{:S(2)}, u32[]{:S(2)}) %collective-permute-start.17) | collective-permute-done | bytes 147488 | tf_op jit(solution)/shard_map/ppermute | solution.py:546
  66.8 0.7 %finish.3 = bf16[96,5120]{1,0:T(8,128)(2,1)} custom-call(bf16[96,768]{1,0:T(8,128)(2,1)S(1)} %get-tuple-element.85.refs_0_, bf16[96,768]{1,0:T(8,128)(2,1)S(1)} %collective-permute-done.17.refs_1_, bf16[96,5120]{1,0:T(8,128)(2,1)} %finish.2.refs_2_), custom_call_target="tpu_custom_call", output_to_operand_aliasing={{}: (2, {})} | custom-call | flops 1024 | bytes 1024 | tf_op jit(solution)/shard_map/finish/pallas_call | solution.py:419
  (12 shorter events, 0.0 us)
Async XLA Ops:
  1.4 5.0 %collective-permute-start = (bf16[192,1280]{1,0:T(8,128)(2,1)S(1)}, bf16[192,1280]{1,0:T(8,128)(2,1)S(1)}, u32[]{:S(2)}, u32[]{:S(2)}) collective-permute-start(bf16[192,1280]{1,0:T(8,128)(2,1)S(1)} %get-tuple-element.49), channel_id=1, source_target_pairs={{0,2},{2,0},{4,6},{6,4},{8,10},{10,8},{12,14},{14,12},{16,18},{18,... | collective-permute-start | bytes 1474568 | tf_op jit(solution)/shard_map/ppermute | solution.py:448
  2.0 5.2 %collective-permute-start.1 = (bf16[200,512]{1,0:T(8,128)(2,1)S(1)}, bf16[200,512]{1,0:T(8,128)(2,1)S(1)}, u32[]{:S(2)}, u32[]{:S(2)}) collective-permute-start(bf16[200,512]{1,0:T(8,128)(2,1)S(1)} %get-tuple-element.51), channel_id=1, source_target_pairs={{0,2},{2,0},{4,6},{6,4},{8,10},{10,8},{12,14},{14,12},{16,18},{18,... | collective-permute-start | bytes 614408 | tf_op jit(solution)/shard_map/ppermute | solution.py:447
  2.0 8.8 %collective-permute-start.2 = (bf16[200,512]{1,0:T(8,128)(2,1)S(1)}, bf16[200,512]{1,0:T(8,128)(2,1)S(1)}, u32[]{:S(2)}, u32[]{:S(2)}) collective-permute-start(bf16[200,512]{1,0:T(8,128)(2,1)S(1)} %get-tuple-element.50.refs_1_.refs_3_), channel_id=1, source_target_pairs={{0,8},{2,10},{8,16},{10,18},{16,24},{18,26},{24,28},{26,30},{28,20... | collective-permute-start | bytes 614408 | tf_op jit(solution)/shard_map/ppermute | solution.py:442
  5.0 7.2 %collective-permute-start.3 = (bf16[200,512]{1,0:T(8,128)(2,1)S(1)}, bf16[200,512]{1,0:T(8,128)(2,1)S(1)}, u32[]{:S(2)}, u32[]{:S(2)}) collective-permute-start(bf16[200,512]{1,0:T(8,128)(2,1)S(1)} %get-tuple-element.51), channel_id=1, source_target_pairs={{0,6},{2,4},{8,2},{10,0},{16,10},{18,8},{24,18},{26,16},{28,26},{3... | collective-permute-start | bytes 614408 | tf_op jit(solution)/shard_map/ppermute | solution.py:481
  5.0 11.9 %collective-permute-start.7 = (bf16[200,512]{1,0:T(8,128)(2,1)S(1)}, bf16[200,512]{1,0:T(8,128)(2,1)S(1)}, u32[]{:S(2)}, u32[]{:S(2)}) collective-permute-start(bf16[200,512]{1,0:T(8,128)(2,1)S(1)} %get-tuple-element.50.refs_1_.refs_3_), channel_id=1, source_target_pairs={{0,4},{2,6},{8,0},{10,2},{16,8},{18,10},{24,16},{26,18},{28,24},{3... | collective-permute-start | bytes 614408 | tf_op jit(solution)/shard_map/ppermute | solution.py:443
  6.4 10.5 %collective-permute-start.6 = (bf16[200,512]{1,0:T(8,128)(2,1)S(1)}, bf16[200,512]{1,0:T(8,128)(2,1)S(1)}, u32[]{:S(2)}, u32[]{:S(2)}) collective-permute-start(bf16[200,512]{1,0:T(8,128)(2,1)S(1)} %get-tuple-element.51), channel_id=1, source_target_pairs={{0,10},{2,8},{8,18},{10,16},{16,26},{18,24},{24,30},{26,28},{28,22... | collective-permute-start | bytes 614408 | tf_op jit(solution)/shard_map/ppermute | solution.py:480
  12.3 9.2 %collective-permute-start.4 = (bf16[200,512]{1,0:T(8,128)(2,1)S(1)}, bf16[200,512]{1,0:T(8,128)(2,1)S(1)}, u32[]{:S(2)}, u32[]{:S(2)}) collective-permute-start(bf16[200,512]{1,0:T(8,128)(2,1)S(1)} %collective-permute-done.2.refs_3_), channel_id=1, source_target_pairs={{0,8},{2,10},{8,16},{10,18},{16,24},{18,26},{24,28},{26,30},{28,20... | collective-permute-start | bytes 614408 | tf_op jit(solution)/shard_map/ppermute | solution.py:442
  13.9 8.0 %collective-permute-start.5 = (bf16[200,512]{1,0:T(8,128)(2,1)S(1)}, bf16[200,512]{1,0:T(8,128)(2,1)S(1)}, u32[]{:S(2)}, u32[]{:S(2)}) collective-permute-start(bf16[200,512]{1,0:T(8,128)(2,1)S(1)} %collective-permute-done.3.refs_6_), channel_id=1, source_target_pairs={{0,4},{2,6},{8,0},{10,2},{16,8},{18,10},{24,16},{26,18},{28,24},{3... | collective-permute-start | bytes 614408 | tf_op jit(solution)/shard_map/ppermute | solution.py:443
  16.9 9.3 %collective-permute-start.11 = (bf16[200,512]{1,0:T(8,128)(2,1)S(1)}, bf16[200,512]{1,0:T(8,128)(2,1)S(1)}, u32[]{:S(2)}, u32[]{:S(2)}) collective-permute-start(bf16[200,512]{1,0:T(8,128)(2,1)S(1)} %collective-permute-done.7.refs_5_), channel_id=1, source_target_pairs={{0,4},{2,6},{8,0},{10,2},{16,8},{18,10},{24,16},{26,18},{28,24},{3... | collective-permute-start | bytes 614408 | tf_op jit(solution)/shard_map/ppermute | solution.py:443
  16.9 9.4 %collective-permute-start.10 = (bf16[200,512]{1,0:T(8,128)(2,1)S(1)}, bf16[200,512]{1,0:T(8,128)(2,1)S(1)}, u32[]{:S(2)}, u32[]{:S(2)}) collective-permute-start(bf16[200,512]{1,0:T(8,128)(2,1)S(1)} %collective-permute-done.6.refs_4_), channel_id=1, source_target_pairs={{0,8},{2,10},{8,16},{10,18},{16,24},{18,26},{24,28},{26,30},{28,20... | collective-permute-start | bytes 614408 | tf_op jit(solution)/shard_map/ppermute | solution.py:442
  21.9 9.5 %collective-permute-start.8 = (bf16[200,512]{1,0:T(8,128)(2,1)S(1)}, bf16[200,512]{1,0:T(8,128)(2,1)S(1)}, u32[]{:S(2)}, u32[]{:S(2)}) collective-permute-start(bf16[200,512]{1,0:T(8,128)(2,1)S(1)} %collective-permute-done.4.refs_3_), channel_id=1, source_target_pairs={{0,8},{2,10},{8,16},{10,18},{16,24},{18,26},{24,28},{26,30},{28,20... | collective-permute-start | bytes 614408 | tf_op jit(solution)/shard_map/ppermute | solution.py:442
  23.5 8.0 %collective-permute-start.9 = (bf16[200,512]{1,0:T(8,128)(2,1)S(1)}, bf16[200,512]{1,0:T(8,128)(2,1)S(1)}, u32[]{:S(2)}, u32[]{:S(2)}) collective-permute-start(bf16[200,512]{1,0:T(8,128)(2,1)S(1)} %collective-permute-done.5.refs_6_), channel_id=1, source_target_pairs={{0,4},{2,6},{8,0},{10,2},{16,8},{18,10},{24,16},{26,18},{28,24},{3... | collective-permute-start | bytes 614408 | tf_op jit(solution)/shard_map/ppermute | solution.py:443
  26.3 8.5 %collective-permute-start.15 = (bf16[200,512]{1,0:T(8,128)(2,1)S(1)}, bf16[200,512]{1,0:T(8,128)(2,1)S(1)}, u32[]{:S(2)}, u32[]{:S(2)}) collective-permute-start(bf16[200,512]{1,0:T(8,128)(2,1)S(1)} %collective-permute-done.11.refs_5_), channel_id=1, source_target_pairs={{0,4},{2,6},{8,0},{10,2},{16,8},{18,10},{24,16},{26,18},{28,24},{3... | collective-permute-start | bytes 614408 | tf_op jit(solution)/shard_map/ppermute | solution.py:443
  26.3 8.5 %collective-permute-start.14 = (bf16[200,512]{1,0:T(8,128)(2,1)S(1)}, bf16[200,512]{1,0:T(8,128)(2,1)S(1)}, u32[]{:S(2)}, u32[]{:S(2)}) collective-permute-start(bf16[200,512]{1,0:T(8,128)(2,1)S(1)} %collective-permute-done.10.refs_4_), channel_id=1, source_target_pairs={{0,8},{2,10},{8,16},{10,18},{16,24},{18,26},{24,28},{26,30},{28,20... | collective-permute-start | bytes 614408 | tf_op jit(solution)/shard_map/ppermute | solution.py:442
  31.5 6.4 %collective-permute-start.12 = (bf16[200,512]{1,0:T(8,128)(2,1)S(1)}, bf16[200,512]{1,0:T(8,128)(2,1)S(1)}, u32[]{:S(2)}, u32[]{:S(2)}) collective-permute-start(bf16[200,512]{1,0:T(8,128)(2,1)S(1)} %collective-permute-done.8.refs_3_), channel_id=1, source_target_pairs={{0,8},{2,10},{8,16},{10,18},{16,24},{18,26},{24,28},{26,30},{28,20... | collective-permute-start | bytes 614408 | tf_op jit(solution)/shard_map/ppermute | solution.py:442
  33.1 5.8 %collective-permute-start.13 = (bf16[200,512]{1,0:T(8,128)(2,1)S(1)}, bf16[200,512]{1,0:T(8,128)(2,1)S(1)}, u32[]{:S(2)}, u32[]{:S(2)}) collective-permute-start(bf16[200,512]{1,0:T(8,128)(2,1)S(1)} %collective-permute-done.9.refs_6_), channel_id=1, source_target_pairs={{0,4},{2,6},{8,0},{10,2},{16,8},{18,10},{24,16},{26,18},{28,24},{3... | collective-permute-start | bytes 614408 | tf_op jit(solution)/shard_map/ppermute | solution.py:443
  39.9 1.9 %collective-permute-start.16 = (bf16[192,1280]{1,0:T(8,128)(2,1)S(1)}, bf16[192,1280]{1,0:T(8,128)(2,1)S(1)}, u32[]{:S(2)}, u32[]{:S(2)}) collective-permute-start(bf16[192,1280]{1,0:T(8,128)(2,1)S(1)} %attend.11), channel_id=1, source_target_pairs={{0,2},{2,0},{4,6},{6,4},{8,10},{10,8},{12,14},{14,12},{16,18},{18,... | collective-permute-start | bytes 1474568 | tf_op jit(solution)/shard_map/ppermute | solution.py:492
  42.6 21.5 %collective-permute-start.18 = (bf16[96,1280]{1,0:T(8,128)(2,1)S(1)}, bf16[96,1280]{1,0:T(8,128)(2,1)S(1)}, u32[]{:S(2)}, u32[]{:S(2)}) collective-permute-start(bf16[96,1280]{1,0:T(8,128)(2,1)S(1)} %get-tuple-element.73), channel_id=1, source_target_pairs={{0,1},{1,0},{2,3},{3,2},{4,5},{5,4},{6,7},{7,6},{8,9},{9,8},{10,11... | collective-permute-start | bytes 737288 | tf_op jit(solution)/shard_map/ppermute | solution.py:546
  47.1 17.0 %collective-permute-start.19 = (bf16[96,1152]{1,0:T(8,128)(2,1)S(1)}, bf16[96,1152]{1,0:T(8,128)(2,1)S(1)}, u32[]{:S(2)}, u32[]{:S(2)}) collective-permute-start(bf16[96,1152]{1,0:T(8,128)(2,1)S(1)} %get-tuple-element.76), channel_id=1, source_target_pairs={{0,1},{1,0},{2,3},{3,2},{4,5},{5,4},{6,7},{7,6},{8,9},{9,8},{10,11... | collective-permute-start | bytes 663560 | tf_op jit(solution)/shard_map/ppermute | solution.py:546
  50.4 13.7 %collective-permute-start.20 = (bf16[96,1024]{1,0:T(8,128)(2,1)S(1)}, bf16[96,1024]{1,0:T(8,128)(2,1)S(1)}, u32[]{:S(2)}, u32[]{:S(2)}) collective-permute-start(bf16[96,1024]{1,0:T(8,128)(2,1)S(1)} %get-tuple-element.79), channel_id=1, source_target_pairs={{0,1},{1,0},{2,3},{3,2},{4,5},{5,4},{6,7},{7,6},{8,9},{9,8},{10,11... | collective-permute-start | bytes 589832 | tf_op jit(solution)/shard_map/ppermute | solution.py:546
  53.1 10.9 %collective-permute-start.21 = (bf16[96,896]{1,0:T(8,128)(2,1)S(1)}, bf16[96,896]{1,0:T(8,128)(2,1)S(1)}, u32[]{:S(2)}, u32[]{:S(2)}) collective-permute-start(bf16[96,896]{1,0:T(8,128)(2,1)S(1)} %get-tuple-element.82), channel_id=1, source_target_pairs={{0,1},{1,0},{2,3},{3,2},{4,5},{5,4},{6,7},{7,6},{8,9},{9,8},{10,11... | collective-permute-start | bytes 516104 | tf_op jit(solution)/shard_map/ppermute | solution.py:546
  54.7 12.1 %collective-permute-start.17 = (bf16[96,768]{1,0:T(8,128)(2,1)S(1)}, bf16[96,768]{1,0:T(8,128)(2,1)S(1)}, u32[]{:S(2)}, u32[]{:S(2)}) collective-permute-start(bf16[96,768]{1,0:T(8,128)(2,1)S(1)} %get-tuple-element.86), channel_id=1, source_target_pairs={{0,1},{1,0},{2,3},{3,2},{4,5},{5,4},{6,7},{7,6},{8,9},{9,8},{10,11... | collective-permute-start | bytes 442376 | tf_op jit(solution)/shard_map/ppermute | solution.py:546

commit v15 on v14

--- a/solution.py
+++ b/solution.py
@@ -90,17 +90,16 @@
     sources = mark_refs + packets
     numbers = [
         jnp.max(
-            sources[packet][row : row + HEADER, column : column + HEAD_WIDTH].astype(jnp.float32)
+            sources[packet][row : row + HEADER].astype(jnp.float32)
         ).astype(jnp.int32)
-        for packet, row, column in plan["owner_headers"] + plan["headers"]
+        for packet, row in plan["owner_headers"] + plan["headers"]
     ]
     owner_c, member_c = numbers[:owners], numbers[owners:]
 
-    def rows_of(j, half, column):
+    def rows_of(j, half, block):
         packet, row = plan["members"][j]
-        at = row + half * chunk
-        at = at if isinstance(half, int) else pl.multiple_of(at, TILE)
-        return packets[packet][pl.ds(at, chunk), pl.ds(column, HEAD_WIDTH)]
+        at = row + (2 * block + half) * chunk
+        return packets[packet][pl.ds(at if isinstance(at, int) else pl.multiple_of(at, TILE), chunk)]
 
     def state_at(i, half, h):
         return (2 * i + half) * heads + h
@@ -113,8 +112,7 @@
 
     def one_chain(group, h, i, shared):
         first, done = group[0], group[-1] == count - 1
-        k_at = pl.multiple_of(h * HEAD_WIDTH, HEAD_WIDTH)
-        v_at = pl.multiple_of((heads + h) * HEAD_WIDTH, HEAD_WIDTH)
+        k_at, v_at = h, heads + h
         late_at, early_at = state_at(i, 1, h), state_at(i, 0, h)
         if "keys" not in shared:
             shared["keys"] = jnp.concatenate([rows_of(j, 0, k_at) for j in group], axis=0)
@@ -357,24 +355,25 @@
     chunk, q_ref, k_ref, v_ref, position_ref, sent_ref, kept_ref, *query_refs_and_scratch
 ):
     *query_refs, first_ref, sems = query_refs_and_scratch
-    rows, width = k_ref.shape[0], k_ref.shape[1] // 2
+    rows, heads = k_ref.shape[0], k_ref.shape[1] // HEAD_WIDTH // 2
     columns = query_refs[0].shape[1]
-    copies = [pltpu.make_async_copy(position_ref, first_ref, sems.at[4])]
-    for n, (ref, core) in enumerate(((sent_ref, 1 - my_core()), (kept_ref, my_core()))):
-        at = pl.ds(pl.multiple_of(core * width, width), width)
+    copies = [pltpu.make_async_copy(position_ref, first_ref, sems.at[0])]
+    for ref, core in ((sent_ref, 1 - my_core()), (kept_ref, my_core())):
         for m, source in enumerate((k_ref, v_ref)):
-            to = ref.at[pl.ds(0, rows), pl.ds(m * width, width)]
-            copies.append(pltpu.make_async_copy(source.at[:, at], to, sems.at[2 * n + m]))
-    for n, (ref, core) in enumerate(zip(query_refs, (1 - my_core(), my_core()))):
+            for h in range(heads):
+                at = pl.ds(pl.multiple_of((core * heads + h) * HEAD_WIDTH, HEAD_WIDTH), HEAD_WIDTH)
+                to = ref.at[pl.ds((m * heads + h) * rows, rows)]
+                copies.append(pltpu.make_async_copy(source.at[:, at], to, sems.at[len(copies)]))
+    for ref, core in zip(query_refs, (1 - my_core(), my_core())):
         at = pl.ds(pl.multiple_of(core * columns, columns), columns)
-        copies.append(pltpu.make_async_copy(q_ref.at[:, at], ref, sems.at[5 + n]))
+        copies.append(pltpu.make_async_copy(q_ref.at[:, at], ref, sems.at[len(copies)]))
     for copy in copies:
         copy.start()
     copies[0].wait()
     c = lax.div(first_ref[0], jnp.int32(chunk)).astype(jnp.float32)
-    header = jnp.full((HEADER, 2 * width), c, jnp.float32).astype(jnp.bfloat16)
-    sent_ref[rows:] = header
-    kept_ref[rows:] = header
+    header = jnp.full((HEADER, HEAD_WIDTH), c, jnp.float32).astype(jnp.bfloat16)
+    sent_ref[2 * heads * rows :] = header
+    kept_ref[2 * heads * rows :] = header
     for copy in copies[1:]:
         copy.wait()
 
@@ -382,17 +381,17 @@
 def prepare(queries, keys, values, positions):
     vmem = pl.BlockSpec(memory_space=pltpu.VMEM)
     hbm = pl.BlockSpec(memory_space=pltpu.HBM)
-    rows, width = keys.shape
+    rows, blocks = keys.shape[0], keys.shape[1] // HEAD_WIDTH
     operands = [pltpu.with_memory_space_constraint(x, pltpu.HBM) for x in (queries, keys, values, positions)]
     return pl.pallas_call(
         functools.partial(prepare_kernel, rows // 2),
-        out_shape=[jax.ShapeDtypeStruct((rows + HEADER, width), jnp.bfloat16)] * 2
+        out_shape=[jax.ShapeDtypeStruct((blocks * rows + HEADER, HEAD_WIDTH), jnp.bfloat16)] * 2
         + [jax.ShapeDtypeStruct((rows, queries.shape[1] // 2), jnp.bfloat16)] * 2,
         in_specs=[hbm] * 4,
         out_specs=[vmem] * 4,
         scratch_shapes=[
             pltpu.SMEM(positions.shape, jnp.int32),
-            pltpu.SemaphoreType.DMA((7,)),
+            pltpu.SemaphoreType.DMA((3 + 2 * blocks,)),
         ],
         compiler_params=pltpu.CompilerParams(vmem_limit_bytes=VMEM_LIMIT),
         name="prepare",
@@ -458,8 +457,8 @@
             own_at=lambda i: i,
             last=last,
             members=[(2 * j + i, 0) for j in each for i in range(2)],
-            headers=[(2 + 2 * j + i, rows, 0) for j in each for i in range(2)],
-            owner_headers=[(0, rows, 0), (1, rows, 0)],
+            headers=[(2 + 2 * j + i, 2 * heads * rows) for j in each for i in range(2)],
+            owner_headers=[(0, 2 * heads * rows), (1, 2 * heads * rows)],
             fetch=fetch,
             which=which,
         )
@@ -498,10 +497,10 @@
     rows, chunk = queries.shape[0], queries.shape[0] // 2
     heads = keys.shape[1] // HEAD_WIDTH
     c = (positions[:1] // chunk).astype(jnp.bfloat16).reshape(1, 1)
-    header = jnp.broadcast_to(c, (TILE, 2 * keys.shape[1]))
-    packet = jnp.concatenate([jnp.concatenate([keys, values], axis=1), header], axis=0)
+    blocks = [x[:, h * HEAD_WIDTH : (h + 1) * HEAD_WIDTH] for x in (keys, values) for h in range(heads)]
+    packet = jnp.concatenate(blocks + [jnp.broadcast_to(c, (TILE, HEAD_WIDTH))], axis=0)
     packets = lax.all_gather(packet, "blk", axis=0, tiled=True)
-    size = rows + TILE
+    size = packet.shape[0]
     here = lax.axis_index("blk")
     order = lax.rem(here + jnp.arange(count), count)
     packets = packets.reshape(count, size, -1)[order].reshape(count * size, -1)
@@ -513,8 +512,8 @@
         own_at=lambda i: 0,
         last=True,
         members=[(0, j * size) for j in range(count)],
-        headers=[(0, j * size + rows, 0) for j in range(count)],
-        owner_headers=[(0, rows, 0)],
+        headers=[(0, (j + 1) * size - TILE) for j in range(count)],
+        owner_headers=[(0, size - TILE)],
     )
     turned = turn(heads, chunk, [queries])
     return attend(plan, turned, [], [packets], None)[0]

time: 67.8 us -> 67.5 us (level)
  waiting for transfers between devices: 19.8 us -> 19.1 us
where the time goes in v15:
time: 67.5 us; the launch traced here: 67.4 us
  Pallas kernels  26.5 us (39%)
  starting transfers between devices  21.4 us (32%)
  waiting for transfers between devices  19.1 us (28%)
    pallas_call x6, Pallas kernels, attend(): pl.pallas_call(functools.partial(attend_kernel, plan), out_shape=out_shap...  13.3 us
    ppermute x6, starting transfers between devices, split_over_cores(): up = lambda x: lax.ppermute(x, 'blk', clock)  11.7 us
    ppermute x5, waiting for transfers between devices, shards(): received.append(lax.ppermute(sent, 'inner', [(0, 1), (1, 0)]))  9.38 us
    pallas_call x5, Pallas kernels, project(): pl.pallas_call(functools.partial(project_kernel, bring, begun is not None...  8.68 us
    ppermute x6, waiting for transfers between devices, split_over_cores(): down = lambda x: lax.ppermute(x, 'blk', counter)  7.26 us
    ppermute x5, starting transfers between devices, shards(): received.append(lax.ppermute(sent, 'inner', [(0, 1), (1, 0)]))  5.87 us
    ppermute x6, starting transfers between devices, split_over_cores(): down = lambda x: lax.ppermute(x, 'blk', counter)  2.79 us
    pallas_call x2, Pallas kernels, finish(): pl.pallas_call(functools.partial(finish_kernel, first, pairs), out_shape=...  1.8 us
  transfers between devices with their start and end apart: 22, of which 10 were waited for; matrix products, arithmetic and copies ran while one was open for 0% of the time, Pallas kernels for 33%

profile of v15, /device:TPU:0, one launch (start us, length us, event | category | flops | bytes accessed | tf_op | source)
XLA Modules:
  0.0 67.4 jit_solution(752551040302884668)
XLA Ops:
  0.0 1.5 %prepare.1 = (bf16[776,128]{1,0:T(8,128)(2,1)S(1)}, bf16[776,128]{1,0:T(8,128)(2,1)S(1)}, bf16[192,1280]{1,0:T(8,128)(2,1)S(1)}, bf16[192,1280]{1,0:T(8,128)(2,1)S(1)}) custom-call(bf16[192,2560]{1,0:T(8,128)(2,1)} %q_ref.1, bf16[192,512]{1,0:T(8,128)(2,1)} %k_ref.1, bf16[192,512]{1,0:T(8,128)(2,1)} %v_ref.1, s32[192]{0:T(256)} %position_ref.1), custom_call_target="tpu_custom_call" | custom-call | tf_op jit(solution)/shard_map/prepare/pallas_call | solution.py:386
  1.5 0.5 collective-permute-start
  2.0 0.1 collective-permute-start.1
  2.1 3.0 %collective-permute-start.2 = (bf16[776,128]{1,0:T(8,128)(2,1)S(1)}, bf16[776,128]{1,0:T(8,128)(2,1)S(1)}, u32[]{:S(2)}, u32[]{:S(2)}) collective-permute-start(bf16[776,128]{1,0:T(8,128)(2,1)S(1)} %get-tuple-element.50.refs_1_.refs_3_), channel_id=1, source_target_pairs={{0,8},{2,10},{8,16},{10,18},{16,24},{18,26},{24,28},{26,30},{28,20... | collective-permute-start | bytes 595976 | tf_op jit(solution)/shard_map/ppermute | solution.py:441
  5.1 0.0 collective-permute-start.3
  5.1 1.4 %collective-permute-start.7 = (bf16[776,128]{1,0:T(8,128)(2,1)S(1)}, bf16[776,128]{1,0:T(8,128)(2,1)S(1)}, u32[]{:S(2)}, u32[]{:S(2)}) collective-permute-start(bf16[776,128]{1,0:T(8,128)(2,1)S(1)} %get-tuple-element.50.refs_1_.refs_3_), channel_id=1, source_target_pairs={{0,4},{2,6},{8,0},{10,2},{16,8},{18,10},{24,16},{26,18},{28,24},{3... | collective-permute-start | bytes 595976 | tf_op jit(solution)/shard_map/ppermute | solution.py:442
  6.5 0.4 collective-permute-start.6
  6.9 0.3 turn.1.refs_0_
  7.2 2.6 %attend.6 = (f32[8,1,480]{2,1,0:T(1,128)S(1)}, f32[8,144,480]{2,1,0:T(8,128)S(1)}, bf16[2560,1024]{1,0:T(8,128)(2,1)S(1)}) custom-call(bf16[8,128,480]{2,1,0:T(8,128)(2,1)S(1)} %turn.1.refs_0_, bf16[776,128]{1,0:T(8,128)(2,1)S(1)} %get-tuple-element.50.refs_1_.refs_3_, bf16[776,128]{1,0:T(8,128)(2,1)S(1)} %collective-permute-done.1.refs_2_.refs_4_, ...), custom_call_target="tpu_custom_call" | custom-call | flops 377487360 | bytes 4194304 | tf_op jit(solution)/shard_map/attend/pallas_call | solution.py:231
  9.8 1.0 %collective-permute-done.2.refs_3_ = bf16[776,128]{1,0:T(8,128)(2,1)S(1)} collective-permute-done((bf16[776,128]{1,0:T(8,128)(2,1)S(1)}, bf16[776,128]{1,0:T(8,128)(2,1)S(1)}, u32[]{:S(2)}, u32[]{:S(2)}) %collective-permute-start.2) | collective-permute-done | bytes 198688 | tf_op jit(solution)/shard_map/ppermute | solution.py:441
  10.8 1.4 %collective-permute-done.3.refs_6_ = bf16[776,128]{1,0:T(8,128)(2,1)S(1)} collective-permute-done((bf16[776,128]{1,0:T(8,128)(2,1)S(1)}, bf16[776,128]{1,0:T(8,128)(2,1)S(1)}, u32[]{:S(2)}, u32[]{:S(2)}) %collective-permute-start.3) | collective-permute-done | bytes 198688 | tf_op jit(solution)/shard_map/ppermute | solution.py:480
  12.2 1.6 %collective-permute-start.4 = (bf16[776,128]{1,0:T(8,128)(2,1)S(1)}, bf16[776,128]{1,0:T(8,128)(2,1)S(1)}, u32[]{:S(2)}, u32[]{:S(2)}) collective-permute-start(bf16[776,128]{1,0:T(8,128)(2,1)S(1)} %collective-permute-done.2.refs_3_), channel_id=1, source_target_pairs={{0,8},{2,10},{8,16},{10,18},{16,24},{18,26},{24,28},{26,30},{28,20... | collective-permute-start | bytes 595976 | tf_op jit(solution)/shard_map/ppermute | solution.py:441
  13.8 0.4 collective-permute-start.5
  14.3 2.4 %collective-permute-done.7.refs_5_ = bf16[776,128]{1,0:T(8,128)(2,1)S(1)} collective-permute-done((bf16[776,128]{1,0:T(8,128)(2,1)S(1)}, bf16[776,128]{1,0:T(8,128)(2,1)S(1)}, u32[]{:S(2)}, u32[]{:S(2)}) %collective-permute-start.7) | collective-permute-done | bytes 198688 | tf_op jit(solution)/shard_map/ppermute | solution.py:442
  16.7 2.0 %collective-permute-start.10 = (bf16[776,128]{1,0:T(8,128)(2,1)S(1)}, bf16[776,128]{1,0:T(8,128)(2,1)S(1)}, u32[]{:S(2)}, u32[]{:S(2)}) collective-permute-start(bf16[776,128]{1,0:T(8,128)(2,1)S(1)} %collective-permute-done.6.refs_4_), channel_id=1, source_target_pairs={{0,8},{2,10},{8,16},{10,18},{16,24},{18,26},{24,28},{26,30},{28,20... | collective-permute-start | bytes 595976 | tf_op jit(solution)/shard_map/ppermute | solution.py:441
  18.7 2.6 %attend.7 = (f32[8,1,480]{2,1,0:T(1,128)S(1)}, f32[8,144,480]{2,1,0:T(8,128)S(1)}) custom-call(bf16[8,128,480]{2,1,0:T(8,128)(2,1)S(1)} %turn.1.refs_0_, bf16[776,128]{1,0:T(8,128)(2,1)S(1)} %get-tuple-element.50.refs_1_.refs_3_, bf16[776,128]{1,0:T(8,128)(2,1)S(1)} %collective-permute-done.1.refs_2_.refs_4_, ...), custom_call_target="tpu_custom_call" | custom-call | flops 754974720 | bytes 4194304 | tf_op jit(solution)/shard_map/attend/pallas_call | solution.py:231
  21.3 0.3 collective-permute-done.5.refs_6_
  21.6 1.7 %collective-permute-start.8 = (bf16[776,128]{1,0:T(8,128)(2,1)S(1)}, bf16[776,128]{1,0:T(8,128)(2,1)S(1)}, u32[]{:S(2)}, u32[]{:S(2)}) collective-permute-start(bf16[776,128]{1,0:T(8,128)(2,1)S(1)} %collective-permute-done.4.refs_3_), channel_id=1, source_target_pairs={{0,8},{2,10},{8,16},{10,18},{16,24},{18,26},{24,28},{26,30},{28,20... | collective-permute-start | bytes 595976 | tf_op jit(solution)/shard_map/ppermute | solution.py:441
  23.3 0.3 collective-permute-start.9
  23.6 1.9 %collective-permute-done.11.refs_5_ = bf16[776,128]{1,0:T(8,128)(2,1)S(1)} collective-permute-done((bf16[776,128]{1,0:T(8,128)(2,1)S(1)}, bf16[776,128]{1,0:T(8,128)(2,1)S(1)}, u32[]{:S(2)}, u32[]{:S(2)}) %collective-permute-start.11) | collective-permute-done | bytes 198688 | tf_op jit(solution)/shard_map/ppermute | solution.py:442
  25.6 0.2 collective-permute-start.15
  25.8 1.8 %collective-permute-start.14 = (bf16[776,128]{1,0:T(8,128)(2,1)S(1)}, bf16[776,128]{1,0:T(8,128)(2,1)S(1)}, u32[]{:S(2)}, u32[]{:S(2)}) collective-permute-start(bf16[776,128]{1,0:T(8,128)(2,1)S(1)} %collective-permute-done.10.refs_4_), channel_id=1, source_target_pairs={{0,8},{2,10},{8,16},{10,18},{16,24},{18,26},{24,28},{26,30},{28,20... | collective-permute-start | bytes 595976 | tf_op jit(solution)/shard_map/ppermute | solution.py:441
  27.6 3.1 %attend.8 = (f32[8,1,480]{2,1,0:T(1,128)S(1)}, f32[8,144,480]{2,1,0:T(8,128)S(1)}, bf16[2560,1280]{1,0:T(8,128)(2,1)S(1)}) custom-call(bf16[8,128,480]{2,1,0:T(8,128)(2,1)S(1)} %turn.1.refs_0_, bf16[776,128]{1,0:T(8,128)(2,1)S(1)} %get-tuple-element.50.refs_1_.refs_3_, bf16[776,128]{1,0:T(8,128)(2,1)S(1)} %collective-permute-done.1.refs_2_.refs_4_, ...), custom_call_target="tpu_custom_call" | custom-call | flops 754974720 | bytes 4194304 | tf_op jit(solution)/shard_map/attend/pallas_call | solution.py:231
  30.7 0.5 collective-permute-done.9.refs_6_
  31.2 1.6 %collective-permute-start.12 = (bf16[776,128]{1,0:T(8,128)(2,1)S(1)}, bf16[776,128]{1,0:T(8,128)(2,1)S(1)}, u32[]{:S(2)}, u32[]{:S(2)}) collective-permute-start(bf16[776,128]{1,0:T(8,128)(2,1)S(1)} %collective-permute-done.8.refs_3_), channel_id=1, source_target_pairs={{0,8},{2,10},{8,16},{10,18},{16,24},{18,26},{24,28},{26,30},{28,20... | collective-permute-start | bytes 595976 | tf_op jit(solution)/shard_map/ppermute | solution.py:441
  32.8 0.4 collective-permute-start.13
  33.2 0.6 collective-permute-done.15.refs_5_
  33.8 3.1 %attend.9 = (f32[8,1,480]{2,1,0:T(1,128)S(1)}, f32[8,144,480]{2,1,0:T(8,128)S(1)}, bf16[2560,1152]{1,0:T(8,128)(2,1)S(1)}) custom-call(bf16[8,128,480]{2,1,0:T(8,128)(2,1)S(1)} %turn.1.refs_0_, bf16[776,128]{1,0:T(8,128)(2,1)S(1)} %get-tuple-element.50.refs_1_.refs_3_, bf16[776,128]{1,0:T(8,128)(2,1)S(1)} %collective-permute-done.1.refs_2_.refs_4_, ...), custom_call_target="tpu_custom_call" | custom-call | flops 754974720 | bytes 4194304 | tf_op jit(solution)/shard_map/attend/pallas_call | solution.py:231
  37.0 1.5 %collective-permute-done.13.refs_4_ = bf16[776,128]{1,0:T(8,128)(2,1)S(1)} collective-permute-done((bf16[776,128]{1,0:T(8,128)(2,1)S(1)}, bf16[776,128]{1,0:T(8,128)(2,1)S(1)}, u32[]{:S(2)}, u32[]{:S(2)}) %collective-permute-start.13) | collective-permute-done | bytes 198688 | tf_op jit(solution)/shard_map/ppermute | solution.py:442
  38.5 1.0 %attend.11 = bf16[192,1280]{1,0:T(8,128)(2,1)S(1)} custom-call(bf16[8,128,480]{2,1,0:T(8,128)(2,1)S(1)} %turn.1.refs_0_, bf16[776,128]{1,0:T(8,128)(2,1)S(1)} %get-tuple-element.50.refs_1_.refs_3_, bf16[776,128]{1,0:T(8,128)(2,1)S(1)} %collective-permute-done.1.refs_2_.refs_4_, bf16[776,128]{1,0:T(8,128)(2,1)S(1)} %collective-permute-done.12.refs_3_, ...), custom_call_target="tpu_custom_call" | custom-call | flops 377487360 | bytes 4194304 | tf_op jit(solution)/shard_map/attend/pallas_call | solution.py:231
  39.5 0.1 collective-permute-start.16
  39.6 1.0 %attend.10.own_ref = bf16[192,1280]{1,0:T(8,128)(2,1)S(1)} custom-call(bf16[8,128,480]{2,1,0:T(8,128)(2,1)S(1)} %turn.1.refs_0_, bf16[776,128]{1,0:T(8,128)(2,1)S(1)} %get-tuple-element.50.refs_1_.refs_3_, bf16[776,128]{1,0:T(8,128)(2,1)S(1)} %collective-permute-done.1.refs_2_.refs_4_, bf16[776,128]{1,0:T(8,128)(2,1)S(1)} %collective-permute-done.12.refs_3_, ...), custom_call_target="tpu_custom_call" | custom-call | flops 377487360 | bytes 4194304 | tf_op jit(solution)/shard_map/attend/pallas_call | solution.py:231
  40.6 0.8 %begin.1.refs_0_ = f32[192,1280]{1,0:T(8,128)S(1)} custom-call(bf16[192,1280]{1,0:T(8,128)(2,1)S(1)} %attend.10.own_ref, bf16[2560,1280]{1,0:T(8,128)(2,1)S(1)} %get-tuple-element.72.held_ref), custom_call_target="tpu_custom_call" | custom-call | flops 1024 | bytes 1024 | tf_op jit(solution)/shard_map/begin/pallas_call | solution.py:290
  41.4 0.0 collective-permute-done.16.other_ref
  41.4 0.9 %project.5 = (bf16[96,1280]{1,0:T(8,128)(2,1)S(1)}, bf16[96,1280]{1,0:T(8,128)(2,1)S(1)}) custom-call(bf16[192,1280]{1,0:T(8,128)(2,1)S(1)} %attend.10.own_ref, bf16[192,1280]{1,0:T(8,128)(2,1)S(1)} %collective-permute-done.16.other_ref, bf16[2560,1280]{1,0:T(8,128)(2,1)S(1)} %get-tuple-element.72.held_ref, f32[192,1280]{1,0:T(8,128)S(1)} %begin.1.refs_0_), custom_call_target="tpu_custom_call" | custom-call | flops 1024 | bytes 1024 | tf_op jit(solution)/shard_map/project/pallas_call | solution.py:342
  42.3 1.6 %collective-permute-start.18 = (bf16[96,1280]{1,0:T(8,128)(2,1)S(1)}, bf16[96,1280]{1,0:T(8,128)(2,1)S(1)}, u32[]{:S(2)}, u32[]{:S(2)}) collective-permute-start(bf16[96,1280]{1,0:T(8,128)(2,1)S(1)} %get-tuple-element.73), channel_id=1, source_target_pairs={{0,1},{1,0},{2,3},{3,2},{4,5},{5,4},{6,7},{7,6},{8,9},{9,8},{10,11... | collective-permute-start | bytes 737288 | tf_op jit(solution)/shard_map/ppermute | solution.py:545
  43.8 2.9 %project.6 = (bf16[96,1152]{1,0:T(8,128)(2,1)S(1)}, bf16[96,1152]{1,0:T(8,128)(2,1)S(1)}, bf16[2560,896]{1,0:T(8,128)(2,1)S(1)}) custom-call(bf16[192,1280]{1,0:T(8,128)(2,1)S(1)} %attend.10.own_ref, bf16[192,1280]{1,0:T(8,128)(2,1)S(1)} %collective-permute-done.16.other_ref, bf16[2560,1152]{1,0:T(8,128)(2,1)S(1)} %get-tuple-element.75.held_ref, ...), custom_call_target="tpu_custom_call" | custom-call | flops 1024 | bytes 1024 | tf_op jit(solution)/shard_map/project/pallas_call | solution.py:342
  46.8 0.6 collective-permute-start.19
  47.4 2.8 %project.7 = (bf16[96,1024]{1,0:T(8,128)(2,1)S(1)}, bf16[96,1024]{1,0:T(8,128)(2,1)S(1)}, bf16[2560,768]{1,0:T(8,128)(2,1)S(1)}) custom-call(bf16[192,1280]{1,0:T(8,128)(2,1)S(1)} %attend.10.own_ref, bf16[192,1280]{1,0:T(8,128)(2,1)S(1)} %collective-permute-done.16.other_ref, bf16[2560,1024]{1,0:T(8,128)(2,1)S(1)} %get-tuple-element.78.held_ref, ...), custom_call_target="tpu_custom_call" | custom-call | flops 1024 | bytes 1024 | tf_op jit(solution)/shard_map/project/pallas_call | solution.py:342
  50.2 1.6 %collective-permute-start.20 = (bf16[96,1024]{1,0:T(8,128)(2,1)S(1)}, bf16[96,1024]{1,0:T(8,128)(2,1)S(1)}, u32[]{:S(2)}, u32[]{:S(2)}) collective-permute-start(bf16[96,1024]{1,0:T(8,128)(2,1)S(1)} %get-tuple-element.79), channel_id=1, source_target_pairs={{0,1},{1,0},{2,3},{3,2},{4,5},{5,4},{6,7},{7,6},{8,9},{9,8},{10,11... | collective-permute-start | bytes 589832 | tf_op jit(solution)/shard_map/ppermute | solution.py:545
  51.7 1.2 %project.8 = (bf16[96,896]{1,0:T(8,128)(2,1)S(1)}, bf16[96,896]{1,0:T(8,128)(2,1)S(1)}) custom-call(bf16[192,1280]{1,0:T(8,128)(2,1)S(1)} %attend.10.own_ref, bf16[192,1280]{1,0:T(8,128)(2,1)S(1)} %collective-permute-done.16.other_ref, bf16[2560,896]{1,0:T(8,128)(2,1)S(1)} %get-tuple-element.81.held_ref), custom_call_target="tpu_custom_call" | custom-call | flops 1024 | bytes 1024 | tf_op jit(solution)/shard_map/project/pallas_call | solution.py:342
  52.9 0.6 collective-permute-start.21
  53.5 0.9 %project.9 = (bf16[96,768]{1,0:T(8,128)(2,1)S(1)}, bf16[96,768]{1,0:T(8,128)(2,1)S(1)}) custom-call(bf16[192,1280]{1,0:T(8,128)(2,1)S(1)} %attend.10.own_ref, bf16[192,1280]{1,0:T(8,128)(2,1)S(1)} %collective-permute-done.16.other_ref, bf16[2560,768]{1,0:T(8,128)(2,1)S(1)} %get-tuple-element.84.held_ref), custom_call_target="tpu_custom_call" | custom-call | flops 1024 | bytes 1024 | tf_op jit(solution)/shard_map/project/pallas_call | solution.py:342
  54.5 1.6 %collective-permute-start.17 = (bf16[96,768]{1,0:T(8,128)(2,1)S(1)}, bf16[96,768]{1,0:T(8,128)(2,1)S(1)}, u32[]{:S(2)}, u32[]{:S(2)}) collective-permute-start(bf16[96,768]{1,0:T(8,128)(2,1)S(1)} %get-tuple-element.86), channel_id=1, source_target_pairs={{0,1},{1,0},{2,3},{3,2},{4,5},{5,4},{6,7},{7,6},{8,9},{9,8},{10,11... | collective-permute-start | bytes 442376 | tf_op jit(solution)/shard_map/ppermute | solution.py:545
  56.0 7.7 %collective-permute-done.21.refs_7_ = bf16[96,896]{1,0:T(8,128)(2,1)S(1)} collective-permute-done((bf16[96,896]{1,0:T(8,128)(2,1)S(1)}, bf16[96,896]{1,0:T(8,128)(2,1)S(1)}, u32[]{:S(2)}, u32[]{:S(2)}) %collective-permute-start.21) | collective-permute-done | bytes 172064 | tf_op jit(solution)/shard_map/ppermute | solution.py:545
  63.8 1.1 %finish.2.refs_2_ = bf16[96,5120]{1,0:T(8,128)(2,1)} custom-call(bf16[96,1280]{1,0:T(8,128)(2,1)S(1)} %get-tuple-element.87.refs_0_, bf16[96,1152]{1,0:T(8,128)(2,1)S(1)} %get-tuple-element.88.refs_1_, bf16[96,1024]{1,0:T(8,128)(2,1)S(1)} %get-tuple-element.89.refs_2_, bf16[96,896]{1,0:T(8,128)(2,1)S(1)} %get-tuple-element.90.refs_3_, ...), custom_call_target="tpu_custom_call" | custom-call | flops 1024 | bytes 1024 | tf_op jit(solution)/shard_map/finish/pallas_call | solution.py:418
  64.9 1.6 %collective-permute-done.17.refs_1_ = bf16[96,768]{1,0:T(8,128)(2,1)S(1)} collective-permute-done((bf16[96,768]{1,0:T(8,128)(2,1)S(1)}, bf16[96,768]{1,0:T(8,128)(2,1)S(1)}, u32[]{:S(2)}, u32[]{:S(2)}) %collective-permute-start.17) | collective-permute-done | bytes 147488 | tf_op jit(solution)/shard_map/ppermute | solution.py:545
  66.5 0.7 %finish.3 = bf16[96,5120]{1,0:T(8,128)(2,1)} custom-call(bf16[96,768]{1,0:T(8,128)(2,1)S(1)} %get-tuple-element.85.refs_0_, bf16[96,768]{1,0:T(8,128)(2,1)S(1)} %collective-permute-done.17.refs_1_, bf16[96,5120]{1,0:T(8,128)(2,1)} %finish.2.refs_2_), custom_call_target="tpu_custom_call", output_to_operand_aliasing={{}: (2, {})} | custom-call | flops 1024 | bytes 1024 | tf_op jit(solution)/shard_map/finish/pallas_call | solution.py:418
  (12 shorter events, 0.0 us)
Async XLA Ops:
  1.5 5.0 %collective-permute-start = (bf16[192,1280]{1,0:T(8,128)(2,1)S(1)}, bf16[192,1280]{1,0:T(8,128)(2,1)S(1)}, u32[]{:S(2)}, u32[]{:S(2)}) collective-permute-start(bf16[192,1280]{1,0:T(8,128)(2,1)S(1)} %get-tuple-element.49), channel_id=1, source_target_pairs={{0,2},{2,0},{4,6},{6,4},{8,10},{10,8},{12,14},{14,12},{16,18},{18,... | collective-permute-start | bytes 1474568 | tf_op jit(solution)/shard_map/ppermute | solution.py:447
  2.0 5.2 %collective-permute-start.1 = (bf16[776,128]{1,0:T(8,128)(2,1)S(1)}, bf16[776,128]{1,0:T(8,128)(2,1)S(1)}, u32[]{:S(2)}, u32[]{:S(2)}) collective-permute-start(bf16[776,128]{1,0:T(8,128)(2,1)S(1)} %get-tuple-element.51), channel_id=1, source_target_pairs={{0,2},{2,0},{4,6},{6,4},{8,10},{10,8},{12,14},{14,12},{16,18},{18,... | collective-permute-start | bytes 595976 | tf_op jit(solution)/shard_map/ppermute | solution.py:446
  2.1 8.7 %collective-permute-start.2 = (bf16[776,128]{1,0:T(8,128)(2,1)S(1)}, bf16[776,128]{1,0:T(8,128)(2,1)S(1)}, u32[]{:S(2)}, u32[]{:S(2)}) collective-permute-start(bf16[776,128]{1,0:T(8,128)(2,1)S(1)} %get-tuple-element.50.refs_1_.refs_3_), channel_id=1, source_target_pairs={{0,8},{2,10},{8,16},{10,18},{16,24},{18,26},{24,28},{26,30},{28,20... | collective-permute-start | bytes 595976 | tf_op jit(solution)/shard_map/ppermute | solution.py:441
  5.1 7.1 %collective-permute-start.3 = (bf16[776,128]{1,0:T(8,128)(2,1)S(1)}, bf16[776,128]{1,0:T(8,128)(2,1)S(1)}, u32[]{:S(2)}, u32[]{:S(2)}) collective-permute-start(bf16[776,128]{1,0:T(8,128)(2,1)S(1)} %get-tuple-element.51), channel_id=1, source_target_pairs={{0,6},{2,4},{8,2},{10,0},{16,10},{18,8},{24,18},{26,16},{28,26},{3... | collective-permute-start | bytes 595976 | tf_op jit(solution)/shard_map/ppermute | solution.py:480
  5.1 11.6 %collective-permute-start.7 = (bf16[776,128]{1,0:T(8,128)(2,1)S(1)}, bf16[776,128]{1,0:T(8,128)(2,1)S(1)}, u32[]{:S(2)}, u32[]{:S(2)}) collective-permute-start(bf16[776,128]{1,0:T(8,128)(2,1)S(1)} %get-tuple-element.50.refs_1_.refs_3_), channel_id=1, source_target_pairs={{0,4},{2,6},{8,0},{10,2},{16,8},{18,10},{24,16},{26,18},{28,24},{3... | collective-permute-start | bytes 595976 | tf_op jit(solution)/shard_map/ppermute | solution.py:442
  6.5 10.2 %collective-permute-start.6 = (bf16[776,128]{1,0:T(8,128)(2,1)S(1)}, bf16[776,128]{1,0:T(8,128)(2,1)S(1)}, u32[]{:S(2)}, u32[]{:S(2)}) collective-permute-start(bf16[776,128]{1,0:T(8,128)(2,1)S(1)} %get-tuple-element.51), channel_id=1, source_target_pairs={{0,10},{2,8},{8,18},{10,16},{16,26},{18,24},{24,30},{26,28},{28,22... | collective-permute-start | bytes 595976 | tf_op jit(solution)/shard_map/ppermute | solution.py:479
  12.2 9.1 %collective-permute-start.4 = (bf16[776,128]{1,0:T(8,128)(2,1)S(1)}, bf16[776,128]{1,0:T(8,128)(2,1)S(1)}, u32[]{:S(2)}, u32[]{:S(2)}) collective-permute-start(bf16[776,128]{1,0:T(8,128)(2,1)S(1)} %collective-permute-done.2.refs_3_), channel_id=1, source_target_pairs={{0,8},{2,10},{8,16},{10,18},{16,24},{18,26},{24,28},{26,30},{28,20... | collective-permute-start | bytes 595976 | tf_op jit(solution)/shard_map/ppermute | solution.py:441
  13.8 7.8 %collective-permute-start.5 = (bf16[776,128]{1,0:T(8,128)(2,1)S(1)}, bf16[776,128]{1,0:T(8,128)(2,1)S(1)}, u32[]{:S(2)}, u32[]{:S(2)}) collective-permute-start(bf16[776,128]{1,0:T(8,128)(2,1)S(1)} %collective-permute-done.3.refs_6_), channel_id=1, source_target_pairs={{0,4},{2,6},{8,0},{10,2},{16,8},{18,10},{24,16},{26,18},{28,24},{3... | collective-permute-start | bytes 595976 | tf_op jit(solution)/shard_map/ppermute | solution.py:442
  16.7 8.9 %collective-permute-start.11 = (bf16[776,128]{1,0:T(8,128)(2,1)S(1)}, bf16[776,128]{1,0:T(8,128)(2,1)S(1)}, u32[]{:S(2)}, u32[]{:S(2)}) collective-permute-start(bf16[776,128]{1,0:T(8,128)(2,1)S(1)} %collective-permute-done.7.refs_5_), channel_id=1, source_target_pairs={{0,4},{2,6},{8,0},{10,2},{16,8},{18,10},{24,16},{26,18},{28,24},{3... | collective-permute-start | bytes 595976 | tf_op jit(solution)/shard_map/ppermute | solution.py:442
  16.7 9.1 %collective-permute-start.10 = (bf16[776,128]{1,0:T(8,128)(2,1)S(1)}, bf16[776,128]{1,0:T(8,128)(2,1)S(1)}, u32[]{:S(2)}, u32[]{:S(2)}) collective-permute-start(bf16[776,128]{1,0:T(8,128)(2,1)S(1)} %collective-permute-done.6.refs_4_), channel_id=1, source_target_pairs={{0,8},{2,10},{8,16},{10,18},{16,24},{18,26},{24,28},{26,30},{28,20... | collective-permute-start | bytes 595976 | tf_op jit(solution)/shard_map/ppermute | solution.py:441
  21.6 9.1 %collective-permute-start.8 = (bf16[776,128]{1,0:T(8,128)(2,1)S(1)}, bf16[776,128]{1,0:T(8,128)(2,1)S(1)}, u32[]{:S(2)}, u32[]{:S(2)}) collective-permute-start(bf16[776,128]{1,0:T(8,128)(2,1)S(1)} %collective-permute-done.4.refs_3_), channel_id=1, source_target_pairs={{0,8},{2,10},{8,16},{10,18},{16,24},{18,26},{24,28},{26,30},{28,20... | collective-permute-start | bytes 595976 | tf_op jit(solution)/shard_map/ppermute | solution.py:441
  23.3 7.9 %collective-permute-start.9 = (bf16[776,128]{1,0:T(8,128)(2,1)S(1)}, bf16[776,128]{1,0:T(8,128)(2,1)S(1)}, u32[]{:S(2)}, u32[]{:S(2)}) collective-permute-start(bf16[776,128]{1,0:T(8,128)(2,1)S(1)} %collective-permute-done.5.refs_6_), channel_id=1, source_target_pairs={{0,4},{2,6},{8,0},{10,2},{16,8},{18,10},{24,16},{26,18},{28,24},{3... | collective-permute-start | bytes 595976 | tf_op jit(solution)/shard_map/ppermute | solution.py:442
  25.6 8.2 %collective-permute-start.15 = (bf16[776,128]{1,0:T(8,128)(2,1)S(1)}, bf16[776,128]{1,0:T(8,128)(2,1)S(1)}, u32[]{:S(2)}, u32[]{:S(2)}) collective-permute-start(bf16[776,128]{1,0:T(8,128)(2,1)S(1)} %collective-permute-done.11.refs_5_), channel_id=1, source_target_pairs={{0,4},{2,6},{8,0},{10,2},{16,8},{18,10},{24,16},{26,18},{28,24},{3... | collective-permute-start | bytes 595976 | tf_op jit(solution)/shard_map/ppermute | solution.py:442
  25.8 8.0 %collective-permute-start.14 = (bf16[776,128]{1,0:T(8,128)(2,1)S(1)}, bf16[776,128]{1,0:T(8,128)(2,1)S(1)}, u32[]{:S(2)}, u32[]{:S(2)}) collective-permute-start(bf16[776,128]{1,0:T(8,128)(2,1)S(1)} %collective-permute-done.10.refs_4_), channel_id=1, source_target_pairs={{0,8},{2,10},{8,16},{10,18},{16,24},{18,26},{24,28},{26,30},{28,20... | collective-permute-start | bytes 595976 | tf_op jit(solution)/shard_map/ppermute | solution.py:441
  31.2 5.7 %collective-permute-start.12 = (bf16[776,128]{1,0:T(8,128)(2,1)S(1)}, bf16[776,128]{1,0:T(8,128)(2,1)S(1)}, u32[]{:S(2)}, u32[]{:S(2)}) collective-permute-start(bf16[776,128]{1,0:T(8,128)(2,1)S(1)} %collective-permute-done.8.refs_3_), channel_id=1, source_target_pairs={{0,8},{2,10},{8,16},{10,18},{16,24},{18,26},{24,28},{26,30},{28,20... | collective-permute-start | bytes 595976 | tf_op jit(solution)/shard_map/ppermute | solution.py:441
  32.8 5.7 %collective-permute-start.13 = (bf16[776,128]{1,0:T(8,128)(2,1)S(1)}, bf16[776,128]{1,0:T(8,128)(2,1)S(1)}, u32[]{:S(2)}, u32[]{:S(2)}) collective-permute-start(bf16[776,128]{1,0:T(8,128)(2,1)S(1)} %collective-permute-done.9.refs_6_), channel_id=1, source_target_pairs={{0,4},{2,6},{8,0},{10,2},{16,8},{18,10},{24,16},{26,18},{28,24},{3... | collective-permute-start | bytes 595976 | tf_op jit(solution)/shard_map/ppermute | solution.py:442
  39.5 1.9 %collective-permute-start.16 = (bf16[192,1280]{1,0:T(8,128)(2,1)S(1)}, bf16[192,1280]{1,0:T(8,128)(2,1)S(1)}, u32[]{:S(2)}, u32[]{:S(2)}) collective-permute-start(bf16[192,1280]{1,0:T(8,128)(2,1)S(1)} %attend.11), channel_id=1, source_target_pairs={{0,2},{2,0},{4,6},{6,4},{8,10},{10,8},{12,14},{14,12},{16,18},{18,... | collective-permute-start | bytes 1474568 | tf_op jit(solution)/shard_map/ppermute | solution.py:491
  42.3 21.5 %collective-permute-start.18 = (bf16[96,1280]{1,0:T(8,128)(2,1)S(1)}, bf16[96,1280]{1,0:T(8,128)(2,1)S(1)}, u32[]{:S(2)}, u32[]{:S(2)}) collective-permute-start(bf16[96,1280]{1,0:T(8,128)(2,1)S(1)} %get-tuple-element.73), channel_id=1, source_target_pairs={{0,1},{1,0},{2,3},{3,2},{4,5},{5,4},{6,7},{7,6},{8,9},{9,8},{10,11... | collective-permute-start | bytes 737288 | tf_op jit(solution)/shard_map/ppermute | solution.py:545
  46.8 17.0 %collective-permute-start.19 = (bf16[96,1152]{1,0:T(8,128)(2,1)S(1)}, bf16[96,1152]{1,0:T(8,128)(2,1)S(1)}, u32[]{:S(2)}, u32[]{:S(2)}) collective-permute-start(bf16[96,1152]{1,0:T(8,128)(2,1)S(1)} %get-tuple-element.76), channel_id=1, source_target_pairs={{0,1},{1,0},{2,3},{3,2},{4,5},{5,4},{6,7},{7,6},{8,9},{9,8},{10,11... | collective-permute-start | bytes 663560 | tf_op jit(solution)/shard_map/ppermute | solution.py:545
  50.2 13.6 %collective-permute-start.20 = (bf16[96,1024]{1,0:T(8,128)(2,1)S(1)}, bf16[96,1024]{1,0:T(8,128)(2,1)S(1)}, u32[]{:S(2)}, u32[]{:S(2)}) collective-permute-start(bf16[96,1024]{1,0:T(8,128)(2,1)S(1)} %get-tuple-element.79), channel_id=1, source_target_pairs={{0,1},{1,0},{2,3},{3,2},{4,5},{5,4},{6,7},{7,6},{8,9},{9,8},{10,11... | collective-permute-start | bytes 589832 | tf_op jit(solution)/shard_map/ppermute | solution.py:545
  52.9 10.8 %collective-permute-start.21 = (bf16[96,896]{1,0:T(8,128)(2,1)S(1)}, bf16[96,896]{1,0:T(8,128)(2,1)S(1)}, u32[]{:S(2)}, u32[]{:S(2)}) collective-permute-start(bf16[96,896]{1,0:T(8,128)(2,1)S(1)} %get-tuple-element.82), channel_id=1, source_target_pairs={{0,1},{1,0},{2,3},{3,2},{4,5},{5,4},{6,7},{7,6},{8,9},{9,8},{10,11... | collective-permute-start | bytes 516104 | tf_op jit(solution)/shard_map/ppermute | solution.py:545
  54.5 12.0 %collective-permute-start.17 = (bf16[96,768]{1,0:T(8,128)(2,1)S(1)}, bf16[96,768]{1,0:T(8,128)(2,1)S(1)}, u32[]{:S(2)}, u32[]{:S(2)}) collective-permute-start(bf16[96,768]{1,0:T(8,128)(2,1)S(1)} %get-tuple-element.86), channel_id=1, source_target_pairs={{0,1},{1,0},{2,3},{3,2},{4,5},{5,4},{6,7},{7,6},{8,9},{9,8},{10,11... | collective-permute-start | bytes 442376 | tf_op jit(solution)/shard_map/ppermute | solution.py:545

commit v16 on v15

--- a/solution.py
+++ b/solution.py
@@ -269,11 +269,14 @@
     )(*queries)
 
 
-def leaving_first(ref):
+def half_of(ref, keep):
     chunk = ref.shape[0] // 2
     mine = lax.axis_index("inner").astype(jnp.int32)
-    halves = [ref[pl.ds(pl.multiple_of(half * chunk, chunk), chunk)] for half in (1 - mine, mine)]
-    return jnp.concatenate(halves, axis=0)
+    return ref[pl.ds(pl.multiple_of((mine if keep else 1 - mine) * chunk, chunk), chunk)]
+
+
+def leaving_first(ref):
+    return jnp.concatenate([half_of(ref, False), half_of(ref, True)], axis=0)
 
 
 def rows_of_core(held_ref, core):
@@ -282,65 +285,67 @@
 
 
 def begin_kernel(own_ref, held_ref, begun_ref):
-    begun_ref[...] = product(leaving_first(own_ref), rows_of_core(held_ref, my_core()))
-
-
-def begin(own, held):
+    begun_ref[...] = product(half_of(own_ref, False), rows_of_core(held_ref, my_core()))
+
+
+def first_kernel(own_ref, other_ref, held_ref, begun_ref, sent_ref):
+    total = begun_ref[...] + product(half_of(other_ref, False), rows_of_core(held_ref, 1 - my_core()))
+    sent_ref[...] = total.astype(sent_ref.dtype)
+
+
+def kept_kernel(own_ref, other_ref, held_ref, kept_ref):
+    core = my_core()
+    total = product(half_of(own_ref, True), rows_of_core(held_ref, core))
+    total = total + product(half_of(other_ref, True), rows_of_core(held_ref, 1 - core))
+    kept_ref[...] = total.astype(kept_ref.dtype)
+
+
+def part_of_first(kernel, kind, *operands):
     vmem = pl.BlockSpec(memory_space=pltpu.VMEM)
+    own, held = operands[0], operands[1 if kernel is begin_kernel else 2]
     return pl.pallas_call(
-        begin_kernel,
-        out_shape=jax.ShapeDtypeStruct((own.shape[0], held.shape[1]), jnp.float32),
-        in_specs=[vmem, vmem],
+        kernel,
+        out_shape=jax.ShapeDtypeStruct((own.shape[0] // 2, held.shape[1]), kind),
+        in_specs=[vmem] * len(operands),
         out_specs=vmem,
         cost_estimate=pl.CostEstimate(flops=1 << 10, bytes_accessed=1 << 10, transcendentals=0),
         compiler_params=pltpu.CompilerParams(vmem_limit_bytes=VMEM_LIMIT),
-        name="begin",
-    )(own, held)
-
-
-def project_kernel(bring, begun, own_ref, other_ref, held_ref, *refs):
+        name="project_first",
+    )(*operands)
+
+
+def project_kernel(bring, own_ref, other_ref, held_ref, *refs):
     refs, copies = list(refs), []
     if bring:
         w_ref, sems = refs.pop(0), refs.pop()
-    if begun:
-        begun_ref = refs.pop(0)
     sent_ref, kept_ref = refs.pop(0), refs.pop(0)
     for n, (first, _) in enumerate(bring):
         copies += fetch_columns(w_ref, first, refs.pop(0), sems, n * PIECES)
-    chunk, core = sent_ref.shape[0], my_core()
-    other = leaving_first(other_ref)
-    if begun:
-        total = begun_ref[...] + product(other, rows_of_core(held_ref, 1 - core))
-    else:
-        (rows_ref,) = refs
-        own, part = leaving_first(own_ref), own_ref.shape[1]
-        rows_ref[:, :part] = jnp.where(core == 0, own, other)
-        rows_ref[:, part:] = jnp.where(core == 0, other, own)
-        total = product(rows_ref[...], held_ref[...])
-    both = total.astype(sent_ref.dtype)
+    (rows_ref,) = refs
+    own, other = leaving_first(own_ref), leaving_first(other_ref)
+    chunk, part, left = sent_ref.shape[0], own_ref.shape[1], my_core() == 0
+    rows_ref[:, :part] = jnp.where(left, own, other)
+    rows_ref[:, part:] = jnp.where(left, other, own)
+    both = product(rows_ref[...], held_ref[...]).astype(sent_ref.dtype)
     sent_ref[...] = both[:chunk]
     kept_ref[...] = both[chunk:]
     for copy in copies:
         copy.wait()
 
 
-def project(own, other, held, out_weight, bring, begun=None):
+def project(own, other, held, out_weight, bring):
     rows, (depth, width) = own.shape[0], held.shape
     vmem = pl.BlockSpec(memory_space=pltpu.VMEM)
     out_shape = [jax.ShapeDtypeStruct((rows // 2, width), jnp.bfloat16)] * 2
     out_shape += [jax.ShapeDtypeStruct((depth, columns), held.dtype) for _, columns in bring]
-    in_specs, operands, scratch = [vmem] * 3, [own, other, held], []
-    if begun is None:
-        scratch.append(pltpu.VMEM((rows, depth), jnp.bfloat16))
+    in_specs, operands = [vmem] * 3, [own, other, held]
+    scratch = [pltpu.VMEM((rows, depth), jnp.bfloat16)]
     if bring:
         in_specs.append(pl.BlockSpec(memory_space=pltpu.HBM))
         operands.append(out_weight)
         scratch.append(pltpu.SemaphoreType.DMA((PIECES * len(bring),)))
-    if begun is not None:
-        in_specs.append(vmem)
-        operands.append(begun)
     return pl.pallas_call(
-        functools.partial(project_kernel, bring, begun is not None),
+        functools.partial(project_kernel, bring),
         out_shape=out_shape,
         in_specs=in_specs,
         out_specs=[vmem] * len(out_shape),
@@ -535,15 +540,18 @@
         count, queries, keys, values, positions, out_weight, cuts[:3]
     )
     bring = [cuts[j + 2 : j + 3] if j > 0 else [] for j in range(len(cuts))]
-    received, kept = [], []
+    begun = part_of_first(begin_kernel, jnp.float32, own, held[0])
+    sent = part_of_first(first_kernel, jnp.bfloat16, own, other, held[0], begun)
+    received, kept = [], [None]
     for j in range(len(cuts)):
-        source = own if j == 0 else after(own, sent)
-        begun = begin(own, held[0]) if j == 0 else None
-        sent, keep, *rest = project(source, other, held[j], out_weight, bring[j], begun)
-        if rest:
-            held[len(held)] = rest[0]
+        if j > 0:
+            source = after(own, sent)
+            sent, keep, *rest = project(source, other, held[j], out_weight, bring[j])
+            kept.append(keep)
+            if rest:
+                held[len(held)] = rest[0]
         received.append(lax.ppermute(sent, "inner", [(0, 1), (1, 0)]))
-        kept.append(keep)
+    kept[0] = part_of_first(kept_kernel, jnp.bfloat16, after(own, sent), other, held[0])
     columns = out_weight.shape[1]
     result = finish(kept[:-1], received[:-1], 0, columns)
     return finish(kept[-1:], received[-1:], cuts[-1][0], columns, result)

time: 67.5 us -> 67.2 us (level)
  waiting for transfers between devices: 19.1 us -> 18 us
  Pallas kernels: 26.5 us -> 27.3 us
    ppermute x5, waiting for transfers between devices: 9.38 us -> 8.12 us  [shards(): received.append(lax.ppermute(sent, 'inner', [(0, 1), (1, 0)]))]
    pallas_call x6 -> x7, Pallas kernels: 9.51 us -> 10.3 us  [the longest x4 7.77 us: project(): pl.pallas_call(functools.partial(project_kernel, bring), out_shape=out_sh...]
  transfers between devices with their start and end apart: 22 -> 22, of which waited for: 10 -> 11; matrix products, arithmetic and copies ran while one was open for 0% -> 0% of each run, Pallas kernels for 33% -> 35%
where the time goes in v16:
time: 67.2 us; the launch traced here: 67.1 us
  Pallas kernels  27.3 us (41%)
  starting transfers between devices  21.4 us (32%)
  waiting for transfers between devices  18 us (27%)
    pallas_call x6, Pallas kernels, attend(): pl.pallas_call(functools.partial(attend_kernel, plan), out_shape=out_shap...  13.3 us
    ppermute x6, starting transfers between devices, split_over_cores(): up = lambda x: lax.ppermute(x, 'blk', clock)  11.7 us
    ppermute x5, waiting for transfers between devices, shards(): received.append(lax.ppermute(sent, 'inner', [(0, 1), (1, 0)]))  8.12 us
    pallas_call x4, Pallas kernels, project(): pl.pallas_call(functools.partial(project_kernel, bring), out_shape=out_sh...  7.77 us
    ppermute x6, waiting for transfers between devices, split_over_cores(): down = lambda x: lax.ppermute(x, 'blk', counter)  7.27 us
    ppermute x5, starting transfers between devices, shards(): received.append(lax.ppermute(sent, 'inner', [(0, 1), (1, 0)]))  5.88 us
    ppermute x6, starting transfers between devices, split_over_cores(): down = lambda x: lax.ppermute(x, 'blk', counter)  2.78 us
    pallas_call x3, Pallas kernels, part_of_first(): pl.pallas_call(kernel, out_shape=jax.ShapeDtypeStruct((own.shape[0] // 2,...  2.53 us
  transfers between devices with their start and end apart: 22, of which 11 were waited for; matrix products, arithmetic and copies ran while one was open for 0% of the time, Pallas kernels for 35%

profile of v16, /device:TPU:0, one launch (start us, length us, event | category | flops | bytes accessed | tf_op | source)
XLA Modules:
  0.0 67.1 jit_solution(12838293081292102122)
XLA Ops:
  0.0 1.5 %prepare.1 = (bf16[776,128]{1,0:T(8,128)(2,1)S(1)}, bf16[776,128]{1,0:T(8,128)(2,1)S(1)}, bf16[192,1280]{1,0:T(8,128)(2,1)S(1)}, bf16[192,1280]{1,0:T(8,128)(2,1)S(1)}) custom-call(bf16[192,2560]{1,0:T(8,128)(2,1)} %q_ref.1, bf16[192,512]{1,0:T(8,128)(2,1)} %k_ref.1, bf16[192,512]{1,0:T(8,128)(2,1)} %v_ref.1, s32[192]{0:T(256)} %position_ref.1), custom_call_target="tpu_custom_call" | custom-call | tf_op jit(solution)/shard_map/prepare/pallas_call | solution.py:391
  1.5 0.5 collective-permute-start
  2.0 0.1 collective-permute-start.1
  2.1 3.0 %collective-permute-start.2 = (bf16[776,128]{1,0:T(8,128)(2,1)S(1)}, bf16[776,128]{1,0:T(8,128)(2,1)S(1)}, u32[]{:S(2)}, u32[]{:S(2)}) collective-permute-start(bf16[776,128]{1,0:T(8,128)(2,1)S(1)} %get-tuple-element.49.refs_1_.refs_3_), channel_id=1, source_target_pairs={{0,8},{2,10},{8,16},{10,18},{16,24},{18,26},{24,28},{26,30},{28,20... | collective-permute-start | bytes 595976 | tf_op jit(solution)/shard_map/ppermute | solution.py:446
  5.1 1.4 %collective-permute-start.7 = (bf16[776,128]{1,0:T(8,128)(2,1)S(1)}, bf16[776,128]{1,0:T(8,128)(2,1)S(1)}, u32[]{:S(2)}, u32[]{:S(2)}) collective-permute-start(bf16[776,128]{1,0:T(8,128)(2,1)S(1)} %get-tuple-element.49.refs_1_.refs_3_), channel_id=1, source_target_pairs={{0,4},{2,6},{8,0},{10,2},{16,8},{18,10},{24,16},{26,18},{28,24},{3... | collective-permute-start | bytes 595976 | tf_op jit(solution)/shard_map/ppermute | solution.py:447
  6.5 0.4 collective-permute-start.6
  6.9 0.3 turn.1.refs_0_
  7.2 2.6 %attend.6 = (f32[8,1,480]{2,1,0:T(1,128)S(1)}, f32[8,144,480]{2,1,0:T(8,128)S(1)}, bf16[2560,1024]{1,0:T(8,128)(2,1)S(1)}) custom-call(bf16[8,128,480]{2,1,0:T(8,128)(2,1)S(1)} %turn.1.refs_0_, bf16[776,128]{1,0:T(8,128)(2,1)S(1)} %get-tuple-element.49.refs_1_.refs_3_, bf16[776,128]{1,0:T(8,128)(2,1)S(1)} %collective-permute-done.1.refs_2_.refs_4_, ...), custom_call_target="tpu_custom_call" | custom-call | flops 377487360 | bytes 4194304 | tf_op jit(solution)/shard_map/attend/pallas_call | solution.py:231
  9.8 1.0 %collective-permute-done.2.refs_3_ = bf16[776,128]{1,0:T(8,128)(2,1)S(1)} collective-permute-done((bf16[776,128]{1,0:T(8,128)(2,1)S(1)}, bf16[776,128]{1,0:T(8,128)(2,1)S(1)}, u32[]{:S(2)}, u32[]{:S(2)}) %collective-permute-start.2) | collective-permute-done | bytes 198688 | tf_op jit(solution)/shard_map/ppermute | solution.py:446
  10.8 1.4 %collective-permute-done.3.refs_6_ = bf16[776,128]{1,0:T(8,128)(2,1)S(1)} collective-permute-done((bf16[776,128]{1,0:T(8,128)(2,1)S(1)}, bf16[776,128]{1,0:T(8,128)(2,1)S(1)}, u32[]{:S(2)}, u32[]{:S(2)}) %collective-permute-start.3) | collective-permute-done | bytes 198688 | tf_op jit(solution)/shard_map/ppermute | solution.py:485
  12.2 1.6 %collective-permute-start.4 = (bf16[776,128]{1,0:T(8,128)(2,1)S(1)}, bf16[776,128]{1,0:T(8,128)(2,1)S(1)}, u32[]{:S(2)}, u32[]{:S(2)}) collective-permute-start(bf16[776,128]{1,0:T(8,128)(2,1)S(1)} %collective-permute-done.2.refs_3_), channel_id=1, source_target_pairs={{0,8},{2,10},{8,16},{10,18},{16,24},{18,26},{24,28},{26,30},{28,20... | collective-permute-start | bytes 595976 | tf_op jit(solution)/shard_map/ppermute | solution.py:446
  13.8 0.4 collective-permute-start.5
  14.3 2.4 %collective-permute-done.7.refs_5_ = bf16[776,128]{1,0:T(8,128)(2,1)S(1)} collective-permute-done((bf16[776,128]{1,0:T(8,128)(2,1)S(1)}, bf16[776,128]{1,0:T(8,128)(2,1)S(1)}, u32[]{:S(2)}, u32[]{:S(2)}) %collective-permute-start.7) | collective-permute-done | bytes 198688 | tf_op jit(solution)/shard_map/ppermute | solution.py:447
  16.7 2.0 %collective-permute-start.10 = (bf16[776,128]{1,0:T(8,128)(2,1)S(1)}, bf16[776,128]{1,0:T(8,128)(2,1)S(1)}, u32[]{:S(2)}, u32[]{:S(2)}) collective-permute-start(bf16[776,128]{1,0:T(8,128)(2,1)S(1)} %collective-permute-done.6.refs_4_), channel_id=1, source_target_pairs={{0,8},{2,10},{8,16},{10,18},{16,24},{18,26},{24,28},{26,30},{28,20... | collective-permute-start | bytes 595976 | tf_op jit(solution)/shard_map/ppermute | solution.py:446
  18.7 2.6 %attend.7 = (f32[8,1,480]{2,1,0:T(1,128)S(1)}, f32[8,144,480]{2,1,0:T(8,128)S(1)}) custom-call(bf16[8,128,480]{2,1,0:T(8,128)(2,1)S(1)} %turn.1.refs_0_, bf16[776,128]{1,0:T(8,128)(2,1)S(1)} %get-tuple-element.49.refs_1_.refs_3_, bf16[776,128]{1,0:T(8,128)(2,1)S(1)} %collective-permute-done.1.refs_2_.refs_4_, ...), custom_call_target="tpu_custom_call" | custom-call | flops 754974720 | bytes 4194304 | tf_op jit(solution)/shard_map/attend/pallas_call | solution.py:231
  21.3 0.3 collective-permute-done.5.refs_6_
  21.6 1.7 %collective-permute-start.8 = (bf16[776,128]{1,0:T(8,128)(2,1)S(1)}, bf16[776,128]{1,0:T(8,128)(2,1)S(1)}, u32[]{:S(2)}, u32[]{:S(2)}) collective-permute-start(bf16[776,128]{1,0:T(8,128)(2,1)S(1)} %collective-permute-done.4.refs_3_), channel_id=1, source_target_pairs={{0,8},{2,10},{8,16},{10,18},{16,24},{18,26},{24,28},{26,30},{28,20... | collective-permute-start | bytes 595976 | tf_op jit(solution)/shard_map/ppermute | solution.py:446
  23.3 0.3 collective-permute-start.9
  23.6 1.9 %collective-permute-done.11.refs_5_ = bf16[776,128]{1,0:T(8,128)(2,1)S(1)} collective-permute-done((bf16[776,128]{1,0:T(8,128)(2,1)S(1)}, bf16[776,128]{1,0:T(8,128)(2,1)S(1)}, u32[]{:S(2)}, u32[]{:S(2)}) %collective-permute-start.11) | collective-permute-done | bytes 198688 | tf_op jit(solution)/shard_map/ppermute | solution.py:447
  25.6 0.2 collective-permute-start.15
  25.8 1.8 %collective-permute-start.14 = (bf16[776,128]{1,0:T(8,128)(2,1)S(1)}, bf16[776,128]{1,0:T(8,128)(2,1)S(1)}, u32[]{:S(2)}, u32[]{:S(2)}) collective-permute-start(bf16[776,128]{1,0:T(8,128)(2,1)S(1)} %collective-permute-done.10.refs_4_), channel_id=1, source_target_pairs={{0,8},{2,10},{8,16},{10,18},{16,24},{18,26},{24,28},{26,30},{28,20... | collective-permute-start | bytes 595976 | tf_op jit(solution)/shard_map/ppermute | solution.py:446
  27.6 3.1 %attend.8 = (f32[8,1,480]{2,1,0:T(1,128)S(1)}, f32[8,144,480]{2,1,0:T(8,128)S(1)}, bf16[2560,1280]{1,0:T(8,128)(2,1)S(1)}) custom-call(bf16[8,128,480]{2,1,0:T(8,128)(2,1)S(1)} %turn.1.refs_0_, bf16[776,128]{1,0:T(8,128)(2,1)S(1)} %get-tuple-element.49.refs_1_.refs_3_, bf16[776,128]{1,0:T(8,128)(2,1)S(1)} %collective-permute-done.1.refs_2_.refs_4_, ...), custom_call_target="tpu_custom_call" | custom-call | flops 754974720 | bytes 4194304 | tf_op jit(solution)/shard_map/attend/pallas_call | solution.py:231
  30.7 0.5 collective-permute-done.9.refs_6_
  31.2 1.6 %collective-permute-start.12 = (bf16[776,128]{1,0:T(8,128)(2,1)S(1)}, bf16[776,128]{1,0:T(8,128)(2,1)S(1)}, u32[]{:S(2)}, u32[]{:S(2)}) collective-permute-start(bf16[776,128]{1,0:T(8,128)(2,1)S(1)} %collective-permute-done.8.refs_3_), channel_id=1, source_target_pairs={{0,8},{2,10},{8,16},{10,18},{16,24},{18,26},{24,28},{26,30},{28,20... | collective-permute-start | bytes 595976 | tf_op jit(solution)/shard_map/ppermute | solution.py:446
  32.8 0.4 collective-permute-start.13
  33.2 0.6 collective-permute-done.15.refs_5_
  33.9 3.1 %attend.9 = (f32[8,1,480]{2,1,0:T(1,128)S(1)}, f32[8,144,480]{2,1,0:T(8,128)S(1)}, bf16[2560,1152]{1,0:T(8,128)(2,1)S(1)}) custom-call(bf16[8,128,480]{2,1,0:T(8,128)(2,1)S(1)} %turn.1.refs_0_, bf16[776,128]{1,0:T(8,128)(2,1)S(1)} %get-tuple-element.49.refs_1_.refs_3_, bf16[776,128]{1,0:T(8,128)(2,1)S(1)} %collective-permute-done.1.refs_2_.refs_4_, ...), custom_call_target="tpu_custom_call" | custom-call | flops 754974720 | bytes 4194304 | tf_op jit(solution)/shard_map/attend/pallas_call | solution.py:231
  37.0 1.5 %collective-permute-done.13.refs_4_ = bf16[776,128]{1,0:T(8,128)(2,1)S(1)} collective-permute-done((bf16[776,128]{1,0:T(8,128)(2,1)S(1)}, bf16[776,128]{1,0:T(8,128)(2,1)S(1)}, u32[]{:S(2)}, u32[]{:S(2)}) %collective-permute-start.13) | collective-permute-done | bytes 198688 | tf_op jit(solution)/shard_map/ppermute | solution.py:447
  38.5 1.0 %attend.11 = bf16[192,1280]{1,0:T(8,128)(2,1)S(1)} custom-call(bf16[8,128,480]{2,1,0:T(8,128)(2,1)S(1)} %turn.1.refs_0_, bf16[776,128]{1,0:T(8,128)(2,1)S(1)} %get-tuple-element.49.refs_1_.refs_3_, bf16[776,128]{1,0:T(8,128)(2,1)S(1)} %collective-permute-done.1.refs_2_.refs_4_, bf16[776,128]{1,0:T(8,128)(2,1)S(1)} %collective-permute-done.12.refs_3_, ...), custom_call_target="tpu_custom_call" | custom-call | flops 377487360 | bytes 4194304 | tf_op jit(solution)/shard_map/attend/pallas_call | solution.py:231
  39.5 0.1 collective-permute-start.16
  39.6 1.0 %attend.10.own_ref = bf16[192,1280]{1,0:T(8,128)(2,1)S(1)} custom-call(bf16[8,128,480]{2,1,0:T(8,128)(2,1)S(1)} %turn.1.refs_0_, bf16[776,128]{1,0:T(8,128)(2,1)S(1)} %get-tuple-element.49.refs_1_.refs_3_, bf16[776,128]{1,0:T(8,128)(2,1)S(1)} %collective-permute-done.1.refs_2_.refs_4_, bf16[776,128]{1,0:T(8,128)(2,1)S(1)} %collective-permute-done.12.refs_3_, ...), custom_call_target="tpu_custom_call" | custom-call | flops 377487360 | bytes 4194304 | tf_op jit(solution)/shard_map/attend/pallas_call | solution.py:231
  40.6 0.7 %project_first.3.begun_ref = f32[96,1280]{1,0:T(8,128)S(1)} custom-call(bf16[192,1280]{1,0:T(8,128)(2,1)S(1)} %attend.10.own_ref, bf16[2560,1280]{1,0:T(8,128)(2,1)S(1)} %get-tuple-element.71.held_ref), custom_call_target="tpu_custom_call" | custom-call | flops 1024 | bytes 1024 | tf_op jit(solution)/shard_map/project_first/pallas_call | solution.py:306
  41.3 0.2 collective-permute-done.16.other_ref
  41.4 0.7 %project_first.4 = bf16[96,1280]{1,0:T(8,128)(2,1)S(1)} custom-call(bf16[192,1280]{1,0:T(8,128)(2,1)S(1)} %attend.10.own_ref, bf16[192,1280]{1,0:T(8,128)(2,1)S(1)} %collective-permute-done.16.other_ref, bf16[2560,1280]{1,0:T(8,128)(2,1)S(1)} %get-tuple-element.71.held_ref, f32[96,1280]{1,0:T(8,128)S(1)} %project_first.3.begun_ref), custom_call_target="tpu_custom_call" | custom-call | flops 1024 | bytes 1024 | tf_op jit(solution)/shard_map/project_first/pallas_call | solution.py:306
  42.1 1.6 %collective-permute-start.18 = (bf16[96,1280]{1,0:T(8,128)(2,1)S(1)}, bf16[96,1280]{1,0:T(8,128)(2,1)S(1)}, u32[]{:S(2)}, u32[]{:S(2)}) collective-permute-start(bf16[96,1280]{1,0:T(8,128)(2,1)S(1)} %project_first.4), channel_id=1, source_target_pairs={{0,1},{1,0},{2,3},{3,2},{4,5},{5,4},{6,7},{7,6},{8,9},{9,8},{10,11... | collective-permute-start | bytes 737288 | tf_op jit(solution)/shard_map/ppermute | solution.py:553
  43.7 2.9 %project.4 = (bf16[96,1152]{1,0:T(8,128)(2,1)S(1)}, bf16[96,1152]{1,0:T(8,128)(2,1)S(1)}, bf16[2560,896]{1,0:T(8,128)(2,1)S(1)}) custom-call(bf16[192,1280]{1,0:T(8,128)(2,1)S(1)} %attend.10.own_ref, bf16[192,1280]{1,0:T(8,128)(2,1)S(1)} %collective-permute-done.16.other_ref, bf16[2560,1152]{1,0:T(8,128)(2,1)S(1)} %get-tuple-element.73.held_ref, ...), custom_call_target="tpu_custom_call" | custom-call | flops 1024 | bytes 1024 | tf_op jit(solution)/shard_map/project/pallas_call | solution.py:347
  46.6 0.6 collective-permute-start.19
  47.2 2.7 %project.5 = (bf16[96,1024]{1,0:T(8,128)(2,1)S(1)}, bf16[96,1024]{1,0:T(8,128)(2,1)S(1)}, bf16[2560,768]{1,0:T(8,128)(2,1)S(1)}) custom-call(bf16[192,1280]{1,0:T(8,128)(2,1)S(1)} %attend.10.own_ref, bf16[192,1280]{1,0:T(8,128)(2,1)S(1)} %collective-permute-done.16.other_ref, bf16[2560,1024]{1,0:T(8,128)(2,1)S(1)} %get-tuple-element.76.held_ref, ...), custom_call_target="tpu_custom_call" | custom-call | flops 1024 | bytes 1024 | tf_op jit(solution)/shard_map/project/pallas_call | solution.py:347
  49.9 1.6 %collective-permute-start.20 = (bf16[96,1024]{1,0:T(8,128)(2,1)S(1)}, bf16[96,1024]{1,0:T(8,128)(2,1)S(1)}, u32[]{:S(2)}, u32[]{:S(2)}) collective-permute-start(bf16[96,1024]{1,0:T(8,128)(2,1)S(1)} %get-tuple-element.77), channel_id=1, source_target_pairs={{0,1},{1,0},{2,3},{3,2},{4,5},{5,4},{6,7},{7,6},{8,9},{9,8},{10,11... | collective-permute-start | bytes 589832 | tf_op jit(solution)/shard_map/ppermute | solution.py:553
  51.5 1.2 %project.6 = (bf16[96,896]{1,0:T(8,128)(2,1)S(1)}, bf16[96,896]{1,0:T(8,128)(2,1)S(1)}) custom-call(bf16[192,1280]{1,0:T(8,128)(2,1)S(1)} %attend.10.own_ref, bf16[192,1280]{1,0:T(8,128)(2,1)S(1)} %collective-permute-done.16.other_ref, bf16[2560,896]{1,0:T(8,128)(2,1)S(1)} %get-tuple-element.79.held_ref), custom_call_target="tpu_custom_call" | custom-call | flops 1024 | bytes 1024 | tf_op jit(solution)/shard_map/project/pallas_call | solution.py:347
  52.7 0.6 collective-permute-start.21
  53.3 0.9 %project.7 = (bf16[96,768]{1,0:T(8,128)(2,1)S(1)}, bf16[96,768]{1,0:T(8,128)(2,1)S(1)}) custom-call(bf16[192,1280]{1,0:T(8,128)(2,1)S(1)} %attend.10.own_ref, bf16[192,1280]{1,0:T(8,128)(2,1)S(1)} %collective-permute-done.16.other_ref, bf16[2560,768]{1,0:T(8,128)(2,1)S(1)} %get-tuple-element.82.held_ref), custom_call_target="tpu_custom_call" | custom-call | flops 1024 | bytes 1024 | tf_op jit(solution)/shard_map/project/pallas_call | solution.py:347
  54.2 1.5 %collective-permute-start.17 = (bf16[96,768]{1,0:T(8,128)(2,1)S(1)}, bf16[96,768]{1,0:T(8,128)(2,1)S(1)}, u32[]{:S(2)}, u32[]{:S(2)}) collective-permute-start(bf16[96,768]{1,0:T(8,128)(2,1)S(1)} %get-tuple-element.84), channel_id=1, source_target_pairs={{0,1},{1,0},{2,3},{3,2},{4,5},{5,4},{6,7},{7,6},{8,9},{9,8},{10,11... | collective-permute-start | bytes 442376 | tf_op jit(solution)/shard_map/ppermute | solution.py:553
  55.8 1.2 %project_first.5.refs_0_ = bf16[96,1280]{1,0:T(8,128)(2,1)S(1)} custom-call(bf16[192,1280]{1,0:T(8,128)(2,1)S(1)} %attend.10.own_ref, bf16[192,1280]{1,0:T(8,128)(2,1)S(1)} %collective-permute-done.16.other_ref, bf16[2560,1280]{1,0:T(8,128)(2,1)S(1)} %get-tuple-element.71.held_ref), custom_call_target="tpu_custom_call" | custom-call | flops 1024 | bytes 1024 | tf_op jit(solution)/shard_map/project_first/pallas_call | solution.py:306
  57.0 6.6 %collective-permute-done.21.refs_7_ = bf16[96,896]{1,0:T(8,128)(2,1)S(1)} collective-permute-done((bf16[96,896]{1,0:T(8,128)(2,1)S(1)}, bf16[96,896]{1,0:T(8,128)(2,1)S(1)}, u32[]{:S(2)}, u32[]{:S(2)}) %collective-permute-start.21) | collective-permute-done | bytes 172064 | tf_op jit(solution)/shard_map/ppermute | solution.py:553
  63.6 1.1 %finish.2.refs_2_ = bf16[96,5120]{1,0:T(8,128)(2,1)} custom-call(bf16[96,1280]{1,0:T(8,128)(2,1)S(1)} %project_first.5.refs_0_, bf16[96,1152]{1,0:T(8,128)(2,1)S(1)} %get-tuple-element.86.refs_1_, bf16[96,1024]{1,0:T(8,128)(2,1)S(1)} %get-tuple-element.87.refs_2_, bf16[96,896]{1,0:T(8,128)(2,1)S(1)} %get-tuple-element.88.refs_3_, ...), custom_call_target="tpu_custom_call" | custom-call | flops 1024 | bytes 1024 | tf_op jit(solution)/shard_map/finish/pallas_call | solution.py:423
  64.7 1.5 %collective-permute-done.17.refs_1_ = bf16[96,768]{1,0:T(8,128)(2,1)S(1)} collective-permute-done((bf16[96,768]{1,0:T(8,128)(2,1)S(1)}, bf16[96,768]{1,0:T(8,128)(2,1)S(1)}, u32[]{:S(2)}, u32[]{:S(2)}) %collective-permute-start.17) | collective-permute-done | bytes 147488 | tf_op jit(solution)/shard_map/ppermute | solution.py:553
  66.2 0.7 %finish.3 = bf16[96,5120]{1,0:T(8,128)(2,1)} custom-call(bf16[96,768]{1,0:T(8,128)(2,1)S(1)} %get-tuple-element.83.refs_0_, bf16[96,768]{1,0:T(8,128)(2,1)S(1)} %collective-permute-done.17.refs_1_, bf16[96,5120]{1,0:T(8,128)(2,1)} %finish.2.refs_2_), custom_call_target="tpu_custom_call", output_to_operand_aliasing={{}: (2, {})} | custom-call | flops 1024 | bytes 1024 | tf_op jit(solution)/shard_map/finish/pallas_call | solution.py:423
  (13 shorter events, 0.0 us)
Async XLA Ops:
  1.5 5.0 %collective-permute-start = (bf16[192,1280]{1,0:T(8,128)(2,1)S(1)}, bf16[192,1280]{1,0:T(8,128)(2,1)S(1)}, u32[]{:S(2)}, u32[]{:S(2)}) collective-permute-start(bf16[192,1280]{1,0:T(8,128)(2,1)S(1)} %get-tuple-element.48), channel_id=1, source_target_pairs={{0,2},{2,0},{4,6},{6,4},{8,10},{10,8},{12,14},{14,12},{16,18},{18,... | collective-permute-start | bytes 1474568 | tf_op jit(solution)/shard_map/ppermute | solution.py:452
  2.0 5.2 %collective-permute-start.1 = (bf16[776,128]{1,0:T(8,128)(2,1)S(1)}, bf16[776,128]{1,0:T(8,128)(2,1)S(1)}, u32[]{:S(2)}, u32[]{:S(2)}) collective-permute-start(bf16[776,128]{1,0:T(8,128)(2,1)S(1)} %get-tuple-element.50), channel_id=1, source_target_pairs={{0,2},{2,0},{4,6},{6,4},{8,10},{10,8},{12,14},{14,12},{16,18},{18,... | collective-permute-start | bytes 595976 | tf_op jit(solution)/shard_map/ppermute | solution.py:451
  2.1 8.7 %collective-permute-start.2 = (bf16[776,128]{1,0:T(8,128)(2,1)S(1)}, bf16[776,128]{1,0:T(8,128)(2,1)S(1)}, u32[]{:S(2)}, u32[]{:S(2)}) collective-permute-start(bf16[776,128]{1,0:T(8,128)(2,1)S(1)} %get-tuple-element.49.refs_1_.refs_3_), channel_id=1, source_target_pairs={{0,8},{2,10},{8,16},{10,18},{16,24},{18,26},{24,28},{26,30},{28,20... | collective-permute-start | bytes 595976 | tf_op jit(solution)/shard_map/ppermute | solution.py:446
  5.1 7.1 %collective-permute-start.3 = (bf16[776,128]{1,0:T(8,128)(2,1)S(1)}, bf16[776,128]{1,0:T(8,128)(2,1)S(1)}, u32[]{:S(2)}, u32[]{:S(2)}) collective-permute-start(bf16[776,128]{1,0:T(8,128)(2,1)S(1)} %get-tuple-element.50), channel_id=1, source_target_pairs={{0,6},{2,4},{8,2},{10,0},{16,10},{18,8},{24,18},{26,16},{28,26},{3... | collective-permute-start | bytes 595976 | tf_op jit(solution)/shard_map/ppermute | solution.py:485
  5.1 11.6 %collective-permute-start.7 = (bf16[776,128]{1,0:T(8,128)(2,1)S(1)}, bf16[776,128]{1,0:T(8,128)(2,1)S(1)}, u32[]{:S(2)}, u32[]{:S(2)}) collective-permute-start(bf16[776,128]{1,0:T(8,128)(2,1)S(1)} %get-tuple-element.49.refs_1_.refs_3_), channel_id=1, source_target_pairs={{0,4},{2,6},{8,0},{10,2},{16,8},{18,10},{24,16},{26,18},{28,24},{3... | collective-permute-start | bytes 595976 | tf_op jit(solution)/shard_map/ppermute | solution.py:447
  6.5 10.2 %collective-permute-start.6 = (bf16[776,128]{1,0:T(8,128)(2,1)S(1)}, bf16[776,128]{1,0:T(8,128)(2,1)S(1)}, u32[]{:S(2)}, u32[]{:S(2)}) collective-permute-start(bf16[776,128]{1,0:T(8,128)(2,1)S(1)} %get-tuple-element.50), channel_id=1, source_target_pairs={{0,10},{2,8},{8,18},{10,16},{16,26},{18,24},{24,30},{26,28},{28,22... | collective-permute-start | bytes 595976 | tf_op jit(solution)/shard_map/ppermute | solution.py:484
  12.2 9.0 %collective-permute-start.4 = (bf16[776,128]{1,0:T(8,128)(2,1)S(1)}, bf16[776,128]{1,0:T(8,128)(2,1)S(1)}, u32[]{:S(2)}, u32[]{:S(2)}) collective-permute-start(bf16[776,128]{1,0:T(8,128)(2,1)S(1)} %collective-permute-done.2.refs_3_), channel_id=1, source_target_pairs={{0,8},{2,10},{8,16},{10,18},{16,24},{18,26},{24,28},{26,30},{28,20... | collective-permute-start | bytes 595976 | tf_op jit(solution)/shard_map/ppermute | solution.py:446
  13.8 7.8 %collective-permute-start.5 = (bf16[776,128]{1,0:T(8,128)(2,1)S(1)}, bf16[776,128]{1,0:T(8,128)(2,1)S(1)}, u32[]{:S(2)}, u32[]{:S(2)}) collective-permute-start(bf16[776,128]{1,0:T(8,128)(2,1)S(1)} %collective-permute-done.3.refs_6_), channel_id=1, source_target_pairs={{0,4},{2,6},{8,0},{10,2},{16,8},{18,10},{24,16},{26,18},{28,24},{3... | collective-permute-start | bytes 595976 | tf_op jit(solution)/shard_map/ppermute | solution.py:447
  16.7 8.9 %collective-permute-start.11 = (bf16[776,128]{1,0:T(8,128)(2,1)S(1)}, bf16[776,128]{1,0:T(8,128)(2,1)S(1)}, u32[]{:S(2)}, u32[]{:S(2)}) collective-permute-start(bf16[776,128]{1,0:T(8,128)(2,1)S(1)} %collective-permute-done.7.refs_5_), channel_id=1, source_target_pairs={{0,4},{2,6},{8,0},{10,2},{16,8},{18,10},{24,16},{26,18},{28,24},{3... | collective-permute-start | bytes 595976 | tf_op jit(solution)/shard_map/ppermute | solution.py:447
  16.7 9.1 %collective-permute-start.10 = (bf16[776,128]{1,0:T(8,128)(2,1)S(1)}, bf16[776,128]{1,0:T(8,128)(2,1)S(1)}, u32[]{:S(2)}, u32[]{:S(2)}) collective-permute-start(bf16[776,128]{1,0:T(8,128)(2,1)S(1)} %collective-permute-done.6.refs_4_), channel_id=1, source_target_pairs={{0,8},{2,10},{8,16},{10,18},{16,24},{18,26},{24,28},{26,30},{28,20... | collective-permute-start | bytes 595976 | tf_op jit(solution)/shard_map/ppermute | solution.py:446
  21.6 9.1 %collective-permute-start.8 = (bf16[776,128]{1,0:T(8,128)(2,1)S(1)}, bf16[776,128]{1,0:T(8,128)(2,1)S(1)}, u32[]{:S(2)}, u32[]{:S(2)}) collective-permute-start(bf16[776,128]{1,0:T(8,128)(2,1)S(1)} %collective-permute-done.4.refs_3_), channel_id=1, source_target_pairs={{0,8},{2,10},{8,16},{10,18},{16,24},{18,26},{24,28},{26,30},{28,20... | collective-permute-start | bytes 595976 | tf_op jit(solution)/shard_map/ppermute | solution.py:446
  23.3 7.9 %collective-permute-start.9 = (bf16[776,128]{1,0:T(8,128)(2,1)S(1)}, bf16[776,128]{1,0:T(8,128)(2,1)S(1)}, u32[]{:S(2)}, u32[]{:S(2)}) collective-permute-start(bf16[776,128]{1,0:T(8,128)(2,1)S(1)} %collective-permute-done.5.refs_6_), channel_id=1, source_target_pairs={{0,4},{2,6},{8,0},{10,2},{16,8},{18,10},{24,16},{26,18},{28,24},{3... | collective-permute-start | bytes 595976 | tf_op jit(solution)/shard_map/ppermute | solution.py:447
  25.6 8.3 %collective-permute-start.15 = (bf16[776,128]{1,0:T(8,128)(2,1)S(1)}, bf16[776,128]{1,0:T(8,128)(2,1)S(1)}, u32[]{:S(2)}, u32[]{:S(2)}) collective-permute-start(bf16[776,128]{1,0:T(8,128)(2,1)S(1)} %collective-permute-done.11.refs_5_), channel_id=1, source_target_pairs={{0,4},{2,6},{8,0},{10,2},{16,8},{18,10},{24,16},{26,18},{28,24},{3... | collective-permute-start | bytes 595976 | tf_op jit(solution)/shard_map/ppermute | solution.py:447
  25.8 8.1 %collective-permute-start.14 = (bf16[776,128]{1,0:T(8,128)(2,1)S(1)}, bf16[776,128]{1,0:T(8,128)(2,1)S(1)}, u32[]{:S(2)}, u32[]{:S(2)}) collective-permute-start(bf16[776,128]{1,0:T(8,128)(2,1)S(1)} %collective-permute-done.10.refs_4_), channel_id=1, source_target_pairs={{0,8},{2,10},{8,16},{10,18},{16,24},{18,26},{24,28},{26,30},{28,20... | collective-permute-start | bytes 595976 | tf_op jit(solution)/shard_map/ppermute | solution.py:446
  31.2 5.8 %collective-permute-start.12 = (bf16[776,128]{1,0:T(8,128)(2,1)S(1)}, bf16[776,128]{1,0:T(8,128)(2,1)S(1)}, u32[]{:S(2)}, u32[]{:S(2)}) collective-permute-start(bf16[776,128]{1,0:T(8,128)(2,1)S(1)} %collective-permute-done.8.refs_3_), channel_id=1, source_target_pairs={{0,8},{2,10},{8,16},{10,18},{16,24},{18,26},{24,28},{26,30},{28,20... | collective-permute-start | bytes 595976 | tf_op jit(solution)/shard_map/ppermute | solution.py:446
  32.8 5.7 %collective-permute-start.13 = (bf16[776,128]{1,0:T(8,128)(2,1)S(1)}, bf16[776,128]{1,0:T(8,128)(2,1)S(1)}, u32[]{:S(2)}, u32[]{:S(2)}) collective-permute-start(bf16[776,128]{1,0:T(8,128)(2,1)S(1)} %collective-permute-done.9.refs_6_), channel_id=1, source_target_pairs={{0,4},{2,6},{8,0},{10,2},{16,8},{18,10},{24,16},{26,18},{28,24},{3... | collective-permute-start | bytes 595976 | tf_op jit(solution)/shard_map/ppermute | solution.py:447
  39.5 1.9 %collective-permute-start.16 = (bf16[192,1280]{1,0:T(8,128)(2,1)S(1)}, bf16[192,1280]{1,0:T(8,128)(2,1)S(1)}, u32[]{:S(2)}, u32[]{:S(2)}) collective-permute-start(bf16[192,1280]{1,0:T(8,128)(2,1)S(1)} %attend.11), channel_id=1, source_target_pairs={{0,2},{2,0},{4,6},{6,4},{8,10},{10,8},{12,14},{14,12},{16,18},{18,... | collective-permute-start | bytes 1474568 | tf_op jit(solution)/shard_map/ppermute | solution.py:496
  42.1 21.5 %collective-permute-start.18 = (bf16[96,1280]{1,0:T(8,128)(2,1)S(1)}, bf16[96,1280]{1,0:T(8,128)(2,1)S(1)}, u32[]{:S(2)}, u32[]{:S(2)}) collective-permute-start(bf16[96,1280]{1,0:T(8,128)(2,1)S(1)} %project_first.4), channel_id=1, source_target_pairs={{0,1},{1,0},{2,3},{3,2},{4,5},{5,4},{6,7},{7,6},{8,9},{9,8},{10,11... | collective-permute-start | bytes 737288 | tf_op jit(solution)/shard_map/ppermute | solution.py:553
  46.6 17.0 %collective-permute-start.19 = (bf16[96,1152]{1,0:T(8,128)(2,1)S(1)}, bf16[96,1152]{1,0:T(8,128)(2,1)S(1)}, u32[]{:S(2)}, u32[]{:S(2)}) collective-permute-start(bf16[96,1152]{1,0:T(8,128)(2,1)S(1)} %get-tuple-element.74), channel_id=1, source_target_pairs={{0,1},{1,0},{2,3},{3,2},{4,5},{5,4},{6,7},{7,6},{8,9},{9,8},{10,11... | collective-permute-start | bytes 663560 | tf_op jit(solution)/shard_map/ppermute | solution.py:553
  49.9 13.7 %collective-permute-start.20 = (bf16[96,1024]{1,0:T(8,128)(2,1)S(1)}, bf16[96,1024]{1,0:T(8,128)(2,1)S(1)}, u32[]{:S(2)}, u32[]{:S(2)}) collective-permute-start(bf16[96,1024]{1,0:T(8,128)(2,1)S(1)} %get-tuple-element.77), channel_id=1, source_target_pairs={{0,1},{1,0},{2,3},{3,2},{4,5},{5,4},{6,7},{7,6},{8,9},{9,8},{10,11... | collective-permute-start | bytes 589832 | tf_op jit(solution)/shard_map/ppermute | solution.py:553
  52.7 10.9 %collective-permute-start.21 = (bf16[96,896]{1,0:T(8,128)(2,1)S(1)}, bf16[96,896]{1,0:T(8,128)(2,1)S(1)}, u32[]{:S(2)}, u32[]{:S(2)}) collective-permute-start(bf16[96,896]{1,0:T(8,128)(2,1)S(1)} %get-tuple-element.80), channel_id=1, source_target_pairs={{0,1},{1,0},{2,3},{3,2},{4,5},{5,4},{6,7},{7,6},{8,9},{9,8},{10,11... | collective-permute-start | bytes 516104 | tf_op jit(solution)/shard_map/ppermute | solution.py:553
  54.2 12.0 %collective-permute-start.17 = (bf16[96,768]{1,0:T(8,128)(2,1)S(1)}, bf16[96,768]{1,0:T(8,128)(2,1)S(1)}, u32[]{:S(2)}, u32[]{:S(2)}) collective-permute-start(bf16[96,768]{1,0:T(8,128)(2,1)S(1)} %get-tuple-element.84), channel_id=1, source_target_pairs={{0,1},{1,0},{2,3},{3,2},{4,5},{5,4},{6,7},{7,6},{8,9},{9,8},{10,11... | collective-permute-start | bytes 442376 | tf_op jit(solution)/shard_map/ppermute | solution.py:553

commit v17 on v16

--- a/solution.py
+++ b/solution.py
@@ -85,7 +85,8 @@
         for n, (first, _) in enumerate(fetch):
             held_ref = refs.pop(0 if plan["last"] else 2)
             copies += fetch_columns(w_ref, first, held_ref, sems, n * PIECES)
-    high_ref, sums_ref = refs
+    if plan["part"] is None:
+        high_ref, sums_ref = refs
 
     sources = mark_refs + packets
     numbers = [
@@ -166,14 +167,47 @@
             if plan["last"] and done:
                 mixed = sums[:HEAD_WIDTH] * (1.0 / sums[HEAD_WIDTH : HEAD_WIDTH + 1])
                 mixed = jnp.transpose(mixed.astype(out_refs[i].dtype))
+                place = side
+                if plan["sent_first"]:
+                    place = (lax.axis_index("inner") == side).astype(jnp.int32)
+                rows_at = pl.ds(pl.multiple_of(place * chunk, TILE), chunk)
                 for g in range(QUERY_PER_KEY):
                     to = pl.multiple_of(h * GROUP + g * HEAD_WIDTH, HEAD_WIDTH)
-                    out_refs[i][side * chunk : (side + 1) * chunk, pl.ds(to, HEAD_WIDTH)] = mixed[
-                        g * chunk : (g + 1) * chunk
-                    ]
+                    out_refs[i][rows_at, pl.ds(to, HEAD_WIDTH)] = mixed[g * chunk : (g + 1) * chunk]
             else:
                 high_ref[at] = highs[side]
                 sums_ref[at] = sums
+        yield
+
+    def one_side(h, i, side):
+        at = state_at(i, side, h)
+        visible = [member_c[j] > owner_c[i] if side else member_c[j] < owner_c[i] for j in range(count)]
+        halves = ([(j, 0) for j in range(count)] if side else []) + [(j, side) for j in range(count)]
+        k = jnp.concatenate([rows_of(j, half, h) for j, half in halves], axis=0)
+        values = turned_values([rows_of(j, half, heads + h) for j, half in halves])
+        s = product(k, q_ref[at])
+        whole = (len(halves) - count) * chunk
+        blocks = [s[whole + j * chunk : whole + (j + 1) * chunk] for j in range(count)]
+        tops = [in_high[at]]
+        if side:
+            tops.append(jnp.max(s[:whole], axis=0, keepdims=True))
+        for block, seen in zip(blocks, visible):
+            tops.append(jnp.where(seen, jnp.max(block, axis=0, keepdims=True), MASKED))
+        high = functools.reduce(jnp.maximum, tops)
+        yield
+        weights = [weigh(s[:whole], high)] if side else []
+        for block, seen in zip(blocks, visible):
+            w = weigh(block, high)
+            weights.append(jnp.where(seen, w, jnp.zeros_like(w)))
+        weights = jnp.concatenate(weights, axis=0)
+        yield
+        shrink = jnp.exp2((in_high[at] - high) * EXP2_SCALE)
+        sums = product(values, weights) + in_sums[at] * shrink
+        mixed = sums[:HEAD_WIDTH] * (1.0 / sums[HEAD_WIDTH : HEAD_WIDTH + 1])
+        mixed = jnp.transpose(mixed.astype(out_refs[i].dtype))
+        for g in range(QUERY_PER_KEY):
+            to = h * GROUP + g * HEAD_WIDTH
+            out_refs[i][:, to : to + HEAD_WIDTH] = mixed[g * chunk : (g + 1) * chunk]
         yield
 
     def staggered(chains):
@@ -181,6 +215,16 @@
             for stage in (2, 1, 0):
                 if 0 <= t - stage < len(chains):
                     next(chains[t - stage])
+
+    if plan["part"] is not None:
+        mine = lax.axis_index("inner").astype(jnp.int32)
+        for side in range(2):
+
+            @pl.when((mine == side) == (plan["part"] == "kept"))
+            def _(side=side):
+                staggered([one_side(h, i, side) for h in range(heads) for i in plan["which"]])
+
+        return
 
     for first in range(0, count, 6):
         group = range(first, min(first + 6, count))
@@ -211,17 +255,22 @@
     plan = dict(plan, marks=len(marks), packets=len(packets), carried=state is not None)
     fetch = plan.setdefault("fetch", None)
     which = plan.setdefault("which", range(owners))
+    part = plan.setdefault("part", None)
+    plan.setdefault("sent_first", False)
     rows = QUERY_PER_KEY * chunk
     slots = owners * 2 * heads
     vmem = pl.BlockSpec(memory_space=pltpu.VMEM)
     kept = [(slots, 1, rows), (slots, HEAD_WIDTH + TILE, rows)]
     if plan["last"]:
-        out_shape = [jax.ShapeDtypeStruct((2 * chunk, heads * GROUP), jnp.bfloat16)] * len(which)
+        shape = ((2 if part is None else 1) * chunk, heads * GROUP)
+        out_shape = [jax.ShapeDtypeStruct(shape, jnp.bfloat16)] * len(which)
     else:
         out_shape = [jax.ShapeDtypeStruct(shape, jnp.float32) for shape in kept]
     operands = 1 + len(marks) + len(packets) + (0 if state is None else 2)
     in_specs = [vmem] * operands
-    scratch = [pltpu.VMEM(shape, jnp.float32) for shape in kept] if plan["last"] else []
+    scratch = []
+    if plan["last"] and part is None:
+        scratch = [pltpu.VMEM(shape, jnp.float32) for shape in kept]
     if fetch:
         in_specs.append(pl.BlockSpec(memory_space=pltpu.HBM))
         for _, columns in fetch:
@@ -269,63 +318,39 @@
     )(*queries)
 
 
-def half_of(ref, keep):
-    chunk = ref.shape[0] // 2
-    mine = lax.axis_index("inner").astype(jnp.int32)
-    return ref[pl.ds(pl.multiple_of((mine if keep else 1 - mine) * chunk, chunk), chunk)]
-
-
-def leaving_first(ref):
-    return jnp.concatenate([half_of(ref, False), half_of(ref, True)], axis=0)
-
-
 def rows_of_core(held_ref, core):
     depth = held_ref.shape[0] // 2
     return held_ref[pl.ds(pl.multiple_of(core * depth, depth), depth)]
 
 
+def join_heads(own_ref, other_ref, rows_ref):
+    part, left = own_ref.shape[1], my_core() == 0
+    rows_ref[:, :part] = jnp.where(left, own_ref[...], other_ref[...])
+    rows_ref[:, part:] = jnp.where(left, other_ref[...], own_ref[...])
+
+
 def begin_kernel(own_ref, held_ref, begun_ref):
-    begun_ref[...] = product(half_of(own_ref, False), rows_of_core(held_ref, my_core()))
-
-
-def first_kernel(own_ref, other_ref, held_ref, begun_ref, sent_ref):
-    total = begun_ref[...] + product(half_of(other_ref, False), rows_of_core(held_ref, 1 - my_core()))
+    begun_ref[...] = product(own_ref[...], rows_of_core(held_ref, my_core()))
+
+
+def first_kernel(other_ref, held_ref, begun_ref, sent_ref):
+    total = begun_ref[...] + product(other_ref[...], rows_of_core(held_ref, 1 - my_core()))
     sent_ref[...] = total.astype(sent_ref.dtype)
 
 
-def kept_kernel(own_ref, other_ref, held_ref, kept_ref):
-    core = my_core()
-    total = product(half_of(own_ref, True), rows_of_core(held_ref, core))
-    total = total + product(half_of(other_ref, True), rows_of_core(held_ref, 1 - core))
-    kept_ref[...] = total.astype(kept_ref.dtype)
-
-
-def part_of_first(kernel, kind, *operands):
-    vmem = pl.BlockSpec(memory_space=pltpu.VMEM)
-    own, held = operands[0], operands[1 if kernel is begin_kernel else 2]
-    return pl.pallas_call(
-        kernel,
-        out_shape=jax.ShapeDtypeStruct((own.shape[0] // 2, held.shape[1]), kind),
-        in_specs=[vmem] * len(operands),
-        out_specs=vmem,
-        cost_estimate=pl.CostEstimate(flops=1 << 10, bytes_accessed=1 << 10, transcendentals=0),
-        compiler_params=pltpu.CompilerParams(vmem_limit_bytes=VMEM_LIMIT),
-        name="project_first",
-    )(*operands)
-
-
-def project_kernel(bring, own_ref, other_ref, held_ref, *refs):
+def project_kernel(bring, *refs):
     refs, copies = list(refs), []
+    sent_rows, kept_rows, held_ref = refs[:2], refs[2:4], refs[4]
+    refs = refs[5:]
     if bring:
         w_ref, sems = refs.pop(0), refs.pop()
     sent_ref, kept_ref = refs.pop(0), refs.pop(0)
     for n, (first, _) in enumerate(bring):
         copies += fetch_columns(w_ref, first, refs.pop(0), sems, n * PIECES)
     (rows_ref,) = refs
-    own, other = leaving_first(own_ref), leaving_first(other_ref)
-    chunk, part, left = sent_ref.shape[0], own_ref.shape[1], my_core() == 0
-    rows_ref[:, :part] = jnp.where(left, own, other)
-    rows_ref[:, part:] = jnp.where(left, other, own)
+    chunk = sent_ref.shape[0]
+    join_heads(*sent_rows, rows_ref.at[:chunk])
+    join_heads(*kept_rows, rows_ref.at[chunk:])
     both = product(rows_ref[...], held_ref[...]).astype(sent_ref.dtype)
     sent_ref[...] = both[:chunk]
     kept_ref[...] = both[chunk:]
@@ -333,27 +358,24 @@
         copy.wait()
 
 
-def project(own, other, held, out_weight, bring):
-    rows, (depth, width) = own.shape[0], held.shape
+def keep_kernel(own_ref, other_ref, held_ref, kept_ref, rows_ref):
+    join_heads(own_ref, other_ref, rows_ref)
+    kept_ref[...] = product(rows_ref[...], held_ref[...]).astype(kept_ref.dtype)
+
+
+def multiply(kernel, operands, outputs, scratch=(), weight=None):
     vmem = pl.BlockSpec(memory_space=pltpu.VMEM)
-    out_shape = [jax.ShapeDtypeStruct((rows // 2, width), jnp.bfloat16)] * 2
-    out_shape += [jax.ShapeDtypeStruct((depth, columns), held.dtype) for _, columns in bring]
-    in_specs, operands = [vmem] * 3, [own, other, held]
-    scratch = [pltpu.VMEM((rows, depth), jnp.bfloat16)]
-    if bring:
-        in_specs.append(pl.BlockSpec(memory_space=pltpu.HBM))
-        operands.append(out_weight)
-        scratch.append(pltpu.SemaphoreType.DMA((PIECES * len(bring),)))
+    more = [] if weight is None else [weight]
     return pl.pallas_call(
-        functools.partial(project_kernel, bring),
-        out_shape=out_shape,
-        in_specs=in_specs,
-        out_specs=[vmem] * len(out_shape),
-        scratch_shapes=scratch,
+        kernel,
+        out_shape=[jax.ShapeDtypeStruct(shape, kind) for shape, kind in outputs],
+        in_specs=[vmem] * len(operands) + [pl.BlockSpec(memory_space=pltpu.HBM)] * len(more),
+        out_specs=[vmem] * len(outputs),
+        scratch_shapes=list(scratch),
         cost_estimate=pl.CostEstimate(flops=1 << 10, bytes_accessed=1 << 10, transcendentals=0),
         compiler_params=pltpu.CompilerParams(vmem_limit_bytes=VMEM_LIMIT),
-        name="project",
-    )(*operands)
+        name="multiply",
+    )(*operands, *more)
 
 
 def prepare_kernel(
@@ -434,7 +456,7 @@
 
 
 def after(value, *events):
-    return lax.optimization_barrier((value, *events))[0]
+    return lax.optimization_barrier((value, events))[0]
 
 
 def split_over_cores(count, queries, keys, values, positions, out_weight, fetch):
@@ -452,7 +474,7 @@
     q_got = lax.ppermute(q_sent, "blk", sibling)
     turned = turn(heads, chunk, [q_own, q_got])
 
-    def call(pairs, state, own=False, last=False, fetch=None, which=(0, 1)):
+    def call(pairs, state, own=False, last=False, fetch=None, which=(0, 1), part=None):
         each = range(len(pairs))
         plan = dict(
             heads=heads,
@@ -466,6 +488,8 @@
             owner_headers=[(0, 2 * heads * rows), (1, 2 * heads * rows)],
             fetch=fetch,
             which=which,
+            part=part,
+            sent_first=True,
         )
         packets = [packet for pair in pairs for packet in pair]
         return attend(plan, turned, [x, y], packets, state, out_weight)
@@ -493,9 +517,13 @@
     far = (up(up_first), down(down_first))
     state = bring_with((1,), arrived, state)
     (theirs,) = call([far], state, last=True, which=(1,))
-    other = lax.ppermute(theirs, "blk", sibling)
-    (own,) = call([far], state, last=True, which=(0,))
-    return own, other, held
+    other = [lax.ppermute(rows, "blk", sibling) for rows in (theirs[:chunk], theirs[chunk:])]
+    (own,) = call([far], state, last=True, which=(0,), part="sent")
+
+    def own_to_keep(event):
+        return call([far], after(state, event), last=True, which=(0,), part="kept")[0]
+
+    return own, other, held, own_to_keep
 
 
 def one_head_a_device(count, queries, keys, values, positions):
@@ -536,22 +564,35 @@
     shares = (10, 9, 8, 7, 6)
     widths = [out_weight.shape[1] * share // sum(shares) for share in shares]
     cuts = [(sum(widths[:j]), columns) for j, columns in enumerate(widths)]
-    own, other, held = split_over_cores(
+    own, (other, other_kept), held, own_to_keep = split_over_cores(
         count, queries, keys, values, positions, out_weight, cuts[:3]
     )
-    bring = [cuts[j + 2 : j + 3] if j > 0 else [] for j in range(len(cuts))]
-    begun = part_of_first(begin_kernel, jnp.float32, own, held[0])
-    sent = part_of_first(first_kernel, jnp.bfloat16, own, other, held[0], begun)
+    chunk, depth, kind = own.shape[0], out_weight.shape[0], own.dtype
+    (begun,) = multiply(begin_kernel, [own, held[0]], [((chunk, widths[0]), jnp.float32)])
+    (sent,) = multiply(first_kernel, [other, held[0], begun], [((chunk, widths[0]), kind)])
+    own_kept = own_to_keep(sent)
     received, kept = [], [None]
     for j in range(len(cuts)):
         if j > 0:
-            source = after(own, sent)
-            sent, keep, *rest = project(source, other, held[j], out_weight, bring[j])
+            bring = cuts[j + 2 : j + 3]
+            results = multiply(
+                functools.partial(project_kernel, bring),
+                [after(own, sent), other, own_kept, other_kept, held[j]],
+                [((chunk, widths[j]), kind)] * 2 + [((depth, columns), kind) for _, columns in bring],
+                [pltpu.VMEM((2 * chunk, depth), kind)] + [pltpu.SemaphoreType.DMA((PIECES,))] * len(bring),
+                out_weight if bring else None,
+            )
+            sent, keep = results[:2]
             kept.append(keep)
-            if rest:
-                held[len(held)] = rest[0]
+            if bring:
+                held[j + 2] = results[2]
         received.append(lax.ppermute(sent, "inner", [(0, 1), (1, 0)]))
-    kept[0] = part_of_first(kept_kernel, jnp.bfloat16, after(own, sent), other, held[0])
+    (kept[0],) = multiply(
+        keep_kernel,
+        [after(own_kept, sent), other_kept, held[0]],
+        [((chunk, widths[0]), kind)],
+        [pltpu.VMEM((chunk, depth), kind)],
+    )
     columns = out_weight.shape[1]
     result = finish(kept[:-1], received[:-1], 0, columns)
     return finish(kept[-1:], received[-1:], cuts[-1][0], columns, result)

time: 67.2 us -> 67.4 us (level)
  waiting for transfers between devices: 18 us -> 17.1 us
  Pallas kernels: 27.3 us -> 28.1 us
    pallas_call x6 -> x7, Pallas kernels: 13.3 us -> 14.3 us  [attend(): pl.pallas_call(functools.partial(attend_kernel, plan), out_shape=out_shap...]
    ppermute x5, waiting for transfers between devices: 8.12 us -> 7.29 us  [shards(): received.append(lax.ppermute(sent, 'inner', [(0, 1), (1, 0)]))]
  transfers between devices with their start and end apart: 22 -> 23, of which waited for: 11 -> 10; matrix products, arithmetic and copies ran while one was open for 0% -> 0% of each run, Pallas kernels for 35% -> 37%
where the time goes in v17:
time: 67.4 us; the launch traced here: 67.2 us
  Pallas kernels  28.1 us (42%)
  starting transfers between devices  21.7 us (32%)
  waiting for transfers between devices  17.1 us (25%)
    pallas_call x7, Pallas kernels, attend(): pl.pallas_call(functools.partial(attend_kernel, plan), out_shape=out_shap...  14.3 us
    ppermute x6, starting transfers between devices, split_over_cores(): up = lambda x: lax.ppermute(x, 'blk', clock)  11.8 us
    pallas_call x7, Pallas kernels, multiply(): pl.pallas_call(kernel, out_shape=[jax.ShapeDtypeStruct(shape, kind) for s...  10.2 us
    ppermute x5, waiting for transfers between devices, shards(): received.append(lax.ppermute(sent, 'inner', [(0, 1), (1, 0)]))  7.29 us
    ppermute x6, waiting for transfers between devices, split_over_cores(): down = lambda x: lax.ppermute(x, 'blk', counter)  7.28 us
    ppermute x5, starting transfers between devices, shards(): received.append(lax.ppermute(sent, 'inner', [(0, 1), (1, 0)]))  5.6 us
    ppermute x6, starting transfers between devices, split_over_cores(): down = lambda x: lax.ppermute(x, 'blk', counter)  2.76 us
    pallas_call x2, Pallas kernels, finish(): pl.pallas_call(functools.partial(finish_kernel, first, pairs), out_shape=...  1.8 us
  transfers between devices with their start and end apart: 23, of which 10 were waited for; matrix products, arithmetic and copies ran while one was open for 0% of the time, Pallas kernels for 37%

profile of v17, /device:TPU:0, one launch (start us, length us, event | category | flops | bytes accessed | tf_op | source)
XLA Modules:
  0.0 67.2 jit_solution(9671114175572867491)
XLA Ops:
  0.0 1.5 %prepare.1 = (bf16[776,128]{1,0:T(8,128)(2,1)S(1)}, bf16[776,128]{1,0:T(8,128)(2,1)S(1)}, bf16[192,1280]{1,0:T(8,128)(2,1)S(1)}, bf16[192,1280]{1,0:T(8,128)(2,1)S(1)}) custom-call(bf16[192,2560]{1,0:T(8,128)(2,1)} %q_ref.1, bf16[192,512]{1,0:T(8,128)(2,1)} %k_ref.1, bf16[192,512]{1,0:T(8,128)(2,1)} %v_ref.1, s32[192]{0:T(256)} %position_ref.1), custom_call_target="tpu_custom_call" | custom-call | tf_op jit(solution)/shard_map/prepare/pallas_call | solution.py:413
  1.5 0.5 collective-permute-start
  2.0 0.1 collective-permute-start.1
  2.1 3.0 %collective-permute-start.2 = (bf16[776,128]{1,0:T(8,128)(2,1)S(1)}, bf16[776,128]{1,0:T(8,128)(2,1)S(1)}, u32[]{:S(2)}, u32[]{:S(2)}) collective-permute-start(bf16[776,128]{1,0:T(8,128)(2,1)S(1)} %get-tuple-element.51.refs_1_.refs_3_), channel_id=1, source_target_pairs={{0,8},{2,10},{8,16},{10,18},{16,24},{18,26},{24,28},{26,30},{28,20... | collective-permute-start | bytes 595976 | tf_op jit(solution)/shard_map/ppermute | solution.py:468
  5.1 1.4 %collective-permute-start.7 = (bf16[776,128]{1,0:T(8,128)(2,1)S(1)}, bf16[776,128]{1,0:T(8,128)(2,1)S(1)}, u32[]{:S(2)}, u32[]{:S(2)}) collective-permute-start(bf16[776,128]{1,0:T(8,128)(2,1)S(1)} %get-tuple-element.51.refs_1_.refs_3_), channel_id=1, source_target_pairs={{0,4},{2,6},{8,0},{10,2},{16,8},{18,10},{24,16},{26,18},{28,24},{3... | collective-permute-start | bytes 595976 | tf_op jit(solution)/shard_map/ppermute | solution.py:469
  6.5 0.4 collective-permute-start.6
  6.9 0.3 turn.1.refs_0_
  7.2 2.6 %attend.7 = (f32[8,1,480]{2,1,0:T(1,128)S(1)}, f32[8,144,480]{2,1,0:T(8,128)S(1)}, bf16[2560,1024]{1,0:T(8,128)(2,1)S(1)}) custom-call(bf16[8,128,480]{2,1,0:T(8,128)(2,1)S(1)} %turn.1.refs_0_, bf16[776,128]{1,0:T(8,128)(2,1)S(1)} %get-tuple-element.51.refs_1_.refs_3_, bf16[776,128]{1,0:T(8,128)(2,1)S(1)} %collective-permute-done.1.refs_2_.refs_4_, ...), custom_call_target="tpu_custom_call" | custom-call | flops 377487360 | bytes 4194304 | tf_op jit(solution)/shard_map/attend/pallas_call | solution.py:280
  9.8 1.0 %collective-permute-done.2.refs_3_ = bf16[776,128]{1,0:T(8,128)(2,1)S(1)} collective-permute-done((bf16[776,128]{1,0:T(8,128)(2,1)S(1)}, bf16[776,128]{1,0:T(8,128)(2,1)S(1)}, u32[]{:S(2)}, u32[]{:S(2)}) %collective-permute-start.2) | collective-permute-done | bytes 198688 | tf_op jit(solution)/shard_map/ppermute | solution.py:468
  10.8 1.4 %collective-permute-done.3.refs_6_ = bf16[776,128]{1,0:T(8,128)(2,1)S(1)} collective-permute-done((bf16[776,128]{1,0:T(8,128)(2,1)S(1)}, bf16[776,128]{1,0:T(8,128)(2,1)S(1)}, u32[]{:S(2)}, u32[]{:S(2)}) %collective-permute-start.3) | collective-permute-done | bytes 198688 | tf_op jit(solution)/shard_map/ppermute | solution.py:509
  12.2 1.6 %collective-permute-start.4 = (bf16[776,128]{1,0:T(8,128)(2,1)S(1)}, bf16[776,128]{1,0:T(8,128)(2,1)S(1)}, u32[]{:S(2)}, u32[]{:S(2)}) collective-permute-start(bf16[776,128]{1,0:T(8,128)(2,1)S(1)} %collective-permute-done.2.refs_3_), channel_id=1, source_target_pairs={{0,8},{2,10},{8,16},{10,18},{16,24},{18,26},{24,28},{26,30},{28,20... | collective-permute-start | bytes 595976 | tf_op jit(solution)/shard_map/ppermute | solution.py:468
  13.8 0.4 collective-permute-start.5
  14.3 2.4 %collective-permute-done.7.refs_5_ = bf16[776,128]{1,0:T(8,128)(2,1)S(1)} collective-permute-done((bf16[776,128]{1,0:T(8,128)(2,1)S(1)}, bf16[776,128]{1,0:T(8,128)(2,1)S(1)}, u32[]{:S(2)}, u32[]{:S(2)}) %collective-permute-start.7) | collective-permute-done | bytes 198688 | tf_op jit(solution)/shard_map/ppermute | solution.py:469
  16.7 2.0 %collective-permute-start.10 = (bf16[776,128]{1,0:T(8,128)(2,1)S(1)}, bf16[776,128]{1,0:T(8,128)(2,1)S(1)}, u32[]{:S(2)}, u32[]{:S(2)}) collective-permute-start(bf16[776,128]{1,0:T(8,128)(2,1)S(1)} %collective-permute-done.6.refs_4_), channel_id=1, source_target_pairs={{0,8},{2,10},{8,16},{10,18},{16,24},{18,26},{24,28},{26,30},{28,20... | collective-permute-start | bytes 595976 | tf_op jit(solution)/shard_map/ppermute | solution.py:468
  18.7 2.6 %attend.8 = (f32[8,1,480]{2,1,0:T(1,128)S(1)}, f32[8,144,480]{2,1,0:T(8,128)S(1)}) custom-call(bf16[8,128,480]{2,1,0:T(8,128)(2,1)S(1)} %turn.1.refs_0_, bf16[776,128]{1,0:T(8,128)(2,1)S(1)} %get-tuple-element.51.refs_1_.refs_3_, bf16[776,128]{1,0:T(8,128)(2,1)S(1)} %collective-permute-done.1.refs_2_.refs_4_, ...), custom_call_target="tpu_custom_call" | custom-call | flops 754974720 | bytes 4194304 | tf_op jit(solution)/shard_map/attend/pallas_call | solution.py:280
  21.3 0.3 collective-permute-done.5.refs_6_
  21.6 1.7 %collective-permute-start.8 = (bf16[776,128]{1,0:T(8,128)(2,1)S(1)}, bf16[776,128]{1,0:T(8,128)(2,1)S(1)}, u32[]{:S(2)}, u32[]{:S(2)}) collective-permute-start(bf16[776,128]{1,0:T(8,128)(2,1)S(1)} %collective-permute-done.4.refs_3_), channel_id=1, source_target_pairs={{0,8},{2,10},{8,16},{10,18},{16,24},{18,26},{24,28},{26,30},{28,20... | collective-permute-start | bytes 595976 | tf_op jit(solution)/shard_map/ppermute | solution.py:468
  23.3 0.3 collective-permute-start.9
  23.6 2.0 %collective-permute-done.11.refs_5_ = bf16[776,128]{1,0:T(8,128)(2,1)S(1)} collective-permute-done((bf16[776,128]{1,0:T(8,128)(2,1)S(1)}, bf16[776,128]{1,0:T(8,128)(2,1)S(1)}, u32[]{:S(2)}, u32[]{:S(2)}) %collective-permute-start.11) | collective-permute-done | bytes 198688 | tf_op jit(solution)/shard_map/ppermute | solution.py:469
  25.6 0.2 collective-permute-start.15
  25.8 1.8 %collective-permute-start.14 = (bf16[776,128]{1,0:T(8,128)(2,1)S(1)}, bf16[776,128]{1,0:T(8,128)(2,1)S(1)}, u32[]{:S(2)}, u32[]{:S(2)}) collective-permute-start(bf16[776,128]{1,0:T(8,128)(2,1)S(1)} %collective-permute-done.10.refs_4_), channel_id=1, source_target_pairs={{0,8},{2,10},{8,16},{10,18},{16,24},{18,26},{24,28},{26,30},{28,20... | collective-permute-start | bytes 595976 | tf_op jit(solution)/shard_map/ppermute | solution.py:468
  27.6 3.1 %attend.9 = (f32[8,1,480]{2,1,0:T(1,128)S(1)}, f32[8,144,480]{2,1,0:T(8,128)S(1)}, bf16[2560,1280]{1,0:T(8,128)(2,1)S(1)}) custom-call(bf16[8,128,480]{2,1,0:T(8,128)(2,1)S(1)} %turn.1.refs_0_, bf16[776,128]{1,0:T(8,128)(2,1)S(1)} %get-tuple-element.51.refs_1_.refs_3_, bf16[776,128]{1,0:T(8,128)(2,1)S(1)} %collective-permute-done.1.refs_2_.refs_4_, ...), custom_call_target="tpu_custom_call" | custom-call | flops 754974720 | bytes 4194304 | tf_op jit(solution)/shard_map/attend/pallas_call | solution.py:280
  30.7 0.5 collective-permute-done.9.refs_6_
  31.2 1.6 %collective-permute-start.12 = (bf16[776,128]{1,0:T(8,128)(2,1)S(1)}, bf16[776,128]{1,0:T(8,128)(2,1)S(1)}, u32[]{:S(2)}, u32[]{:S(2)}) collective-permute-start(bf16[776,128]{1,0:T(8,128)(2,1)S(1)} %collective-permute-done.8.refs_3_), channel_id=1, source_target_pairs={{0,8},{2,10},{8,16},{10,18},{16,24},{18,26},{24,28},{26,30},{28,20... | collective-permute-start | bytes 595976 | tf_op jit(solution)/shard_map/ppermute | solution.py:468
  32.8 0.4 collective-permute-start.13
  33.2 0.6 collective-permute-done.15.refs_5_
  33.8 3.1 %attend.10 = (f32[8,1,480]{2,1,0:T(1,128)S(1)}, f32[8,144,480]{2,1,0:T(8,128)S(1)}, bf16[2560,1152]{1,0:T(8,128)(2,1)S(1)}) custom-call(bf16[8,128,480]{2,1,0:T(8,128)(2,1)S(1)} %turn.1.refs_0_, bf16[776,128]{1,0:T(8,128)(2,1)S(1)} %get-tuple-element.51.refs_1_.refs_3_, bf16[776,128]{1,0:T(8,128)(2,1)S(1)} %collective-permute-done.1.refs_2_.refs_4_, ...), custom_call_target="tpu_custom_call" | custom-call | flops 754974720 | bytes 4194304 | tf_op jit(solution)/shard_map/attend/pallas_call | solution.py:280
  37.0 1.5 %collective-permute-done.13.refs_4_ = bf16[776,128]{1,0:T(8,128)(2,1)S(1)} collective-permute-done((bf16[776,128]{1,0:T(8,128)(2,1)S(1)}, bf16[776,128]{1,0:T(8,128)(2,1)S(1)}, u32[]{:S(2)}, u32[]{:S(2)}) %collective-permute-start.13) | collective-permute-done | bytes 198688 | tf_op jit(solution)/shard_map/ppermute | solution.py:469
  38.5 1.0 %attend.12 = bf16[192,1280]{1,0:T(8,128)(2,1)S(1)} custom-call(bf16[8,128,480]{2,1,0:T(8,128)(2,1)S(1)} %turn.1.refs_0_, bf16[776,128]{1,0:T(8,128)(2,1)S(1)} %get-tuple-element.51.refs_1_.refs_3_, bf16[776,128]{1,0:T(8,128)(2,1)S(1)} %collective-permute-done.1.refs_2_.refs_4_, bf16[776,128]{1,0:T(8,128)(2,1)S(1)} %collective-permute-done.12.refs_3_, ...), custom_call_target="tpu_custom_call" | custom-call | flops 377487360 | bytes 4194304 | tf_op jit(solution)/shard_map/attend/pallas_call | solution.py:280
  39.6 0.5 collective-permute-start.17
  40.1 1.0 %attend.11.own_ref.refs_0_ = bf16[96,1280]{1,0:T(8,128)(2,1)S(1)} custom-call(bf16[8,128,480]{2,1,0:T(8,128)(2,1)S(1)} %turn.1.refs_0_, bf16[776,128]{1,0:T(8,128)(2,1)S(1)} %get-tuple-element.51.refs_1_.refs_3_, bf16[776,128]{1,0:T(8,128)(2,1)S(1)} %collective-permute-done.1.refs_2_.refs_4_, bf16[776,128]{1,0:T(8,128)(2,1)S(1)} %collective-permute-done.12.refs_3_, ...), custom_call_target="tpu_custom_call" | custom-call | flops 377487360 | bytes 4194304 | tf_op jit(solution)/shard_map/attend/pallas_call | solution.py:280
  41.1 0.7 %multiply.7.begun_ref = f32[96,1280]{1,0:T(8,128)S(1)} custom-call(bf16[96,1280]{1,0:T(8,128)(2,1)S(1)} %attend.11.own_ref.refs_0_, bf16[2560,1280]{1,0:T(8,128)(2,1)S(1)} %get-tuple-element.73.held_ref), custom_call_target="tpu_custom_call" | custom-call | flops 1024 | bytes 1024 | tf_op jit(solution)/shard_map/multiply/pallas_call | solution.py:369
  41.8 0.7 %multiply.8 = bf16[96,1280]{1,0:T(8,128)(2,1)S(1)} custom-call(bf16[96,1280]{1,0:T(8,128)(2,1)S(1)} %collective-permute-done.16.other_ref.refs_1_, bf16[2560,1280]{1,0:T(8,128)(2,1)S(1)} %get-tuple-element.73.held_ref, f32[96,1280]{1,0:T(8,128)S(1)} %multiply.7.begun_ref), custom_call_target="tpu_custom_call" | custom-call | flops 1024 | bytes 1024 | tf_op jit(solution)/shard_map/multiply/pallas_call | solution.py:369
  42.6 1.3 %collective-permute-start.19 = (bf16[96,1280]{1,0:T(8,128)(2,1)S(1)}, bf16[96,1280]{1,0:T(8,128)(2,1)S(1)}, u32[]{:S(2)}, u32[]{:S(2)}) collective-permute-start(bf16[96,1280]{1,0:T(8,128)(2,1)S(1)} %multiply.8), channel_id=1, source_target_pairs={{0,1},{1,0},{2,3},{3,2},{4,5},{5,4},{6,7},{7,6},{8,9},{9,8},{10,11... | collective-permute-start | bytes 737288 | tf_op jit(solution)/shard_map/ppermute | solution.py:589
  43.8 0.9 %attend.13.refs_2_.own_ref = bf16[96,1280]{1,0:T(8,128)(2,1)S(1)} custom-call(bf16[8,128,480]{2,1,0:T(8,128)(2,1)S(1)} %turn.1.refs_0_, bf16[776,128]{1,0:T(8,128)(2,1)S(1)} %get-tuple-element.51.refs_1_.refs_3_, bf16[776,128]{1,0:T(8,128)(2,1)S(1)} %collective-permute-done.1.refs_2_.refs_4_, bf16[776,128]{1,0:T(8,128)(2,1)S(1)} %collective-permute-done.12.refs_3_, ...), custom_call_target="tpu_custom_call" | custom-call | flops 377487360 | bytes 4194304 | tf_op jit(solution)/shard_map/attend/pallas_call | solution.py:280
  44.8 2.9 %multiply.9 = (bf16[96,1152]{1,0:T(8,128)(2,1)S(1)}, bf16[96,1152]{1,0:T(8,128)(2,1)S(1)}, bf16[2560,896]{1,0:T(8,128)(2,1)S(1)}) custom-call(bf16[96,1280]{1,0:T(8,128)(2,1)S(1)} %attend.11.own_ref.refs_0_, bf16[96,1280]{1,0:T(8,128)(2,1)S(1)} %collective-permute-done.16.other_ref.refs_1_, bf16[96,1280]{1,0:T(8,128)(2,1)S(1)} %attend.13.refs_2_.own_ref, ...), custom_call_target="tpu_custom_call" | custom-call | flops 1024 | bytes 1024 | tf_op jit(solution)/shard_map/multiply/pallas_call | solution.py:369
  47.7 1.1 %collective-permute-start.20 = (bf16[96,1152]{1,0:T(8,128)(2,1)S(1)}, bf16[96,1152]{1,0:T(8,128)(2,1)S(1)}, u32[]{:S(2)}, u32[]{:S(2)}) collective-permute-start(bf16[96,1152]{1,0:T(8,128)(2,1)S(1)} %get-tuple-element.78), channel_id=1, source_target_pairs={{0,1},{1,0},{2,3},{3,2},{4,5},{5,4},{6,7},{7,6},{8,9},{9,8},{10,11... | collective-permute-start | bytes 663560 | tf_op jit(solution)/shard_map/ppermute | solution.py:589
  48.9 2.5 %multiply.10 = (bf16[96,1024]{1,0:T(8,128)(2,1)S(1)}, bf16[96,1024]{1,0:T(8,128)(2,1)S(1)}, bf16[2560,768]{1,0:T(8,128)(2,1)S(1)}) custom-call(bf16[96,1280]{1,0:T(8,128)(2,1)S(1)} %attend.11.own_ref.refs_0_, bf16[96,1280]{1,0:T(8,128)(2,1)S(1)} %collective-permute-done.16.other_ref.refs_1_, bf16[96,1280]{1,0:T(8,128)(2,1)S(1)} %attend.13.refs_2_.own_ref, ...), custom_call_target="tpu_custom_call" | custom-call | flops 1024 | bytes 1024 | tf_op jit(solution)/shard_map/multiply/pallas_call | solution.py:369
  51.4 1.0 %collective-permute-start.21 = (bf16[96,1024]{1,0:T(8,128)(2,1)S(1)}, bf16[96,1024]{1,0:T(8,128)(2,1)S(1)}, u32[]{:S(2)}, u32[]{:S(2)}) collective-permute-start(bf16[96,1024]{1,0:T(8,128)(2,1)S(1)} %get-tuple-element.81), channel_id=1, source_target_pairs={{0,1},{1,0},{2,3},{3,2},{4,5},{5,4},{6,7},{7,6},{8,9},{9,8},{10,11... | collective-permute-start | bytes 589832 | tf_op jit(solution)/shard_map/ppermute | solution.py:589
  52.4 1.2 %multiply.11 = (bf16[96,896]{1,0:T(8,128)(2,1)S(1)}, bf16[96,896]{1,0:T(8,128)(2,1)S(1)}) custom-call(bf16[96,1280]{1,0:T(8,128)(2,1)S(1)} %attend.11.own_ref.refs_0_, bf16[96,1280]{1,0:T(8,128)(2,1)S(1)} %collective-permute-done.16.other_ref.refs_1_, bf16[96,1280]{1,0:T(8,128)(2,1)S(1)} %attend.13.refs_2_.own_ref, ...), custom_call_target="tpu_custom_call" | custom-call | flops 1024 | bytes 1024 | tf_op jit(solution)/shard_map/multiply/pallas_call | solution.py:369
  53.7 1.1 %collective-permute-start.22 = (bf16[96,896]{1,0:T(8,128)(2,1)S(1)}, bf16[96,896]{1,0:T(8,128)(2,1)S(1)}, u32[]{:S(2)}, u32[]{:S(2)}) collective-permute-start(bf16[96,896]{1,0:T(8,128)(2,1)S(1)} %get-tuple-element.84), channel_id=1, source_target_pairs={{0,1},{1,0},{2,3},{3,2},{4,5},{5,4},{6,7},{7,6},{8,9},{9,8},{10,11... | collective-permute-start | bytes 516104 | tf_op jit(solution)/shard_map/ppermute | solution.py:589
  54.8 0.9 %multiply.12 = (bf16[96,768]{1,0:T(8,128)(2,1)S(1)}, bf16[96,768]{1,0:T(8,128)(2,1)S(1)}) custom-call(bf16[96,1280]{1,0:T(8,128)(2,1)S(1)} %attend.11.own_ref.refs_0_, bf16[96,1280]{1,0:T(8,128)(2,1)S(1)} %collective-permute-done.16.other_ref.refs_1_, bf16[96,1280]{1,0:T(8,128)(2,1)S(1)} %attend.13.refs_2_.own_ref, ...), custom_call_target="tpu_custom_call" | custom-call | flops 1024 | bytes 1024 | tf_op jit(solution)/shard_map/multiply/pallas_call | solution.py:369
  55.7 1.0 %collective-permute-start.18 = (bf16[96,768]{1,0:T(8,128)(2,1)S(1)}, bf16[96,768]{1,0:T(8,128)(2,1)S(1)}, u32[]{:S(2)}, u32[]{:S(2)}) collective-permute-start(bf16[96,768]{1,0:T(8,128)(2,1)S(1)} %get-tuple-element.88), channel_id=1, source_target_pairs={{0,1},{1,0},{2,3},{3,2},{4,5},{5,4},{6,7},{7,6},{8,9},{9,8},{10,11... | collective-permute-start | bytes 442376 | tf_op jit(solution)/shard_map/ppermute | solution.py:589
  56.8 1.2 %multiply.13.refs_0_ = bf16[96,1280]{1,0:T(8,128)(2,1)S(1)} custom-call(bf16[96,1280]{1,0:T(8,128)(2,1)S(1)} %attend.13.refs_2_.own_ref, bf16[96,1280]{1,0:T(8,128)(2,1)S(1)} %collective-permute-done.17.refs_3_.other_ref, bf16[2560,1280]{1,0:T(8,128)(2,1)S(1)} %get-tuple-element.73.held_ref), custom_call_target="tpu_custom_call" | custom-call | flops 1024 | bytes 1024 | tf_op jit(solution)/shard_map/multiply/pallas_call | solution.py:369
  58.0 6.1 %collective-permute-done.22.refs_7_ = bf16[96,896]{1,0:T(8,128)(2,1)S(1)} collective-permute-done((bf16[96,896]{1,0:T(8,128)(2,1)S(1)}, bf16[96,896]{1,0:T(8,128)(2,1)S(1)}, u32[]{:S(2)}, u32[]{:S(2)}) %collective-permute-start.22) | collective-permute-done | bytes 172064 | tf_op jit(solution)/shard_map/ppermute | solution.py:589
  64.0 1.1 %finish.2.refs_2_ = bf16[96,5120]{1,0:T(8,128)(2,1)} custom-call(bf16[96,1280]{1,0:T(8,128)(2,1)S(1)} %multiply.13.refs_0_, bf16[96,1152]{1,0:T(8,128)(2,1)S(1)} %get-tuple-element.90.refs_1_, bf16[96,1024]{1,0:T(8,128)(2,1)S(1)} %get-tuple-element.91.refs_2_, bf16[96,896]{1,0:T(8,128)(2,1)S(1)} %get-tuple-element.92.refs_3_, ...), custom_call_target="tpu_custom_call" | custom-call | flops 1024 | bytes 1024 | tf_op jit(solution)/shard_map/finish/pallas_call | solution.py:445
  65.1 1.2 %collective-permute-done.18.refs_1_ = bf16[96,768]{1,0:T(8,128)(2,1)S(1)} collective-permute-done((bf16[96,768]{1,0:T(8,128)(2,1)S(1)}, bf16[96,768]{1,0:T(8,128)(2,1)S(1)}, u32[]{:S(2)}, u32[]{:S(2)}) %collective-permute-start.18) | collective-permute-done | bytes 147488 | tf_op jit(solution)/shard_map/ppermute | solution.py:589
  66.4 0.7 %finish.3 = bf16[96,5120]{1,0:T(8,128)(2,1)} custom-call(bf16[96,768]{1,0:T(8,128)(2,1)S(1)} %get-tuple-element.87.refs_0_, bf16[96,768]{1,0:T(8,128)(2,1)S(1)} %collective-permute-done.18.refs_1_, bf16[96,5120]{1,0:T(8,128)(2,1)} %finish.2.refs_2_), custom_call_target="tpu_custom_call", output_to_operand_aliasing={{}: (2, {})} | custom-call | flops 1024 | bytes 1024 | tf_op jit(solution)/shard_map/finish/pallas_call | solution.py:445
  (17 shorter events, 0.1 us)
Async XLA Ops:
  1.5 5.0 %collective-permute-start = (bf16[192,1280]{1,0:T(8,128)(2,1)S(1)}, bf16[192,1280]{1,0:T(8,128)(2,1)S(1)}, u32[]{:S(2)}, u32[]{:S(2)}) collective-permute-start(bf16[192,1280]{1,0:T(8,128)(2,1)S(1)} %get-tuple-element.50), channel_id=1, source_target_pairs={{0,2},{2,0},{4,6},{6,4},{8,10},{10,8},{12,14},{14,12},{16,18},{18,... | collective-permute-start | bytes 1474568 | tf_op jit(solution)/shard_map/ppermute | solution.py:474
  2.0 5.2 %collective-permute-start.1 = (bf16[776,128]{1,0:T(8,128)(2,1)S(1)}, bf16[776,128]{1,0:T(8,128)(2,1)S(1)}, u32[]{:S(2)}, u32[]{:S(2)}) collective-permute-start(bf16[776,128]{1,0:T(8,128)(2,1)S(1)} %get-tuple-element.52), channel_id=1, source_target_pairs={{0,2},{2,0},{4,6},{6,4},{8,10},{10,8},{12,14},{14,12},{16,18},{18,... | collective-permute-start | bytes 595976 | tf_op jit(solution)/shard_map/ppermute | solution.py:473
  2.1 8.7 %collective-permute-start.2 = (bf16[776,128]{1,0:T(8,128)(2,1)S(1)}, bf16[776,128]{1,0:T(8,128)(2,1)S(1)}, u32[]{:S(2)}, u32[]{:S(2)}) collective-permute-start(bf16[776,128]{1,0:T(8,128)(2,1)S(1)} %get-tuple-element.51.refs_1_.refs_3_), channel_id=1, source_target_pairs={{0,8},{2,10},{8,16},{10,18},{16,24},{18,26},{24,28},{26,30},{28,20... | collective-permute-start | bytes 595976 | tf_op jit(solution)/shard_map/ppermute | solution.py:468
  5.1 7.1 %collective-permute-start.3 = (bf16[776,128]{1,0:T(8,128)(2,1)S(1)}, bf16[776,128]{1,0:T(8,128)(2,1)S(1)}, u32[]{:S(2)}, u32[]{:S(2)}) collective-permute-start(bf16[776,128]{1,0:T(8,128)(2,1)S(1)} %get-tuple-element.52), channel_id=1, source_target_pairs={{0,6},{2,4},{8,2},{10,0},{16,10},{18,8},{24,18},{26,16},{28,26},{3... | collective-permute-start | bytes 595976 | tf_op jit(solution)/shard_map/ppermute | solution.py:509
  5.1 11.6 %collective-permute-start.7 = (bf16[776,128]{1,0:T(8,128)(2,1)S(1)}, bf16[776,128]{1,0:T(8,128)(2,1)S(1)}, u32[]{:S(2)}, u32[]{:S(2)}) collective-permute-start(bf16[776,128]{1,0:T(8,128)(2,1)S(1)} %get-tuple-element.51.refs_1_.refs_3_), channel_id=1, source_target_pairs={{0,4},{2,6},{8,0},{10,2},{16,8},{18,10},{24,16},{26,18},{28,24},{3... | collective-permute-start | bytes 595976 | tf_op jit(solution)/shard_map/ppermute | solution.py:469
  6.5 10.2 %collective-permute-start.6 = (bf16[776,128]{1,0:T(8,128)(2,1)S(1)}, bf16[776,128]{1,0:T(8,128)(2,1)S(1)}, u32[]{:S(2)}, u32[]{:S(2)}) collective-permute-start(bf16[776,128]{1,0:T(8,128)(2,1)S(1)} %get-tuple-element.52), channel_id=1, source_target_pairs={{0,10},{2,8},{8,18},{10,16},{16,26},{18,24},{24,30},{26,28},{28,22... | collective-permute-start | bytes 595976 | tf_op jit(solution)/shard_map/ppermute | solution.py:508
  12.2 9.1 %collective-permute-start.4 = (bf16[776,128]{1,0:T(8,128)(2,1)S(1)}, bf16[776,128]{1,0:T(8,128)(2,1)S(1)}, u32[]{:S(2)}, u32[]{:S(2)}) collective-permute-start(bf16[776,128]{1,0:T(8,128)(2,1)S(1)} %collective-permute-done.2.refs_3_), channel_id=1, source_target_pairs={{0,8},{2,10},{8,16},{10,18},{16,24},{18,26},{24,28},{26,30},{28,20... | collective-permute-start | bytes 595976 | tf_op jit(solution)/shard_map/ppermute | solution.py:468
  13.8 7.8 %collective-permute-start.5 = (bf16[776,128]{1,0:T(8,128)(2,1)S(1)}, bf16[776,128]{1,0:T(8,128)(2,1)S(1)}, u32[]{:S(2)}, u32[]{:S(2)}) collective-permute-start(bf16[776,128]{1,0:T(8,128)(2,1)S(1)} %collective-permute-done.3.refs_6_), channel_id=1, source_target_pairs={{0,4},{2,6},{8,0},{10,2},{16,8},{18,10},{24,16},{26,18},{28,24},{3... | collective-permute-start | bytes 595976 | tf_op jit(solution)/shard_map/ppermute | solution.py:469
  16.7 8.9 %collective-permute-start.11 = (bf16[776,128]{1,0:T(8,128)(2,1)S(1)}, bf16[776,128]{1,0:T(8,128)(2,1)S(1)}, u32[]{:S(2)}, u32[]{:S(2)}) collective-permute-start(bf16[776,128]{1,0:T(8,128)(2,1)S(1)} %collective-permute-done.7.refs_5_), channel_id=1, source_target_pairs={{0,4},{2,6},{8,0},{10,2},{16,8},{18,10},{24,16},{26,18},{28,24},{3... | collective-permute-start | bytes 595976 | tf_op jit(solution)/shard_map/ppermute | solution.py:469
  16.7 9.1 %collective-permute-start.10 = (bf16[776,128]{1,0:T(8,128)(2,1)S(1)}, bf16[776,128]{1,0:T(8,128)(2,1)S(1)}, u32[]{:S(2)}, u32[]{:S(2)}) collective-permute-start(bf16[776,128]{1,0:T(8,128)(2,1)S(1)} %collective-permute-done.6.refs_4_), channel_id=1, source_target_pairs={{0,8},{2,10},{8,16},{10,18},{16,24},{18,26},{24,28},{26,30},{28,20... | collective-permute-start | bytes 595976 | tf_op jit(solution)/shard_map/ppermute | solution.py:468
  21.6 9.1 %collective-permute-start.8 = (bf16[776,128]{1,0:T(8,128)(2,1)S(1)}, bf16[776,128]{1,0:T(8,128)(2,1)S(1)}, u32[]{:S(2)}, u32[]{:S(2)}) collective-permute-start(bf16[776,128]{1,0:T(8,128)(2,1)S(1)} %collective-permute-done.4.refs_3_), channel_id=1, source_target_pairs={{0,8},{2,10},{8,16},{10,18},{16,24},{18,26},{24,28},{26,30},{28,20... | collective-permute-start | bytes 595976 | tf_op jit(solution)/shard_map/ppermute | solution.py:468
  23.3 7.9 %collective-permute-start.9 = (bf16[776,128]{1,0:T(8,128)(2,1)S(1)}, bf16[776,128]{1,0:T(8,128)(2,1)S(1)}, u32[]{:S(2)}, u32[]{:S(2)}) collective-permute-start(bf16[776,128]{1,0:T(8,128)(2,1)S(1)} %collective-permute-done.5.refs_6_), channel_id=1, source_target_pairs={{0,4},{2,6},{8,0},{10,2},{16,8},{18,10},{24,16},{26,18},{28,24},{3... | collective-permute-start | bytes 595976 | tf_op jit(solution)/shard_map/ppermute | solution.py:469
  25.6 8.2 %collective-permute-start.15 = (bf16[776,128]{1,0:T(8,128)(2,1)S(1)}, bf16[776,128]{1,0:T(8,128)(2,1)S(1)}, u32[]{:S(2)}, u32[]{:S(2)}) collective-permute-start(bf16[776,128]{1,0:T(8,128)(2,1)S(1)} %collective-permute-done.11.refs_5_), channel_id=1, source_target_pairs={{0,4},{2,6},{8,0},{10,2},{16,8},{18,10},{24,16},{26,18},{28,24},{3... | collective-permute-start | bytes 595976 | tf_op jit(solution)/shard_map/ppermute | solution.py:469
  25.8 8.1 %collective-permute-start.14 = (bf16[776,128]{1,0:T(8,128)(2,1)S(1)}, bf16[776,128]{1,0:T(8,128)(2,1)S(1)}, u32[]{:S(2)}, u32[]{:S(2)}) collective-permute-start(bf16[776,128]{1,0:T(8,128)(2,1)S(1)} %collective-permute-done.10.refs_4_), channel_id=1, source_target_pairs={{0,8},{2,10},{8,16},{10,18},{16,24},{18,26},{24,28},{26,30},{28,20... | collective-permute-start | bytes 595976 | tf_op jit(solution)/shard_map/ppermute | solution.py:468
  31.2 5.7 %collective-permute-start.12 = (bf16[776,128]{1,0:T(8,128)(2,1)S(1)}, bf16[776,128]{1,0:T(8,128)(2,1)S(1)}, u32[]{:S(2)}, u32[]{:S(2)}) collective-permute-start(bf16[776,128]{1,0:T(8,128)(2,1)S(1)} %collective-permute-done.8.refs_3_), channel_id=1, source_target_pairs={{0,8},{2,10},{8,16},{10,18},{16,24},{18,26},{24,28},{26,30},{28,20... | collective-permute-start | bytes 595976 | tf_op jit(solution)/shard_map/ppermute | solution.py:468
  32.8 5.7 %collective-permute-start.13 = (bf16[776,128]{1,0:T(8,128)(2,1)S(1)}, bf16[776,128]{1,0:T(8,128)(2,1)S(1)}, u32[]{:S(2)}, u32[]{:S(2)}) collective-permute-start(bf16[776,128]{1,0:T(8,128)(2,1)S(1)} %collective-permute-done.9.refs_6_), channel_id=1, source_target_pairs={{0,4},{2,6},{8,0},{10,2},{16,8},{18,10},{24,16},{26,18},{28,24},{3... | collective-permute-start | bytes 595976 | tf_op jit(solution)/shard_map/ppermute | solution.py:469
  39.5 2.3 %collective-permute-start.16 = (bf16[96,1280]{1,0:T(8,128)(2,1)S(1)}, bf16[96,1280]{1,0:T(8,128)(2,1)S(1)}, u32[]{:S(2)}, u32[]{:S(2)}) collective-permute-start(bf16[96,1280]{1,0:T(8,128)(2,1)S(1)} %get-tuple-element.94), channel_id=1, source_target_pairs={{0,2},{2,0},{4,6},{6,4},{8,10},{10,8},{12,14},{14,12},{16,18},{18,... | collective-permute-start | bytes 737288 | tf_op jit(solution)/shard_map/ppermute | solution.py:520
  39.6 5.2 %collective-permute-start.17 = (bf16[96,1280]{1,0:T(8,128)(2,1)S(1)}, bf16[96,1280]{1,0:T(8,128)(2,1)S(1)}, u32[]{:S(2)}, u32[]{:S(2)}) collective-permute-start(bf16[96,1280]{1,0:T(8,128)(2,1)S(1)} %get-tuple-element.93), channel_id=1, source_target_pairs={{0,2},{2,0},{4,6},{6,4},{8,10},{10,8},{12,14},{14,12},{16,18},{18,... | collective-permute-start | bytes 737288 | tf_op jit(solution)/shard_map/ppermute | solution.py:520
  42.6 21.5 %collective-permute-start.19 = (bf16[96,1280]{1,0:T(8,128)(2,1)S(1)}, bf16[96,1280]{1,0:T(8,128)(2,1)S(1)}, u32[]{:S(2)}, u32[]{:S(2)}) collective-permute-start(bf16[96,1280]{1,0:T(8,128)(2,1)S(1)} %multiply.8), channel_id=1, source_target_pairs={{0,1},{1,0},{2,3},{3,2},{4,5},{5,4},{6,7},{7,6},{8,9},{9,8},{10,11... | collective-permute-start | bytes 737288 | tf_op jit(solution)/shard_map/ppermute | solution.py:589
  47.7 16.3 %collective-permute-start.20 = (bf16[96,1152]{1,0:T(8,128)(2,1)S(1)}, bf16[96,1152]{1,0:T(8,128)(2,1)S(1)}, u32[]{:S(2)}, u32[]{:S(2)}) collective-permute-start(bf16[96,1152]{1,0:T(8,128)(2,1)S(1)} %get-tuple-element.78), channel_id=1, source_target_pairs={{0,1},{1,0},{2,3},{3,2},{4,5},{5,4},{6,7},{7,6},{8,9},{9,8},{10,11... | collective-permute-start | bytes 663560 | tf_op jit(solution)/shard_map/ppermute | solution.py:589
  51.4 12.6 %collective-permute-start.21 = (bf16[96,1024]{1,0:T(8,128)(2,1)S(1)}, bf16[96,1024]{1,0:T(8,128)(2,1)S(1)}, u32[]{:S(2)}, u32[]{:S(2)}) collective-permute-start(bf16[96,1024]{1,0:T(8,128)(2,1)S(1)} %get-tuple-element.81), channel_id=1, source_target_pairs={{0,1},{1,0},{2,3},{3,2},{4,5},{5,4},{6,7},{7,6},{8,9},{9,8},{10,11... | collective-permute-start | bytes 589832 | tf_op jit(solution)/shard_map/ppermute | solution.py:589
  53.7 10.4 %collective-permute-start.22 = (bf16[96,896]{1,0:T(8,128)(2,1)S(1)}, bf16[96,896]{1,0:T(8,128)(2,1)S(1)}, u32[]{:S(2)}, u32[]{:S(2)}) collective-permute-start(bf16[96,896]{1,0:T(8,128)(2,1)S(1)} %get-tuple-element.84), channel_id=1, source_target_pairs={{0,1},{1,0},{2,3},{3,2},{4,5},{5,4},{6,7},{7,6},{8,9},{9,8},{10,11... | collective-permute-start | bytes 516104 | tf_op jit(solution)/shard_map/ppermute | solution.py:589
  55.7 10.6 %collective-permute-start.18 = (bf16[96,768]{1,0:T(8,128)(2,1)S(1)}, bf16[96,768]{1,0:T(8,128)(2,1)S(1)}, u32[]{:S(2)}, u32[]{:S(2)}) collective-permute-start(bf16[96,768]{1,0:T(8,128)(2,1)S(1)} %get-tuple-element.88), channel_id=1, source_target_pairs={{0,1},{1,0},{2,3},{3,2},{4,5},{5,4},{6,7},{7,6},{8,9},{9,8},{10,11... | collective-permute-start | bytes 442376 | tf_op jit(solution)/shard_map/ppermute | solution.py:589

commit v18 on v17

--- a/solution.py
+++ b/solution.py
@@ -517,13 +517,14 @@
     far = (up(up_first), down(down_first))
     state = bring_with((1,), arrived, state)
     (theirs,) = call([far], state, last=True, which=(1,))
-    other = [lax.ppermute(rows, "blk", sibling) for rows in (theirs[:chunk], theirs[chunk:])]
+    other = lax.ppermute(theirs[:chunk], "blk", sibling)
     (own,) = call([far], state, last=True, which=(0,), part="sent")
 
-    def own_to_keep(event):
-        return call([far], after(state, event), last=True, which=(0,), part="kept")[0]
-
-    return own, other, held, own_to_keep
+    def rows_to_keep(event):
+        other = lax.ppermute(after(theirs[chunk:], event), "blk", sibling)
+        return call([far], after(state, event), last=True, which=(0,), part="kept")[0], other
+
+    return own, other, held, rows_to_keep
 
 
 def one_head_a_device(count, queries, keys, values, positions):
@@ -564,13 +565,13 @@
     shares = (10, 9, 8, 7, 6)
     widths = [out_weight.shape[1] * share // sum(shares) for share in shares]
     cuts = [(sum(widths[:j]), columns) for j, columns in enumerate(widths)]
-    own, (other, other_kept), held, own_to_keep = split_over_cores(
+    own, other, held, rows_to_keep = split_over_cores(
         count, queries, keys, values, positions, out_weight, cuts[:3]
     )
     chunk, depth, kind = own.shape[0], out_weight.shape[0], own.dtype
     (begun,) = multiply(begin_kernel, [own, held[0]], [((chunk, widths[0]), jnp.float32)])
     (sent,) = multiply(first_kernel, [other, held[0], begun], [((chunk, widths[0]), kind)])
-    own_kept = own_to_keep(sent)
+    own_kept, other_kept = rows_to_keep(sent)
     received, kept = [], [None]
     for j in range(len(cuts)):
         if j > 0:

time: 67.4 us -> 67.4 us (level)
  transfers between devices with their start and end apart: 23 -> 23, of which waited for: 10 -> 10; matrix products, arithmetic and copies ran while one was open for 0% -> 0% of each run, Pallas kernels for 37% -> 36%
where the time goes in v18:
time: 67.4 us; the launch traced here: 67.2 us
  Pallas kernels  28.1 us (42%)
  starting transfers between devices  21.7 us (32%)
  waiting for transfers between devices  17.1 us (25%)
    pallas_call x7, Pallas kernels, attend(): pl.pallas_call(functools.partial(attend_kernel, plan), out_shape=out_shap...  14.3 us
    ppermute x6, starting transfers between devices, split_over_cores(): up = lambda x: lax.ppermute(x, 'blk', clock)  11.7 us
    pallas_call x7, Pallas kernels, multiply(): pl.pallas_call(kernel, out_shape=[jax.ShapeDtypeStruct(shape, kind) for s...  10.2 us
    ppermute x5, waiting for transfers between devices, shards(): received.append(lax.ppermute(sent, 'inner', [(0, 1), (1, 0)]))  7.29 us
    ppermute x6, waiting for transfers between devices, split_over_cores(): down = lambda x: lax.ppermute(x, 'blk', counter)  7.29 us
    ppermute x5, starting transfers between devices, shards(): received.append(lax.ppermute(sent, 'inner', [(0, 1), (1, 0)]))  5.53 us
    ppermute x6, starting transfers between devices, split_over_cores(): down = lambda x: lax.ppermute(x, 'blk', counter)  2.77 us
    pallas_call x2, Pallas kernels, finish(): pl.pallas_call(functools.partial(finish_kernel, first, pairs), out_shape=...  1.8 us
  transfers between devices with their start and end apart: 23, of which 10 were waited for; matrix products, arithmetic and copies ran while one was open for 0% of the time, Pallas kernels for 36%

profile of v18, /device:TPU:0, one launch (start us, length us, event | category | flops | bytes accessed | tf_op | source)
XLA Modules:
  0.0 67.2 jit_solution(4912682565909513428)
XLA Ops:
  0.0 1.5 %prepare.1 = (bf16[776,128]{1,0:T(8,128)(2,1)S(1)}, bf16[776,128]{1,0:T(8,128)(2,1)S(1)}, bf16[192,1280]{1,0:T(8,128)(2,1)S(1)}, bf16[192,1280]{1,0:T(8,128)(2,1)S(1)}) custom-call(bf16[192,2560]{1,0:T(8,128)(2,1)} %q_ref.1, bf16[192,512]{1,0:T(8,128)(2,1)} %k_ref.1, bf16[192,512]{1,0:T(8,128)(2,1)} %v_ref.1, s32[192]{0:T(256)} %position_ref.1), custom_call_target="tpu_custom_call" | custom-call | tf_op jit(solution)/shard_map/prepare/pallas_call | solution.py:413
  1.5 0.5 collective-permute-start
  2.0 0.1 collective-permute-start.1
  2.1 3.0 %collective-permute-start.2 = (bf16[776,128]{1,0:T(8,128)(2,1)S(1)}, bf16[776,128]{1,0:T(8,128)(2,1)S(1)}, u32[]{:S(2)}, u32[]{:S(2)}) collective-permute-start(bf16[776,128]{1,0:T(8,128)(2,1)S(1)} %get-tuple-element.52.refs_1_.refs_3_), channel_id=1, source_target_pairs={{0,8},{2,10},{8,16},{10,18},{16,24},{18,26},{24,28},{26,30},{28,20... | collective-permute-start | bytes 595976 | tf_op jit(solution)/shard_map/ppermute | solution.py:468
  5.1 1.4 %collective-permute-start.7 = (bf16[776,128]{1,0:T(8,128)(2,1)S(1)}, bf16[776,128]{1,0:T(8,128)(2,1)S(1)}, u32[]{:S(2)}, u32[]{:S(2)}) collective-permute-start(bf16[776,128]{1,0:T(8,128)(2,1)S(1)} %get-tuple-element.52.refs_1_.refs_3_), channel_id=1, source_target_pairs={{0,4},{2,6},{8,0},{10,2},{16,8},{18,10},{24,16},{26,18},{28,24},{3... | collective-permute-start | bytes 595976 | tf_op jit(solution)/shard_map/ppermute | solution.py:469
  6.5 0.4 collective-permute-start.6
  6.9 0.3 turn.1.refs_0_
  7.2 2.6 %attend.7 = (f32[8,1,480]{2,1,0:T(1,128)S(1)}, f32[8,144,480]{2,1,0:T(8,128)S(1)}, bf16[2560,1024]{1,0:T(8,128)(2,1)S(1)}) custom-call(bf16[8,128,480]{2,1,0:T(8,128)(2,1)S(1)} %turn.1.refs_0_, bf16[776,128]{1,0:T(8,128)(2,1)S(1)} %get-tuple-element.52.refs_1_.refs_3_, bf16[776,128]{1,0:T(8,128)(2,1)S(1)} %collective-permute-done.1.refs_2_.refs_4_, ...), custom_call_target="tpu_custom_call" | custom-call | flops 377487360 | bytes 4194304 | tf_op jit(solution)/shard_map/attend/pallas_call | solution.py:280
  9.8 1.0 %collective-permute-done.2.refs_3_ = bf16[776,128]{1,0:T(8,128)(2,1)S(1)} collective-permute-done((bf16[776,128]{1,0:T(8,128)(2,1)S(1)}, bf16[776,128]{1,0:T(8,128)(2,1)S(1)}, u32[]{:S(2)}, u32[]{:S(2)}) %collective-permute-start.2) | collective-permute-done | bytes 198688 | tf_op jit(solution)/shard_map/ppermute | solution.py:468
  10.8 1.4 %collective-permute-done.3.refs_6_ = bf16[776,128]{1,0:T(8,128)(2,1)S(1)} collective-permute-done((bf16[776,128]{1,0:T(8,128)(2,1)S(1)}, bf16[776,128]{1,0:T(8,128)(2,1)S(1)}, u32[]{:S(2)}, u32[]{:S(2)}) %collective-permute-start.3) | collective-permute-done | bytes 198688 | tf_op jit(solution)/shard_map/ppermute | solution.py:509
  12.2 1.6 %collective-permute-start.4 = (bf16[776,128]{1,0:T(8,128)(2,1)S(1)}, bf16[776,128]{1,0:T(8,128)(2,1)S(1)}, u32[]{:S(2)}, u32[]{:S(2)}) collective-permute-start(bf16[776,128]{1,0:T(8,128)(2,1)S(1)} %collective-permute-done.2.refs_3_), channel_id=1, source_target_pairs={{0,8},{2,10},{8,16},{10,18},{16,24},{18,26},{24,28},{26,30},{28,20... | collective-permute-start | bytes 595976 | tf_op jit(solution)/shard_map/ppermute | solution.py:468
  13.8 0.4 collective-permute-start.5
  14.3 2.4 %collective-permute-done.7.refs_5_ = bf16[776,128]{1,0:T(8,128)(2,1)S(1)} collective-permute-done((bf16[776,128]{1,0:T(8,128)(2,1)S(1)}, bf16[776,128]{1,0:T(8,128)(2,1)S(1)}, u32[]{:S(2)}, u32[]{:S(2)}) %collective-permute-start.7) | collective-permute-done | bytes 198688 | tf_op jit(solution)/shard_map/ppermute | solution.py:469
  16.7 2.0 %collective-permute-start.10 = (bf16[776,128]{1,0:T(8,128)(2,1)S(1)}, bf16[776,128]{1,0:T(8,128)(2,1)S(1)}, u32[]{:S(2)}, u32[]{:S(2)}) collective-permute-start(bf16[776,128]{1,0:T(8,128)(2,1)S(1)} %collective-permute-done.6.refs_4_), channel_id=1, source_target_pairs={{0,8},{2,10},{8,16},{10,18},{16,24},{18,26},{24,28},{26,30},{28,20... | collective-permute-start | bytes 595976 | tf_op jit(solution)/shard_map/ppermute | solution.py:468
  18.7 2.5 %attend.8 = (f32[8,1,480]{2,1,0:T(1,128)S(1)}, f32[8,144,480]{2,1,0:T(8,128)S(1)}) custom-call(bf16[8,128,480]{2,1,0:T(8,128)(2,1)S(1)} %turn.1.refs_0_, bf16[776,128]{1,0:T(8,128)(2,1)S(1)} %get-tuple-element.52.refs_1_.refs_3_, bf16[776,128]{1,0:T(8,128)(2,1)S(1)} %collective-permute-done.1.refs_2_.refs_4_, ...), custom_call_target="tpu_custom_call" | custom-call | flops 754974720 | bytes 4194304 | tf_op jit(solution)/shard_map/attend/pallas_call | solution.py:280
  21.3 0.3 collective-permute-done.5.refs_6_
  21.6 1.7 %collective-permute-start.8 = (bf16[776,128]{1,0:T(8,128)(2,1)S(1)}, bf16[776,128]{1,0:T(8,128)(2,1)S(1)}, u32[]{:S(2)}, u32[]{:S(2)}) collective-permute-start(bf16[776,128]{1,0:T(8,128)(2,1)S(1)} %collective-permute-done.4.refs_3_), channel_id=1, source_target_pairs={{0,8},{2,10},{8,16},{10,18},{16,24},{18,26},{24,28},{26,30},{28,20... | collective-permute-start | bytes 595976 | tf_op jit(solution)/shard_map/ppermute | solution.py:468
  23.3 0.3 collective-permute-start.9
  23.6 2.0 %collective-permute-done.11.refs_5_ = bf16[776,128]{1,0:T(8,128)(2,1)S(1)} collective-permute-done((bf16[776,128]{1,0:T(8,128)(2,1)S(1)}, bf16[776,128]{1,0:T(8,128)(2,1)S(1)}, u32[]{:S(2)}, u32[]{:S(2)}) %collective-permute-start.11) | collective-permute-done | bytes 198688 | tf_op jit(solution)/shard_map/ppermute | solution.py:469
  25.6 0.2 collective-permute-start.15
  25.8 1.8 %collective-permute-start.14 = (bf16[776,128]{1,0:T(8,128)(2,1)S(1)}, bf16[776,128]{1,0:T(8,128)(2,1)S(1)}, u32[]{:S(2)}, u32[]{:S(2)}) collective-permute-start(bf16[776,128]{1,0:T(8,128)(2,1)S(1)} %collective-permute-done.10.refs_4_), channel_id=1, source_target_pairs={{0,8},{2,10},{8,16},{10,18},{16,24},{18,26},{24,28},{26,30},{28,20... | collective-permute-start | bytes 595976 | tf_op jit(solution)/shard_map/ppermute | solution.py:468
  27.6 3.1 %attend.9 = (f32[8,1,480]{2,1,0:T(1,128)S(1)}, f32[8,144,480]{2,1,0:T(8,128)S(1)}, bf16[2560,1280]{1,0:T(8,128)(2,1)S(1)}) custom-call(bf16[8,128,480]{2,1,0:T(8,128)(2,1)S(1)} %turn.1.refs_0_, bf16[776,128]{1,0:T(8,128)(2,1)S(1)} %get-tuple-element.52.refs_1_.refs_3_, bf16[776,128]{1,0:T(8,128)(2,1)S(1)} %collective-permute-done.1.refs_2_.refs_4_, ...), custom_call_target="tpu_custom_call" | custom-call | flops 754974720 | bytes 4194304 | tf_op jit(solution)/shard_map/attend/pallas_call | solution.py:280
  30.8 0.4 collective-permute-done.9.refs_6_
  31.2 1.6 %collective-permute-start.12 = (bf16[776,128]{1,0:T(8,128)(2,1)S(1)}, bf16[776,128]{1,0:T(8,128)(2,1)S(1)}, u32[]{:S(2)}, u32[]{:S(2)}) collective-permute-start(bf16[776,128]{1,0:T(8,128)(2,1)S(1)} %collective-permute-done.8.refs_3_), channel_id=1, source_target_pairs={{0,8},{2,10},{8,16},{10,18},{16,24},{18,26},{24,28},{26,30},{28,20... | collective-permute-start | bytes 595976 | tf_op jit(solution)/shard_map/ppermute | solution.py:468
  32.8 0.4 collective-permute-start.13
  33.2 0.6 collective-permute-done.15.refs_5_
  33.8 3.1 %attend.10 = (f32[8,1,480]{2,1,0:T(1,128)S(1)}, f32[8,144,480]{2,1,0:T(8,128)S(1)}, bf16[2560,1152]{1,0:T(8,128)(2,1)S(1)}) custom-call(bf16[8,128,480]{2,1,0:T(8,128)(2,1)S(1)} %turn.1.refs_0_, bf16[776,128]{1,0:T(8,128)(2,1)S(1)} %get-tuple-element.52.refs_1_.refs_3_, bf16[776,128]{1,0:T(8,128)(2,1)S(1)} %collective-permute-done.1.refs_2_.refs_4_, ...), custom_call_target="tpu_custom_call" | custom-call | flops 754974720 | bytes 4194304 | tf_op jit(solution)/shard_map/attend/pallas_call | solution.py:280
  37.0 1.5 %collective-permute-done.13.refs_4_ = bf16[776,128]{1,0:T(8,128)(2,1)S(1)} collective-permute-done((bf16[776,128]{1,0:T(8,128)(2,1)S(1)}, bf16[776,128]{1,0:T(8,128)(2,1)S(1)}, u32[]{:S(2)}, u32[]{:S(2)}) %collective-permute-start.13) | collective-permute-done | bytes 198688 | tf_op jit(solution)/shard_map/ppermute | solution.py:469
  38.5 1.0 %attend.12 = bf16[192,1280]{1,0:T(8,128)(2,1)S(1)} custom-call(bf16[8,128,480]{2,1,0:T(8,128)(2,1)S(1)} %turn.1.refs_0_, bf16[776,128]{1,0:T(8,128)(2,1)S(1)} %get-tuple-element.52.refs_1_.refs_3_, bf16[776,128]{1,0:T(8,128)(2,1)S(1)} %collective-permute-done.1.refs_2_.refs_4_, bf16[776,128]{1,0:T(8,128)(2,1)S(1)} %collective-permute-done.12.refs_3_, ...), custom_call_target="tpu_custom_call" | custom-call | flops 377487360 | bytes 4194304 | tf_op jit(solution)/shard_map/attend/pallas_call | solution.py:280
  39.6 1.0 %attend.11.own_ref.refs_0_ = bf16[96,1280]{1,0:T(8,128)(2,1)S(1)} custom-call(bf16[8,128,480]{2,1,0:T(8,128)(2,1)S(1)} %turn.1.refs_0_, bf16[776,128]{1,0:T(8,128)(2,1)S(1)} %get-tuple-element.52.refs_1_.refs_3_, bf16[776,128]{1,0:T(8,128)(2,1)S(1)} %collective-permute-done.1.refs_2_.refs_4_, bf16[776,128]{1,0:T(8,128)(2,1)S(1)} %collective-permute-done.12.refs_3_, ...), custom_call_target="tpu_custom_call" | custom-call | flops 377487360 | bytes 4194304 | tf_op jit(solution)/shard_map/attend/pallas_call | solution.py:280
  40.6 0.7 %multiply.7.begun_ref = f32[96,1280]{1,0:T(8,128)S(1)} custom-call(bf16[96,1280]{1,0:T(8,128)(2,1)S(1)} %attend.11.own_ref.refs_0_, bf16[2560,1280]{1,0:T(8,128)(2,1)S(1)} %get-tuple-element.74.held_ref), custom_call_target="tpu_custom_call" | custom-call | flops 1024 | bytes 1024 | tf_op jit(solution)/shard_map/multiply/pallas_call | solution.py:369
  41.3 0.7 %multiply.8 = bf16[96,1280]{1,0:T(8,128)(2,1)S(1)} custom-call(bf16[96,1280]{1,0:T(8,128)(2,1)S(1)} %collective-permute-done.16.other_ref.refs_1_, bf16[2560,1280]{1,0:T(8,128)(2,1)S(1)} %get-tuple-element.74.held_ref, f32[96,1280]{1,0:T(8,128)S(1)} %multiply.7.begun_ref), custom_call_target="tpu_custom_call" | custom-call | flops 1024 | bytes 1024 | tf_op jit(solution)/shard_map/multiply/pallas_call | solution.py:369
  42.1 0.6 collective-permute-start.17
  42.6 1.2 %collective-permute-start.19 = (bf16[96,1280]{1,0:T(8,128)(2,1)S(1)}, bf16[96,1280]{1,0:T(8,128)(2,1)S(1)}, u32[]{:S(2)}, u32[]{:S(2)}) collective-permute-start(bf16[96,1280]{1,0:T(8,128)(2,1)S(1)} %multiply.8), channel_id=1, source_target_pairs={{0,1},{1,0},{2,3},{3,2},{4,5},{5,4},{6,7},{7,6},{8,9},{9,8},{10,11... | collective-permute-start | bytes 737288 | tf_op jit(solution)/shard_map/ppermute | solution.py:590
  43.8 0.9 %attend.13.refs_2_.own_ref = bf16[96,1280]{1,0:T(8,128)(2,1)S(1)} custom-call(bf16[8,128,480]{2,1,0:T(8,128)(2,1)S(1)} %turn.1.refs_0_, bf16[776,128]{1,0:T(8,128)(2,1)S(1)} %get-tuple-element.52.refs_1_.refs_3_, bf16[776,128]{1,0:T(8,128)(2,1)S(1)} %collective-permute-done.1.refs_2_.refs_4_, bf16[776,128]{1,0:T(8,128)(2,1)S(1)} %collective-permute-done.12.refs_3_, ...), custom_call_target="tpu_custom_call" | custom-call | flops 377487360 | bytes 4194304 | tf_op jit(solution)/shard_map/attend/pallas_call | solution.py:280
  44.8 2.9 %multiply.9 = (bf16[96,1152]{1,0:T(8,128)(2,1)S(1)}, bf16[96,1152]{1,0:T(8,128)(2,1)S(1)}, bf16[2560,896]{1,0:T(8,128)(2,1)S(1)}) custom-call(bf16[96,1280]{1,0:T(8,128)(2,1)S(1)} %attend.11.own_ref.refs_0_, bf16[96,1280]{1,0:T(8,128)(2,1)S(1)} %collective-permute-done.16.other_ref.refs_1_, bf16[96,1280]{1,0:T(8,128)(2,1)S(1)} %attend.13.refs_2_.own_ref, ...), custom_call_target="tpu_custom_call" | custom-call | flops 1024 | bytes 1024 | tf_op jit(solution)/shard_map/multiply/pallas_call | solution.py:369
  47.7 1.2 %collective-permute-start.20 = (bf16[96,1152]{1,0:T(8,128)(2,1)S(1)}, bf16[96,1152]{1,0:T(8,128)(2,1)S(1)}, u32[]{:S(2)}, u32[]{:S(2)}) collective-permute-start(bf16[96,1152]{1,0:T(8,128)(2,1)S(1)} %get-tuple-element.80), channel_id=1, source_target_pairs={{0,1},{1,0},{2,3},{3,2},{4,5},{5,4},{6,7},{7,6},{8,9},{9,8},{10,11... | collective-permute-start | bytes 663560 | tf_op jit(solution)/shard_map/ppermute | solution.py:590
  48.9 2.5 %multiply.10 = (bf16[96,1024]{1,0:T(8,128)(2,1)S(1)}, bf16[96,1024]{1,0:T(8,128)(2,1)S(1)}, bf16[2560,768]{1,0:T(8,128)(2,1)S(1)}) custom-call(bf16[96,1280]{1,0:T(8,128)(2,1)S(1)} %attend.11.own_ref.refs_0_, bf16[96,1280]{1,0:T(8,128)(2,1)S(1)} %collective-permute-done.16.other_ref.refs_1_, bf16[96,1280]{1,0:T(8,128)(2,1)S(1)} %attend.13.refs_2_.own_ref, ...), custom_call_target="tpu_custom_call" | custom-call | flops 1024 | bytes 1024 | tf_op jit(solution)/shard_map/multiply/pallas_call | solution.py:369
  51.4 1.0 %collective-permute-start.21 = (bf16[96,1024]{1,0:T(8,128)(2,1)S(1)}, bf16[96,1024]{1,0:T(8,128)(2,1)S(1)}, u32[]{:S(2)}, u32[]{:S(2)}) collective-permute-start(bf16[96,1024]{1,0:T(8,128)(2,1)S(1)} %get-tuple-element.83), channel_id=1, source_target_pairs={{0,1},{1,0},{2,3},{3,2},{4,5},{5,4},{6,7},{7,6},{8,9},{9,8},{10,11... | collective-permute-start | bytes 589832 | tf_op jit(solution)/shard_map/ppermute | solution.py:590
  52.4 1.2 %multiply.11 = (bf16[96,896]{1,0:T(8,128)(2,1)S(1)}, bf16[96,896]{1,0:T(8,128)(2,1)S(1)}) custom-call(bf16[96,1280]{1,0:T(8,128)(2,1)S(1)} %attend.11.own_ref.refs_0_, bf16[96,1280]{1,0:T(8,128)(2,1)S(1)} %collective-permute-done.16.other_ref.refs_1_, bf16[96,1280]{1,0:T(8,128)(2,1)S(1)} %attend.13.refs_2_.own_ref, ...), custom_call_target="tpu_custom_call" | custom-call | flops 1024 | bytes 1024 | tf_op jit(solution)/shard_map/multiply/pallas_call | solution.py:369
  53.6 1.2 %collective-permute-start.22 = (bf16[96,896]{1,0:T(8,128)(2,1)S(1)}, bf16[96,896]{1,0:T(8,128)(2,1)S(1)}, u32[]{:S(2)}, u32[]{:S(2)}) collective-permute-start(bf16[96,896]{1,0:T(8,128)(2,1)S(1)} %get-tuple-element.86), channel_id=1, source_target_pairs={{0,1},{1,0},{2,3},{3,2},{4,5},{5,4},{6,7},{7,6},{8,9},{9,8},{10,11... | collective-permute-start | bytes 516104 | tf_op jit(solution)/shard_map/ppermute | solution.py:590
  54.8 0.9 %multiply.12 = (bf16[96,768]{1,0:T(8,128)(2,1)S(1)}, bf16[96,768]{1,0:T(8,128)(2,1)S(1)}) custom-call(bf16[96,1280]{1,0:T(8,128)(2,1)S(1)} %attend.11.own_ref.refs_0_, bf16[96,1280]{1,0:T(8,128)(2,1)S(1)} %collective-permute-done.16.other_ref.refs_1_, bf16[96,1280]{1,0:T(8,128)(2,1)S(1)} %attend.13.refs_2_.own_ref, ...), custom_call_target="tpu_custom_call" | custom-call | flops 1024 | bytes 1024 | tf_op jit(solution)/shard_map/multiply/pallas_call | solution.py:369
  55.7 1.0 %collective-permute-start.18 = (bf16[96,768]{1,0:T(8,128)(2,1)S(1)}, bf16[96,768]{1,0:T(8,128)(2,1)S(1)}, u32[]{:S(2)}, u32[]{:S(2)}) collective-permute-start(bf16[96,768]{1,0:T(8,128)(2,1)S(1)} %get-tuple-element.90), channel_id=1, source_target_pairs={{0,1},{1,0},{2,3},{3,2},{4,5},{5,4},{6,7},{7,6},{8,9},{9,8},{10,11... | collective-permute-start | bytes 442376 | tf_op jit(solution)/shard_map/ppermute | solution.py:590
  56.7 1.2 %multiply.13.refs_0_ = bf16[96,1280]{1,0:T(8,128)(2,1)S(1)} custom-call(bf16[96,1280]{1,0:T(8,128)(2,1)S(1)} %attend.13.refs_2_.own_ref, bf16[96,1280]{1,0:T(8,128)(2,1)S(1)} %collective-permute-done.17.refs_3_.other_ref, bf16[2560,1280]{1,0:T(8,128)(2,1)S(1)} %get-tuple-element.74.held_ref), custom_call_target="tpu_custom_call" | custom-call | flops 1024 | bytes 1024 | tf_op jit(solution)/shard_map/multiply/pallas_call | solution.py:369
  58.0 6.1 %collective-permute-done.22.refs_7_ = bf16[96,896]{1,0:T(8,128)(2,1)S(1)} collective-permute-done((bf16[96,896]{1,0:T(8,128)(2,1)S(1)}, bf16[96,896]{1,0:T(8,128)(2,1)S(1)}, u32[]{:S(2)}, u32[]{:S(2)}) %collective-permute-start.22) | collective-permute-done | bytes 172064 | tf_op jit(solution)/shard_map/ppermute | solution.py:590
  64.0 1.1 %finish.2.refs_2_ = bf16[96,5120]{1,0:T(8,128)(2,1)} custom-call(bf16[96,1280]{1,0:T(8,128)(2,1)S(1)} %multiply.13.refs_0_, bf16[96,1152]{1,0:T(8,128)(2,1)S(1)} %get-tuple-element.92.refs_1_, bf16[96,1024]{1,0:T(8,128)(2,1)S(1)} %get-tuple-element.93.refs_2_, bf16[96,896]{1,0:T(8,128)(2,1)S(1)} %get-tuple-element.94.refs_3_, ...), custom_call_target="tpu_custom_call" | custom-call | flops 1024 | bytes 1024 | tf_op jit(solution)/shard_map/finish/pallas_call | solution.py:445
  65.1 1.2 %collective-permute-done.18.refs_1_ = bf16[96,768]{1,0:T(8,128)(2,1)S(1)} collective-permute-done((bf16[96,768]{1,0:T(8,128)(2,1)S(1)}, bf16[96,768]{1,0:T(8,128)(2,1)S(1)}, u32[]{:S(2)}, u32[]{:S(2)}) %collective-permute-start.18) | collective-permute-done | bytes 147488 | tf_op jit(solution)/shard_map/ppermute | solution.py:590
  66.4 0.7 %finish.3 = bf16[96,5120]{1,0:T(8,128)(2,1)} custom-call(bf16[96,768]{1,0:T(8,128)(2,1)S(1)} %get-tuple-element.89.refs_0_, bf16[96,768]{1,0:T(8,128)(2,1)S(1)} %collective-permute-done.18.refs_1_, bf16[96,5120]{1,0:T(8,128)(2,1)} %finish.2.refs_2_), custom_call_target="tpu_custom_call", output_to_operand_aliasing={{}: (2, {})} | custom-call | flops 1024 | bytes 1024 | tf_op jit(solution)/shard_map/finish/pallas_call | solution.py:445
  (17 shorter events, 0.1 us)
Async XLA Ops:
  1.5 5.0 %collective-permute-start = (bf16[192,1280]{1,0:T(8,128)(2,1)S(1)}, bf16[192,1280]{1,0:T(8,128)(2,1)S(1)}, u32[]{:S(2)}, u32[]{:S(2)}) collective-permute-start(bf16[192,1280]{1,0:T(8,128)(2,1)S(1)} %get-tuple-element.51), channel_id=1, source_target_pairs={{0,2},{2,0},{4,6},{6,4},{8,10},{10,8},{12,14},{14,12},{16,18},{18,... | collective-permute-start | bytes 1474568 | tf_op jit(solution)/shard_map/ppermute | solution.py:474
  2.0 5.2 %collective-permute-start.1 = (bf16[776,128]{1,0:T(8,128)(2,1)S(1)}, bf16[776,128]{1,0:T(8,128)(2,1)S(1)}, u32[]{:S(2)}, u32[]{:S(2)}) collective-permute-start(bf16[776,128]{1,0:T(8,128)(2,1)S(1)} %get-tuple-element.53), channel_id=1, source_target_pairs={{0,2},{2,0},{4,6},{6,4},{8,10},{10,8},{12,14},{14,12},{16,18},{18,... | collective-permute-start | bytes 595976 | tf_op jit(solution)/shard_map/ppermute | solution.py:473
  2.1 8.7 %collective-permute-start.2 = (bf16[776,128]{1,0:T(8,128)(2,1)S(1)}, bf16[776,128]{1,0:T(8,128)(2,1)S(1)}, u32[]{:S(2)}, u32[]{:S(2)}) collective-permute-start(bf16[776,128]{1,0:T(8,128)(2,1)S(1)} %get-tuple-element.52.refs_1_.refs_3_), channel_id=1, source_target_pairs={{0,8},{2,10},{8,16},{10,18},{16,24},{18,26},{24,28},{26,30},{28,20... | collective-permute-start | bytes 595976 | tf_op jit(solution)/shard_map/ppermute | solution.py:468
  5.1 7.1 %collective-permute-start.3 = (bf16[776,128]{1,0:T(8,128)(2,1)S(1)}, bf16[776,128]{1,0:T(8,128)(2,1)S(1)}, u32[]{:S(2)}, u32[]{:S(2)}) collective-permute-start(bf16[776,128]{1,0:T(8,128)(2,1)S(1)} %get-tuple-element.53), channel_id=1, source_target_pairs={{0,6},{2,4},{8,2},{10,0},{16,10},{18,8},{24,18},{26,16},{28,26},{3... | collective-permute-start | bytes 595976 | tf_op jit(solution)/shard_map/ppermute | solution.py:509
  5.1 11.6 %collective-permute-start.7 = (bf16[776,128]{1,0:T(8,128)(2,1)S(1)}, bf16[776,128]{1,0:T(8,128)(2,1)S(1)}, u32[]{:S(2)}, u32[]{:S(2)}) collective-permute-start(bf16[776,128]{1,0:T(8,128)(2,1)S(1)} %get-tuple-element.52.refs_1_.refs_3_), channel_id=1, source_target_pairs={{0,4},{2,6},{8,0},{10,2},{16,8},{18,10},{24,16},{26,18},{28,24},{3... | collective-permute-start | bytes 595976 | tf_op jit(solution)/shard_map/ppermute | solution.py:469
  6.5 10.2 %collective-permute-start.6 = (bf16[776,128]{1,0:T(8,128)(2,1)S(1)}, bf16[776,128]{1,0:T(8,128)(2,1)S(1)}, u32[]{:S(2)}, u32[]{:S(2)}) collective-permute-start(bf16[776,128]{1,0:T(8,128)(2,1)S(1)} %get-tuple-element.53), channel_id=1, source_target_pairs={{0,10},{2,8},{8,18},{10,16},{16,26},{18,24},{24,30},{26,28},{28,22... | collective-permute-start | bytes 595976 | tf_op jit(solution)/shard_map/ppermute | solution.py:508
  12.2 9.0 %collective-permute-start.4 = (bf16[776,128]{1,0:T(8,128)(2,1)S(1)}, bf16[776,128]{1,0:T(8,128)(2,1)S(1)}, u32[]{:S(2)}, u32[]{:S(2)}) collective-permute-start(bf16[776,128]{1,0:T(8,128)(2,1)S(1)} %collective-permute-done.2.refs_3_), channel_id=1, source_target_pairs={{0,8},{2,10},{8,16},{10,18},{16,24},{18,26},{24,28},{26,30},{28,20... | collective-permute-start | bytes 595976 | tf_op jit(solution)/shard_map/ppermute | solution.py:468
  13.8 7.8 %collective-permute-start.5 = (bf16[776,128]{1,0:T(8,128)(2,1)S(1)}, bf16[776,128]{1,0:T(8,128)(2,1)S(1)}, u32[]{:S(2)}, u32[]{:S(2)}) collective-permute-start(bf16[776,128]{1,0:T(8,128)(2,1)S(1)} %collective-permute-done.3.refs_6_), channel_id=1, source_target_pairs={{0,4},{2,6},{8,0},{10,2},{16,8},{18,10},{24,16},{26,18},{28,24},{3... | collective-permute-start | bytes 595976 | tf_op jit(solution)/shard_map/ppermute | solution.py:469
  16.7 8.9 %collective-permute-start.11 = (bf16[776,128]{1,0:T(8,128)(2,1)S(1)}, bf16[776,128]{1,0:T(8,128)(2,1)S(1)}, u32[]{:S(2)}, u32[]{:S(2)}) collective-permute-start(bf16[776,128]{1,0:T(8,128)(2,1)S(1)} %collective-permute-done.7.refs_5_), channel_id=1, source_target_pairs={{0,4},{2,6},{8,0},{10,2},{16,8},{18,10},{24,16},{26,18},{28,24},{3... | collective-permute-start | bytes 595976 | tf_op jit(solution)/shard_map/ppermute | solution.py:469
  16.7 9.1 %collective-permute-start.10 = (bf16[776,128]{1,0:T(8,128)(2,1)S(1)}, bf16[776,128]{1,0:T(8,128)(2,1)S(1)}, u32[]{:S(2)}, u32[]{:S(2)}) collective-permute-start(bf16[776,128]{1,0:T(8,128)(2,1)S(1)} %collective-permute-done.6.refs_4_), channel_id=1, source_target_pairs={{0,8},{2,10},{8,16},{10,18},{16,24},{18,26},{24,28},{26,30},{28,20... | collective-permute-start | bytes 595976 | tf_op jit(solution)/shard_map/ppermute | solution.py:468
  21.6 9.1 %collective-permute-start.8 = (bf16[776,128]{1,0:T(8,128)(2,1)S(1)}, bf16[776,128]{1,0:T(8,128)(2,1)S(1)}, u32[]{:S(2)}, u32[]{:S(2)}) collective-permute-start(bf16[776,128]{1,0:T(8,128)(2,1)S(1)} %collective-permute-done.4.refs_3_), channel_id=1, source_target_pairs={{0,8},{2,10},{8,16},{10,18},{16,24},{18,26},{24,28},{26,30},{28,20... | collective-permute-start | bytes 595976 | tf_op jit(solution)/shard_map/ppermute | solution.py:468
  23.3 7.9 %collective-permute-start.9 = (bf16[776,128]{1,0:T(8,128)(2,1)S(1)}, bf16[776,128]{1,0:T(8,128)(2,1)S(1)}, u32[]{:S(2)}, u32[]{:S(2)}) collective-permute-start(bf16[776,128]{1,0:T(8,128)(2,1)S(1)} %collective-permute-done.5.refs_6_), channel_id=1, source_target_pairs={{0,4},{2,6},{8,0},{10,2},{16,8},{18,10},{24,16},{26,18},{28,24},{3... | collective-permute-start | bytes 595976 | tf_op jit(solution)/shard_map/ppermute | solution.py:469
  25.6 8.2 %collective-permute-start.15 = (bf16[776,128]{1,0:T(8,128)(2,1)S(1)}, bf16[776,128]{1,0:T(8,128)(2,1)S(1)}, u32[]{:S(2)}, u32[]{:S(2)}) collective-permute-start(bf16[776,128]{1,0:T(8,128)(2,1)S(1)} %collective-permute-done.11.refs_5_), channel_id=1, source_target_pairs={{0,4},{2,6},{8,0},{10,2},{16,8},{18,10},{24,16},{26,18},{28,24},{3... | collective-permute-start | bytes 595976 | tf_op jit(solution)/shard_map/ppermute | solution.py:469
  25.8 8.0 %collective-permute-start.14 = (bf16[776,128]{1,0:T(8,128)(2,1)S(1)}, bf16[776,128]{1,0:T(8,128)(2,1)S(1)}, u32[]{:S(2)}, u32[]{:S(2)}) collective-permute-start(bf16[776,128]{1,0:T(8,128)(2,1)S(1)} %collective-permute-done.10.refs_4_), channel_id=1, source_target_pairs={{0,8},{2,10},{8,16},{10,18},{16,24},{18,26},{24,28},{26,30},{28,20... | collective-permute-start | bytes 595976 | tf_op jit(solution)/shard_map/ppermute | solution.py:468
  31.2 5.7 %collective-permute-start.12 = (bf16[776,128]{1,0:T(8,128)(2,1)S(1)}, bf16[776,128]{1,0:T(8,128)(2,1)S(1)}, u32[]{:S(2)}, u32[]{:S(2)}) collective-permute-start(bf16[776,128]{1,0:T(8,128)(2,1)S(1)} %collective-permute-done.8.refs_3_), channel_id=1, source_target_pairs={{0,8},{2,10},{8,16},{10,18},{16,24},{18,26},{24,28},{26,30},{28,20... | collective-permute-start | bytes 595976 | tf_op jit(solution)/shard_map/ppermute | solution.py:468
  32.8 5.7 %collective-permute-start.13 = (bf16[776,128]{1,0:T(8,128)(2,1)S(1)}, bf16[776,128]{1,0:T(8,128)(2,1)S(1)}, u32[]{:S(2)}, u32[]{:S(2)}) collective-permute-start(bf16[776,128]{1,0:T(8,128)(2,1)S(1)} %collective-permute-done.9.refs_6_), channel_id=1, source_target_pairs={{0,4},{2,6},{8,0},{10,2},{16,8},{18,10},{24,16},{26,18},{28,24},{3... | collective-permute-start | bytes 595976 | tf_op jit(solution)/shard_map/ppermute | solution.py:469
  39.5 1.8 %collective-permute-start.16 = (bf16[96,1280]{1,0:T(8,128)(2,1)S(1)}, bf16[96,1280]{1,0:T(8,128)(2,1)S(1)}, u32[]{:S(2)}, u32[]{:S(2)}) collective-permute-start(bf16[96,1280]{1,0:T(8,128)(2,1)S(1)} %get-tuple-element.96), channel_id=1, source_target_pairs={{0,2},{2,0},{4,6},{6,4},{8,10},{10,8},{12,14},{14,12},{16,18},{18,... | collective-permute-start | bytes 737288 | tf_op jit(solution)/shard_map/ppermute | solution.py:520
  42.1 2.7 %collective-permute-start.17 = (bf16[96,1280]{1,0:T(8,128)(2,1)S(1)}, bf16[96,1280]{1,0:T(8,128)(2,1)S(1)}, u32[]{:S(2)}, u32[]{:S(2)}) collective-permute-start(bf16[96,1280]{1,0:T(8,128)(2,1)S(1)} %get-tuple-element.78), channel_id=1, source_target_pairs={{0,2},{2,0},{4,6},{6,4},{8,10},{10,8},{12,14},{14,12},{16,18},{18,... | collective-permute-start | bytes 737288 | tf_op jit(solution)/shard_map/ppermute | solution.py:524
  42.6 15.3 %collective-permute-start.19 = (bf16[96,1280]{1,0:T(8,128)(2,1)S(1)}, bf16[96,1280]{1,0:T(8,128)(2,1)S(1)}, u32[]{:S(2)}, u32[]{:S(2)}) collective-permute-start(bf16[96,1280]{1,0:T(8,128)(2,1)S(1)} %multiply.8), channel_id=1, source_target_pairs={{0,1},{1,0},{2,3},{3,2},{4,5},{5,4},{6,7},{7,6},{8,9},{9,8},{10,11... | collective-permute-start | bytes 737288 | tf_op jit(solution)/shard_map/ppermute | solution.py:590
  47.7 16.3 %collective-permute-start.20 = (bf16[96,1152]{1,0:T(8,128)(2,1)S(1)}, bf16[96,1152]{1,0:T(8,128)(2,1)S(1)}, u32[]{:S(2)}, u32[]{:S(2)}) collective-permute-start(bf16[96,1152]{1,0:T(8,128)(2,1)S(1)} %get-tuple-element.80), channel_id=1, source_target_pairs={{0,1},{1,0},{2,3},{3,2},{4,5},{5,4},{6,7},{7,6},{8,9},{9,8},{10,11... | collective-permute-start | bytes 663560 | tf_op jit(solution)/shard_map/ppermute | solution.py:590
  51.4 12.6 %collective-permute-start.21 = (bf16[96,1024]{1,0:T(8,128)(2,1)S(1)}, bf16[96,1024]{1,0:T(8,128)(2,1)S(1)}, u32[]{:S(2)}, u32[]{:S(2)}) collective-permute-start(bf16[96,1024]{1,0:T(8,128)(2,1)S(1)} %get-tuple-element.83), channel_id=1, source_target_pairs={{0,1},{1,0},{2,3},{3,2},{4,5},{5,4},{6,7},{7,6},{8,9},{9,8},{10,11... | collective-permute-start | bytes 589832 | tf_op jit(solution)/shard_map/ppermute | solution.py:590
  53.6 10.4 %collective-permute-start.22 = (bf16[96,896]{1,0:T(8,128)(2,1)S(1)}, bf16[96,896]{1,0:T(8,128)(2,1)S(1)}, u32[]{:S(2)}, u32[]{:S(2)}) collective-permute-start(bf16[96,896]{1,0:T(8,128)(2,1)S(1)} %get-tuple-element.86), channel_id=1, source_target_pairs={{0,1},{1,0},{2,3},{3,2},{4,5},{5,4},{6,7},{7,6},{8,9},{9,8},{10,11... | collective-permute-start | bytes 516104 | tf_op jit(solution)/shard_map/ppermute | solution.py:590
  55.7 10.6 %collective-permute-start.18 = (bf16[96,768]{1,0:T(8,128)(2,1)S(1)}, bf16[96,768]{1,0:T(8,128)(2,1)S(1)}, u32[]{:S(2)}, u32[]{:S(2)}) collective-permute-start(bf16[96,768]{1,0:T(8,128)(2,1)S(1)} %get-tuple-element.90), channel_id=1, source_target_pairs={{0,1},{1,0},{2,3},{3,2},{4,5},{5,4},{6,7},{7,6},{8,9},{9,8},{10,11... | collective-permute-start | bytes 442376 | tf_op jit(solution)/shard_map/ppermute | solution.py:590

commit v19 on v17

--- a/solution.py
+++ b/solution.py
@@ -561,7 +561,7 @@
             partial.astype(jnp.bfloat16), "inner", scatter_dimension=0, tiled=True
         )
     out_weight = pltpu.with_memory_space_constraint(out_weight, pltpu.HBM)
-    shares = (10, 9, 8, 7, 6)
+    shares = (11, 10, 8, 6, 5)
     widths = [out_weight.shape[1] * share // sum(shares) for share in shares]
     cuts = [(sum(widths[:j]), columns) for j, columns in enumerate(widths)]
     own, (other, other_kept), held, own_to_keep = split_over_cores(

time: 67.4 us -> 67.5 us (level)
  Pallas kernels: 28.1 us -> 27.3 us
  waiting for transfers between devices: 17.1 us -> 17.9 us
    ppermute x5, waiting for transfers between devices: 7.29 us -> 8.24 us  [shards(): received.append(lax.ppermute(sent, 'inner', [(0, 1), (1, 0)]))]
    pallas_call x7, Pallas kernels: 10.2 us -> 9.35 us  [multiply(): pl.pallas_call(kernel, out_shape=[jax.ShapeDtypeStruct(shape, kind) for s...]
  transfers between devices with their start and end apart: 23 -> 23, of which waited for: 10 -> 10; matrix products, arithmetic and copies ran while one was open for 0% -> 0% of each run, Pallas kernels for 37% -> 36%
where the time goes in v19:
time: 67.5 us; the launch traced here: 67.3 us
  Pallas kernels  27.3 us (40%)
  starting transfers between devices  21.7 us (32%)
  waiting for transfers between devices  17.9 us (27%)
    pallas_call x7, Pallas kernels, attend(): pl.pallas_call(functools.partial(attend_kernel, plan), out_shape=out_shap...  14.3 us
    ppermute x6, starting transfers between devices, split_over_cores(): up = lambda x: lax.ppermute(x, 'blk', clock)  11.7 us
    pallas_call x7, Pallas kernels, multiply(): pl.pallas_call(kernel, out_shape=[jax.ShapeDtypeStruct(shape, kind) for s...  9.35 us
    ppermute x5, waiting for transfers between devices, shards(): received.append(lax.ppermute(sent, 'inner', [(0, 1), (1, 0)]))  8.24 us
    ppermute x6, waiting for transfers between devices, split_over_cores(): down = lambda x: lax.ppermute(x, 'blk', counter)  7.23 us
    ppermute x5, starting transfers between devices, shards(): received.append(lax.ppermute(sent, 'inner', [(0, 1), (1, 0)]))  5.62 us
    ppermute x6, starting transfers between devices, split_over_cores(): down = lambda x: lax.ppermute(x, 'blk', counter)  2.78 us
    pallas_call x2, Pallas kernels, finish(): pl.pallas_call(functools.partial(finish_kernel, first, pairs), out_shape=...  1.8 us
  transfers between devices with their start and end apart: 23, of which 10 were waited for; matrix products, arithmetic and copies ran while one was open for 0% of the time, Pallas kernels for 36%

profile of v19, /device:TPU:0, one launch (start us, length us, event | category | flops | bytes accessed | tf_op | source)
XLA Modules:
  0.0 67.3 jit_solution(7600118759610075266)
XLA Ops:
  0.0 1.5 %prepare.1 = (bf16[776,128]{1,0:T(8,128)(2,1)S(1)}, bf16[776,128]{1,0:T(8,128)(2,1)S(1)}, bf16[192,1280]{1,0:T(8,128)(2,1)S(1)}, bf16[192,1280]{1,0:T(8,128)(2,1)S(1)}) custom-call(bf16[192,2560]{1,0:T(8,128)(2,1)} %q_ref.1, bf16[192,512]{1,0:T(8,128)(2,1)} %k_ref.1, bf16[192,512]{1,0:T(8,128)(2,1)} %v_ref.1, s32[192]{0:T(256)} %position_ref.1), custom_call_target="tpu_custom_call" | custom-call | tf_op jit(solution)/shard_map/prepare/pallas_call | solution.py:413
  1.5 0.5 collective-permute-start
  2.0 0.1 collective-permute-start.1
  2.1 3.0 %collective-permute-start.2 = (bf16[776,128]{1,0:T(8,128)(2,1)S(1)}, bf16[776,128]{1,0:T(8,128)(2,1)S(1)}, u32[]{:S(2)}, u32[]{:S(2)}) collective-permute-start(bf16[776,128]{1,0:T(8,128)(2,1)S(1)} %get-tuple-element.51.refs_1_.refs_3_), channel_id=1, source_target_pairs={{0,8},{2,10},{8,16},{10,18},{16,24},{18,26},{24,28},{26,30},{28,20... | collective-permute-start | bytes 595976 | tf_op jit(solution)/shard_map/ppermute | solution.py:468
  5.1 1.4 %collective-permute-start.7 = (bf16[776,128]{1,0:T(8,128)(2,1)S(1)}, bf16[776,128]{1,0:T(8,128)(2,1)S(1)}, u32[]{:S(2)}, u32[]{:S(2)}) collective-permute-start(bf16[776,128]{1,0:T(8,128)(2,1)S(1)} %get-tuple-element.51.refs_1_.refs_3_), channel_id=1, source_target_pairs={{0,4},{2,6},{8,0},{10,2},{16,8},{18,10},{24,16},{26,18},{28,24},{3... | collective-permute-start | bytes 595976 | tf_op jit(solution)/shard_map/ppermute | solution.py:469
  6.5 0.4 collective-permute-start.6
  6.9 0.3 turn.1.refs_0_
  7.2 2.6 %attend.7 = (f32[8,1,480]{2,1,0:T(1,128)S(1)}, f32[8,144,480]{2,1,0:T(8,128)S(1)}, bf16[2560,1024]{1,0:T(8,128)(2,1)S(1)}) custom-call(bf16[8,128,480]{2,1,0:T(8,128)(2,1)S(1)} %turn.1.refs_0_, bf16[776,128]{1,0:T(8,128)(2,1)S(1)} %get-tuple-element.51.refs_1_.refs_3_, bf16[776,128]{1,0:T(8,128)(2,1)S(1)} %collective-permute-done.1.refs_2_.refs_4_, ...), custom_call_target="tpu_custom_call" | custom-call | flops 377487360 | bytes 4194304 | tf_op jit(solution)/shard_map/attend/pallas_call | solution.py:280
  9.8 1.0 %collective-permute-done.2.refs_3_ = bf16[776,128]{1,0:T(8,128)(2,1)S(1)} collective-permute-done((bf16[776,128]{1,0:T(8,128)(2,1)S(1)}, bf16[776,128]{1,0:T(8,128)(2,1)S(1)}, u32[]{:S(2)}, u32[]{:S(2)}) %collective-permute-start.2) | collective-permute-done | bytes 198688 | tf_op jit(solution)/shard_map/ppermute | solution.py:468
  10.8 1.4 %collective-permute-done.3.refs_6_ = bf16[776,128]{1,0:T(8,128)(2,1)S(1)} collective-permute-done((bf16[776,128]{1,0:T(8,128)(2,1)S(1)}, bf16[776,128]{1,0:T(8,128)(2,1)S(1)}, u32[]{:S(2)}, u32[]{:S(2)}) %collective-permute-start.3) | collective-permute-done | bytes 198688 | tf_op jit(solution)/shard_map/ppermute | solution.py:509
  12.2 1.6 %collective-permute-start.4 = (bf16[776,128]{1,0:T(8,128)(2,1)S(1)}, bf16[776,128]{1,0:T(8,128)(2,1)S(1)}, u32[]{:S(2)}, u32[]{:S(2)}) collective-permute-start(bf16[776,128]{1,0:T(8,128)(2,1)S(1)} %collective-permute-done.2.refs_3_), channel_id=1, source_target_pairs={{0,8},{2,10},{8,16},{10,18},{16,24},{18,26},{24,28},{26,30},{28,20... | collective-permute-start | bytes 595976 | tf_op jit(solution)/shard_map/ppermute | solution.py:468
  13.8 0.4 collective-permute-start.5
  14.3 2.4 %collective-permute-done.7.refs_5_ = bf16[776,128]{1,0:T(8,128)(2,1)S(1)} collective-permute-done((bf16[776,128]{1,0:T(8,128)(2,1)S(1)}, bf16[776,128]{1,0:T(8,128)(2,1)S(1)}, u32[]{:S(2)}, u32[]{:S(2)}) %collective-permute-start.7) | collective-permute-done | bytes 198688 | tf_op jit(solution)/shard_map/ppermute | solution.py:469
  16.7 2.0 %collective-permute-start.10 = (bf16[776,128]{1,0:T(8,128)(2,1)S(1)}, bf16[776,128]{1,0:T(8,128)(2,1)S(1)}, u32[]{:S(2)}, u32[]{:S(2)}) collective-permute-start(bf16[776,128]{1,0:T(8,128)(2,1)S(1)} %collective-permute-done.6.refs_4_), channel_id=1, source_target_pairs={{0,8},{2,10},{8,16},{10,18},{16,24},{18,26},{24,28},{26,30},{28,20... | collective-permute-start | bytes 595976 | tf_op jit(solution)/shard_map/ppermute | solution.py:468
  18.7 2.6 %attend.8 = (f32[8,1,480]{2,1,0:T(1,128)S(1)}, f32[8,144,480]{2,1,0:T(8,128)S(1)}) custom-call(bf16[8,128,480]{2,1,0:T(8,128)(2,1)S(1)} %turn.1.refs_0_, bf16[776,128]{1,0:T(8,128)(2,1)S(1)} %get-tuple-element.51.refs_1_.refs_3_, bf16[776,128]{1,0:T(8,128)(2,1)S(1)} %collective-permute-done.1.refs_2_.refs_4_, ...), custom_call_target="tpu_custom_call" | custom-call | flops 754974720 | bytes 4194304 | tf_op jit(solution)/shard_map/attend/pallas_call | solution.py:280
  21.3 0.3 collective-permute-done.5.refs_6_
  21.6 1.7 %collective-permute-start.8 = (bf16[776,128]{1,0:T(8,128)(2,1)S(1)}, bf16[776,128]{1,0:T(8,128)(2,1)S(1)}, u32[]{:S(2)}, u32[]{:S(2)}) collective-permute-start(bf16[776,128]{1,0:T(8,128)(2,1)S(1)} %collective-permute-done.4.refs_3_), channel_id=1, source_target_pairs={{0,8},{2,10},{8,16},{10,18},{16,24},{18,26},{24,28},{26,30},{28,20... | collective-permute-start | bytes 595976 | tf_op jit(solution)/shard_map/ppermute | solution.py:468
  23.3 0.3 collective-permute-start.9
  23.6 2.0 %collective-permute-done.11.refs_5_ = bf16[776,128]{1,0:T(8,128)(2,1)S(1)} collective-permute-done((bf16[776,128]{1,0:T(8,128)(2,1)S(1)}, bf16[776,128]{1,0:T(8,128)(2,1)S(1)}, u32[]{:S(2)}, u32[]{:S(2)}) %collective-permute-start.11) | collective-permute-done | bytes 198688 | tf_op jit(solution)/shard_map/ppermute | solution.py:469
  25.6 0.2 collective-permute-start.15
  25.8 1.8 %collective-permute-start.14 = (bf16[776,128]{1,0:T(8,128)(2,1)S(1)}, bf16[776,128]{1,0:T(8,128)(2,1)S(1)}, u32[]{:S(2)}, u32[]{:S(2)}) collective-permute-start(bf16[776,128]{1,0:T(8,128)(2,1)S(1)} %collective-permute-done.10.refs_4_), channel_id=1, source_target_pairs={{0,8},{2,10},{8,16},{10,18},{16,24},{18,26},{24,28},{26,30},{28,20... | collective-permute-start | bytes 595976 | tf_op jit(solution)/shard_map/ppermute | solution.py:468
  27.6 3.2 %attend.9 = (f32[8,1,480]{2,1,0:T(1,128)S(1)}, f32[8,144,480]{2,1,0:T(8,128)S(1)}, bf16[2560,1408]{1,0:T(8,128)(2,1)S(1)}) custom-call(bf16[8,128,480]{2,1,0:T(8,128)(2,1)S(1)} %turn.1.refs_0_, bf16[776,128]{1,0:T(8,128)(2,1)S(1)} %get-tuple-element.51.refs_1_.refs_3_, bf16[776,128]{1,0:T(8,128)(2,1)S(1)} %collective-permute-done.1.refs_2_.refs_4_, ...), custom_call_target="tpu_custom_call" | custom-call | flops 754974720 | bytes 4194304 | tf_op jit(solution)/shard_map/attend/pallas_call | solution.py:280
  30.8 0.4 collective-permute-done.9.refs_6_
  31.2 1.6 %collective-permute-start.12 = (bf16[776,128]{1,0:T(8,128)(2,1)S(1)}, bf16[776,128]{1,0:T(8,128)(2,1)S(1)}, u32[]{:S(2)}, u32[]{:S(2)}) collective-permute-start(bf16[776,128]{1,0:T(8,128)(2,1)S(1)} %collective-permute-done.8.refs_3_), channel_id=1, source_target_pairs={{0,8},{2,10},{8,16},{10,18},{16,24},{18,26},{24,28},{26,30},{28,20... | collective-permute-start | bytes 595976 | tf_op jit(solution)/shard_map/ppermute | solution.py:468
  32.8 0.4 collective-permute-start.13
  33.2 0.6 collective-permute-done.15.refs_5_
  33.8 3.1 %attend.10 = (f32[8,1,480]{2,1,0:T(1,128)S(1)}, f32[8,144,480]{2,1,0:T(8,128)S(1)}, bf16[2560,1280]{1,0:T(8,128)(2,1)S(1)}) custom-call(bf16[8,128,480]{2,1,0:T(8,128)(2,1)S(1)} %turn.1.refs_0_, bf16[776,128]{1,0:T(8,128)(2,1)S(1)} %get-tuple-element.51.refs_1_.refs_3_, bf16[776,128]{1,0:T(8,128)(2,1)S(1)} %collective-permute-done.1.refs_2_.refs_4_, ...), custom_call_target="tpu_custom_call" | custom-call | flops 754974720 | bytes 4194304 | tf_op jit(solution)/shard_map/attend/pallas_call | solution.py:280
  36.9 1.6 %collective-permute-done.13.refs_4_ = bf16[776,128]{1,0:T(8,128)(2,1)S(1)} collective-permute-done((bf16[776,128]{1,0:T(8,128)(2,1)S(1)}, bf16[776,128]{1,0:T(8,128)(2,1)S(1)}, u32[]{:S(2)}, u32[]{:S(2)}) %collective-permute-start.13) | collective-permute-done | bytes 198688 | tf_op jit(solution)/shard_map/ppermute | solution.py:469
  38.5 1.0 %attend.12 = bf16[192,1280]{1,0:T(8,128)(2,1)S(1)} custom-call(bf16[8,128,480]{2,1,0:T(8,128)(2,1)S(1)} %turn.1.refs_0_, bf16[776,128]{1,0:T(8,128)(2,1)S(1)} %get-tuple-element.51.refs_1_.refs_3_, bf16[776,128]{1,0:T(8,128)(2,1)S(1)} %collective-permute-done.1.refs_2_.refs_4_, bf16[776,128]{1,0:T(8,128)(2,1)S(1)} %collective-permute-done.12.refs_3_, ...), custom_call_target="tpu_custom_call" | custom-call | flops 377487360 | bytes 4194304 | tf_op jit(solution)/shard_map/attend/pallas_call | solution.py:280
  39.6 0.5 collective-permute-start.17
  40.1 1.0 %attend.11.own_ref.refs_0_ = bf16[96,1280]{1,0:T(8,128)(2,1)S(1)} custom-call(bf16[8,128,480]{2,1,0:T(8,128)(2,1)S(1)} %turn.1.refs_0_, bf16[776,128]{1,0:T(8,128)(2,1)S(1)} %get-tuple-element.51.refs_1_.refs_3_, bf16[776,128]{1,0:T(8,128)(2,1)S(1)} %collective-permute-done.1.refs_2_.refs_4_, bf16[776,128]{1,0:T(8,128)(2,1)S(1)} %collective-permute-done.12.refs_3_, ...), custom_call_target="tpu_custom_call" | custom-call | flops 377487360 | bytes 4194304 | tf_op jit(solution)/shard_map/attend/pallas_call | solution.py:280
  41.1 0.7 %multiply.7.begun_ref = f32[96,1408]{1,0:T(8,128)S(1)} custom-call(bf16[96,1280]{1,0:T(8,128)(2,1)S(1)} %attend.11.own_ref.refs_0_, bf16[2560,1408]{1,0:T(8,128)(2,1)S(1)} %get-tuple-element.73.held_ref), custom_call_target="tpu_custom_call" | custom-call | flops 1024 | bytes 1024 | tf_op jit(solution)/shard_map/multiply/pallas_call | solution.py:369
  41.9 0.8 %multiply.8 = bf16[96,1408]{1,0:T(8,128)(2,1)S(1)} custom-call(bf16[96,1280]{1,0:T(8,128)(2,1)S(1)} %collective-permute-done.16.other_ref.refs_1_, bf16[2560,1408]{1,0:T(8,128)(2,1)S(1)} %get-tuple-element.73.held_ref, f32[96,1408]{1,0:T(8,128)S(1)} %multiply.7.begun_ref), custom_call_target="tpu_custom_call" | custom-call | flops 1024 | bytes 1024 | tf_op jit(solution)/shard_map/multiply/pallas_call | solution.py:369
  42.7 1.3 %collective-permute-start.19 = (bf16[96,1408]{1,0:T(8,128)(2,1)S(1)}, bf16[96,1408]{1,0:T(8,128)(2,1)S(1)}, u32[]{:S(2)}, u32[]{:S(2)}) collective-permute-start(bf16[96,1408]{1,0:T(8,128)(2,1)S(1)} %multiply.8), channel_id=1, source_target_pairs={{0,1},{1,0},{2,3},{3,2},{4,5},{5,4},{6,7},{7,6},{8,9},{9,8},{10,11... | collective-permute-start | bytes 811016 | tf_op jit(solution)/shard_map/ppermute | solution.py:589
  44.0 0.9 %attend.13.refs_2_.own_ref = bf16[96,1280]{1,0:T(8,128)(2,1)S(1)} custom-call(bf16[8,128,480]{2,1,0:T(8,128)(2,1)S(1)} %turn.1.refs_0_, bf16[776,128]{1,0:T(8,128)(2,1)S(1)} %get-tuple-element.51.refs_1_.refs_3_, bf16[776,128]{1,0:T(8,128)(2,1)S(1)} %collective-permute-done.1.refs_2_.refs_4_, bf16[776,128]{1,0:T(8,128)(2,1)S(1)} %collective-permute-done.12.refs_3_, ...), custom_call_target="tpu_custom_call" | custom-call | flops 377487360 | bytes 4194304 | tf_op jit(solution)/shard_map/attend/pallas_call | solution.py:280
  44.9 2.3 %multiply.9 = (bf16[96,1280]{1,0:T(8,128)(2,1)S(1)}, bf16[96,1280]{1,0:T(8,128)(2,1)S(1)}, bf16[2560,768]{1,0:T(8,128)(2,1)S(1)}) custom-call(bf16[96,1280]{1,0:T(8,128)(2,1)S(1)} %attend.11.own_ref.refs_0_, bf16[96,1280]{1,0:T(8,128)(2,1)S(1)} %collective-permute-done.16.other_ref.refs_1_, bf16[96,1280]{1,0:T(8,128)(2,1)S(1)} %attend.13.refs_2_.own_ref, ...), custom_call_target="tpu_custom_call" | custom-call | flops 1024 | bytes 1024 | tf_op jit(solution)/shard_map/multiply/pallas_call | solution.py:369
  47.2 1.2 %collective-permute-start.20 = (bf16[96,1280]{1,0:T(8,128)(2,1)S(1)}, bf16[96,1280]{1,0:T(8,128)(2,1)S(1)}, u32[]{:S(2)}, u32[]{:S(2)}) collective-permute-start(bf16[96,1280]{1,0:T(8,128)(2,1)S(1)} %get-tuple-element.78), channel_id=1, source_target_pairs={{0,1},{1,0},{2,3},{3,2},{4,5},{5,4},{6,7},{7,6},{8,9},{9,8},{10,11... | collective-permute-start | bytes 737288 | tf_op jit(solution)/shard_map/ppermute | solution.py:589
  48.3 2.4 %multiply.10 = (bf16[96,1024]{1,0:T(8,128)(2,1)S(1)}, bf16[96,1024]{1,0:T(8,128)(2,1)S(1)}, bf16[2560,640]{1,0:T(8,128)(2,1)S(1)}) custom-call(bf16[96,1280]{1,0:T(8,128)(2,1)S(1)} %attend.11.own_ref.refs_0_, bf16[96,1280]{1,0:T(8,128)(2,1)S(1)} %collective-permute-done.16.other_ref.refs_1_, bf16[96,1280]{1,0:T(8,128)(2,1)S(1)} %attend.13.refs_2_.own_ref, ...), custom_call_target="tpu_custom_call" | custom-call | flops 1024 | bytes 1024 | tf_op jit(solution)/shard_map/multiply/pallas_call | solution.py:369
  50.7 1.0 %collective-permute-start.21 = (bf16[96,1024]{1,0:T(8,128)(2,1)S(1)}, bf16[96,1024]{1,0:T(8,128)(2,1)S(1)}, u32[]{:S(2)}, u32[]{:S(2)}) collective-permute-start(bf16[96,1024]{1,0:T(8,128)(2,1)S(1)} %get-tuple-element.81), channel_id=1, source_target_pairs={{0,1},{1,0},{2,3},{3,2},{4,5},{5,4},{6,7},{7,6},{8,9},{9,8},{10,11... | collective-permute-start | bytes 589832 | tf_op jit(solution)/shard_map/ppermute | solution.py:589
  51.7 0.9 %multiply.11 = (bf16[96,768]{1,0:T(8,128)(2,1)S(1)}, bf16[96,768]{1,0:T(8,128)(2,1)S(1)}) custom-call(bf16[96,1280]{1,0:T(8,128)(2,1)S(1)} %attend.11.own_ref.refs_0_, bf16[96,1280]{1,0:T(8,128)(2,1)S(1)} %collective-permute-done.16.other_ref.refs_1_, bf16[96,1280]{1,0:T(8,128)(2,1)S(1)} %attend.13.refs_2_.own_ref, ...), custom_call_target="tpu_custom_call" | custom-call | flops 1024 | bytes 1024 | tf_op jit(solution)/shard_map/multiply/pallas_call | solution.py:369
  52.7 1.1 %collective-permute-start.22 = (bf16[96,768]{1,0:T(8,128)(2,1)S(1)}, bf16[96,768]{1,0:T(8,128)(2,1)S(1)}, u32[]{:S(2)}, u32[]{:S(2)}) collective-permute-start(bf16[96,768]{1,0:T(8,128)(2,1)S(1)} %get-tuple-element.84), channel_id=1, source_target_pairs={{0,1},{1,0},{2,3},{3,2},{4,5},{5,4},{6,7},{7,6},{8,9},{9,8},{10,11... | collective-permute-start | bytes 442376 | tf_op jit(solution)/shard_map/ppermute | solution.py:589
  53.8 0.9 %multiply.12 = (bf16[96,640]{1,0:T(8,128)(2,1)S(1)}, bf16[96,640]{1,0:T(8,128)(2,1)S(1)}) custom-call(bf16[96,1280]{1,0:T(8,128)(2,1)S(1)} %attend.11.own_ref.refs_0_, bf16[96,1280]{1,0:T(8,128)(2,1)S(1)} %collective-permute-done.16.other_ref.refs_1_, bf16[96,1280]{1,0:T(8,128)(2,1)S(1)} %attend.13.refs_2_.own_ref, ...), custom_call_target="tpu_custom_call" | custom-call | flops 1024 | bytes 1024 | tf_op jit(solution)/shard_map/multiply/pallas_call | solution.py:369
  54.8 1.0 %collective-permute-start.18 = (bf16[96,640]{1,0:T(8,128)(2,1)S(1)}, bf16[96,640]{1,0:T(8,128)(2,1)S(1)}, u32[]{:S(2)}, u32[]{:S(2)}) collective-permute-start(bf16[96,640]{1,0:T(8,128)(2,1)S(1)} %get-tuple-element.88), channel_id=1, source_target_pairs={{0,1},{1,0},{2,3},{3,2},{4,5},{5,4},{6,7},{7,6},{8,9},{9,8},{10,11... | collective-permute-start | bytes 368648 | tf_op jit(solution)/shard_map/ppermute | solution.py:589
  55.8 1.3 %multiply.13.refs_0_ = bf16[96,1408]{1,0:T(8,128)(2,1)S(1)} custom-call(bf16[96,1280]{1,0:T(8,128)(2,1)S(1)} %attend.13.refs_2_.own_ref, bf16[96,1280]{1,0:T(8,128)(2,1)S(1)} %collective-permute-done.17.refs_3_.other_ref, bf16[2560,1408]{1,0:T(8,128)(2,1)S(1)} %get-tuple-element.73.held_ref), custom_call_target="tpu_custom_call" | custom-call | flops 1024 | bytes 1024 | tf_op jit(solution)/shard_map/multiply/pallas_call | solution.py:369
  57.1 7.6 %collective-permute-done.22.refs_7_ = bf16[96,768]{1,0:T(8,128)(2,1)S(1)} collective-permute-done((bf16[96,768]{1,0:T(8,128)(2,1)S(1)}, bf16[96,768]{1,0:T(8,128)(2,1)S(1)}, u32[]{:S(2)}, u32[]{:S(2)}) %collective-permute-start.22) | collective-permute-done | bytes 147488 | tf_op jit(solution)/shard_map/ppermute | solution.py:589
  64.7 1.1 %finish.2.refs_2_ = bf16[96,5120]{1,0:T(8,128)(2,1)} custom-call(bf16[96,1408]{1,0:T(8,128)(2,1)S(1)} %multiply.13.refs_0_, bf16[96,1280]{1,0:T(8,128)(2,1)S(1)} %get-tuple-element.90.refs_1_, bf16[96,1024]{1,0:T(8,128)(2,1)S(1)} %get-tuple-element.91.refs_2_, bf16[96,768]{1,0:T(8,128)(2,1)S(1)} %get-tuple-element.92.refs_3_, ...), custom_call_target="tpu_custom_call" | custom-call | flops 1024 | bytes 1024 | tf_op jit(solution)/shard_map/finish/pallas_call | solution.py:445
  65.9 0.6 collective-permute-done.18.refs_1_
  66.5 0.7 %finish.3 = bf16[96,5120]{1,0:T(8,128)(2,1)} custom-call(bf16[96,640]{1,0:T(8,128)(2,1)S(1)} %get-tuple-element.87.refs_0_, bf16[96,640]{1,0:T(8,128)(2,1)S(1)} %collective-permute-done.18.refs_1_, bf16[96,5120]{1,0:T(8,128)(2,1)} %finish.2.refs_2_), custom_call_target="tpu_custom_call", output_to_operand_aliasing={{}: (2, {})} | custom-call | flops 1024 | bytes 1024 | tf_op jit(solution)/shard_map/finish/pallas_call | solution.py:445
  (17 shorter events, 0.1 us)
Async XLA Ops:
  1.5 5.0 %collective-permute-start = (bf16[192,1280]{1,0:T(8,128)(2,1)S(1)}, bf16[192,1280]{1,0:T(8,128)(2,1)S(1)}, u32[]{:S(2)}, u32[]{:S(2)}) collective-permute-start(bf16[192,1280]{1,0:T(8,128)(2,1)S(1)} %get-tuple-element.50), channel_id=1, source_target_pairs={{0,2},{2,0},{4,6},{6,4},{8,10},{10,8},{12,14},{14,12},{16,18},{18,... | collective-permute-start | bytes 1474568 | tf_op jit(solution)/shard_map/ppermute | solution.py:474
  2.0 5.2 %collective-permute-start.1 = (bf16[776,128]{1,0:T(8,128)(2,1)S(1)}, bf16[776,128]{1,0:T(8,128)(2,1)S(1)}, u32[]{:S(2)}, u32[]{:S(2)}) collective-permute-start(bf16[776,128]{1,0:T(8,128)(2,1)S(1)} %get-tuple-element.52), channel_id=1, source_target_pairs={{0,2},{2,0},{4,6},{6,4},{8,10},{10,8},{12,14},{14,12},{16,18},{18,... | collective-permute-start | bytes 595976 | tf_op jit(solution)/shard_map/ppermute | solution.py:473
  2.1 8.7 %collective-permute-start.2 = (bf16[776,128]{1,0:T(8,128)(2,1)S(1)}, bf16[776,128]{1,0:T(8,128)(2,1)S(1)}, u32[]{:S(2)}, u32[]{:S(2)}) collective-permute-start(bf16[776,128]{1,0:T(8,128)(2,1)S(1)} %get-tuple-element.51.refs_1_.refs_3_), channel_id=1, source_target_pairs={{0,8},{2,10},{8,16},{10,18},{16,24},{18,26},{24,28},{26,30},{28,20... | collective-permute-start | bytes 595976 | tf_op jit(solution)/shard_map/ppermute | solution.py:468
  5.1 7.1 %collective-permute-start.3 = (bf16[776,128]{1,0:T(8,128)(2,1)S(1)}, bf16[776,128]{1,0:T(8,128)(2,1)S(1)}, u32[]{:S(2)}, u32[]{:S(2)}) collective-permute-start(bf16[776,128]{1,0:T(8,128)(2,1)S(1)} %get-tuple-element.52), channel_id=1, source_target_pairs={{0,6},{2,4},{8,2},{10,0},{16,10},{18,8},{24,18},{26,16},{28,26},{3... | collective-permute-start | bytes 595976 | tf_op jit(solution)/shard_map/ppermute | solution.py:509
  5.1 11.6 %collective-permute-start.7 = (bf16[776,128]{1,0:T(8,128)(2,1)S(1)}, bf16[776,128]{1,0:T(8,128)(2,1)S(1)}, u32[]{:S(2)}, u32[]{:S(2)}) collective-permute-start(bf16[776,128]{1,0:T(8,128)(2,1)S(1)} %get-tuple-element.51.refs_1_.refs_3_), channel_id=1, source_target_pairs={{0,4},{2,6},{8,0},{10,2},{16,8},{18,10},{24,16},{26,18},{28,24},{3... | collective-permute-start | bytes 595976 | tf_op jit(solution)/shard_map/ppermute | solution.py:469
  6.5 10.2 %collective-permute-start.6 = (bf16[776,128]{1,0:T(8,128)(2,1)S(1)}, bf16[776,128]{1,0:T(8,128)(2,1)S(1)}, u32[]{:S(2)}, u32[]{:S(2)}) collective-permute-start(bf16[776,128]{1,0:T(8,128)(2,1)S(1)} %get-tuple-element.52), channel_id=1, source_target_pairs={{0,10},{2,8},{8,18},{10,16},{16,26},{18,24},{24,30},{26,28},{28,22... | collective-permute-start | bytes 595976 | tf_op jit(solution)/shard_map/ppermute | solution.py:508
  12.2 9.1 %collective-permute-start.4 = (bf16[776,128]{1,0:T(8,128)(2,1)S(1)}, bf16[776,128]{1,0:T(8,128)(2,1)S(1)}, u32[]{:S(2)}, u32[]{:S(2)}) collective-permute-start(bf16[776,128]{1,0:T(8,128)(2,1)S(1)} %collective-permute-done.2.refs_3_), channel_id=1, source_target_pairs={{0,8},{2,10},{8,16},{10,18},{16,24},{18,26},{24,28},{26,30},{28,20... | collective-permute-start | bytes 595976 | tf_op jit(solution)/shard_map/ppermute | solution.py:468
  13.8 7.8 %collective-permute-start.5 = (bf16[776,128]{1,0:T(8,128)(2,1)S(1)}, bf16[776,128]{1,0:T(8,128)(2,1)S(1)}, u32[]{:S(2)}, u32[]{:S(2)}) collective-permute-start(bf16[776,128]{1,0:T(8,128)(2,1)S(1)} %collective-permute-done.3.refs_6_), channel_id=1, source_target_pairs={{0,4},{2,6},{8,0},{10,2},{16,8},{18,10},{24,16},{26,18},{28,24},{3... | collective-permute-start | bytes 595976 | tf_op jit(solution)/shard_map/ppermute | solution.py:469
  16.7 8.9 %collective-permute-start.11 = (bf16[776,128]{1,0:T(8,128)(2,1)S(1)}, bf16[776,128]{1,0:T(8,128)(2,1)S(1)}, u32[]{:S(2)}, u32[]{:S(2)}) collective-permute-start(bf16[776,128]{1,0:T(8,128)(2,1)S(1)} %collective-permute-done.7.refs_5_), channel_id=1, source_target_pairs={{0,4},{2,6},{8,0},{10,2},{16,8},{18,10},{24,16},{26,18},{28,24},{3... | collective-permute-start | bytes 595976 | tf_op jit(solution)/shard_map/ppermute | solution.py:469
  16.7 9.1 %collective-permute-start.10 = (bf16[776,128]{1,0:T(8,128)(2,1)S(1)}, bf16[776,128]{1,0:T(8,128)(2,1)S(1)}, u32[]{:S(2)}, u32[]{:S(2)}) collective-permute-start(bf16[776,128]{1,0:T(8,128)(2,1)S(1)} %collective-permute-done.6.refs_4_), channel_id=1, source_target_pairs={{0,8},{2,10},{8,16},{10,18},{16,24},{18,26},{24,28},{26,30},{28,20... | collective-permute-start | bytes 595976 | tf_op jit(solution)/shard_map/ppermute | solution.py:468
  21.6 9.2 %collective-permute-start.8 = (bf16[776,128]{1,0:T(8,128)(2,1)S(1)}, bf16[776,128]{1,0:T(8,128)(2,1)S(1)}, u32[]{:S(2)}, u32[]{:S(2)}) collective-permute-start(bf16[776,128]{1,0:T(8,128)(2,1)S(1)} %collective-permute-done.4.refs_3_), channel_id=1, source_target_pairs={{0,8},{2,10},{8,16},{10,18},{16,24},{18,26},{24,28},{26,30},{28,20... | collective-permute-start | bytes 595976 | tf_op jit(solution)/shard_map/ppermute | solution.py:468
  23.3 7.9 %collective-permute-start.9 = (bf16[776,128]{1,0:T(8,128)(2,1)S(1)}, bf16[776,128]{1,0:T(8,128)(2,1)S(1)}, u32[]{:S(2)}, u32[]{:S(2)}) collective-permute-start(bf16[776,128]{1,0:T(8,128)(2,1)S(1)} %collective-permute-done.5.refs_6_), channel_id=1, source_target_pairs={{0,4},{2,6},{8,0},{10,2},{16,8},{18,10},{24,16},{26,18},{28,24},{3... | collective-permute-start | bytes 595976 | tf_op jit(solution)/shard_map/ppermute | solution.py:469
  25.6 8.2 %collective-permute-start.15 = (bf16[776,128]{1,0:T(8,128)(2,1)S(1)}, bf16[776,128]{1,0:T(8,128)(2,1)S(1)}, u32[]{:S(2)}, u32[]{:S(2)}) collective-permute-start(bf16[776,128]{1,0:T(8,128)(2,1)S(1)} %collective-permute-done.11.refs_5_), channel_id=1, source_target_pairs={{0,4},{2,6},{8,0},{10,2},{16,8},{18,10},{24,16},{26,18},{28,24},{3... | collective-permute-start | bytes 595976 | tf_op jit(solution)/shard_map/ppermute | solution.py:469
  25.8 8.0 %collective-permute-start.14 = (bf16[776,128]{1,0:T(8,128)(2,1)S(1)}, bf16[776,128]{1,0:T(8,128)(2,1)S(1)}, u32[]{:S(2)}, u32[]{:S(2)}) collective-permute-start(bf16[776,128]{1,0:T(8,128)(2,1)S(1)} %collective-permute-done.10.refs_4_), channel_id=1, source_target_pairs={{0,8},{2,10},{8,16},{10,18},{16,24},{18,26},{24,28},{26,30},{28,20... | collective-permute-start | bytes 595976 | tf_op jit(solution)/shard_map/ppermute | solution.py:468
  31.2 5.7 %collective-permute-start.12 = (bf16[776,128]{1,0:T(8,128)(2,1)S(1)}, bf16[776,128]{1,0:T(8,128)(2,1)S(1)}, u32[]{:S(2)}, u32[]{:S(2)}) collective-permute-start(bf16[776,128]{1,0:T(8,128)(2,1)S(1)} %collective-permute-done.8.refs_3_), channel_id=1, source_target_pairs={{0,8},{2,10},{8,16},{10,18},{16,24},{18,26},{24,28},{26,30},{28,20... | collective-permute-start | bytes 595976 | tf_op jit(solution)/shard_map/ppermute | solution.py:468
  32.8 5.7 %collective-permute-start.13 = (bf16[776,128]{1,0:T(8,128)(2,1)S(1)}, bf16[776,128]{1,0:T(8,128)(2,1)S(1)}, u32[]{:S(2)}, u32[]{:S(2)}) collective-permute-start(bf16[776,128]{1,0:T(8,128)(2,1)S(1)} %collective-permute-done.9.refs_6_), channel_id=1, source_target_pairs={{0,4},{2,6},{8,0},{10,2},{16,8},{18,10},{24,16},{26,18},{28,24},{3... | collective-permute-start | bytes 595976 | tf_op jit(solution)/shard_map/ppermute | solution.py:469
  39.5 2.4 %collective-permute-start.16 = (bf16[96,1280]{1,0:T(8,128)(2,1)S(1)}, bf16[96,1280]{1,0:T(8,128)(2,1)S(1)}, u32[]{:S(2)}, u32[]{:S(2)}) collective-permute-start(bf16[96,1280]{1,0:T(8,128)(2,1)S(1)} %get-tuple-element.94), channel_id=1, source_target_pairs={{0,2},{2,0},{4,6},{6,4},{8,10},{10,8},{12,14},{14,12},{16,18},{18,... | collective-permute-start | bytes 737288 | tf_op jit(solution)/shard_map/ppermute | solution.py:520
  39.6 5.3 %collective-permute-start.17 = (bf16[96,1280]{1,0:T(8,128)(2,1)S(1)}, bf16[96,1280]{1,0:T(8,128)(2,1)S(1)}, u32[]{:S(2)}, u32[]{:S(2)}) collective-permute-start(bf16[96,1280]{1,0:T(8,128)(2,1)S(1)} %get-tuple-element.93), channel_id=1, source_target_pairs={{0,2},{2,0},{4,6},{6,4},{8,10},{10,8},{12,14},{14,12},{16,18},{18,... | collective-permute-start | bytes 737288 | tf_op jit(solution)/shard_map/ppermute | solution.py:520
  42.7 22.1 %collective-permute-start.19 = (bf16[96,1408]{1,0:T(8,128)(2,1)S(1)}, bf16[96,1408]{1,0:T(8,128)(2,1)S(1)}, u32[]{:S(2)}, u32[]{:S(2)}) collective-permute-start(bf16[96,1408]{1,0:T(8,128)(2,1)S(1)} %multiply.8), channel_id=1, source_target_pairs={{0,1},{1,0},{2,3},{3,2},{4,5},{5,4},{6,7},{7,6},{8,9},{9,8},{10,11... | collective-permute-start | bytes 811016 | tf_op jit(solution)/shard_map/ppermute | solution.py:589
  47.2 17.5 %collective-permute-start.20 = (bf16[96,1280]{1,0:T(8,128)(2,1)S(1)}, bf16[96,1280]{1,0:T(8,128)(2,1)S(1)}, u32[]{:S(2)}, u32[]{:S(2)}) collective-permute-start(bf16[96,1280]{1,0:T(8,128)(2,1)S(1)} %get-tuple-element.78), channel_id=1, source_target_pairs={{0,1},{1,0},{2,3},{3,2},{4,5},{5,4},{6,7},{7,6},{8,9},{9,8},{10,11... | collective-permute-start | bytes 737288 | tf_op jit(solution)/shard_map/ppermute | solution.py:589
  50.7 14.0 %collective-permute-start.21 = (bf16[96,1024]{1,0:T(8,128)(2,1)S(1)}, bf16[96,1024]{1,0:T(8,128)(2,1)S(1)}, u32[]{:S(2)}, u32[]{:S(2)}) collective-permute-start(bf16[96,1024]{1,0:T(8,128)(2,1)S(1)} %get-tuple-element.81), channel_id=1, source_target_pairs={{0,1},{1,0},{2,3},{3,2},{4,5},{5,4},{6,7},{7,6},{8,9},{9,8},{10,11... | collective-permute-start | bytes 589832 | tf_op jit(solution)/shard_map/ppermute | solution.py:589
  52.7 12.0 %collective-permute-start.22 = (bf16[96,768]{1,0:T(8,128)(2,1)S(1)}, bf16[96,768]{1,0:T(8,128)(2,1)S(1)}, u32[]{:S(2)}, u32[]{:S(2)}) collective-permute-start(bf16[96,768]{1,0:T(8,128)(2,1)S(1)} %get-tuple-element.84), channel_id=1, source_target_pairs={{0,1},{1,0},{2,3},{3,2},{4,5},{5,4},{6,7},{7,6},{8,9},{9,8},{10,11... | collective-permute-start | bytes 442376 | tf_op jit(solution)/shard_map/ppermute | solution.py:589
  54.8 11.7 %collective-permute-start.18 = (bf16[96,640]{1,0:T(8,128)(2,1)S(1)}, bf16[96,640]{1,0:T(8,128)(2,1)S(1)}, u32[]{:S(2)}, u32[]{:S(2)}) collective-permute-start(bf16[96,640]{1,0:T(8,128)(2,1)S(1)} %get-tuple-element.88), channel_id=1, source_target_pairs={{0,1},{1,0},{2,3},{3,2},{4,5},{5,4},{6,7},{7,6},{8,9},{9,8},{10,11... | collective-permute-start | bytes 368648 | tf_op jit(solution)/shard_map/ppermute | solution.py:589
